TPU v7x, 32 devices: a whole 2x2x4 slice. The times are simulated.
32 devices in a mesh: dp: 4 (over z), tensor: 8 (over y, x, core).
Axes of the slice: x: 2, y: 2, z: 4, core: 2. Of those that a mesh axis runs over, the one named last changes fastest.
Arguments:
- acts: bfloat16 [4, 512, 4096], P('dp', None, 'tensor'), may hold values from -6 to 6
- grads: bfloat16 [4, 512, 4096], P('dp', None, 'tensor'), may hold values from -6 to 6
- basis_in_held: bfloat16 [4, 4096, 4096], P('dp', None, 'tensor'), may hold values from -0.09375 to 0.09375
- basis_out_held: bfloat16 [4, 4096, 4096], P('dp', None, 'tensor'), may hold values from -0.09375 to 0.09375
- owners: int32 [2, 8], replicated, may hold values from 0 to 3
- eig_lambda: bfloat16 [4096, 4096], P('tensor'), may hold values from 0.0049743652 to 0.19921875
Outputs:
- precond: bfloat16 [4, 4096, 4096], P('dp', 'tensor')
Inputs may be any that keep to these rules, and one draw needn't show every extreme that they name: `owners`: row 0 is for the input eigenbasis, row 1 for the output eigenbasis; entry j names the dp group whose copy of column block j is current, the other copies of that block are stale.
All inputs are finite; a program needn't handle non-finite values.
Results may differ from a plain program's by a relative error of at most 0.0057.
Values may be sent and summed in bfloat16 or wider, within the bound.
No kernel may reach another device: no remote copies, remote signals or barrier semaphores. Data moves between devices by JAX's collectives and lax.ppermute only.
A program may use at most 64 MiB of HBM per device.

v0:
```python
import jax
import jax.numpy as jnp
from jax import lax
from jax.sharding import PartitionSpec as P

damping = 0.01


def from_root(block, axis, owner):
    block = jnp.where(lax.axis_index(axis) == owner, block, jnp.zeros_like(block))
    return lax.psum(block, axis)


def shards(acts, grads, basis_in_held, basis_out_held, owners, eig_lambda):
    column = lax.axis_index("tensor")
    owner_in = owners[0, column]
    owner_out = owners[1, column]
    basis_in = from_root(basis_in_held[0], "dp", owner_in)
    basis_out = from_root(basis_out_held[0], "dp", owner_out)
    tokens = acts.shape[1]
    rot_in = jnp.dot(
        lax.all_gather(acts[0], "tensor", axis=1, tiled=True),
        basis_in,
        preferred_element_type=jnp.float32,
    )
    rot_out = jnp.dot(
        lax.all_gather(grads[0], "tensor", axis=1, tiled=True),
        basis_out,
        preferred_element_type=jnp.float32,
    )
    rot_in = rot_in.astype(jnp.bfloat16)
    rot_out = rot_out.astype(jnp.bfloat16)
    denom = eig_lambda.astype(jnp.float32) + damping
    contract = (((0,), (0,)), ((), ()))
    product = (
        lax.dot_general(
            rot_out,
            lax.all_gather(rot_in, "tensor", axis=1, tiled=True),
            contract,
            preferred_element_type=jnp.float32,
        )
        / tokens
    )
    return (product / denom).astype(jnp.bfloat16)[None]


def solution(mesh):
    placed = (
        P("dp", None, "tensor"),
        P("dp", None, "tensor"),
        P("dp", None, "tensor"),
        P("dp", None, "tensor"),
        P(),
        P("tensor", None),
    )
    return jax.shard_map(
        shards, mesh=mesh, in_specs=placed, out_specs=P("dp", "tensor", None), check_vma=False
    )
```

profile of v0, /device:TPU:16, one launch (start us, length us, event | category | flops | bytes accessed | tf_op | source)
XLA Modules:
  0.0 371.6 jit_solution(10752449647438098650)
XLA Ops:
  7.4 0.0 all-gather.10.cloned.1.call-start
  7.4 0.7 all-gather.10.cloned.1.call-update
  8.1 0.0 all-reduce.3.cloned.1.call-start
  8.1 1.4 constant_dynamic-slice_fusion
  10.9 3.9 %select_bitcast_fusion = (bf16[4096,512]{1,0:T(8,128)(2,1)}, bf16[4096,512]{1,0:T(8,128)(2,1)}) fusion(bf16[1,4096,512]{2,1,0:T(8,128)(2,1)} %param.8, pred[]{:T(512)S(6)} %eq.7, bf16[1,4096,512]{2,1,0:T(8,128)(2,1)} %param.9, pred[]{:T(512)S(6)} %eq.6), kind=kLoop, calls=%fused_computation.6 | loop fusion | flops 4194304 | bytes 16777218 | tf_op jit(solution)/shard_map/jit(_where)/select_n | solution.py:10
  14.8 0.0 all-reduce.3.cloned.1.call-update
  14.8 0.0 all-gather.8.cloned.1.call-start
  14.8 0.7 all-gather.8.cloned.1.call-update
  15.5 0.0 all-gather.6.cloned.1.call-start
  15.6 33.1 %all-gather.10.cloned.1.call-done = bf16[1,512,4096]{2,1,0:T(8,128)(2,1)} async-done(((bf16[1,512,512]{2,1,0:T(8,128)(2,1)}), bf16[1,512,4096]{2,1,0:T(8,128)(2,1)}) %all-gather.10.cloned.1.call-update) | async-done | bytes 4194320 | tf_op jit(solution)/shard_map/all_gather | solution.py:22
  48.6 259.9 %all-reduce.3.cloned.1.call-done = (bf16[4096,512]{1,0:T(8,128)(2,1)}, bf16[4096,512]{1,0:T(8,128)(2,1)}) async-done(((bf16[4096,512]{1,0:T(8,128)(2,1)}, bf16[4096,512]{1,0:T(8,128)(2,1)}), (bf16[4096,512]{1,0:T(8,128)(2,1)}, bf16[4096,512]{1,0:T(8,128)(2,1)})) %all-reduce.3.cloned.1.call-update) | async-done | bytes 8388624 | tf_op jit(solution)/shard_map/psum | solution.py:11
  308.5 6.6 %fusion.13 = bf16[512,512]{0,1:T(8,128)(2,1)} fusion(bf16[4096,512]{1,0:T(8,128)(2,1)} %get-tuple-element.5, bf16[1,512,4096]{2,1,0:T(8,128)(2,1)} %all-gather.10.cloned.1.call-done), kind=kOutput, calls=%fused_computation.10 | convolution fusion | flops 2147745792 | bytes 8912896 | tf_op jit(solution)/shard_map/dot_general | solution.py:21
  315.1 0.0 all-gather.6.cloned.1.call-update
  315.2 0.0 all-gather.8.cloned.1.call-done
  315.2 36.8 %all-gather.6.cloned.1.call-done = bf16[512,4096]{0,1:T(8,128)(2,1)} async-done(((bf16[512,512]{0,1:T(8,128)(2,1)}), bf16[512,4096]{0,1:T(8,128)(2,1)}) %all-gather.6.cloned.1.call-update) | async-done | bytes 4194320 | tf_op jit(solution)/shard_map/all_gather | solution.py:38
  352.0 12.5 %fusion = bf16[1,512,4096]{2,1,0:T(8,128)(2,1)} fusion(bf16[512,4096]{1,0:T(8,128)(2,1)} %param.11, bf16[512,4096]{0,1:T(8,128)(2,1)} %all-gather.6.cloned.1.call-done, bf16[4096,512]{1,0:T(8,128)(2,1)} %get-tuple-element.6, bf16[1,512,4096]{2,1,0:T(8,128)(2,1)} %all-gather.8.cloned.1.call-done), kind=kOutput, calls=%fused_computation.1 | convolution fusion | flops 4305715200 | bytes 20971520 | tf_op jit(solution)/shard_map/dot_general | solution.py:36
Async XLA Ops:
  7.4 41.3 %all-gather.10.cloned.1.call-start = ((), (), s32[]{:S(2)}) async-start(), calls=%async_computation.2 | async-start | bytes 4718592 | tf_op jit(solution)/shard_map/all_gather | solution.py:22
  8.1 300.4 %all-reduce.3.cloned.1.call-start = ((), (), s32[]{:S(2)}) async-start(), calls=%async_computation.3 | async-start | bytes 16777216 | tf_op jit(solution)/shard_map/psum | solution.py:11
  14.8 300.4 %all-gather.8.cloned.1.call-start = ((), (), s32[]{:S(2)}) async-start(), calls=%async_computation.1 | async-start | bytes 4718592 | tf_op jit(solution)/shard_map/all_gather | solution.py:27
  15.5 336.5 %all-gather.6.cloned.1.call-start = ((), (), s32[]{:S(2)}) async-start(), calls=%async_computation | async-start | bytes 4718592 | tf_op jit(solution)/shard_map/all_gather | solution.py:38
Sparse Core Ops, SparseCore 0:
  10.1 38.5 all-gather.9
  50.5 37.4 all-gather.7
  315.3 36.6 all-gather.5
Sparse Core Ops, SparseCore 1:
  14.9 293.6 all-reduce.2
where the time goes:
time: 373 us; the launch traced here: 372 us
  waiting for transfers between devices  331 us (89%)
  matrix products  19.1 us (5%)
  between operations  15.9 us (4%)
  other arithmetic  3.88 us (1%)
    psum x1, waiting for transfers between devices, from_root(): return lax.psum(block, axis)  260 us
    all_gather x1, waiting for transfers between devices, shards(): lax.all_gather(rot_in, 'tensor', axis=1, tiled=True)  36.8 us
    all_gather x1, waiting for transfers between devices, shards(): lax.all_gather(acts[0], 'tensor', axis=1, tiled=True)  33.1 us
    dot_general x1, matrix products, shards(): lax.dot_general(rot_out, lax.all_gather(rot_in, 'tensor', axis=1, tiled=T...  12.5 us
  transfers between devices with their start and end apart: 4, of which 3 were waited for; matrix products, arithmetic and copies ran while one was open for 3% of the time, Pallas kernels for 0%

commit v1 on v0

v1 whole, which is shorter than its diff:
```python
import jax
import jax.numpy as jnp
from jax import lax
from jax.sharding import PartitionSpec as P

damping = 0.01
CHUNKS = 16
STREAMS = 2


def chain_broadcast(helds, owners, axis, n):
    me = lax.axis_index(axis)
    rows, cols = helds[0].shape
    size = rows // CHUNKS
    per = CHUNKS // STREAMS
    total = per * len(helds)
    outs = list(helds)

    def place(stream, c, k):
        return ((c - k * per) * STREAMS + stream) * size

    def own(stream, c, first, last):
        low, high = max(first, 0) // per, min(last, total - 1) // per
        picked = None
        for k in range(low, high + 1):
            at = place(stream, jnp.clip(c, k * per, (k + 1) * per - 1), k)
            block = lax.dynamic_slice(helds[k], (at, 0), (size, cols))
            picked = block if picked is None else jnp.where(c >= k * per, block, picked)
        return picked

    def owner_of(c):
        owner = owners[0]
        for k in range(1, len(helds)):
            owner = jnp.where(c >= k * per, owners[k], owner)
        return owner

    came = [[None, None] for _ in range(STREAMS)]
    sent = None
    for t in range(total + n - 2):
        for s in range(STREAMS):
            if came[s][0] is not None:
                came[s], _ = lax.optimization_barrier((came[s], sent))
            right = t - me
            left = t - (n - 1 - me)
            to_right = own(s, right, t - (n - 2), t)
            to_left = own(s, left, t - (n - 2), t)
            if came[s][0] is not None:
                to_right = jnp.where(owner_of(right) < me, came[s][0], to_right)
                to_left = jnp.where(owner_of(left) > me, came[s][1], to_left)
            live = [z for z in range(n - 1) if 0 <= t - z < total]
            from_left = lax.ppermute(to_right, axis, [(z, z + 1) for z in live])
            from_right = lax.ppermute(to_left, axis, [(n - 1 - z, n - 2 - z) for z in live])
            came[s] = [from_left, from_right]
            sent = [to_right, to_left]
            at_left, at_right = t - (me - 1), t - (n - 2 - me)
            first, last = max(t - (n - 2), 0), min(t, total - 1)
            for k in range(first // per, last // per + 1):
                behind = owners[k] < me
                c = jnp.where(behind, at_left, at_right)
                kept = jnp.clip(c, k * per, (k + 1) * per - 1)
                valid = (owners[k] != me) & (c == kept)
                at = place(s, kept, k)
                old = lax.dynamic_slice(outs[k], (at, 0), (size, cols))
                new = jnp.where(valid, jnp.where(behind, from_left, from_right), old)
                outs[k] = lax.dynamic_update_slice(outs[k], new, (at, 0))
    return outs


def shards(n_dp, acts, grads, basis_in_held, basis_out_held, owners, eig_lambda):
    column = lax.axis_index("tensor")
    all_acts = lax.all_gather(acts[0], "tensor", axis=1, tiled=True)
    all_grads = lax.all_gather(grads[0], "tensor", axis=1, tiled=True)
    basis_in, basis_out = chain_broadcast(
        [basis_in_held[0], basis_out_held[0]], [owners[0, column], owners[1, column]], "dp", n_dp
    )
    tokens = acts.shape[1]
    rot_in = jnp.dot(all_acts, basis_in, preferred_element_type=jnp.float32).astype(jnp.bfloat16)
    all_rot_in = lax.all_gather(rot_in, "tensor", axis=1, tiled=True)
    rot_out = jnp.dot(all_grads, basis_out, preferred_element_type=jnp.float32).astype(jnp.bfloat16)
    denom = eig_lambda.astype(jnp.float32) + damping
    contract = (((0,), (0,)), ((), ()))
    product = lax.dot_general(rot_out, all_rot_in, contract, preferred_element_type=jnp.float32) / tokens
    return (product / denom).astype(jnp.bfloat16)[None]


def solution(mesh):
    placed = (
        P("dp", None, "tensor"),
        P("dp", None, "tensor"),
        P("dp", None, "tensor"),
        P("dp", None, "tensor"),
        P(),
        P("tensor", None),
    )

    def step(*args):
        return shards(mesh.shape["dp"], *args)

    return jax.shard_map(step, mesh=mesh, in_specs=placed, out_specs=P("dp", "tensor", None), check_vma=False)
```

time: 373 us -> 411 us (1.10)
  waiting for transfers between devices: 331 us -> 11.8 us
  starting transfers between devices: 0.12 us -> 201 us
  other arithmetic: 3.88 us -> 102 us
  between operations: 15.9 us -> 59.5 us
  local copies, waits for them, and re-layouts: 1.41 us -> 11.9 us
    psum x1 -> x0, waiting for transfers between devices: 260 us -> none  [from_root(): return lax.psum(block, axis)]
    ppermute x0 -> x72, starting transfers between devices: none -> 201 us  [the longest x36 116 us: chain_broadcast(): from_left = lax.ppermute(to_right, axis, [(z, z + 1) for z in live])]
    all_gather x3, waiting for transfers between devices: 69.9 us -> 4.7 us  [the longest x1 4.7 us: shards(): all_rot_in = lax.all_gather(rot_in, 'tensor', axis=1, tiled=True)]
    dynamic_update_slice x0 -> x34, other arithmetic: none -> 61.8 us  [chain_broadcast(): outs[k] = lax.dynamic_update_slice(outs[k], new, (at, 0))]
    select_n x1 -> x34, other arithmetic: 3.88 us -> 40.7 us  [chain_broadcast(): to_left = jnp.where(owner_of(left) > me, came[s][1], to_left)]
    unnamed x0 -> x64, local copies, waits for them, and re-layouts: none -> 9.13 us
    ppermute x0 -> x72, waiting for transfers between devices: none -> 6.34 us  [the longest x36 6.24 us: chain_broadcast(): lax.ppermute(to_left, axis, [(n - 1 - z, n - 2 - z) for z in live])]
  transfers between devices with their start and end apart: 4 -> 75, of which waited for: 3 -> 6; matrix products, arithmetic and copies ran while one was open for 3% -> 30% of each run, Pallas kernels for 0% -> 0%
where the time goes in v1:
time: 411 us; the launch traced here: 406 us
  starting transfers between devices  201 us (49%)
  other arithmetic  102 us (25%)
  between operations  59.5 us (14%)
  matrix products  19.1 us (5%)
  local copies, waits for them, and re-layouts  11.9 us (3%)
  waiting for transfers between devices  11.8 us (3%)
    ppermute x36, starting transfers between devices, chain_broadcast(): from_left = lax.ppermute(to_right, axis, [(z, z + 1) for z in live])  116 us
    ppermute x36, starting transfers between devices, chain_broadcast(): lax.ppermute(to_left, axis, [(n - 1 - z, n - 2 - z) for z in live])  85.1 us
    dynamic_update_slice x34, other arithmetic, chain_broadcast(): outs[k] = lax.dynamic_update_slice(outs[k], new, (at, 0))  61.8 us
    select_n x34, other arithmetic, chain_broadcast(): to_left = jnp.where(owner_of(left) > me, came[s][1], to_left)  40.7 us
    dot_general x1, matrix products, shards(): lax.dot_general(rot_out, all_rot_in, contract, preferred_element_type=jnp...  12.5 us
    unnamed x64, local copies, waits for them, and re-layouts  9.13 us
  transfers between devices with their start and end apart: 75, of which 6 were waited for; matrix products, arithmetic and copies ran while one was open for 30% of the time, Pallas kernels for 0%

profile of v1, /device:TPU:16, one launch (start us, length us, event | category | flops | bytes accessed | tf_op | source)
XLA Modules:
  0.0 405.9 jit_solution(2466082683410458132)
XLA Ops:
  16.6 3.9 collective-permute-done.1
  23.0 4.6 %collective-permute-start.3 = (bf16[256,512]{1,0:T(8,128)(2,1)S(1)}, bf16[256,512]{1,0:T(8,128)(2,1)S(1)}, u32[]{:S(2)}, u32[]{:S(2)}) collective-permute-start(bf16[256,512]{1,0:T(8,128)(2,1)S(1)} %get-tuple-element.209), channel_id=1, source_target_pairs={{24,16},{16,8},{25,17},{17,9},{26,18},{18,10},{27,19},{19,11},{28,... | collective-permute-start | bytes 786440 | tf_op jit(solution)/shard_map/ppermute | solution.py:52
  30.1 4.6 %collective-permute-start.9 = (bf16[256,512]{1,0:T(8,128)(2,1)S(1)}, bf16[256,512]{1,0:T(8,128)(2,1)S(1)}, u32[]{:S(2)}, u32[]{:S(2)}) collective-permute-start(bf16[256,512]{1,0:T(8,128)(2,1)S(1)} %get-tuple-element.207), channel_id=1, source_target_pairs={{24,16},{16,8},{25,17},{17,9},{26,18},{18,10},{27,19},{19,11},{28,... | collective-permute-start | bytes 786440 | tf_op jit(solution)/shard_map/ppermute | solution.py:52
  40.9 3.9 collective-permute-start.7
  48.8 3.9 collective-permute-start.13
  59.1 3.9 collective-permute-start.11
  83.3 4.0 collective-permute-start.20
  93.8 4.6 %collective-permute-start.18 = (bf16[256,512]{1,0:T(8,128)(2,1)}, bf16[256,512]{1,0:T(8,128)(2,1)}, u32[]{:S(2)}, u32[]{:S(2)}) collective-permute-start(bf16[256,512]{1,0:T(8,128)(2,1)} %get-tuple-element.194), channel_id=1, source_target_pairs={{0,8},{8,16},{16,24},{1,9},{9,17},{17,25},{2,10},{10,18},{18,26},{... | collective-permute-start | bytes 786440 | tf_op jit(solution)/shard_map/ppermute | solution.py:51
  102.4 4.6 %collective-permute-start.24 = (bf16[256,512]{1,0:T(8,128)(2,1)}, bf16[256,512]{1,0:T(8,128)(2,1)}, u32[]{:S(2)}, u32[]{:S(2)}) collective-permute-start(bf16[256,512]{1,0:T(8,128)(2,1)} %get-tuple-element.192), channel_id=1, source_target_pairs={{0,8},{8,16},{16,24},{1,9},{9,17},{17,25},{2,10},{10,18},{18,26},{... | collective-permute-start | bytes 786440 | tf_op jit(solution)/shard_map/ppermute | solution.py:51
  113.5 4.6 %collective-permute-start.22 = (bf16[256,512]{1,0:T(8,128)(2,1)}, bf16[256,512]{1,0:T(8,128)(2,1)}, u32[]{:S(2)}, u32[]{:S(2)}) collective-permute-start(bf16[256,512]{1,0:T(8,128)(2,1)} %get-tuple-element.190), channel_id=1, source_target_pairs={{0,8},{8,16},{16,24},{1,9},{9,17},{17,25},{2,10},{10,18},{18,26},{... | collective-permute-start | bytes 786440 | tf_op jit(solution)/shard_map/ppermute | solution.py:51
  122.1 4.6 %collective-permute-start.28 = (bf16[256,512]{1,0:T(8,128)(2,1)}, bf16[256,512]{1,0:T(8,128)(2,1)}, u32[]{:S(2)}, u32[]{:S(2)}) collective-permute-start(bf16[256,512]{1,0:T(8,128)(2,1)} %get-tuple-element.188), channel_id=1, source_target_pairs={{0,8},{8,16},{16,24},{1,9},{9,17},{17,25},{2,10},{10,18},{18,26},{... | collective-permute-start | bytes 786440 | tf_op jit(solution)/shard_map/ppermute | solution.py:51
  134.5 4.6 %collective-permute-start.26 = (bf16[256,512]{1,0:T(8,128)(2,1)}, bf16[256,512]{1,0:T(8,128)(2,1)}, u32[]{:S(2)}, u32[]{:S(2)}) collective-permute-start(bf16[256,512]{1,0:T(8,128)(2,1)} %get-tuple-element.186), channel_id=1, source_target_pairs={{0,8},{8,16},{16,24},{1,9},{9,17},{17,25},{2,10},{10,18},{18,26},{... | collective-permute-start | bytes 786440 | tf_op jit(solution)/shard_map/ppermute | solution.py:51
  143.1 4.6 %collective-permute-start.32 = (bf16[256,512]{1,0:T(8,128)(2,1)}, bf16[256,512]{1,0:T(8,128)(2,1)}, u32[]{:S(2)}, u32[]{:S(2)}) collective-permute-start(bf16[256,512]{1,0:T(8,128)(2,1)} %get-tuple-element.184), channel_id=1, source_target_pairs={{0,8},{8,16},{16,24},{1,9},{9,17},{17,25},{2,10},{10,18},{18,26},{... | collective-permute-start | bytes 786440 | tf_op jit(solution)/shard_map/ppermute | solution.py:51
  154.9 4.2 %collective-permute-start.30 = (bf16[256,512]{1,0:T(8,128)(2,1)}, bf16[256,512]{1,0:T(8,128)(2,1)}, u32[]{:S(2)}, u32[]{:S(2)}) collective-permute-start(bf16[256,512]{1,0:T(8,128)(2,1)} %get-tuple-element.148), channel_id=1, source_target_pairs={{0,8},{8,16},{16,24},{1,9},{9,17},{17,25},{2,10},{10,18},{18,26},{... | collective-permute-start | bytes 786440 | tf_op jit(solution)/shard_map/ppermute | solution.py:51
  163.4 4.5 %collective-permute-start.34 = (bf16[256,512]{1,0:T(8,128)(2,1)}, bf16[256,512]{1,0:T(8,128)(2,1)}, u32[]{:S(2)}, u32[]{:S(2)}) collective-permute-start(bf16[256,512]{1,0:T(8,128)(2,1)} %get-tuple-element.146), channel_id=1, source_target_pairs={{0,8},{8,16},{16,24},{1,9},{9,17},{17,25},{2,10},{10,18},{18,26},{... | collective-permute-start | bytes 786440 | tf_op jit(solution)/shard_map/ppermute | solution.py:51
  173.7 4.5 %copy.7 = bf16[4096,512]{1,0:T(8,128)(2,1)} copy(bf16[4096,512]{1,0:T(8,128)(2,1)} %bitcast.177) | data formatting | bytes 8388608
  198.0 4.5 %copy.23 = bf16[4096,512]{1,0:T(8,128)(2,1)} copy(bf16[4096,512]{1,0:T(8,128)(2,1)} %bitcast.178) | data formatting | bytes 8388608
  204.1 4.6 %collective-permute-start.36 = (bf16[256,512]{1,0:T(8,128)(2,1)S(1)}, bf16[256,512]{1,0:T(8,128)(2,1)S(1)}, u32[]{:S(2)}, u32[]{:S(2)}) collective-permute-start(bf16[256,512]{1,0:T(8,128)(2,1)S(1)} %get-tuple-element.144), channel_id=1, source_target_pairs={{0,8},{8,16},{16,24},{1,9},{9,17},{17,25},{2,10},{10,18},{18,26},{... | collective-permute-start | bytes 786440 | tf_op jit(solution)/shard_map/ppermute | solution.py:51
  213.0 3.9 collective-permute-start.38
  233.4 3.9 collective-permute-start.40
  239.4 3.9 collective-permute-start.42
  247.4 3.8 collective-permute-start.44
  253.4 3.8 collective-permute-start.46
  261.3 3.8 collective-permute-start.48
  267.5 3.9 collective-permute-start.50
  275.3 3.9 collective-permute-start.52
  281.4 3.9 collective-permute-start.54
  295.5 3.7 collective-permute-start.58
  326.2 3.9 collective-permute-start.67
  342.5 6.6 %fusion.13 = bf16[512,512]{0,1:T(8,128)(2,1)} fusion(bf16[4096,512]{1,0:T(8,128)(2,1)} %get-tuple-element.217, bf16[1,512,4096]{2,1,0:T(8,128)(2,1)} %all-gather.10.cloned.1.call-done), kind=kOutput, calls=%fused_computation.8 | convolution fusion | flops 2147745792 | bytes 8912896 | tf_op jit(solution)/shard_map/dot_general | solution.py:77
  382.2 4.7 %all-gather.6.cloned.1.call-done = bf16[512,4096]{0,1:T(8,128)(2,1)} async-done(((bf16[512,512]{0,1:T(8,128)(2,1)}), bf16[512,4096]{0,1:T(8,128)(2,1)}) %all-gather.6.cloned.1.call-update) | async-done | bytes 4194320 | tf_op jit(solution)/shard_map/all_gather | solution.py:78
  386.9 12.5 %fusion = bf16[1,512,4096]{2,1,0:T(8,128)(2,1)} fusion(bf16[512,4096]{1,0:T(8,128)(2,1)} %param.11, bf16[512,4096]{0,1:T(8,128)(2,1)} %all-gather.6.cloned.1.call-done, bf16[4096,512]{1,0:T(8,128)(2,1)} %select_dynamic-update-slice_fusion.19, bf16[1,512,4096]{2,1,0:T(8,128)(2,1)} %all-gather.8.cloned.1.call-done), kind=kOutput, calls=%fused_computation.1 | convolution fusion | flops 4305715200 | bytes 20971520 | tf_op jit(solution)/shard_map/dot_general | solution.py:82
  (257 shorter events, 201.5 us)
Async XLA Ops:
  6.5 336.0 %all-gather.10.cloned.1.call-start = ((), (), s32[]{:S(2)}) async-start(), calls=%async_computation.2 | async-start | bytes 4718592 | tf_op jit(solution)/shard_map/all_gather | solution.py:71
  7.3 375.0 %all-gather.8.cloned.1.call-start = ((), (), s32[]{:S(2)}) async-start(), calls=%async_computation.1 | async-start | bytes 4718592 | tf_op jit(solution)/shard_map/all_gather | solution.py:72
  10.7 16.9 %collective-permute-start.4 = (bf16[256,512]{1,0:T(8,128)(2,1)S(1)}, bf16[256,512]{1,0:T(8,128)(2,1)S(1)}, u32[]{:S(2)}, u32[]{:S(2)}) collective-permute-start(bf16[256,512]{1,0:T(8,128)(2,1)S(1)} %get-tuple-element.212), channel_id=1, source_target_pairs={{0,8},{1,9},{2,10},{3,11},{4,12},{5,13},{6,14},{7,15}} | collective-permute-start | bytes 786440 | tf_op jit(solution)/shard_map/ppermute | solution.py:51
  11.4 16.2 %collective-permute-start.5 = (bf16[256,512]{1,0:T(8,128)(2,1)S(1)}, bf16[256,512]{1,0:T(8,128)(2,1)S(1)}, u32[]{:S(2)}, u32[]{:S(2)}) collective-permute-start(bf16[256,512]{1,0:T(8,128)(2,1)S(1)} %get-tuple-element.211), channel_id=1, source_target_pairs={{24,16},{25,17},{26,18},{27,19},{28,20},{29,21},{30,22},{31,23}} | collective-permute-start | bytes 786440 | tf_op jit(solution)/shard_map/ppermute | solution.py:52
  21.7 15.4 %collective-permute-start.2 = (bf16[256,512]{1,0:T(8,128)(2,1)S(1)}, bf16[256,512]{1,0:T(8,128)(2,1)S(1)}, u32[]{:S(2)}, u32[]{:S(2)}) collective-permute-start(bf16[256,512]{1,0:T(8,128)(2,1)S(1)} %get-tuple-element.210), channel_id=1, source_target_pairs={{0,8},{8,16},{1,9},{9,17},{2,10},{10,18},{3,11},{11,19},{4,12},{12... | collective-permute-start | bytes 786440 | tf_op jit(solution)/shard_map/ppermute | solution.py:51
  28.8 16.1 %collective-permute-start.8 = (bf16[256,512]{1,0:T(8,128)(2,1)S(1)}, bf16[256,512]{1,0:T(8,128)(2,1)S(1)}, u32[]{:S(2)}, u32[]{:S(2)}) collective-permute-start(bf16[256,512]{1,0:T(8,128)(2,1)S(1)} %get-tuple-element.208), channel_id=1, source_target_pairs={{0,8},{8,16},{1,9},{9,17},{2,10},{10,18},{3,11},{11,19},{4,12},{12... | collective-permute-start | bytes 786440 | tf_op jit(solution)/shard_map/ppermute | solution.py:51
  30.1 14.8 %collective-permute-start.9 = (bf16[256,512]{1,0:T(8,128)(2,1)S(1)}, bf16[256,512]{1,0:T(8,128)(2,1)S(1)}, u32[]{:S(2)}, u32[]{:S(2)}) collective-permute-start(bf16[256,512]{1,0:T(8,128)(2,1)S(1)} %get-tuple-element.207), channel_id=1, source_target_pairs={{24,16},{16,8},{25,17},{17,9},{26,18},{18,10},{27,19},{19,11},{28,... | collective-permute-start | bytes 786440 | tf_op jit(solution)/shard_map/ppermute | solution.py:52
  39.0 16.2 %collective-permute-start.6 = (bf16[256,512]{1,0:T(8,128)(2,1)}, bf16[256,512]{1,0:T(8,128)(2,1)S(1)}, u32[]{:S(2)}, u32[]{:S(2)}) collective-permute-start(bf16[256,512]{1,0:T(8,128)(2,1)} %get-tuple-element.206), channel_id=1, source_target_pairs={{0,8},{8,16},{16,24},{1,9},{9,17},{17,25},{2,10},{10,18},{18,26},{... | collective-permute-start | bytes 786440 | tf_op jit(solution)/shard_map/ppermute | solution.py:51
  46.9 16.2 %collective-permute-start.12 = (bf16[256,512]{1,0:T(8,128)(2,1)}, bf16[256,512]{1,0:T(8,128)(2,1)S(1)}, u32[]{:S(2)}, u32[]{:S(2)}) collective-permute-start(bf16[256,512]{1,0:T(8,128)(2,1)} %get-tuple-element.204), channel_id=1, source_target_pairs={{0,8},{8,16},{16,24},{1,9},{9,17},{17,25},{2,10},{10,18},{18,26},{... | collective-permute-start | bytes 786440 | tf_op jit(solution)/shard_map/ppermute | solution.py:51
  57.2 16.2 %collective-permute-start.10 = (bf16[256,512]{1,0:T(8,128)(2,1)}, bf16[256,512]{1,0:T(8,128)(2,1)S(1)}, u32[]{:S(2)}, u32[]{:S(2)}) collective-permute-start(bf16[256,512]{1,0:T(8,128)(2,1)} %get-tuple-element.202), channel_id=1, source_target_pairs={{0,8},{8,16},{16,24},{1,9},{9,17},{17,25},{2,10},{10,18},{18,26},{... | collective-permute-start | bytes 786440 | tf_op jit(solution)/shard_map/ppermute | solution.py:51
  65.0 16.2 %collective-permute-start.16 = (bf16[256,512]{1,0:T(8,128)(2,1)}, bf16[256,512]{1,0:T(8,128)(2,1)}, u32[]{:S(2)}, u32[]{:S(2)}) collective-permute-start(bf16[256,512]{1,0:T(8,128)(2,1)} %get-tuple-element.200), channel_id=1, source_target_pairs={{0,8},{8,16},{16,24},{1,9},{9,17},{17,25},{2,10},{10,18},{18,26},{... | collective-permute-start | bytes 786440 | tf_op jit(solution)/shard_map/ppermute | solution.py:51
  75.4 16.3 %collective-permute-start.14 = (bf16[256,512]{1,0:T(8,128)(2,1)}, bf16[256,512]{1,0:T(8,128)(2,1)}, u32[]{:S(2)}, u32[]{:S(2)}) collective-permute-start(bf16[256,512]{1,0:T(8,128)(2,1)} %get-tuple-element.198), channel_id=1, source_target_pairs={{0,8},{8,16},{16,24},{1,9},{9,17},{17,25},{2,10},{10,18},{18,26},{... | collective-permute-start | bytes 786440 | tf_op jit(solution)/shard_map/ppermute | solution.py:51
  83.3 17.0 %collective-permute-start.20 = (bf16[256,512]{1,0:T(8,128)(2,1)}, bf16[256,512]{1,0:T(8,128)(2,1)}, u32[]{:S(2)}, u32[]{:S(2)}) collective-permute-start(bf16[256,512]{1,0:T(8,128)(2,1)} %get-tuple-element.196), channel_id=1, source_target_pairs={{0,8},{8,16},{16,24},{1,9},{9,17},{17,25},{2,10},{10,18},{18,26},{... | collective-permute-start | bytes 786440 | tf_op jit(solution)/shard_map/ppermute | solution.py:51
  93.8 17.6 %collective-permute-start.18 = (bf16[256,512]{1,0:T(8,128)(2,1)}, bf16[256,512]{1,0:T(8,128)(2,1)}, u32[]{:S(2)}, u32[]{:S(2)}) collective-permute-start(bf16[256,512]{1,0:T(8,128)(2,1)} %get-tuple-element.194), channel_id=1, source_target_pairs={{0,8},{8,16},{16,24},{1,9},{9,17},{17,25},{2,10},{10,18},{18,26},{... | collective-permute-start | bytes 786440 | tf_op jit(solution)/shard_map/ppermute | solution.py:51
  102.4 17.6 %collective-permute-start.24 = (bf16[256,512]{1,0:T(8,128)(2,1)}, bf16[256,512]{1,0:T(8,128)(2,1)}, u32[]{:S(2)}, u32[]{:S(2)}) collective-permute-start(bf16[256,512]{1,0:T(8,128)(2,1)} %get-tuple-element.192), channel_id=1, source_target_pairs={{0,8},{8,16},{16,24},{1,9},{9,17},{17,25},{2,10},{10,18},{18,26},{... | collective-permute-start | bytes 786440 | tf_op jit(solution)/shard_map/ppermute | solution.py:51
  113.5 19.0 %collective-permute-start.22 = (bf16[256,512]{1,0:T(8,128)(2,1)}, bf16[256,512]{1,0:T(8,128)(2,1)}, u32[]{:S(2)}, u32[]{:S(2)}) collective-permute-start(bf16[256,512]{1,0:T(8,128)(2,1)} %get-tuple-element.190), channel_id=1, source_target_pairs={{0,8},{8,16},{16,24},{1,9},{9,17},{17,25},{2,10},{10,18},{18,26},{... | collective-permute-start | bytes 786440 | tf_op jit(solution)/shard_map/ppermute | solution.py:51
  122.1 19.0 %collective-permute-start.28 = (bf16[256,512]{1,0:T(8,128)(2,1)}, bf16[256,512]{1,0:T(8,128)(2,1)}, u32[]{:S(2)}, u32[]{:S(2)}) collective-permute-start(bf16[256,512]{1,0:T(8,128)(2,1)} %get-tuple-element.188), channel_id=1, source_target_pairs={{0,8},{8,16},{16,24},{1,9},{9,17},{17,25},{2,10},{10,18},{18,26},{... | collective-permute-start | bytes 786440 | tf_op jit(solution)/shard_map/ppermute | solution.py:51
  128.6 258.3 %all-gather.6.cloned.1.call-start = ((), (), s32[]{:S(2)}) async-start(), calls=%async_computation | async-start | bytes 4718592 | tf_op jit(solution)/shard_map/all_gather | solution.py:78
  134.5 17.7 %collective-permute-start.26 = (bf16[256,512]{1,0:T(8,128)(2,1)}, bf16[256,512]{1,0:T(8,128)(2,1)}, u32[]{:S(2)}, u32[]{:S(2)}) collective-permute-start(bf16[256,512]{1,0:T(8,128)(2,1)} %get-tuple-element.186), channel_id=1, source_target_pairs={{0,8},{8,16},{16,24},{1,9},{9,17},{17,25},{2,10},{10,18},{18,26},{... | collective-permute-start | bytes 786440 | tf_op jit(solution)/shard_map/ppermute | solution.py:51
  143.1 17.9 %collective-permute-start.32 = (bf16[256,512]{1,0:T(8,128)(2,1)}, bf16[256,512]{1,0:T(8,128)(2,1)}, u32[]{:S(2)}, u32[]{:S(2)}) collective-permute-start(bf16[256,512]{1,0:T(8,128)(2,1)} %get-tuple-element.184), channel_id=1, source_target_pairs={{0,8},{8,16},{16,24},{1,9},{9,17},{17,25},{2,10},{10,18},{18,26},{... | collective-permute-start | bytes 786440 | tf_op jit(solution)/shard_map/ppermute | solution.py:51
  154.9 47.6 %collective-permute-start.30 = (bf16[256,512]{1,0:T(8,128)(2,1)}, bf16[256,512]{1,0:T(8,128)(2,1)}, u32[]{:S(2)}, u32[]{:S(2)}) collective-permute-start(bf16[256,512]{1,0:T(8,128)(2,1)} %get-tuple-element.148), channel_id=1, source_target_pairs={{0,8},{8,16},{16,24},{1,9},{9,17},{17,25},{2,10},{10,18},{18,26},{... | collective-permute-start | bytes 786440 | tf_op jit(solution)/shard_map/ppermute | solution.py:51
  159.2 43.4 %collective-permute-start.31 = (bf16[256,512]{1,0:T(8,128)(2,1)}, bf16[256,512]{1,0:T(8,128)(2,1)}, u32[]{:S(2)}, u32[]{:S(2)}) collective-permute-start(bf16[256,512]{1,0:T(8,128)(2,1)} %get-tuple-element.147), channel_id=1, source_target_pairs={{24,16},{16,8},{8,0},{25,17},{17,9},{9,1},{26,18},{18,10},{10,2},{... | collective-permute-start | bytes 786440 | tf_op jit(solution)/shard_map/ppermute | solution.py:52
  163.4 47.2 %collective-permute-start.34 = (bf16[256,512]{1,0:T(8,128)(2,1)}, bf16[256,512]{1,0:T(8,128)(2,1)}, u32[]{:S(2)}, u32[]{:S(2)}) collective-permute-start(bf16[256,512]{1,0:T(8,128)(2,1)} %get-tuple-element.146), channel_id=1, source_target_pairs={{0,8},{8,16},{16,24},{1,9},{9,17},{17,25},{2,10},{10,18},{18,26},{... | collective-permute-start | bytes 786440 | tf_op jit(solution)/shard_map/ppermute | solution.py:51
  168.0 42.6 %collective-permute-start.35 = (bf16[256,512]{1,0:T(8,128)(2,1)}, bf16[256,512]{1,0:T(8,128)(2,1)}, u32[]{:S(2)}, u32[]{:S(2)}) collective-permute-start(bf16[256,512]{1,0:T(8,128)(2,1)} %get-tuple-element.145), channel_id=1, source_target_pairs={{24,16},{16,8},{8,0},{25,17},{17,9},{9,1},{26,18},{18,10},{10,2},{... | collective-permute-start | bytes 786440 | tf_op jit(solution)/shard_map/ppermute | solution.py:52
  204.1 29.1 %collective-permute-start.36 = (bf16[256,512]{1,0:T(8,128)(2,1)S(1)}, bf16[256,512]{1,0:T(8,128)(2,1)S(1)}, u32[]{:S(2)}, u32[]{:S(2)}) collective-permute-start(bf16[256,512]{1,0:T(8,128)(2,1)S(1)} %get-tuple-element.144), channel_id=1, source_target_pairs={{0,8},{8,16},{16,24},{1,9},{9,17},{17,25},{2,10},{10,18},{18,26},{... | collective-permute-start | bytes 786440 | tf_op jit(solution)/shard_map/ppermute | solution.py:51
  208.7 24.5 %collective-permute-start.37 = (bf16[256,512]{1,0:T(8,128)(2,1)S(1)}, bf16[256,512]{1,0:T(8,128)(2,1)S(1)}, u32[]{:S(2)}, u32[]{:S(2)}) collective-permute-start(bf16[256,512]{1,0:T(8,128)(2,1)S(1)} %get-tuple-element.143), channel_id=1, source_target_pairs={{24,16},{16,8},{8,0},{25,17},{17,9},{9,1},{26,18},{18,10},{10,2},{... | collective-permute-start | bytes 786440 | tf_op jit(solution)/shard_map/ppermute | solution.py:52
  213.0 26.2 %collective-permute-start.38 = (bf16[256,512]{1,0:T(8,128)(2,1)S(1)}, bf16[256,512]{1,0:T(8,128)(2,1)S(1)}, u32[]{:S(2)}, u32[]{:S(2)}) collective-permute-start(bf16[256,512]{1,0:T(8,128)(2,1)S(1)} %get-tuple-element.142), channel_id=1, source_target_pairs={{0,8},{8,16},{16,24},{1,9},{9,17},{17,25},{2,10},{10,18},{18,26},{... | collective-permute-start | bytes 786440 | tf_op jit(solution)/shard_map/ppermute | solution.py:51
  216.9 22.3 %collective-permute-start.39 = (bf16[256,512]{1,0:T(8,128)(2,1)S(1)}, bf16[256,512]{1,0:T(8,128)(2,1)S(1)}, u32[]{:S(2)}, u32[]{:S(2)}) collective-permute-start(bf16[256,512]{1,0:T(8,128)(2,1)S(1)} %get-tuple-element.141), channel_id=1, source_target_pairs={{24,16},{16,8},{8,0},{25,17},{17,9},{9,1},{26,18},{18,10},{10,2},{... | collective-permute-start | bytes 786440 | tf_op jit(solution)/shard_map/ppermute | solution.py:52
  349.3 29.4 %collective-permute-start.68 = (bf16[256,512]{1,0:T(8,128)(2,1)}, bf16[256,512]{1,0:T(8,128)(2,1)S(1)}, u32[]{:S(2)}, u32[]{:S(2)}) collective-permute-start(bf16[256,512]{1,0:T(8,128)(2,1)} %get-tuple-element.153), channel_id=1, source_target_pairs={{16,24},{17,25},{18,26},{19,27},{20,28},{21,29},{22,30},{23,31}} | collective-permute-start | bytes 786440 | tf_op jit(solution)/shard_map/ppermute | solution.py:51
  350.7 28.0 %collective-permute-start.69 = (bf16[256,512]{1,0:T(8,128)(2,1)}, bf16[256,512]{1,0:T(8,128)(2,1)S(1)}, u32[]{:S(2)}, u32[]{:S(2)}) collective-permute-start(bf16[256,512]{1,0:T(8,128)(2,1)} %get-tuple-element.152), channel_id=1, source_target_pairs={{8,0},{9,1},{10,2},{11,3},{12,4},{13,5},{14,6},{15,7}} | collective-permute-start | bytes 786440 | tf_op jit(solution)/shard_map/ppermute | solution.py:52
  351.4 29.0 %collective-permute-start.70 = (bf16[256,512]{1,0:T(8,128)(2,1)}, bf16[256,512]{1,0:T(8,128)(2,1)S(1)}, u32[]{:S(2)}, u32[]{:S(2)}) collective-permute-start(bf16[256,512]{1,0:T(8,128)(2,1)} %get-tuple-element.151), channel_id=1, source_target_pairs={{16,24},{17,25},{18,26},{19,27},{20,28},{21,29},{22,30},{23,31}} | collective-permute-start | bytes 786440 | tf_op jit(solution)/shard_map/ppermute | solution.py:51
  352.7 27.7 %collective-permute-start.71 = (bf16[256,512]{1,0:T(8,128)(2,1)}, bf16[256,512]{1,0:T(8,128)(2,1)S(1)}, u32[]{:S(2)}, u32[]{:S(2)}) collective-permute-start(bf16[256,512]{1,0:T(8,128)(2,1)} %get-tuple-element.149), channel_id=1, source_target_pairs={{8,0},{9,1},{10,2},{11,3},{12,4},{13,5},{14,6},{15,7}} | collective-permute-start | bytes 786440 | tf_op jit(solution)/shard_map/ppermute | solution.py:52
  (74 other events, 1048.4 us)
Sparse Core Ops, SparseCore 0:
  9.2 38.4 all-gather.9
  128.8 39.7 all-gather.7
  349.3 37.5 all-gather.5

commit v2 on v0

v2 whole, which is shorter than its diff:
```python
import jax
import jax.numpy as jnp
from jax import lax
from jax.sharding import PartitionSpec as P

damping = 0.01
PARTS = 2


def from_owner(held, owner, n):
    rows = held.shape[0] // PARTS
    mine = lax.axis_index("dp") == owner
    out = []
    for part in range(PARTS):
        block = held[part * rows : (part + 1) * rows]
        block = jnp.where(mine, block, jnp.zeros_like(block))
        share = lax.psum_scatter(block, "dp", scatter_dimension=0, tiled=True)
        out.append(lax.all_gather(share, "dp", axis=0, tiled=True))
    return out


def rotate(rows, basis_parts):
    depth = basis_parts[0].shape[0]
    total = None
    for part, block in enumerate(basis_parts):
        term = jnp.dot(rows[:, part * depth : (part + 1) * depth], block, preferred_element_type=jnp.float32)
        total = term if total is None else total + term
    return total.astype(jnp.bfloat16)


def shards(n_dp, acts, grads, basis_in_held, basis_out_held, owners, eig_lambda):
    column = lax.axis_index("tensor")
    all_acts = lax.all_gather(acts[0], "tensor", axis=1, tiled=True)
    all_grads = lax.all_gather(grads[0], "tensor", axis=1, tiled=True)
    basis_in = from_owner(basis_in_held[0], owners[0, column], n_dp)
    basis_out = from_owner(basis_out_held[0], owners[1, column], n_dp)
    tokens = acts.shape[1]
    rot_in = rotate(all_acts, basis_in)
    all_rot_in = lax.all_gather(rot_in, "tensor", axis=1, tiled=True)
    rot_out = rotate(all_grads, basis_out)
    denom = eig_lambda.astype(jnp.float32) + damping
    contract = (((0,), (0,)), ((), ()))
    product = lax.dot_general(rot_out, all_rot_in, contract, preferred_element_type=jnp.float32) / tokens
    return (product / denom).astype(jnp.bfloat16)[None]


def solution(mesh):
    placed = (
        P("dp", None, "tensor"),
        P("dp", None, "tensor"),
        P("dp", None, "tensor"),
        P("dp", None, "tensor"),
        P(),
        P("tensor", None),
    )

    def step(*args):
        return shards(mesh.shape["dp"], *args)

    return jax.shard_map(step, mesh=mesh, in_specs=placed, out_specs=P("dp", "tensor", None), check_vma=False)
```

time: 373 us -> 514 us (1.38)
  waiting for transfers between devices: 331 us -> 466 us
  other arithmetic: 3.88 us -> 9.13 us
    psum x1 -> x0, waiting for transfers between devices: 260 us -> none  [from_root(): return lax.psum(block, axis)]
    all_gather x3 -> x7, waiting for transfers between devices: 69.9 us -> 290 us  [the longest x4 173 us: from_owner(): out.append(lax.all_gather(share, 'dp', axis=0, tiled=True))]
    reduce_scatter x0 -> x4, waiting for transfers between devices: none -> 173 us  [from_owner(): share = lax.psum_scatter(block, 'dp', scatter_dimension=0, tiled=True)]
    select_n x1 -> x2, other arithmetic: 3.88 us -> 9.13 us  [from_owner(): block = jnp.where(mine, block, jnp.zeros_like(block))]
    dot_general x2 -> x4, matrix products: 19.1 us -> 21 us  [the longest x3 11.3 us: rotate(): jnp.dot(rows[:, part * depth:(part + 1) * depth], block, preferred_elemen...]
  transfers between devices with their start and end apart: 4 -> 11, of which waited for: 3 -> 11; matrix products, arithmetic and copies ran while one was open for 3% -> 3% of each run, Pallas kernels for 0% -> 0%
where the time goes in v2:
time: 514 us; the launch traced here: 512 us
  waiting for transfers between devices  466 us (91%)
  matrix products  21 us (4%)
  between operations  14.6 us (3%)
  other arithmetic  9.13 us (2%)
    all_gather x4, waiting for transfers between devices, from_owner(): out.append(lax.all_gather(share, 'dp', axis=0, tiled=True))  173 us
    reduce_scatter x4, waiting for transfers between devices, from_owner(): share = lax.psum_scatter(block, 'dp', scatter_dimension=0, tiled=True)  173 us
    all_gather x1, waiting for transfers between devices, shards(): all_grads = lax.all_gather(grads[0], 'tensor', axis=1, tiled=True)  39.4 us
    all_gather x1, waiting for transfers between devices, shards(): all_acts = lax.all_gather(acts[0], 'tensor', axis=1, tiled=True)  39.3 us
    all_gather x1, waiting for transfers between devices, shards(): all_rot_in = lax.all_gather(rot_in, 'tensor', axis=1, tiled=True)  38.7 us
    dot_general x3, matrix products, rotate(): jnp.dot(rows[:, part * depth:(part + 1) * depth], block, preferred_elemen...  11.3 us
  transfers between devices with their start and end apart: 11, of which 11 were waited for; matrix products, arithmetic and copies ran while one was open for 3% of the time, Pallas kernels for 0%

profile of v2, /device:TPU:16, one launch (start us, length us, event | category | flops | bytes accessed | tf_op | source)
XLA Modules:
  0.0 512.2 jit_solution(945569871485007756)
XLA Ops:
  6.5 1.4 constant_dynamic-slice_fusion
  8.6 4.5 select_bitcast_fusion.1
  13.2 0.0 reduce-scatter.9.cloned.1.call-start
  13.2 0.7 reduce-scatter.9.cloned.1.call-update
  13.9 0.0 reduce-scatter.7.cloned.1.call-start
  14.6 4.6 select_bitcast_fusion.3
  19.3 0.0 reduce-scatter.5.cloned.1.call-start
  19.3 0.5 reduce-scatter.5.cloned.1.call-update
  19.9 0.0 all-gather.16.cloned.1.call-start
  19.9 37.7 %reduce-scatter.11.cloned.1.call-done = bf16[512,512]{1,0:T(8,128)(2,1)} async-done(((bf16[2048,512]{1,0:T(8,128)(2,1)}), bf16[512,512]{1,0:T(8,128)(2,1)}) %reduce-scatter.11.cloned.1.call-update) | async-done | bytes 524304 | tf_op jit(solution)/shard_map/reduce_scatter | solution.py:17
  57.6 0.0 all-gather.22.cloned.1.call-start
  57.7 0.5 all-gather.22.cloned.1.call-update
  58.2 0.0 all-gather.14.cloned.1.call-start
  58.2 45.0 %reduce-scatter.9.cloned.1.call-done = bf16[512,512]{1,0:T(8,128)(2,1)} async-done(((bf16[2048,512]{1,0:T(8,128)(2,1)}), bf16[512,512]{1,0:T(8,128)(2,1)}) %reduce-scatter.9.cloned.1.call-update) | async-done | bytes 524304 | tf_op jit(solution)/shard_map/reduce_scatter | solution.py:17
  103.2 0.0 all-gather.12.cloned.1.call-start
  103.3 45.4 %reduce-scatter.7.cloned.1.call-done = bf16[512,512]{1,0:T(8,128)(2,1)} async-done(((bf16[2048,512]{1,0:T(8,128)(2,1)}), bf16[512,512]{1,0:T(8,128)(2,1)}) %reduce-scatter.7.cloned.1.call-update) | async-done | bytes 524304 | tf_op jit(solution)/shard_map/reduce_scatter | solution.py:17
  148.7 0.0 all-gather.20.cloned.1.call-start
  148.8 0.7 all-gather.20.cloned.1.call-update
  149.5 0.0 all-gather.10.cloned.1.call-start
  149.5 44.7 %reduce-scatter.5.cloned.1.call-done = bf16[512,512]{1,0:T(8,128)(2,1)} async-done(((bf16[2048,512]{1,0:T(8,128)(2,1)}), bf16[512,512]{1,0:T(8,128)(2,1)}) %reduce-scatter.5.cloned.1.call-update) | async-done | bytes 524304 | tf_op jit(solution)/shard_map/reduce_scatter | solution.py:17
  194.2 0.0 all-gather.18.cloned.1.call-start
  194.2 46.0 %all-gather.16.cloned.1.call-done = bf16[2048,512]{1,0:T(8,128)(2,1)} async-done(((bf16[512,512]{1,0:T(8,128)(2,1)}), bf16[2048,512]{1,0:T(8,128)(2,1)}) %all-gather.16.cloned.1.call-update) | async-done | bytes 2097168 | tf_op jit(solution)/shard_map/all_gather | solution.py:18
  240.2 39.3 %all-gather.22.cloned.1.call-done = bf16[1,512,4096]{2,1,0:T(8,128)(2,1)} async-done(((bf16[1,512,512]{2,1,0:T(8,128)(2,1)}), bf16[1,512,4096]{2,1,0:T(8,128)(2,1)}) %all-gather.22.cloned.1.call-update) | async-done | bytes 4194320 | tf_op jit(solution)/shard_map/all_gather | solution.py:33
  279.5 3.5 fusion.1
  283.0 42.7 %all-gather.14.cloned.1.call-done = bf16[2048,512]{1,0:T(8,128)(2,1)} async-done(((bf16[512,512]{1,0:T(8,128)(2,1)}), bf16[2048,512]{1,0:T(8,128)(2,1)}) %all-gather.14.cloned.1.call-update) | async-done | bytes 2097168 | tf_op jit(solution)/shard_map/all_gather | solution.py:18
  325.6 4.3 fusion.21
  330.0 41.9 %all-gather.12.cloned.1.call-done = bf16[2048,512]{1,0:T(8,128)(2,1)} async-done(((bf16[512,512]{1,0:T(8,128)(2,1)}), bf16[2048,512]{1,0:T(8,128)(2,1)}) %all-gather.12.cloned.1.call-update) | async-done | bytes 2097168 | tf_op jit(solution)/shard_map/all_gather | solution.py:18
  371.9 39.4 %all-gather.20.cloned.1.call-done = bf16[1,512,4096]{2,1,0:T(8,128)(2,1)} async-done(((bf16[1,512,512]{2,1,0:T(8,128)(2,1)}), bf16[1,512,4096]{2,1,0:T(8,128)(2,1)}) %all-gather.20.cloned.1.call-update) | async-done | bytes 4194320 | tf_op jit(solution)/shard_map/all_gather | solution.py:34
  411.3 3.5 fusion.5
  414.8 42.5 %all-gather.10.cloned.1.call-done = bf16[2048,512]{1,0:T(8,128)(2,1)} async-done(((bf16[512,512]{1,0:T(8,128)(2,1)}), bf16[2048,512]{1,0:T(8,128)(2,1)}) %all-gather.10.cloned.1.call-update) | async-done | bytes 2097168 | tf_op jit(solution)/shard_map/all_gather | solution.py:18
  457.4 38.7 %all-gather.18.cloned.1.call-done = bf16[512,4096]{0,1:T(8,128)(2,1)} async-done(((bf16[512,512]{0,1:T(8,128)(2,1)}), bf16[512,4096]{0,1:T(8,128)(2,1)}) %all-gather.18.cloned.1.call-update) | async-done | bytes 4194320 | tf_op jit(solution)/shard_map/all_gather | solution.py:39
  496.1 9.6 %fusion = bf16[1,512,4096]{2,1,0:T(8,128)(2,1)} fusion(bf16[512,4096]{1,0:T(8,128)(2,1)} %param.11, bf16[512,4096]{0,1:T(8,128)(2,1)} %all-gather.18.cloned.1.call-done, f32[512,512]{1,0:T(8,128)S(1)} %fusion.5, bf16[2048,512]{1,0:T(8,128)(2,1)} %all-gather.10.cloned.1.call-done, bf16[512,4096]{1,0:T(8,128)(2,1)} %bitcast.24), kind=kOutput, calls=%fused_computation.1 | convolution fusion | flops 3232235520 | bytes 17825792 | tf_op jit(solution)/shard_map/dot_general | solution.py:43
  (8 shorter events, 0.1 us)
Async XLA Ops:
  6.5 51.1 %reduce-scatter.11.cloned.1.call-start = ((), (), s32[]{:S(2)}) async-start(), calls=%async_computation.10 | async-start | bytes 2621440 | tf_op jit(solution)/shard_map/reduce_scatter | solution.py:17
  13.2 90.0 %reduce-scatter.9.cloned.1.call-start = ((), (), s32[]{:S(2)}) async-start(), calls=%async_computation.8 | async-start | bytes 2621440 | tf_op jit(solution)/shard_map/reduce_scatter | solution.py:17
  13.9 134.8 %reduce-scatter.7.cloned.1.call-start = ((), (), s32[]{:S(2)}) async-start(), calls=%async_computation.6 | async-start | bytes 2621440 | tf_op jit(solution)/shard_map/reduce_scatter | solution.py:17
  19.3 174.9 %reduce-scatter.5.cloned.1.call-start = ((), (), s32[]{:S(2)}) async-start(), calls=%async_computation.4 | async-start | bytes 2621440 | tf_op jit(solution)/shard_map/reduce_scatter | solution.py:17
  19.9 220.3 %all-gather.16.cloned.1.call-start = ((), (), s32[]{:S(2)}) async-start(), calls=%async_computation.11 | async-start | bytes 2621440 | tf_op jit(solution)/shard_map/all_gather | solution.py:18
  57.6 221.9 %all-gather.22.cloned.1.call-start = ((), (), s32[]{:S(2)}) async-start(), calls=%async_computation.14 | async-start | bytes 4718592 | tf_op jit(solution)/shard_map/all_gather | solution.py:33
  58.2 267.5 %all-gather.14.cloned.1.call-start = ((), (), s32[]{:S(2)}) async-start(), calls=%async_computation.9 | async-start | bytes 2621440 | tf_op jit(solution)/shard_map/all_gather | solution.py:18
  103.2 268.7 %all-gather.12.cloned.1.call-start = ((), (), s32[]{:S(2)}) async-start(), calls=%async_computation.7 | async-start | bytes 2621440 | tf_op jit(solution)/shard_map/all_gather | solution.py:18
  148.7 262.6 %all-gather.20.cloned.1.call-start = ((), (), s32[]{:S(2)}) async-start(), calls=%async_computation.13 | async-start | bytes 4718592 | tf_op jit(solution)/shard_map/all_gather | solution.py:34
  149.5 307.9 %all-gather.10.cloned.1.call-start = ((), (), s32[]{:S(2)}) async-start(), calls=%async_computation.5 | async-start | bytes 2621440 | tf_op jit(solution)/shard_map/all_gather | solution.py:18
  194.2 301.9 %all-gather.18.cloned.1.call-start = ((), (), s32[]{:S(2)}) async-start(), calls=%async_computation.12 | async-start | bytes 4718592 | tf_op jit(solution)/shard_map/all_gather | solution.py:39
Sparse Core Ops, SparseCore 0:
  13.3 44.2 reduce-scatter.10
  60.0 43.1 reduce-scatter.8
  105.5 43.1 reduce-scatter.6
  151.0 43.1 reduce-scatter.4
  195.6 44.5 all-gather.15
  241.9 37.5 all-gather.21
  281.0 44.5 all-gather.13
  327.2 44.6 all-gather.11
  373.8 37.5 all-gather.19
  412.7 44.5 all-gather.9
  459.3 36.7 all-gather.17

commit v3 on v2

v3 whole, which is shorter than its diff:
```python
import jax
import jax.numpy as jnp
from jax import lax
from jax.sharding import PartitionSpec as P

damping = 0.01
CHUNKS = 8
SHARE = 2


def summed(held, owner, axis):
    mine = lax.axis_index(axis) == owner
    return lax.psum(jnp.where(mine, held, jnp.zeros_like(held)), axis)


def chain_broadcast(helds, owners, first_row, axis, n):
    me = lax.axis_index(axis)
    rows, cols = helds[0].shape
    size = (rows - first_row) // CHUNKS
    per = CHUNKS
    total = per * len(helds)
    outs = [held[first_row:] for held in helds]

    def own(c, first, last):
        low, high = max(first, 0) // per, min(last, total - 1) // per
        picked = None
        for k in range(low, high + 1):
            at = first_row + jnp.clip(c - k * per, 0, per - 1) * size
            block = lax.dynamic_slice(helds[k], (at, 0), (size, cols))
            picked = block if picked is None else jnp.where(c >= k * per, block, picked)
        return picked

    def owner_of(c):
        owner = owners[0]
        for k in range(1, len(helds)):
            owner = jnp.where(c >= k * per, owners[k], owner)
        return owner

    came = None
    for t in range(total + n - 2):
        right = t - me
        left = t - (n - 1 - me)
        to_right = own(right, t - (n - 2), t)
        to_left = own(left, t - (n - 2), t)
        if came is not None:
            to_right = jnp.where(owner_of(right) < me, came[0], to_right)
            to_left = jnp.where(owner_of(left) > me, came[1], to_left)
        live = [z for z in range(n - 1) if 0 <= t - z < total]
        from_left = lax.ppermute(to_right, axis, [(z, z + 1) for z in live])
        from_right = lax.ppermute(to_left, axis, [(n - 1 - z, n - 2 - z) for z in live])
        came = [from_left, from_right]
        at_left, at_right = t - (me - 1), t - (n - 2 - me)
        first, last = max(t - (n - 2), 0), min(t, total - 1)
        for k in range(first // per, last // per + 1):
            behind = owners[k] < me
            c = jnp.where(behind, at_left, at_right) - k * per
            kept = jnp.clip(c, 0, per - 1)
            valid = (owners[k] != me) & (c == kept)
            at = kept * size
            old = lax.dynamic_slice(outs[k], (at, 0), (size, cols))
            new = jnp.where(valid, jnp.where(behind, from_left, from_right), old)
            outs[k] = lax.dynamic_update_slice(outs[k], new, (at, 0))
    return outs


def rotate(rows, parts):
    total, at = None, 0
    for block in parts:
        term = jnp.dot(rows[:, at : at + block.shape[0]], block, preferred_element_type=jnp.float32)
        total = term if total is None else total + term
        at += block.shape[0]
    return total.astype(jnp.bfloat16)


def shards(n_dp, acts, grads, basis_in_held, basis_out_held, owners, eig_lambda):
    column = lax.axis_index("tensor")
    owner_in, owner_out = owners[0, column], owners[1, column]
    held_in, held_out = basis_in_held[0], basis_out_held[0]
    split = held_in.shape[0] - held_in.shape[0] // SHARE
    all_acts = lax.all_gather(acts[0], "tensor", axis=1, tiled=True)
    all_grads = lax.all_gather(grads[0], "tensor", axis=1, tiled=True)
    top_in = summed(held_in[:split], owner_in, "dp")
    later, _ = lax.optimization_barrier((held_out[:split], top_in))
    top_out = summed(later, owner_out, "dp")
    low_in, low_out = chain_broadcast([held_in, held_out], [owner_in, owner_out], split, "dp", n_dp)
    tokens = acts.shape[1]
    rot_in = rotate(all_acts, [top_in, low_in])
    all_rot_in = lax.all_gather(rot_in, "tensor", axis=1, tiled=True)
    rot_out = rotate(all_grads, [top_out, low_out])
    denom = eig_lambda.astype(jnp.float32) + damping
    contract = (((0,), (0,)), ((), ()))
    product = lax.dot_general(rot_out, all_rot_in, contract, preferred_element_type=jnp.float32) / tokens
    return (product / denom).astype(jnp.bfloat16)[None]


def solution(mesh):
    placed = (
        P("dp", None, "tensor"),
        P("dp", None, "tensor"),
        P("dp", None, "tensor"),
        P("dp", None, "tensor"),
        P(),
        P("tensor", None),
    )

    def step(*args):
        return shards(mesh.shape["dp"], *args)

    return jax.shard_map(step, mesh=mesh, in_specs=placed, out_specs=P("dp", "tensor", None), check_vma=False)
```

time: 514 us -> 406 us (0.79)
  the two profiles are of different devices: /device:TPU:16 before, /device:TPU:28 now
where the time goes in v3:
time: 406 us; the launch traced here: 400 us
  waiting for transfers between devices  186 us (46%)
  starting transfers between devices  86.1 us (21%)
  between operations  62.3 us (15%)
  other arithmetic  39.5 us (10%)
  matrix products  18.4 us (5%)
  local copies, waits for them, and re-layouts  8.38 us (2%)
    psum x2, waiting for transfers between devices, summed(): return lax.psum(jnp.where(mine, held, jnp.zeros_like(held)), axis)  79.3 us
    ppermute x18, starting transfers between devices, chain_broadcast(): lax.ppermute(to_left, axis, [(n - 1 - z, n - 2 - z) for z in live])  64 us
    ppermute x18, waiting for transfers between devices, chain_broadcast(): from_left = lax.ppermute(to_right, axis, [(z, z + 1) for z in live])  58.7 us
    ppermute x18, waiting for transfers between devices, chain_broadcast(): lax.ppermute(to_left, axis, [(n - 1 - z, n - 2 - z) for z in live])  46.5 us
    select_n x17, other arithmetic, chain_broadcast(): to_left = jnp.where(owner_of(left) > me, came[1], to_left)  28.1 us
    ppermute x18, starting transfers between devices, chain_broadcast(): from_left = lax.ppermute(to_right, axis, [(z, z + 1) for z in live])  21.9 us
    dot_general x3, matrix products, rotate(): jnp.dot(rows[:, at:at + block.shape[0]], block, preferred_element_type=jn...  9.42 us
    dot_general x1, matrix products, shards(): lax.dot_general(rot_out, all_rot_in, contract, preferred_element_type=jnp...  9.03 us
  transfers between devices with their start and end apart: 41, of which 26 were waited for; matrix products, arithmetic and copies ran while one was open for 13% of the time, Pallas kernels for 0%

profile of v3, /device:TPU:28, one launch (start us, length us, event | category | flops | bytes accessed | tf_op | source)
XLA Modules:
  0.0 400.3 jit_solution(5473867921814386227)
XLA Ops:
  9.5 4.7 %fusion.29 = (bf16[1,2048,512]{2,1,0:T(8,128)(2,1)}, bf16[2048,512]{1,0:T(8,128)(2,1)S(1)}, bf16[2048,512]{1,0:T(8,128)(2,1)}) fusion(bf16[1,4096,512]{2,1,0:T(8,128)(2,1)} %param.8, pred[]{:T(512)S(6)} %eq.67), kind=kLoop, calls=%fused_computation.81 | loop fusion | flops 1048576 | bytes 10485761 | tf_op jit(solution)/shard_map/slice | solution.py:22
  15.4 5.2 %fusion.28 = (bf16[1,2048,512]{2,1,0:T(8,128)(2,1)}, bf16[2048,512]{1,0:T(8,128)(2,1)}, bf16[2048,512]{1,0:T(8,128)(2,1)}) fusion(bf16[1,4096,512]{2,1,0:T(8,128)(2,1)} %param.9), kind=kLoop, calls=%fused_computation.80 | loop fusion | bytes 10485760 | tf_op jit(solution)/shard_map/slice | solution.py:22
  20.5 79.3 %all-reduce.3.cloned.1.call-done = bf16[2048,512]{1,0:T(8,128)(2,1)} async-done(((bf16[2048,512]{1,0:T(8,128)(2,1)}), bf16[2048,512]{1,0:T(8,128)(2,1)}) %all-reduce.3.cloned.1.call-update) | async-done | bytes 2097168 | tf_op jit(solution)/shard_map/psum | solution.py:13
  99.8 3.0 broadcast_select_fusion
  110.9 6.3 %collective-permute-done.9 = bf16[256,512]{1,0:T(8,128)(2,1)S(1)} collective-permute-done((bf16[256,512]{1,0:T(8,128)(2,1)S(1)}, bf16[256,512]{1,0:T(8,128)(2,1)S(1)}, u32[]{:S(2)}, u32[]{:S(2)}) %collective-permute-start.9) | collective-permute-done | bytes 262176 | tf_op jit(solution)/shard_map/ppermute | solution.py:50
  119.1 5.0 %collective-permute-start.10 = (bf16[256,512]{1,0:T(8,128)(2,1)S(1)}, bf16[256,512]{1,0:T(8,128)(2,1)S(1)}, u32[]{:S(2)}, u32[]{:S(2)}) collective-permute-start(bf16[256,512]{1,0:T(8,128)(2,1)S(1)} %get-tuple-element.40), channel_id=1, source_target_pairs={{24,16},{16,8},{25,17},{17,9},{26,18},{18,10},{27,19},{19,11},{28,... | collective-permute-start | bytes 786440 | tf_op jit(solution)/shard_map/ppermute | solution.py:50
  126.7 9.8 %collective-permute-done.10 = bf16[256,512]{1,0:T(8,128)(2,1)S(1)} collective-permute-done((bf16[256,512]{1,0:T(8,128)(2,1)S(1)}, bf16[256,512]{1,0:T(8,128)(2,1)S(1)}, u32[]{:S(2)}, u32[]{:S(2)}) %collective-permute-start.10) | collective-permute-done | bytes 262176 | tf_op jit(solution)/shard_map/ppermute | solution.py:50
  137.8 7.0 %collective-permute-start.11 = (bf16[256,512]{1,0:T(8,128)(2,1)S(1)}, bf16[256,512]{1,0:T(8,128)(2,1)S(1)}, u32[]{:S(2)}, u32[]{:S(2)}) collective-permute-start(bf16[256,512]{1,0:T(8,128)(2,1)S(1)} %get-tuple-element.38), channel_id=1, source_target_pairs={{24,16},{16,8},{8,0},{25,17},{17,9},{9,1},{26,18},{18,10},{10,2},{... | collective-permute-start | bytes 786440 | tf_op jit(solution)/shard_map/ppermute | solution.py:50
  148.6 8.3 %collective-permute-done.11 = bf16[256,512]{1,0:T(8,128)(2,1)S(1)} collective-permute-done((bf16[256,512]{1,0:T(8,128)(2,1)S(1)}, bf16[256,512]{1,0:T(8,128)(2,1)S(1)}, u32[]{:S(2)}, u32[]{:S(2)}) %collective-permute-start.11) | collective-permute-done | bytes 262176 | tf_op jit(solution)/shard_map/ppermute | solution.py:50
  158.1 4.4 %collective-permute-start.12 = (bf16[256,512]{1,0:T(8,128)(2,1)S(1)}, bf16[256,512]{1,0:T(8,128)(2,1)S(1)}, u32[]{:S(2)}, u32[]{:S(2)}) collective-permute-start(bf16[256,512]{1,0:T(8,128)(2,1)S(1)} %get-tuple-element.36), channel_id=1, source_target_pairs={{24,16},{16,8},{8,0},{25,17},{17,9},{9,1},{26,18},{18,10},{10,2},{... | collective-permute-start | bytes 786440 | tf_op jit(solution)/shard_map/ppermute | solution.py:50
  167.8 9.2 %collective-permute-done.3 = bf16[256,512]{1,0:T(8,128)(2,1)S(1)} collective-permute-done((bf16[256,512]{1,0:T(8,128)(2,1)S(1)}, bf16[256,512]{1,0:T(8,128)(2,1)S(1)}, u32[]{:S(2)}, u32[]{:S(2)}) %collective-permute-start.3) | collective-permute-done | bytes 262176 | tf_op jit(solution)/shard_map/ppermute | solution.py:49
  178.3 2.8 collective-permute-start.13
  184.9 6.0 %collective-permute-done.13 = bf16[256,512]{1,0:T(8,128)(2,1)S(1)} collective-permute-done((bf16[256,512]{1,0:T(8,128)(2,1)S(1)}, bf16[256,512]{1,0:T(8,128)(2,1)S(1)}, u32[]{:S(2)}, u32[]{:S(2)}) %collective-permute-start.13) | collective-permute-done | bytes 262176 | tf_op jit(solution)/shard_map/ppermute | solution.py:50
  191.0 10.5 %collective-permute-done.4 = bf16[256,512]{1,0:T(8,128)(2,1)S(1)} collective-permute-done((bf16[256,512]{1,0:T(8,128)(2,1)S(1)}, bf16[256,512]{1,0:T(8,128)(2,1)S(1)}, u32[]{:S(2)}, u32[]{:S(2)}) %collective-permute-start.4) | collective-permute-done | bytes 262176 | tf_op jit(solution)/shard_map/ppermute | solution.py:49
  202.8 3.1 collective-permute-start.14
  209.7 4.9 %collective-permute-done.14 = bf16[256,512]{1,0:T(8,128)(2,1)S(1)} collective-permute-done((bf16[256,512]{1,0:T(8,128)(2,1)S(1)}, bf16[256,512]{1,0:T(8,128)(2,1)S(1)}, u32[]{:S(2)}, u32[]{:S(2)}) %collective-permute-start.14) | collective-permute-done | bytes 262176 | tf_op jit(solution)/shard_map/ppermute | solution.py:50
  218.2 2.5 collective-permute-start.15
  224.8 4.2 %collective-permute-done.6 = bf16[256,512]{1,0:T(8,128)(2,1)S(1)} collective-permute-done((bf16[256,512]{1,0:T(8,128)(2,1)S(1)}, bf16[256,512]{1,0:T(8,128)(2,1)S(1)}, u32[]{:S(2)}, u32[]{:S(2)}) %collective-permute-start.6) | collective-permute-done | bytes 262176 | tf_op jit(solution)/shard_map/ppermute | solution.py:49
  236.5 4.4 %collective-permute-done.7 = bf16[256,512]{1,0:T(8,128)(2,1)S(1)} collective-permute-done((bf16[256,512]{1,0:T(8,128)(2,1)S(1)}, bf16[256,512]{1,0:T(8,128)(2,1)S(1)}, u32[]{:S(2)}, u32[]{:S(2)}) %collective-permute-start.7) | collective-permute-done | bytes 262176 | tf_op jit(solution)/shard_map/ppermute | solution.py:49
  250.1 3.3 collective-permute-done.8
  263.0 4.4 %collective-permute-start.21 = (bf16[256,512]{1,0:T(8,128)(2,1)S(1)}, bf16[256,512]{1,0:T(8,128)(2,1)S(1)}, u32[]{:S(2)}, u32[]{:S(2)}) collective-permute-start(bf16[256,512]{1,0:T(8,128)(2,1)S(1)} %bitcast_select_fusion.15), channel_id=1, source_target_pairs={{24,16},{16,8},{8,0},{25,17},{17,9},{9,1},{26,18},{18,10},{10,2},{... | collective-permute-start | bytes 786440 | tf_op jit(solution)/shard_map/ppermute | solution.py:50
  273.4 3.7 fusion.3
  280.5 5.1 %collective-permute-start.23 = (bf16[256,512]{1,0:T(8,128)(2,1)S(1)}, bf16[256,512]{1,0:T(8,128)(2,1)S(1)}, u32[]{:S(2)}, u32[]{:S(2)}) collective-permute-start(bf16[256,512]{1,0:T(8,128)(2,1)S(1)} %get-tuple-element.23), channel_id=1, source_target_pairs={{24,16},{16,8},{8,0},{25,17},{17,9},{9,1},{26,18},{18,10},{10,2},{... | collective-permute-start | bytes 786440 | tf_op jit(solution)/shard_map/ppermute | solution.py:50
  292.8 5.0 %collective-permute-start.25 = (bf16[256,512]{1,0:T(8,128)(2,1)S(1)}, bf16[256,512]{1,0:T(8,128)(2,1)S(1)}, u32[]{:S(2)}, u32[]{:S(2)}) collective-permute-start(bf16[256,512]{1,0:T(8,128)(2,1)S(1)} %get-tuple-element.21), channel_id=1, source_target_pairs={{24,16},{16,8},{8,0},{25,17},{17,9},{9,1},{26,18},{18,10},{10,2},{... | collective-permute-start | bytes 786440 | tf_op jit(solution)/shard_map/ppermute | solution.py:50
  305.1 5.3 %collective-permute-start.27 = (bf16[256,512]{1,0:T(8,128)(2,1)S(1)}, bf16[256,512]{1,0:T(8,128)(2,1)S(1)}, u32[]{:S(2)}, u32[]{:S(2)}) collective-permute-start(bf16[256,512]{1,0:T(8,128)(2,1)S(1)} %get-tuple-element.19), channel_id=1, source_target_pairs={{24,16},{16,8},{8,0},{25,17},{17,9},{9,1},{26,18},{18,10},{10,2},{... | collective-permute-start | bytes 786440 | tf_op jit(solution)/shard_map/ppermute | solution.py:50
  318.7 5.0 %collective-permute-start.29 = (bf16[256,512]{1,0:T(8,128)(2,1)S(1)}, bf16[256,512]{1,0:T(8,128)(2,1)S(1)}, u32[]{:S(2)}, u32[]{:S(2)}) collective-permute-start(bf16[256,512]{1,0:T(8,128)(2,1)S(1)} %get-tuple-element.17), channel_id=1, source_target_pairs={{24,16},{16,8},{8,0},{25,17},{17,9},{9,1},{26,18},{18,10},{10,2},{... | collective-permute-start | bytes 786440 | tf_op jit(solution)/shard_map/ppermute | solution.py:50
  333.2 5.0 %collective-permute-start.31 = (bf16[256,512]{1,0:T(8,128)(2,1)S(1)}, bf16[256,512]{1,0:T(8,128)(2,1)S(1)}, u32[]{:S(2)}, u32[]{:S(2)}) collective-permute-start(bf16[256,512]{1,0:T(8,128)(2,1)S(1)} %get-tuple-element.15), channel_id=1, source_target_pairs={{24,16},{16,8},{8,0},{25,17},{17,9},{9,1},{26,18},{18,10},{10,2},{... | collective-permute-start | bytes 786440 | tf_op jit(solution)/shard_map/ppermute | solution.py:50
  349.8 7.1 %collective-permute-done.30 = bf16[256,512]{1,0:T(8,128)(2,1)S(1)} collective-permute-done((bf16[256,512]{1,0:T(8,128)(2,1)S(1)}, bf16[256,512]{1,0:T(8,128)(2,1)S(1)}, u32[]{:S(2)}, u32[]{:S(2)}) %collective-permute-start.30) | collective-permute-done | bytes 262176 | tf_op jit(solution)/shard_map/ppermute | solution.py:49
  362.1 6.0 %collective-permute-done.32 = bf16[256,512]{1,0:T(8,128)(2,1)S(1)} collective-permute-done((bf16[256,512]{1,0:T(8,128)(2,1)S(1)}, bf16[256,512]{1,0:T(8,128)(2,1)S(1)}, u32[]{:S(2)}, u32[]{:S(2)}) %collective-permute-start.32) | collective-permute-done | bytes 262176 | tf_op jit(solution)/shard_map/ppermute | solution.py:49
  371.3 6.9 %collective-permute-done.34 = bf16[256,512]{1,0:T(8,128)(2,1)S(1)} collective-permute-done((bf16[256,512]{1,0:T(8,128)(2,1)S(1)}, bf16[256,512]{1,0:T(8,128)(2,1)S(1)}, u32[]{:S(2)}, u32[]{:S(2)}) %collective-permute-start.34) | collective-permute-done | bytes 262176 | tf_op jit(solution)/shard_map/ppermute | solution.py:49
  380.0 3.7 fusion.7
  383.7 9.0 %fusion = bf16[1,512,4096]{2,1,0:T(8,128)(2,1)} fusion(bf16[512,4096]{1,0:T(8,128)(2,1)} %param.11, bf16[512,4096]{0,1:T(8,128)(2,1)} %all-gather.6.cloned.1.call-done, f32[512,512]{1,0:T(8,128)S(1)} %fusion.7, bf16[2048,512]{1,0:T(8,128)(2,1)S(1)} %copy-done, bf16[512,4096]{1,0:T(8,128)(2,1)} %bitcast.102), kind=kOutput, calls=%fused_computation.1 | convolution fusion | flops 3232235520 | bytes 17825792 | tf_op jit(solution)/shard_map/dot_general | solution.py:92
  (90 shorter events, 88.1 us)
Async XLA Ops:
  7.4 92.4 %all-reduce.3.cloned.1.call-start = ((), (), s32[]{:S(2)}) async-start(), calls=%async_computation | async-start | bytes 4194304 | tf_op jit(solution)/shard_map/psum | solution.py:13
  14.2 259.3 %all-gather.10.cloned.1.call-start = ((), (), s32[]{:S(2)}) async-start(), calls=%async_computation.4 | async-start | bytes 4718592 | tf_op jit(solution)/shard_map/all_gather | solution.py:80
  14.7 365.3 %all-reduce.5.cloned.1.call-start = ((), (), s32[]{:S(2)}) async-start(), calls=%async_computation.1 | async-start | bytes 4194304 | tf_op jit(solution)/shard_map/psum | solution.py:13
  102.9 277.1 %all-gather.8.cloned.1.call-start = ((), (), s32[]{:S(2)}) async-start(), calls=%async_computation.3 | async-start | bytes 4718592 | tf_op jit(solution)/shard_map/all_gather | solution.py:81
  103.5 280.2 %all-gather.6.cloned.1.call-start = ((), (), s32[]{:S(2)}) async-start(), calls=%async_computation.2 | async-start | bytes 4718592 | tf_op jit(solution)/shard_map/all_gather | solution.py:88
  105.3 11.8 %collective-permute-start.9 = (bf16[256,512]{1,0:T(8,128)(2,1)S(1)}, bf16[256,512]{1,0:T(8,128)(2,1)S(1)}, u32[]{:S(2)}, u32[]{:S(2)}) collective-permute-start(bf16[256,512]{1,0:T(8,128)(2,1)S(1)} %get-tuple-element.42), channel_id=1, source_target_pairs={{24,16},{25,17},{26,18},{27,19},{28,20},{29,21},{30,22},{31,23}} | collective-permute-start | bytes 786440 | tf_op jit(solution)/shard_map/ppermute | solution.py:50
  119.1 17.4 %collective-permute-start.10 = (bf16[256,512]{1,0:T(8,128)(2,1)S(1)}, bf16[256,512]{1,0:T(8,128)(2,1)S(1)}, u32[]{:S(2)}, u32[]{:S(2)}) collective-permute-start(bf16[256,512]{1,0:T(8,128)(2,1)S(1)} %get-tuple-element.40), channel_id=1, source_target_pairs={{24,16},{16,8},{25,17},{17,9},{26,18},{18,10},{27,19},{19,11},{28,... | collective-permute-start | bytes 786440 | tf_op jit(solution)/shard_map/ppermute | solution.py:50
  137.8 19.1 %collective-permute-start.11 = (bf16[256,512]{1,0:T(8,128)(2,1)S(1)}, bf16[256,512]{1,0:T(8,128)(2,1)S(1)}, u32[]{:S(2)}, u32[]{:S(2)}) collective-permute-start(bf16[256,512]{1,0:T(8,128)(2,1)S(1)} %get-tuple-element.38), channel_id=1, source_target_pairs={{24,16},{16,8},{8,0},{25,17},{17,9},{9,1},{26,18},{18,10},{10,2},{... | collective-permute-start | bytes 786440 | tf_op jit(solution)/shard_map/ppermute | solution.py:50
  144.8 12.1 %collective-permute-start.2 = (bf16[256,512]{1,0:T(8,128)(2,1)S(1)}, bf16[256,512]{1,0:T(8,128)(2,1)S(1)}, u32[]{:S(2)}, u32[]{:S(2)}) collective-permute-start(bf16[256,512]{1,0:T(8,128)(2,1)S(1)} %get-tuple-element.39), channel_id=1, source_target_pairs={{0,8},{8,16},{16,24},{1,9},{9,17},{17,25},{2,10},{10,18},{18,26},{... | collective-permute-start | bytes 786440 | tf_op jit(solution)/shard_map/ppermute | solution.py:49
  158.1 9.7 %collective-permute-start.12 = (bf16[256,512]{1,0:T(8,128)(2,1)S(1)}, bf16[256,512]{1,0:T(8,128)(2,1)S(1)}, u32[]{:S(2)}, u32[]{:S(2)}) collective-permute-start(bf16[256,512]{1,0:T(8,128)(2,1)S(1)} %get-tuple-element.36), channel_id=1, source_target_pairs={{24,16},{16,8},{8,0},{25,17},{17,9},{9,1},{26,18},{18,10},{10,2},{... | collective-permute-start | bytes 786440 | tf_op jit(solution)/shard_map/ppermute | solution.py:50
  162.5 14.5 %collective-permute-start.3 = (bf16[256,512]{1,0:T(8,128)(2,1)S(1)}, bf16[256,512]{1,0:T(8,128)(2,1)S(1)}, u32[]{:S(2)}, u32[]{:S(2)}) collective-permute-start(bf16[256,512]{1,0:T(8,128)(2,1)S(1)} %get-tuple-element.37), channel_id=1, source_target_pairs={{0,8},{8,16},{16,24},{1,9},{9,17},{17,25},{2,10},{10,18},{18,26},{... | collective-permute-start | bytes 786440 | tf_op jit(solution)/shard_map/ppermute | solution.py:49
  178.3 12.7 %collective-permute-start.13 = (bf16[256,512]{1,0:T(8,128)(2,1)S(1)}, bf16[256,512]{1,0:T(8,128)(2,1)S(1)}, u32[]{:S(2)}, u32[]{:S(2)}) collective-permute-start(bf16[256,512]{1,0:T(8,128)(2,1)S(1)} %get-tuple-element.34), channel_id=1, source_target_pairs={{24,16},{16,8},{8,0},{25,17},{17,9},{9,1},{26,18},{18,10},{10,2},{... | collective-permute-start | bytes 786440 | tf_op jit(solution)/shard_map/ppermute | solution.py:50
  181.1 20.4 %collective-permute-start.4 = (bf16[256,512]{1,0:T(8,128)(2,1)S(1)}, bf16[256,512]{1,0:T(8,128)(2,1)S(1)}, u32[]{:S(2)}, u32[]{:S(2)}) collective-permute-start(bf16[256,512]{1,0:T(8,128)(2,1)S(1)} %get-tuple-element.35), channel_id=1, source_target_pairs={{0,8},{8,16},{16,24},{1,9},{9,17},{17,25},{2,10},{10,18},{18,26},{... | collective-permute-start | bytes 786440 | tf_op jit(solution)/shard_map/ppermute | solution.py:49
  202.8 11.8 %collective-permute-start.14 = (bf16[256,512]{1,0:T(8,128)(2,1)S(1)}, bf16[256,512]{1,0:T(8,128)(2,1)S(1)}, u32[]{:S(2)}, u32[]{:S(2)}) collective-permute-start(bf16[256,512]{1,0:T(8,128)(2,1)S(1)} %get-tuple-element.32), channel_id=1, source_target_pairs={{24,16},{16,8},{8,0},{25,17},{17,9},{9,1},{26,18},{18,10},{10,2},{... | collective-permute-start | bytes 786440 | tf_op jit(solution)/shard_map/ppermute | solution.py:50
  205.9 11.0 %collective-permute-start.5 = (bf16[256,512]{1,0:T(8,128)(2,1)S(1)}, bf16[256,512]{1,0:T(8,128)(2,1)S(1)}, u32[]{:S(2)}, u32[]{:S(2)}) collective-permute-start(bf16[256,512]{1,0:T(8,128)(2,1)S(1)} %get-tuple-element.33), channel_id=1, source_target_pairs={{0,8},{8,16},{16,24},{1,9},{9,17},{17,25},{2,10},{10,18},{18,26},{... | collective-permute-start | bytes 786440 | tf_op jit(solution)/shard_map/ppermute | solution.py:49
  232.7 8.3 %collective-permute-start.7 = (bf16[256,512]{1,0:T(8,128)(2,1)S(1)}, bf16[256,512]{1,0:T(8,128)(2,1)S(1)}, u32[]{:S(2)}, u32[]{:S(2)}) collective-permute-start(bf16[256,512]{1,0:T(8,128)(2,1)S(1)} %get-tuple-element.29), channel_id=1, source_target_pairs={{0,8},{8,16},{16,24},{1,9},{9,17},{17,25},{2,10},{10,18},{18,26},{... | collective-permute-start | bytes 786440 | tf_op jit(solution)/shard_map/ppermute | solution.py:49
  258.8 11.2 %collective-permute-start.18 = (bf16[256,512]{1,0:T(8,128)(2,1)}, bf16[256,512]{1,0:T(8,128)(2,1)}, u32[]{:S(2)}, u32[]{:S(2)}) collective-permute-start(bf16[256,512]{1,0:T(8,128)(2,1)} %get-tuple-element.8), channel_id=1, source_target_pairs={{0,8},{8,16},{16,24},{1,9},{9,17},{17,25},{2,10},{10,18},{18,26},{... | collective-permute-start | bytes 786440 | tf_op jit(solution)/shard_map/ppermute | solution.py:49
  263.0 8.3 %collective-permute-start.21 = (bf16[256,512]{1,0:T(8,128)(2,1)S(1)}, bf16[256,512]{1,0:T(8,128)(2,1)S(1)}, u32[]{:S(2)}, u32[]{:S(2)}) collective-permute-start(bf16[256,512]{1,0:T(8,128)(2,1)S(1)} %bitcast_select_fusion.15), channel_id=1, source_target_pairs={{24,16},{16,8},{8,0},{25,17},{17,9},{9,1},{26,18},{18,10},{10,2},{... | collective-permute-start | bytes 786440 | tf_op jit(solution)/shard_map/ppermute | solution.py:50
  279.2 8.9 %collective-permute-start.20 = (bf16[256,512]{1,0:T(8,128)(2,1)S(1)}, bf16[256,512]{1,0:T(8,128)(2,1)S(1)}, u32[]{:S(2)}, u32[]{:S(2)}) collective-permute-start(bf16[256,512]{1,0:T(8,128)(2,1)S(1)} %get-tuple-element.24), channel_id=1, source_target_pairs={{0,8},{8,16},{16,24},{1,9},{9,17},{17,25},{2,10},{10,18},{18,26},{... | collective-permute-start | bytes 786440 | tf_op jit(solution)/shard_map/ppermute | solution.py:49
  280.5 8.9 %collective-permute-start.23 = (bf16[256,512]{1,0:T(8,128)(2,1)S(1)}, bf16[256,512]{1,0:T(8,128)(2,1)S(1)}, u32[]{:S(2)}, u32[]{:S(2)}) collective-permute-start(bf16[256,512]{1,0:T(8,128)(2,1)S(1)} %get-tuple-element.23), channel_id=1, source_target_pairs={{24,16},{16,8},{8,0},{25,17},{17,9},{9,1},{26,18},{18,10},{10,2},{... | collective-permute-start | bytes 786440 | tf_op jit(solution)/shard_map/ppermute | solution.py:50
  291.5 8.8 %collective-permute-start.22 = (bf16[256,512]{1,0:T(8,128)(2,1)S(1)}, bf16[256,512]{1,0:T(8,128)(2,1)S(1)}, u32[]{:S(2)}, u32[]{:S(2)}) collective-permute-start(bf16[256,512]{1,0:T(8,128)(2,1)S(1)} %get-tuple-element.22), channel_id=1, source_target_pairs={{0,8},{8,16},{16,24},{1,9},{9,17},{17,25},{2,10},{10,18},{18,26},{... | collective-permute-start | bytes 786440 | tf_op jit(solution)/shard_map/ppermute | solution.py:49
  292.8 9.0 %collective-permute-start.25 = (bf16[256,512]{1,0:T(8,128)(2,1)S(1)}, bf16[256,512]{1,0:T(8,128)(2,1)S(1)}, u32[]{:S(2)}, u32[]{:S(2)}) collective-permute-start(bf16[256,512]{1,0:T(8,128)(2,1)S(1)} %get-tuple-element.21), channel_id=1, source_target_pairs={{24,16},{16,8},{8,0},{25,17},{17,9},{9,1},{26,18},{18,10},{10,2},{... | collective-permute-start | bytes 786440 | tf_op jit(solution)/shard_map/ppermute | solution.py:50
  303.9 9.8 %collective-permute-start.24 = (bf16[256,512]{1,0:T(8,128)(2,1)S(1)}, bf16[256,512]{1,0:T(8,128)(2,1)S(1)}, u32[]{:S(2)}, u32[]{:S(2)}) collective-permute-start(bf16[256,512]{1,0:T(8,128)(2,1)S(1)} %get-tuple-element.20), channel_id=1, source_target_pairs={{0,8},{8,16},{16,24},{1,9},{9,17},{17,25},{2,10},{10,18},{18,26},{... | collective-permute-start | bytes 786440 | tf_op jit(solution)/shard_map/ppermute | solution.py:49
  305.1 10.2 %collective-permute-start.27 = (bf16[256,512]{1,0:T(8,128)(2,1)S(1)}, bf16[256,512]{1,0:T(8,128)(2,1)S(1)}, u32[]{:S(2)}, u32[]{:S(2)}) collective-permute-start(bf16[256,512]{1,0:T(8,128)(2,1)S(1)} %get-tuple-element.19), channel_id=1, source_target_pairs={{24,16},{16,8},{8,0},{25,17},{17,9},{9,1},{26,18},{18,10},{10,2},{... | collective-permute-start | bytes 786440 | tf_op jit(solution)/shard_map/ppermute | solution.py:50
  317.4 10.7 %collective-permute-start.26 = (bf16[256,512]{1,0:T(8,128)(2,1)S(1)}, bf16[256,512]{1,0:T(8,128)(2,1)S(1)}, u32[]{:S(2)}, u32[]{:S(2)}) collective-permute-start(bf16[256,512]{1,0:T(8,128)(2,1)S(1)} %get-tuple-element.18), channel_id=1, source_target_pairs={{0,8},{8,16},{16,24},{1,9},{9,17},{17,25},{2,10},{10,18},{18,26},{... | collective-permute-start | bytes 786440 | tf_op jit(solution)/shard_map/ppermute | solution.py:49
  318.7 11.2 %collective-permute-start.29 = (bf16[256,512]{1,0:T(8,128)(2,1)S(1)}, bf16[256,512]{1,0:T(8,128)(2,1)S(1)}, u32[]{:S(2)}, u32[]{:S(2)}) collective-permute-start(bf16[256,512]{1,0:T(8,128)(2,1)S(1)} %get-tuple-element.17), channel_id=1, source_target_pairs={{24,16},{16,8},{8,0},{25,17},{17,9},{9,1},{26,18},{18,10},{10,2},{... | collective-permute-start | bytes 786440 | tf_op jit(solution)/shard_map/ppermute | solution.py:50
  331.9 11.2 %collective-permute-start.28 = (bf16[256,512]{1,0:T(8,128)(2,1)S(1)}, bf16[256,512]{1,0:T(8,128)(2,1)S(1)}, u32[]{:S(2)}, u32[]{:S(2)}) collective-permute-start(bf16[256,512]{1,0:T(8,128)(2,1)S(1)} %get-tuple-element.16), channel_id=1, source_target_pairs={{0,8},{8,16},{16,24},{1,9},{9,17},{17,25},{2,10},{10,18},{18,26},{... | collective-permute-start | bytes 786440 | tf_op jit(solution)/shard_map/ppermute | solution.py:49
  333.2 9.9 %collective-permute-start.31 = (bf16[256,512]{1,0:T(8,128)(2,1)S(1)}, bf16[256,512]{1,0:T(8,128)(2,1)S(1)}, u32[]{:S(2)}, u32[]{:S(2)}) collective-permute-start(bf16[256,512]{1,0:T(8,128)(2,1)S(1)} %get-tuple-element.15), channel_id=1, source_target_pairs={{24,16},{16,8},{8,0},{25,17},{17,9},{9,1},{26,18},{18,10},{10,2},{... | collective-permute-start | bytes 786440 | tf_op jit(solution)/shard_map/ppermute | solution.py:50
  345.1 11.7 %collective-permute-start.30 = (bf16[256,512]{1,0:T(8,128)(2,1)S(1)}, bf16[256,512]{1,0:T(8,128)(2,1)S(1)}, u32[]{:S(2)}, u32[]{:S(2)}) collective-permute-start(bf16[256,512]{1,0:T(8,128)(2,1)S(1)} %get-tuple-element.14), channel_id=1, source_target_pairs={{0,8},{8,16},{16,24},{1,9},{9,17},{17,25},{2,10},{10,18},{18,26},{... | collective-permute-start | bytes 786440 | tf_op jit(solution)/shard_map/ppermute | solution.py:49
  346.4 10.5 %collective-permute-start.33 = (bf16[256,512]{1,0:T(8,128)(2,1)S(1)}, bf16[256,512]{1,0:T(8,128)(2,1)S(1)}, u32[]{:S(2)}, u32[]{:S(2)}) collective-permute-start(bf16[256,512]{1,0:T(8,128)(2,1)S(1)} %get-tuple-element.13), channel_id=1, source_target_pairs={{16,8},{8,0},{17,9},{9,1},{18,10},{10,2},{19,11},{11,3},{20,12},{1... | collective-permute-start | bytes 786440 | tf_op jit(solution)/shard_map/ppermute | solution.py:50
  358.9 9.2 %collective-permute-start.32 = (bf16[256,512]{1,0:T(8,128)(2,1)S(1)}, bf16[256,512]{1,0:T(8,128)(2,1)S(1)}, u32[]{:S(2)}, u32[]{:S(2)}) collective-permute-start(bf16[256,512]{1,0:T(8,128)(2,1)S(1)} %get-tuple-element.12), channel_id=1, source_target_pairs={{8,16},{16,24},{9,17},{17,25},{10,18},{18,26},{11,19},{19,27},{12,... | collective-permute-start | bytes 786440 | tf_op jit(solution)/shard_map/ppermute | solution.py:49
  361.4 9.8 %collective-permute-start.35 = (bf16[256,512]{1,0:T(8,128)(2,1)S(1)}, bf16[256,512]{1,0:T(8,128)(2,1)S(1)}, u32[]{:S(2)}, u32[]{:S(2)}) collective-permute-start(bf16[256,512]{1,0:T(8,128)(2,1)S(1)} %get-tuple-element.11), channel_id=1, source_target_pairs={{8,0},{9,1},{10,2},{11,3},{12,4},{13,5},{14,6},{15,7}} | collective-permute-start | bytes 786440 | tf_op jit(solution)/shard_map/ppermute | solution.py:50
  (12 other events, 73.5 us)
Sparse Core Ops, SparseCore 0:
  14.3 85.4 all-reduce.2
  103.0 111.3 all-reduce.4
Sparse Core Ops, SparseCore 1:
  16.5 37.5 all-gather.9
  105.2 37.5 all-gather.7
  279.3 39.6 all-gather.5

commit v4 on v2

v4 whole, which is shorter than its diff:
```python
import jax
import jax.numpy as jnp
from jax import lax
from jax.sharding import PartitionSpec as P

damping = 0.01
ROOM = 2**24


def product_and_divide(rot_out, all_rot_in, eig_lambda, tokens):
    denom = eig_lambda.astype(jnp.float32) + damping
    contract = (((0,), (0,)), ((), ()))
    product = lax.dot_general(rot_out, all_rot_in, contract, preferred_element_type=jnp.float32) / tokens
    return (product / denom).astype(jnp.bfloat16)[None]


def from_owner(held, owner):
    return lax.psum(jnp.where(lax.axis_index("dp") == owner, held, jnp.zeros_like(held)), "dp")


def dot(a, b):
    return jnp.dot(a, b, preferred_element_type=jnp.float32)


def move_bases(acts, grads, basis_in_held, basis_out_held, owners, eig_lambda):
    column = lax.axis_index("tensor")
    basis_in = from_owner(basis_in_held[0], owners[0, column])
    basis_out = from_owner(basis_out_held[0], owners[1, column])
    rot_in = dot(lax.all_gather(acts[0], "tensor", axis=1, tiled=True), basis_in).astype(jnp.bfloat16)
    rot_out = dot(lax.all_gather(grads[0], "tensor", axis=1, tiled=True), basis_out).astype(jnp.bfloat16)
    return product_and_divide(
        rot_out, lax.all_gather(rot_in, "tensor", axis=1, tiled=True), eig_lambda, acts.shape[1]
    )


def swap(block, bit, n):
    return lax.ppermute(block, "tensor", [(j, j ^ bit) for j in range(n)])


def gather_plane(block, bits, n):
    width = block.shape[1]
    found = {0: block}
    for bit in bits:
        order = sorted(found)
        came = swap(jnp.concatenate([found[i] for i in order], axis=1), bit, n)
        for at, i in enumerate(order):
            found[i ^ bit] = came[:, at * width : (at + 1) * width]
    return jnp.concatenate([found[i] for i in sorted(found)], axis=1)


def in_order(held, column, n, keep=None):
    width = held.shape[0] // n
    offsets = list(range(0, n, 2)) + list(range(1, n, 2))
    blocks = [lax.dynamic_slice(held, ((column ^ i) * width, 0), (width, held.shape[1])) for i in offsets]
    if keep is not None:
        blocks = [jnp.where(keep, block, jnp.zeros_like(block)) for block in blocks]
    return jnp.concatenate(blocks, axis=0)


def move_inputs(n_dp, n, acts, grads, basis_in_held, basis_out_held, owners, eig_lambda):
    column = lax.axis_index("tensor")
    me = lax.axis_index("dp")
    owner_in, owner_out = owners[0, column], owners[1, column]
    half = basis_in_held.shape[1] // 2
    bits = []
    while 2 << len(bits) < n:
        bits.append(2 << len(bits))
    orders = (bits, bits[::-1])

    pieces = [acts[0]]
    for i in range(1, n_dp):
        pieces.append(lax.ppermute(acts[0], "dp", [(z, (z - i) % n_dp) for z in range(n_dp)]))

    masked_out = in_order(basis_out_held[0], column, n, me == owner_out)
    basis_out = lax.psum(masked_out, "dp")
    pieces = [lax.optimization_barrier((piece, masked_out))[0] for piece in pieces]
    own_grads, _ = lax.optimization_barrier((grads[0], masked_out))
    basis_in = in_order(basis_in_held[0], column, n)

    def rotate(even, odd, basis):
        return (dot(even, basis[:half]) + dot(odd, basis[half:])).astype(jnp.bfloat16)

    grads_even = gather_plane(own_grads, orders[1], n)
    grads_odd = swap(grads_even, 1, n)

    rot_in = None
    for i in range(n_dp):
        if i == n_dp - 1:
            tokens = acts.shape[1] // 2
            even = jnp.concatenate(
                [gather_plane(pieces[i][:tokens], orders[0], n), gather_plane(pieces[i][tokens:], orders[1], n)], axis=0
            )
        else:
            even = gather_plane(pieces[i], orders[0 if i == 0 else (i + 1) % 2], n)
        rot = rotate(even, swap(even, 1, n), basis_in)
        if i == 0:
            rot_in = rot
        else:
            rot = lax.ppermute(rot, "dp", [(z, (z + i) % n_dp) for z in range(n_dp)])
            rot_in = jnp.where((me - owner_in) % n_dp == i, rot, rot_in)

    all_rot_in = lax.all_gather(rot_in, "tensor", axis=1, tiled=True)
    rot_out = rotate(grads_even, grads_odd, basis_out)
    return product_and_divide(rot_out, all_rot_in, eig_lambda, acts.shape[1])


def solution(mesh):
    placed = (
        P("dp", None, "tensor"),
        P("dp", None, "tensor"),
        P("dp", None, "tensor"),
        P("dp", None, "tensor"),
        P(),
        P("tensor", None),
    )
    n_dp, n_tensor = mesh.shape["dp"], mesh.shape["tensor"]

    def step(acts, *rest):
        whole = n_dp * acts.shape[1] * acts.shape[2] * n_tensor * acts.dtype.itemsize
        if whole <= ROOM and n_tensor & (n_tensor - 1) == 0:
            return move_inputs(n_dp, n_tensor, acts, *rest)
        return move_bases(acts, *rest)

    return jax.shard_map(step, mesh=mesh, in_specs=placed, out_specs=P("dp", "tensor", None), check_vma=False)
```

time: 514 us -> 338 us (0.66)
  waiting for transfers between devices: 466 us -> 222 us
  other arithmetic: 9.13 us -> 32.5 us
  starting transfers between devices: 0.39 us -> 22.6 us
  local copies, waits for them, and re-layouts: 1.42 us -> 13.2 us
  matrix products: 21 us -> 27.4 us
    all_gather x7 -> x1, waiting for transfers between devices: 290 us -> 0.03 us  [move_inputs(): all_rot_in = lax.all_gather(rot_in, 'tensor', axis=1, tiled=True)]
    ppermute x0 -> x23, waiting for transfers between devices: none -> 205 us  [the longest x17 121 us: swap(): return lax.ppermute(block, 'tensor', [(j, j ^ bit) for j in range(n)])]
    reduce_scatter x4 -> x0, waiting for transfers between devices: 173 us -> none  [from_owner(): share = lax.psum_scatter(block, 'dp', scatter_dimension=0, tiled=True)]
    ppermute x0 -> x23, starting transfers between devices: none -> 22.6 us  [the longest x17 14.5 us: swap(): return lax.ppermute(block, 'tensor', [(j, j ^ bit) for j in range(n)])]
    concatenate x0 -> x10, other arithmetic: none -> 18 us  [the longest x1 11.5 us: move_inputs(): jnp.concatenate([gather_plane(pieces[i][:tokens], orders[0], n), gather_p...]
    psum x0 -> x1, waiting for transfers between devices: none -> 17.2 us  [move_inputs(): basis_out = lax.psum(masked_out, 'dp')]
    unnamed x0 -> x7, other arithmetic: none -> 13.5 us
    select_n x2 -> x1, other arithmetic: 9.13 us -> 0.95 us  [move_inputs(): rot_in = jnp.where((me - owner_in) % n_dp == i, rot, rot_in)]
  transfers between devices with their start and end apart: 11 -> 25, of which waited for: 11 -> 16; matrix products, arithmetic and copies ran while one was open for 3% -> 18% of each run, Pallas kernels for 0% -> 0%
where the time goes in v4:
time: 338 us; the launch traced here: 335 us
  waiting for transfers between devices  222 us (66%)
  other arithmetic  32.5 us (10%)
  matrix products  27.4 us (8%)
  starting transfers between devices  22.6 us (7%)
  between operations  16.7 us (5%)
  local copies, waits for them, and re-layouts  13.2 us (4%)
    ppermute x17, waiting for transfers between devices, swap(): return lax.ppermute(block, 'tensor', [(j, j ^ bit) for j in range(n)])  121 us
    ppermute x3, waiting for transfers between devices, move_inputs(): rot = lax.ppermute(rot, 'dp', [(z, (z + i) % n_dp) for z in range(n_dp)])  69.3 us
    psum x1, waiting for transfers between devices, move_inputs(): basis_out = lax.psum(masked_out, 'dp')  17.2 us
    dot_general x9, matrix products, dot(): return jnp.dot(a, b, preferred_element_type=jnp.float32)  17 us
    ppermute x17, starting transfers between devices, swap(): return lax.ppermute(block, 'tensor', [(j, j ^ bit) for j in range(n)])  14.5 us
    ppermute x3, waiting for transfers between devices, move_inputs(): lax.ppermute(acts[0], 'dp', [(z, (z - i) % n_dp) for z in range(n_dp)])  14.2 us
    unnamed x7, other arithmetic  13.5 us
    concatenate x1, other arithmetic, move_inputs(): jnp.concatenate([gather_plane(pieces[i][:tokens], orders[0], n), gather_p...  11.5 us
  transfers between devices with their start and end apart: 25, of which 16 were waited for; matrix products, arithmetic and copies ran while one was open for 18% of the time, Pallas kernels for 0%

profile of v4, /device:TPU:16, one launch (start us, length us, event | category | flops | bytes accessed | tf_op | source)
XLA Modules:
  0.0 334.5 jit_solution(16364306558742175781)
XLA Ops:
  11.4 1.9 bitcast_dynamic-update-slice_fusion.7
  13.3 2.0 bitcast_dynamic-update-slice_fusion.6
  15.3 1.9 bitcast_dynamic-update-slice_fusion.5
  17.2 1.9 bitcast_dynamic-update-slice_fusion.4
  19.1 1.9 bitcast_dynamic-update-slice_fusion.3
  21.0 1.9 bitcast_dynamic-update-slice_fusion.2
  23.0 1.9 bitcast_dynamic-update-slice_fusion.1
  24.9 1.9 bitcast_dynamic-update-slice_fusion
  26.8 6.8 %collective-permute-done.3 = bf16[512,512]{1,0:T(8,128)(2,1)S(1)} collective-permute-done((bf16[512,512]{1,0:T(8,128)(2,1)}, bf16[512,512]{1,0:T(8,128)(2,1)S(1)}, u32[]{:S(2)}, u32[]{:S(2)}) %collective-permute-start.3) | collective-permute-done | bytes 524320 | tf_op jit(solution)/shard_map/ppermute | solution.py:72
  35.2 7.4 %collective-permute-done.10 = bf16[512,512]{1,0:T(8,128)(2,1)S(1)} collective-permute-done((bf16[512,512]{1,0:T(8,128)(2,1)}, bf16[512,512]{1,0:T(8,128)(2,1)S(1)}, u32[]{:S(2)}, u32[]{:S(2)}) %collective-permute-start.10) | collective-permute-done | bytes 524320 | tf_op jit(solution)/shard_map/ppermute | solution.py:72
  47.1 6.3 %collective-permute-done.4 = bf16[256,512]{1,0:T(8,128)(2,1)S(1)} collective-permute-done((bf16[256,512]{1,0:T(8,128)(2,1)S(1)}, bf16[256,512]{1,0:T(8,128)(2,1)S(1)}, u32[]{:S(2)}, u32[]{:S(2)}) %collective-permute-start.4) | collective-permute-done | bytes 262176 | tf_op jit(solution)/shard_map/ppermute | solution.py:37
  54.0 3.4 %collective-permute-done.11 = bf16[512,512]{1,0:T(8,128)(2,1)S(1)} collective-permute-done((bf16[512,512]{1,0:T(8,128)(2,1)S(1)}, bf16[512,512]{1,0:T(8,128)(2,1)S(1)}, u32[]{:S(2)}, u32[]{:S(2)}) %collective-permute-start.11) | collective-permute-done | bytes 524320 | tf_op jit(solution)/shard_map/ppermute | solution.py:37
  61.2 3.4 %collective-permute-done.7 = bf16[256,1024]{1,0:T(8,128)(2,1)S(1)} collective-permute-done((bf16[256,1024]{1,0:T(8,128)(2,1)S(1)}, bf16[256,1024]{1,0:T(8,128)(2,1)S(1)}, u32[]{:S(2)}, u32[]{:S(2)}) %collective-permute-start.7) | collective-permute-done | bytes 524320 | tf_op jit(solution)/shard_map/ppermute | solution.py:37
  64.6 3.1 collective-permute-done.5
  67.7 11.5 %maximum_maximum_fusion = bf16[512,2048]{1,0:T(8,128)(2,1)S(1)} fusion(bf16[256,512]{1,0:T(8,128)(2,1)S(1)} %get-tuple-element.30, bf16[256,512]{1,0:T(8,128)(2,1)S(1)} %collective-permute-done.6, bf16[256,512]{1,0:T(8,128)(2,1)S(1)} %get-tuple-element.29, bf16[256,512]{1,0:T(8,128)(2,1)S(1)} %get-tuple-element.28, ...), kind=kLoop, calls=%fused_computation.7 | loop fusion | flops 14680064 | bytes 4194304 | tf_op jit(solution)/shard_map/concatenate | solution.py:90
  79.3 19.0 %collective-permute-done.20 = bf16[512,512]{1,0:T(8,128)(2,1)S(1)} collective-permute-done((bf16[512,512]{1,0:T(8,128)(2,1)S(1)}, bf16[512,512]{1,0:T(8,128)(2,1)S(1)}, u32[]{:S(2)}, u32[]{:S(2)}) %collective-permute-start.20) | collective-permute-done | bytes 524320 | tf_op jit(solution)/shard_map/ppermute | solution.py:37
  99.9 8.3 %collective-permute-done.16 = bf16[512,512]{1,0:T(8,128)(2,1)S(1)} collective-permute-done((bf16[512,512]{1,0:T(8,128)(2,1)S(1)}, bf16[512,512]{1,0:T(8,128)(2,1)S(1)}, u32[]{:S(2)}, u32[]{:S(2)}) %collective-permute-start.16) | collective-permute-done | bytes 524320 | tf_op jit(solution)/shard_map/ppermute | solution.py:37
  113.4 4.1 %dynamic-slice_bitcast_fusion.7 = (bf16[512,512]{1,0:T(8,128)(2,1)}, bf16[512,512]{1,0:T(8,128)(2,1)}, bf16[512,512]{1,0:T(8,128)(2,1)}, bf16[512,512]{1,0:T(8,1...) fusion(bf16[1,4096,512]{2,1,0:T(8,128)(2,1)} %param.8, ...), kind=kLoop, calls=%fused_computation.43 | loop fusion | bytes 8388640 | tf_op jit(solution)/shard_map/dynamic_slice | solution.py:54
  120.5 24.3 %collective-permute-done.17 = bf16[512,1024]{1,0:T(8,128)(2,1)} collective-permute-done((bf16[512,1024]{1,0:T(8,128)(2,1)}, bf16[512,1024]{1,0:T(8,128)(2,1)}, u32[]{:S(2)}, u32[]{:S(2)}) %collective-permute-start.17) | collective-permute-done | bytes 1048608 | tf_op jit(solution)/shard_map/ppermute | solution.py:37
  146.3 2.3 constant_dynamic-update-slice_fusion.3
  149.1 3.0 fusion.20
  153.7 3.0 fusion.19
  158.0 3.3 collective-permute-start.14
  163.9 1.9 collective-permute-start.19
  168.3 27.3 %collective-permute-done.9 = bf16[512,512]{1,0:T(8,128)(2,1)S(1)} collective-permute-done((bf16[512,512]{1,0:T(8,128)(2,1)S(1)}, bf16[512,512]{1,0:T(8,128)(2,1)S(1)}, u32[]{:S(2)}, u32[]{:S(2)}) %collective-permute-start.9) | collective-permute-done | bytes 524320 | tf_op jit(solution)/shard_map/ppermute | solution.py:99
  195.6 41.3 %collective-permute-done.14 = bf16[512,512]{1,0:T(8,128)(2,1)S(1)} collective-permute-done((bf16[512,512]{1,0:T(8,128)(2,1)S(1)}, bf16[512,512]{1,0:T(8,128)(2,1)S(1)}, u32[]{:S(2)}, u32[]{:S(2)}) %collective-permute-start.14) | collective-permute-done | bytes 524320 | tf_op jit(solution)/shard_map/ppermute | solution.py:99
  240.4 16.6 %collective-permute-done = bf16[512,512]{1,0:T(8,128)(2,1)S(1)} collective-permute-done((bf16[512,512]{1,0:T(8,128)(2,1)S(1)}, bf16[512,512]{1,0:T(8,128)(2,1)S(1)}, u32[]{:S(2)}, u32[]{:S(2)}) %collective-permute-start) | collective-permute-done | bytes 524320 | tf_op jit(solution)/shard_map/ppermute | solution.py:37
  258.8 32.4 %collective-permute-done.1 = bf16[512,1024]{1,0:T(8,128)(2,1)S(1)} collective-permute-done((bf16[512,1024]{1,0:T(8,128)(2,1)S(1)}, bf16[512,1024]{1,0:T(8,128)(2,1)S(1)}, u32[]{:S(2)}, u32[]{:S(2)}) %collective-permute-start.1) | collective-permute-done | bytes 1048608 | tf_op jit(solution)/shard_map/ppermute | solution.py:37
  291.6 4.3 %collective-permute-done.2 = bf16[512,2048]{1,0:T(8,128)(2,1)} collective-permute-done((bf16[512,2048]{1,0:T(8,128)(2,1)S(1)}, bf16[512,2048]{1,0:T(8,128)(2,1)}, u32[]{:S(2)}, u32[]{:S(2)}) %collective-permute-start.2) | collective-permute-done | bytes 2097184 | tf_op jit(solution)/shard_map/ppermute | solution.py:37
  295.9 17.2 %all-reduce.2.cloned.1.call-done = bf16[4096,512]{1,0:T(8,128)(2,1)} async-done(((bf16[4096,512]{1,0:T(8,128)(2,1)}), bf16[4096,512]{1,0:T(8,128)(2,1)}) %all-reduce.2.cloned.1.call-update) | async-done | bytes 4194320 | tf_op jit(solution)/shard_map/psum | solution.py:75
  313.1 3.5 %fusion.1 = f32[512,512]{1,0:T(8,128)S(1)} fusion(bf16[512,2048]{1,0:T(8,128)(2,1)} %collective-permute-done.2, bf16[4096,512]{1,0:T(8,128)(2,1)} %all-reduce.2.cloned.1.call-done), kind=kOutput, calls=%fused_computation.2 | convolution fusion | flops 1073741824 | bytes 5242880 | tf_op jit(solution)/shard_map/dot_general | solution.py:22
  316.6 10.5 %fusion = bf16[1,512,4096]{2,1,0:T(8,128)(2,1)} fusion(bf16[512,4096]{1,0:T(8,128)(2,1)} %param.11, bf16[512,4096]{1,0:T(8,128)(2,1)} %all-gather.2.cloned.1.call-done, f32[512,512]{1,0:T(8,128)S(1)} %fusion.1, bf16[4096,512]{1,0:T(8,128)(2,1)} %all-reduce.2.cloned.1.call-done, bf16[512,512]{1,0:T(8,128)(2,1)S(1)} %get-tuple-element.24, ...), kind=kOutput, calls=%fused_computation.1 | convolution fusion | flops 3240624128 | bytes 17825792 | tf_op jit(solution)/shard_map/dot_general | solution.py:13
  (106 shorter events, 38.1 us)
Async XLA Ops:
  7.4 305.7 %all-reduce.2.cloned.1.call-start = ((), (), s32[]{:S(2)}) async-start(), calls=%async_computation | async-start | bytes 8388608 | tf_op jit(solution)/shard_map/psum | solution.py:75
  7.4 26.3 %collective-permute-start.3 = (bf16[512,512]{1,0:T(8,128)(2,1)}, bf16[512,512]{1,0:T(8,128)(2,1)S(1)}, u32[]{:S(2)}, u32[]{:S(2)}) collective-permute-start(bf16[512,512]{1,0:T(8,128)(2,1)} %bitcast.47), channel_id=1, source_target_pairs={{0,8},{8,16},{16,24},{24,0},{1,9},{9,17},{17,25},{25,1},{2,10},{10... | collective-permute-start | bytes 1572872 | tf_op jit(solution)/shard_map/ppermute | solution.py:72
  8.9 33.7 %collective-permute-start.10 = (bf16[512,512]{1,0:T(8,128)(2,1)}, bf16[512,512]{1,0:T(8,128)(2,1)S(1)}, u32[]{:S(2)}, u32[]{:S(2)}) collective-permute-start(bf16[512,512]{1,0:T(8,128)(2,1)} %bitcast.48), channel_id=1, source_target_pairs={{0,16},{8,24},{16,0},{24,8},{1,17},{9,25},{17,1},{25,9},{2,18},{10... | collective-permute-start | bytes 1572872 | tf_op jit(solution)/shard_map/ppermute | solution.py:72
  13.3 32.4 %copy-start = (bf16[1,512,512]{2,1,0:T(8,128)(2,1)S(1)}, bf16[1,512,512]{2,1,0:T(8,128)(2,1)}, u32[]{:S(2)}) copy-start(bf16[1,512,512]{2,1,0:T(8,128)(2,1)} %param.6) | copy-start | bytes 1572868
  33.7 12.7 %collective-permute-start.6 = (bf16[256,512]{1,0:T(8,128)(2,1)S(1)}, bf16[256,512]{1,0:T(8,128)(2,1)S(1)}, u32[]{:S(2)}, u32[]{:S(2)}) collective-permute-start(bf16[256,512]{1,0:T(8,128)(2,1)S(1)} %get-tuple-element.28), channel_id=1, source_target_pairs={{0,4},{1,5},{2,6},{3,7},{4,0},{5,1},{6,2},{7,3},{8,12},{9,13},{10,... | collective-permute-start | bytes 786440 | tf_op jit(solution)/shard_map/ppermute | solution.py:37
  42.6 14.8 %collective-permute-start.11 = (bf16[512,512]{1,0:T(8,128)(2,1)S(1)}, bf16[512,512]{1,0:T(8,128)(2,1)S(1)}, u32[]{:S(2)}, u32[]{:S(2)}) collective-permute-start(bf16[512,512]{1,0:T(8,128)(2,1)S(1)} %collective-permute-done.10), channel_id=1, source_target_pairs={{0,4},{1,5},{2,6},{3,7},{4,0},{5,1},{6,2},{7,3},{8,12},{9,13},{10,... | collective-permute-start | bytes 1572872 | tf_op jit(solution)/shard_map/ppermute | solution.py:37
  44.2 9.2 %collective-permute-start.4 = (bf16[256,512]{1,0:T(8,128)(2,1)S(1)}, bf16[256,512]{1,0:T(8,128)(2,1)S(1)}, u32[]{:S(2)}, u32[]{:S(2)}) collective-permute-start(bf16[256,512]{1,0:T(8,128)(2,1)S(1)} %get-tuple-element.27), channel_id=1, source_target_pairs={{0,2},{1,3},{2,0},{3,1},{4,6},{5,7},{6,4},{7,5},{8,10},{9,11},{10,... | collective-permute-start | bytes 786440 | tf_op jit(solution)/shard_map/ppermute | solution.py:37
  45.7 14.0 %collective-permute-start.15 = (bf16[512,512]{1,0:T(8,128)(2,1)S(1)}, bf16[512,512]{1,0:T(8,128)(2,1)S(1)}, u32[]{:S(2)}, u32[]{:S(2)}) collective-permute-start(bf16[512,512]{1,0:T(8,128)(2,1)S(1)} %bitcast.49), channel_id=1, source_target_pairs={{0,24},{8,0},{16,8},{24,16},{1,25},{9,1},{17,9},{25,17},{2,26},{10... | collective-permute-start | bytes 1572872 | tf_op jit(solution)/shard_map/ppermute | solution.py:72
  46.5 18.2 %collective-permute-start.7 = (bf16[256,1024]{1,0:T(8,128)(2,1)S(1)}, bf16[256,1024]{1,0:T(8,128)(2,1)S(1)}, u32[]{:S(2)}, u32[]{:S(2)}) collective-permute-start(bf16[256,1024]{1,0:T(8,128)(2,1)S(1)} %pad_maximum_fusion.9), channel_id=1, source_target_pairs={{0,2},{1,3},{2,0},{3,1},{4,6},{5,7},{6,4},{7,5},{8,10},{9,11},{10,... | collective-permute-start | bytes 1572872 | tf_op jit(solution)/shard_map/ppermute | solution.py:37
  53.4 14.3 %collective-permute-start.5 = (bf16[256,1024]{1,0:T(8,128)(2,1)S(1)}, bf16[256,1024]{1,0:T(8,128)(2,1)S(1)}, u32[]{:S(2)}, u32[]{:S(2)}) collective-permute-start(bf16[256,1024]{1,0:T(8,128)(2,1)S(1)} %pad_maximum_fusion.8), channel_id=1, source_target_pairs={{0,4},{1,5},{2,6},{3,7},{4,0},{5,1},{6,2},{7,3},{8,12},{9,13},{10,... | collective-permute-start | bytes 1572872 | tf_op jit(solution)/shard_map/ppermute | solution.py:37
  57.4 52.6 %copy-start.8 = (bf16[512,512]{1,0:T(8,128)(2,1)}, bf16[512,512]{1,0:T(8,128)(2,1)S(1)}, u32[]{:S(2)}) copy-start(bf16[512,512]{1,0:T(8,128)(2,1)S(1)} %collective-permute-done.11) | copy-start | bytes 1572868
  57.6 52.4 %collective-permute-start.12 = (bf16[512,1024]{1,0:T(8,128)(2,1)S(1)}, bf16[512,1024]{1,0:T(8,128)(2,1)S(1)}, u32[]{:S(2)}, u32[]{:S(2)}) collective-permute-start(bf16[512,1024]{1,0:T(8,128)(2,1)S(1)} %pad_maximum_fusion.5), channel_id=1, source_target_pairs={{0,2},{1,3},{2,0},{3,1},{4,6},{5,7},{6,4},{7,5},{8,10},{9,11},{10,... | collective-permute-start | bytes 3145736 | tf_op jit(solution)/shard_map/ppermute | solution.py:37
  59.1 39.2 %collective-permute-start.20 = (bf16[512,512]{1,0:T(8,128)(2,1)S(1)}, bf16[512,512]{1,0:T(8,128)(2,1)S(1)}, u32[]{:S(2)}, u32[]{:S(2)}) collective-permute-start(bf16[512,512]{1,0:T(8,128)(2,1)S(1)} %bitcast.50), channel_id=1, source_target_pairs={{0,2},{1,3},{2,0},{3,1},{4,6},{5,7},{6,4},{7,5},{8,10},{9,11},{10,... | collective-permute-start | bytes 1572872 | tf_op jit(solution)/shard_map/ppermute | solution.py:37
  59.7 48.6 %collective-permute-start.16 = (bf16[512,512]{1,0:T(8,128)(2,1)S(1)}, bf16[512,512]{1,0:T(8,128)(2,1)S(1)}, u32[]{:S(2)}, u32[]{:S(2)}) collective-permute-start(bf16[512,512]{1,0:T(8,128)(2,1)S(1)} %collective-permute-done.15), channel_id=1, source_target_pairs={{0,2},{1,3},{2,0},{3,1},{4,6},{5,7},{6,4},{7,5},{8,10},{9,11},{10,... | collective-permute-start | bytes 1572872 | tf_op jit(solution)/shard_map/ppermute | solution.py:37
  79.2 69.9 %collective-permute-start.8 = (bf16[512,2048]{1,0:T(8,128)(2,1)S(1)}, bf16[512,2048]{1,0:T(8,128)(2,1)}, u32[]{:S(2)}, u32[]{:S(2)}) collective-permute-start(bf16[512,2048]{1,0:T(8,128)(2,1)S(1)} %maximum_maximum_fusion), channel_id=1, source_target_pairs={{0,1},{1,0},{2,3},{3,2},{4,5},{5,4},{6,7},{7,6},{8,9},{9,8},{10,11... | collective-permute-start | bytes 6291464 | tf_op jit(solution)/shard_map/ppermute | solution.py:37
  99.4 46.8 %collective-permute-start.21 = (bf16[512,1024]{1,0:T(8,128)(2,1)}, bf16[512,1024]{1,0:T(8,128)(2,1)}, u32[]{:S(2)}, u32[]{:S(2)}) collective-permute-start(bf16[512,1024]{1,0:T(8,128)(2,1)} %pad_maximum_fusion.7), channel_id=1, source_target_pairs={{0,4},{1,5},{2,6},{3,7},{4,0},{5,1},{6,2},{7,3},{8,12},{9,13},{10,... | collective-permute-start | bytes 3145736 | tf_op jit(solution)/shard_map/ppermute | solution.py:37
  109.4 35.4 %collective-permute-start.17 = (bf16[512,1024]{1,0:T(8,128)(2,1)}, bf16[512,1024]{1,0:T(8,128)(2,1)}, u32[]{:S(2)}, u32[]{:S(2)}) collective-permute-start(bf16[512,1024]{1,0:T(8,128)(2,1)} %pad_maximum_fusion.6), channel_id=1, source_target_pairs={{0,4},{1,5},{2,6},{3,7},{4,0},{5,1},{6,2},{7,3},{8,12},{9,13},{10,... | collective-permute-start | bytes 3145736 | tf_op jit(solution)/shard_map/ppermute | solution.py:37
  111.8 41.9 %collective-permute-start.13 = (bf16[512,2048]{1,0:T(8,128)(2,1)}, bf16[512,2048]{1,0:T(8,128)(2,1)}, u32[]{:S(2)}, u32[]{:S(2)}) collective-permute-start(bf16[512,2048]{1,0:T(8,128)(2,1)} %pad_maximum_fusion.3), channel_id=1, source_target_pairs={{0,1},{1,0},{2,3},{3,2},{4,5},{5,4},{6,7},{7,6},{8,9},{9,8},{10,11... | collective-permute-start | bytes 6291464 | tf_op jit(solution)/shard_map/ppermute | solution.py:37
  117.5 199.1 %all-gather.2.cloned.1.call-start = ((), (), s32[]{:S(2)}) async-start(), calls=%async_computation.1 | async-start | bytes 4718592 | tf_op jit(solution)/shard_map/all_gather | solution.py:102
  117.6 31.5 %copy-start.18 = (bf16[512,512]{1,0:T(8,128)(2,1)S(1)}, bf16[512,512]{1,0:T(8,128)(2,1)}, u32[]{:S(2)}) copy-start(bf16[512,512]{1,0:T(8,128)(2,1)} %get-tuple-element.16) | copy-start | bytes 1572868
  117.6 31.5 %copy-start.19 = (bf16[512,512]{1,0:T(8,128)(2,1)S(1)}, bf16[512,512]{1,0:T(8,128)(2,1)}, u32[]{:S(2)}) copy-start(bf16[512,512]{1,0:T(8,128)(2,1)} %get-tuple-element.17) | copy-start | bytes 1572868
  117.6 31.5 %copy-start.20 = (bf16[512,512]{1,0:T(8,128)(2,1)S(1)}, bf16[512,512]{1,0:T(8,128)(2,1)}, u32[]{:S(2)}) copy-start(bf16[512,512]{1,0:T(8,128)(2,1)} %get-tuple-element.21) | copy-start | bytes 1572868
  117.6 31.5 %copy-start.21 = (bf16[512,512]{1,0:T(8,128)(2,1)S(1)}, bf16[512,512]{1,0:T(8,128)(2,1)}, u32[]{:S(2)}) copy-start(bf16[512,512]{1,0:T(8,128)(2,1)} %get-tuple-element.22) | copy-start | bytes 1572868
  146.2 15.2 %collective-permute-start.18 = (bf16[512,2048]{1,0:T(8,128)(2,1)S(1)}, bf16[512,2048]{1,0:T(8,128)(2,1)S(1)}, u32[]{:S(2)}, u32[]{:S(2)}) collective-permute-start(bf16[512,2048]{1,0:T(8,128)(2,1)S(1)} %constant_dynamic-update-slice_fusion), channel_id=1, source_target_pairs={{0,1},{1,0},{2,3},{3,2},{4,5},{5,4},{6,7},{7,6},{8,9},{9,8},{10,11... | collective-permute-start | bytes 6291464 | tf_op jit(solution)/shard_map/ppermute | solution.py:37
  148.6 17.2 %collective-permute-start.22 = (bf16[512,2048]{1,0:T(8,128)(2,1)}, bf16[512,2048]{1,0:T(8,128)(2,1)S(1)}, u32[]{:S(2)}, u32[]{:S(2)}) collective-permute-start(bf16[512,2048]{1,0:T(8,128)(2,1)} %constant_dynamic-update-slice_fusion.3), channel_id=1, source_target_pairs={{0,1},{1,0},{2,3},{3,2},{4,5},{5,4},{6,7},{7,6},{8,9},{9,8},{10,11... | collective-permute-start | bytes 6291464 | tf_op jit(solution)/shard_map/ppermute | solution.py:37
  153.5 42.1 %collective-permute-start.9 = (bf16[512,512]{1,0:T(8,128)(2,1)S(1)}, bf16[512,512]{1,0:T(8,128)(2,1)S(1)}, u32[]{:S(2)}, u32[]{:S(2)}) collective-permute-start(bf16[512,512]{1,0:T(8,128)(2,1)S(1)} %fusion.8), channel_id=1, source_target_pairs={{0,24},{8,0},{16,8},{24,16},{1,25},{9,1},{17,9},{25,17},{2,26},{10... | collective-permute-start | bytes 1572872 | tf_op jit(solution)/shard_map/ppermute | solution.py:99
  158.0 78.8 %collective-permute-start.14 = (bf16[512,512]{1,0:T(8,128)(2,1)S(1)}, bf16[512,512]{1,0:T(8,128)(2,1)S(1)}, u32[]{:S(2)}, u32[]{:S(2)}) collective-permute-start(bf16[512,512]{1,0:T(8,128)(2,1)S(1)} %fusion.9), channel_id=1, source_target_pairs={{0,16},{8,24},{16,0},{24,8},{1,17},{9,25},{17,1},{25,9},{2,18},{10... | collective-permute-start | bytes 1572872 | tf_op jit(solution)/shard_map/ppermute | solution.py:99
  163.9 73.7 %collective-permute-start.19 = (bf16[512,512]{1,0:T(8,128)(2,1)S(1)}, bf16[512,512]{1,0:T(8,128)(2,1)S(1)}, u32[]{:S(2)}, u32[]{:S(2)}) collective-permute-start(bf16[512,512]{1,0:T(8,128)(2,1)S(1)} %fusion.10), channel_id=1, source_target_pairs={{0,8},{8,16},{16,24},{24,0},{1,9},{9,17},{17,25},{25,1},{2,10},{10... | collective-permute-start | bytes 1572872 | tf_op jit(solution)/shard_map/ppermute | solution.py:99
  167.0 71.6 %copy-start.4 = (bf16[1,512,512]{2,1,0:T(8,128)(2,1)S(1)}, bf16[1,512,512]{2,1,0:T(8,128)(2,1)}, u32[]{:S(2)}) copy-start(bf16[1,512,512]{2,1,0:T(8,128)(2,1)} %param.7) | copy-start | bytes 1572868
  238.6 18.4 %collective-permute-start = (bf16[512,512]{1,0:T(8,128)(2,1)S(1)}, bf16[512,512]{1,0:T(8,128)(2,1)S(1)}, u32[]{:S(2)}, u32[]{:S(2)}) collective-permute-start(bf16[512,512]{1,0:T(8,128)(2,1)S(1)} %bitcast.53), channel_id=1, source_target_pairs={{0,4},{1,5},{2,6},{3,7},{4,0},{5,1},{6,2},{7,3},{8,12},{9,13},{10,... | collective-permute-start | bytes 1572872 | tf_op jit(solution)/shard_map/ppermute | solution.py:37
  257.1 34.0 %collective-permute-start.1 = (bf16[512,1024]{1,0:T(8,128)(2,1)S(1)}, bf16[512,1024]{1,0:T(8,128)(2,1)S(1)}, u32[]{:S(2)}, u32[]{:S(2)}) collective-permute-start(bf16[512,1024]{1,0:T(8,128)(2,1)S(1)} %pad_maximum_fusion.4), channel_id=1, source_target_pairs={{0,2},{1,3},{2,0},{3,1},{4,6},{5,7},{6,4},{7,5},{8,10},{9,11},{10,... | collective-permute-start | bytes 3145736 | tf_op jit(solution)/shard_map/ppermute | solution.py:37
  291.5 4.4 %collective-permute-start.2 = (bf16[512,2048]{1,0:T(8,128)(2,1)S(1)}, bf16[512,2048]{1,0:T(8,128)(2,1)}, u32[]{:S(2)}, u32[]{:S(2)}) collective-permute-start(bf16[512,2048]{1,0:T(8,128)(2,1)S(1)} %pad_maximum_fusion), channel_id=1, source_target_pairs={{0,1},{1,0},{2,3},{3,2},{4,5},{5,4},{6,7},{7,6},{8,9},{9,8},{10,11... | collective-permute-start | bytes 6291464 | tf_op jit(solution)/shard_map/ppermute | solution.py:37
  (16 other events, 106.0 us)
Sparse Core Ops, SparseCore 0:
  117.7 195.3 all-reduce.1
Sparse Core Ops, SparseCore 1:
  238.7 52.2 all-gather.1

commit v5 on v4

v5 whole, which is shorter than its diff:
```python
import jax
import jax.numpy as jnp
from jax import lax
from jax.sharding import PartitionSpec as P

damping = 0.01
ROOM = 2**25


def product_and_divide(rot_out, all_rot_in, eig_lambda, tokens):
    denom = eig_lambda.astype(jnp.float32) + damping
    contract = (((0,), (0,)), ((), ()))
    product = lax.dot_general(rot_out, all_rot_in, contract, preferred_element_type=jnp.float32) / tokens
    return (product / denom).astype(jnp.bfloat16)[None]


def from_owner(held, owner):
    return lax.psum(jnp.where(lax.axis_index("dp") == owner, held, jnp.zeros_like(held)), "dp")


def dot(a, b):
    return jnp.dot(a, b, preferred_element_type=jnp.float32)


def move_bases(acts, grads, basis_in_held, basis_out_held, owners, eig_lambda):
    column = lax.axis_index("tensor")
    basis_in = from_owner(basis_in_held[0], owners[0, column])
    basis_out = from_owner(basis_out_held[0], owners[1, column])
    rot_in = dot(lax.all_gather(acts[0], "tensor", axis=1, tiled=True), basis_in).astype(jnp.bfloat16)
    rot_out = dot(lax.all_gather(grads[0], "tensor", axis=1, tiled=True), basis_out).astype(jnp.bfloat16)
    return product_and_divide(
        rot_out, lax.all_gather(rot_in, "tensor", axis=1, tiled=True), eig_lambda, acts.shape[1]
    )


def swap(block, bit, n):
    return lax.ppermute(block, "tensor", [(j, j ^ bit) for j in range(n)])


def side_by_side(found):
    return jnp.concatenate([found[i] for i in sorted(found)], axis=1)


def exchange(found, bit, n):
    order = sorted(found)
    came = swap(side_by_side(found), bit, n)
    width = came.shape[1] // len(order)
    return found | {i ^ bit: came[:, at * width : (at + 1) * width] for at, i in enumerate(order)}


def in_order(held, column, n):
    width = held.shape[0] // n
    offsets = list(range(0, n, 2)) + list(range(1, n, 2))
    blocks = [lax.dynamic_slice(held, ((column ^ i) * width, 0), (width, held.shape[1])) for i in offsets]
    return jnp.concatenate(blocks, axis=0)


def after(value, *others):
    return lax.optimization_barrier((value, *others))[0]


def move_inputs(n_dp, n, acts, grads, basis_in_held, basis_out_held, owners, eig_lambda):
    column = lax.axis_index("tensor")
    me = lax.axis_index("dp")
    mine = (acts[0], grads[0])
    held = (basis_in_held[0], basis_out_held[0])
    behind = [(me - owners[side, column]) % n_dp for side in (0, 1)]
    half = held[0].shape[0] // 2
    bits = []
    while 2 << len(bits) < n:
        bits.append(2 << len(bits))

    keys = [(side, i) for side in (0, 1) for i in range(1, n_dp)]
    pieces = {(side, i): lax.ppermute(mine[side], "dp", [(z, (z - i) % n_dp) for z in range(n_dp)]) for side, i in keys}
    gathered = [lax.all_gather(block, "tensor", axis=1, tiled=True) for block in mine]
    ordered = [in_order(block, column, n) for block in held]
    rotated = [dot(gathered[side], held[side]).astype(jnp.bfloat16) for side in (0, 1)]

    def finish(key, found):
        side, i = key
        even = side_by_side(found)
        odd = swap(even, 1, n)
        rot = (dot(even, ordered[side][:half]) + dot(odd, ordered[side][half:])).astype(jnp.bfloat16)
        rot = lax.ppermute(rot, "dp", [(z, (z + i) % n_dp) for z in range(n_dp)])
        rotated[side] = jnp.where(behind[side] == i, rot, rotated[side])

    last = None
    for at in range(0, len(keys), 2):
        pair = keys[at : at + 2]
        found = [{0: pieces[key]} for key in pair]
        for level in range(len(bits)):
            if last is not None:
                found = after(found, last)
            last = found
            found = [exchange(f, (bits, bits[::-1])[p][level], n) for p, f in enumerate(found)]
        for key, f in zip(pair, found):
            finish(key, f)

    rot_in, rot_out = rotated
    all_rot_in = lax.all_gather(rot_in, "tensor", axis=1, tiled=True)
    return product_and_divide(rot_out, all_rot_in, eig_lambda, acts.shape[1])


def solution(mesh):
    placed = (
        P("dp", None, "tensor"),
        P("dp", None, "tensor"),
        P("dp", None, "tensor"),
        P("dp", None, "tensor"),
        P(),
        P("tensor", None),
    )
    n_dp, n_tensor = mesh.shape["dp"], mesh.shape["tensor"]

    def step(acts, *rest):
        whole = 2 * n_dp * acts.shape[1] * acts.shape[2] * n_tensor * acts.dtype.itemsize
        if whole <= ROOM and n_tensor & (n_tensor - 1) == 0:
            return move_inputs(n_dp, n_tensor, acts, *rest)
        return move_bases(acts, *rest)

    return jax.shard_map(step, mesh=mesh, in_specs=placed, out_specs=P("dp", "tensor", None), check_vma=False)
```

time: 338 us -> 337 us (level)
  other arithmetic: 32.5 us -> 7.9 us
  matrix products: 27.4 us -> 42.4 us
  starting transfers between devices: 22.6 us -> 33.4 us
  local copies, waits for them, and re-layouts: 13.2 us -> 8.94 us
    ppermute x6 -> x12, waiting for transfers between devices: 83.5 us -> 113 us  [the longest x6 63.7 us: finish(): rot = lax.ppermute(rot, 'dp', [(z, (z + i) % n_dp) for z in range(n_dp)])]
    psum x1 -> x0, waiting for transfers between devices: 17.2 us -> none  [move_inputs(): basis_out = lax.psum(masked_out, 'dp')]
    unnamed x7 -> x0, other arithmetic: 13.5 us -> none
    concatenate x10 -> x9, other arithmetic: 18 us -> 5.95 us  [side_by_side(): return jnp.concatenate([found[i] for i in sorted(found)], axis=1)]
    dot_general x9 -> x13, matrix products: 17 us -> 29 us  [dot(): return jnp.dot(a, b, preferred_element_type=jnp.float32)]
    ppermute x17 -> x18, waiting for transfers between devices: 121 us -> 111 us  [swap(): return lax.ppermute(block, 'tensor', [(j, j ^ bit) for j in range(n)])]
    ppermute x6 -> x12, starting transfers between devices: 8.11 us -> 16.7 us  [the longest x6 8.38 us: finish(): rot = lax.ppermute(rot, 'dp', [(z, (z + i) % n_dp) for z in range(n_dp)])]
    ppermute x17 -> x18, starting transfers between devices: 14.5 us -> 16.6 us  [swap(): return lax.ppermute(block, 'tensor', [(j, j ^ bit) for j in range(n)])]
  transfers between devices with their start and end apart: 25 -> 33, of which waited for: 16 -> 13; matrix products, arithmetic and copies ran while one was open for 18% -> 14% of each run, Pallas kernels for 0% -> 0%
where the time goes in v5:
time: 337 us; the launch traced here: 332 us
  waiting for transfers between devices  225 us (67%)
  matrix products  42.4 us (13%)
  starting transfers between devices  33.4 us (10%)
  between operations  14.8 us (4%)
  local copies, waits for them, and re-layouts  8.94 us (3%)
  other arithmetic  7.9 us (2%)
    ppermute x18, waiting for transfers between devices, swap(): return lax.ppermute(block, 'tensor', [(j, j ^ bit) for j in range(n)])  111 us
    ppermute x6, waiting for transfers between devices, finish(): rot = lax.ppermute(rot, 'dp', [(z, (z + i) % n_dp) for z in range(n_dp)])  63.7 us
    ppermute x6, waiting for transfers between devices, move_inputs(): lax.ppermute(mine[side], 'dp', [(z, (z - i) % n_dp) for z in range(n_dp)])  49.1 us
    dot_general x13, matrix products, dot(): return jnp.dot(a, b, preferred_element_type=jnp.float32)  29 us
    ppermute x18, starting transfers between devices, swap(): return lax.ppermute(block, 'tensor', [(j, j ^ bit) for j in range(n)])  16.6 us
    dot_general x1, matrix products, product_and_divide(): lax.dot_general(rot_out, all_rot_in, contract, preferred_element_type=jnp...  13.4 us
    ppermute x6, starting transfers between devices, finish(): rot = lax.ppermute(rot, 'dp', [(z, (z + i) % n_dp) for z in range(n_dp)])  8.38 us
    ppermute x6, starting transfers between devices, move_inputs(): lax.ppermute(mine[side], 'dp', [(z, (z - i) % n_dp) for z in range(n_dp)])  8.34 us
  transfers between devices with their start and end apart: 33, of which 13 were waited for; matrix products, arithmetic and copies ran while one was open for 14% of the time, Pallas kernels for 0%

profile of v5, /device:TPU:16, one launch (start us, length us, event | category | flops | bytes accessed | tf_op | source)
XLA Modules:
  0.0 332.1 jit_solution(13374281866645787866)
XLA Ops:
  7.8 3.5 %collective-permute-start.6 = (bf16[512,512]{1,0:T(8,128)(2,1)}, bf16[512,512]{1,0:T(8,128)(2,1)S(1)}, u32[]{:S(2)}, u32[]{:S(2)}) collective-permute-start(bf16[512,512]{1,0:T(8,128)(2,1)} %bitcast.2), channel_id=1, source_target_pairs={{0,16},{8,24},{16,0},{24,8},{1,17},{9,25},{17,1},{25,9},{2,18},{10... | collective-permute-start | bytes 1572872 | tf_op jit(solution)/shard_map/ppermute | solution.py:74
  11.3 11.1 %collective-permute-done.4 = bf16[512,512]{1,0:T(8,128)(2,1)S(1)} collective-permute-done((bf16[512,512]{1,0:T(8,128)(2,1)}, bf16[512,512]{1,0:T(8,128)(2,1)S(1)}, u32[]{:S(2)}, u32[]{:S(2)}) %collective-permute-start.4) | collective-permute-done | bytes 524320 | tf_op jit(solution)/shard_map/ppermute | solution.py:74
  23.9 17.9 %collective-permute-done.6 = bf16[512,512]{1,0:T(8,128)(2,1)S(1)} collective-permute-done((bf16[512,512]{1,0:T(8,128)(2,1)}, bf16[512,512]{1,0:T(8,128)(2,1)S(1)}, u32[]{:S(2)}, u32[]{:S(2)}) %collective-permute-start.6) | collective-permute-done | bytes 524320 | tf_op jit(solution)/shard_map/ppermute | solution.py:74
  41.8 1.5 collective-permute-start.7
  43.4 14.4 %collective-permute-done.7 = bf16[512,512]{1,0:T(8,128)(2,1)S(1)} collective-permute-done((bf16[512,512]{1,0:T(8,128)(2,1)S(1)}, bf16[512,512]{1,0:T(8,128)(2,1)S(1)}, u32[]{:S(2)}, u32[]{:S(2)}) %collective-permute-start.7) | collective-permute-done | bytes 524320 | tf_op jit(solution)/shard_map/ppermute | solution.py:37
  58.5 2.6 collective-permute-start.2
  61.3 1.6 collective-permute-start.24
  62.8 20.1 %collective-permute-done.2 = bf16[512,512]{1,0:T(8,128)(2,1)S(1)} collective-permute-done((bf16[512,512]{1,0:T(8,128)(2,1)}, bf16[512,512]{1,0:T(8,128)(2,1)S(1)}, u32[]{:S(2)}, u32[]{:S(2)}) %collective-permute-start.2) | collective-permute-done | bytes 524320 | tf_op jit(solution)/shard_map/ppermute | solution.py:74
  87.6 8.9 %collective-permute-done.27 = bf16[512,1024]{1,0:T(8,128)(2,1)S(1)} collective-permute-done((bf16[512,1024]{1,0:T(8,128)(2,1)S(1)}, bf16[512,1024]{1,0:T(8,128)(2,1)S(1)}, u32[]{:S(2)}, u32[]{:S(2)}) %collective-permute-start.27) | collective-permute-done | bytes 1048608 | tf_op jit(solution)/shard_map/ppermute | solution.py:37
  97.5 14.9 %collective-permute-done.8 = bf16[512,512]{1,0:T(8,128)(2,1)S(1)} collective-permute-done((bf16[512,512]{1,0:T(8,128)(2,1)S(1)}, bf16[512,512]{1,0:T(8,128)(2,1)S(1)}, u32[]{:S(2)}, u32[]{:S(2)}) %collective-permute-start.8) | collective-permute-done | bytes 524320 | tf_op jit(solution)/shard_map/ppermute | solution.py:37
  119.3 2.5 dynamic-slice_bitcast_fusion.7
  121.9 15.3 %collective-permute-done.21 = bf16[512,1024]{1,0:T(8,128)(2,1)} collective-permute-done((bf16[512,1024]{1,0:T(8,128)(2,1)}, bf16[512,1024]{1,0:T(8,128)(2,1)}, u32[]{:S(2)}, u32[]{:S(2)}) %collective-permute-start.21) | collective-permute-done | bytes 1048608 | tf_op jit(solution)/shard_map/ppermute | solution.py:37
  139.8 2.8 fusion.29
  142.6 3.7 %fusion.22 = bf16[512,512]{1,0:T(8,128)(2,1)} fusion(f32[512,512]{1,0:T(8,128)S(1)} %fusion.29, bf16[512,2048]{1,0:T(8,128)(2,1)} %constant_dynamic-update-slice_fusion.6, bf16[512,512]{1,0:T(8,128)(2,1)S(1)} %get-tuple-element.49, bf16[512,512]{1,0:T(8,128)(2,1)S(1)} %get-tuple-element.50, bf16[512,512]{1,0:T(8,128)(2,1)S(1)} %get-tuple-element.51, ...), kind=kOutput, calls=%fused_computation.28 | convolution fusion | flops 1082654720 | bytes 5767168 | tf_op jit(solution)/shard_map/dot_general | solution.py:22
  147.6 2.8 fusion.30
  150.4 2.1 fusion.21
  152.5 1.9 collective-permute-start.26
  155.7 2.0 fusion.20
  157.7 2.8 collective-permute-start.23
  160.5 5.8 %fusion.12 = bf16[512,512]{1,0:T(8,128)(2,1)S(1)} fusion(bf16[1,4096,512]{2,1,0:T(8,128)(2,1)} %param.8, bf16[1,512,4096]{2,1,0:T(8,128)(2,1)} %all-gather.10.cloned.1.call-done), kind=kOutput, calls=%fused_computation.22 | convolution fusion | flops 2147745792 | bytes 8912896 | tf_op jit(solution)/shard_map/dot_general | solution.py:22
  166.3 21.0 %collective-permute-done.29 = bf16[512,512]{1,0:T(8,128)(2,1)S(1)} collective-permute-done((bf16[512,512]{1,0:T(8,128)(2,1)}, bf16[512,512]{1,0:T(8,128)(2,1)S(1)}, u32[]{:S(2)}, u32[]{:S(2)}) %collective-permute-start.29) | collective-permute-done | bytes 524320 | tf_op jit(solution)/shard_map/ppermute | solution.py:84
  188.8 8.3 %collective-permute-done.23 = bf16[512,512]{1,0:T(8,128)(2,1)} collective-permute-done((bf16[512,512]{1,0:T(8,128)(2,1)}, bf16[512,512]{1,0:T(8,128)(2,1)}, u32[]{:S(2)}, u32[]{:S(2)}) %collective-permute-start.23) | collective-permute-done | bytes 524320 | tf_op jit(solution)/shard_map/ppermute | solution.py:84
  197.1 2.0 select_select_fusion
  199.9 28.7 %collective-permute-done.10 = bf16[512,512]{1,0:T(8,128)(2,1)S(1)} collective-permute-done((bf16[512,512]{1,0:T(8,128)(2,1)S(1)}, bf16[512,512]{1,0:T(8,128)(2,1)S(1)}, u32[]{:S(2)}, u32[]{:S(2)}) %collective-permute-start.10) | collective-permute-done | bytes 524320 | tf_op jit(solution)/shard_map/ppermute | solution.py:37
  228.7 1.9 collective-permute-start.15
  232.3 2.0 collective-permute-start.12
  234.5 28.7 %collective-permute-done.15 = bf16[512,1024]{1,0:T(8,128)(2,1)S(1)} collective-permute-done((bf16[512,1024]{1,0:T(8,128)(2,1)S(1)}, bf16[512,1024]{1,0:T(8,128)(2,1)S(1)}, u32[]{:S(2)}, u32[]{:S(2)}) %collective-permute-start.15) | collective-permute-done | bytes 1048608 | tf_op jit(solution)/shard_map/ppermute | solution.py:37
  271.3 2.0 collective-permute-start.17
  274.6 2.3 fusion.17
  277.8 28.2 %collective-permute-done.20 = bf16[512,512]{1,0:T(8,128)(2,1)S(1)} collective-permute-done((bf16[512,512]{1,0:T(8,128)(2,1)S(1)}, bf16[512,512]{1,0:T(8,128)(2,1)S(1)}, u32[]{:S(2)}, u32[]{:S(2)}) %collective-permute-start.20) | collective-permute-done | bytes 524320 | tf_op jit(solution)/shard_map/ppermute | solution.py:84
  306.0 6.2 %collective-permute-done.14 = bf16[512,512]{1,0:T(8,128)(2,1)S(1)} collective-permute-done((bf16[512,512]{1,0:T(8,128)(2,1)S(1)}, bf16[512,512]{1,0:T(8,128)(2,1)S(1)}, u32[]{:S(2)}, u32[]{:S(2)}) %collective-permute-start.14) | collective-permute-done | bytes 524320 | tf_op jit(solution)/shard_map/ppermute | solution.py:84
  312.2 13.4 %fusion = bf16[1,512,4096]{2,1,0:T(8,128)(2,1)} fusion(bf16[512,4096]{1,0:T(8,128)(2,1)} %param.11, bf16[512,4096]{1,0:T(8,128)(2,1)} %all-gather.6.cloned.1.call-done, bf16[512,512]{1,0:T(8,128)(2,1)S(1)} %collective-permute-done.14, bf16[512,512]{1,0:T(8,128)(2,1)S(1)} %collective-permute-done.17, bf16[512,512]{1,0:T(8,128)(2,1)S(1)} %collective-permute-done.20, ...), kind=kOutput, calls=%fused_computation.1 | convolution fusion | flops 4306501632 | bytes 22544388 | tf_op jit(solution)/shard_map/dot_general | solution.py:13
  (116 shorter events, 34.2 us)
Async XLA Ops:
  6.5 154.0 %all-gather.10.cloned.1.call-start = ((), (), s32[]{:S(2)}) async-start(), calls=%async_computation.2 | async-start | bytes 4718592 | tf_op jit(solution)/shard_map/all_gather | solution.py:75
  7.3 304.9 %all-gather.8.cloned.1.call-start = ((), (), s32[]{:S(2)}) async-start(), calls=%async_computation.1 | async-start | bytes 4718592 | tf_op jit(solution)/shard_map/all_gather | solution.py:75
  7.3 15.1 %collective-permute-start.4 = (bf16[512,512]{1,0:T(8,128)(2,1)}, bf16[512,512]{1,0:T(8,128)(2,1)S(1)}, u32[]{:S(2)}, u32[]{:S(2)}) collective-permute-start(bf16[512,512]{1,0:T(8,128)(2,1)} %bitcast.2), channel_id=1, source_target_pairs={{0,24},{8,0},{16,8},{24,16},{1,25},{9,1},{17,9},{25,17},{2,26},{10... | collective-permute-start | bytes 1572872 | tf_op jit(solution)/shard_map/ppermute | solution.py:74
  7.8 34.0 %collective-permute-start.6 = (bf16[512,512]{1,0:T(8,128)(2,1)}, bf16[512,512]{1,0:T(8,128)(2,1)S(1)}, u32[]{:S(2)}, u32[]{:S(2)}) collective-permute-start(bf16[512,512]{1,0:T(8,128)(2,1)} %bitcast.2), channel_id=1, source_target_pairs={{0,16},{8,24},{16,0},{24,8},{1,17},{9,25},{17,1},{25,9},{2,18},{10... | collective-permute-start | bytes 1572872 | tf_op jit(solution)/shard_map/ppermute | solution.py:74
  22.4 21.0 %collective-permute-start.5 = (bf16[512,512]{1,0:T(8,128)(2,1)S(1)}, bf16[512,512]{1,0:T(8,128)(2,1)S(1)}, u32[]{:S(2)}, u32[]{:S(2)}) collective-permute-start(bf16[512,512]{1,0:T(8,128)(2,1)S(1)} %collective-permute-done.4), channel_id=1, source_target_pairs={{0,2},{1,3},{2,0},{3,1},{4,6},{5,7},{6,4},{7,5},{8,10},{9,11},{10,... | collective-permute-start | bytes 1572872 | tf_op jit(solution)/shard_map/ppermute | solution.py:37
  41.8 16.0 %collective-permute-start.7 = (bf16[512,512]{1,0:T(8,128)(2,1)S(1)}, bf16[512,512]{1,0:T(8,128)(2,1)S(1)}, u32[]{:S(2)}, u32[]{:S(2)}) collective-permute-start(bf16[512,512]{1,0:T(8,128)(2,1)S(1)} %collective-permute-done.6), channel_id=1, source_target_pairs={{0,4},{1,5},{2,6},{3,7},{4,0},{5,1},{6,2},{7,3},{8,12},{9,13},{10,... | collective-permute-start | bytes 1572872 | tf_op jit(solution)/shard_map/ppermute | solution.py:37
  43.3 268.9 %all-gather.6.cloned.1.call-start = ((), (), s32[]{:S(2)}) async-start(), calls=%async_computation | async-start | bytes 4718592 | tf_op jit(solution)/shard_map/all_gather | solution.py:100
  57.9 38.6 %collective-permute-start.27 = (bf16[512,1024]{1,0:T(8,128)(2,1)S(1)}, bf16[512,1024]{1,0:T(8,128)(2,1)S(1)}, u32[]{:S(2)}, u32[]{:S(2)}) collective-permute-start(bf16[512,1024]{1,0:T(8,128)(2,1)S(1)} %pad_maximum_fusion.12), channel_id=1, source_target_pairs={{0,4},{1,5},{2,6},{3,7},{4,0},{5,1},{6,2},{7,3},{8,12},{9,13},{10,... | collective-permute-start | bytes 3145736 | tf_op jit(solution)/shard_map/ppermute | solution.py:37
  58.5 24.4 %collective-permute-start.2 = (bf16[512,512]{1,0:T(8,128)(2,1)}, bf16[512,512]{1,0:T(8,128)(2,1)S(1)}, u32[]{:S(2)}, u32[]{:S(2)}) collective-permute-start(bf16[512,512]{1,0:T(8,128)(2,1)} %bitcast.2), channel_id=1, source_target_pairs={{0,8},{8,16},{16,24},{24,0},{1,9},{9,17},{17,25},{25,1},{2,10},{10... | collective-permute-start | bytes 1572872 | tf_op jit(solution)/shard_map/ppermute | solution.py:74
  61.1 21.8 %collective-permute-start.3 = (bf16[512,512]{1,0:T(8,128)(2,1)}, bf16[512,512]{1,0:T(8,128)(2,1)S(1)}, u32[]{:S(2)}, u32[]{:S(2)}) collective-permute-start(bf16[512,512]{1,0:T(8,128)(2,1)} %bitcast.1), channel_id=1, source_target_pairs={{0,24},{8,0},{16,8},{24,16},{1,25},{9,1},{17,9},{25,17},{2,26},{10... | collective-permute-start | bytes 1572872 | tf_op jit(solution)/shard_map/ppermute | solution.py:74
  61.3 54.0 %collective-permute-start.24 = (bf16[512,1024]{1,0:T(8,128)(2,1)S(1)}, bf16[512,1024]{1,0:T(8,128)(2,1)S(1)}, u32[]{:S(2)}, u32[]{:S(2)}) collective-permute-start(bf16[512,1024]{1,0:T(8,128)(2,1)S(1)} %pad_maximum_fusion.11), channel_id=1, source_target_pairs={{0,2},{1,3},{2,0},{3,1},{4,6},{5,7},{6,4},{7,5},{8,10},{9,11},{10,... | collective-permute-start | bytes 3145736 | tf_op jit(solution)/shard_map/ppermute | solution.py:37
  83.0 29.5 %collective-permute-start.8 = (bf16[512,512]{1,0:T(8,128)(2,1)S(1)}, bf16[512,512]{1,0:T(8,128)(2,1)S(1)}, u32[]{:S(2)}, u32[]{:S(2)}) collective-permute-start(bf16[512,512]{1,0:T(8,128)(2,1)S(1)} %collective-permute-done.2), channel_id=1, source_target_pairs={{0,2},{1,3},{2,0},{3,1},{4,6},{5,7},{6,4},{7,5},{8,10},{9,11},{10,... | collective-permute-start | bytes 1572872 | tf_op jit(solution)/shard_map/ppermute | solution.py:37
  84.4 28.1 %collective-permute-start.9 = (bf16[512,512]{1,0:T(8,128)(2,1)S(1)}, bf16[512,512]{1,0:T(8,128)(2,1)S(1)}, u32[]{:S(2)}, u32[]{:S(2)}) collective-permute-start(bf16[512,512]{1,0:T(8,128)(2,1)S(1)} %collective-permute-done.3), channel_id=1, source_target_pairs={{0,4},{1,5},{2,6},{3,7},{4,0},{5,1},{6,2},{7,3},{8,12},{9,13},{10,... | collective-permute-start | bytes 1572872 | tf_op jit(solution)/shard_map/ppermute | solution.py:37
  97.5 42.2 %collective-permute-start.28 = (bf16[512,2048]{1,0:T(8,128)(2,1)}, bf16[512,2048]{1,0:T(8,128)(2,1)}, u32[]{:S(2)}, u32[]{:S(2)}) collective-permute-start(bf16[512,2048]{1,0:T(8,128)(2,1)} %constant_dynamic-update-slice_fusion.6), channel_id=1, source_target_pairs={{0,1},{1,0},{2,3},{3,2},{4,5},{5,4},{6,7},{7,6},{8,9},{9,8},{10,11... | collective-permute-start | bytes 6291464 | tf_op jit(solution)/shard_map/ppermute | solution.py:37
  113.7 23.5 %collective-permute-start.21 = (bf16[512,1024]{1,0:T(8,128)(2,1)}, bf16[512,1024]{1,0:T(8,128)(2,1)}, u32[]{:S(2)}, u32[]{:S(2)}) collective-permute-start(bf16[512,1024]{1,0:T(8,128)(2,1)} %pad_maximum_fusion.10), channel_id=1, source_target_pairs={{0,4},{1,5},{2,6},{3,7},{4,0},{5,1},{6,2},{7,3},{8,12},{9,13},{10,... | collective-permute-start | bytes 3145736 | tf_op jit(solution)/shard_map/ppermute | solution.py:37
  116.3 31.3 %collective-permute-start.25 = (bf16[512,2048]{1,0:T(8,128)(2,1)S(1)}, bf16[512,2048]{1,0:T(8,128)(2,1)}, u32[]{:S(2)}, u32[]{:S(2)}) collective-permute-start(bf16[512,2048]{1,0:T(8,128)(2,1)S(1)} %pad_maximum_fusion.6), channel_id=1, source_target_pairs={{0,1},{1,0},{2,3},{3,2},{4,5},{5,4},{6,7},{7,6},{8,9},{9,8},{10,11... | collective-permute-start | bytes 6291464 | tf_op jit(solution)/shard_map/ppermute | solution.py:37
  116.3 82.8 %collective-permute-start = (bf16[512,512]{1,0:T(8,128)(2,1)}, bf16[512,512]{1,0:T(8,128)(2,1)S(1)}, u32[]{:S(2)}, u32[]{:S(2)}) collective-permute-start(bf16[512,512]{1,0:T(8,128)(2,1)} %bitcast.1), channel_id=1, source_target_pairs={{0,16},{8,24},{16,0},{24,8},{1,17},{9,25},{17,1},{25,9},{2,18},{10... | collective-permute-start | bytes 1572872 | tf_op jit(solution)/shard_map/ppermute | solution.py:74
  117.6 81.5 %collective-permute-start.1 = (bf16[512,512]{1,0:T(8,128)(2,1)}, bf16[512,512]{1,0:T(8,128)(2,1)}, u32[]{:S(2)}, u32[]{:S(2)}) collective-permute-start(bf16[512,512]{1,0:T(8,128)(2,1)} %bitcast.1), channel_id=1, source_target_pairs={{0,8},{8,16},{16,24},{24,0},{1,9},{9,17},{17,25},{25,1},{2,10},{10... | collective-permute-start | bytes 1572872 | tf_op jit(solution)/shard_map/ppermute | solution.py:74
  138.6 15.9 %collective-permute-start.22 = (bf16[512,2048]{1,0:T(8,128)(2,1)S(1)}, bf16[512,2048]{1,0:T(8,128)(2,1)S(1)}, u32[]{:S(2)}, u32[]{:S(2)}) collective-permute-start(bf16[512,2048]{1,0:T(8,128)(2,1)S(1)} %constant_dynamic-update-slice_fusion.3), channel_id=1, source_target_pairs={{0,1},{1,0},{2,3},{3,2},{4,5},{5,4},{6,7},{7,6},{8,9},{9,8},{10,11... | collective-permute-start | bytes 6291464 | tf_op jit(solution)/shard_map/ppermute | solution.py:37
  146.3 41.0 %collective-permute-start.29 = (bf16[512,512]{1,0:T(8,128)(2,1)}, bf16[512,512]{1,0:T(8,128)(2,1)S(1)}, u32[]{:S(2)}, u32[]{:S(2)}) collective-permute-start(bf16[512,512]{1,0:T(8,128)(2,1)} %fusion.22), channel_id=1, source_target_pairs={{0,8},{8,16},{16,24},{24,0},{1,9},{9,17},{17,25},{25,1},{2,10},{10... | collective-permute-start | bytes 1572872 | tf_op jit(solution)/shard_map/ppermute | solution.py:84
  152.5 36.3 %collective-permute-start.26 = (bf16[512,512]{1,0:T(8,128)(2,1)}, bf16[512,512]{1,0:T(8,128)(2,1)}, u32[]{:S(2)}, u32[]{:S(2)}) collective-permute-start(bf16[512,512]{1,0:T(8,128)(2,1)} %fusion.21), channel_id=1, source_target_pairs={{0,16},{8,24},{16,0},{24,8},{1,17},{9,25},{17,1},{25,9},{2,18},{10... | collective-permute-start | bytes 1572872 | tf_op jit(solution)/shard_map/ppermute | solution.py:84
  157.7 39.4 %collective-permute-start.23 = (bf16[512,512]{1,0:T(8,128)(2,1)}, bf16[512,512]{1,0:T(8,128)(2,1)}, u32[]{:S(2)}, u32[]{:S(2)}) collective-permute-start(bf16[512,512]{1,0:T(8,128)(2,1)} %fusion.20), channel_id=1, source_target_pairs={{0,24},{8,0},{16,8},{24,16},{1,25},{9,1},{17,9},{25,17},{2,26},{10... | collective-permute-start | bytes 1572872 | tf_op jit(solution)/shard_map/ppermute | solution.py:84
  187.3 43.3 %collective-permute-start.18 = (bf16[512,1024]{1,0:T(8,128)(2,1)S(1)}, bf16[512,1024]{1,0:T(8,128)(2,1)S(1)}, u32[]{:S(2)}, u32[]{:S(2)}) collective-permute-start(bf16[512,1024]{1,0:T(8,128)(2,1)S(1)} %copy-done.18), channel_id=1, source_target_pairs={{0,2},{1,3},{2,0},{3,1},{4,6},{5,7},{6,4},{7,5},{8,10},{9,11},{10,... | collective-permute-start | bytes 3145736 | tf_op jit(solution)/shard_map/ppermute | solution.py:37
  199.1 29.5 %collective-permute-start.10 = (bf16[512,512]{1,0:T(8,128)(2,1)S(1)}, bf16[512,512]{1,0:T(8,128)(2,1)S(1)}, u32[]{:S(2)}, u32[]{:S(2)}) collective-permute-start(bf16[512,512]{1,0:T(8,128)(2,1)S(1)} %collective-permute-done), channel_id=1, source_target_pairs={{0,2},{1,3},{2,0},{3,1},{4,6},{5,7},{6,4},{7,5},{8,10},{9,11},{10,... | collective-permute-start | bytes 1572872 | tf_op jit(solution)/shard_map/ppermute | solution.py:37
  199.6 29.0 %collective-permute-start.11 = (bf16[512,512]{1,0:T(8,128)(2,1)}, bf16[512,512]{1,0:T(8,128)(2,1)S(1)}, u32[]{:S(2)}, u32[]{:S(2)}) collective-permute-start(bf16[512,512]{1,0:T(8,128)(2,1)} %collective-permute-done.1), channel_id=1, source_target_pairs={{0,4},{1,5},{2,6},{3,7},{4,0},{5,1},{6,2},{7,3},{8,12},{9,13},{10,... | collective-permute-start | bytes 1572872 | tf_op jit(solution)/shard_map/ppermute | solution.py:37
  228.7 34.5 %collective-permute-start.15 = (bf16[512,1024]{1,0:T(8,128)(2,1)S(1)}, bf16[512,1024]{1,0:T(8,128)(2,1)S(1)}, u32[]{:S(2)}, u32[]{:S(2)}) collective-permute-start(bf16[512,1024]{1,0:T(8,128)(2,1)S(1)} %pad_maximum_fusion.8), channel_id=1, source_target_pairs={{0,4},{1,5},{2,6},{3,7},{4,0},{5,1},{6,2},{7,3},{8,12},{9,13},{10,... | collective-permute-start | bytes 3145736 | tf_op jit(solution)/shard_map/ppermute | solution.py:37
  231.1 35.1 %collective-permute-start.19 = (bf16[512,2048]{1,0:T(8,128)(2,1)S(1)}, bf16[512,2048]{1,0:T(8,128)(2,1)S(1)}, u32[]{:S(2)}, u32[]{:S(2)}) collective-permute-start(bf16[512,2048]{1,0:T(8,128)(2,1)S(1)} %pad_maximum_fusion.3), channel_id=1, source_target_pairs={{0,1},{1,0},{2,3},{3,2},{4,5},{5,4},{6,7},{7,6},{8,9},{9,8},{10,11... | collective-permute-start | bytes 6291464 | tf_op jit(solution)/shard_map/ppermute | solution.py:37
  232.3 31.1 %collective-permute-start.12 = (bf16[512,1024]{1,0:T(8,128)(2,1)S(1)}, bf16[512,1024]{1,0:T(8,128)(2,1)S(1)}, u32[]{:S(2)}, u32[]{:S(2)}) collective-permute-start(bf16[512,1024]{1,0:T(8,128)(2,1)S(1)} %pad_maximum_fusion.7), channel_id=1, source_target_pairs={{0,2},{1,3},{2,0},{3,1},{4,6},{5,7},{6,4},{7,5},{8,10},{9,11},{10,... | collective-permute-start | bytes 3145736 | tf_op jit(solution)/shard_map/ppermute | solution.py:37
  265.0 8.3 %collective-permute-start.13 = (bf16[512,2048]{1,0:T(8,128)(2,1)S(1)}, bf16[512,2048]{1,0:T(8,128)(2,1)S(1)}, u32[]{:S(2)}, u32[]{:S(2)}) collective-permute-start(bf16[512,2048]{1,0:T(8,128)(2,1)S(1)} %pad_maximum_fusion), channel_id=1, source_target_pairs={{0,1},{1,0},{2,3},{3,2},{4,5},{5,4},{6,7},{7,6},{8,9},{9,8},{10,11... | collective-permute-start | bytes 6291464 | tf_op jit(solution)/shard_map/ppermute | solution.py:37
  268.7 37.2 %collective-permute-start.20 = (bf16[512,512]{1,0:T(8,128)(2,1)S(1)}, bf16[512,512]{1,0:T(8,128)(2,1)S(1)}, u32[]{:S(2)}, u32[]{:S(2)}) collective-permute-start(bf16[512,512]{1,0:T(8,128)(2,1)S(1)} %fusion.19), channel_id=1, source_target_pairs={{0,8},{8,16},{16,24},{24,0},{1,9},{9,17},{17,25},{25,1},{2,10},{10... | collective-permute-start | bytes 1572872 | tf_op jit(solution)/shard_map/ppermute | solution.py:84
  271.3 34.7 %collective-permute-start.17 = (bf16[512,512]{1,0:T(8,128)(2,1)S(1)}, bf16[512,512]{1,0:T(8,128)(2,1)S(1)}, u32[]{:S(2)}, u32[]{:S(2)}) collective-permute-start(bf16[512,512]{1,0:T(8,128)(2,1)S(1)} %fusion.18), channel_id=1, source_target_pairs={{0,16},{8,24},{16,0},{24,8},{1,17},{9,25},{17,1},{25,9},{2,18},{10... | collective-permute-start | bytes 1572872 | tf_op jit(solution)/shard_map/ppermute | solution.py:84
  276.9 35.3 %collective-permute-start.14 = (bf16[512,512]{1,0:T(8,128)(2,1)S(1)}, bf16[512,512]{1,0:T(8,128)(2,1)S(1)}, u32[]{:S(2)}, u32[]{:S(2)}) collective-permute-start(bf16[512,512]{1,0:T(8,128)(2,1)S(1)} %fusion.17), channel_id=1, source_target_pairs={{0,24},{8,0},{16,8},{24,16},{1,25},{9,1},{17,9},{25,17},{2,26},{10... | collective-permute-start | bytes 1572872 | tf_op jit(solution)/shard_map/ppermute | solution.py:84
  (21 other events, 273.2 us)
Sparse Core Ops, SparseCore 0:
  9.2 42.5 all-gather.9
  53.7 54.0 all-gather.7
  199.2 54.0 all-gather.5

commit v6 on v5

v6 whole, which is shorter than its diff:
```python
import jax
import jax.numpy as jnp
from jax import lax
from jax.sharding import PartitionSpec as P

damping = 0.01
ROOM = 2**25


def product_and_divide(rot_out, all_rot_in, eig_lambda, tokens):
    denom = eig_lambda.astype(jnp.float32) + damping
    contract = (((0,), (0,)), ((), ()))
    product = lax.dot_general(rot_out, all_rot_in, contract, preferred_element_type=jnp.float32) / tokens
    return (product / denom).astype(jnp.bfloat16)[None]


def from_owner(held, owner):
    return lax.psum(jnp.where(lax.axis_index("dp") == owner, held, jnp.zeros_like(held)), "dp")


def dot(a, b):
    return jnp.dot(a, b, preferred_element_type=jnp.float32)


def move_bases(acts, grads, basis_in_held, basis_out_held, owners, eig_lambda):
    column = lax.axis_index("tensor")
    basis_in = from_owner(basis_in_held[0], owners[0, column])
    basis_out = from_owner(basis_out_held[0], owners[1, column])
    rot_in = dot(lax.all_gather(acts[0], "tensor", axis=1, tiled=True), basis_in).astype(jnp.bfloat16)
    rot_out = dot(lax.all_gather(grads[0], "tensor", axis=1, tiled=True), basis_out).astype(jnp.bfloat16)
    return product_and_divide(
        rot_out, lax.all_gather(rot_in, "tensor", axis=1, tiled=True), eig_lambda, acts.shape[1]
    )


X, Y, CORE = 2, 4, 1


def swap(block, bit):
    return lax.ppermute(block, "tensor", [(j, j ^ bit) for j in range(X + Y + CORE + 1)])


def in_order(held, column):
    width = held.shape[0] // (X + Y + CORE + 1)
    offsets = [0, X, Y, X + Y]
    offsets += [CORE + i for i in offsets]
    blocks = [lax.dynamic_slice(held, ((column ^ i) * width, 0), (width, held.shape[1])) for i in offsets]
    return jnp.concatenate(blocks, axis=0)


def after(values, *others):
    return lax.optimization_barrier((values, others))[0]


def move_inputs(n_dp, acts, grads, basis_in_held, basis_out_held, owners, eig_lambda):
    column = lax.axis_index("tensor")
    me = lax.axis_index("dp")
    mine = (acts[0], grads[0])
    held = (basis_in_held[0], basis_out_held[0])
    behind = [(me - owners[side, column]) % n_dp for side in (0, 1)]
    half = held[0].shape[0] // 2
    everyone = [lax.all_gather(block, "dp") for block in mine]
    ordered = [in_order(block, column) for block in held]

    def piece(side, i):
        if i == 0:
            return mine[side]
        return lax.dynamic_index_in_dim(everyone[side], (me + i) % n_dp, 0, keepdims=False)

    rotated, returned = {}, {}

    def rotate(key, blocks):
        side, i = key
        even = jnp.concatenate(blocks, axis=1)
        odd = swap(even, CORE)
        rotated[key] = (dot(even, ordered[side][:half]) + dot(odd, ordered[side][half:])).astype(jnp.bfloat16)
        returned[key] = rotated[key]
        if i:
            returned[key] = lax.ppermute(rotated[key], "dp", [(z, (z + i) % n_dp) for z in range(n_dp)])

    keys = [(0, 0), (1, 0)] + [(0, i) for i in range(1, n_dp)]
    keys += [(1, i) for i in sorted(range(1, n_dp), key=lambda i: -min(i, n_dp - i))]
    slots = []

    def slot(to_x, to_y):
        if slots:
            others = [slots[-1][0]]
            if len(slots) > 1:
                others.append(slots[-2][1])
            at = len(slots) // 3
            if at > 1 and len(slots) % 3 == 2:
                others.append([rotated[key] for key in keys[2 * at - 4 : 2 * at - 2]])
            if at > 2 and len(slots) % 3 == 2:
                others.append([returned[key] for key in keys[2 * at - 6 : 2 * at - 4]])
            to_x, to_y = after([to_x, to_y], *others)
        slots.append(([to_x, to_y], [swap(to_x, X), swap(to_y, Y)]))
        return slots[-1][1]

    for at in range(0, len(keys), 2):
        p, q = piece(*keys[at]), piece(*keys[at + 1])
        p_x, q_y = slot(p, q)
        q_x, p_y = slot(q, p)
        q_xy, p_xy = slot(q_y, p_x)
        rotate(keys[at], [p, p_x, p_y, p_xy])
        rotate(keys[at + 1], [q, q_x, q_y, q_xy])

    found = []
    for side in (0, 1):
        total = returned[side, 0]
        for i in range(1, n_dp):
            total = jnp.where(behind[side] == i, returned[side, i], total)
        found.append(total)
    all_rot_in = lax.all_gather(found[0], "tensor", axis=1, tiled=True)
    return product_and_divide(found[1], all_rot_in, eig_lambda, acts.shape[1])


def solution(mesh):
    placed = (
        P("dp", None, "tensor"),
        P("dp", None, "tensor"),
        P("dp", None, "tensor"),
        P("dp", None, "tensor"),
        P(),
        P("tensor", None),
    )
    n_dp, n_tensor = mesh.shape["dp"], mesh.shape["tensor"]

    def step(acts, *rest):
        whole = 2 * n_dp * acts.shape[1] * acts.shape[2] * n_tensor * acts.dtype.itemsize
        if whole <= ROOM and n_tensor == X + Y + CORE + 1:
            return move_inputs(n_dp, acts, *rest)
        return move_bases(acts, *rest)

    return jax.shard_map(step, mesh=mesh, in_specs=placed, out_specs=P("dp", "tensor", None), check_vma=False)
```

time: 337 us -> 389 us (1.15)
  waiting for transfers between devices: 225 us -> 273 us
  local copies, waits for them, and re-layouts: 8.94 us -> 13 us
    ppermute x30 -> x38, waiting for transfers between devices: 224 us -> 273 us  [the longest x32 198 us: swap(): lax.ppermute(block, 'tensor', [(j, j ^ bit) for j in range(X + Y + CORE +...]
    dynamic_slice x2, local copies, waits for them, and re-layouts: 2.8 us -> 7.96 us  [in_order(): lax.dynamic_slice(held, ((column ^ i) * width, 0), (width, held.shape[1]))]
    dot_general x1, matrix products: 13.4 us -> 8.9 us  [product_and_divide(): lax.dot_general(rot_out, all_rot_in, contract, preferred_element_type=jnp...]
    dot_general x13 -> x16, matrix products: 29 us -> 33.1 us  [dot(): return jnp.dot(a, b, preferred_element_type=jnp.float32)]
    concatenate x9 -> x8, other arithmetic: 5.95 us -> 9.73 us  [rotate(): even = jnp.concatenate(blocks, axis=1)]
    ppermute x30 -> x38, starting transfers between devices: 33.4 us -> 30.6 us  [the longest x32 25.3 us: swap(): lax.ppermute(block, 'tensor', [(j, j ^ bit) for j in range(X + Y + CORE +...]
  transfers between devices with their start and end apart: 33 -> 41, of which waited for: 13 -> 25; matrix products, arithmetic and copies ran while one was open for 14% -> 14% of each run, Pallas kernels for 0% -> 0%
where the time goes in v6:
time: 389 us; the launch traced here: 386 us
  waiting for transfers between devices  273 us (70%)
  matrix products  42 us (11%)
  starting transfers between devices  30.6 us (8%)
  between operations  15.5 us (4%)
  local copies, waits for them, and re-layouts  13 us (3%)
  other arithmetic  11.7 us (3%)
    ppermute x32, waiting for transfers between devices, swap(): lax.ppermute(block, 'tensor', [(j, j ^ bit) for j in range(X + Y + CORE +...  198 us
    ppermute x6, waiting for transfers between devices, rotate(): lax.ppermute(rotated[key], 'dp', [(z, (z + i) % n_dp) for z in range(n_dp)])  74.2 us
    dot_general x16, matrix products, dot(): return jnp.dot(a, b, preferred_element_type=jnp.float32)  33.1 us
    ppermute x32, starting transfers between devices, swap(): lax.ppermute(block, 'tensor', [(j, j ^ bit) for j in range(X + Y + CORE +...  25.3 us
    concatenate x8, other arithmetic, rotate(): even = jnp.concatenate(blocks, axis=1)  9.73 us
    dot_general x1, matrix products, product_and_divide(): lax.dot_general(rot_out, all_rot_in, contract, preferred_element_type=jnp...  8.9 us
    dynamic_slice x2, local copies, waits for them, and re-layouts, in_order(): lax.dynamic_slice(held, ((column ^ i) * width, 0), (width, held.shape[1]))  7.96 us
  transfers between devices with their start and end apart: 41, of which 25 were waited for; matrix products, arithmetic and copies ran while one was open for 14% of the time, Pallas kernels for 0%

profile of v6, /device:TPU:16, one launch (start us, length us, event | category | flops | bytes accessed | tf_op | source)
XLA Modules:
  0.0 386.1 jit_solution(6585615029830318546)
XLA Ops:
  10.9 11.5 %collective-permute-done = bf16[512,512]{1,0:T(8,128)(2,1)S(1)} collective-permute-done((bf16[512,512]{1,0:T(8,128)(2,1)}, bf16[512,512]{1,0:T(8,128)(2,1)S(1)}, u32[]{:S(2)}, u32[]{:S(2)}) %collective-permute-start) | collective-permute-done | bytes 524320 | tf_op jit(solution)/shard_map/ppermute | solution.py:40
  24.0 9.6 %collective-permute-done.3 = bf16[512,512]{1,0:T(8,128)(2,1)S(1)} collective-permute-done((bf16[512,512]{1,0:T(8,128)(2,1)}, bf16[512,512]{1,0:T(8,128)(2,1)S(1)}, u32[]{:S(2)}, u32[]{:S(2)}) %collective-permute-start.3) | collective-permute-done | bytes 524320 | tf_op jit(solution)/shard_map/ppermute | solution.py:40
  33.6 10.1 %collective-permute-done.7 = bf16[512,512]{1,0:T(8,128)(2,1)S(1)} collective-permute-done((bf16[512,512]{1,0:T(8,128)(2,1)S(1)}, bf16[512,512]{1,0:T(8,128)(2,1)S(1)}, u32[]{:S(2)}, u32[]{:S(2)}) %collective-permute-start.7) | collective-permute-done | bytes 524320 | tf_op jit(solution)/shard_map/ppermute | solution.py:40
  43.7 2.9 pad_maximum_fusion
  48.8 12.6 %collective-permute-done.2 = bf16[512,512]{1,0:T(8,128)(2,1)S(1)} collective-permute-done((bf16[512,512]{1,0:T(8,128)(2,1)S(1)}, bf16[512,512]{1,0:T(8,128)(2,1)S(1)}, u32[]{:S(2)}, u32[]{:S(2)}) %collective-permute-start.2) | collective-permute-done | bytes 524320 | tf_op jit(solution)/shard_map/ppermute | solution.py:40
  62.2 10.1 %collective-permute-done.6 = bf16[512,512]{1,0:T(8,128)(2,1)} collective-permute-done((bf16[512,512]{1,0:T(8,128)(2,1)S(1)}, bf16[512,512]{1,0:T(8,128)(2,1)}, u32[]{:S(2)}, u32[]{:S(2)}) %collective-permute-start.6) | collective-permute-done | bytes 524320 | tf_op jit(solution)/shard_map/ppermute | solution.py:40
  73.9 4.2 %dynamic-slice_bitcast_fusion.15 = (bf16[512,512]{1,0:T(8,128)(2,1)}, bf16[512,512]{1,0:T(8,128)(2,1)}, bf16[512,512]{1,0:T(8,128)(2,1)}, bf16[512,512]{1,0:T(8,...) fusion(bf16[1,4096,512]{2,1,0:T(8,128)(2,1)} %param.8, ...), kind=kLoop, calls=%fused_computation.49 | loop fusion | bytes 8388640 | tf_op jit(solution)/shard_map/dynamic_slice | solution.py:47
  82.7 3.7 dynamic-slice_bitcast_fusion.7
  86.6 3.6 fusion.22
  90.8 3.2 collective-permute-done.4
  101.7 5.5 %collective-permute-done.8 = bf16[512,512]{1,0:T(8,128)(2,1)S(1)} collective-permute-done((bf16[512,512]{1,0:T(8,128)(2,1)S(1)}, bf16[512,512]{1,0:T(8,128)(2,1)S(1)}, u32[]{:S(2)}, u32[]{:S(2)}) %collective-permute-start.8) | collective-permute-done | bytes 524320 | tf_op jit(solution)/shard_map/ppermute | solution.py:40
  107.2 10.4 %collective-permute-done.12 = bf16[512,512]{1,0:T(8,128)(2,1)S(1)} collective-permute-done((bf16[512,512]{1,0:T(8,128)(2,1)S(1)}, bf16[512,512]{1,0:T(8,128)(2,1)S(1)}, u32[]{:S(2)}, u32[]{:S(2)}) %collective-permute-start.12) | collective-permute-done | bytes 524320 | tf_op jit(solution)/shard_map/ppermute | solution.py:40
  119.4 3.9 %fusion.18 = f32[512,512]{1,0:T(8,128)} fusion(bf16[512,2048]{1,0:T(8,128)(2,1)} %collective-permute-done.15, bf16[512,512]{1,0:T(8,128)(2,1)S(1)} %get-tuple-element.55, bf16[512,512]{1,0:T(8,128)(2,1)S(1)} %get-tuple-element.56, bf16[512,512]{1,0:T(8,128)(2,1)S(1)} %get-tuple-element.50, bf16[512,512]{1,0:T(8,128)(2,1)S(1)} %get-tuple-element.51), kind=kOutput, calls=%fused_computation.64 | convolution fusion | flops 1082130432 | bytes 5242880 | tf_op jit(solution)/shard_map/dot_general | solution.py:22
  128.8 3.1 fusion.2
  131.9 7.4 %collective-permute-done.10 = bf16[512,512]{1,0:T(8,128)(2,1)S(1)} collective-permute-done((bf16[512,512]{1,0:T(8,128)(2,1)S(1)}, bf16[512,512]{1,0:T(8,128)(2,1)S(1)}, u32[]{:S(2)}, u32[]{:S(2)}) %collective-permute-start.10) | collective-permute-done | bytes 524320 | tf_op jit(solution)/shard_map/ppermute | solution.py:40
  141.6 12.8 %collective-permute-done.19 = bf16[512,512]{1,0:T(8,128)(2,1)S(1)} collective-permute-done((bf16[512,512]{1,0:T(8,128)(2,1)S(1)}, bf16[512,512]{1,0:T(8,128)(2,1)S(1)}, u32[]{:S(2)}, u32[]{:S(2)}) %collective-permute-start.19) | collective-permute-done | bytes 524320 | tf_op jit(solution)/shard_map/ppermute | solution.py:40
  154.4 9.7 %collective-permute-done.17 = bf16[512,512]{1,0:T(8,128)(2,1)S(1)} collective-permute-done((bf16[512,512]{1,0:T(8,128)(2,1)S(1)}, bf16[512,512]{1,0:T(8,128)(2,1)S(1)}, u32[]{:S(2)}, u32[]{:S(2)}) %collective-permute-start.17) | collective-permute-done | bytes 524320 | tf_op jit(solution)/shard_map/ppermute | solution.py:40
  164.6 3.0 fusion.20
  171.3 3.4 fusion.3
  182.2 23.0 %collective-permute-done.36 = bf16[512,512]{1,0:T(8,128)(2,1)} collective-permute-done((bf16[512,512]{1,0:T(8,128)(2,1)}, bf16[512,512]{1,0:T(8,128)(2,1)}, u32[]{:S(2)}, u32[]{:S(2)}) %collective-permute-start.36) | collective-permute-done | bytes 524320 | tf_op jit(solution)/shard_map/ppermute | solution.py:79
  205.2 13.6 %collective-permute-done.37 = bf16[512,512]{1,0:T(8,128)(2,1)S(1)} collective-permute-done((bf16[512,512]{1,0:T(8,128)(2,1)}, bf16[512,512]{1,0:T(8,128)(2,1)S(1)}, u32[]{:S(2)}, u32[]{:S(2)}) %collective-permute-start.37) | collective-permute-done | bytes 524320 | tf_op jit(solution)/shard_map/ppermute | solution.py:79
  222.8 17.6 %collective-permute-done.16 = bf16[512,512]{1,0:T(8,128)(2,1)S(1)} collective-permute-done((bf16[512,512]{1,0:T(8,128)(2,1)S(1)}, bf16[512,512]{1,0:T(8,128)(2,1)S(1)}, u32[]{:S(2)}, u32[]{:S(2)}) %collective-permute-start.16) | collective-permute-done | bytes 524320 | tf_op jit(solution)/shard_map/ppermute | solution.py:40
  241.8 13.4 %collective-permute-done.18 = bf16[512,512]{1,0:T(8,128)(2,1)S(1)} collective-permute-done((bf16[512,512]{1,0:T(8,128)(2,1)}, bf16[512,512]{1,0:T(8,128)(2,1)S(1)}, u32[]{:S(2)}, u32[]{:S(2)}) %collective-permute-start.18) | collective-permute-done | bytes 524320 | tf_op jit(solution)/shard_map/ppermute | solution.py:40
  256.9 18.1 %collective-permute-done.22 = bf16[512,512]{1,0:T(8,128)(2,1)S(1)} collective-permute-done((bf16[512,512]{1,0:T(8,128)(2,1)S(1)}, bf16[512,512]{1,0:T(8,128)(2,1)S(1)}, u32[]{:S(2)}, u32[]{:S(2)}) %collective-permute-start.22) | collective-permute-done | bytes 524320 | tf_op jit(solution)/shard_map/ppermute | solution.py:40
  275.4 10.9 %collective-permute-done.20 = bf16[512,512]{1,0:T(8,128)(2,1)S(1)} collective-permute-done((bf16[512,512]{1,0:T(8,128)(2,1)S(1)}, bf16[512,512]{1,0:T(8,128)(2,1)S(1)}, u32[]{:S(2)}, u32[]{:S(2)}) %collective-permute-start.20) | collective-permute-done | bytes 524320 | tf_op jit(solution)/shard_map/ppermute | solution.py:40
  286.2 9.2 %collective-permute-done.25 = bf16[512,512]{1,0:T(8,128)(2,1)S(1)} collective-permute-done((bf16[512,512]{1,0:T(8,128)(2,1)S(1)}, bf16[512,512]{1,0:T(8,128)(2,1)S(1)}, u32[]{:S(2)}, u32[]{:S(2)}) %collective-permute-start.25) | collective-permute-done | bytes 524320 | tf_op jit(solution)/shard_map/ppermute | solution.py:40
  295.8 2.3 collective-permute-start.30
  298.2 12.7 %collective-permute-done.30 = bf16[512,512]{1,0:T(8,128)(2,1)S(1)} collective-permute-done((bf16[512,512]{1,0:T(8,128)(2,1)S(1)}, bf16[512,512]{1,0:T(8,128)(2,1)S(1)}, u32[]{:S(2)}, u32[]{:S(2)}) %collective-permute-start.30) | collective-permute-done | bytes 524320 | tf_op jit(solution)/shard_map/ppermute | solution.py:40
  310.9 11.0 %collective-permute-done.31 = bf16[512,512]{1,0:T(8,128)(2,1)S(1)} collective-permute-done((bf16[512,512]{1,0:T(8,128)(2,1)S(1)}, bf16[512,512]{1,0:T(8,128)(2,1)S(1)}, u32[]{:S(2)}, u32[]{:S(2)}) %collective-permute-start.31) | collective-permute-done | bytes 524320 | tf_op jit(solution)/shard_map/ppermute | solution.py:40
  333.0 15.6 %collective-permute-done.29 = bf16[512,512]{1,0:T(8,128)(2,1)S(1)} collective-permute-done((bf16[512,512]{1,0:T(8,128)(2,1)S(1)}, bf16[512,512]{1,0:T(8,128)(2,1)S(1)}, u32[]{:S(2)}, u32[]{:S(2)}) %collective-permute-start.29) | collective-permute-done | bytes 524320 | tf_op jit(solution)/shard_map/ppermute | solution.py:79
  348.7 22.0 %collective-permute-done.27 = bf16[512,512]{1,0:T(8,128)(2,1)S(1)} collective-permute-done((bf16[512,512]{1,0:T(8,128)(2,1)S(1)}, bf16[512,512]{1,0:T(8,128)(2,1)S(1)}, u32[]{:S(2)}, u32[]{:S(2)}) %collective-permute-start.27) | collective-permute-done | bytes 524320 | tf_op jit(solution)/shard_map/ppermute | solution.py:79
  370.7 8.9 %fusion = bf16[1,512,4096]{2,1,0:T(8,128)(2,1)} fusion(bf16[512,4096]{1,0:T(8,128)(2,1)} %param.11, bf16[512,4096]{1,0:T(8,128)(2,1)} %all-gather.8.cloned.1.call-done, bf16[512,512]{1,0:T(8,128)(2,1)S(1)} %collective-permute-done.27, bf16[512,512]{1,0:T(8,128)(2,1)S(1)} %collective-permute-done.29, bf16[512,512]{1,0:T(8,128)(2,1)S(1)} %collective-permute-done.33, ...), kind=kOutput, calls=%fused_computation.1 | convolution fusion | flops 2158755840 | bytes 14680067 | tf_op jit(solution)/shard_map/dot_general | solution.py:13
  (202 shorter events, 61.5 us)
Async XLA Ops:
  6.5 71.6 %all-gather.6.cloned.1.call-start = ((), (), s32[]{:S(2)}) async-start(), calls=%async_computation.1 | async-start | bytes 2621440 | tf_op jit(solution)/shard_map/all_gather | solution.py:62
  7.3 116.0 %all-gather.4.cloned.1.call-start = ((), (), s32[]{:S(2)}) async-start(), calls=%async_computation | async-start | bytes 2621440 | tf_op jit(solution)/shard_map/all_gather | solution.py:62
  7.3 15.1 %collective-permute-start = (bf16[512,512]{1,0:T(8,128)(2,1)}, bf16[512,512]{1,0:T(8,128)(2,1)S(1)}, u32[]{:S(2)}, u32[]{:S(2)}) collective-permute-start(bf16[512,512]{1,0:T(8,128)(2,1)} %bitcast.63), channel_id=1, source_target_pairs={{0,4},{1,5},{2,6},{3,7},{4,0},{5,1},{6,2},{7,3},{8,12},{9,13},{10,... | collective-permute-start | bytes 1572872 | tf_op jit(solution)/shard_map/ppermute | solution.py:40
  10.4 23.2 %collective-permute-start.3 = (bf16[512,512]{1,0:T(8,128)(2,1)}, bf16[512,512]{1,0:T(8,128)(2,1)S(1)}, u32[]{:S(2)}, u32[]{:S(2)}) collective-permute-start(bf16[512,512]{1,0:T(8,128)(2,1)} %bitcast.60), channel_id=1, source_target_pairs={{0,4},{1,5},{2,6},{3,7},{4,0},{5,1},{6,2},{7,3},{8,12},{9,13},{10,... | collective-permute-start | bytes 1572872 | tf_op jit(solution)/shard_map/ppermute | solution.py:40
  22.5 21.2 %collective-permute-start.7 = (bf16[512,512]{1,0:T(8,128)(2,1)S(1)}, bf16[512,512]{1,0:T(8,128)(2,1)S(1)}, u32[]{:S(2)}, u32[]{:S(2)}) collective-permute-start(bf16[512,512]{1,0:T(8,128)(2,1)S(1)} %collective-permute-done.1), channel_id=1, source_target_pairs={{0,4},{1,5},{2,6},{3,7},{4,0},{5,1},{6,2},{7,3},{8,12},{9,13},{10,... | collective-permute-start | bytes 1572872 | tf_op jit(solution)/shard_map/ppermute | solution.py:40
  46.6 39.9 %collective-permute-start.14 = (bf16[512,2048]{1,0:T(8,128)(2,1)}, bf16[512,2048]{1,0:T(8,128)(2,1)}, u32[]{:S(2)}, u32[]{:S(2)}) collective-permute-start(bf16[512,2048]{1,0:T(8,128)(2,1)} %pad_maximum_fusion), channel_id=1, source_target_pairs={{0,1},{1,0},{2,3},{3,2},{4,5},{5,4},{6,7},{7,6},{8,9},{9,8},{10,11... | collective-permute-start | bytes 6291464 | tf_op jit(solution)/shard_map/ppermute | solution.py:40
  48.1 24.1 %collective-permute-start.6 = (bf16[512,512]{1,0:T(8,128)(2,1)S(1)}, bf16[512,512]{1,0:T(8,128)(2,1)}, u32[]{:S(2)}, u32[]{:S(2)}) collective-permute-start(bf16[512,512]{1,0:T(8,128)(2,1)S(1)} %collective-permute-done), channel_id=1, source_target_pairs={{0,2},{1,3},{2,0},{3,1},{4,6},{5,7},{6,4},{7,5},{8,10},{9,11},{10,... | collective-permute-start | bytes 1572872 | tf_op jit(solution)/shard_map/ppermute | solution.py:40
  48.7 321.9 %all-gather.8.cloned.1.call-start = ((), (), s32[]{:S(2)}) async-start(), calls=%async_computation.2 | async-start | bytes 4718592 | tf_op jit(solution)/shard_map/all_gather | solution.py:113
  73.7 45.6 %collective-permute-start.15 = (bf16[512,2048]{1,0:T(8,128)(2,1)S(1)}, bf16[512,2048]{1,0:T(8,128)(2,1)}, u32[]{:S(2)}, u32[]{:S(2)}) collective-permute-start(bf16[512,2048]{1,0:T(8,128)(2,1)S(1)} %pad_maximum_fusion.3), channel_id=1, source_target_pairs={{0,1},{1,0},{2,3},{3,2},{4,5},{5,4},{6,7},{7,6},{8,9},{9,8},{10,11... | collective-permute-start | bytes 6291464 | tf_op jit(solution)/shard_map/ppermute | solution.py:40
  90.2 17.0 %collective-permute-start.8 = (bf16[512,512]{1,0:T(8,128)(2,1)S(1)}, bf16[512,512]{1,0:T(8,128)(2,1)S(1)}, u32[]{:S(2)}, u32[]{:S(2)}) collective-permute-start(bf16[512,512]{1,0:T(8,128)(2,1)S(1)} %get-tuple-element.33), channel_id=1, source_target_pairs={{0,2},{1,3},{2,0},{3,1},{4,6},{5,7},{6,4},{7,5},{8,10},{9,11},{10,... | collective-permute-start | bytes 1572872 | tf_op jit(solution)/shard_map/ppermute | solution.py:40
  96.1 21.6 %collective-permute-start.12 = (bf16[512,512]{1,0:T(8,128)(2,1)S(1)}, bf16[512,512]{1,0:T(8,128)(2,1)S(1)}, u32[]{:S(2)}, u32[]{:S(2)}) collective-permute-start(bf16[512,512]{1,0:T(8,128)(2,1)S(1)} %collective-permute-done.4), channel_id=1, source_target_pairs={{0,2},{1,3},{2,0},{3,1},{4,6},{5,7},{6,4},{7,5},{8,10},{9,11},{10,... | collective-permute-start | bytes 1572872 | tf_op jit(solution)/shard_map/ppermute | solution.py:40
  99.7 25.2 %collective-permute-start.9 = (bf16[512,512]{1,0:T(8,128)(2,1)S(1)}, bf16[512,512]{1,0:T(8,128)(2,1)}, u32[]{:S(2)}, u32[]{:S(2)}) collective-permute-start(bf16[512,512]{1,0:T(8,128)(2,1)S(1)} %get-tuple-element.34), channel_id=1, source_target_pairs={{0,4},{1,5},{2,6},{3,7},{4,0},{5,1},{6,2},{7,3},{8,12},{9,13},{10,... | collective-permute-start | bytes 1572872 | tf_op jit(solution)/shard_map/ppermute | solution.py:40
  100.2 26.8 %collective-permute-start.13 = (bf16[512,512]{1,0:T(8,128)(2,1)}, bf16[512,512]{1,0:T(8,128)(2,1)}, u32[]{:S(2)}, u32[]{:S(2)}) collective-permute-start(bf16[512,512]{1,0:T(8,128)(2,1)} %collective-permute-done.5), channel_id=1, source_target_pairs={{0,4},{1,5},{2,6},{3,7},{4,0},{5,1},{6,2},{7,3},{8,12},{9,13},{10,... | collective-permute-start | bytes 1572872 | tf_op jit(solution)/shard_map/ppermute | solution.py:40
  119.3 45.3 %collective-permute-start.24 = (bf16[512,2048]{1,0:T(8,128)(2,1)}, bf16[512,2048]{1,0:T(8,128)(2,1)}, u32[]{:S(2)}, u32[]{:S(2)}) collective-permute-start(bf16[512,2048]{1,0:T(8,128)(2,1)} %pad_maximum_fusion.7), channel_id=1, source_target_pairs={{0,1},{1,0},{2,3},{3,2},{4,5},{5,4},{6,7},{7,6},{8,9},{9,8},{10,11... | collective-permute-start | bytes 6291464 | tf_op jit(solution)/shard_map/ppermute | solution.py:40
  128.6 41.5 %collective-permute-start.23 = (bf16[512,2048]{1,0:T(8,128)(2,1)S(1)}, bf16[512,2048]{1,0:T(8,128)(2,1)S(1)}, u32[]{:S(2)}, u32[]{:S(2)}) collective-permute-start(bf16[512,2048]{1,0:T(8,128)(2,1)S(1)} %pad_maximum_fusion.6), channel_id=1, source_target_pairs={{0,1},{1,0},{2,3},{3,2},{4,5},{5,4},{6,7},{7,6},{8,9},{9,8},{10,11... | collective-permute-start | bytes 6291464 | tf_op jit(solution)/shard_map/ppermute | solution.py:40
  141.1 23.0 %collective-permute-start.17 = (bf16[512,512]{1,0:T(8,128)(2,1)S(1)}, bf16[512,512]{1,0:T(8,128)(2,1)S(1)}, u32[]{:S(2)}, u32[]{:S(2)}) collective-permute-start(bf16[512,512]{1,0:T(8,128)(2,1)S(1)} %get-tuple-element.40), channel_id=1, source_target_pairs={{0,4},{1,5},{2,6},{3,7},{4,0},{5,1},{6,2},{7,3},{8,12},{9,13},{10,... | collective-permute-start | bytes 1572872 | tf_op jit(solution)/shard_map/ppermute | solution.py:40
  169.8 35.4 %collective-permute-start.36 = (bf16[512,512]{1,0:T(8,128)(2,1)}, bf16[512,512]{1,0:T(8,128)(2,1)}, u32[]{:S(2)}, u32[]{:S(2)}) collective-permute-start(bf16[512,512]{1,0:T(8,128)(2,1)} %fusion.4), channel_id=1, source_target_pairs={{0,16},{8,24},{16,0},{24,8},{1,17},{9,25},{17,1},{25,9},{2,18},{10... | collective-permute-start | bytes 1572872 | tf_op jit(solution)/shard_map/ppermute | solution.py:79
  174.8 44.0 %collective-permute-start.37 = (bf16[512,512]{1,0:T(8,128)(2,1)}, bf16[512,512]{1,0:T(8,128)(2,1)S(1)}, u32[]{:S(2)}, u32[]{:S(2)}) collective-permute-start(bf16[512,512]{1,0:T(8,128)(2,1)} %fusion.3), channel_id=1, source_target_pairs={{0,8},{8,16},{16,24},{24,0},{1,9},{9,17},{17,25},{25,1},{2,10},{10... | collective-permute-start | bytes 1572872 | tf_op jit(solution)/shard_map/ppermute | solution.py:79
  179.7 39.1 %collective-permute-start.35 = (bf16[512,512]{1,0:T(8,128)(2,1)}, bf16[512,512]{1,0:T(8,128)(2,1)S(1)}, u32[]{:S(2)}, u32[]{:S(2)}) collective-permute-start(bf16[512,512]{1,0:T(8,128)(2,1)} %fusion.8), channel_id=1, source_target_pairs={{0,24},{8,0},{16,8},{24,16},{1,25},{9,1},{17,9},{25,17},{2,26},{10... | collective-permute-start | bytes 1572872 | tf_op jit(solution)/shard_map/ppermute | solution.py:79
  220.7 19.7 %collective-permute-start.16 = (bf16[512,512]{1,0:T(8,128)(2,1)S(1)}, bf16[512,512]{1,0:T(8,128)(2,1)S(1)}, u32[]{:S(2)}, u32[]{:S(2)}) collective-permute-start(bf16[512,512]{1,0:T(8,128)(2,1)S(1)} %get-tuple-element.39), channel_id=1, source_target_pairs={{0,2},{1,3},{2,0},{3,1},{4,6},{5,7},{6,4},{7,5},{8,10},{9,11},{10,... | collective-permute-start | bytes 1572872 | tf_op jit(solution)/shard_map/ppermute | solution.py:40
  221.3 34.0 %collective-permute-start.18 = (bf16[512,512]{1,0:T(8,128)(2,1)}, bf16[512,512]{1,0:T(8,128)(2,1)S(1)}, u32[]{:S(2)}, u32[]{:S(2)}) collective-permute-start(bf16[512,512]{1,0:T(8,128)(2,1)} %copy-done.17), channel_id=1, source_target_pairs={{0,2},{1,3},{2,0},{3,1},{4,6},{5,7},{6,4},{7,5},{8,10},{9,11},{10,... | collective-permute-start | bytes 1572872 | tf_op jit(solution)/shard_map/ppermute | solution.py:40
  240.5 16.5 %collective-permute-start.21 = (bf16[512,512]{1,0:T(8,128)(2,1)S(1)}, bf16[512,512]{1,0:T(8,128)(2,1)S(1)}, u32[]{:S(2)}, u32[]{:S(2)}) collective-permute-start(bf16[512,512]{1,0:T(8,128)(2,1)S(1)} %get-tuple-element.45), channel_id=1, source_target_pairs={{0,4},{1,5},{2,6},{3,7},{4,0},{5,1},{6,2},{7,3},{8,12},{9,13},{10,... | collective-permute-start | bytes 1572872 | tf_op jit(solution)/shard_map/ppermute | solution.py:40
  240.5 34.5 %collective-permute-start.22 = (bf16[512,512]{1,0:T(8,128)(2,1)S(1)}, bf16[512,512]{1,0:T(8,128)(2,1)S(1)}, u32[]{:S(2)}, u32[]{:S(2)}) collective-permute-start(bf16[512,512]{1,0:T(8,128)(2,1)S(1)} %get-tuple-element.46), channel_id=1, source_target_pairs={{0,2},{1,3},{2,0},{3,1},{4,6},{5,7},{6,4},{7,5},{8,10},{9,11},{10,... | collective-permute-start | bytes 1572872 | tf_op jit(solution)/shard_map/ppermute | solution.py:40
  256.6 65.7 %collective-permute-start.28 = (bf16[512,2048]{1,0:T(8,128)(2,1)S(1)}, bf16[512,2048]{1,0:T(8,128)(2,1)S(1)}, u32[]{:S(2)}, u32[]{:S(2)}) collective-permute-start(bf16[512,2048]{1,0:T(8,128)(2,1)S(1)} %pad_maximum_fusion.9), channel_id=1, source_target_pairs={{0,1},{1,0},{2,3},{3,2},{4,5},{5,4},{6,7},{7,6},{8,9},{9,8},{10,11... | collective-permute-start | bytes 6291464 | tf_op jit(solution)/shard_map/ppermute | solution.py:40
  256.7 29.6 %collective-permute-start.20 = (bf16[512,512]{1,0:T(8,128)(2,1)S(1)}, bf16[512,512]{1,0:T(8,128)(2,1)S(1)}, u32[]{:S(2)}, u32[]{:S(2)}) collective-permute-start(bf16[512,512]{1,0:T(8,128)(2,1)S(1)} %get-tuple-element.45), channel_id=1, source_target_pairs={{0,2},{1,3},{2,0},{3,1},{4,6},{5,7},{6,4},{7,5},{8,10},{9,11},{10,... | collective-permute-start | bytes 1572872 | tf_op jit(solution)/shard_map/ppermute | solution.py:40
  275.0 20.5 %collective-permute-start.25 = (bf16[512,512]{1,0:T(8,128)(2,1)S(1)}, bf16[512,512]{1,0:T(8,128)(2,1)S(1)}, u32[]{:S(2)}, u32[]{:S(2)}) collective-permute-start(bf16[512,512]{1,0:T(8,128)(2,1)S(1)} %collective-permute-done.21), channel_id=1, source_target_pairs={{0,2},{1,3},{2,0},{3,1},{4,6},{5,7},{6,4},{7,5},{8,10},{9,11},{10,... | collective-permute-start | bytes 1572872 | tf_op jit(solution)/shard_map/ppermute | solution.py:40
  295.7 29.4 %collective-permute-start.26 = (bf16[512,2048]{1,0:T(8,128)(2,1)S(1)}, bf16[512,2048]{1,0:T(8,128)(2,1)S(1)}, u32[]{:S(2)}, u32[]{:S(2)}) collective-permute-start(bf16[512,2048]{1,0:T(8,128)(2,1)S(1)} %pad_maximum_fusion.8), channel_id=1, source_target_pairs={{0,1},{1,0},{2,3},{3,2},{4,5},{5,4},{6,7},{7,6},{8,9},{9,8},{10,11... | collective-permute-start | bytes 6291464 | tf_op jit(solution)/shard_map/ppermute | solution.py:40
  295.8 15.1 %collective-permute-start.30 = (bf16[512,512]{1,0:T(8,128)(2,1)S(1)}, bf16[512,512]{1,0:T(8,128)(2,1)S(1)}, u32[]{:S(2)}, u32[]{:S(2)}) collective-permute-start(bf16[512,512]{1,0:T(8,128)(2,1)S(1)} %get-tuple-element.46), channel_id=1, source_target_pairs={{0,4},{1,5},{2,6},{3,7},{4,0},{5,1},{6,2},{7,3},{8,12},{9,13},{10,... | collective-permute-start | bytes 1572872 | tf_op jit(solution)/shard_map/ppermute | solution.py:40
  298.1 23.8 %collective-permute-start.31 = (bf16[512,512]{1,0:T(8,128)(2,1)S(1)}, bf16[512,512]{1,0:T(8,128)(2,1)S(1)}, u32[]{:S(2)}, u32[]{:S(2)}) collective-permute-start(bf16[512,512]{1,0:T(8,128)(2,1)S(1)} %collective-permute-done.22), channel_id=1, source_target_pairs={{0,4},{1,5},{2,6},{3,7},{4,0},{5,1},{6,2},{7,3},{8,12},{9,13},{10,... | collective-permute-start | bytes 1572872 | tf_op jit(solution)/shard_map/ppermute | solution.py:40
  325.1 23.6 %collective-permute-start.29 = (bf16[512,512]{1,0:T(8,128)(2,1)S(1)}, bf16[512,512]{1,0:T(8,128)(2,1)S(1)}, u32[]{:S(2)}, u32[]{:S(2)}) collective-permute-start(bf16[512,512]{1,0:T(8,128)(2,1)S(1)} %fusion.6), channel_id=1, source_target_pairs={{0,16},{8,24},{16,0},{24,8},{1,17},{9,25},{17,1},{25,9},{2,18},{10... | collective-permute-start | bytes 1572872 | tf_op jit(solution)/shard_map/ppermute | solution.py:79
  327.7 43.0 %collective-permute-start.27 = (bf16[512,512]{1,0:T(8,128)(2,1)S(1)}, bf16[512,512]{1,0:T(8,128)(2,1)S(1)}, u32[]{:S(2)}, u32[]{:S(2)}) collective-permute-start(bf16[512,512]{1,0:T(8,128)(2,1)S(1)} %fusion.5), channel_id=1, source_target_pairs={{0,24},{8,0},{16,8},{24,16},{1,25},{9,1},{17,9},{25,17},{2,26},{10... | collective-permute-start | bytes 1572872 | tf_op jit(solution)/shard_map/ppermute | solution.py:79
  330.3 40.4 %collective-permute-start.33 = (bf16[512,512]{1,0:T(8,128)(2,1)S(1)}, bf16[512,512]{1,0:T(8,128)(2,1)S(1)}, u32[]{:S(2)}, u32[]{:S(2)}) collective-permute-start(bf16[512,512]{1,0:T(8,128)(2,1)S(1)} %fusion.7), channel_id=1, source_target_pairs={{0,8},{8,16},{16,24},{24,0},{1,9},{9,17},{17,25},{25,1},{2,10},{10... | collective-permute-start | bytes 1572872 | tf_op jit(solution)/shard_map/ppermute | solution.py:79
  (68 other events, 1198.9 us)
Sparse Core Ops, SparseCore 0:
  8.9 45.6 all-gather.5
  56.2 44.6 all-gather.3
  220.9 53.2 all-gather.7

commit v7 on v6

--- a/solution.py
+++ b/solution.py
@@ -40,6 +40,10 @@
     return lax.ppermute(block, "tensor", [(j, j ^ bit) for j in range(X + Y + CORE + 1)])
 
 
+def shift(block, by, n):
+    return lax.ppermute(block, "dp", [(z, (z + by) % n) for z in range(n)])
+
+
 def in_order(held, column):
     width = held.shape[0] // (X + Y + CORE + 1)
     offsets = [0, X, Y, X + Y]
@@ -48,7 +52,7 @@
     return jnp.concatenate(blocks, axis=0)
 
 
-def after(values, *others):
+def after(values, others):
     return lax.optimization_barrier((values, others))[0]
 
 
@@ -56,53 +60,78 @@
     column = lax.axis_index("tensor")
     me = lax.axis_index("dp")
     mine = (acts[0], grads[0])
-    held = (basis_in_held[0], basis_out_held[0])
+    tokens = acts.shape[1]
     behind = [(me - owners[side, column]) % n_dp for side in (0, 1)]
-    half = held[0].shape[0] // 2
-    everyone = [lax.all_gather(block, "dp") for block in mine]
-    ordered = [in_order(block, column) for block in held]
+    ordered = [in_order(block[0], column) for block in (basis_in_held, basis_out_held)]
+    half = ordered[0].shape[0] // 2
 
-    def piece(side, i):
-        if i == 0:
-            return mine[side]
-        return lax.dynamic_index_in_dim(everyone[side], (me + i) % n_dp, 0, keepdims=False)
+    def near(i):
+        return min(i, n_dp - i)
 
+    acts_order = sorted(range(1, n_dp), key=near)
+    grads_order = sorted(range(n_dp), key=lambda i: (-near(i), -i))
+    groups = [[(0, 0)]]
+    groups += [[(0, i) for i in acts_order[at : at + 2]] for at in range(0, len(acts_order), 2)]
+    groups += [[(1, i) for i in grads_order[at : at + 2]] for at in range(0, len(grads_order), 2)]
+
+    all_grads = lax.all_gather(mine[1], "dp")
+    pieces = {(0, 0): mine[0], (1, 0): mine[1]}
+    for i in acts_order[:2]:
+        pieces[0, i] = shift(mine[0], -i, n_dp)
+    for i in range(1, n_dp):
+        pieces[1, i] = lax.dynamic_index_in_dim(all_grads, (me + i) % n_dp, 0, keepdims=False)
+
+    due = []
     rotated, returned = {}, {}
+    even = odd = None
 
-    def rotate(key, blocks):
-        side, i = key
-        even = jnp.concatenate(blocks, axis=1)
-        odd = swap(even, CORE)
-        rotated[key] = (dot(even, ordered[side][:half]) + dot(odd, ordered[side][half:])).astype(jnp.bfloat16)
-        returned[key] = rotated[key]
-        if i:
-            returned[key] = lax.ppermute(rotated[key], "dp", [(z, (z + i) % n_dp) for z in range(n_dp)])
+    def rotate(group):
+        side = group[0][0]
+        low, high = ordered[side][:half], ordered[side][half:]
+        rot = [(dot(e, low) + dot(o, high)).astype(jnp.bfloat16) for e, o in zip(even, odd)]
+        if len(group) == 1:
+            rotated[group[0]] = jnp.concatenate(rot, axis=0)
+        else:
+            rotated.update(zip(group, rot))
+        return [rotated[key] for key in group]
 
-    keys = [(0, 0), (1, 0)] + [(0, i) for i in range(1, n_dp)]
-    keys += [(1, i) for i in sorted(range(1, n_dp), key=lambda i: -min(i, n_dp - i))]
-    slots = []
+    def send_back(group):
+        for side, i in group:
+            returned[side, i] = shift(rotated[side, i], i, n_dp) if i else rotated[side, i]
 
-    def slot(to_x, to_y):
-        if slots:
-            others = [slots[-1][0]]
-            if len(slots) > 1:
-                others.append(slots[-2][1])
-            at = len(slots) // 3
-            if at > 1 and len(slots) % 3 == 2:
-                others.append([rotated[key] for key in keys[2 * at - 4 : 2 * at - 2]])
-            if at > 2 and len(slots) % 3 == 2:
-                others.append([returned[key] for key in keys[2 * at - 6 : 2 * at - 4]])
-            to_x, to_y = after([to_x, to_y], *others)
-        slots.append(([to_x, to_y], [swap(to_x, X), swap(to_y, Y)]))
-        return slots[-1][1]
+    for at, group in enumerate(groups):
+        stack = jnp.concatenate([pieces[key] for key in group], axis=0)
+        stack = after(stack, due)
+        x, y = swap(stack, X), swap(stack, Y)
+        due = [x, y]
+        if at == 1:
+            for i in acts_order[2:]:
+                pieces[0, i] = shift(after(mine[0], stack), -i, n_dp)
+        if at > 0:
+            odd = [swap(block, CORE) for block in even]
+            due.append(odd)
+        if at > 1:
+            send_back(groups[at - 2])
+            due.append([returned[key] for key in groups[at - 2]])
+        if at == 0:
+            due.append([pieces[0, i] for i in acts_order[:2]])
+        rows = stack.shape[0] // 2
+        to_x, to_y = after((y[rows:], x[:rows]), due)
+        diagonal = [swap(to_y, Y), swap(to_x, X)]
+        due = [diagonal]
+        if at > 0:
+            due.append(rotate(groups[at - 1]))
+        if at == 1:
+            due.append([pieces[0, i] for i in acts_order[2:]])
+        upper = jnp.concatenate([stack[:rows], x[:rows], y[:rows], diagonal[0]], axis=1)
+        lower = jnp.concatenate([stack[rows:], x[rows:], y[rows:], diagonal[1]], axis=1)
+        even = [upper, lower]
 
-    for at in range(0, len(keys), 2):
-        p, q = piece(*keys[at]), piece(*keys[at + 1])
-        p_x, q_y = slot(p, q)
-        q_x, p_y = slot(q, p)
-        q_xy, p_xy = slot(q_y, p_x)
-        rotate(keys[at], [p, p_x, p_y, p_xy])
-        rotate(keys[at + 1], [q, q_x, q_y, q_xy])
+    send_back(groups[-2])
+    even = after(even, due)
+    odd = [swap(block, CORE) for block in even]
+    rotate(groups[-1])
+    send_back(groups[-1])
 
     found = []
     for side in (0, 1):
@@ -111,7 +140,7 @@
             total = jnp.where(behind[side] == i, returned[side, i], total)
         found.append(total)
     all_rot_in = lax.all_gather(found[0], "tensor", axis=1, tiled=True)
-    return product_and_divide(found[1], all_rot_in, eig_lambda, acts.shape[1])
+    return product_and_divide(found[1], all_rot_in, eig_lambda, tokens)
 
 
 def solution(mesh):

time: 389 us -> 311 us (0.80)
  waiting for transfers between devices: 273 us -> 184 us
  starting transfers between devices: 30.6 us -> 39.9 us
    ppermute x32 -> x30, waiting for transfers between devices: 198 us -> 87.6 us  [swap(): lax.ppermute(block, 'tensor', [(j, j ^ bit) for j in range(X + Y + CORE +...]
    ppermute x6 -> x9, waiting for transfers between devices: 74.2 us -> 96.6 us  [shift(): return lax.ppermute(block, 'dp', [(z, (z + by) % n) for z in range(n)])]
    ppermute x6 -> x9, starting transfers between devices: 5.22 us -> 18.4 us  [shift(): return lax.ppermute(block, 'dp', [(z, (z + by) % n) for z in range(n)])]
    slice x0 -> x15, local copies, waits for them, and re-layouts: none -> 9.62 us  [the longest x5 3.98 us: move_inputs(): y[:rows]]
    dynamic_slice x2, local copies, waits for them, and re-layouts: 7.96 us -> 2.76 us  [in_order(): lax.dynamic_slice(held, ((column ^ i) * width, 0), (width, held.shape[1]))]
    ppermute x32 -> x30, starting transfers between devices: 25.3 us -> 21.5 us  [swap(): lax.ppermute(block, 'tensor', [(j, j ^ bit) for j in range(X + Y + CORE +...]
    concatenate x8 -> x15, other arithmetic: 9.73 us -> 7.54 us  [the longest x5 3.86 us: move_inputs(): jnp.concatenate([stack[:rows], x[:rows], y[:rows], diagonal[0]], axis=1)]
    dot_general x16 -> x19, matrix products: 33.1 us -> 33.3 us  [dot(): return jnp.dot(a, b, preferred_element_type=jnp.float32)]
  transfers between devices with their start and end apart: 41 -> 41, of which waited for: 25 -> 20; matrix products, arithmetic and copies ran while one was open for 14% -> 19% of each run, Pallas kernels for 0% -> 0%
where the time goes in v7:
time: 311 us; the launch traced here: 310 us
  waiting for transfers between devices  184 us (59%)
  matrix products  43.9 us (14%)
  starting transfers between devices  39.9 us (13%)
  between operations  17.2 us (6%)
  local copies, waits for them, and re-layouts  15.3 us (5%)
  other arithmetic  9.77 us (3%)
    ppermute x9, waiting for transfers between devices, shift(): return lax.ppermute(block, 'dp', [(z, (z + by) % n) for z in range(n)])  96.6 us
    ppermute x30, waiting for transfers between devices, swap(): lax.ppermute(block, 'tensor', [(j, j ^ bit) for j in range(X + Y + CORE +...  87.6 us
    dot_general x19, matrix products, dot(): return jnp.dot(a, b, preferred_element_type=jnp.float32)  33.3 us
    ppermute x30, starting transfers between devices, swap(): lax.ppermute(block, 'tensor', [(j, j ^ bit) for j in range(X + Y + CORE +...  21.5 us
    ppermute x9, starting transfers between devices, shift(): return lax.ppermute(block, 'dp', [(z, (z + by) % n) for z in range(n)])  18.4 us
    dot_general x1, matrix products, product_and_divide(): lax.dot_general(rot_out, all_rot_in, contract, preferred_element_type=jnp...  10.7 us
  transfers between devices with their start and end apart: 41, of which 20 were waited for; matrix products, arithmetic and copies ran while one was open for 19% of the time, Pallas kernels for 0%

profile of v7, /device:TPU:16, one launch (start us, length us, event | category | flops | bytes accessed | tf_op | source)
XLA Modules:
  0.0 310.5 jit_solution(4453407504394528686)
XLA Ops:
  12.5 8.7 %collective-permute-done.2 = bf16[512,512]{1,0:T(8,128)(2,1)S(1)} collective-permute-done((bf16[512,512]{1,0:T(8,128)(2,1)}, bf16[512,512]{1,0:T(8,128)(2,1)S(1)}, u32[]{:S(2)}, u32[]{:S(2)}) %collective-permute-start.2) | collective-permute-done | bytes 524320 | tf_op jit(solution)/shard_map/ppermute | solution.py:40
  22.5 15.2 %collective-permute-done.1 = bf16[512,512]{1,0:T(8,128)(2,1)S(1)} collective-permute-done((bf16[512,512]{1,0:T(8,128)(2,1)}, bf16[512,512]{1,0:T(8,128)(2,1)S(1)}, u32[]{:S(2)}, u32[]{:S(2)}) %collective-permute-start.1) | collective-permute-done | bytes 524320 | tf_op jit(solution)/shard_map/ppermute | solution.py:44
  37.8 18.6 %collective-permute-done = bf16[512,512]{1,0:T(8,128)(2,1)S(1)} collective-permute-done((bf16[512,512]{1,0:T(8,128)(2,1)}, bf16[512,512]{1,0:T(8,128)(2,1)S(1)}, u32[]{:S(2)}, u32[]{:S(2)}) %collective-permute-start) | collective-permute-done | bytes 524320 | tf_op jit(solution)/shard_map/ppermute | solution.py:44
  57.8 6.1 %collective-permute-done.4 = bf16[256,512]{1,0:T(8,128)(2,1)S(1)} collective-permute-done((bf16[256,512]{1,0:T(8,128)(2,1)S(1)}, bf16[256,512]{1,0:T(8,128)(2,1)S(1)}, u32[]{:S(2)}, u32[]{:S(2)}) %collective-permute-start.4) | collective-permute-done | bytes 262176 | tf_op jit(solution)/shard_map/ppermute | solution.py:40
  67.4 2.1 collective-permute-start.6
  69.6 17.9 %collective-permute-done.7 = bf16[1024,512]{1,0:T(8,128)(2,1)S(1)} collective-permute-done((bf16[1024,512]{1,0:T(8,128)(2,1)S(1)}, bf16[1024,512]{1,0:T(8,128)(2,1)S(1)}, u32[]{:S(2)}, u32[]{:S(2)}) %collective-permute-start.7) | collective-permute-done | bytes 1048608 | tf_op jit(solution)/shard_map/ppermute | solution.py:40
  92.2 8.1 %collective-permute-done.12 = bf16[512,512]{1,0:T(8,128)(2,1)S(1)} collective-permute-done((bf16[512,512]{1,0:T(8,128)(2,1)S(1)}, bf16[512,512]{1,0:T(8,128)(2,1)S(1)}, u32[]{:S(2)}, u32[]{:S(2)}) %collective-permute-start.12) | collective-permute-done | bytes 524320 | tf_op jit(solution)/shard_map/ppermute | solution.py:40
  107.3 13.2 %collective-permute-done.13 = bf16[512,512]{1,0:T(8,128)(2,1)} collective-permute-done((bf16[512,512]{1,0:T(8,128)(2,1)}, bf16[512,512]{1,0:T(8,128)(2,1)}, u32[]{:S(2)}, u32[]{:S(2)}) %collective-permute-start.13) | collective-permute-done | bytes 524320 | tf_op jit(solution)/shard_map/ppermute | solution.py:40
  122.3 1.9 fusion.32
  126.8 2.8 fusion.39
  129.7 3.0 fusion.38
  140.6 3.7 %collective-permute-start.24 = (bf16[512,512]{1,0:T(8,128)(2,1)S(1)}, bf16[512,512]{1,0:T(8,128)(2,1)S(1)}, u32[]{:S(2)}, u32[]{:S(2)}) collective-permute-start(bf16[512,512]{1,0:T(8,128)(2,1)S(1)} %fusion.2), channel_id=1, source_target_pairs={{0,24},{8,0},{16,8},{24,16},{1,25},{9,1},{17,9},{25,17},{2,26},{10... | collective-permute-start | bytes 1572872 | tf_op jit(solution)/shard_map/ppermute | solution.py:44
  144.4 14.8 %collective-permute-done.20 = bf16[1024,512]{1,0:T(8,128)(2,1)S(1)} collective-permute-done((bf16[1024,512]{1,0:T(8,128)(2,1)S(1)}, bf16[1024,512]{1,0:T(8,128)(2,1)S(1)}, u32[]{:S(2)}, u32[]{:S(2)}) %collective-permute-start.20) | collective-permute-done | bytes 1048608 | tf_op jit(solution)/shard_map/ppermute | solution.py:40
  159.3 2.1 collective-permute-done.19
  161.6 11.5 %collective-permute-done.23 = bf16[512,512]{1,0:T(8,128)(2,1)S(1)} collective-permute-done((bf16[512,512]{1,0:T(8,128)(2,1)S(1)}, bf16[512,512]{1,0:T(8,128)(2,1)S(1)}, u32[]{:S(2)}, u32[]{:S(2)}) %collective-permute-start.23) | collective-permute-done | bytes 524320 | tf_op jit(solution)/shard_map/ppermute | solution.py:44
  178.0 6.1 %collective-permute-done.25 = bf16[512,512]{1,0:T(8,128)(2,1)S(1)} collective-permute-done((bf16[512,512]{1,0:T(8,128)(2,1)S(1)}, bf16[512,512]{1,0:T(8,128)(2,1)S(1)}, u32[]{:S(2)}, u32[]{:S(2)}) %collective-permute-start.25) | collective-permute-done | bytes 524320 | tf_op jit(solution)/shard_map/ppermute | solution.py:40
  193.2 19.3 %collective-permute-done.33 = bf16[512,512]{1,0:T(8,128)(2,1)} collective-permute-done((bf16[512,512]{1,0:T(8,128)(2,1)}, bf16[512,512]{1,0:T(8,128)(2,1)}, u32[]{:S(2)}, u32[]{:S(2)}) %collective-permute-start.33) | collective-permute-done | bytes 524320 | tf_op jit(solution)/shard_map/ppermute | solution.py:44
  212.4 2.2 select_select_fusion
  214.7 2.4 dynamic-slice_bitcast_fusion.8
  217.3 2.1 fusion.23
  222.9 3.0 fusion.20
  226.0 3.0 fusion.19
  229.0 2.0 fusion.3
  231.1 2.1 fusion.4
  233.1 6.7 %collective-permute-done.34 = bf16[512,512]{1,0:T(8,128)(2,1)S(1)} collective-permute-done((bf16[512,512]{1,0:T(8,128)(2,1)S(1)}, bf16[512,512]{1,0:T(8,128)(2,1)S(1)}, u32[]{:S(2)}, u32[]{:S(2)}) %collective-permute-start.34) | collective-permute-done | bytes 524320 | tf_op jit(solution)/shard_map/ppermute | solution.py:40
  242.9 4.4 %collective-permute-start.30 = (bf16[512,512]{1,0:T(8,128)(2,1)}, bf16[512,512]{1,0:T(8,128)(2,1)}, u32[]{:S(2)}, u32[]{:S(2)}) collective-permute-start(bf16[512,512]{1,0:T(8,128)(2,1)} %fusion.4), channel_id=1, source_target_pairs={{0,16},{8,24},{16,0},{24,8},{1,17},{9,25},{17,1},{25,9},{2,18},{10... | collective-permute-start | bytes 1572872 | tf_op jit(solution)/shard_map/ppermute | solution.py:44
  248.7 2.1 fusion.5
  250.8 4.3 %collective-permute-start.37 = (bf16[512,512]{1,0:T(8,128)(2,1)}, bf16[512,512]{1,0:T(8,128)(2,1)}, u32[]{:S(2)}, u32[]{:S(2)}) collective-permute-start(bf16[512,512]{1,0:T(8,128)(2,1)} %fusion.5), channel_id=1, source_target_pairs={{0,8},{8,16},{16,24},{24,0},{1,9},{9,17},{17,25},{25,1},{2,10},{10... | collective-permute-start | bytes 1572872 | tf_op jit(solution)/shard_map/ppermute | solution.py:44
  255.8 4.5 %fusion.17 = f32[512,512]{1,0:T(8,128)} fusion(bf16[512,2048]{1,0:T(8,128)(2,1)} %collective-permute-done.38, bf16[512,512]{1,0:T(8,128)(2,1)} %copy-done.51, bf16[512,512]{1,0:T(8,128)(2,1)} %copy-done.52, bf16[512,512]{1,0:T(8,128)(2,1)} %copy-done.49, bf16[512,512]{1,0:T(8,128)(2,1)} %copy-done.50), kind=kOutput, calls=%fused_computation.69 | convolution fusion | flops 1082130432 | bytes 5242880 | tf_op jit(solution)/shard_map/dot_general | solution.py:22
  260.3 28.0 %collective-permute-done.30 = bf16[512,512]{1,0:T(8,128)(2,1)} collective-permute-done((bf16[512,512]{1,0:T(8,128)(2,1)}, bf16[512,512]{1,0:T(8,128)(2,1)}, u32[]{:S(2)}, u32[]{:S(2)}) %collective-permute-start.30) | collective-permute-done | bytes 524320 | tf_op jit(solution)/shard_map/ppermute | solution.py:44
  288.3 4.0 %collective-permute-done.37 = bf16[512,512]{1,0:T(8,128)(2,1)} collective-permute-done((bf16[512,512]{1,0:T(8,128)(2,1)}, bf16[512,512]{1,0:T(8,128)(2,1)}, u32[]{:S(2)}, u32[]{:S(2)}) %collective-permute-start.37) | collective-permute-done | bytes 524320 | tf_op jit(solution)/shard_map/ppermute | solution.py:44
  292.4 10.7 %fusion = bf16[1,512,4096]{2,1,0:T(8,128)(2,1)} fusion(bf16[512,4096]{1,0:T(8,128)(2,1)} %param.11, bf16[512,4096]{1,0:T(8,128)(2,1)} %all-gather.5.cloned.1.call-done, bf16[512,512]{1,0:T(8,128)(2,1)} %collective-permute-done.27, bf16[512,512]{1,0:T(8,128)(2,1)} %collective-permute-done.30, bf16[512,512]{1,0:T(8,128)(2,1)} %collective-permute-done.37, ...), kind=kOutput, calls=%fused_computation.1 | convolution fusion | flops 3241410560 | bytes 19398660 | tf_op jit(solution)/shard_map/dot_general | solution.py:13
  (217 shorter events, 56.6 us)
Async XLA Ops:
  7.4 116.8 %all-gather.3.cloned.1.call-start = ((), (), s32[]{:S(2)}) async-start(), calls=%async_computation | async-start | bytes 2621440 | tf_op jit(solution)/shard_map/all_gather | solution.py:77
  7.4 13.9 %collective-permute-start.2 = (bf16[512,512]{1,0:T(8,128)(2,1)}, bf16[512,512]{1,0:T(8,128)(2,1)S(1)}, u32[]{:S(2)}, u32[]{:S(2)}) collective-permute-start(bf16[512,512]{1,0:T(8,128)(2,1)} %bitcast.3), channel_id=1, source_target_pairs={{0,4},{1,5},{2,6},{3,7},{4,0},{5,1},{6,2},{7,3},{8,12},{9,13},{10,... | collective-permute-start | bytes 1572872 | tf_op jit(solution)/shard_map/ppermute | solution.py:40
  8.9 13.6 %collective-permute-start.3 = (bf16[512,512]{1,0:T(8,128)(2,1)}, bf16[512,512]{1,0:T(8,128)(2,1)S(1)}, u32[]{:S(2)}, u32[]{:S(2)}) collective-permute-start(bf16[512,512]{1,0:T(8,128)(2,1)} %bitcast.3), channel_id=1, source_target_pairs={{0,2},{1,3},{2,0},{3,1},{4,6},{5,7},{6,4},{7,5},{8,10},{9,11},{10,... | collective-permute-start | bytes 1572872 | tf_op jit(solution)/shard_map/ppermute | solution.py:40
  10.4 27.4 %collective-permute-start.1 = (bf16[512,512]{1,0:T(8,128)(2,1)}, bf16[512,512]{1,0:T(8,128)(2,1)S(1)}, u32[]{:S(2)}, u32[]{:S(2)}) collective-permute-start(bf16[512,512]{1,0:T(8,128)(2,1)} %bitcast.3), channel_id=1, source_target_pairs={{0,8},{8,16},{16,24},{24,0},{1,9},{9,17},{17,25},{25,1},{2,10},{10... | collective-permute-start | bytes 1572872 | tf_op jit(solution)/shard_map/ppermute | solution.py:44
  12.0 44.4 %collective-permute-start = (bf16[512,512]{1,0:T(8,128)(2,1)}, bf16[512,512]{1,0:T(8,128)(2,1)S(1)}, u32[]{:S(2)}, u32[]{:S(2)}) collective-permute-start(bf16[512,512]{1,0:T(8,128)(2,1)} %bitcast.3), channel_id=1, source_target_pairs={{0,24},{8,0},{16,8},{24,16},{1,25},{9,1},{17,9},{25,17},{2,26},{10... | collective-permute-start | bytes 1572872 | tf_op jit(solution)/shard_map/ppermute | solution.py:44
  12.4 279.9 %all-gather.5.cloned.1.call-start = ((), (), s32[]{:S(2)}) async-start(), calls=%async_computation.1 | async-start | bytes 4718592 | tf_op jit(solution)/shard_map/all_gather | solution.py:142
  63.9 23.6 %collective-permute-start.7 = (bf16[1024,512]{1,0:T(8,128)(2,1)S(1)}, bf16[1024,512]{1,0:T(8,128)(2,1)S(1)}, u32[]{:S(2)}, u32[]{:S(2)}) collective-permute-start(bf16[1024,512]{1,0:T(8,128)(2,1)S(1)} %pad_maximum_fusion.11), channel_id=1, source_target_pairs={{0,4},{1,5},{2,6},{3,7},{4,0},{5,1},{6,2},{7,3},{8,12},{9,13},{10,... | collective-permute-start | bytes 3145736 | tf_op jit(solution)/shard_map/ppermute | solution.py:40
  66.0 23.2 %collective-permute-start.8 = (bf16[1024,512]{1,0:T(8,128)(2,1)S(1)}, bf16[1024,512]{1,0:T(8,128)(2,1)S(1)}, u32[]{:S(2)}, u32[]{:S(2)}) collective-permute-start(bf16[1024,512]{1,0:T(8,128)(2,1)S(1)} %pad_maximum_fusion.11), channel_id=1, source_target_pairs={{0,2},{1,3},{2,0},{3,1},{4,6},{5,7},{6,4},{7,5},{8,10},{9,11},{10,... | collective-permute-start | bytes 3145736 | tf_op jit(solution)/shard_map/ppermute | solution.py:40
  66.5 22.8 %collective-permute-start.9 = (bf16[256,2048]{1,0:T(8,128)(2,1)S(1)}, bf16[256,2048]{1,0:T(8,128)(2,1)S(1)}, u32[]{:S(2)}, u32[]{:S(2)}) collective-permute-start(bf16[256,2048]{1,0:T(8,128)(2,1)S(1)} %pad_maximum_fusion.12), channel_id=1, source_target_pairs={{0,1},{1,0},{2,3},{3,2},{4,5},{5,4},{6,7},{7,6},{8,9},{9,8},{10,11... | collective-permute-start | bytes 3145736 | tf_op jit(solution)/shard_map/ppermute | solution.py:40
  66.7 22.6 %collective-permute-start.10 = (bf16[256,2048]{1,0:T(8,128)(2,1)S(1)}, bf16[256,2048]{1,0:T(8,128)(2,1)S(1)}, u32[]{:S(2)}, u32[]{:S(2)}) collective-permute-start(bf16[256,2048]{1,0:T(8,128)(2,1)S(1)} %pad_maximum_fusion.13), channel_id=1, source_target_pairs={{0,1},{1,0},{2,3},{3,2},{4,5},{5,4},{6,7},{7,6},{8,9},{9,8},{10,11... | collective-permute-start | bytes 3145736 | tf_op jit(solution)/shard_map/ppermute | solution.py:40
  67.4 38.9 %collective-permute-start.6 = (bf16[512,512]{1,0:T(8,128)(2,1)}, bf16[512,512]{1,0:T(8,128)(2,1)}, u32[]{:S(2)}, u32[]{:S(2)}) collective-permute-start(bf16[512,512]{1,0:T(8,128)(2,1)} %bitcast.3), channel_id=1, source_target_pairs={{0,16},{8,24},{16,0},{24,8},{1,17},{9,25},{17,1},{25,9},{2,18},{10... | collective-permute-start | bytes 1572872 | tf_op jit(solution)/shard_map/ppermute | solution.py:44
  102.0 23.8 %collective-permute-start.16 = (bf16[512,2048]{1,0:T(8,128)(2,1)}, bf16[512,2048]{1,0:T(8,128)(2,1)}, u32[]{:S(2)}, u32[]{:S(2)}) collective-permute-start(bf16[512,2048]{1,0:T(8,128)(2,1)} %pad_maximum_fusion.3), channel_id=1, source_target_pairs={{0,1},{1,0},{2,3},{3,2},{4,5},{5,4},{6,7},{7,6},{8,9},{9,8},{10,11... | collective-permute-start | bytes 6291464 | tf_op jit(solution)/shard_map/ppermute | solution.py:40
  103.7 22.1 %collective-permute-start.15 = (bf16[512,2048]{1,0:T(8,128)(2,1)}, bf16[512,2048]{1,0:T(8,128)(2,1)}, u32[]{:S(2)}, u32[]{:S(2)}) collective-permute-start(bf16[512,2048]{1,0:T(8,128)(2,1)} %pad_maximum_fusion.2), channel_id=1, source_target_pairs={{0,1},{1,0},{2,3},{3,2},{4,5},{5,4},{6,7},{7,6},{8,9},{9,8},{10,11... | collective-permute-start | bytes 6291464 | tf_op jit(solution)/shard_map/ppermute | solution.py:40
  106.4 14.2 %collective-permute-start.13 = (bf16[512,512]{1,0:T(8,128)(2,1)}, bf16[512,512]{1,0:T(8,128)(2,1)}, u32[]{:S(2)}, u32[]{:S(2)}) collective-permute-start(bf16[512,512]{1,0:T(8,128)(2,1)} %collective-permute-done.6), channel_id=1, source_target_pairs={{0,4},{1,5},{2,6},{3,7},{4,0},{5,1},{6,2},{7,3},{8,12},{9,13},{10,... | collective-permute-start | bytes 1572872 | tf_op jit(solution)/shard_map/ppermute | solution.py:40
  107.0 15.3 %collective-permute-start.14 = (bf16[512,512]{1,0:T(8,128)(2,1)}, bf16[512,512]{1,0:T(8,128)(2,1)}, u32[]{:S(2)}, u32[]{:S(2)}) collective-permute-start(bf16[512,512]{1,0:T(8,128)(2,1)} %collective-permute-done.6), channel_id=1, source_target_pairs={{0,2},{1,3},{2,0},{3,1},{4,6},{5,7},{6,4},{7,5},{8,10},{9,11},{10,... | collective-permute-start | bytes 1572872 | tf_op jit(solution)/shard_map/ppermute | solution.py:40
  135.4 23.8 %collective-permute-start.20 = (bf16[1024,512]{1,0:T(8,128)(2,1)S(1)}, bf16[1024,512]{1,0:T(8,128)(2,1)S(1)}, u32[]{:S(2)}, u32[]{:S(2)}) collective-permute-start(bf16[1024,512]{1,0:T(8,128)(2,1)S(1)} %pad_maximum_fusion.10), channel_id=1, source_target_pairs={{0,4},{1,5},{2,6},{3,7},{4,0},{5,1},{6,2},{7,3},{8,12},{9,13},{10,... | collective-permute-start | bytes 3145736 | tf_op jit(solution)/shard_map/ppermute | solution.py:40
  137.9 23.6 %collective-permute-start.19 = (bf16[1024,512]{1,0:T(8,128)(2,1)S(1)}, bf16[1024,512]{1,0:T(8,128)(2,1)S(1)}, u32[]{:S(2)}, u32[]{:S(2)}) collective-permute-start(bf16[1024,512]{1,0:T(8,128)(2,1)S(1)} %pad_maximum_fusion.10), channel_id=1, source_target_pairs={{0,2},{1,3},{2,0},{3,1},{4,6},{5,7},{6,4},{7,5},{8,10},{9,11},{10,... | collective-permute-start | bytes 3145736 | tf_op jit(solution)/shard_map/ppermute | solution.py:40
  139.8 33.2 %collective-permute-start.22 = (bf16[256,2048]{1,0:T(8,128)(2,1)S(1)}, bf16[256,2048]{1,0:T(8,128)(2,1)S(1)}, u32[]{:S(2)}, u32[]{:S(2)}) collective-permute-start(bf16[256,2048]{1,0:T(8,128)(2,1)S(1)} %pad_maximum_fusion.15), channel_id=1, source_target_pairs={{0,1},{1,0},{2,3},{3,2},{4,5},{5,4},{6,7},{7,6},{8,9},{9,8},{10,11... | collective-permute-start | bytes 3145736 | tf_op jit(solution)/shard_map/ppermute | solution.py:40
  140.0 33.0 %collective-permute-start.21 = (bf16[256,2048]{1,0:T(8,128)(2,1)S(1)}, bf16[256,2048]{1,0:T(8,128)(2,1)S(1)}, u32[]{:S(2)}, u32[]{:S(2)}) collective-permute-start(bf16[256,2048]{1,0:T(8,128)(2,1)S(1)} %pad_maximum_fusion.14), channel_id=1, source_target_pairs={{0,1},{1,0},{2,3},{3,2},{4,5},{5,4},{6,7},{7,6},{8,9},{9,8},{10,11... | collective-permute-start | bytes 3145736 | tf_op jit(solution)/shard_map/ppermute | solution.py:40
  140.6 21.0 %collective-permute-start.24 = (bf16[512,512]{1,0:T(8,128)(2,1)S(1)}, bf16[512,512]{1,0:T(8,128)(2,1)S(1)}, u32[]{:S(2)}, u32[]{:S(2)}) collective-permute-start(bf16[512,512]{1,0:T(8,128)(2,1)S(1)} %fusion.2), channel_id=1, source_target_pairs={{0,24},{8,0},{16,8},{24,16},{1,25},{9,1},{17,9},{25,17},{2,26},{10... | collective-permute-start | bytes 1572872 | tf_op jit(solution)/shard_map/ppermute | solution.py:44
  159.2 13.8 %collective-permute-start.23 = (bf16[512,512]{1,0:T(8,128)(2,1)S(1)}, bf16[512,512]{1,0:T(8,128)(2,1)S(1)}, u32[]{:S(2)}, u32[]{:S(2)}) collective-permute-start(bf16[512,512]{1,0:T(8,128)(2,1)S(1)} %fusion.1), channel_id=1, source_target_pairs={{0,8},{8,16},{16,24},{24,0},{1,9},{9,17},{17,25},{25,1},{2,10},{10... | collective-permute-start | bytes 1572872 | tf_op jit(solution)/shard_map/ppermute | solution.py:44
  184.9 35.8 %collective-permute-start.26 = (bf16[512,2048]{1,0:T(8,128)(2,1)S(1)}, bf16[512,2048]{1,0:T(8,128)(2,1)}, u32[]{:S(2)}, u32[]{:S(2)}) collective-permute-start(bf16[512,2048]{1,0:T(8,128)(2,1)S(1)} %pad_maximum_fusion.4), channel_id=1, source_target_pairs={{0,1},{1,0},{2,3},{3,2},{4,5},{5,4},{6,7},{7,6},{8,9},{9,8},{10,11... | collective-permute-start | bytes 6291464 | tf_op jit(solution)/shard_map/ppermute | solution.py:40
  186.9 33.7 %collective-permute-start.29 = (bf16[512,2048]{1,0:T(8,128)(2,1)}, bf16[512,2048]{1,0:T(8,128)(2,1)}, u32[]{:S(2)}, u32[]{:S(2)}) collective-permute-start(bf16[512,2048]{1,0:T(8,128)(2,1)} %pad_maximum_fusion.7), channel_id=1, source_target_pairs={{0,1},{1,0},{2,3},{3,2},{4,5},{5,4},{6,7},{7,6},{8,9},{9,8},{10,11... | collective-permute-start | bytes 6291464 | tf_op jit(solution)/shard_map/ppermute | solution.py:40
  188.7 23.8 %collective-permute-start.33 = (bf16[512,512]{1,0:T(8,128)(2,1)}, bf16[512,512]{1,0:T(8,128)(2,1)}, u32[]{:S(2)}, u32[]{:S(2)}) collective-permute-start(bf16[512,512]{1,0:T(8,128)(2,1)} %pad_maximum_fusion.18), channel_id=1, source_target_pairs={{0,16},{8,24},{16,0},{24,8},{1,17},{9,25},{17,1},{25,9},{2,18},{10... | collective-permute-start | bytes 1572872 | tf_op jit(solution)/shard_map/ppermute | solution.py:44
  189.2 28.1 %collective-permute-start.32 = (bf16[1024,512]{1,0:T(8,128)(2,1)S(1)}, bf16[1024,512]{1,0:T(8,128)(2,1)}, u32[]{:S(2)}, u32[]{:S(2)}) collective-permute-start(bf16[1024,512]{1,0:T(8,128)(2,1)S(1)} %pad_maximum_fusion.16), channel_id=1, source_target_pairs={{0,4},{1,5},{2,6},{3,7},{4,0},{5,1},{6,2},{7,3},{8,12},{9,13},{10,... | collective-permute-start | bytes 3145736 | tf_op jit(solution)/shard_map/ppermute | solution.py:40
  190.4 29.0 %collective-permute-start.31 = (bf16[1024,512]{1,0:T(8,128)(2,1)S(1)}, bf16[1024,512]{1,0:T(8,128)(2,1)}, u32[]{:S(2)}, u32[]{:S(2)}) collective-permute-start(bf16[1024,512]{1,0:T(8,128)(2,1)S(1)} %pad_maximum_fusion.16), channel_id=1, source_target_pairs={{0,2},{1,3},{2,0},{3,1},{4,6},{5,7},{6,4},{7,5},{8,10},{9,11},{10,... | collective-permute-start | bytes 3145736 | tf_op jit(solution)/shard_map/ppermute | solution.py:40
  220.7 19.2 %collective-permute-start.34 = (bf16[512,512]{1,0:T(8,128)(2,1)S(1)}, bf16[512,512]{1,0:T(8,128)(2,1)S(1)}, u32[]{:S(2)}, u32[]{:S(2)}) collective-permute-start(bf16[512,512]{1,0:T(8,128)(2,1)S(1)} %get-tuple-element.35), channel_id=1, source_target_pairs={{0,4},{1,5},{2,6},{3,7},{4,0},{5,1},{6,2},{7,3},{8,12},{9,13},{10,... | collective-permute-start | bytes 1572872 | tf_op jit(solution)/shard_map/ppermute | solution.py:40
  221.7 19.0 %collective-permute-start.35 = (bf16[512,512]{1,0:T(8,128)(2,1)S(1)}, bf16[512,512]{1,0:T(8,128)(2,1)S(1)}, u32[]{:S(2)}, u32[]{:S(2)}) collective-permute-start(bf16[512,512]{1,0:T(8,128)(2,1)S(1)} %get-tuple-element.36), channel_id=1, source_target_pairs={{0,2},{1,3},{2,0},{3,1},{4,6},{5,7},{6,4},{7,5},{8,10},{9,11},{10,... | collective-permute-start | bytes 1572872 | tf_op jit(solution)/shard_map/ppermute | solution.py:40
  241.0 14.7 %collective-permute-start.38 = (bf16[512,2048]{1,0:T(8,128)(2,1)S(1)}, bf16[512,2048]{1,0:T(8,128)(2,1)}, u32[]{:S(2)}, u32[]{:S(2)}) collective-permute-start(bf16[512,2048]{1,0:T(8,128)(2,1)S(1)} %pad_maximum_fusion.9), channel_id=1, source_target_pairs={{0,1},{1,0},{2,3},{3,2},{4,5},{5,4},{6,7},{7,6},{8,9},{9,8},{10,11... | collective-permute-start | bytes 6291464 | tf_op jit(solution)/shard_map/ppermute | solution.py:40
  241.5 18.8 %collective-permute-start.27 = (bf16[512,512]{1,0:T(8,128)(2,1)}, bf16[512,512]{1,0:T(8,128)(2,1)}, u32[]{:S(2)}, u32[]{:S(2)}) collective-permute-start(bf16[512,512]{1,0:T(8,128)(2,1)} %fusion.3), channel_id=1, source_target_pairs={{0,24},{8,0},{16,8},{24,16},{1,25},{9,1},{17,9},{25,17},{2,26},{10... | collective-permute-start | bytes 1572872 | tf_op jit(solution)/shard_map/ppermute | solution.py:44
  242.9 45.4 %collective-permute-start.30 = (bf16[512,512]{1,0:T(8,128)(2,1)}, bf16[512,512]{1,0:T(8,128)(2,1)}, u32[]{:S(2)}, u32[]{:S(2)}) collective-permute-start(bf16[512,512]{1,0:T(8,128)(2,1)} %fusion.4), channel_id=1, source_target_pairs={{0,16},{8,24},{16,0},{24,8},{1,17},{9,25},{17,1},{25,9},{2,18},{10... | collective-permute-start | bytes 1572872 | tf_op jit(solution)/shard_map/ppermute | solution.py:44
  250.8 41.6 %collective-permute-start.37 = (bf16[512,512]{1,0:T(8,128)(2,1)}, bf16[512,512]{1,0:T(8,128)(2,1)}, u32[]{:S(2)}, u32[]{:S(2)}) collective-permute-start(bf16[512,512]{1,0:T(8,128)(2,1)} %fusion.5), channel_id=1, source_target_pairs={{0,8},{8,16},{16,24},{24,0},{1,9},{9,17},{17,25},{25,1},{2,10},{10... | collective-permute-start | bytes 1572872 | tf_op jit(solution)/shard_map/ppermute | solution.py:44
  (64 other events, 938.9 us)
Sparse Core Ops, SparseCore 0:
  12.6 56.5 all-gather.2
Sparse Core Ops, SparseCore 1:
  214.8 44.9 all-gather.4

commit v8 on v7

--- a/solution.py
+++ b/solution.py
@@ -69,68 +69,73 @@
         return min(i, n_dp - i)
 
     acts_order = sorted(range(1, n_dp), key=near)
-    grads_order = sorted(range(n_dp), key=lambda i: (-near(i), -i))
+    grads_order = sorted(range(1, n_dp), key=lambda i: (-near(i), -i))
     groups = [[(0, 0)]]
     groups += [[(0, i) for i in acts_order[at : at + 2]] for at in range(0, len(acts_order), 2)]
     groups += [[(1, i) for i in grads_order[at : at + 2]] for at in range(0, len(grads_order), 2)]
+    groups += [[(1, 0)]]
 
-    all_grads = lax.all_gather(mine[1], "dp")
     pieces = {(0, 0): mine[0], (1, 0): mine[1]}
     for i in acts_order[:2]:
         pieces[0, i] = shift(mine[0], -i, n_dp)
-    for i in range(1, n_dp):
-        pieces[1, i] = lax.dynamic_index_in_dim(all_grads, (me + i) % n_dp, 0, keepdims=False)
 
     due = []
-    rotated, returned = {}, {}
     even = odd = None
+    rotated, returned, over = {}, {}, set()
 
     def rotate(group):
         side = group[0][0]
         low, high = ordered[side][:half], ordered[side][half:]
         rot = [(dot(e, low) + dot(o, high)).astype(jnp.bfloat16) for e, o in zip(even, odd)]
-        if len(group) == 1:
-            rotated[group[0]] = jnp.concatenate(rot, axis=0)
-        else:
-            rotated.update(zip(group, rot))
-        return [rotated[key] for key in group]
+        rotated.update(zip(group, rot))
+        return rot
 
     def send_back(group):
         for side, i in group:
-            returned[side, i] = shift(rotated[side, i], i, n_dp) if i else rotated[side, i]
+            returned[side, i] = shift(after(rotated[side, i], due), i, n_dp) if i else rotated[side, i]
 
     for at, group in enumerate(groups):
+        before = groups[at - 1] if at else []
         stack = jnp.concatenate([pieces[key] for key in group], axis=0)
         stack = after(stack, due)
-        x, y = swap(stack, X), swap(stack, Y)
-        due = [x, y]
         if at == 1:
             for i in acts_order[2:]:
-                pieces[0, i] = shift(after(mine[0], stack), -i, n_dp)
-        if at > 0:
+                pieces[0, i] = shift(after(mine[0], due), -i, n_dp)
+            all_grads = lax.all_gather(after(mine[1], due), "dp")
+            for i in range(1, n_dp):
+                pieces[1, i] = lax.dynamic_index_in_dim(all_grads, (me + i) % n_dp, 0, keepdims=False)
+        late = [key for key in rotated if key not in returned]
+        send_back(late)
+        x, y = swap(stack, X), swap(stack, Y)
+        due = [x, y, [returned[key] for key in returned if key not in over and key[0] == 0]]
+        over = set(returned)
+        if at:
             odd = [swap(block, CORE) for block in even]
-            due.append(odd)
-        if at > 1:
-            send_back(groups[at - 2])
-            due.append([returned[key] for key in groups[at - 2]])
-        if at == 0:
-            due.append([pieces[0, i] for i in acts_order[:2]])
+        early = len(group) >= len(before) and at > 1
+        if early:
+            due.append(rotate(before))
         rows = stack.shape[0] // 2
         to_x, to_y = after((y[rows:], x[:rows]), due)
+        if early:
+            send_back(before)
         diagonal = [swap(to_y, Y), swap(to_x, X)]
         due = [diagonal]
-        if at > 0:
-            due.append(rotate(groups[at - 1]))
-        if at == 1:
-            due.append([pieces[0, i] for i in acts_order[2:]])
-        upper = jnp.concatenate([stack[:rows], x[:rows], y[:rows], diagonal[0]], axis=1)
-        lower = jnp.concatenate([stack[rows:], x[rows:], y[rows:], diagonal[1]], axis=1)
-        even = [upper, lower]
+        if at and not early:
+            due.append(rotate(before))
+        if at < 2:
+            due.append([pieces[0, i] for i in (acts_order[2:] if at else acts_order[:2])])
+        if len(group) == 1:
+            even = [jnp.concatenate([stack, x, y, after(jnp.concatenate(diagonal, axis=0), [])], axis=1)]
+        else:
+            even = [
+                jnp.concatenate([stack[:rows], x[:rows], y[:rows], diagonal[0]], axis=1),
+                jnp.concatenate([stack[rows:], x[rows:], y[rows:], diagonal[1]], axis=1),
+            ]
 
-    send_back(groups[-2])
     even = after(even, due)
     odd = [swap(block, CORE) for block in even]
     rotate(groups[-1])
+    due = []
     send_back(groups[-1])
 
     found = []

time: 311 us -> 348 us (1.12)
  waiting for transfers between devices: 184 us -> 202 us
  other arithmetic: 9.77 us -> 16.5 us
  matrix products: 43.9 us -> 50.5 us
  starting transfers between devices: 39.9 us -> 44.5 us
    ppermute x30 -> x32, waiting for transfers between devices: 87.6 us -> 121 us  [swap(): lax.ppermute(block, 'tensor', [(j, j ^ bit) for j in range(X + Y + CORE +...]
    ppermute x9, waiting for transfers between devices: 96.6 us -> 81.8 us  [shift(): return lax.ppermute(block, 'dp', [(z, (z + by) % n) for z in range(n)])]
    concatenate x2 -> x8, other arithmetic: 1.02 us -> 9.35 us  [the longest x4 7.23 us: move_inputs(): jnp.concatenate([stack, x, y, after(jnp.concatenate(diagonal, axis=0), []...]
    dot_general x19 -> x15, matrix products: 33.3 us -> 39.9 us  [dot(): return jnp.dot(a, b, preferred_element_type=jnp.float32)]
    ppermute x30 -> x32, starting transfers between devices: 21.5 us -> 26.2 us  [swap(): lax.ppermute(block, 'tensor', [(j, j ^ bit) for j in range(X + Y + CORE +...]
    dynamic_slice x2, local copies, waits for them, and re-layouts: 2.76 us -> 6.84 us  [in_order(): lax.dynamic_slice(held, ((column ^ i) * width, 0), (width, held.shape[1]))]
  transfers between devices with their start and end apart: 41 -> 43, of which waited for: 20 -> 25; matrix products, arithmetic and copies ran while one was open for 19% -> 21% of each run, Pallas kernels for 0% -> 0%
where the time goes in v8:
time: 348 us
  waiting for transfers between devices  202 us (58%)
  matrix products  50.5 us (15%)
  starting transfers between devices  44.5 us (13%)
  local copies, waits for them, and re-layouts  18.1 us (5%)
  other arithmetic  16.5 us (5%)
  between operations  15.8 us (5%)
    ppermute x32, waiting for transfers between devices, swap(): lax.ppermute(block, 'tensor', [(j, j ^ bit) for j in range(X + Y + CORE +...  121 us
    ppermute x9, waiting for transfers between devices, shift(): return lax.ppermute(block, 'dp', [(z, (z + by) % n) for z in range(n)])  81.8 us
    dot_general x15, matrix products, dot(): return jnp.dot(a, b, preferred_element_type=jnp.float32)  39.9 us
    ppermute x32, starting transfers between devices, swap(): lax.ppermute(block, 'tensor', [(j, j ^ bit) for j in range(X + Y + CORE +...  26.2 us
    ppermute x9, starting transfers between devices, shift(): return lax.ppermute(block, 'dp', [(z, (z + by) % n) for z in range(n)])  18.3 us
    dot_general x1, matrix products, product_and_divide(): lax.dot_general(rot_out, all_rot_in, contract, preferred_element_type=jnp...  10.6 us
    concatenate x4, other arithmetic, move_inputs(): jnp.concatenate([stack, x, y, after(jnp.concatenate(diagonal, axis=0), []...  7.23 us
  transfers between devices with their start and end apart: 43, of which 25 were waited for; matrix products, arithmetic and copies ran while one was open for 21% of the time, Pallas kernels for 0%

profile of v8, /device:TPU:16, one launch (start us, length us, event | category | flops | bytes accessed | tf_op | source)
XLA Modules:
  0.0 347.8 jit_solution(13983955354929504953)
XLA Ops:
  11.6 8.8 %collective-permute-done = bf16[512,512]{1,0:T(8,128)(2,1)S(1)} collective-permute-done((bf16[512,512]{1,0:T(8,128)(2,1)}, bf16[512,512]{1,0:T(8,128)(2,1)S(1)}, u32[]{:S(2)}, u32[]{:S(2)}) %collective-permute-start) | collective-permute-done | bytes 524320 | tf_op jit(solution)/shard_map/ppermute | solution.py:40
  23.7 10.4 %collective-permute-done.5 = bf16[512,512]{1,0:T(8,128)(2,1)S(1)} collective-permute-done((bf16[512,512]{1,0:T(8,128)(2,1)}, bf16[512,512]{1,0:T(8,128)(2,1)S(1)}, u32[]{:S(2)}, u32[]{:S(2)}) %collective-permute-start.5) | collective-permute-done | bytes 524320 | tf_op jit(solution)/shard_map/ppermute | solution.py:44
  38.1 20.3 %collective-permute-done.7 = bf16[1024,512]{1,0:T(8,128)(2,1)} collective-permute-done((bf16[1024,512]{1,0:T(8,128)(2,1)S(1)}, bf16[1024,512]{1,0:T(8,128)(2,1)}, u32[]{:S(2)}, u32[]{:S(2)}) %collective-permute-start.7) | collective-permute-done | bytes 1048608 | tf_op jit(solution)/shard_map/ppermute | solution.py:40
  68.2 6.0 %collective-permute-done.10 = bf16[512,512]{1,0:T(8,128)(2,1)S(1)} collective-permute-done((bf16[512,512]{1,0:T(8,128)(2,1)S(1)}, bf16[512,512]{1,0:T(8,128)(2,1)S(1)}, u32[]{:S(2)}, u32[]{:S(2)}) %collective-permute-start.10) | collective-permute-done | bytes 524320 | tf_op jit(solution)/shard_map/ppermute | solution.py:40
  76.6 2.9 fusion.22
  79.6 3.1 fusion.1
  82.8 21.8 %collective-permute-done.6 = bf16[512,512]{1,0:T(8,128)(2,1)S(1)} collective-permute-done((bf16[512,512]{1,0:T(8,128)(2,1)}, bf16[512,512]{1,0:T(8,128)(2,1)S(1)}, u32[]{:S(2)}, u32[]{:S(2)}) %collective-permute-start.6) | collective-permute-done | bytes 524320 | tf_op jit(solution)/shard_map/ppermute | solution.py:44
  110.2 7.9 %collective-permute-done.12 = bf16[512,512]{1,0:T(8,128)(2,1)S(1)} collective-permute-done((bf16[512,512]{1,0:T(8,128)(2,1)S(1)}, bf16[512,512]{1,0:T(8,128)(2,1)S(1)}, u32[]{:S(2)}, u32[]{:S(2)}) %collective-permute-start.12) | collective-permute-done | bytes 524320 | tf_op jit(solution)/shard_map/ppermute | solution.py:40
  122.2 4.8 %collective-permute-done.14 = bf16[256,512]{1,0:T(8,128)(2,1)S(1)} collective-permute-done((bf16[256,512]{1,0:T(8,128)(2,1)S(1)}, bf16[256,512]{1,0:T(8,128)(2,1)S(1)}, u32[]{:S(2)}, u32[]{:S(2)}) %collective-permute-start.14) | collective-permute-done | bytes 262176 | tf_op jit(solution)/shard_map/ppermute | solution.py:40
  128.5 2.8 pad_maximum_fusion.5
  133.3 3.0 fusion.20
  137.7 3.0 fusion.21
  148.2 20.4 %collective-permute-done.19 = bf16[1024,512]{1,0:T(8,128)(2,1)S(1)} collective-permute-done((bf16[1024,512]{1,0:T(8,128)(2,1)S(1)}, bf16[1024,512]{1,0:T(8,128)(2,1)S(1)}, u32[]{:S(2)}, u32[]{:S(2)}) %collective-permute-start.19) | collective-permute-done | bytes 1048608 | tf_op jit(solution)/shard_map/ppermute | solution.py:40
  169.8 3.2 fusion.19
  177.4 11.0 %collective-permute-done.23 = bf16[512,512]{1,0:T(8,128)(2,1)S(1)} collective-permute-done((bf16[512,512]{1,0:T(8,128)(2,1)S(1)}, bf16[512,512]{1,0:T(8,128)(2,1)S(1)}, u32[]{:S(2)}, u32[]{:S(2)}) %collective-permute-start.23) | collective-permute-done | bytes 524320 | tf_op jit(solution)/shard_map/ppermute | solution.py:40
  193.4 3.3 collective-permute-start.28
  198.2 4.4 %dynamic-slice_bitcast_fusion.8 = (bf16[512,512]{1,0:T(8,128)(2,1)}, bf16[512,512]{1,0:T(8,128)(2,1)}, bf16[512,512]{1,0:T(8,128)(2,1)}, bf16[512,512]{1,0:T(8,1...) fusion(bf16[1,4096,512]{2,1,0:T(8,128)(2,1)} %param.9, ...), kind=kLoop, calls=%fused_computation.48 | loop fusion | bytes 8388640 | tf_op jit(solution)/shard_map/dynamic_slice | solution.py:51
  202.6 3.2 collective-permute-done.26
  208.4 9.8 %collective-permute-done.28 = bf16[512,512]{1,0:T(8,128)(2,1)} collective-permute-done((bf16[512,512]{1,0:T(8,128)(2,1)}, bf16[512,512]{1,0:T(8,128)(2,1)}, u32[]{:S(2)}, u32[]{:S(2)}) %collective-permute-start.28) | collective-permute-done | bytes 524320 | tf_op jit(solution)/shard_map/ppermute | solution.py:44
  221.3 5.4 %collective-permute-done.29 = bf16[256,512]{1,0:T(8,128)(2,1)} collective-permute-done((bf16[256,512]{1,0:T(8,128)(2,1)}, bf16[256,512]{1,0:T(8,128)(2,1)}, u32[]{:S(2)}, u32[]{:S(2)}) %collective-permute-start.29) | collective-permute-done | bytes 262176 | tf_op jit(solution)/shard_map/ppermute | solution.py:40
  230.0 3.0 fusion.18
  233.1 3.0 fusion.17
  242.3 20.0 %collective-permute-done.36 = bf16[512,512]{1,0:T(8,128)(2,1)S(1)} collective-permute-done((bf16[512,512]{1,0:T(8,128)(2,1)S(1)}, bf16[512,512]{1,0:T(8,128)(2,1)S(1)}, u32[]{:S(2)}, u32[]{:S(2)}) %collective-permute-start.36) | collective-permute-done | bytes 524320 | tf_op jit(solution)/shard_map/ppermute | solution.py:40
  265.3 3.3 fusion.7
  270.8 4.2 %collective-permute-done.39 = bf16[256,512]{1,0:T(8,128)(2,1)S(1)} collective-permute-done((bf16[256,512]{1,0:T(8,128)(2,1)S(1)}, bf16[256,512]{1,0:T(8,128)(2,1)S(1)}, u32[]{:S(2)}, u32[]{:S(2)}) %collective-permute-start.39) | collective-permute-done | bytes 262176 | tf_op jit(solution)/shard_map/ppermute | solution.py:40
  276.9 2.8 collective-permute-start.32
  279.7 5.0 %collective-permute-start.33 = (bf16[512,512]{1,0:T(8,128)(2,1)}, bf16[512,512]{1,0:T(8,128)(2,1)}, u32[]{:S(2)}, u32[]{:S(2)}) collective-permute-start(bf16[512,512]{1,0:T(8,128)(2,1)} %fusion.6), channel_id=1, source_target_pairs={{0,16},{8,24},{16,0},{24,8},{1,17},{9,25},{17,1},{25,9},{2,18},{10... | collective-permute-start | bytes 1572872 | tf_op jit(solution)/shard_map/ppermute | solution.py:44
  286.0 4.5 %fusion.15 = f32[512,512]{1,0:T(8,128)} fusion(bf16[512,2048]{1,0:T(8,128)(2,1)} %collective-permute-done.40, bf16[512,512]{1,0:T(8,128)(2,1)} %get-tuple-element.63, bf16[512,512]{1,0:T(8,128)(2,1)} %get-tuple-element.64, bf16[512,512]{1,0:T(8,128)(2,1)} %get-tuple-element.58, bf16[512,512]{1,0:T(8,128)(2,1)} %get-tuple-element.59), kind=kOutput, calls=%fused_computation.64 | convolution fusion | flops 1082130432 | bytes 5242880 | tf_op jit(solution)/shard_map/dot_general | solution.py:22
  290.5 5.0 %collective-permute-done.32 = bf16[512,512]{1,0:T(8,128)(2,1)} collective-permute-done((bf16[512,512]{1,0:T(8,128)(2,1)}, bf16[512,512]{1,0:T(8,128)(2,1)}, u32[]{:S(2)}, u32[]{:S(2)}) %collective-permute-start.32) | collective-permute-done | bytes 524320 | tf_op jit(solution)/shard_map/ppermute | solution.py:44
  295.5 30.1 %collective-permute-done.33 = bf16[512,512]{1,0:T(8,128)(2,1)} collective-permute-done((bf16[512,512]{1,0:T(8,128)(2,1)}, bf16[512,512]{1,0:T(8,128)(2,1)}, u32[]{:S(2)}, u32[]{:S(2)}) %collective-permute-start.33) | collective-permute-done | bytes 524320 | tf_op jit(solution)/shard_map/ppermute | solution.py:44
  325.6 4.7 %collective-permute-done.37 = bf16[512,512]{1,0:T(8,128)(2,1)} collective-permute-done((bf16[512,512]{1,0:T(8,128)(2,1)}, bf16[512,512]{1,0:T(8,128)(2,1)}, u32[]{:S(2)}, u32[]{:S(2)}) %collective-permute-start.37) | collective-permute-done | bytes 524320 | tf_op jit(solution)/shard_map/ppermute | solution.py:44
  330.3 10.6 %fusion = bf16[1,512,4096]{2,1,0:T(8,128)(2,1)} fusion(bf16[512,4096]{1,0:T(8,128)(2,1)} %param.11, bf16[512,4096]{1,0:T(8,128)(2,1)} %all-gather.4.cloned.1.call-done, bf16[512,512]{1,0:T(8,128)(2,1)} %collective-permute-done.32, bf16[512,512]{1,0:T(8,128)(2,1)} %collective-permute-done.33, bf16[512,512]{1,0:T(8,128)(2,1)} %collective-permute-done.37, ...), kind=kOutput, calls=%fused_computation.1 | convolution fusion | flops 3241410560 | bytes 19398660 | tf_op jit(solution)/shard_map/dot_general | solution.py:13
  (243 shorter events, 80.2 us)
Async XLA Ops:
  6.5 124.8 %all-gather.6.cloned.1.call-start = ((), (), s32[]{:S(2)}) async-start(), calls=%async_computation.1 | async-start | bytes 2621440 | tf_op jit(solution)/shard_map/all_gather | solution.py:104
  6.5 13.9 %collective-permute-start = (bf16[512,512]{1,0:T(8,128)(2,1)}, bf16[512,512]{1,0:T(8,128)(2,1)S(1)}, u32[]{:S(2)}, u32[]{:S(2)}) collective-permute-start(bf16[512,512]{1,0:T(8,128)(2,1)} %bitcast.2), channel_id=1, source_target_pairs={{0,4},{1,5},{2,6},{3,7},{4,0},{5,1},{6,2},{7,3},{8,12},{9,13},{10,... | collective-permute-start | bytes 1572872 | tf_op jit(solution)/shard_map/ppermute | solution.py:40
  8.1 13.6 %collective-permute-start.1 = (bf16[512,512]{1,0:T(8,128)(2,1)}, bf16[512,512]{1,0:T(8,128)(2,1)S(1)}, u32[]{:S(2)}, u32[]{:S(2)}) collective-permute-start(bf16[512,512]{1,0:T(8,128)(2,1)} %bitcast.2), channel_id=1, source_target_pairs={{0,2},{1,3},{2,0},{3,1},{4,6},{5,7},{6,4},{7,5},{8,10},{9,11},{10,... | collective-permute-start | bytes 1572872 | tf_op jit(solution)/shard_map/ppermute | solution.py:40
  9.5 24.5 %collective-permute-start.5 = (bf16[512,512]{1,0:T(8,128)(2,1)}, bf16[512,512]{1,0:T(8,128)(2,1)S(1)}, u32[]{:S(2)}, u32[]{:S(2)}) collective-permute-start(bf16[512,512]{1,0:T(8,128)(2,1)} %bitcast.2), channel_id=1, source_target_pairs={{0,8},{8,16},{16,24},{24,0},{1,9},{9,17},{17,25},{25,1},{2,10},{10... | collective-permute-start | bytes 1572872 | tf_op jit(solution)/shard_map/ppermute | solution.py:44
  11.1 23.0 %collective-permute-start.4 = (bf16[512,512]{1,0:T(8,128)(2,1)}, bf16[512,512]{1,0:T(8,128)(2,1)S(1)}, u32[]{:S(2)}, u32[]{:S(2)}) collective-permute-start(bf16[512,512]{1,0:T(8,128)(2,1)} %bitcast.2), channel_id=1, source_target_pairs={{0,24},{8,0},{16,8},{24,16},{1,25},{9,1},{17,9},{25,17},{2,26},{10... | collective-permute-start | bytes 1572872 | tf_op jit(solution)/shard_map/ppermute | solution.py:44
  34.2 24.2 %collective-permute-start.7 = (bf16[1024,512]{1,0:T(8,128)(2,1)S(1)}, bf16[1024,512]{1,0:T(8,128)(2,1)}, u32[]{:S(2)}, u32[]{:S(2)}) collective-permute-start(bf16[1024,512]{1,0:T(8,128)(2,1)S(1)} %pad_maximum_fusion.13), channel_id=1, source_target_pairs={{0,4},{1,5},{2,6},{3,7},{4,0},{5,1},{6,2},{7,3},{8,12},{9,13},{10,... | collective-permute-start | bytes 3145736 | tf_op jit(solution)/shard_map/ppermute | solution.py:40
  34.8 24.9 %collective-permute-start.8 = (bf16[1024,512]{1,0:T(8,128)(2,1)S(1)}, bf16[1024,512]{1,0:T(8,128)(2,1)}, u32[]{:S(2)}, u32[]{:S(2)}) collective-permute-start(bf16[1024,512]{1,0:T(8,128)(2,1)S(1)} %pad_maximum_fusion.13), channel_id=1, source_target_pairs={{0,2},{1,3},{2,0},{3,1},{4,6},{5,7},{6,4},{7,5},{8,10},{9,11},{10,... | collective-permute-start | bytes 3145736 | tf_op jit(solution)/shard_map/ppermute | solution.py:40
  38.0 38.6 %collective-permute-start.11 = (bf16[512,2048]{1,0:T(8,128)(2,1)}, bf16[512,2048]{1,0:T(8,128)(2,1)}, u32[]{:S(2)}, u32[]{:S(2)}) collective-permute-start(bf16[512,2048]{1,0:T(8,128)(2,1)} %pad_maximum_fusion), channel_id=1, source_target_pairs={{0,1},{1,0},{2,3},{3,2},{4,5},{5,4},{6,7},{7,6},{8,9},{9,8},{10,11... | collective-permute-start | bytes 6291464 | tf_op jit(solution)/shard_map/ppermute | solution.py:40
  38.0 292.2 %all-gather.4.cloned.1.call-start = ((), (), s32[]{:S(2)}) async-start(), calls=%async_computation | async-start | bytes 4718592 | tf_op jit(solution)/shard_map/all_gather | solution.py:147
  65.5 39.1 %collective-permute-start.6 = (bf16[512,512]{1,0:T(8,128)(2,1)}, bf16[512,512]{1,0:T(8,128)(2,1)S(1)}, u32[]{:S(2)}, u32[]{:S(2)}) collective-permute-start(bf16[512,512]{1,0:T(8,128)(2,1)} %bitcast.2), channel_id=1, source_target_pairs={{0,16},{8,24},{16,0},{24,8},{1,17},{9,25},{17,1},{25,9},{2,18},{10... | collective-permute-start | bytes 1572872 | tf_op jit(solution)/shard_map/ppermute | solution.py:44
  67.6 37.0 %collective-permute-start.9 = (bf16[512,512]{1,0:T(8,128)(2,1)}, bf16[512,512]{1,0:T(8,128)(2,1)S(1)}, u32[]{:S(2)}, u32[]{:S(2)}) collective-permute-start(bf16[512,512]{1,0:T(8,128)(2,1)} %get-tuple-element.36), channel_id=1, source_target_pairs={{0,4},{1,5},{2,6},{3,7},{4,0},{5,1},{6,2},{7,3},{8,12},{9,13},{10,... | collective-permute-start | bytes 1572872 | tf_op jit(solution)/shard_map/ppermute | solution.py:40
  76.5 56.6 %collective-permute-start.17 = (bf16[512,2048]{1,0:T(8,128)(2,1)S(1)}, bf16[512,2048]{1,0:T(8,128)(2,1)}, u32[]{:S(2)}, u32[]{:S(2)}) collective-permute-start(bf16[512,2048]{1,0:T(8,128)(2,1)S(1)} %pad_maximum_fusion.4), channel_id=1, source_target_pairs={{0,1},{1,0},{2,3},{3,2},{4,5},{5,4},{6,7},{7,6},{8,9},{9,8},{10,11... | collective-permute-start | bytes 6291464 | tf_op jit(solution)/shard_map/ppermute | solution.py:40
  104.6 13.5 %collective-permute-start.12 = (bf16[512,512]{1,0:T(8,128)(2,1)S(1)}, bf16[512,512]{1,0:T(8,128)(2,1)S(1)}, u32[]{:S(2)}, u32[]{:S(2)}) collective-permute-start(bf16[512,512]{1,0:T(8,128)(2,1)S(1)} %collective-permute-done.6), channel_id=1, source_target_pairs={{0,4},{1,5},{2,6},{3,7},{4,0},{5,1},{6,2},{7,3},{8,12},{9,13},{10,... | collective-permute-start | bytes 1572872 | tf_op jit(solution)/shard_map/ppermute | solution.py:40
  106.1 13.3 %collective-permute-start.13 = (bf16[512,512]{1,0:T(8,128)(2,1)S(1)}, bf16[512,512]{1,0:T(8,128)(2,1)S(1)}, u32[]{:S(2)}, u32[]{:S(2)}) collective-permute-start(bf16[512,512]{1,0:T(8,128)(2,1)S(1)} %collective-permute-done.6), channel_id=1, source_target_pairs={{0,2},{1,3},{2,0},{3,1},{4,6},{5,7},{6,4},{7,5},{8,10},{9,11},{10,... | collective-permute-start | bytes 1572872 | tf_op jit(solution)/shard_map/ppermute | solution.py:40
  110.2 27.4 %collective-permute-start.16 = (bf16[512,2048]{1,0:T(8,128)(2,1)}, bf16[512,2048]{1,0:T(8,128)(2,1)}, u32[]{:S(2)}, u32[]{:S(2)}) collective-permute-start(bf16[512,2048]{1,0:T(8,128)(2,1)} %pad_maximum_fusion.3), channel_id=1, source_target_pairs={{0,1},{1,0},{2,3},{3,2},{4,5},{5,4},{6,7},{7,6},{8,9},{9,8},{10,11... | collective-permute-start | bytes 6291464 | tf_op jit(solution)/shard_map/ppermute | solution.py:40
  131.3 38.5 %collective-permute-start.22 = (bf16[512,2048]{1,0:T(8,128)(2,1)}, bf16[512,2048]{1,0:T(8,128)(2,1)}, u32[]{:S(2)}, u32[]{:S(2)}) collective-permute-start(bf16[512,2048]{1,0:T(8,128)(2,1)} %pad_maximum_fusion.5), channel_id=1, source_target_pairs={{0,1},{1,0},{2,3},{3,2},{4,5},{5,4},{6,7},{7,6},{8,9},{9,8},{10,11... | collective-permute-start | bytes 6291464 | tf_op jit(solution)/shard_map/ppermute | solution.py:40
  142.9 25.6 %collective-permute-start.19 = (bf16[1024,512]{1,0:T(8,128)(2,1)S(1)}, bf16[1024,512]{1,0:T(8,128)(2,1)S(1)}, u32[]{:S(2)}, u32[]{:S(2)}) collective-permute-start(bf16[1024,512]{1,0:T(8,128)(2,1)S(1)} %pad_maximum_fusion.12), channel_id=1, source_target_pairs={{0,4},{1,5},{2,6},{3,7},{4,0},{5,1},{6,2},{7,3},{8,12},{9,13},{10,... | collective-permute-start | bytes 3145736 | tf_op jit(solution)/shard_map/ppermute | solution.py:40
  144.4 25.3 %collective-permute-start.18 = (bf16[1024,512]{1,0:T(8,128)(2,1)S(1)}, bf16[1024,512]{1,0:T(8,128)(2,1)S(1)}, u32[]{:S(2)}, u32[]{:S(2)}) collective-permute-start(bf16[1024,512]{1,0:T(8,128)(2,1)S(1)} %pad_maximum_fusion.12), channel_id=1, source_target_pairs={{0,2},{1,3},{2,0},{3,1},{4,6},{5,7},{6,4},{7,5},{8,10},{9,11},{10,... | collective-permute-start | bytes 3145736 | tf_op jit(solution)/shard_map/ppermute | solution.py:40
  145.8 29.3 %collective-permute-start.21 = (bf16[512,512]{1,0:T(8,128)(2,1)S(1)}, bf16[512,512]{1,0:T(8,128)(2,1)S(1)}, u32[]{:S(2)}, u32[]{:S(2)}) collective-permute-start(bf16[512,512]{1,0:T(8,128)(2,1)S(1)} %fusion.3), channel_id=1, source_target_pairs={{0,24},{8,0},{16,8},{24,16},{1,25},{9,1},{17,9},{25,17},{2,26},{10... | collective-permute-start | bytes 1572872 | tf_op jit(solution)/shard_map/ppermute | solution.py:44
  146.3 28.8 %collective-permute-start.20 = (bf16[512,512]{1,0:T(8,128)(2,1)S(1)}, bf16[512,512]{1,0:T(8,128)(2,1)S(1)}, u32[]{:S(2)}, u32[]{:S(2)}) collective-permute-start(bf16[512,512]{1,0:T(8,128)(2,1)S(1)} %fusion.2), channel_id=1, source_target_pairs={{0,8},{8,16},{16,24},{24,0},{1,9},{9,17},{17,25},{25,1},{2,10},{10... | collective-permute-start | bytes 1572872 | tf_op jit(solution)/shard_map/ppermute | solution.py:44
  175.1 13.3 %collective-permute-start.23 = (bf16[512,512]{1,0:T(8,128)(2,1)S(1)}, bf16[512,512]{1,0:T(8,128)(2,1)S(1)}, u32[]{:S(2)}, u32[]{:S(2)}) collective-permute-start(bf16[512,512]{1,0:T(8,128)(2,1)S(1)} %get-tuple-element.44), channel_id=1, source_target_pairs={{0,2},{1,3},{2,0},{3,1},{4,6},{5,7},{6,4},{7,5},{8,10},{9,11},{10,... | collective-permute-start | bytes 1572872 | tf_op jit(solution)/shard_map/ppermute | solution.py:40
  188.7 41.2 %collective-permute-start.24 = (bf16[512,2048]{1,0:T(8,128)(2,1)S(1)}, bf16[512,2048]{1,0:T(8,128)(2,1)}, u32[]{:S(2)}, u32[]{:S(2)}) collective-permute-start(bf16[512,2048]{1,0:T(8,128)(2,1)S(1)} %pad_maximum_fusion.6), channel_id=1, source_target_pairs={{0,1},{1,0},{2,3},{3,2},{4,5},{5,4},{6,7},{7,6},{8,9},{9,8},{10,11... | collective-permute-start | bytes 6291464 | tf_op jit(solution)/shard_map/ppermute | solution.py:40
  191.2 41.8 %collective-permute-start.31 = (bf16[512,2048]{1,0:T(8,128)(2,1)}, bf16[512,2048]{1,0:T(8,128)(2,1)}, u32[]{:S(2)}, u32[]{:S(2)}) collective-permute-start(bf16[512,2048]{1,0:T(8,128)(2,1)} %pad_maximum_fusion.9), channel_id=1, source_target_pairs={{0,1},{1,0},{2,3},{3,2},{4,5},{5,4},{6,7},{7,6},{8,9},{9,8},{10,11... | collective-permute-start | bytes 6291464 | tf_op jit(solution)/shard_map/ppermute | solution.py:40
  191.3 14.4 %collective-permute-start.26 = (bf16[512,512]{1,0:T(8,128)(2,1)S(1)}, bf16[512,512]{1,0:T(8,128)(2,1)}, u32[]{:S(2)}, u32[]{:S(2)}) collective-permute-start(bf16[512,512]{1,0:T(8,128)(2,1)S(1)} %get-tuple-element.46), channel_id=1, source_target_pairs={{0,4},{1,5},{2,6},{3,7},{4,0},{5,1},{6,2},{7,3},{8,12},{9,13},{10,... | collective-permute-start | bytes 1572872 | tf_op jit(solution)/shard_map/ppermute | solution.py:40
  192.4 14.4 %collective-permute-start.27 = (bf16[512,512]{1,0:T(8,128)(2,1)S(1)}, bf16[512,512]{1,0:T(8,128)(2,1)}, u32[]{:S(2)}, u32[]{:S(2)}) collective-permute-start(bf16[512,512]{1,0:T(8,128)(2,1)S(1)} %get-tuple-element.46), channel_id=1, source_target_pairs={{0,2},{1,3},{2,0},{3,1},{4,6},{5,7},{6,4},{7,5},{8,10},{9,11},{10,... | collective-permute-start | bytes 1572872 | tf_op jit(solution)/shard_map/ppermute | solution.py:40
  193.4 24.8 %collective-permute-start.28 = (bf16[512,512]{1,0:T(8,128)(2,1)}, bf16[512,512]{1,0:T(8,128)(2,1)}, u32[]{:S(2)}, u32[]{:S(2)}) collective-permute-start(bf16[512,512]{1,0:T(8,128)(2,1)} %fusion.4), channel_id=1, source_target_pairs={{0,16},{8,24},{16,0},{24,8},{1,17},{9,25},{17,1},{25,9},{2,18},{10... | collective-permute-start | bytes 1572872 | tf_op jit(solution)/shard_map/ppermute | solution.py:44
  229.9 34.2 %collective-permute-start.34 = (bf16[512,2048]{1,0:T(8,128)(2,1)S(1)}, bf16[512,2048]{1,0:T(8,128)(2,1)S(1)}, u32[]{:S(2)}, u32[]{:S(2)}) collective-permute-start(bf16[512,2048]{1,0:T(8,128)(2,1)S(1)} %pad_maximum_fusion.10), channel_id=1, source_target_pairs={{0,1},{1,0},{2,3},{3,2},{4,5},{5,4},{6,7},{7,6},{8,9},{9,8},{10,11... | collective-permute-start | bytes 6291464 | tf_op jit(solution)/shard_map/ppermute | solution.py:40
  240.3 22.1 %collective-permute-start.36 = (bf16[512,512]{1,0:T(8,128)(2,1)S(1)}, bf16[512,512]{1,0:T(8,128)(2,1)S(1)}, u32[]{:S(2)}, u32[]{:S(2)}) collective-permute-start(bf16[512,512]{1,0:T(8,128)(2,1)S(1)} %bitcast.56), channel_id=1, source_target_pairs={{0,4},{1,5},{2,6},{3,7},{4,0},{5,1},{6,2},{7,3},{8,12},{9,13},{10,... | collective-permute-start | bytes 1572872 | tf_op jit(solution)/shard_map/ppermute | solution.py:40
  241.3 22.7 %collective-permute-start.35 = (bf16[512,512]{1,0:T(8,128)(2,1)S(1)}, bf16[512,512]{1,0:T(8,128)(2,1)S(1)}, u32[]{:S(2)}, u32[]{:S(2)}) collective-permute-start(bf16[512,512]{1,0:T(8,128)(2,1)S(1)} %bitcast.57), channel_id=1, source_target_pairs={{0,2},{1,3},{2,0},{3,1},{4,6},{5,7},{6,4},{7,5},{8,10},{9,11},{10,... | collective-permute-start | bytes 1572872 | tf_op jit(solution)/shard_map/ppermute | solution.py:40
  276.9 18.6 %collective-permute-start.32 = (bf16[512,512]{1,0:T(8,128)(2,1)}, bf16[512,512]{1,0:T(8,128)(2,1)}, u32[]{:S(2)}, u32[]{:S(2)}) collective-permute-start(bf16[512,512]{1,0:T(8,128)(2,1)} %fusion.5), channel_id=1, source_target_pairs={{0,24},{8,0},{16,8},{24,16},{1,25},{9,1},{17,9},{25,17},{2,26},{10... | collective-permute-start | bytes 1572872 | tf_op jit(solution)/shard_map/ppermute | solution.py:44
  279.7 45.9 %collective-permute-start.33 = (bf16[512,512]{1,0:T(8,128)(2,1)}, bf16[512,512]{1,0:T(8,128)(2,1)}, u32[]{:S(2)}, u32[]{:S(2)}) collective-permute-start(bf16[512,512]{1,0:T(8,128)(2,1)} %fusion.6), channel_id=1, source_target_pairs={{0,16},{8,24},{16,0},{24,8},{1,17},{9,25},{17,1},{25,9},{2,18},{10... | collective-permute-start | bytes 1572872 | tf_op jit(solution)/shard_map/ppermute | solution.py:44
  284.8 45.5 %collective-permute-start.37 = (bf16[512,512]{1,0:T(8,128)(2,1)}, bf16[512,512]{1,0:T(8,128)(2,1)}, u32[]{:S(2)}, u32[]{:S(2)}) collective-permute-start(bf16[512,512]{1,0:T(8,128)(2,1)} %fusion.7), channel_id=1, source_target_pairs={{0,8},{8,16},{16,24},{24,0},{1,9},{9,17},{17,25},{25,1},{2,10},{10... | collective-permute-start | bytes 1572872 | tf_op jit(solution)/shard_map/ppermute | solution.py:44
  (80 other events, 741.5 us)
Sparse Core Ops, SparseCore 0:
  38.2 62.8 all-gather.5
  221.4 46.9 all-gather.3

commit v9 on v6

v9 whole, which is shorter than its diff:
```python
import jax
import jax.numpy as jnp
from jax import lax
from jax.sharding import PartitionSpec as P

damping = 0.01
ROOM = 2**25


def product_and_divide(rot_out, all_rot_in, eig_lambda, tokens):
    denom = eig_lambda.astype(jnp.float32) + damping
    contract = (((0,), (0,)), ((), ()))
    product = lax.dot_general(rot_out, all_rot_in, contract, preferred_element_type=jnp.float32) / tokens
    return (product / denom).astype(jnp.bfloat16)[None]


def from_owner(held, owner):
    return lax.psum(jnp.where(lax.axis_index("dp") == owner, held, jnp.zeros_like(held)), "dp")


def dot(a, b):
    return jnp.dot(a, b, preferred_element_type=jnp.float32)


def move_bases(acts, grads, basis_in_held, basis_out_held, owners, eig_lambda):
    column = lax.axis_index("tensor")
    basis_in = from_owner(basis_in_held[0], owners[0, column])
    basis_out = from_owner(basis_out_held[0], owners[1, column])
    rot_in = dot(lax.all_gather(acts[0], "tensor", axis=1, tiled=True), basis_in).astype(jnp.bfloat16)
    rot_out = dot(lax.all_gather(grads[0], "tensor", axis=1, tiled=True), basis_out).astype(jnp.bfloat16)
    return product_and_divide(
        rot_out, lax.all_gather(rot_in, "tensor", axis=1, tiled=True), eig_lambda, acts.shape[1]
    )


X, Y, CORE = 2, 4, 1


def swap(block, bit):
    return lax.ppermute(block, "tensor", [(j, j ^ bit) for j in range(X + Y + CORE + 1)])


def shift(block, by, n):
    return lax.ppermute(block, "dp", [(z, (z + by) % n) for z in range(n)])


def in_order(held, column, offsets):
    width = held.shape[0] // (X + Y + CORE + 1)
    blocks = [lax.dynamic_slice(held, ((column ^ i) * width, 0), (width, held.shape[1])) for i in offsets]
    return jnp.concatenate(blocks, axis=0)


def after(values, others):
    return lax.optimization_barrier((values, others))[0]


def move_inputs(n_dp, acts, grads, basis_in_held, basis_out_held, owners, eig_lambda):
    column = lax.axis_index("tensor")
    me = lax.axis_index("dp")
    own = (acts[0], grads[0])
    tokens = acts.shape[1]
    behind = [(me - owners[side, column]) % n_dp for side in (0, 1)]
    found = [0, X, Y, X + Y]
    held = (basis_in_held[0], basis_out_held[0])
    theirs = [swap(in_order(block, column, [CORE + i for i in found]), CORE) for block in held]
    ours = [in_order(block, column, found) for block in held]

    pieces = {(0, 0): own[0], (1, 0): own[1]}
    rotated, returned = {}, {}

    def fetch(key, gate):
        side, i = key
        pieces[key] = shift(after(own[side], gate), -i, n_dp)
        return pieces[key]

    def send_back(key, gate):
        side, i = key
        returned[key] = shift(after(rotated[key], gate), i, n_dp)
        return returned[key]

    def rotate(group, evens):
        crossing = [swap(dot(even, theirs[side]), CORE) for (side, _), even in zip(group, evens)]
        for (side, i), even, other in zip(group, evens, crossing):
            rotated[side, i] = (dot(even, ours[side]) + other).astype(jnp.bfloat16)
        return [rotated[key] for key in group]

    groups = [[(0, 0), (1, 0)], [(0, 2), (1, 2)], [(0, 1), (0, 3)], [(1, 1), (1, 3)]]
    fetched = [[[(0, 2)], [(1, 2)]], [[(0, 1), (0, 3)], [(1, 1)]], [[(1, 3)], []], [[], []]]
    sent = [[[], []], [[], []], [[], []], [[(0, 2)], [(0, 1), (0, 3)]]]

    due = []
    evens = []
    for at, group in enumerate(groups):
        gate = due
        stack = after(jnp.concatenate([pieces[key] for key in group], axis=0), gate)
        x, y = swap(stack, X), swap(stack, Y)
        due = [x, y] + [fetch(key, gate) for key in fetched[at][0]] + [send_back(key, gate) for key in sent[at][0]]
        if at:
            due += rotate(groups[at - 1], evens)
        gate = due
        to_x, to_y = after((y[tokens:], x[:tokens]), gate)
        xy = [swap(to_y, Y), swap(to_x, X)]
        due = xy + [fetch(key, gate) for key in fetched[at][1]] + [send_back(key, gate) for key in sent[at][1]]
        rows = [slice(0, tokens), slice(tokens, None)]
        evens = [jnp.concatenate([stack[r], x[r], y[r], last], axis=1) for r, last in zip(rows, xy)]

    send_back((1, 2), due)
    rotate(groups[-1], evens)
    for key in groups[-1]:
        send_back(key, [])

    total = []
    for side in (0, 1):
        kept = rotated[side, 0]
        for i in range(1, n_dp):
            kept = jnp.where(behind[side] == i, returned[side, i], kept)
        total.append(kept)
    all_rot_in = lax.all_gather(total[0], "tensor", axis=1, tiled=True)
    return product_and_divide(total[1], all_rot_in, eig_lambda, tokens)


def solution(mesh):
    placed = (
        P("dp", None, "tensor"),
        P("dp", None, "tensor"),
        P("dp", None, "tensor"),
        P("dp", None, "tensor"),
        P(),
        P("tensor", None),
    )
    n_dp, n_tensor = mesh.shape["dp"], mesh.shape["tensor"]

    def step(acts, *rest):
        whole = 2 * n_dp * acts.shape[1] * acts.shape[2] * n_tensor * acts.dtype.itemsize
        if whole <= ROOM and n_dp == 4 and n_tensor == X + Y + CORE + 1:
            return move_inputs(n_dp, acts, *rest)
        return move_bases(acts, *rest)

    return jax.shard_map(step, mesh=mesh, in_specs=placed, out_specs=P("dp", "tensor", None), check_vma=False)
```

time: 389 us -> 293 us (0.75)
  waiting for transfers between devices: 273 us -> 195 us
  matrix products: 42 us -> 32.9 us
  other arithmetic: 11.7 us -> 3.88 us
  starting transfers between devices: 30.6 us -> 38.4 us
  local copies, waits for them, and re-layouts: 13 us -> 7.41 us
    ppermute x32 -> x26, waiting for transfers between devices: 198 us -> 69.1 us  [swap(): lax.ppermute(block, 'tensor', [(j, j ^ bit) for j in range(X + Y + CORE +...]
    ppermute x6 -> x12, waiting for transfers between devices: 74.2 us -> 126 us  [shift(): return lax.ppermute(block, 'dp', [(z, (z + by) % n) for z in range(n)])]
    ppermute x6 -> x12, starting transfers between devices: 5.22 us -> 19.8 us  [shift(): return lax.ppermute(block, 'dp', [(z, (z + by) % n) for z in range(n)])]
    dot_general x16, matrix products: 33.1 us -> 24 us  [dot(): return jnp.dot(a, b, preferred_element_type=jnp.float32)]
    concatenate x8 -> x6, other arithmetic: 9.73 us -> 1.75 us  [the longest x4 1.47 us: move_inputs(): stack = after(jnp.concatenate([pieces[key] for key in group], axis=0), gate)]
    ppermute x32 -> x26, starting transfers between devices: 25.3 us -> 18.6 us  [swap(): lax.ppermute(block, 'tensor', [(j, j ^ bit) for j in range(X + Y + CORE +...]
    dynamic_slice x2, local copies, waits for them, and re-layouts: 7.96 us -> 2.8 us  [in_order(): lax.dynamic_slice(held, ((column ^ i) * width, 0), (width, held.shape[1]))]
  transfers between devices with their start and end apart: 41 -> 39, of which waited for: 25 -> 19; matrix products, arithmetic and copies ran while one was open for 14% -> 10% of each run, Pallas kernels for 0% -> 0%
where the time goes in v9:
time: 293 us
  waiting for transfers between devices  195 us (67%)
  starting transfers between devices  38.4 us (13%)
  matrix products  32.9 us (11%)
  between operations  15.2 us (5%)
  local copies, waits for them, and re-layouts  7.41 us (3%)
  other arithmetic  3.88 us (1%)
    ppermute x12, waiting for transfers between devices, shift(): return lax.ppermute(block, 'dp', [(z, (z + by) % n) for z in range(n)])  126 us
    ppermute x26, waiting for transfers between devices, swap(): lax.ppermute(block, 'tensor', [(j, j ^ bit) for j in range(X + Y + CORE +...  69.1 us
    dot_general x16, matrix products, dot(): return jnp.dot(a, b, preferred_element_type=jnp.float32)  24 us
    ppermute x12, starting transfers between devices, shift(): return lax.ppermute(block, 'dp', [(z, (z + by) % n) for z in range(n)])  19.8 us
    ppermute x26, starting transfers between devices, swap(): lax.ppermute(block, 'tensor', [(j, j ^ bit) for j in range(X + Y + CORE +...  18.6 us
    dot_general x1, matrix products, product_and_divide(): lax.dot_general(rot_out, all_rot_in, contract, preferred_element_type=jnp...  8.89 us
  transfers between devices with their start and end apart: 39, of which 19 were waited for; matrix products, arithmetic and copies ran while one was open for 10% of the time, Pallas kernels for 0%

profile of v9, /device:TPU:16, one launch (start us, length us, event | category | flops | bytes accessed | tf_op | source)
XLA Modules:
  0.0 293.0 jit_solution(11139747730420875705)
XLA Ops:
  7.8 1.6 collective-permute-start.1
  9.4 1.5 collective-permute-start.2
  10.9 2.5 dynamic-slice_bitcast_fusion.7
  14.1 2.3 copy-done
  16.9 20.2 %collective-permute-done = bf16[512,512]{1,0:T(8,128)(2,1)S(1)} collective-permute-done((bf16[512,512]{1,0:T(8,128)(2,1)S(1)}, bf16[512,512]{1,0:T(8,128)(2,1)S(1)}, u32[]{:S(2)}, u32[]{:S(2)}) %collective-permute-start) | collective-permute-done | bytes 524320 | tf_op jit(solution)/shard_map/ppermute | solution.py:44
  37.1 3.4 %collective-permute-start.3 = (bf16[512,512]{1,0:T(8,128)(2,1)S(1)}, bf16[512,512]{1,0:T(8,128)(2,1)S(1)}, u32[]{:S(2)}, u32[]{:S(2)}) collective-permute-start(bf16[512,512]{1,0:T(8,128)(2,1)S(1)} %bitcast.52), channel_id=1, source_target_pairs={{0,16},{8,24},{16,0},{24,8},{1,17},{9,25},{17,1},{25,9},{2,18},{10... | collective-permute-start | bytes 1572872 | tf_op jit(solution)/shard_map/ppermute | solution.py:44
  41.7 21.0 %collective-permute-done.3 = bf16[512,512]{1,0:T(8,128)(2,1)S(1)} collective-permute-done((bf16[512,512]{1,0:T(8,128)(2,1)S(1)}, bf16[512,512]{1,0:T(8,128)(2,1)S(1)}, u32[]{:S(2)}, u32[]{:S(2)}) %collective-permute-start.3) | collective-permute-done | bytes 524320 | tf_op jit(solution)/shard_map/ppermute | solution.py:44
  65.9 2.0 collective-permute-start.9
  69.2 17.6 %collective-permute-done.6 = bf16[1024,512]{1,0:T(8,128)(2,1)S(1)} collective-permute-done((bf16[1024,512]{1,0:T(8,128)(2,1)S(1)}, bf16[1024,512]{1,0:T(8,128)(2,1)S(1)}, u32[]{:S(2)}, u32[]{:S(2)}) %collective-permute-start.6) | collective-permute-done | bytes 1048608 | tf_op jit(solution)/shard_map/ppermute | solution.py:40
  87.2 2.1 fusion.2
  89.4 2.1 fusion.1
  91.5 1.6 collective-permute-done.9
  94.4 1.5 collective-permute-start.15
  97.2 9.3 %collective-permute-done.16 = bf16[512,512]{1,0:T(8,128)(2,1)S(1)} collective-permute-done((bf16[512,512]{1,0:T(8,128)(2,1)S(1)}, bf16[512,512]{1,0:T(8,128)(2,1)S(1)}, u32[]{:S(2)}, u32[]{:S(2)}) %collective-permute-start.16) | collective-permute-done | bytes 524320 | tf_op jit(solution)/shard_map/ppermute | solution.py:40
  114.0 3.5 %collective-permute-start.17 = (bf16[512,512]{1,0:T(8,128)(2,1)S(1)}, bf16[512,512]{1,0:T(8,128)(2,1)S(1)}, u32[]{:S(2)}, u32[]{:S(2)}) collective-permute-start(bf16[512,512]{1,0:T(8,128)(2,1)S(1)} %bitcast.54), channel_id=1, source_target_pairs={{0,8},{8,16},{16,24},{24,0},{1,9},{9,17},{17,25},{25,1},{2,10},{10... | collective-permute-start | bytes 1572872 | tf_op jit(solution)/shard_map/ppermute | solution.py:44
  117.5 14.6 %collective-permute-done.18 = bf16[1024,512]{1,0:T(8,128)(2,1)S(1)} collective-permute-done((bf16[1024,512]{1,0:T(8,128)(2,1)S(1)}, bf16[1024,512]{1,0:T(8,128)(2,1)S(1)}, u32[]{:S(2)}, u32[]{:S(2)}) %collective-permute-start.18) | collective-permute-done | bytes 1048608 | tf_op jit(solution)/shard_map/ppermute | solution.py:40
  132.9 2.1 fusion.4
  138.5 8.9 %collective-permute-done.22 = bf16[512,512]{1,0:T(8,128)(2,1)S(1)} collective-permute-done((bf16[512,512]{1,0:T(8,128)(2,1)S(1)}, bf16[512,512]{1,0:T(8,128)(2,1)S(1)}, u32[]{:S(2)}, u32[]{:S(2)}) %collective-permute-start.22) | collective-permute-done | bytes 524320 | tf_op jit(solution)/shard_map/ppermute | solution.py:40
  151.6 1.7 collective-permute-start.24
  154.8 2.0 fusion.5
  156.8 2.1 fusion.6
  158.9 17.9 %collective-permute-done.26 = bf16[512,512]{1,0:T(8,128)(2,1)S(1)} collective-permute-done((bf16[512,512]{1,0:T(8,128)(2,1)S(1)}, bf16[512,512]{1,0:T(8,128)(2,1)S(1)}, u32[]{:S(2)}, u32[]{:S(2)}) %collective-permute-start.26) | collective-permute-done | bytes 524320 | tf_op jit(solution)/shard_map/ppermute | solution.py:44
  177.6 3.5 %collective-permute-start.33 = (bf16[512,512]{1,0:T(8,128)(2,1)}, bf16[512,512]{1,0:T(8,128)(2,1)}, u32[]{:S(2)}, u32[]{:S(2)}) collective-permute-start(bf16[512,512]{1,0:T(8,128)(2,1)} %fusion.5), channel_id=1, source_target_pairs={{0,8},{8,16},{16,24},{24,0},{1,9},{9,17},{17,25},{25,1},{2,10},{10... | collective-permute-start | bytes 1572872 | tf_op jit(solution)/shard_map/ppermute | solution.py:44
  182.4 21.6 %collective-permute-done.33 = bf16[512,512]{1,0:T(8,128)(2,1)} collective-permute-done((bf16[512,512]{1,0:T(8,128)(2,1)}, bf16[512,512]{1,0:T(8,128)(2,1)}, u32[]{:S(2)}, u32[]{:S(2)}) %collective-permute-start.33) | collective-permute-done | bytes 524320 | tf_op jit(solution)/shard_map/ppermute | solution.py:44
  204.7 2.1 select_select_fusion
  207.1 1.5 collective-permute-start.32
  209.0 15.1 %collective-permute-done.32 = bf16[512,512]{1,0:T(8,128)(2,1)S(1)} collective-permute-done((bf16[512,512]{1,0:T(8,128)(2,1)S(1)}, bf16[512,512]{1,0:T(8,128)(2,1)S(1)}, u32[]{:S(2)}, u32[]{:S(2)}) %collective-permute-start.32) | collective-permute-done | bytes 524320 | tf_op jit(solution)/shard_map/ppermute | solution.py:40
  225.4 1.4 collective-permute-done.29
  230.0 3.4 %collective-permute-start.37 = (bf16[512,512]{1,0:T(8,128)(2,1)S(1)}, bf16[512,512]{1,0:T(8,128)(2,1)S(1)}, u32[]{:S(2)}, u32[]{:S(2)}) collective-permute-start(bf16[512,512]{1,0:T(8,128)(2,1)S(1)} %fusion.8), channel_id=1, source_target_pairs={{0,8},{8,16},{16,24},{24,0},{1,9},{9,17},{17,25},{25,1},{2,10},{10... | collective-permute-start | bytes 1572872 | tf_op jit(solution)/shard_map/ppermute | solution.py:44
  235.4 28.1 %collective-permute-done.35 = bf16[512,512]{1,0:T(8,128)(2,1)S(1)} collective-permute-done((bf16[512,512]{1,0:T(8,128)(2,1)S(1)}, bf16[512,512]{1,0:T(8,128)(2,1)S(1)}, u32[]{:S(2)}, u32[]{:S(2)}) %collective-permute-start.35) | collective-permute-done | bytes 524320 | tf_op jit(solution)/shard_map/ppermute | solution.py:44
  263.5 13.7 %collective-permute-done.37 = bf16[512,512]{1,0:T(8,128)(2,1)S(1)} collective-permute-done((bf16[512,512]{1,0:T(8,128)(2,1)S(1)}, bf16[512,512]{1,0:T(8,128)(2,1)S(1)}, u32[]{:S(2)}, u32[]{:S(2)}) %collective-permute-start.37) | collective-permute-done | bytes 524320 | tf_op jit(solution)/shard_map/ppermute | solution.py:44
  277.2 8.9 %fusion = bf16[1,512,4096]{2,1,0:T(8,128)(2,1)} fusion(bf16[512,4096]{1,0:T(8,128)(2,1)} %param.11, bf16[512,4096]{1,0:T(8,128)(2,1)} %all-gather.2.cloned.1.call-done, bf16[512,512]{1,0:T(8,128)(2,1)S(1)} %collective-permute-done.31, bf16[512,512]{1,0:T(8,128)(2,1)S(1)} %collective-permute-done.35, bf16[512,512]{1,0:T(8,128)(2,1)S(1)} %collective-permute-done.37, ...), kind=kOutput, calls=%fused_computation.1 | convolution fusion | flops 2158755840 | bytes 14680067 | tf_op jit(solution)/shard_map/dot_general | solution.py:13
  (118 shorter events, 37.0 us)
Async XLA Ops:
  6.5 270.7 %all-gather.2.cloned.1.call-start = ((), (), s32[]{:S(2)}) async-start(), calls=%async_computation | async-start | bytes 4718592 | tf_op jit(solution)/shard_map/all_gather | solution.py:118
  7.8 29.3 %collective-permute-start.1 = (bf16[1024,512]{1,0:T(8,128)(2,1)S(1)}, bf16[1024,512]{1,0:T(8,128)(2,1)S(1)}, u32[]{:S(2)}, u32[]{:S(2)}) collective-permute-start(bf16[1024,512]{1,0:T(8,128)(2,1)S(1)} %pad_maximum_fusion.12), channel_id=1, source_target_pairs={{0,2},{1,3},{2,0},{3,1},{4,6},{5,7},{6,4},{7,5},{8,10},{9,11},{10,... | collective-permute-start | bytes 3145736 | tf_op jit(solution)/shard_map/ppermute | solution.py:40
  9.4 27.7 %collective-permute-start.2 = (bf16[1024,512]{1,0:T(8,128)(2,1)S(1)}, bf16[1024,512]{1,0:T(8,128)(2,1)S(1)}, u32[]{:S(2)}, u32[]{:S(2)}) collective-permute-start(bf16[1024,512]{1,0:T(8,128)(2,1)S(1)} %pad_maximum_fusion.12), channel_id=1, source_target_pairs={{0,4},{1,5},{2,6},{3,7},{4,0},{5,1},{6,2},{7,3},{8,12},{9,13},{10,... | collective-permute-start | bytes 3145736 | tf_op jit(solution)/shard_map/ppermute | solution.py:40
  13.6 50.7 %collective-permute-start.12 = (bf16[2048,512]{1,0:T(8,128)(2,1)S(1)}, bf16[2048,512]{1,0:T(8,128)(2,1)S(1)}, u32[]{:S(2)}, u32[]{:S(2)}) collective-permute-start(bf16[2048,512]{1,0:T(8,128)(2,1)S(1)} %pad_maximum_fusion.5), channel_id=1, source_target_pairs={{0,1},{1,0},{2,3},{3,2},{4,5},{5,4},{6,7},{7,6},{8,9},{9,8},{10,11... | collective-permute-start | bytes 6291464 | tf_op jit(solution)/shard_map/ppermute | solution.py:40
  13.7 23.4 %collective-permute-start = (bf16[512,512]{1,0:T(8,128)(2,1)S(1)}, bf16[512,512]{1,0:T(8,128)(2,1)S(1)}, u32[]{:S(2)}, u32[]{:S(2)}) collective-permute-start(bf16[512,512]{1,0:T(8,128)(2,1)S(1)} %bitcast.48), channel_id=1, source_target_pairs={{0,16},{8,24},{16,0},{24,8},{1,17},{9,25},{17,1},{25,9},{2,18},{10... | collective-permute-start | bytes 1572872 | tf_op jit(solution)/shard_map/ppermute | solution.py:44
  16.8 49.1 %collective-permute-start.10 = (bf16[2048,512]{1,0:T(8,128)(2,1)S(1)}, bf16[2048,512]{1,0:T(8,128)(2,1)S(1)}, u32[]{:S(2)}, u32[]{:S(2)}) collective-permute-start(bf16[2048,512]{1,0:T(8,128)(2,1)S(1)} %pad_maximum_fusion.2), channel_id=1, source_target_pairs={{0,1},{1,0},{2,3},{3,2},{4,5},{5,4},{6,7},{7,6},{8,9},{9,8},{10,11... | collective-permute-start | bytes 6291464 | tf_op jit(solution)/shard_map/ppermute | solution.py:40
  37.1 25.7 %collective-permute-start.3 = (bf16[512,512]{1,0:T(8,128)(2,1)S(1)}, bf16[512,512]{1,0:T(8,128)(2,1)S(1)}, u32[]{:S(2)}, u32[]{:S(2)}) collective-permute-start(bf16[512,512]{1,0:T(8,128)(2,1)S(1)} %bitcast.52), channel_id=1, source_target_pairs={{0,16},{8,24},{16,0},{24,8},{1,17},{9,25},{17,1},{25,9},{2,18},{10... | collective-permute-start | bytes 1572872 | tf_op jit(solution)/shard_map/ppermute | solution.py:44
  40.7 22.2 %collective-permute-start.5 = (bf16[512,512]{1,0:T(8,128)(2,1)S(1)}, bf16[512,512]{1,0:T(8,128)(2,1)S(1)}, u32[]{:S(2)}, u32[]{:S(2)}) collective-permute-start(bf16[512,512]{1,0:T(8,128)(2,1)S(1)} %get-tuple-element.26), channel_id=1, source_target_pairs={{0,2},{1,3},{2,0},{3,1},{4,6},{5,7},{6,4},{7,5},{8,10},{9,11},{10,... | collective-permute-start | bytes 1572872 | tf_op jit(solution)/shard_map/ppermute | solution.py:40
  41.3 21.6 %collective-permute-start.4 = (bf16[512,512]{1,0:T(8,128)(2,1)S(1)}, bf16[512,512]{1,0:T(8,128)(2,1)S(1)}, u32[]{:S(2)}, u32[]{:S(2)}) collective-permute-start(bf16[512,512]{1,0:T(8,128)(2,1)S(1)} %get-tuple-element.25), channel_id=1, source_target_pairs={{0,4},{1,5},{2,6},{3,7},{4,0},{5,1},{6,2},{7,3},{8,12},{9,13},{10,... | collective-permute-start | bytes 1572872 | tf_op jit(solution)/shard_map/ppermute | solution.py:40
  62.9 23.9 %collective-permute-start.6 = (bf16[1024,512]{1,0:T(8,128)(2,1)S(1)}, bf16[1024,512]{1,0:T(8,128)(2,1)S(1)}, u32[]{:S(2)}, u32[]{:S(2)}) collective-permute-start(bf16[1024,512]{1,0:T(8,128)(2,1)S(1)} %pad_maximum_fusion.13), channel_id=1, source_target_pairs={{0,2},{1,3},{2,0},{3,1},{4,6},{5,7},{6,4},{7,5},{8,10},{9,11},{10,... | collective-permute-start | bytes 3145736 | tf_op jit(solution)/shard_map/ppermute | solution.py:40
  63.5 23.6 %collective-permute-start.7 = (bf16[1024,512]{1,0:T(8,128)(2,1)S(1)}, bf16[1024,512]{1,0:T(8,128)(2,1)S(1)}, u32[]{:S(2)}, u32[]{:S(2)}) collective-permute-start(bf16[1024,512]{1,0:T(8,128)(2,1)S(1)} %pad_maximum_fusion.13), channel_id=1, source_target_pairs={{0,4},{1,5},{2,6},{3,7},{4,0},{5,1},{6,2},{7,3},{8,12},{9,13},{10,... | collective-permute-start | bytes 3145736 | tf_op jit(solution)/shard_map/ppermute | solution.py:40
  65.5 21.7 %collective-permute-start.13 = (f32[512,512]{1,0:T(8,128)S(1)}, f32[512,512]{1,0:T(8,128)S(1)}, u32[]{:S(2)}, u32[]{:S(2)}) collective-permute-start(f32[512,512]{1,0:T(8,128)S(1)} %fusion.21), channel_id=1, source_target_pairs={{0,1},{1,0},{2,3},{3,2},{4,5},{5,4},{6,7},{7,6},{8,9},{9,8},{10,11... | collective-permute-start | bytes 3145736 | tf_op jit(solution)/shard_map/ppermute | solution.py:40
  65.6 25.9 %collective-permute-start.8 = (bf16[512,512]{1,0:T(8,128)(2,1)S(1)}, bf16[512,512]{1,0:T(8,128)(2,1)S(1)}, u32[]{:S(2)}, u32[]{:S(2)}) collective-permute-start(bf16[512,512]{1,0:T(8,128)(2,1)S(1)} %bitcast.49), channel_id=1, source_target_pairs={{0,24},{8,0},{16,8},{24,16},{1,25},{9,1},{17,9},{25,17},{2,26},{10... | collective-permute-start | bytes 1572872 | tf_op jit(solution)/shard_map/ppermute | solution.py:44
  65.9 27.1 %collective-permute-start.9 = (bf16[512,512]{1,0:T(8,128)(2,1)S(1)}, bf16[512,512]{1,0:T(8,128)(2,1)S(1)}, u32[]{:S(2)}, u32[]{:S(2)}) collective-permute-start(bf16[512,512]{1,0:T(8,128)(2,1)S(1)} %bitcast.50), channel_id=1, source_target_pairs={{0,8},{8,16},{16,24},{24,0},{1,9},{9,17},{17,25},{25,1},{2,10},{10... | collective-permute-start | bytes 1572872 | tf_op jit(solution)/shard_map/ppermute | solution.py:44
  93.1 13.5 %collective-permute-start.16 = (bf16[512,512]{1,0:T(8,128)(2,1)S(1)}, bf16[512,512]{1,0:T(8,128)(2,1)S(1)}, u32[]{:S(2)}, u32[]{:S(2)}) collective-permute-start(bf16[512,512]{1,0:T(8,128)(2,1)S(1)} %get-tuple-element.31), channel_id=1, source_target_pairs={{0,2},{1,3},{2,0},{3,1},{4,6},{5,7},{6,4},{7,5},{8,10},{9,11},{10,... | collective-permute-start | bytes 1572872 | tf_op jit(solution)/shard_map/ppermute | solution.py:40
  94.4 13.2 %collective-permute-start.15 = (bf16[512,512]{1,0:T(8,128)(2,1)S(1)}, bf16[512,512]{1,0:T(8,128)(2,1)S(1)}, u32[]{:S(2)}, u32[]{:S(2)}) collective-permute-start(bf16[512,512]{1,0:T(8,128)(2,1)S(1)} %get-tuple-element.30), channel_id=1, source_target_pairs={{0,4},{1,5},{2,6},{3,7},{4,0},{5,1},{6,2},{7,3},{8,12},{9,13},{10,... | collective-permute-start | bytes 1572872 | tf_op jit(solution)/shard_map/ppermute | solution.py:40
  95.9 12.9 %collective-permute-start.14 = (bf16[512,512]{1,0:T(8,128)(2,1)S(1)}, bf16[512,512]{1,0:T(8,128)(2,1)S(1)}, u32[]{:S(2)}, u32[]{:S(2)}) collective-permute-start(bf16[512,512]{1,0:T(8,128)(2,1)S(1)} %bitcast.53), channel_id=1, source_target_pairs={{0,24},{8,0},{16,8},{24,16},{1,25},{9,1},{17,9},{25,17},{2,26},{10... | collective-permute-start | bytes 1572872 | tf_op jit(solution)/shard_map/ppermute | solution.py:44
  108.9 23.2 %collective-permute-start.18 = (bf16[1024,512]{1,0:T(8,128)(2,1)S(1)}, bf16[1024,512]{1,0:T(8,128)(2,1)S(1)}, u32[]{:S(2)}, u32[]{:S(2)}) collective-permute-start(bf16[1024,512]{1,0:T(8,128)(2,1)S(1)} %pad_maximum_fusion.15), channel_id=1, source_target_pairs={{0,4},{1,5},{2,6},{3,7},{4,0},{5,1},{6,2},{7,3},{8,12},{9,13},{10,... | collective-permute-start | bytes 3145736 | tf_op jit(solution)/shard_map/ppermute | solution.py:40
  109.5 23.3 %collective-permute-start.19 = (bf16[1024,512]{1,0:T(8,128)(2,1)S(1)}, bf16[1024,512]{1,0:T(8,128)(2,1)S(1)}, u32[]{:S(2)}, u32[]{:S(2)}) collective-permute-start(bf16[1024,512]{1,0:T(8,128)(2,1)S(1)} %pad_maximum_fusion.15), channel_id=1, source_target_pairs={{0,2},{1,3},{2,0},{3,1},{4,6},{5,7},{6,4},{7,5},{8,10},{9,11},{10,... | collective-permute-start | bytes 3145736 | tf_op jit(solution)/shard_map/ppermute | solution.py:40
  112.1 20.7 %collective-permute-start.21 = (f32[512,512]{1,0:T(8,128)S(1)}, f32[512,512]{1,0:T(8,128)S(1)}, u32[]{:S(2)}, u32[]{:S(2)}) collective-permute-start(f32[512,512]{1,0:T(8,128)S(1)} %fusion.19), channel_id=1, source_target_pairs={{0,1},{1,0},{2,3},{3,2},{4,5},{5,4},{6,7},{7,6},{8,9},{9,8},{10,11... | collective-permute-start | bytes 3145736 | tf_op jit(solution)/shard_map/ppermute | solution.py:40
  113.4 21.6 %collective-permute-start.20 = (f32[512,512]{1,0:T(8,128)S(1)}, f32[512,512]{1,0:T(8,128)S(1)}, u32[]{:S(2)}, u32[]{:S(2)}) collective-permute-start(f32[512,512]{1,0:T(8,128)S(1)} %fusion.20), channel_id=1, source_target_pairs={{0,1},{1,0},{2,3},{3,2},{4,5},{5,4},{6,7},{7,6},{8,9},{9,8},{10,11... | collective-permute-start | bytes 3145736 | tf_op jit(solution)/shard_map/ppermute | solution.py:40
  114.0 22.3 %collective-permute-start.17 = (bf16[512,512]{1,0:T(8,128)(2,1)S(1)}, bf16[512,512]{1,0:T(8,128)(2,1)S(1)}, u32[]{:S(2)}, u32[]{:S(2)}) collective-permute-start(bf16[512,512]{1,0:T(8,128)(2,1)S(1)} %bitcast.54), channel_id=1, source_target_pairs={{0,8},{8,16},{16,24},{24,0},{1,9},{9,17},{17,25},{25,1},{2,10},{10... | collective-permute-start | bytes 1572872 | tf_op jit(solution)/shard_map/ppermute | solution.py:44
  150.6 26.2 %collective-permute-start.25 = (bf16[1024,512]{1,0:T(8,128)(2,1)S(1)}, bf16[1024,512]{1,0:T(8,128)(2,1)S(1)}, u32[]{:S(2)}, u32[]{:S(2)}) collective-permute-start(bf16[1024,512]{1,0:T(8,128)(2,1)S(1)} %pad_maximum_fusion.14), channel_id=1, source_target_pairs={{0,4},{1,5},{2,6},{3,7},{4,0},{5,1},{6,2},{7,3},{8,12},{9,13},{10,... | collective-permute-start | bytes 3145736 | tf_op jit(solution)/shard_map/ppermute | solution.py:40
  151.6 25.2 %collective-permute-start.24 = (bf16[1024,512]{1,0:T(8,128)(2,1)S(1)}, bf16[1024,512]{1,0:T(8,128)(2,1)S(1)}, u32[]{:S(2)}, u32[]{:S(2)}) collective-permute-start(bf16[1024,512]{1,0:T(8,128)(2,1)S(1)} %pad_maximum_fusion.14), channel_id=1, source_target_pairs={{0,2},{1,3},{2,0},{3,1},{4,6},{5,7},{6,4},{7,5},{8,10},{9,11},{10,... | collective-permute-start | bytes 3145736 | tf_op jit(solution)/shard_map/ppermute | solution.py:40
  153.3 23.5 %collective-permute-start.26 = (bf16[512,512]{1,0:T(8,128)(2,1)S(1)}, bf16[512,512]{1,0:T(8,128)(2,1)S(1)}, u32[]{:S(2)}, u32[]{:S(2)}) collective-permute-start(bf16[512,512]{1,0:T(8,128)(2,1)S(1)} %fusion.3), channel_id=1, source_target_pairs={{0,16},{8,24},{16,0},{24,8},{1,17},{9,25},{17,1},{25,9},{2,18},{10... | collective-permute-start | bytes 1572872 | tf_op jit(solution)/shard_map/ppermute | solution.py:44
  177.6 26.4 %collective-permute-start.33 = (bf16[512,512]{1,0:T(8,128)(2,1)}, bf16[512,512]{1,0:T(8,128)(2,1)}, u32[]{:S(2)}, u32[]{:S(2)}) collective-permute-start(bf16[512,512]{1,0:T(8,128)(2,1)} %fusion.5), channel_id=1, source_target_pairs={{0,8},{8,16},{16,24},{24,0},{1,9},{9,17},{17,25},{25,1},{2,10},{10... | collective-permute-start | bytes 1572872 | tf_op jit(solution)/shard_map/ppermute | solution.py:44
  181.0 23.7 %collective-permute-start.34 = (bf16[512,512]{1,0:T(8,128)(2,1)}, bf16[512,512]{1,0:T(8,128)(2,1)}, u32[]{:S(2)}, u32[]{:S(2)}) collective-permute-start(bf16[512,512]{1,0:T(8,128)(2,1)} %fusion.6), channel_id=1, source_target_pairs={{0,24},{8,0},{16,8},{24,16},{1,25},{9,1},{17,9},{25,17},{2,26},{10... | collective-permute-start | bytes 1572872 | tf_op jit(solution)/shard_map/ppermute | solution.py:44
  207.1 17.0 %collective-permute-start.32 = (bf16[512,512]{1,0:T(8,128)(2,1)S(1)}, bf16[512,512]{1,0:T(8,128)(2,1)S(1)}, u32[]{:S(2)}, u32[]{:S(2)}) collective-permute-start(bf16[512,512]{1,0:T(8,128)(2,1)S(1)} %get-tuple-element.39), channel_id=1, source_target_pairs={{0,4},{1,5},{2,6},{3,7},{4,0},{5,1},{6,2},{7,3},{8,12},{9,13},{10,... | collective-permute-start | bytes 1572872 | tf_op jit(solution)/shard_map/ppermute | solution.py:40
  208.7 18.2 %collective-permute-start.29 = (bf16[512,512]{1,0:T(8,128)(2,1)S(1)}, bf16[512,512]{1,0:T(8,128)(2,1)S(1)}, u32[]{:S(2)}, u32[]{:S(2)}) collective-permute-start(bf16[512,512]{1,0:T(8,128)(2,1)S(1)} %get-tuple-element.38), channel_id=1, source_target_pairs={{0,2},{1,3},{2,0},{3,1},{4,6},{5,7},{6,4},{7,5},{8,10},{9,11},{10,... | collective-permute-start | bytes 1572872 | tf_op jit(solution)/shard_map/ppermute | solution.py:40
  228.2 35.3 %collective-permute-start.35 = (bf16[512,512]{1,0:T(8,128)(2,1)S(1)}, bf16[512,512]{1,0:T(8,128)(2,1)S(1)}, u32[]{:S(2)}, u32[]{:S(2)}) collective-permute-start(bf16[512,512]{1,0:T(8,128)(2,1)S(1)} %copy-done.15), channel_id=1, source_target_pairs={{0,16},{8,24},{16,0},{24,8},{1,17},{9,25},{17,1},{25,9},{2,18},{10... | collective-permute-start | bytes 1572872 | tf_op jit(solution)/shard_map/ppermute | solution.py:44
  230.0 47.2 %collective-permute-start.37 = (bf16[512,512]{1,0:T(8,128)(2,1)S(1)}, bf16[512,512]{1,0:T(8,128)(2,1)S(1)}, u32[]{:S(2)}, u32[]{:S(2)}) collective-permute-start(bf16[512,512]{1,0:T(8,128)(2,1)S(1)} %fusion.8), channel_id=1, source_target_pairs={{0,8},{8,16},{16,24},{24,0},{1,9},{9,17},{17,25},{25,1},{2,10},{10... | collective-permute-start | bytes 1572872 | tf_op jit(solution)/shard_map/ppermute | solution.py:44
  234.7 42.5 %collective-permute-start.31 = (bf16[512,512]{1,0:T(8,128)(2,1)S(1)}, bf16[512,512]{1,0:T(8,128)(2,1)S(1)}, u32[]{:S(2)}, u32[]{:S(2)}) collective-permute-start(bf16[512,512]{1,0:T(8,128)(2,1)S(1)} %fusion.7), channel_id=1, source_target_pairs={{0,24},{8,0},{16,8},{24,16},{1,25},{9,1},{17,9},{25,17},{2,26},{10... | collective-permute-start | bytes 1572872 | tf_op jit(solution)/shard_map/ppermute | solution.py:44
  (23 other events, 648.3 us)
Sparse Core Ops, SparseCore 0:
  207.0 40.5 all-gather.1

commit v10 on v9

--- a/solution.py
+++ b/solution.py
@@ -66,57 +66,70 @@
     ours = [in_order(block, column, found) for block in held]
 
     pieces = {(0, 0): own[0], (1, 0): own[1]}
-    rotated, returned = {}, {}
+    rotated = {}
 
-    def fetch(key, gate):
-        side, i = key
-        pieces[key] = shift(after(own[side], gate), -i, n_dp)
-        return pieces[key]
-
-    def send_back(key, gate):
-        side, i = key
-        returned[key] = shift(after(rotated[key], gate), i, n_dp)
-        return returned[key]
+    def fetch(side, i, gate):
+        block, by = {1: (own[side], -1), 2: (pieces.get((side, 1)), -1), 3: (own[side], 1)}[i]
+        pieces[side, i] = shift(after(block, gate), by, n_dp)
+        return pieces[side, i]
 
     def rotate(group, evens):
         crossing = [swap(dot(even, theirs[side]), CORE) for (side, _), even in zip(group, evens)]
         for (side, i), even, other in zip(group, evens, crossing):
             rotated[side, i] = (dot(even, ours[side]) + other).astype(jnp.bfloat16)
-        return [rotated[key] for key in group]
 
-    groups = [[(0, 0), (1, 0)], [(0, 2), (1, 2)], [(0, 1), (0, 3)], [(1, 1), (1, 3)]]
-    fetched = [[[(0, 2)], [(1, 2)]], [[(0, 1), (0, 3)], [(1, 1)]], [[(1, 3)], []], [[], []]]
-    sent = [[[], []], [[], []], [[], []], [[(0, 2)], [(0, 1), (0, 3)]]]
+    def pass_on(side):
+        return shift(rotated[side, 2], 1, n_dp)
 
+    def send_ahead(side, passed, gate):
+        best = jnp.where(behind[side] == 0, rotated[side, 1], passed)
+        return shift(after(best, gate), 1, n_dp)
+
+    def send_behind(side):
+        return shift(rotated[side, 3], -1, n_dp)
+
+    def keep(side, from_behind, from_ahead):
+        foreign = jnp.where(behind[side] == n_dp - 1, from_ahead, from_behind)
+        return jnp.where(behind[side] == 0, rotated[side, 0], foreign)
+
+    groups = [[(0, 0), (1, 0)], [(0, 1), (0, 2)], [(0, 3), (1, 2)], [(1, 1), (1, 3)]]
     due = []
     evens = []
     for at, group in enumerate(groups):
         gate = due
         stack = after(jnp.concatenate([pieces[key] for key in group], axis=0), gate)
         x, y = swap(stack, X), swap(stack, Y)
-        due = [x, y] + [fetch(key, gate) for key in fetched[at][0]] + [send_back(key, gate) for key in sent[at][0]]
+        due = [x, y]
         if at:
-            due += rotate(groups[at - 1], evens)
+            rotate(groups[at - 1], evens)
+        if at < 2:
+            due += [fetch(at, 1, gate), fetch(at, 3, gate)]
+        if at == 2:
+            passed_in = pass_on(0)
+            due += [passed_in, rotated[0, 1]]
+        if at == 3:
+            in_from_ahead = send_behind(0)
+            passed_out = pass_on(1)
+            due += [in_from_ahead, rotated[1, 2]]
         gate = due
         to_x, to_y = after((y[tokens:], x[:tokens]), gate)
         xy = [swap(to_y, Y), swap(to_x, X)]
-        due = xy + [fetch(key, gate) for key in fetched[at][1]] + [send_back(key, gate) for key in sent[at][1]]
+        due = xy + []
+        if at < 2:
+            due.append(fetch(at, 2, gate))
+        if at == 2:
+            in_from_behind = send_ahead(0, passed_in, gate)
+            due.append(in_from_behind)
+        if at == 3:
+            due.append(passed_out)
         rows = [slice(0, tokens), slice(tokens, None)]
         evens = [jnp.concatenate([stack[r], x[r], y[r], last], axis=1) for r, last in zip(rows, xy)]
 
-    send_back((1, 2), due)
+    rot_in = keep(0, in_from_behind, in_from_ahead)
+    all_rot_in = lax.all_gather(rot_in, "tensor", axis=1, tiled=True)
     rotate(groups[-1], evens)
-    for key in groups[-1]:
-        send_back(key, [])
-
-    total = []
-    for side in (0, 1):
-        kept = rotated[side, 0]
-        for i in range(1, n_dp):
-            kept = jnp.where(behind[side] == i, returned[side, i], kept)
-        total.append(kept)
-    all_rot_in = lax.all_gather(total[0], "tensor", axis=1, tiled=True)
-    return product_and_divide(total[1], all_rot_in, eig_lambda, tokens)
+    rot_out = keep(1, send_ahead(1, passed_out, []), send_behind(1))
+    return product_and_divide(rot_out, all_rot_in, eig_lambda, tokens)
 
 
 def solution(mesh):

time: 293 us -> 334 us (1.14); the launches traced: 293 us -> 329 us
  matrix products: 32.9 us -> 57.2 us
  local copies, waits for them, and re-layouts: 7.41 us -> 15 us
    ppermute x12, waiting for transfers between devices: 126 us -> 75.6 us  [shift(): return lax.ppermute(block, 'dp', [(z, (z + by) % n) for z in range(n)])]
    ppermute x26, waiting for transfers between devices: 69.1 us -> 120 us  [swap(): lax.ppermute(block, 'tensor', [(j, j ^ bit) for j in range(X + Y + CORE +...]
    dot_general x16 -> x15, matrix products: 24 us -> 46.4 us  [dot(): return jnp.dot(a, b, preferred_element_type=jnp.float32)]
    concatenate x4, other arithmetic: 1.47 us -> 4.92 us  [move_inputs(): stack = after(jnp.concatenate([pieces[key] for key in group], axis=0), gate)]
  transfers between devices with their start and end apart: 39 -> 39, of which waited for: 19 -> 20; matrix products, arithmetic and copies ran while one was open for 10% -> 18% of each run, Pallas kernels for 0% -> 0%
where the time goes in v10:
time: 334 us; the launch traced here: 329 us
  waiting for transfers between devices  195 us (58%)
  matrix products  57.2 us (17%)
  starting transfers between devices  41 us (12%)
  between operations  15.3 us (5%)
  local copies, waits for them, and re-layouts  15 us (4%)
  other arithmetic  5.19 us (2%)
    ppermute x26, waiting for transfers between devices, swap(): lax.ppermute(block, 'tensor', [(j, j ^ bit) for j in range(X + Y + CORE +...  120 us
    ppermute x12, waiting for transfers between devices, shift(): return lax.ppermute(block, 'dp', [(z, (z + by) % n) for z in range(n)])  75.6 us
    dot_general x15, matrix products, dot(): return jnp.dot(a, b, preferred_element_type=jnp.float32)  46.4 us
    ppermute x26, starting transfers between devices, swap(): lax.ppermute(block, 'tensor', [(j, j ^ bit) for j in range(X + Y + CORE +...  20.5 us
    ppermute x12, starting transfers between devices, shift(): return lax.ppermute(block, 'dp', [(z, (z + by) % n) for z in range(n)])  20.4 us
    dot_general x1, matrix products, product_and_divide(): lax.dot_general(rot_out, all_rot_in, contract, preferred_element_type=jnp...  10.9 us
  transfers between devices with their start and end apart: 39, of which 20 were waited for; matrix products, arithmetic and copies ran while one was open for 18% of the time, Pallas kernels for 0%

profile of v10, /device:TPU:16, one launch (start us, length us, event | category | flops | bytes accessed | tf_op | source)
XLA Modules:
  0.0 328.9 jit_solution(469349686523900513)
XLA Ops:
  12.9 13.2 %collective-permute-done.2 = bf16[512,512]{1,0:T(8,128)(2,1)} collective-permute-done((bf16[512,512]{1,0:T(8,128)(2,1)}, bf16[512,512]{1,0:T(8,128)(2,1)}, u32[]{:S(2)}, u32[]{:S(2)}) %collective-permute-start.2) | collective-permute-done | bytes 524320 | tf_op jit(solution)/shard_map/ppermute | solution.py:44
  26.1 9.5 %collective-permute-done.3 = bf16[512,512]{1,0:T(8,128)(2,1)S(1)} collective-permute-done((bf16[512,512]{1,0:T(8,128)(2,1)}, bf16[512,512]{1,0:T(8,128)(2,1)S(1)}, u32[]{:S(2)}, u32[]{:S(2)}) %collective-permute-start.3) | collective-permute-done | bytes 524320 | tf_op jit(solution)/shard_map/ppermute | solution.py:44
  40.1 3.8 %dynamic-slice_bitcast_fusion.7 = (bf16[512,512]{1,0:T(8,128)(2,1)}, bf16[512,512]{1,0:T(8,128)(2,1)S(1)}, bf16[512,512]{1,0:T(8,128)(2,1)S(1)}, bf16[512,512]{1...) fusion(bf16[1,4096,512]{2,1,0:T(8,128)(2,1)} %param.8, ...), kind=kLoop, calls=%fused_computation.45 | loop fusion | bytes 8388640 | tf_op jit(solution)/shard_map/dynamic_slice | solution.py:49
  43.8 4.2 %collective-permute-done.8 = bf16[512,512]{1,0:T(8,128)(2,1)} collective-permute-done((bf16[512,512]{1,0:T(8,128)(2,1)}, bf16[512,512]{1,0:T(8,128)(2,1)}, u32[]{:S(2)}, u32[]{:S(2)}) %collective-permute-start.8) | collective-permute-done | bytes 524320 | tf_op jit(solution)/shard_map/ppermute | solution.py:44
  55.7 17.8 %collective-permute-done.12 = bf16[1024,512]{1,0:T(8,128)(2,1)S(1)} collective-permute-done((bf16[1024,512]{1,0:T(8,128)(2,1)S(1)}, bf16[1024,512]{1,0:T(8,128)(2,1)S(1)}, u32[]{:S(2)}, u32[]{:S(2)}) %collective-permute-start.12) | collective-permute-done | bytes 1048608 | tf_op jit(solution)/shard_map/ppermute | solution.py:40
  74.3 4.3 %collective-permute-done.11 = bf16[1024,512]{1,0:T(8,128)(2,1)S(1)} collective-permute-done((bf16[1024,512]{1,0:T(8,128)(2,1)S(1)}, bf16[1024,512]{1,0:T(8,128)(2,1)S(1)}, u32[]{:S(2)}, u32[]{:S(2)}) %collective-permute-start.11) | collective-permute-done | bytes 1048608 | tf_op jit(solution)/shard_map/ppermute | solution.py:40
  82.6 10.4 %collective-permute-done.15 = bf16[512,512]{1,0:T(8,128)(2,1)S(1)} collective-permute-done((bf16[512,512]{1,0:T(8,128)(2,1)S(1)}, bf16[512,512]{1,0:T(8,128)(2,1)S(1)}, u32[]{:S(2)}, u32[]{:S(2)}) %collective-permute-start.15) | collective-permute-done | bytes 524320 | tf_op jit(solution)/shard_map/ppermute | solution.py:40
  98.4 11.7 %collective-permute-done.14 = bf16[512,512]{1,0:T(8,128)(2,1)} collective-permute-done((bf16[512,512]{1,0:T(8,128)(2,1)}, bf16[512,512]{1,0:T(8,128)(2,1)}, u32[]{:S(2)}, u32[]{:S(2)}) %collective-permute-start.14) | collective-permute-done | bytes 524320 | tf_op jit(solution)/shard_map/ppermute | solution.py:40
  111.1 3.6 %fusion.20 = f32[512,512]{1,0:T(8,128)S(1)} fusion(bf16[2048,512]{1,0:T(8,128)(2,1)} %copy-done.40, bf16[512,512]{1,0:T(8,128)(2,1)} %collective-permute-done.14, bf16[512,512]{1,0:T(8,128)(2,1)} %get-tuple-element.69, bf16[512,512]{1,0:T(8,128)(2,1)} %get-tuple-element.26, bf16[512,512]{1,0:T(8,128)(2,1)} %get-tuple-element.67), kind=kOutput, calls=%fused_computation.62 | convolution fusion | flops 1082130432 | bytes 5242880 | tf_op jit(solution)/shard_map/dot_general | solution.py:22
  119.0 15.7 %collective-permute-done.16 = bf16[1024,512]{1,0:T(8,128)(2,1)S(1)} collective-permute-done((bf16[1024,512]{1,0:T(8,128)(2,1)S(1)}, bf16[1024,512]{1,0:T(8,128)(2,1)S(1)}, u32[]{:S(2)}, u32[]{:S(2)}) %collective-permute-start.16) | collective-permute-done | bytes 1048608 | tf_op jit(solution)/shard_map/ppermute | solution.py:40
  136.5 3.4 %broadcast_select_fusion = bf16[512,512]{1,0:T(8,128)(2,1)} fusion(bf16[512,512]{1,0:T(8,128)(2,1)S(1)} %collective-permute-done.20, pred[]{:T(512)S(6)} %eq.19, f32[512,512]{1,0:T(8,128)S(1)} %collective-permute-done.21, bf16[512,512]{1,0:T(8,128)(2,1)S(1)} %copy-done.27, bf16[512,512]{1,0:T(8,128)(2,1)S(1)} %copy-done.28, ...), kind=kOutput, calls=%fused_computation.54 | convolution fusion | flops 1091305472 | bytes 6291457 | tf_op jit(solution)/shard_map/dot_general | solution.py:22
  141.6 10.9 %collective-permute-done.22 = bf16[512,512]{1,0:T(8,128)(2,1)S(1)} collective-permute-done((bf16[512,512]{1,0:T(8,128)(2,1)S(1)}, bf16[512,512]{1,0:T(8,128)(2,1)S(1)}, u32[]{:S(2)}, u32[]{:S(2)}) %collective-permute-start.22) | collective-permute-done | bytes 524320 | tf_op jit(solution)/shard_map/ppermute | solution.py:40
  154.7 3.4 %fusion.15 = f32[512,512]{1,0:T(8,128)} fusion(bf16[2048,512]{1,0:T(8,128)(2,1)S(1)} %copy-done.41, bf16[512,512]{1,0:T(8,128)(2,1)} %collective-permute-done.7, bf16[512,512]{1,0:T(8,128)(2,1)S(1)} %get-tuple-element.73, bf16[512,512]{1,0:T(8,128)(2,1)S(1)} %get-tuple-element.21, bf16[512,512]{1,0:T(8,128)(2,1)S(1)} %get-tuple-element.62), kind=kOutput, calls=%fused_computation.57 | convolution fusion | flops 1082130432 | bytes 5242880 | tf_op jit(solution)/shard_map/dot_general | solution.py:22
  164.5 9.2 %collective-permute-done.24 = bf16[512,512]{1,0:T(8,128)(2,1)} collective-permute-done((bf16[512,512]{1,0:T(8,128)(2,1)}, bf16[512,512]{1,0:T(8,128)(2,1)}, u32[]{:S(2)}, u32[]{:S(2)}) %collective-permute-start.24) | collective-permute-done | bytes 524320 | tf_op jit(solution)/shard_map/ppermute | solution.py:44
  173.8 11.3 %collective-permute-done.28 = bf16[512,512]{1,0:T(8,128)(2,1)} collective-permute-done((bf16[512,512]{1,0:T(8,128)(2,1)}, bf16[512,512]{1,0:T(8,128)(2,1)}, u32[]{:S(2)}, u32[]{:S(2)}) %collective-permute-start.28) | collective-permute-done | bytes 524320 | tf_op jit(solution)/shard_map/ppermute | solution.py:44
  185.1 4.7 %fusion.9 = bf16[512,512]{1,0:T(8,128)(2,1)} fusion(f32[512,512]{1,0:T(8,128)} %collective-permute-done.37, bf16[512,512]{1,0:T(8,128)(2,1)} %collective-permute-done.28, bf16[512,512]{1,0:T(8,128)(2,1)} %collective-permute-done.24, pred[]{:T(512)S(6)} %eq.20, pred[]{:T(512)S(6)} %eq.19, bf16[512,512]{1,0:T(8,128)(2,1)} %collective-permute-done.7, ...), kind=kOutput, calls=%fused_computation.30 | convolution fusion | flops 1091567616 | bytes 6815746 | tf_op jit(solution)/shard_map/dot_general | solution.py:22
  192.5 16.1 %collective-permute-done.23 = bf16[512,512]{1,0:T(8,128)(2,1)S(1)} collective-permute-done((bf16[512,512]{1,0:T(8,128)(2,1)}, bf16[512,512]{1,0:T(8,128)(2,1)S(1)}, u32[]{:S(2)}, u32[]{:S(2)}) %collective-permute-start.23) | collective-permute-done | bytes 524320 | tf_op jit(solution)/shard_map/ppermute | solution.py:40
  211.0 3.3 %fusion.18 = f32[512,512]{1,0:T(8,128)S(1)} fusion(bf16[2048,512]{1,0:T(8,128)(2,1)} %collective-permute-done.5, bf16[512,512]{1,0:T(8,128)(2,1)S(1)} %collective-permute-done.23, bf16[512,512]{1,0:T(8,128)(2,1)} %get-tuple-element.30, bf16[512,512]{1,0:T(8,128)(2,1)} %get-tuple-element.59, bf16[512,512]{1,0:T(8,128)(2,1)} %get-tuple-element.57), kind=kOutput, calls=%fused_computation.60 | convolution fusion | flops 1082130432 | bytes 5242880 | tf_op jit(solution)/shard_map/dot_general | solution.py:22
  214.5 25.1 %collective-permute-done.26 = bf16[1024,512]{1,0:T(8,128)(2,1)S(1)} collective-permute-done((bf16[1024,512]{1,0:T(8,128)(2,1)S(1)}, bf16[1024,512]{1,0:T(8,128)(2,1)S(1)}, u32[]{:S(2)}, u32[]{:S(2)}) %collective-permute-start.26) | collective-permute-done | bytes 1048608 | tf_op jit(solution)/shard_map/ppermute | solution.py:40
  242.6 3.2 fusion.5
  248.1 4.0 %collective-permute-start.33 = (bf16[512,512]{1,0:T(8,128)(2,1)S(1)}, bf16[512,512]{1,0:T(8,128)(2,1)S(1)}, u32[]{:S(2)}, u32[]{:S(2)}) collective-permute-start(bf16[512,512]{1,0:T(8,128)(2,1)S(1)} %get-tuple-element.34), channel_id=1, source_target_pairs={{0,4},{1,5},{2,6},{3,7},{4,0},{5,1},{6,2},{7,3},{8,12},{9,13},{10,... | collective-permute-start | bytes 1572872 | tf_op jit(solution)/shard_map/ppermute | solution.py:40
  252.1 2.9 collective-permute-done.30
  255.0 4.0 %fusion.17 = f32[512,512]{1,0:T(8,128)} fusion(bf16[2048,512]{1,0:T(8,128)(2,1)} %collective-permute-done.5, bf16[512,512]{1,0:T(8,128)(2,1)S(1)} %collective-permute-done.30, bf16[512,512]{1,0:T(8,128)(2,1)S(1)} %get-tuple-element.33, bf16[512,512]{1,0:T(8,128)(2,1)S(1)} %get-tuple-element.55, bf16[512,512]{1,0:T(8,128)(2,1)S(1)} %get-tuple-element.52), kind=kOutput, calls=%fused_computation.59 | convolution fusion | flops 1082130432 | bytes 5242880 | tf_op jit(solution)/shard_map/dot_general | solution.py:22
  260.5 3.3 fusion.16
  264.4 4.1 %fusion.22 = f32[512,512]{1,0:T(8,128)} fusion(bf16[2048,512]{1,0:T(8,128)(2,1)} %collective-permute-done.5, bf16[512,512]{1,0:T(8,128)(2,1)} %collective-permute-done.4, bf16[512,512]{1,0:T(8,128)(2,1)S(1)} %copy-done.3, bf16[512,512]{1,0:T(8,128)(2,1)S(1)} %copy-done.4, bf16[512,512]{1,0:T(8,128)(2,1)S(1)} %copy-done.9), kind=kOutput, calls=%fused_computation.64 | convolution fusion | flops 1082130432 | bytes 5242880 | tf_op jit(solution)/shard_map/dot_general | solution.py:22
  270.2 3.3 fusion.6
  273.5 3.2 collective-permute-start.32
  276.7 9.1 %collective-permute-done.35 = bf16[512,512]{1,0:T(8,128)(2,1)S(1)} collective-permute-done((bf16[512,512]{1,0:T(8,128)(2,1)S(1)}, bf16[512,512]{1,0:T(8,128)(2,1)S(1)}, u32[]{:S(2)}, u32[]{:S(2)}) %collective-permute-start.35) | collective-permute-done | bytes 524320 | tf_op jit(solution)/shard_map/ppermute | solution.py:44
  287.8 4.2 %collective-permute-start.36 = (bf16[512,512]{1,0:T(8,128)(2,1)}, bf16[512,512]{1,0:T(8,128)(2,1)S(1)}, u32[]{:S(2)}, u32[]{:S(2)}) collective-permute-start(bf16[512,512]{1,0:T(8,128)(2,1)} %fusion.10), channel_id=1, source_target_pairs={{0,8},{8,16},{16,24},{24,0},{1,9},{9,17},{17,25},{25,1},{2,10},{10... | collective-permute-start | bytes 1572872 | tf_op jit(solution)/shard_map/ppermute | solution.py:44
  292.1 9.7 %collective-permute-done.32 = bf16[512,512]{1,0:T(8,128)(2,1)} collective-permute-done((bf16[512,512]{1,0:T(8,128)(2,1)}, bf16[512,512]{1,0:T(8,128)(2,1)}, u32[]{:S(2)}, u32[]{:S(2)}) %collective-permute-start.32) | collective-permute-done | bytes 524320 | tf_op jit(solution)/shard_map/ppermute | solution.py:44
  301.8 9.4 %collective-permute-done.36 = bf16[512,512]{1,0:T(8,128)(2,1)S(1)} collective-permute-done((bf16[512,512]{1,0:T(8,128)(2,1)}, bf16[512,512]{1,0:T(8,128)(2,1)S(1)}, u32[]{:S(2)}, u32[]{:S(2)}) %collective-permute-start.36) | collective-permute-done | bytes 524320 | tf_op jit(solution)/shard_map/ppermute | solution.py:44
  311.2 10.9 %fusion = bf16[1,512,4096]{2,1,0:T(8,128)(2,1)} fusion(bf16[512,4096]{1,0:T(8,128)(2,1)} %param.11, bf16[512,4096]{1,0:T(8,128)(2,1)} %all-gather.2.cloned.1.call-done, f32[512,512]{1,0:T(8,128)} %collective-permute-done.6, bf16[512,512]{1,0:T(8,128)(2,1)} %collective-permute-done.32, bf16[512,512]{1,0:T(8,128)(2,1)S(1)} %collective-permute-done.36, ...), kind=kOutput, calls=%fused_computation.1 | convolution fusion | flops 3249537024 | bytes 18874370 | tf_op jit(solution)/shard_map/dot_general | solution.py:13
  (182 shorter events, 60.8 us)
Async XLA Ops:
  6.5 304.7 %all-gather.2.cloned.1.call-start = ((), (), s32[]{:S(2)}) async-start(), calls=%async_computation | async-start | bytes 4718592 | tf_op jit(solution)/shard_map/all_gather | solution.py:129
  7.8 27.8 %collective-permute-start.1 = (bf16[1024,512]{1,0:T(8,128)(2,1)S(1)}, bf16[1024,512]{1,0:T(8,128)(2,1)S(1)}, u32[]{:S(2)}, u32[]{:S(2)}) collective-permute-start(bf16[1024,512]{1,0:T(8,128)(2,1)S(1)} %pad_maximum_fusion.12), channel_id=1, source_target_pairs={{0,4},{1,5},{2,6},{3,7},{4,0},{5,1},{6,2},{7,3},{8,12},{9,13},{10,... | collective-permute-start | bytes 3145736 | tf_op jit(solution)/shard_map/ppermute | solution.py:40
  9.4 26.2 %collective-permute-start = (bf16[1024,512]{1,0:T(8,128)(2,1)S(1)}, bf16[1024,512]{1,0:T(8,128)(2,1)S(1)}, u32[]{:S(2)}, u32[]{:S(2)}) collective-permute-start(bf16[1024,512]{1,0:T(8,128)(2,1)S(1)} %pad_maximum_fusion.12), channel_id=1, source_target_pairs={{0,2},{1,3},{2,0},{3,1},{4,6},{5,7},{6,4},{7,5},{8,10},{9,11},{10,... | collective-permute-start | bytes 3145736 | tf_op jit(solution)/shard_map/ppermute | solution.py:40
  10.9 15.2 %collective-permute-start.2 = (bf16[512,512]{1,0:T(8,128)(2,1)}, bf16[512,512]{1,0:T(8,128)(2,1)}, u32[]{:S(2)}, u32[]{:S(2)}) collective-permute-start(bf16[512,512]{1,0:T(8,128)(2,1)} %bitcast.48), channel_id=1, source_target_pairs={{0,24},{8,0},{16,8},{24,16},{1,25},{9,1},{17,9},{25,17},{2,26},{10... | collective-permute-start | bytes 1572872 | tf_op jit(solution)/shard_map/ppermute | solution.py:44
  11.3 24.3 %collective-permute-start.3 = (bf16[512,512]{1,0:T(8,128)(2,1)}, bf16[512,512]{1,0:T(8,128)(2,1)S(1)}, u32[]{:S(2)}, u32[]{:S(2)}) collective-permute-start(bf16[512,512]{1,0:T(8,128)(2,1)} %bitcast.49), channel_id=1, source_target_pairs={{0,8},{8,16},{16,24},{24,0},{1,9},{9,17},{17,25},{25,1},{2,10},{10... | collective-permute-start | bytes 1572872 | tf_op jit(solution)/shard_map/ppermute | solution.py:44
  35.6 12.4 %collective-permute-start.8 = (bf16[512,512]{1,0:T(8,128)(2,1)}, bf16[512,512]{1,0:T(8,128)(2,1)}, u32[]{:S(2)}, u32[]{:S(2)}) collective-permute-start(bf16[512,512]{1,0:T(8,128)(2,1)} %collective-permute-done.2), channel_id=1, source_target_pairs={{0,24},{8,0},{16,8},{24,16},{1,25},{9,1},{17,9},{25,17},{2,26},{10... | collective-permute-start | bytes 1572872 | tf_op jit(solution)/shard_map/ppermute | solution.py:44
  51.3 22.1 %collective-permute-start.12 = (bf16[1024,512]{1,0:T(8,128)(2,1)S(1)}, bf16[1024,512]{1,0:T(8,128)(2,1)S(1)}, u32[]{:S(2)}, u32[]{:S(2)}) collective-permute-start(bf16[1024,512]{1,0:T(8,128)(2,1)S(1)} %pad_maximum_fusion.14), channel_id=1, source_target_pairs={{0,4},{1,5},{2,6},{3,7},{4,0},{5,1},{6,2},{7,3},{8,12},{9,13},{10,... | collective-permute-start | bytes 3145736 | tf_op jit(solution)/shard_map/ppermute | solution.py:40
  53.0 29.7 %collective-permute-start.18 = (bf16[2048,512]{1,0:T(8,128)(2,1)S(1)}, bf16[2048,512]{1,0:T(8,128)(2,1)S(1)}, u32[]{:S(2)}, u32[]{:S(2)}) collective-permute-start(bf16[2048,512]{1,0:T(8,128)(2,1)S(1)} %pad_maximum_fusion.5), channel_id=1, source_target_pairs={{0,1},{1,0},{2,3},{3,2},{4,5},{5,4},{6,7},{7,6},{8,9},{9,8},{10,11... | collective-permute-start | bytes 6291464 | tf_op jit(solution)/shard_map/ppermute | solution.py:40
  53.0 25.6 %collective-permute-start.11 = (bf16[1024,512]{1,0:T(8,128)(2,1)S(1)}, bf16[1024,512]{1,0:T(8,128)(2,1)S(1)}, u32[]{:S(2)}, u32[]{:S(2)}) collective-permute-start(bf16[1024,512]{1,0:T(8,128)(2,1)S(1)} %pad_maximum_fusion.14), channel_id=1, source_target_pairs={{0,2},{1,3},{2,0},{3,1},{4,6},{5,7},{6,4},{7,5},{8,10},{9,11},{10,... | collective-permute-start | bytes 3145736 | tf_op jit(solution)/shard_map/ppermute | solution.py:40
  53.6 25.8 %collective-permute-start.9 = (bf16[512,512]{1,0:T(8,128)(2,1)S(1)}, bf16[512,512]{1,0:T(8,128)(2,1)S(1)}, u32[]{:S(2)}, u32[]{:S(2)}) collective-permute-start(bf16[512,512]{1,0:T(8,128)(2,1)S(1)} %bitcast.51), channel_id=1, source_target_pairs={{0,24},{8,0},{16,8},{24,16},{1,25},{9,1},{17,9},{25,17},{2,26},{10... | collective-permute-start | bytes 1572872 | tf_op jit(solution)/shard_map/ppermute | solution.py:44
  54.0 25.5 %collective-permute-start.10 = (bf16[512,512]{1,0:T(8,128)(2,1)S(1)}, bf16[512,512]{1,0:T(8,128)(2,1)S(1)}, u32[]{:S(2)}, u32[]{:S(2)}) collective-permute-start(bf16[512,512]{1,0:T(8,128)(2,1)S(1)} %bitcast.52), channel_id=1, source_target_pairs={{0,8},{8,16},{16,24},{24,0},{1,9},{9,17},{17,25},{25,1},{2,10},{10... | collective-permute-start | bytes 1572872 | tf_op jit(solution)/shard_map/ppermute | solution.py:44
  79.5 13.6 %collective-permute-start.15 = (bf16[512,512]{1,0:T(8,128)(2,1)S(1)}, bf16[512,512]{1,0:T(8,128)(2,1)S(1)}, u32[]{:S(2)}, u32[]{:S(2)}) collective-permute-start(bf16[512,512]{1,0:T(8,128)(2,1)S(1)} %get-tuple-element.27), channel_id=1, source_target_pairs={{0,2},{1,3},{2,0},{3,1},{4,6},{5,7},{6,4},{7,5},{8,10},{9,11},{10,... | collective-permute-start | bytes 1572872 | tf_op jit(solution)/shard_map/ppermute | solution.py:40
  81.3 15.9 %collective-permute-start.13 = (bf16[512,512]{1,0:T(8,128)(2,1)S(1)}, bf16[512,512]{1,0:T(8,128)(2,1)}, u32[]{:S(2)}, u32[]{:S(2)}) collective-permute-start(bf16[512,512]{1,0:T(8,128)(2,1)S(1)} %collective-permute-done.9), channel_id=1, source_target_pairs={{0,24},{8,0},{16,8},{24,16},{1,25},{9,1},{17,9},{25,17},{2,26},{10... | collective-permute-start | bytes 1572872 | tf_op jit(solution)/shard_map/ppermute | solution.py:44
  95.3 19.5 %collective-permute-start.19 = (f32[512,512]{1,0:T(8,128)}, f32[512,512]{1,0:T(8,128)}, u32[]{:S(2)}, u32[]{:S(2)}) collective-permute-start(f32[512,512]{1,0:T(8,128)} %fusion.21), channel_id=1, source_target_pairs={{0,1},{1,0},{2,3},{3,2},{4,5},{5,4},{6,7},{7,6},{8,9},{9,8},{10,11... | collective-permute-start | bytes 3145736 | tf_op jit(solution)/shard_map/ppermute | solution.py:40
  95.4 14.7 %collective-permute-start.14 = (bf16[512,512]{1,0:T(8,128)(2,1)}, bf16[512,512]{1,0:T(8,128)(2,1)}, u32[]{:S(2)}, u32[]{:S(2)}) collective-permute-start(bf16[512,512]{1,0:T(8,128)(2,1)} %get-tuple-element.26), channel_id=1, source_target_pairs={{0,4},{1,5},{2,6},{3,7},{4,0},{5,1},{6,2},{7,3},{8,12},{9,13},{10,... | collective-permute-start | bytes 1572872 | tf_op jit(solution)/shard_map/ppermute | solution.py:40
  110.0 24.7 %collective-permute-start.16 = (bf16[1024,512]{1,0:T(8,128)(2,1)S(1)}, bf16[1024,512]{1,0:T(8,128)(2,1)S(1)}, u32[]{:S(2)}, u32[]{:S(2)}) collective-permute-start(bf16[1024,512]{1,0:T(8,128)(2,1)S(1)} %pad_maximum_fusion.15), channel_id=1, source_target_pairs={{0,4},{1,5},{2,6},{3,7},{4,0},{5,1},{6,2},{7,3},{8,12},{9,13},{10,... | collective-permute-start | bytes 3145736 | tf_op jit(solution)/shard_map/ppermute | solution.py:40
  110.5 25.1 %collective-permute-start.17 = (bf16[1024,512]{1,0:T(8,128)(2,1)S(1)}, bf16[1024,512]{1,0:T(8,128)(2,1)S(1)}, u32[]{:S(2)}, u32[]{:S(2)}) collective-permute-start(bf16[1024,512]{1,0:T(8,128)(2,1)S(1)} %pad_maximum_fusion.15), channel_id=1, source_target_pairs={{0,2},{1,3},{2,0},{3,1},{4,6},{5,7},{6,4},{7,5},{8,10},{9,11},{10,... | collective-permute-start | bytes 3145736 | tf_op jit(solution)/shard_map/ppermute | solution.py:40
  114.7 21.7 %collective-permute-start.21 = (f32[512,512]{1,0:T(8,128)S(1)}, f32[512,512]{1,0:T(8,128)S(1)}, u32[]{:S(2)}, u32[]{:S(2)}) collective-permute-start(f32[512,512]{1,0:T(8,128)S(1)} %fusion.20), channel_id=1, source_target_pairs={{0,1},{1,0},{2,3},{3,2},{4,5},{5,4},{6,7},{7,6},{8,9},{9,8},{10,11... | collective-permute-start | bytes 3145736 | tf_op jit(solution)/shard_map/ppermute | solution.py:40
  117.4 19.1 %collective-permute-start.20 = (bf16[512,512]{1,0:T(8,128)(2,1)S(1)}, bf16[512,512]{1,0:T(8,128)(2,1)S(1)}, u32[]{:S(2)}, u32[]{:S(2)}) collective-permute-start(bf16[512,512]{1,0:T(8,128)(2,1)S(1)} %fusion.2), channel_id=1, source_target_pairs={{0,8},{8,16},{16,24},{24,0},{1,9},{9,17},{17,25},{25,1},{2,10},{10... | collective-permute-start | bytes 1572872 | tf_op jit(solution)/shard_map/ppermute | solution.py:44
  139.9 12.6 %collective-permute-start.22 = (bf16[512,512]{1,0:T(8,128)(2,1)S(1)}, bf16[512,512]{1,0:T(8,128)(2,1)S(1)}, u32[]{:S(2)}, u32[]{:S(2)}) collective-permute-start(bf16[512,512]{1,0:T(8,128)(2,1)S(1)} %get-tuple-element.29), channel_id=1, source_target_pairs={{0,4},{1,5},{2,6},{3,7},{4,0},{5,1},{6,2},{7,3},{8,12},{9,13},{10,... | collective-permute-start | bytes 1572872 | tf_op jit(solution)/shard_map/ppermute | solution.py:40
  158.7 15.1 %collective-permute-start.24 = (bf16[512,512]{1,0:T(8,128)(2,1)}, bf16[512,512]{1,0:T(8,128)(2,1)}, u32[]{:S(2)}, u32[]{:S(2)}) collective-permute-start(bf16[512,512]{1,0:T(8,128)(2,1)} %broadcast_select_fusion), channel_id=1, source_target_pairs={{0,8},{8,16},{16,24},{24,0},{1,9},{9,17},{17,25},{25,1},{2,10},{10... | collective-permute-start | bytes 1572872 | tf_op jit(solution)/shard_map/ppermute | solution.py:44
  161.5 23.5 %collective-permute-start.28 = (bf16[512,512]{1,0:T(8,128)(2,1)}, bf16[512,512]{1,0:T(8,128)(2,1)}, u32[]{:S(2)}, u32[]{:S(2)}) collective-permute-start(bf16[512,512]{1,0:T(8,128)(2,1)} %fusion.4), channel_id=1, source_target_pairs={{0,24},{8,0},{16,8},{24,16},{1,25},{9,1},{17,9},{25,17},{2,26},{10... | collective-permute-start | bytes 1572872 | tf_op jit(solution)/shard_map/ppermute | solution.py:44
  164.4 46.6 %collective-permute-start.5 = (bf16[2048,512]{1,0:T(8,128)(2,1)S(1)}, bf16[2048,512]{1,0:T(8,128)(2,1)}, u32[]{:S(2)}, u32[]{:S(2)}) collective-permute-start(bf16[2048,512]{1,0:T(8,128)(2,1)S(1)} %pad_maximum_fusion.2), channel_id=1, source_target_pairs={{0,1},{1,0},{2,3},{3,2},{4,5},{5,4},{6,7},{7,6},{8,9},{9,8},{10,11... | collective-permute-start | bytes 6291464 | tf_op jit(solution)/shard_map/ppermute | solution.py:40
  189.8 18.9 %collective-permute-start.23 = (bf16[512,512]{1,0:T(8,128)(2,1)}, bf16[512,512]{1,0:T(8,128)(2,1)S(1)}, u32[]{:S(2)}, u32[]{:S(2)}) collective-permute-start(bf16[512,512]{1,0:T(8,128)(2,1)} %get-tuple-element.30), channel_id=1, source_target_pairs={{0,2},{1,3},{2,0},{3,1},{4,6},{5,7},{6,4},{7,5},{8,10},{9,11},{10,... | collective-permute-start | bytes 1572872 | tf_op jit(solution)/shard_map/ppermute | solution.py:40
  208.6 30.9 %collective-permute-start.26 = (bf16[1024,512]{1,0:T(8,128)(2,1)S(1)}, bf16[1024,512]{1,0:T(8,128)(2,1)S(1)}, u32[]{:S(2)}, u32[]{:S(2)}) collective-permute-start(bf16[1024,512]{1,0:T(8,128)(2,1)S(1)} %pad_maximum_fusion.13), channel_id=1, source_target_pairs={{0,4},{1,5},{2,6},{3,7},{4,0},{5,1},{6,2},{7,3},{8,12},{9,13},{10,... | collective-permute-start | bytes 3145736 | tf_op jit(solution)/shard_map/ppermute | solution.py:40
  208.6 33.8 %collective-permute-start.25 = (bf16[1024,512]{1,0:T(8,128)(2,1)S(1)}, bf16[1024,512]{1,0:T(8,128)(2,1)S(1)}, u32[]{:S(2)}, u32[]{:S(2)}) collective-permute-start(bf16[1024,512]{1,0:T(8,128)(2,1)S(1)} %pad_maximum_fusion.13), channel_id=1, source_target_pairs={{0,2},{1,3},{2,0},{3,1},{4,6},{5,7},{6,4},{7,5},{8,10},{9,11},{10,... | collective-permute-start | bytes 3145736 | tf_op jit(solution)/shard_map/ppermute | solution.py:40
  214.4 28.1 %collective-permute-start.29 = (f32[512,512]{1,0:T(8,128)S(1)}, f32[512,512]{1,0:T(8,128)S(1)}, u32[]{:S(2)}, u32[]{:S(2)}) collective-permute-start(f32[512,512]{1,0:T(8,128)S(1)} %fusion.18), channel_id=1, source_target_pairs={{0,1},{1,0},{2,3},{3,2},{4,5},{5,4},{6,7},{7,6},{8,9},{9,8},{10,11... | collective-permute-start | bytes 3145736 | tf_op jit(solution)/shard_map/ppermute | solution.py:40
  263.7 22.0 %collective-permute-start.34 = (f32[512,512]{1,0:T(8,128)S(1)}, f32[512,512]{1,0:T(8,128)S(1)}, u32[]{:S(2)}, u32[]{:S(2)}) collective-permute-start(f32[512,512]{1,0:T(8,128)S(1)} %fusion.16), channel_id=1, source_target_pairs={{0,1},{1,0},{2,3},{3,2},{4,5},{5,4},{6,7},{7,6},{8,9},{9,8},{10,11... | collective-permute-start | bytes 3145736 | tf_op jit(solution)/shard_map/ppermute | solution.py:40
  268.5 23.6 %collective-permute-start.6 = (f32[512,512]{1,0:T(8,128)}, f32[512,512]{1,0:T(8,128)}, u32[]{:S(2)}, u32[]{:S(2)}) collective-permute-start(f32[512,512]{1,0:T(8,128)} %fusion.22), channel_id=1, source_target_pairs={{0,1},{1,0},{2,3},{3,2},{4,5},{5,4},{6,7},{7,6},{8,9},{9,8},{10,11... | collective-permute-start | bytes 3145736 | tf_op jit(solution)/shard_map/ppermute | solution.py:40
  268.5 17.2 %collective-permute-start.35 = (bf16[512,512]{1,0:T(8,128)(2,1)S(1)}, bf16[512,512]{1,0:T(8,128)(2,1)S(1)}, u32[]{:S(2)}, u32[]{:S(2)}) collective-permute-start(bf16[512,512]{1,0:T(8,128)(2,1)S(1)} %copy-done.44), channel_id=1, source_target_pairs={{0,8},{8,16},{16,24},{24,0},{1,9},{9,17},{17,25},{25,1},{2,10},{10... | collective-permute-start | bytes 1572872 | tf_op jit(solution)/shard_map/ppermute | solution.py:44
  273.5 28.3 %collective-permute-start.32 = (bf16[512,512]{1,0:T(8,128)(2,1)}, bf16[512,512]{1,0:T(8,128)(2,1)}, u32[]{:S(2)}, u32[]{:S(2)}) collective-permute-start(bf16[512,512]{1,0:T(8,128)(2,1)} %fusion.6), channel_id=1, source_target_pairs={{0,24},{8,0},{16,8},{24,16},{1,25},{9,1},{17,9},{25,17},{2,26},{10... | collective-permute-start | bytes 1572872 | tf_op jit(solution)/shard_map/ppermute | solution.py:44
  287.8 23.4 %collective-permute-start.36 = (bf16[512,512]{1,0:T(8,128)(2,1)}, bf16[512,512]{1,0:T(8,128)(2,1)S(1)}, u32[]{:S(2)}, u32[]{:S(2)}) collective-permute-start(bf16[512,512]{1,0:T(8,128)(2,1)} %fusion.10), channel_id=1, source_target_pairs={{0,8},{8,16},{16,24},{24,0},{1,9},{9,17},{17,25},{25,1},{2,10},{10... | collective-permute-start | bytes 1572872 | tf_op jit(solution)/shard_map/ppermute | solution.py:44
  (56 other events, 841.6 us)
Sparse Core Ops, SparseCore 0:
  189.9 51.1 all-gather.1

commit v11 on v10

--- a/solution.py
+++ b/solution.py
@@ -77,6 +77,7 @@
         crossing = [swap(dot(even, theirs[side]), CORE) for (side, _), even in zip(group, evens)]
         for (side, i), even, other in zip(group, evens, crossing):
             rotated[side, i] = (dot(even, ours[side]) + other).astype(jnp.bfloat16)
+        return [rotated[key] for key in group]
 
     def pass_on(side):
         return shift(rotated[side, 2], 1, n_dp)
@@ -101,20 +102,20 @@
         x, y = swap(stack, X), swap(stack, Y)
         due = [x, y]
         if at:
-            rotate(groups[at - 1], evens)
+            due += rotate(groups[at - 1], evens)
         if at < 2:
             due += [fetch(at, 1, gate), fetch(at, 3, gate)]
         if at == 2:
             passed_in = pass_on(0)
-            due += [passed_in, rotated[0, 1]]
+            due.append(passed_in)
         if at == 3:
             in_from_ahead = send_behind(0)
             passed_out = pass_on(1)
-            due += [in_from_ahead, rotated[1, 2]]
+            due.append(in_from_ahead)
         gate = due
         to_x, to_y = after((y[tokens:], x[:tokens]), gate)
         xy = [swap(to_y, Y), swap(to_x, X)]
-        due = xy + []
+        due = list(xy)
         if at < 2:
             due.append(fetch(at, 2, gate))
         if at == 2:
@@ -122,10 +123,11 @@
             due.append(in_from_behind)
         if at == 3:
             due.append(passed_out)
+        xy = after(xy, [])
         rows = [slice(0, tokens), slice(tokens, None)]
         evens = [jnp.concatenate([stack[r], x[r], y[r], last], axis=1) for r, last in zip(rows, xy)]
 
-    rot_in = keep(0, in_from_behind, in_from_ahead)
+    rot_in = after(keep(0, in_from_behind, in_from_ahead), due)
     all_rot_in = lax.all_gather(rot_in, "tensor", axis=1, tiled=True)
     rotate(groups[-1], evens)
     rot_out = keep(1, send_ahead(1, passed_out, []), send_behind(1))

time: 334 us -> 264 us (0.79)
  waiting for transfers between devices: 195 us -> 158 us
  matrix products: 57.2 us -> 44.2 us
  starting transfers between devices: 41 us -> 28.2 us
  local copies, waits for them, and re-layouts: 15 us -> 10.3 us
    ppermute x26, waiting for transfers between devices: 120 us -> 87.3 us  [swap(): lax.ppermute(block, 'tensor', [(j, j ^ bit) for j in range(X + Y + CORE +...]
    dot_general x15 -> x16, matrix products: 46.4 us -> 35.4 us  [dot(): return jnp.dot(a, b, preferred_element_type=jnp.float32)]
    ppermute x12, starting transfers between devices: 20.4 us -> 10.6 us  [shift(): return lax.ppermute(block, 'dp', [(z, (z + by) % n) for z in range(n)])]
    ppermute x12, waiting for transfers between devices: 75.6 us -> 70.6 us  [shift(): return lax.ppermute(block, 'dp', [(z, (z + by) % n) for z in range(n)])]
  transfers between devices with their start and end apart: 39 -> 39, of which waited for: 20 -> 21; matrix products, arithmetic and copies ran while one was open for 18% -> 16% of each run, Pallas kernels for 0% -> 0%
where the time goes in v11:
time: 264 us; the launch traced here: 260 us
  waiting for transfers between devices  158 us (60%)
  matrix products  44.2 us (17%)
  starting transfers between devices  28.2 us (11%)
  between operations  15.3 us (6%)
  local copies, waits for them, and re-layouts  10.3 us (4%)
  other arithmetic  3.84 us (1%)
    ppermute x26, waiting for transfers between devices, swap(): lax.ppermute(block, 'tensor', [(j, j ^ bit) for j in range(X + Y + CORE +...  87.3 us
    ppermute x12, waiting for transfers between devices, shift(): return lax.ppermute(block, 'dp', [(z, (z + by) % n) for z in range(n)])  70.6 us
    dot_general x16, matrix products, dot(): return jnp.dot(a, b, preferred_element_type=jnp.float32)  35.4 us
    ppermute x26, starting transfers between devices, swap(): lax.ppermute(block, 'tensor', [(j, j ^ bit) for j in range(X + Y + CORE +...  17.6 us
    ppermute x12, starting transfers between devices, shift(): return lax.ppermute(block, 'dp', [(z, (z + by) % n) for z in range(n)])  10.6 us
    dot_general x1, matrix products, product_and_divide(): lax.dot_general(rot_out, all_rot_in, contract, preferred_element_type=jnp...  8.82 us
  transfers between devices with their start and end apart: 39, of which 21 were waited for; matrix products, arithmetic and copies ran while one was open for 16% of the time, Pallas kernels for 0%

profile of v11, /device:TPU:16, one launch (start us, length us, event | category | flops | bytes accessed | tf_op | source)
XLA Modules:
  0.0 259.8 jit_solution(17091968609076454198)
XLA Ops:
  7.8 1.6 collective-permute-start.1
  10.9 1.6 collective-permute-start.3
  12.5 2.7 %dynamic-slice_bitcast_fusion.7 = (bf16[512,512]{1,0:T(8,128)(2,1)S(1)}, bf16[512,512]{1,0:T(8,128)(2,1)S(1)}, bf16[512,512]{1,0:T(8,128)(2,1)S(1)}, bf16[512,51...) fusion(bf16[1,4096,512]{2,1,0:T(8,128)(2,1)} %param.8, ...), kind=kLoop, calls=%fused_computation.45 | loop fusion | bytes 8388640 | tf_op jit(solution)/shard_map/dynamic_slice | solution.py:49
  15.9 2.2 copy-done
  18.6 16.9 %collective-permute-done.3 = bf16[512,512]{1,0:T(8,128)(2,1)} collective-permute-done((bf16[512,512]{1,0:T(8,128)(2,1)}, bf16[512,512]{1,0:T(8,128)(2,1)}, u32[]{:S(2)}, u32[]{:S(2)}) %collective-permute-start.3) | collective-permute-done | bytes 524320 | tf_op jit(solution)/shard_map/ppermute | solution.py:44
  38.0 11.9 %collective-permute-done.8 = bf16[512,512]{1,0:T(8,128)(2,1)S(1)} collective-permute-done((bf16[512,512]{1,0:T(8,128)(2,1)S(1)}, bf16[512,512]{1,0:T(8,128)(2,1)S(1)}, u32[]{:S(2)}, u32[]{:S(2)}) %collective-permute-start.8) | collective-permute-done | bytes 524320 | tf_op jit(solution)/shard_map/ppermute | solution.py:44
  50.8 1.5 collective-permute-start.12
  54.4 1.7 collective-permute-start.10
  57.7 17.2 %collective-permute-done.12 = bf16[1024,512]{1,0:T(8,128)(2,1)S(1)} collective-permute-done((bf16[1024,512]{1,0:T(8,128)(2,1)S(1)}, bf16[1024,512]{1,0:T(8,128)(2,1)S(1)}, u32[]{:S(2)}, u32[]{:S(2)}) %collective-permute-start.12) | collective-permute-done | bytes 1048608 | tf_op jit(solution)/shard_map/ppermute | solution.py:40
  77.6 2.0 fusion.1
  79.6 3.0 %collective-permute-done.9 = bf16[512,512]{1,0:T(8,128)(2,1)S(1)} collective-permute-done((bf16[512,512]{1,0:T(8,128)(2,1)S(1)}, bf16[512,512]{1,0:T(8,128)(2,1)S(1)}, u32[]{:S(2)}, u32[]{:S(2)}) %collective-permute-start.9) | collective-permute-done | bytes 524320 | tf_op jit(solution)/shard_map/ppermute | solution.py:44
  85.5 10.6 %collective-permute-done.16 = bf16[512,512]{1,0:T(8,128)(2,1)S(1)} collective-permute-done((bf16[512,512]{1,0:T(8,128)(2,1)S(1)}, bf16[512,512]{1,0:T(8,128)(2,1)S(1)}, u32[]{:S(2)}, u32[]{:S(2)}) %collective-permute-start.16) | collective-permute-done | bytes 524320 | tf_op jit(solution)/shard_map/ppermute | solution.py:40
  96.3 2.2 fusion.18
  101.3 1.6 collective-permute-start.19
  104.4 3.3 %fusion.19 = f32[512,512]{1,0:T(8,128)S(1)} fusion(bf16[2048,512]{1,0:T(8,128)(2,1)} %copy-done.37, bf16[512,512]{1,0:T(8,128)(2,1)} %copy-done.39, bf16[512,512]{1,0:T(8,128)(2,1)S(1)} %get-tuple-element.85, bf16[512,512]{1,0:T(8,128)(2,1)S(1)} %get-tuple-element.37, bf16[512,512]{1,0:T(8,128)(2,1)} %get-tuple-element.82), kind=kOutput, calls=%fused_computation.62 | convolution fusion | flops 1082130432 | bytes 5242880 | tf_op jit(solution)/shard_map/dot_general | solution.py:22
  107.9 2.5 fusion.4
  110.8 16.1 %collective-permute-done.19 = bf16[1024,512]{1,0:T(8,128)(2,1)S(1)} collective-permute-done((bf16[1024,512]{1,0:T(8,128)(2,1)S(1)}, bf16[1024,512]{1,0:T(8,128)(2,1)S(1)}, u32[]{:S(2)}, u32[]{:S(2)}) %collective-permute-start.19) | collective-permute-done | bytes 1048608 | tf_op jit(solution)/shard_map/ppermute | solution.py:40
  129.5 1.6 collective-permute-start.23
  131.7 11.1 %collective-permute-done.23 = bf16[512,512]{1,0:T(8,128)(2,1)S(1)} collective-permute-done((bf16[512,512]{1,0:T(8,128)(2,1)S(1)}, bf16[512,512]{1,0:T(8,128)(2,1)S(1)}, u32[]{:S(2)}, u32[]{:S(2)}) %collective-permute-start.23) | collective-permute-done | bytes 524320 | tf_op jit(solution)/shard_map/ppermute | solution.py:40
  147.4 12.3 %collective-permute-done.25 = bf16[512,512]{1,0:T(8,128)(2,1)S(1)} collective-permute-done((bf16[512,512]{1,0:T(8,128)(2,1)S(1)}, bf16[512,512]{1,0:T(8,128)(2,1)S(1)}, u32[]{:S(2)}, u32[]{:S(2)}) %collective-permute-start.25) | collective-permute-done | bytes 524320 | tf_op jit(solution)/shard_map/ppermute | solution.py:44
  160.9 2.1 fusion.6
  166.3 18.1 %collective-permute-done.27 = bf16[1024,512]{1,0:T(8,128)(2,1)S(1)} collective-permute-done((bf16[1024,512]{1,0:T(8,128)(2,1)S(1)}, bf16[1024,512]{1,0:T(8,128)(2,1)S(1)}, u32[]{:S(2)}, u32[]{:S(2)}) %collective-permute-start.27) | collective-permute-done | bytes 1048608 | tf_op jit(solution)/shard_map/ppermute | solution.py:40
  186.3 3.9 %collective-permute-done.30 = bf16[512,512]{1,0:T(8,128)(2,1)S(1)} collective-permute-done((bf16[512,512]{1,0:T(8,128)(2,1)S(1)}, bf16[512,512]{1,0:T(8,128)(2,1)S(1)}, u32[]{:S(2)}, u32[]{:S(2)}) %collective-permute-start.30) | collective-permute-done | bytes 524320 | tf_op jit(solution)/shard_map/ppermute | solution.py:44
  193.8 9.7 %collective-permute-done.31 = bf16[512,512]{1,0:T(8,128)(2,1)} collective-permute-done((bf16[512,512]{1,0:T(8,128)(2,1)}, bf16[512,512]{1,0:T(8,128)(2,1)}, u32[]{:S(2)}, u32[]{:S(2)}) %collective-permute-start.31) | collective-permute-done | bytes 524320 | tf_op jit(solution)/shard_map/ppermute | solution.py:40
  203.7 4.4 %fusion.14 = f32[512,512]{1,0:T(8,128)} fusion(bf16[2048,512]{1,0:T(8,128)(2,1)} %copy-done.34, bf16[512,512]{1,0:T(8,128)(2,1)} %collective-permute-done.31, bf16[512,512]{1,0:T(8,128)(2,1)S(1)} %copy-done.7, bf16[512,512]{1,0:T(8,128)(2,1)} %get-tuple-element.48, bf16[512,512]{1,0:T(8,128)(2,1)S(1)} %get-tuple-element.69), kind=kOutput, calls=%fused_computation.57 | convolution fusion | flops 1082130432 | bytes 5242880 | tf_op jit(solution)/shard_map/dot_general | solution.py:22
  208.1 3.3 %fusion.15 = f32[512,512]{1,0:T(8,128)} fusion(bf16[2048,512]{1,0:T(8,128)(2,1)S(1)} %copy-done.36, bf16[512,512]{1,0:T(8,128)(2,1)} %collective-permute-done.32, bf16[512,512]{1,0:T(8,128)(2,1)S(1)} %get-tuple-element.49, bf16[512,512]{1,0:T(8,128)(2,1)S(1)} %copy-done.6, bf16[512,512]{1,0:T(8,128)(2,1)S(1)} %get-tuple-element.70), kind=kOutput, calls=%fused_computation.58 | convolution fusion | flops 1082130432 | bytes 5242880 | tf_op jit(solution)/shard_map/dot_general | solution.py:22
  212.6 4.2 %fusion.9 = bf16[512,512]{1,0:T(8,128)(2,1)} fusion(bf16[512,512]{1,0:T(8,128)(2,1)} %collective-permute-done.36, f32[512,512]{1,0:T(8,128)} %collective-permute-done.35, pred[]{:T(512)S(6)} %eq.17, bf16[512,512]{1,0:T(8,128)(2,1)} %collective-permute-done.31, bf16[512,512]{1,0:T(8,128)(2,1)S(1)} %copy-done.7, bf16[512,512]{1,0:T(8,128)(2,1)} %get-tuple-element.48, ...), kind=kOutput, calls=%fused_computation.30 | convolution fusion | flops 1091305472 | bytes 6291457 | tf_op jit(solution)/shard_map/dot_general | solution.py:22
  217.5 2.6 %fusion.7 = bf16[512,512]{1,0:T(8,128)(2,1)S(1)} fusion(f32[512,512]{1,0:T(8,128)} %collective-permute-done.33, bf16[512,512]{1,0:T(8,128)(2,1)} %collective-permute-done.32, bf16[512,512]{1,0:T(8,128)(2,1)S(1)} %get-tuple-element.49, bf16[512,512]{1,0:T(8,128)(2,1)S(1)} %copy-done.6, bf16[512,512]{1,0:T(8,128)(2,1)S(1)} %get-tuple-element.70, ...), kind=kOutput, calls=%fused_computation.28 | convolution fusion | flops 1091043328 | bytes 5767168 | tf_op jit(solution)/shard_map/dot_general | solution.py:22
  220.2 1.5 collective-permute-start.34
  221.7 9.6 %collective-permute-done.37 = bf16[512,512]{1,0:T(8,128)(2,1)S(1)} collective-permute-done((bf16[512,512]{1,0:T(8,128)(2,1)}, bf16[512,512]{1,0:T(8,128)(2,1)S(1)}, u32[]{:S(2)}, u32[]{:S(2)}) %collective-permute-start.37) | collective-permute-done | bytes 524320 | tf_op jit(solution)/shard_map/ppermute | solution.py:44
  231.3 12.9 %collective-permute-done.34 = bf16[512,512]{1,0:T(8,128)(2,1)S(1)} collective-permute-done((bf16[512,512]{1,0:T(8,128)(2,1)S(1)}, bf16[512,512]{1,0:T(8,128)(2,1)S(1)}, u32[]{:S(2)}, u32[]{:S(2)}) %collective-permute-start.34) | collective-permute-done | bytes 524320 | tf_op jit(solution)/shard_map/ppermute | solution.py:44
  244.2 8.8 %fusion = bf16[1,512,4096]{2,1,0:T(8,128)(2,1)} fusion(bf16[512,4096]{1,0:T(8,128)(2,1)} %param.11, bf16[512,4096]{1,0:T(8,128)(2,1)} %all-gather.2.cloned.1.call-done, bf16[512,512]{1,0:T(8,128)(2,1)} %fusion.1, bf16[512,512]{1,0:T(8,128)(2,1)S(1)} %collective-permute-done.34, bf16[512,512]{1,0:T(8,128)(2,1)S(1)} %collective-permute-done.37, pred[]{:T(512)S(6)} %eq.18, ...), kind=kOutput, calls=%fused_computation.1 | convolution fusion | flops 2158493696 | bytes 14155778 | tf_op jit(solution)/shard_map/dot_general | solution.py:13
  (172 shorter events, 39.9 us)
Async XLA Ops:
  6.5 237.6 %all-gather.2.cloned.1.call-start = ((), (), s32[]{:S(2)}) async-start(), calls=%async_computation | async-start | bytes 4718592 | tf_op jit(solution)/shard_map/all_gather | solution.py:131
  7.8 27.7 %collective-permute-start.1 = (bf16[1024,512]{1,0:T(8,128)(2,1)S(1)}, bf16[1024,512]{1,0:T(8,128)(2,1)S(1)}, u32[]{:S(2)}, u32[]{:S(2)}) collective-permute-start(bf16[1024,512]{1,0:T(8,128)(2,1)S(1)} %pad_maximum_fusion.12), channel_id=1, source_target_pairs={{0,4},{1,5},{2,6},{3,7},{4,0},{5,1},{6,2},{7,3},{8,12},{9,13},{10,... | collective-permute-start | bytes 3145736 | tf_op jit(solution)/shard_map/ppermute | solution.py:40
  9.4 26.2 %collective-permute-start = (bf16[1024,512]{1,0:T(8,128)(2,1)S(1)}, bf16[1024,512]{1,0:T(8,128)(2,1)S(1)}, u32[]{:S(2)}, u32[]{:S(2)}) collective-permute-start(bf16[1024,512]{1,0:T(8,128)(2,1)S(1)} %pad_maximum_fusion.12), channel_id=1, source_target_pairs={{0,2},{1,3},{2,0},{3,1},{4,6},{5,7},{6,4},{7,5},{8,10},{9,11},{10,... | collective-permute-start | bytes 3145736 | tf_op jit(solution)/shard_map/ppermute | solution.py:40
  10.9 24.7 %collective-permute-start.3 = (bf16[512,512]{1,0:T(8,128)(2,1)}, bf16[512,512]{1,0:T(8,128)(2,1)}, u32[]{:S(2)}, u32[]{:S(2)}) collective-permute-start(bf16[512,512]{1,0:T(8,128)(2,1)} %bitcast.48), channel_id=1, source_target_pairs={{0,8},{8,16},{16,24},{24,0},{1,9},{9,17},{17,25},{25,1},{2,10},{10... | collective-permute-start | bytes 1572872 | tf_op jit(solution)/shard_map/ppermute | solution.py:44
  15.3 37.7 %collective-permute-start.13 = (bf16[2048,512]{1,0:T(8,128)(2,1)S(1)}, bf16[2048,512]{1,0:T(8,128)(2,1)S(1)}, u32[]{:S(2)}, u32[]{:S(2)}) collective-permute-start(bf16[2048,512]{1,0:T(8,128)(2,1)S(1)} %pad_maximum_fusion.5), channel_id=1, source_target_pairs={{0,1},{1,0},{2,3},{3,2},{4,5},{5,4},{6,7},{7,6},{8,9},{9,8},{10,11... | collective-permute-start | bytes 6291464 | tf_op jit(solution)/shard_map/ppermute | solution.py:40
  15.4 20.1 %collective-permute-start.2 = (bf16[512,512]{1,0:T(8,128)(2,1)S(1)}, bf16[512,512]{1,0:T(8,128)(2,1)S(1)}, u32[]{:S(2)}, u32[]{:S(2)}) collective-permute-start(bf16[512,512]{1,0:T(8,128)(2,1)S(1)} %bitcast.49), channel_id=1, source_target_pairs={{0,24},{8,0},{16,8},{24,16},{1,25},{9,1},{17,9},{25,17},{2,26},{10... | collective-permute-start | bytes 1572872 | tf_op jit(solution)/shard_map/ppermute | solution.py:44
  35.5 20.5 %collective-permute-start.6 = (bf16[2048,512]{1,0:T(8,128)(2,1)S(1)}, bf16[2048,512]{1,0:T(8,128)(2,1)S(1)}, u32[]{:S(2)}, u32[]{:S(2)}) collective-permute-start(bf16[2048,512]{1,0:T(8,128)(2,1)S(1)} %pad_maximum_fusion.2), channel_id=1, source_target_pairs={{0,1},{1,0},{2,3},{3,2},{4,5},{5,4},{6,7},{7,6},{8,9},{9,8},{10,11... | collective-permute-start | bytes 6291464 | tf_op jit(solution)/shard_map/ppermute | solution.py:40
  35.6 14.4 %collective-permute-start.8 = (bf16[512,512]{1,0:T(8,128)(2,1)S(1)}, bf16[512,512]{1,0:T(8,128)(2,1)S(1)}, u32[]{:S(2)}, u32[]{:S(2)}) collective-permute-start(bf16[512,512]{1,0:T(8,128)(2,1)S(1)} %collective-permute-done.2), channel_id=1, source_target_pairs={{0,24},{8,0},{16,8},{24,16},{1,25},{9,1},{17,9},{25,17},{2,26},{10... | collective-permute-start | bytes 1572872 | tf_op jit(solution)/shard_map/ppermute | solution.py:44
  36.9 13.7 %collective-permute-start.4 = (bf16[512,512]{1,0:T(8,128)(2,1)S(1)}, bf16[512,512]{1,0:T(8,128)(2,1)S(1)}, u32[]{:S(2)}, u32[]{:S(2)}) collective-permute-start(bf16[512,512]{1,0:T(8,128)(2,1)S(1)} %get-tuple-element.29), channel_id=1, source_target_pairs={{0,4},{1,5},{2,6},{3,7},{4,0},{5,1},{6,2},{7,3},{8,12},{9,13},{10,... | collective-permute-start | bytes 1572872 | tf_op jit(solution)/shard_map/ppermute | solution.py:40
  37.5 13.3 %collective-permute-start.5 = (bf16[512,512]{1,0:T(8,128)(2,1)S(1)}, bf16[512,512]{1,0:T(8,128)(2,1)S(1)}, u32[]{:S(2)}, u32[]{:S(2)}) collective-permute-start(bf16[512,512]{1,0:T(8,128)(2,1)S(1)} %get-tuple-element.30), channel_id=1, source_target_pairs={{0,2},{1,3},{2,0},{3,1},{4,6},{5,7},{6,4},{7,5},{8,10},{9,11},{10,... | collective-permute-start | bytes 1572872 | tf_op jit(solution)/shard_map/ppermute | solution.py:40
  50.8 24.1 %collective-permute-start.12 = (bf16[1024,512]{1,0:T(8,128)(2,1)S(1)}, bf16[1024,512]{1,0:T(8,128)(2,1)S(1)}, u32[]{:S(2)}, u32[]{:S(2)}) collective-permute-start(bf16[1024,512]{1,0:T(8,128)(2,1)S(1)} %pad_maximum_fusion.14), channel_id=1, source_target_pairs={{0,4},{1,5},{2,6},{3,7},{4,0},{5,1},{6,2},{7,3},{8,12},{9,13},{10,... | collective-permute-start | bytes 3145736 | tf_op jit(solution)/shard_map/ppermute | solution.py:40
  52.4 23.4 %collective-permute-start.11 = (bf16[1024,512]{1,0:T(8,128)(2,1)S(1)}, bf16[1024,512]{1,0:T(8,128)(2,1)S(1)}, u32[]{:S(2)}, u32[]{:S(2)}) collective-permute-start(bf16[1024,512]{1,0:T(8,128)(2,1)S(1)} %pad_maximum_fusion.14), channel_id=1, source_target_pairs={{0,2},{1,3},{2,0},{3,1},{4,6},{5,7},{6,4},{7,5},{8,10},{9,11},{10,... | collective-permute-start | bytes 3145736 | tf_op jit(solution)/shard_map/ppermute | solution.py:40
  54.2 21.7 %collective-permute-start.14 = (f32[512,512]{1,0:T(8,128)S(1)}, f32[512,512]{1,0:T(8,128)S(1)}, u32[]{:S(2)}, u32[]{:S(2)}) collective-permute-start(f32[512,512]{1,0:T(8,128)S(1)} %fusion.20), channel_id=1, source_target_pairs={{0,1},{1,0},{2,3},{3,2},{4,5},{5,4},{6,7},{7,6},{8,9},{9,8},{10,11... | collective-permute-start | bytes 3145736 | tf_op jit(solution)/shard_map/ppermute | solution.py:40
  54.4 25.2 %collective-permute-start.10 = (bf16[512,512]{1,0:T(8,128)(2,1)S(1)}, bf16[512,512]{1,0:T(8,128)(2,1)S(1)}, u32[]{:S(2)}, u32[]{:S(2)}) collective-permute-start(bf16[512,512]{1,0:T(8,128)(2,1)S(1)} %bitcast.51), channel_id=1, source_target_pairs={{0,8},{8,16},{16,24},{24,0},{1,9},{9,17},{17,25},{25,1},{2,10},{10... | collective-permute-start | bytes 1572872 | tf_op jit(solution)/shard_map/ppermute | solution.py:44
  56.1 26.6 %collective-permute-start.9 = (bf16[512,512]{1,0:T(8,128)(2,1)S(1)}, bf16[512,512]{1,0:T(8,128)(2,1)S(1)}, u32[]{:S(2)}, u32[]{:S(2)}) collective-permute-start(bf16[512,512]{1,0:T(8,128)(2,1)S(1)} %bitcast.52), channel_id=1, source_target_pairs={{0,24},{8,0},{16,8},{24,16},{1,25},{9,1},{17,9},{25,17},{2,26},{10... | collective-permute-start | bytes 1572872 | tf_op jit(solution)/shard_map/ppermute | solution.py:44
  82.6 13.5 %collective-permute-start.16 = (bf16[512,512]{1,0:T(8,128)(2,1)S(1)}, bf16[512,512]{1,0:T(8,128)(2,1)S(1)}, u32[]{:S(2)}, u32[]{:S(2)}) collective-permute-start(bf16[512,512]{1,0:T(8,128)(2,1)S(1)} %get-tuple-element.37), channel_id=1, source_target_pairs={{0,4},{1,5},{2,6},{3,7},{4,0},{5,1},{6,2},{7,3},{8,12},{9,13},{10,... | collective-permute-start | bytes 1572872 | tf_op jit(solution)/shard_map/ppermute | solution.py:40
  83.1 13.2 %collective-permute-start.17 = (bf16[512,512]{1,0:T(8,128)(2,1)S(1)}, bf16[512,512]{1,0:T(8,128)(2,1)S(1)}, u32[]{:S(2)}, u32[]{:S(2)}) collective-permute-start(bf16[512,512]{1,0:T(8,128)(2,1)S(1)} %get-tuple-element.38), channel_id=1, source_target_pairs={{0,2},{1,3},{2,0},{3,1},{4,6},{5,7},{6,4},{7,5},{8,10},{9,11},{10,... | collective-permute-start | bytes 1572872 | tf_op jit(solution)/shard_map/ppermute | solution.py:40
  85.5 14.4 %collective-permute-start.15 = (bf16[512,512]{1,0:T(8,128)(2,1)S(1)}, bf16[512,512]{1,0:T(8,128)(2,1)}, u32[]{:S(2)}, u32[]{:S(2)}) collective-permute-start(bf16[512,512]{1,0:T(8,128)(2,1)S(1)} %collective-permute-done.9), channel_id=1, source_target_pairs={{0,24},{8,0},{16,8},{24,16},{1,25},{9,1},{17,9},{25,17},{2,26},{10... | collective-permute-start | bytes 1572872 | tf_op jit(solution)/shard_map/ppermute | solution.py:44
  101.3 25.6 %collective-permute-start.19 = (bf16[1024,512]{1,0:T(8,128)(2,1)S(1)}, bf16[1024,512]{1,0:T(8,128)(2,1)S(1)}, u32[]{:S(2)}, u32[]{:S(2)}) collective-permute-start(bf16[1024,512]{1,0:T(8,128)(2,1)S(1)} %pad_maximum_fusion.15), channel_id=1, source_target_pairs={{0,2},{1,3},{2,0},{3,1},{4,6},{5,7},{6,4},{7,5},{8,10},{9,11},{10,... | collective-permute-start | bytes 3145736 | tf_op jit(solution)/shard_map/ppermute | solution.py:40
  102.8 25.3 %collective-permute-start.18 = (bf16[1024,512]{1,0:T(8,128)(2,1)S(1)}, bf16[1024,512]{1,0:T(8,128)(2,1)S(1)}, u32[]{:S(2)}, u32[]{:S(2)}) collective-permute-start(bf16[1024,512]{1,0:T(8,128)(2,1)S(1)} %pad_maximum_fusion.15), channel_id=1, source_target_pairs={{0,4},{1,5},{2,6},{3,7},{4,0},{5,1},{6,2},{7,3},{8,12},{9,13},{10,... | collective-permute-start | bytes 3145736 | tf_op jit(solution)/shard_map/ppermute | solution.py:40
  107.7 20.5 %collective-permute-start.20 = (f32[512,512]{1,0:T(8,128)S(1)}, f32[512,512]{1,0:T(8,128)S(1)}, u32[]{:S(2)}, u32[]{:S(2)}) collective-permute-start(f32[512,512]{1,0:T(8,128)S(1)} %fusion.19), channel_id=1, source_target_pairs={{0,1},{1,0},{2,3},{3,2},{4,5},{5,4},{6,7},{7,6},{8,9},{9,8},{10,11... | collective-permute-start | bytes 3145736 | tf_op jit(solution)/shard_map/ppermute | solution.py:40
  110.4 17.8 %collective-permute-start.22 = (bf16[512,512]{1,0:T(8,128)(2,1)S(1)}, bf16[512,512]{1,0:T(8,128)(2,1)S(1)}, u32[]{:S(2)}, u32[]{:S(2)}) collective-permute-start(bf16[512,512]{1,0:T(8,128)(2,1)S(1)} %fusion.4), channel_id=1, source_target_pairs={{0,8},{8,16},{16,24},{24,0},{1,9},{9,17},{17,25},{25,1},{2,10},{10... | collective-permute-start | bytes 1572872 | tf_op jit(solution)/shard_map/ppermute | solution.py:44
  129.5 13.3 %collective-permute-start.23 = (bf16[512,512]{1,0:T(8,128)(2,1)S(1)}, bf16[512,512]{1,0:T(8,128)(2,1)S(1)}, u32[]{:S(2)}, u32[]{:S(2)}) collective-permute-start(bf16[512,512]{1,0:T(8,128)(2,1)S(1)} %get-tuple-element.42), channel_id=1, source_target_pairs={{0,4},{1,5},{2,6},{3,7},{4,0},{5,1},{6,2},{7,3},{8,12},{9,13},{10,... | collective-permute-start | bytes 1572872 | tf_op jit(solution)/shard_map/ppermute | solution.py:40
  145.2 15.6 %collective-permute-start.29 = (f32[512,512]{1,0:T(8,128)S(1)}, f32[512,512]{1,0:T(8,128)S(1)}, u32[]{:S(2)}, u32[]{:S(2)}) collective-permute-start(f32[512,512]{1,0:T(8,128)S(1)} %fusion.16), channel_id=1, source_target_pairs={{0,1},{1,0},{2,3},{3,2},{4,5},{5,4},{6,7},{7,6},{8,9},{9,8},{10,11... | collective-permute-start | bytes 3145736 | tf_op jit(solution)/shard_map/ppermute | solution.py:40
  145.3 14.3 %collective-permute-start.25 = (bf16[512,512]{1,0:T(8,128)(2,1)S(1)}, bf16[512,512]{1,0:T(8,128)(2,1)S(1)}, u32[]{:S(2)}, u32[]{:S(2)}) collective-permute-start(bf16[512,512]{1,0:T(8,128)(2,1)S(1)} %broadcast_select_fusion), channel_id=1, source_target_pairs={{0,8},{8,16},{16,24},{24,0},{1,9},{9,17},{17,25},{25,1},{2,10},{10... | collective-permute-start | bytes 1572872 | tf_op jit(solution)/shard_map/ppermute | solution.py:44
  147.1 16.6 %collective-permute-start.28 = (f32[512,512]{1,0:T(8,128)S(1)}, f32[512,512]{1,0:T(8,128)S(1)}, u32[]{:S(2)}, u32[]{:S(2)}) collective-permute-start(f32[512,512]{1,0:T(8,128)S(1)} %fusion.17), channel_id=1, source_target_pairs={{0,1},{1,0},{2,3},{3,2},{4,5},{5,4},{6,7},{7,6},{8,9},{9,8},{10,11... | collective-permute-start | bytes 3145736 | tf_op jit(solution)/shard_map/ppermute | solution.py:40
  159.6 24.7 %collective-permute-start.27 = (bf16[1024,512]{1,0:T(8,128)(2,1)S(1)}, bf16[1024,512]{1,0:T(8,128)(2,1)S(1)}, u32[]{:S(2)}, u32[]{:S(2)}) collective-permute-start(bf16[1024,512]{1,0:T(8,128)(2,1)S(1)} %pad_maximum_fusion.13), channel_id=1, source_target_pairs={{0,4},{1,5},{2,6},{3,7},{4,0},{5,1},{6,2},{7,3},{8,12},{9,13},{10,... | collective-permute-start | bytes 3145736 | tf_op jit(solution)/shard_map/ppermute | solution.py:40
  160.1 25.1 %collective-permute-start.26 = (bf16[1024,512]{1,0:T(8,128)(2,1)S(1)}, bf16[1024,512]{1,0:T(8,128)(2,1)S(1)}, u32[]{:S(2)}, u32[]{:S(2)}) collective-permute-start(bf16[1024,512]{1,0:T(8,128)(2,1)S(1)} %pad_maximum_fusion.13), channel_id=1, source_target_pairs={{0,2},{1,3},{2,0},{3,1},{4,6},{5,7},{6,4},{7,5},{8,10},{9,11},{10,... | collective-permute-start | bytes 3145736 | tf_op jit(solution)/shard_map/ppermute | solution.py:40
  163.0 30.8 %collective-permute-start.36 = (bf16[512,512]{1,0:T(8,128)(2,1)}, bf16[512,512]{1,0:T(8,128)(2,1)}, u32[]{:S(2)}, u32[]{:S(2)}) collective-permute-start(bf16[512,512]{1,0:T(8,128)(2,1)} %fusion.6), channel_id=1, source_target_pairs={{0,8},{8,16},{16,24},{24,0},{1,9},{9,17},{17,25},{25,1},{2,10},{10... | collective-permute-start | bytes 1572872 | tf_op jit(solution)/shard_map/ppermute | solution.py:44
  164.9 25.3 %collective-permute-start.30 = (bf16[512,512]{1,0:T(8,128)(2,1)S(1)}, bf16[512,512]{1,0:T(8,128)(2,1)S(1)}, u32[]{:S(2)}, u32[]{:S(2)}) collective-permute-start(bf16[512,512]{1,0:T(8,128)(2,1)S(1)} %fusion.5), channel_id=1, source_target_pairs={{0,24},{8,0},{16,8},{24,16},{1,25},{9,1},{17,9},{25,17},{2,26},{10... | collective-permute-start | bytes 1572872 | tf_op jit(solution)/shard_map/ppermute | solution.py:44
  216.8 14.5 %collective-permute-start.37 = (bf16[512,512]{1,0:T(8,128)(2,1)}, bf16[512,512]{1,0:T(8,128)(2,1)S(1)}, u32[]{:S(2)}, u32[]{:S(2)}) collective-permute-start(bf16[512,512]{1,0:T(8,128)(2,1)} %fusion.9), channel_id=1, source_target_pairs={{0,8},{8,16},{16,24},{24,0},{1,9},{9,17},{17,25},{25,1},{2,10},{10... | collective-permute-start | bytes 1572872 | tf_op jit(solution)/shard_map/ppermute | solution.py:44
  220.2 24.0 %collective-permute-start.34 = (bf16[512,512]{1,0:T(8,128)(2,1)S(1)}, bf16[512,512]{1,0:T(8,128)(2,1)S(1)}, u32[]{:S(2)}, u32[]{:S(2)}) collective-permute-start(bf16[512,512]{1,0:T(8,128)(2,1)S(1)} %fusion.7), channel_id=1, source_target_pairs={{0,24},{8,0},{16,8},{24,16},{1,25},{9,1},{17,9},{25,17},{2,26},{10... | collective-permute-start | bytes 1572872 | tf_op jit(solution)/shard_map/ppermute | solution.py:44
  (50 other events, 825.1 us)
Sparse Core Ops, SparseCore 0:
  203.7 37.0 all-gather.1

commit v12 on v11

--- a/solution.py
+++ b/solution.py
@@ -93,44 +93,55 @@
         foreign = jnp.where(behind[side] == n_dp - 1, from_ahead, from_behind)
         return jnp.where(behind[side] == 0, rotated[side, 0], foreign)
 
-    groups = [[(0, 0), (1, 0)], [(0, 1), (0, 2)], [(0, 3), (1, 2)], [(1, 1), (1, 3)]]
-    due = []
-    evens = []
-    for at, group in enumerate(groups):
-        gate = due
-        stack = after(jnp.concatenate([pieces[key] for key in group], axis=0), gate)
-        x, y = swap(stack, X), swap(stack, Y)
-        due = [x, y]
+    groups = [[(0, 0), (1, 0)], [(0, 1), (0, 2)], [(0, 3), (1, 3)], [(1, 1), (1, 2)]]
+    first, second = slice(0, tokens), slice(tokens, 2 * tokens)
+
+    def slot(at, gate):
+        to_x, to_y = [], []
         if at:
-            due += rotate(groups[at - 1], evens)
-        if at < 2:
-            due += [fetch(at, 1, gate), fetch(at, 3, gate)]
-        if at == 2:
-            passed_in = pass_on(0)
-            due.append(passed_in)
-        if at == 3:
-            in_from_ahead = send_behind(0)
-            passed_out = pass_on(1)
-            due.append(in_from_ahead)
-        gate = due
-        to_x, to_y = after((y[tokens:], x[:tokens]), gate)
-        xy = [swap(to_y, Y), swap(to_x, X)]
-        due = list(xy)
-        if at < 2:
-            due.append(fetch(at, 2, gate))
-        if at == 2:
-            in_from_behind = send_ahead(0, passed_in, gate)
-            due.append(in_from_behind)
-        if at == 3:
-            due.append(passed_out)
-        xy = after(xy, [])
-        rows = [slice(0, tokens), slice(tokens, None)]
-        evens = [jnp.concatenate([stack[r], x[r], y[r], last], axis=1) for r, last in zip(rows, xy)]
+            stack, x, y = stacks[at - 1]
+            to_x.append(y[second])
+            to_y.append(x[first])
+        if at < len(groups):
+            new = jnp.concatenate([pieces[key] for key in groups[at]], axis=0)
+            to_x.append(new)
+            to_y.append(new)
+        to_x, to_y = after((jnp.concatenate(to_x, axis=0), jnp.concatenate(to_y, axis=0)), gate)
+        got = [swap(to_x, X), swap(to_y, Y)]
+        from_x, from_y = after(got, [])
+        if at:
+            evens[at - 1] = [
+                jnp.concatenate([stack[first], x[first], y[first], from_y[:tokens]], axis=1),
+                jnp.concatenate([stack[second], x[second], y[second], from_x[:tokens]], axis=1),
+            ]
+        if at < len(groups):
+            stacks[at] = (new, from_x[-2 * tokens :], from_y[-2 * tokens :])
+        return got
 
-    rot_in = after(keep(0, in_from_behind, in_from_ahead), due)
+    stacks, evens = {}, {}
+    due = slot(0, [])
+    due += [fetch(0, 1, []), fetch(0, 2, [])]
+
+    gate, due = due, slot(1, due)
+    due += [fetch(0, 3, gate), fetch(1, 3, gate), fetch(1, 1, gate)]
+
+    gate, due = due, slot(2, due)
+    due += [fetch(1, 2, gate)] + rotate(groups[0], evens[0])
+
+    gate, due = due, slot(3, due)
+    due += rotate(groups[1], evens[1])
+    passed_in = pass_on(0)
+    due.append(passed_in)
+
+    gate, due = due, slot(4, due)
+    due += rotate(groups[2], evens[2])
+    in_from_behind = send_ahead(0, passed_in, gate)
+    rot_in = after(keep(0, in_from_behind, send_behind(0)), due)
     all_rot_in = lax.all_gather(rot_in, "tensor", axis=1, tiled=True)
-    rotate(groups[-1], evens)
-    rot_out = keep(1, send_ahead(1, passed_out, []), send_behind(1))
+
+    out_from_ahead = send_behind(1)
+    rotate(groups[3], evens[3])
+    rot_out = keep(1, send_ahead(1, pass_on(1), []), out_from_ahead)
     return product_and_divide(rot_out, all_rot_in, eig_lambda, tokens)
 
 

time: 264 us -> 283 us (1.072)
  waiting for transfers between devices: 158 us -> 167 us
  local copies, waits for them, and re-layouts: 10.3 us -> 16.4 us
    ppermute x12, starting transfers between devices: 10.6 us -> 19.7 us  [shift(): return lax.ppermute(block, 'dp', [(z, (z + by) % n) for z in range(n)])]
    ppermute x26 -> x20, starting transfers between devices: 17.6 us -> 11.1 us  [swap(): lax.ppermute(block, 'tensor', [(j, j ^ bit) for j in range(X + Y + CORE +...]
    slice x12 -> x7, local copies, waits for them, and re-layouts: 3.48 us -> 9.42 us  [the longest x4 4.95 us: slot(): x[second]]
    ppermute x12, waiting for transfers between devices: 70.6 us -> 75.4 us  [shift(): return lax.ppermute(block, 'dp', [(z, (z + by) % n) for z in range(n)])]
    ppermute x26 -> x20, waiting for transfers between devices: 87.3 us -> 91.5 us  [swap(): lax.ppermute(block, 'tensor', [(j, j ^ bit) for j in range(X + Y + CORE +...]
  transfers between devices with their start and end apart: 39 -> 33, of which waited for: 21 -> 15; matrix products, arithmetic and copies ran while one was open for 16% -> 19% of each run, Pallas kernels for 0% -> 0%
where the time goes in v12:
time: 283 us; the launch traced here: 279 us
  waiting for transfers between devices  167 us (59%)
  matrix products  44.2 us (16%)
  starting transfers between devices  30.8 us (11%)
  local copies, waits for them, and re-layouts  16.4 us (6%)
  between operations  15.4 us (5%)
  other arithmetic  4.77 us (2%)
    ppermute x20, waiting for transfers between devices, swap(): lax.ppermute(block, 'tensor', [(j, j ^ bit) for j in range(X + Y + CORE +...  91.5 us
    ppermute x12, waiting for transfers between devices, shift(): return lax.ppermute(block, 'dp', [(z, (z + by) % n) for z in range(n)])  75.4 us
    dot_general x16, matrix products, dot(): return jnp.dot(a, b, preferred_element_type=jnp.float32)  35.6 us
    ppermute x12, starting transfers between devices, shift(): return lax.ppermute(block, 'dp', [(z, (z + by) % n) for z in range(n)])  19.7 us
    ppermute x20, starting transfers between devices, swap(): lax.ppermute(block, 'tensor', [(j, j ^ bit) for j in range(X + Y + CORE +...  11.1 us
    dot_general x1, matrix products, product_and_divide(): lax.dot_general(rot_out, all_rot_in, contract, preferred_element_type=jnp...  8.67 us
  transfers between devices with their start and end apart: 33, of which 15 were waited for; matrix products, arithmetic and copies ran while one was open for 19% of the time, Pallas kernels for 0%

profile of v12, /device:TPU:16, one launch (start us, length us, event | category | flops | bytes accessed | tf_op | source)
XLA Modules:
  0.0 278.5 jit_solution(9093421317908748043)
XLA Ops:
  11.3 2.4 dynamic-slice_bitcast_fusion.15
  13.8 10.4 %collective-permute-done.2 = bf16[512,512]{1,0:T(8,128)(2,1)S(1)} collective-permute-done((bf16[512,512]{1,0:T(8,128)(2,1)}, bf16[512,512]{1,0:T(8,128)(2,1)S(1)}, u32[]{:S(2)}, u32[]{:S(2)}) %collective-permute-start.2) | collective-permute-done | bytes 524320 | tf_op jit(solution)/shard_map/ppermute | solution.py:44
  24.9 7.9 %collective-permute-done = bf16[1024,512]{1,0:T(8,128)(2,1)S(1)} collective-permute-done((bf16[1024,512]{1,0:T(8,128)(2,1)S(1)}, bf16[1024,512]{1,0:T(8,128)(2,1)S(1)}, u32[]{:S(2)}, u32[]{:S(2)}) %collective-permute-start) | collective-permute-done | bytes 1048608 | tf_op jit(solution)/shard_map/ppermute | solution.py:40
  35.5 2.5 collective-permute-done.3
  41.1 3.5 %collective-permute-start.8 = (bf16[512,512]{1,0:T(8,128)(2,1)S(1)}, bf16[512,512]{1,0:T(8,128)(2,1)S(1)}, u32[]{:S(2)}, u32[]{:S(2)}) collective-permute-start(bf16[512,512]{1,0:T(8,128)(2,1)S(1)} %bitcast.48), channel_id=1, source_target_pairs={{0,8},{8,16},{16,24},{24,0},{1,9},{9,17},{17,25},{25,1},{2,10},{10... | collective-permute-start | bytes 1572872 | tf_op jit(solution)/shard_map/ppermute | solution.py:44
  44.7 27.6 %collective-permute-done.4 = bf16[1536,512]{1,0:T(8,128)(2,1)S(1)} collective-permute-done((bf16[1536,512]{1,0:T(8,128)(2,1)S(1)}, bf16[1536,512]{1,0:T(8,128)(2,1)S(1)}, u32[]{:S(2)}, u32[]{:S(2)}) %collective-permute-start.4) | collective-permute-done | bytes 1572896 | tf_op jit(solution)/shard_map/ppermute | solution.py:40
  72.6 3.3 %collective-permute-start.9 = (bf16[512,512]{1,0:T(8,128)(2,1)S(1)}, bf16[512,512]{1,0:T(8,128)(2,1)S(1)}, u32[]{:S(2)}, u32[]{:S(2)}) collective-permute-start(bf16[512,512]{1,0:T(8,128)(2,1)S(1)} %bitcast.54), channel_id=1, source_target_pairs={{0,8},{8,16},{16,24},{24,0},{1,9},{9,17},{17,25},{25,1},{2,10},{10... | collective-permute-start | bytes 1572872 | tf_op jit(solution)/shard_map/ppermute | solution.py:44
  80.1 14.6 %collective-permute-done.9 = bf16[512,512]{1,0:T(8,128)(2,1)S(1)} collective-permute-done((bf16[512,512]{1,0:T(8,128)(2,1)S(1)}, bf16[512,512]{1,0:T(8,128)(2,1)S(1)}, u32[]{:S(2)}, u32[]{:S(2)}) %collective-permute-start.9) | collective-permute-done | bytes 524320 | tf_op jit(solution)/shard_map/ppermute | solution.py:44
  97.4 2.5 collective-permute-start.13
  99.9 2.0 add_convert_fusion.1
  102.0 2.1 add_convert_fusion
  104.1 26.4 %collective-permute-done.11 = bf16[1536,512]{1,0:T(8,128)(2,1)S(1)} collective-permute-done((bf16[1536,512]{1,0:T(8,128)(2,1)S(1)}, bf16[1536,512]{1,0:T(8,128)(2,1)S(1)}, u32[]{:S(2)}, u32[]{:S(2)}) %collective-permute-start.11) | collective-permute-done | bytes 1572896 | tf_op jit(solution)/shard_map/ppermute | solution.py:40
  132.9 2.2 fusion.15
  137.0 2.0 pad_maximum_fusion.20
  141.1 3.3 %fusion.16 = f32[512,512]{1,0:T(8,128)S(1)} fusion(bf16[2048,512]{1,0:T(8,128)(2,1)} %copy-done.46, bf16[512,512]{1,0:T(8,128)(2,1)} %get-tuple-element.86, bf16[512,512]{1,0:T(8,128)(2,1)} %get-tuple-element.83, bf16[512,512]{1,0:T(8,128)(2,1)S(1)} %get-tuple-element.81, bf16[512,512]{1,0:T(8,128)(2,1)S(1)} %collective-permute-done.2), kind=kOutput, calls=%fused_computation.68 | convolution fusion | flops 1082130432 | bytes 5242880 | tf_op jit(solution)/shard_map/dot_general | solution.py:22
  144.6 2.5 fusion.3
  147.1 2.5 collective-permute-start.22
  149.6 26.5 %collective-permute-done.16 = bf16[1536,512]{1,0:T(8,128)(2,1)} collective-permute-done((bf16[1536,512]{1,0:T(8,128)(2,1)}, bf16[1536,512]{1,0:T(8,128)(2,1)}, u32[]{:S(2)}, u32[]{:S(2)}) %collective-permute-start.16) | collective-permute-done | bytes 1572896 | tf_op jit(solution)/shard_map/ppermute | solution.py:40
  176.1 2.4 fusion.38
  179.8 2.6 fusion.39
  187.9 2.5 collective-permute-start.31
  191.9 2.1 fusion.1
  194.0 18.4 %collective-permute-done.31 = bf16[512,512]{1,0:T(8,128)(2,1)S(1)} collective-permute-done((bf16[512,512]{1,0:T(8,128)(2,1)S(1)}, bf16[512,512]{1,0:T(8,128)(2,1)S(1)}, u32[]{:S(2)}, u32[]{:S(2)}) %collective-permute-start.31) | collective-permute-done | bytes 524320 | tf_op jit(solution)/shard_map/ppermute | solution.py:44
  214.9 3.3 %fusion.13 = f32[512,512]{1,0:T(8,128)S(1)} fusion(bf16[2048,512]{1,0:T(8,128)(2,1)} %copy-done.43, bf16[512,512]{1,0:T(8,128)(2,1)} %collective-permute-done.23, bf16[512,512]{1,0:T(8,128)(2,1)} %get-tuple-element.49, bf16[512,512]{1,0:T(8,128)(2,1)S(1)} %copy-done.19, bf16[512,512]{1,0:T(8,128)(2,1)S(1)} %copy-done.4), kind=kOutput, calls=%fused_computation.65 | convolution fusion | flops 1082130432 | bytes 5242880 | tf_op jit(solution)/shard_map/dot_general | solution.py:22
  218.4 3.4 %fusion.14 = f32[512,512]{1,0:T(8,128)} fusion(bf16[2048,512]{1,0:T(8,128)(2,1)S(1)} %copy-done.45, bf16[512,512]{1,0:T(8,128)(2,1)S(1)} %copy-done.49, bf16[512,512]{1,0:T(8,128)(2,1)S(1)} %copy-done.13, bf16[512,512]{1,0:T(8,128)(2,1)} %get-tuple-element.50, bf16[512,512]{1,0:T(8,128)(2,1)S(1)} %collective-permute-done.10), kind=kOutput, calls=%fused_computation.66 | convolution fusion | flops 1082130432 | bytes 5242880 | tf_op jit(solution)/shard_map/dot_general | solution.py:22
  222.3 3.3 %fusion.5 = bf16[512,512]{1,0:T(8,128)(2,1)} fusion(f32[512,512]{1,0:T(8,128)S(1)} %collective-permute-done.26, bf16[512,512]{1,0:T(8,128)(2,1)} %collective-permute-done.23, bf16[512,512]{1,0:T(8,128)(2,1)} %get-tuple-element.49, bf16[512,512]{1,0:T(8,128)(2,1)S(1)} %copy-done.19, bf16[512,512]{1,0:T(8,128)(2,1)S(1)} %copy-done.4, ...), kind=kOutput, calls=%fused_computation.36 | convolution fusion | flops 1091043328 | bytes 5767168 | tf_op jit(solution)/shard_map/dot_general | solution.py:22
  228.3 11.4 %collective-permute-done.27 = bf16[512,512]{1,0:T(8,128)(2,1)S(1)} collective-permute-done((bf16[512,512]{1,0:T(8,128)(2,1)}, bf16[512,512]{1,0:T(8,128)(2,1)S(1)}, u32[]{:S(2)}, u32[]{:S(2)}) %collective-permute-start.27) | collective-permute-done | bytes 524320 | tf_op jit(solution)/shard_map/ppermute | solution.py:44
  239.7 3.9 %fusion.7 = bf16[512,512]{1,0:T(8,128)(2,1)} fusion(bf16[512,512]{1,0:T(8,128)(2,1)S(1)} %collective-permute-done.27, f32[512,512]{1,0:T(8,128)} %collective-permute-done.25, pred[]{:T(512)S(6)} %eq.17, bf16[512,512]{1,0:T(8,128)(2,1)} %copy-done.48, bf16[512,512]{1,0:T(8,128)(2,1)S(1)} %copy-done.13, bf16[512,512]{1,0:T(8,128)(2,1)} %get-tuple-element.50, ...), kind=kOutput, calls=%fused_computation.38 | convolution fusion | flops 1091305472 | bytes 6291457 | tf_op jit(solution)/shard_map/dot_general | solution.py:22
  243.6 2.2 collective-permute-start.28
  245.8 7.7 %collective-permute-done.19 = bf16[512,512]{1,0:T(8,128)(2,1)S(1)} collective-permute-done((bf16[512,512]{1,0:T(8,128)(2,1)}, bf16[512,512]{1,0:T(8,128)(2,1)S(1)}, u32[]{:S(2)}, u32[]{:S(2)}) %collective-permute-start.19) | collective-permute-done | bytes 524320 | tf_op jit(solution)/shard_map/ppermute | solution.py:44
  253.5 9.5 %collective-permute-done.28 = bf16[512,512]{1,0:T(8,128)(2,1)S(1)} collective-permute-done((bf16[512,512]{1,0:T(8,128)(2,1)}, bf16[512,512]{1,0:T(8,128)(2,1)S(1)}, u32[]{:S(2)}, u32[]{:S(2)}) %collective-permute-start.28) | collective-permute-done | bytes 524320 | tf_op jit(solution)/shard_map/ppermute | solution.py:44
  263.0 8.7 %fusion = bf16[1,512,4096]{2,1,0:T(8,128)(2,1)} fusion(bf16[512,4096]{1,0:T(8,128)(2,1)} %param.11, bf16[512,4096]{1,0:T(8,128)(2,1)} %all-gather.2.cloned.1.call-done, bf16[512,512]{1,0:T(8,128)(2,1)} %add_convert_fusion.1, bf16[512,512]{1,0:T(8,128)(2,1)S(1)} %collective-permute-done.19, bf16[512,512]{1,0:T(8,128)(2,1)S(1)} %collective-permute-done.28, ...), kind=kOutput, calls=%fused_computation.1 | convolution fusion | flops 2158493696 | bytes 14155778 | tf_op jit(solution)/shard_map/dot_general | solution.py:13
  (169 shorter events, 37.5 us)
Async XLA Ops:
  6.5 256.5 %all-gather.2.cloned.1.call-start = ((), (), s32[]{:S(2)}) async-start(), calls=%async_computation | async-start | bytes 4718592 | tf_op jit(solution)/shard_map/all_gather | solution.py:140
  7.8 25.0 %collective-permute-start = (bf16[1024,512]{1,0:T(8,128)(2,1)S(1)}, bf16[1024,512]{1,0:T(8,128)(2,1)S(1)}, u32[]{:S(2)}, u32[]{:S(2)}) collective-permute-start(bf16[1024,512]{1,0:T(8,128)(2,1)S(1)} %pad_maximum_fusion.24), channel_id=1, source_target_pairs={{0,2},{1,3},{2,0},{3,1},{4,6},{5,7},{6,4},{7,5},{8,10},{9,11},{10,... | collective-permute-start | bytes 3145736 | tf_op jit(solution)/shard_map/ppermute | solution.py:40
  9.4 24.7 %collective-permute-start.1 = (bf16[1024,512]{1,0:T(8,128)(2,1)S(1)}, bf16[1024,512]{1,0:T(8,128)(2,1)}, u32[]{:S(2)}, u32[]{:S(2)}) collective-permute-start(bf16[1024,512]{1,0:T(8,128)(2,1)S(1)} %pad_maximum_fusion.24), channel_id=1, source_target_pairs={{0,4},{1,5},{2,6},{3,7},{4,0},{5,1},{6,2},{7,3},{8,12},{9,13},{10,... | collective-permute-start | bytes 3145736 | tf_op jit(solution)/shard_map/ppermute | solution.py:40
  10.9 13.3 %collective-permute-start.2 = (bf16[512,512]{1,0:T(8,128)(2,1)}, bf16[512,512]{1,0:T(8,128)(2,1)S(1)}, u32[]{:S(2)}, u32[]{:S(2)}) collective-permute-start(bf16[512,512]{1,0:T(8,128)(2,1)} %bitcast.53), channel_id=1, source_target_pairs={{0,24},{8,0},{16,8},{24,16},{1,25},{9,1},{17,9},{25,17},{2,26},{10... | collective-permute-start | bytes 1572872 | tf_op jit(solution)/shard_map/ppermute | solution.py:44
  24.2 13.8 %collective-permute-start.3 = (bf16[512,512]{1,0:T(8,128)(2,1)S(1)}, bf16[512,512]{1,0:T(8,128)(2,1)S(1)}, u32[]{:S(2)}, u32[]{:S(2)}) collective-permute-start(bf16[512,512]{1,0:T(8,128)(2,1)S(1)} %collective-permute-done.2), channel_id=1, source_target_pairs={{0,24},{8,0},{16,8},{24,16},{1,25},{9,1},{17,9},{25,17},{2,26},{10... | collective-permute-start | bytes 1572872 | tf_op jit(solution)/shard_map/ppermute | solution.py:44
  24.8 51.2 %collective-permute-start.6 = (bf16[2048,512]{1,0:T(8,128)(2,1)S(1)}, bf16[2048,512]{1,0:T(8,128)(2,1)S(1)}, u32[]{:S(2)}, u32[]{:S(2)}) collective-permute-start(bf16[2048,512]{1,0:T(8,128)(2,1)S(1)} %pad_maximum_fusion.2), channel_id=1, source_target_pairs={{0,1},{1,0},{2,3},{3,2},{4,5},{5,4},{6,7},{7,6},{8,9},{9,8},{10,11... | collective-permute-start | bytes 6291464 | tf_op jit(solution)/shard_map/ppermute | solution.py:40
  38.2 34.1 %collective-permute-start.4 = (bf16[1536,512]{1,0:T(8,128)(2,1)S(1)}, bf16[1536,512]{1,0:T(8,128)(2,1)S(1)}, u32[]{:S(2)}, u32[]{:S(2)}) collective-permute-start(bf16[1536,512]{1,0:T(8,128)(2,1)S(1)} %get-tuple-element.34), channel_id=1, source_target_pairs={{0,2},{1,3},{2,0},{3,1},{4,6},{5,7},{6,4},{7,5},{8,10},{9,11},{10,... | collective-permute-start | bytes 4718600 | tf_op jit(solution)/shard_map/ppermute | solution.py:40
  38.8 33.7 %collective-permute-start.5 = (bf16[1536,512]{1,0:T(8,128)(2,1)S(1)}, bf16[1536,512]{1,0:T(8,128)(2,1)S(1)}, u32[]{:S(2)}, u32[]{:S(2)}) collective-permute-start(bf16[1536,512]{1,0:T(8,128)(2,1)S(1)} %get-tuple-element.35), channel_id=1, source_target_pairs={{0,4},{1,5},{2,6},{3,7},{4,0},{5,1},{6,2},{7,3},{8,12},{9,13},{10,... | collective-permute-start | bytes 4718600 | tf_op jit(solution)/shard_map/ppermute | solution.py:40
  39.9 38.4 %collective-permute-start.14 = (bf16[2048,512]{1,0:T(8,128)(2,1)S(1)}, bf16[2048,512]{1,0:T(8,128)(2,1)S(1)}, u32[]{:S(2)}, u32[]{:S(2)}) collective-permute-start(bf16[2048,512]{1,0:T(8,128)(2,1)S(1)} %pad_maximum_fusion.5), channel_id=1, source_target_pairs={{0,1},{1,0},{2,3},{3,2},{4,5},{5,4},{6,7},{7,6},{8,9},{9,8},{10,11... | collective-permute-start | bytes 6291464 | tf_op jit(solution)/shard_map/ppermute | solution.py:40
  41.1 38.9 %collective-permute-start.8 = (bf16[512,512]{1,0:T(8,128)(2,1)S(1)}, bf16[512,512]{1,0:T(8,128)(2,1)S(1)}, u32[]{:S(2)}, u32[]{:S(2)}) collective-permute-start(bf16[512,512]{1,0:T(8,128)(2,1)S(1)} %bitcast.48), channel_id=1, source_target_pairs={{0,8},{8,16},{16,24},{24,0},{1,9},{9,17},{17,25},{25,1},{2,10},{10... | collective-permute-start | bytes 1572872 | tf_op jit(solution)/shard_map/ppermute | solution.py:44
  72.3 22.6 %collective-permute-start.10 = (bf16[512,512]{1,0:T(8,128)(2,1)S(1)}, bf16[512,512]{1,0:T(8,128)(2,1)S(1)}, u32[]{:S(2)}, u32[]{:S(2)}) collective-permute-start(bf16[512,512]{1,0:T(8,128)(2,1)S(1)} %bitcast.49), channel_id=1, source_target_pairs={{0,24},{8,0},{16,8},{24,16},{1,25},{9,1},{17,9},{25,17},{2,26},{10... | collective-permute-start | bytes 1572872 | tf_op jit(solution)/shard_map/ppermute | solution.py:44
  72.6 22.2 %collective-permute-start.9 = (bf16[512,512]{1,0:T(8,128)(2,1)S(1)}, bf16[512,512]{1,0:T(8,128)(2,1)S(1)}, u32[]{:S(2)}, u32[]{:S(2)}) collective-permute-start(bf16[512,512]{1,0:T(8,128)(2,1)S(1)} %bitcast.54), channel_id=1, source_target_pairs={{0,8},{8,16},{16,24},{24,0},{1,9},{9,17},{17,25},{25,1},{2,10},{10... | collective-permute-start | bytes 1572872 | tf_op jit(solution)/shard_map/ppermute | solution.py:44
  78.2 21.7 %collective-permute-start.7 = (f32[512,512]{1,0:T(8,128)S(1)}, f32[512,512]{1,0:T(8,128)S(1)}, u32[]{:S(2)}, u32[]{:S(2)}) collective-permute-start(f32[512,512]{1,0:T(8,128)S(1)} %fusion.20), channel_id=1, source_target_pairs={{0,1},{1,0},{2,3},{3,2},{4,5},{5,4},{6,7},{7,6},{8,9},{9,8},{10,11... | collective-permute-start | bytes 3145736 | tf_op jit(solution)/shard_map/ppermute | solution.py:40
  79.5 22.5 %collective-permute-start.15 = (f32[512,512]{1,0:T(8,128)S(1)}, f32[512,512]{1,0:T(8,128)S(1)}, u32[]{:S(2)}, u32[]{:S(2)}) collective-permute-start(f32[512,512]{1,0:T(8,128)S(1)} %fusion.18), channel_id=1, source_target_pairs={{0,1},{1,0},{2,3},{3,2},{4,5},{5,4},{6,7},{7,6},{8,9},{9,8},{10,11... | collective-permute-start | bytes 3145736 | tf_op jit(solution)/shard_map/ppermute | solution.py:40
  95.5 35.0 %collective-permute-start.11 = (bf16[1536,512]{1,0:T(8,128)(2,1)S(1)}, bf16[1536,512]{1,0:T(8,128)(2,1)S(1)}, u32[]{:S(2)}, u32[]{:S(2)}) collective-permute-start(bf16[1536,512]{1,0:T(8,128)(2,1)S(1)} %get-tuple-element.40), channel_id=1, source_target_pairs={{0,2},{1,3},{2,0},{3,1},{4,6},{5,7},{6,4},{7,5},{8,10},{9,11},{10,... | collective-permute-start | bytes 4718600 | tf_op jit(solution)/shard_map/ppermute | solution.py:40
  96.9 35.0 %collective-permute-start.12 = (bf16[1536,512]{1,0:T(8,128)(2,1)S(1)}, bf16[1536,512]{1,0:T(8,128)(2,1)S(1)}, u32[]{:S(2)}, u32[]{:S(2)}) collective-permute-start(bf16[1536,512]{1,0:T(8,128)(2,1)S(1)} %get-tuple-element.41), channel_id=1, source_target_pairs={{0,4},{1,5},{2,6},{3,7},{4,0},{5,1},{6,2},{7,3},{8,12},{9,13},{10,... | collective-permute-start | bytes 4718600 | tf_op jit(solution)/shard_map/ppermute | solution.py:40
  97.4 38.8 %collective-permute-start.13 = (bf16[512,512]{1,0:T(8,128)(2,1)S(1)}, bf16[512,512]{1,0:T(8,128)(2,1)S(1)}, u32[]{:S(2)}, u32[]{:S(2)}) collective-permute-start(bf16[512,512]{1,0:T(8,128)(2,1)S(1)} %collective-permute-done.10), channel_id=1, source_target_pairs={{0,24},{8,0},{16,8},{24,16},{1,25},{9,1},{17,9},{25,17},{2,26},{10... | collective-permute-start | bytes 1572872 | tf_op jit(solution)/shard_map/ppermute | solution.py:44
  135.1 9.4 %collective-permute-start.21 = (f32[512,512]{1,0:T(8,128)}, f32[512,512]{1,0:T(8,128)}, u32[]{:S(2)}, u32[]{:S(2)}) collective-permute-start(f32[512,512]{1,0:T(8,128)} %fusion.15), channel_id=1, source_target_pairs={{0,1},{1,0},{2,3},{3,2},{4,5},{5,4},{6,7},{7,6},{8,9},{9,8},{10,11... | collective-permute-start | bytes 3145736 | tf_op jit(solution)/shard_map/ppermute | solution.py:40
  139.0 37.1 %collective-permute-start.16 = (bf16[1536,512]{1,0:T(8,128)(2,1)}, bf16[1536,512]{1,0:T(8,128)(2,1)}, u32[]{:S(2)}, u32[]{:S(2)}) collective-permute-start(bf16[1536,512]{1,0:T(8,128)(2,1)} %get-tuple-element.45), channel_id=1, source_target_pairs={{0,2},{1,3},{2,0},{3,1},{4,6},{5,7},{6,4},{7,5},{8,10},{9,11},{10,... | collective-permute-start | bytes 4718600 | tf_op jit(solution)/shard_map/ppermute | solution.py:40
  139.2 36.8 %collective-permute-start.17 = (bf16[1536,512]{1,0:T(8,128)(2,1)}, bf16[1536,512]{1,0:T(8,128)(2,1)}, u32[]{:S(2)}, u32[]{:S(2)}) collective-permute-start(bf16[1536,512]{1,0:T(8,128)(2,1)} %get-tuple-element.46), channel_id=1, source_target_pairs={{0,4},{1,5},{2,6},{3,7},{4,0},{5,1},{6,2},{7,3},{8,12},{9,13},{10,... | collective-permute-start | bytes 4718600 | tf_op jit(solution)/shard_map/ppermute | solution.py:40
  144.4 39.8 %collective-permute-start.20 = (f32[512,512]{1,0:T(8,128)S(1)}, f32[512,512]{1,0:T(8,128)S(1)}, u32[]{:S(2)}, u32[]{:S(2)}) collective-permute-start(f32[512,512]{1,0:T(8,128)S(1)} %fusion.16), channel_id=1, source_target_pairs={{0,1},{1,0},{2,3},{3,2},{4,5},{5,4},{6,7},{7,6},{8,9},{9,8},{10,11... | collective-permute-start | bytes 3145736 | tf_op jit(solution)/shard_map/ppermute | solution.py:40
  147.1 37.2 %collective-permute-start.22 = (bf16[512,512]{1,0:T(8,128)(2,1)S(1)}, bf16[512,512]{1,0:T(8,128)(2,1)S(1)}, u32[]{:S(2)}, u32[]{:S(2)}) collective-permute-start(bf16[512,512]{1,0:T(8,128)(2,1)S(1)} %fusion.3), channel_id=1, source_target_pairs={{0,8},{8,16},{16,24},{24,0},{1,9},{9,17},{17,25},{25,1},{2,10},{10... | collective-permute-start | bytes 1572872 | tf_op jit(solution)/shard_map/ppermute | solution.py:44
  182.4 8.0 %collective-permute-start.29 = (f32[512,512]{1,0:T(8,128)S(1)}, f32[512,512]{1,0:T(8,128)S(1)}, u32[]{:S(2)}, u32[]{:S(2)}) collective-permute-start(f32[512,512]{1,0:T(8,128)S(1)} %fusion.12), channel_id=1, source_target_pairs={{0,1},{1,0},{2,3},{3,2},{4,5},{5,4},{6,7},{7,6},{8,9},{9,8},{10,11... | collective-permute-start | bytes 3145736 | tf_op jit(solution)/shard_map/ppermute | solution.py:40
  183.7 8.2 %collective-permute-start.18 = (f32[512,512]{1,0:T(8,128)S(1)}, f32[512,512]{1,0:T(8,128)S(1)}, u32[]{:S(2)}, u32[]{:S(2)}) collective-permute-start(f32[512,512]{1,0:T(8,128)S(1)} %fusion.17), channel_id=1, source_target_pairs={{0,1},{1,0},{2,3},{3,2},{4,5},{5,4},{6,7},{7,6},{8,9},{9,8},{10,11... | collective-permute-start | bytes 3145736 | tf_op jit(solution)/shard_map/ppermute | solution.py:40
  185.6 28.5 %collective-permute-start.23 = (bf16[512,512]{1,0:T(8,128)(2,1)}, bf16[512,512]{1,0:T(8,128)(2,1)}, u32[]{:S(2)}, u32[]{:S(2)}) collective-permute-start(bf16[512,512]{1,0:T(8,128)(2,1)} %get-tuple-element.49), channel_id=1, source_target_pairs={{0,2},{1,3},{2,0},{3,1},{4,6},{5,7},{6,4},{7,5},{8,10},{9,11},{10,... | collective-permute-start | bytes 1572872 | tf_op jit(solution)/shard_map/ppermute | solution.py:40
  187.4 26.7 %collective-permute-start.24 = (bf16[512,512]{1,0:T(8,128)(2,1)}, bf16[512,512]{1,0:T(8,128)(2,1)S(1)}, u32[]{:S(2)}, u32[]{:S(2)}) collective-permute-start(bf16[512,512]{1,0:T(8,128)(2,1)} %get-tuple-element.50), channel_id=1, source_target_pairs={{0,4},{1,5},{2,6},{3,7},{4,0},{5,1},{6,2},{7,3},{8,12},{9,13},{10,... | collective-permute-start | bytes 1572872 | tf_op jit(solution)/shard_map/ppermute | solution.py:40
  187.9 24.5 %collective-permute-start.31 = (bf16[512,512]{1,0:T(8,128)(2,1)S(1)}, bf16[512,512]{1,0:T(8,128)(2,1)S(1)}, u32[]{:S(2)}, u32[]{:S(2)}) collective-permute-start(bf16[512,512]{1,0:T(8,128)(2,1)S(1)} %broadcast_select_fusion), channel_id=1, source_target_pairs={{0,8},{8,16},{16,24},{24,0},{1,9},{9,17},{17,25},{25,1},{2,10},{10... | collective-permute-start | bytes 1572872 | tf_op jit(solution)/shard_map/ppermute | solution.py:44
  191.6 21.6 %collective-permute-start.30 = (bf16[512,512]{1,0:T(8,128)(2,1)S(1)}, bf16[512,512]{1,0:T(8,128)(2,1)S(1)}, u32[]{:S(2)}, u32[]{:S(2)}) collective-permute-start(bf16[512,512]{1,0:T(8,128)(2,1)S(1)} %fusion.6), channel_id=1, source_target_pairs={{0,24},{8,0},{16,8},{24,16},{1,25},{9,1},{17,9},{25,17},{2,26},{10... | collective-permute-start | bytes 1572872 | tf_op jit(solution)/shard_map/ppermute | solution.py:44
  221.8 6.5 %collective-permute-start.25 = (f32[512,512]{1,0:T(8,128)}, f32[512,512]{1,0:T(8,128)}, u32[]{:S(2)}, u32[]{:S(2)}) collective-permute-start(f32[512,512]{1,0:T(8,128)} %fusion.14), channel_id=1, source_target_pairs={{0,1},{1,0},{2,3},{3,2},{4,5},{5,4},{6,7},{7,6},{8,9},{9,8},{10,11... | collective-permute-start | bytes 3145736 | tf_op jit(solution)/shard_map/ppermute | solution.py:40
  225.6 14.1 %collective-permute-start.27 = (bf16[512,512]{1,0:T(8,128)(2,1)}, bf16[512,512]{1,0:T(8,128)(2,1)S(1)}, u32[]{:S(2)}, u32[]{:S(2)}) collective-permute-start(bf16[512,512]{1,0:T(8,128)(2,1)} %fusion.5), channel_id=1, source_target_pairs={{0,8},{8,16},{16,24},{24,0},{1,9},{9,17},{17,25},{25,1},{2,10},{10... | collective-permute-start | bytes 1572872 | tf_op jit(solution)/shard_map/ppermute | solution.py:44
  227.9 25.6 %collective-permute-start.19 = (bf16[512,512]{1,0:T(8,128)(2,1)}, bf16[512,512]{1,0:T(8,128)(2,1)S(1)}, u32[]{:S(2)}, u32[]{:S(2)}) collective-permute-start(bf16[512,512]{1,0:T(8,128)(2,1)} %fusion.1), channel_id=1, source_target_pairs={{0,24},{8,0},{16,8},{24,16},{1,25},{9,1},{17,9},{25,17},{2,26},{10... | collective-permute-start | bytes 1572872 | tf_op jit(solution)/shard_map/ppermute | solution.py:44
  243.6 19.4 %collective-permute-start.28 = (bf16[512,512]{1,0:T(8,128)(2,1)}, bf16[512,512]{1,0:T(8,128)(2,1)S(1)}, u32[]{:S(2)}, u32[]{:S(2)}) collective-permute-start(bf16[512,512]{1,0:T(8,128)(2,1)} %fusion.7), channel_id=1, source_target_pairs={{0,8},{8,16},{16,24},{24,0},{1,9},{9,17},{17,25},{25,1},{2,10},{10... | collective-permute-start | bytes 1572872 | tf_op jit(solution)/shard_map/ppermute | solution.py:44
  (51 other events, 1116.6 us)
Sparse Core Ops, SparseCore 0:
  214.3 37.6 all-gather.1

commit v13 on v12

--- a/solution.py
+++ b/solution.py
@@ -62,8 +62,8 @@
     behind = [(me - owners[side, column]) % n_dp for side in (0, 1)]
     found = [0, X, Y, X + Y]
     held = (basis_in_held[0], basis_out_held[0])
-    theirs = [swap(in_order(block, column, [CORE + i for i in found]), CORE) for block in held]
     ours = [in_order(block, column, found) for block in held]
+    theirs = jnp.split(swap(jnp.concatenate([in_order(block, column, [CORE + i for i in found]) for block in held]), CORE), 2)
 
     pieces = {(0, 0): own[0], (1, 0): own[1]}
     rotated = {}
@@ -93,7 +93,7 @@
         foreign = jnp.where(behind[side] == n_dp - 1, from_ahead, from_behind)
         return jnp.where(behind[side] == 0, rotated[side, 0], foreign)
 
-    groups = [[(0, 0), (1, 0)], [(0, 1), (0, 2)], [(0, 3), (1, 3)], [(1, 1), (1, 2)]]
+    groups = [[(0, 0), (1, 0)], [(0, 1), (0, 2)], [(0, 3), (1, 2)], [(1, 1), (1, 3)]]
     first, second = slice(0, tokens), slice(tokens, 2 * tokens)
 
     def slot(at, gate):
@@ -123,25 +123,28 @@
     due += [fetch(0, 1, []), fetch(0, 2, [])]
 
     gate, due = due, slot(1, due)
-    due += [fetch(0, 3, gate), fetch(1, 3, gate), fetch(1, 1, gate)]
+    due += [fetch(0, 3, gate), fetch(1, 1, gate), fetch(1, 2, gate)]
+
+    def begun(at, gate):
+        corner = after(stacks[at][1][:16, :128], gate)
+        return after(evens[at], swap(corner, CORE))
 
     gate, due = due, slot(2, due)
-    due += [fetch(1, 2, gate)] + rotate(groups[0], evens[0])
+    due += [fetch(1, 3, gate)] + rotate(groups[0], begun(0, gate))
 
     gate, due = due, slot(3, due)
-    due += rotate(groups[1], evens[1])
-    passed_in = pass_on(0)
-    due.append(passed_in)
+    due += rotate(groups[1], begun(1, gate))
+    in_from_behind = send_ahead(0, pass_on(0), [])
+    due.append(in_from_behind)
 
     gate, due = due, slot(4, due)
-    due += rotate(groups[2], evens[2])
-    in_from_behind = send_ahead(0, passed_in, gate)
+    rotate(groups[2], begun(2, gate))
     rot_in = after(keep(0, in_from_behind, send_behind(0)), due)
     all_rot_in = lax.all_gather(rot_in, "tensor", axis=1, tiled=True)
 
-    out_from_ahead = send_behind(1)
+    passed_out = pass_on(1)
     rotate(groups[3], evens[3])
-    rot_out = keep(1, send_ahead(1, pass_on(1), []), out_from_ahead)
+    rot_out = keep(1, send_ahead(1, passed_out, []), send_behind(1))
     return product_and_divide(rot_out, all_rot_in, eig_lambda, tokens)
 
 

time: 283 us -> 291 us (1.028)
  the two profiles are of different devices: /device:TPU:16 before, /device:TPU:0 now
where the time goes in v13:
time: 291 us; the launch traced here: 287 us
  waiting for transfers between devices  135 us (46%)
  matrix products  59.8 us (21%)
  starting transfers between devices  39.6 us (14%)
  local copies, waits for them, and re-layouts  28.6 us (10%)
  between operations  15.3 us (5%)
  other arithmetic  9.61 us (3%)
    ppermute x12, waiting for transfers between devices, shift(): return lax.ppermute(block, 'dp', [(z, (z + by) % n) for z in range(n)])  70.6 us
    ppermute x19, waiting for transfers between devices, swap(): lax.ppermute(block, 'tensor', [(j, j ^ bit) for j in range(X + Y + CORE +...  63.9 us
    dot_general x16, matrix products, dot(): return jnp.dot(a, b, preferred_element_type=jnp.float32)  50.9 us
    ppermute x12, starting transfers between devices, shift(): return lax.ppermute(block, 'dp', [(z, (z + by) % n) for z in range(n)])  26.6 us
    unnamed x73, local copies, waits for them, and re-layouts  16.3 us
    ppermute x19, starting transfers between devices, swap(): lax.ppermute(block, 'tensor', [(j, j ^ bit) for j in range(X + Y + CORE +...  13 us
    dot_general x1, matrix products, product_and_divide(): lax.dot_general(rot_out, all_rot_in, contract, preferred_element_type=jnp...  8.85 us
  transfers between devices with their start and end apart: 32, of which 18 were waited for; matrix products, arithmetic and copies ran while one was open for 29% of the time, Pallas kernels for 0%

profile of v13, /device:TPU:0, one launch (start us, length us, event | category | flops | bytes accessed | tf_op | source)
XLA Modules:
  0.0 287.3 jit_solution(18330679445615600861)
XLA Ops:
  7.8 3.0 %collective-permute-start = (bf16[1024,512]{1,0:T(8,128)(2,1)S(1)}, bf16[1024,512]{1,0:T(8,128)(2,1)}, u32[]{:S(2)}, u32[]{:S(2)}) collective-permute-start(bf16[1024,512]{1,0:T(8,128)(2,1)S(1)} %pad_maximum_fusion.22), channel_id=1, source_target_pairs={{0,2},{1,3},{2,0},{3,1},{4,6},{5,7},{6,4},{7,5},{8,10},{9,11},{10,... | collective-permute-start | bytes 3145736 | tf_op jit(solution)/shard_map/ppermute | solution.py:40
  12.3 3.6 %collective-permute-start.2 = (bf16[512,512]{1,0:T(8,128)(2,1)}, bf16[512,512]{1,0:T(8,128)(2,1)S(1)}, u32[]{:S(2)}, u32[]{:S(2)}) collective-permute-start(bf16[512,512]{1,0:T(8,128)(2,1)} %bitcast.52), channel_id=1, source_target_pairs={{0,24},{8,0},{16,8},{24,16},{1,25},{9,1},{17,9},{25,17},{2,26},{10... | collective-permute-start | bytes 1572872 | tf_op jit(solution)/shard_map/ppermute | solution.py:44
  27.1 3.9 %collective-permute-start.3 = (bf16[512,512]{1,0:T(8,128)(2,1)S(1)}, bf16[512,512]{1,0:T(8,128)(2,1)S(1)}, u32[]{:S(2)}, u32[]{:S(2)}) collective-permute-start(bf16[512,512]{1,0:T(8,128)(2,1)S(1)} %collective-permute-done.2), channel_id=1, source_target_pairs={{0,24},{8,0},{16,8},{24,16},{1,25},{9,1},{17,9},{25,17},{2,26},{10... | collective-permute-start | bytes 1572872 | tf_op jit(solution)/shard_map/ppermute | solution.py:44
  35.5 2.5 fusion.40
  38.1 2.7 collective-permute-done.3
  43.7 4.3 %collective-permute-start.9 = (bf16[512,512]{1,0:T(8,128)(2,1)S(1)}, bf16[512,512]{1,0:T(8,128)(2,1)}, u32[]{:S(2)}, u32[]{:S(2)}) collective-permute-start(bf16[512,512]{1,0:T(8,128)(2,1)S(1)} %bitcast.56), channel_id=1, source_target_pairs={{0,24},{8,0},{16,8},{24,16},{1,25},{9,1},{17,9},{25,17},{2,26},{10... | collective-permute-start | bytes 1572872 | tf_op jit(solution)/shard_map/ppermute | solution.py:44
  52.3 8.1 %collective-permute-done.9 = bf16[512,512]{1,0:T(8,128)(2,1)} collective-permute-done((bf16[512,512]{1,0:T(8,128)(2,1)S(1)}, bf16[512,512]{1,0:T(8,128)(2,1)}, u32[]{:S(2)}, u32[]{:S(2)}) %collective-permute-start.9) | collective-permute-done | bytes 524320 | tf_op jit(solution)/shard_map/ppermute | solution.py:44
  60.4 4.4 %collective-permute-start.10 = (bf16[512,512]{1,0:T(8,128)(2,1)}, bf16[512,512]{1,0:T(8,128)(2,1)S(1)}, u32[]{:S(2)}, u32[]{:S(2)}) collective-permute-start(bf16[512,512]{1,0:T(8,128)(2,1)} %collective-permute-done.9), channel_id=1, source_target_pairs={{0,24},{8,0},{16,8},{24,16},{1,25},{9,1},{17,9},{25,17},{2,26},{10... | collective-permute-start | bytes 1572872 | tf_op jit(solution)/shard_map/ppermute | solution.py:44
  64.8 11.9 %collective-permute-done.4 = bf16[1536,512]{1,0:T(8,128)(2,1)} collective-permute-done((bf16[1536,512]{1,0:T(8,128)(2,1)}, bf16[1536,512]{1,0:T(8,128)(2,1)}, u32[]{:S(2)}, u32[]{:S(2)}) %collective-permute-start.4) | collective-permute-done | bytes 1572896 | tf_op jit(solution)/shard_map/ppermute | solution.py:40
  86.5 2.8 fusion.15
  89.4 2.8 fusion.7
  92.2 20.5 %collective-permute-done.12 = bf16[1536,512]{1,0:T(8,128)(2,1)S(1)} collective-permute-done((bf16[1536,512]{1,0:T(8,128)(2,1)S(1)}, bf16[1536,512]{1,0:T(8,128)(2,1)S(1)}, u32[]{:S(2)}, u32[]{:S(2)}) %collective-permute-start.12) | collective-permute-done | bytes 1572896 | tf_op jit(solution)/shard_map/ppermute | solution.py:40
  118.6 3.6 %fusion.3 = f32[512,512]{1,0:T(8,128)S(1)} fusion(bf16[512,2048]{1,0:T(8,128)(2,1)S(1)} %pad_maximum_fusion.5, bf16[4096,512]{1,0:T(8,128)(2,1)} %collective-permute-done.6), kind=kOutput, calls=%fused_computation.26 | convolution fusion | flops 1073741824 | bytes 5242880 | tf_op jit(solution)/shard_map/dot_general | solution.py:22
  122.2 3.8 %fusion.5 = f32[512,512]{1,0:T(8,128)} fusion(bf16[512,2048]{1,0:T(8,128)(2,1)S(1)} %pad_maximum_fusion.4, bf16[4096,512]{1,0:T(8,128)(2,1)} %collective-permute-done.6), kind=kOutput, calls=%fused_computation.28 | convolution fusion | flops 1073741824 | bytes 5242880 | tf_op jit(solution)/shard_map/dot_general | solution.py:22
  126.5 26.9 %collective-permute-done.15 = bf16[1536,512]{1,0:T(8,128)(2,1)S(1)} collective-permute-done((bf16[1536,512]{1,0:T(8,128)(2,1)S(1)}, bf16[1536,512]{1,0:T(8,128)(2,1)S(1)}, u32[]{:S(2)}, u32[]{:S(2)}) %collective-permute-start.15) | collective-permute-done | bytes 1572896 | tf_op jit(solution)/shard_map/ppermute | solution.py:40
  156.6 4.6 %fusion.1 = f32[512,512]{1,0:T(8,128)} fusion(bf16[512,2048]{1,0:T(8,128)(2,1)S(1)} %pad_maximum_fusion.8, bf16[4096,512]{1,0:T(8,128)(2,1)} %collective-permute-done.6), kind=kOutput, calls=%fused_computation.24 | convolution fusion | flops 1073741824 | bytes 5242880 | tf_op jit(solution)/shard_map/dot_general | solution.py:22
  166.0 3.9 %add_convert_fusion.3 = bf16[512,512]{1,0:T(8,128)(2,1)S(1)} fusion(f32[512,512]{1,0:T(8,128)} %collective-permute-done.17, bf16[512,2048]{1,0:T(8,128)(2,1)} %copy-done.1, bf16[512,512]{1,0:T(8,128)(2,1)} %copy-done.28, bf16[512,512]{1,0:T(8,128)(2,1)} %copy-done.30, bf16[512,512]{1,0:T(8,128)(2,1)} %copy-done.26, bf16[512,512]{1,0:T(8,128)(2,1)} %copy-done.24), kind=kOutput, calls=%fused_computation.49 | convolution fusion | flops 1082654720 | bytes 5767168 | tf_op jit(solution)/shard_map/dot_general | solution.py:22
  169.9 10.5 %collective-permute-done.19 = bf16[512,512]{1,0:T(8,128)(2,1)} collective-permute-done((bf16[512,512]{1,0:T(8,128)(2,1)}, bf16[512,512]{1,0:T(8,128)(2,1)}, u32[]{:S(2)}, u32[]{:S(2)}) %collective-permute-start.19) | collective-permute-done | bytes 524320 | tf_op jit(solution)/shard_map/ppermute | solution.py:44
  180.7 3.3 %add_convert_fusion = bf16[512,512]{1,0:T(8,128)(2,1)} fusion(f32[512,512]{1,0:T(8,128)} %collective-permute-done.29, bf16[512,2048]{1,0:T(8,128)(2,1)S(1)} %copy-done.3, bf16[512,512]{1,0:T(8,128)(2,1)S(1)} %copy-done.29, bf16[512,512]{1,0:T(8,128)(2,1)S(1)} %copy-done.31, bf16[512,512]{1,0:T(8,128)(2,1)S(1)} %copy-done.27, bf16[512,512]{1,0:T(8,128)(2,1)S(1)} %copy-done.25), kind=kOutput, calls=%fused_computation.46 | convolution fusion | flops 1082654720 | bytes 5767168 | tf_op jit(solution)/shard_map/dot_general | solution.py:22
  183.9 3.8 %collective-permute-start.30 = (bf16[512,512]{1,0:T(8,128)(2,1)}, bf16[512,512]{1,0:T(8,128)(2,1)}, u32[]{:S(2)}, u32[]{:S(2)}) collective-permute-start(bf16[512,512]{1,0:T(8,128)(2,1)} %add_convert_fusion), channel_id=1, source_target_pairs={{0,24},{8,0},{16,8},{24,16},{1,25},{9,1},{17,9},{25,17},{2,26},{10... | collective-permute-start | bytes 1572872 | tf_op jit(solution)/shard_map/ppermute | solution.py:44
  187.7 9.6 %collective-permute-done.20 = bf16[512,512]{1,0:T(8,128)(2,1)S(1)} collective-permute-done((bf16[512,512]{1,0:T(8,128)(2,1)S(1)}, bf16[512,512]{1,0:T(8,128)(2,1)S(1)}, u32[]{:S(2)}, u32[]{:S(2)}) %collective-permute-start.20) | collective-permute-done | bytes 524320 | tf_op jit(solution)/shard_map/ppermute | solution.py:44
  201.1 7.4 %collective-permute-done.30 = bf16[512,512]{1,0:T(8,128)(2,1)} collective-permute-done((bf16[512,512]{1,0:T(8,128)(2,1)}, bf16[512,512]{1,0:T(8,128)(2,1)}, u32[]{:S(2)}, u32[]{:S(2)}) %collective-permute-start.30) | collective-permute-done | bytes 524320 | tf_op jit(solution)/shard_map/ppermute | solution.py:44
  212.4 2.9 %fusion.9 = f32[512,512]{1,0:T(8,128)S(1)} fusion(bf16[512,2048]{1,0:T(8,128)(2,1)S(1)} %pad_maximum_fusion.9, bf16[4096,512]{1,0:T(8,128)(2,1)} %collective-permute-done.6), kind=kOutput, calls=%fused_computation.32 | convolution fusion | flops 1073741824 | bytes 5242880 | tf_op jit(solution)/shard_map/dot_general | solution.py:22
  215.5 4.4 %fusion.11 = f32[512,512]{1,0:T(8,128)} fusion(bf16[4096,512]{1,0:T(8,128)(2,1)} %collective-permute-done.6, bf16[512,512]{1,0:T(8,128)(2,1)} %collective-permute-done.22, bf16[512,512]{1,0:T(8,128)(2,1)S(1)} %copy-done.9, bf16[512,512]{1,0:T(8,128)(2,1)} %get-tuple-element.61, bf16[512,512]{1,0:T(8,128)(2,1)} %collective-permute-done.9), kind=kOutput, calls=%fused_computation.34 | convolution fusion | flops 1082130432 | bytes 5242880 | tf_op jit(solution)/shard_map/dot_general | solution.py:22
  222.5 4.4 %fusion.13 = f32[512,512]{1,0:T(8,128)} fusion(bf16[4096,512]{1,0:T(8,128)(2,1)} %collective-permute-done.6, bf16[512,512]{1,0:T(8,128)(2,1)} %collective-permute-done.21, bf16[512,512]{1,0:T(8,128)(2,1)} %get-tuple-element.60, bf16[512,512]{1,0:T(8,128)(2,1)S(1)} %copy-done.8, bf16[512,512]{1,0:T(8,128)(2,1)S(1)} %collective-permute-done.11), kind=kOutput, calls=%fused_computation.36 | convolution fusion | flops 1082130432 | bytes 5242880 | tf_op jit(solution)/shard_map/dot_general | solution.py:22
  227.7 13.2 %collective-permute-done.27 = bf16[512,512]{1,0:T(8,128)(2,1)} collective-permute-done((bf16[512,512]{1,0:T(8,128)(2,1)}, bf16[512,512]{1,0:T(8,128)(2,1)}, u32[]{:S(2)}, u32[]{:S(2)}) %collective-permute-start.27) | collective-permute-done | bytes 524320 | tf_op jit(solution)/shard_map/ppermute | solution.py:44
  240.9 4.1 %fusion.19 = bf16[512,512]{1,0:T(8,128)(2,1)} fusion(bf16[512,512]{1,0:T(8,128)(2,1)} %collective-permute-done.27, f32[512,512]{1,0:T(8,128)} %collective-permute-done.25, pred[]{:T(512)S(6)} %eq.17, bf16[512,512]{1,0:T(8,128)(2,1)} %collective-permute-done.22, bf16[512,512]{1,0:T(8,128)(2,1)S(1)} %copy-done.10, bf16[512,512]{1,0:T(8,128)(2,1)} %get-tuple-element.61, ...), kind=kOutput, calls=%fused_computation.44 | convolution fusion | flops 1091305472 | bytes 6291457 | tf_op jit(solution)/shard_map/dot_general | solution.py:22
  245.1 3.7 %fusion.17 = bf16[512,512]{1,0:T(8,128)(2,1)} fusion(f32[512,512]{1,0:T(8,128)} %collective-permute-done.23, bf16[512,512]{1,0:T(8,128)(2,1)} %collective-permute-done.21, bf16[512,512]{1,0:T(8,128)(2,1)} %get-tuple-element.60, bf16[512,512]{1,0:T(8,128)(2,1)S(1)} %copy-done.8, bf16[512,512]{1,0:T(8,128)(2,1)S(1)} %collective-permute-done.11, ...), kind=kOutput, calls=%fused_computation.42 | convolution fusion | flops 1091043328 | bytes 5767168 | tf_op jit(solution)/shard_map/dot_general | solution.py:22
  248.7 3.8 %collective-permute-start.24 = (bf16[512,512]{1,0:T(8,128)(2,1)}, bf16[512,512]{1,0:T(8,128)(2,1)S(1)}, u32[]{:S(2)}, u32[]{:S(2)}) collective-permute-start(bf16[512,512]{1,0:T(8,128)(2,1)} %fusion.17), channel_id=1, source_target_pairs={{0,24},{8,0},{16,8},{24,16},{1,25},{9,1},{17,9},{25,17},{2,26},{10... | collective-permute-start | bytes 1572872 | tf_op jit(solution)/shard_map/ppermute | solution.py:44
  252.6 9.5 %collective-permute-done.28 = bf16[512,512]{1,0:T(8,128)(2,1)} collective-permute-done((bf16[512,512]{1,0:T(8,128)(2,1)}, bf16[512,512]{1,0:T(8,128)(2,1)}, u32[]{:S(2)}, u32[]{:S(2)}) %collective-permute-start.28) | collective-permute-done | bytes 524320 | tf_op jit(solution)/shard_map/ppermute | solution.py:44
  262.1 9.6 %collective-permute-done.24 = bf16[512,512]{1,0:T(8,128)(2,1)S(1)} collective-permute-done((bf16[512,512]{1,0:T(8,128)(2,1)}, bf16[512,512]{1,0:T(8,128)(2,1)S(1)}, u32[]{:S(2)}, u32[]{:S(2)}) %collective-permute-start.24) | collective-permute-done | bytes 524320 | tf_op jit(solution)/shard_map/ppermute | solution.py:44
  271.6 8.8 %fusion = bf16[1,512,4096]{2,1,0:T(8,128)(2,1)} fusion(bf16[512,4096]{1,0:T(8,128)(2,1)} %param.11, bf16[512,4096]{1,0:T(8,128)(2,1)} %all-gather.2.cloned.1.call-done, bf16[512,512]{1,0:T(8,128)(2,1)S(1)} %copy-done.7, bf16[512,512]{1,0:T(8,128)(2,1)S(1)} %collective-permute-done.24, bf16[512,512]{1,0:T(8,128)(2,1)} %collective-permute-done.28, ...), kind=kOutput, calls=%fused_computation.1 | convolution fusion | flops 2158493696 | bytes 14155778 | tf_op jit(solution)/shard_map/dot_general | solution.py:13
  (148 shorter events, 59.7 us)
Async XLA Ops:
  6.5 265.1 %all-gather.2.cloned.1.call-start = ((), (), s32[]{:S(2)}) async-start(), calls=%async_computation | async-start | bytes 4718592 | tf_op jit(solution)/shard_map/all_gather | solution.py:143
  7.8 27.0 %collective-permute-start = (bf16[1024,512]{1,0:T(8,128)(2,1)S(1)}, bf16[1024,512]{1,0:T(8,128)(2,1)}, u32[]{:S(2)}, u32[]{:S(2)}) collective-permute-start(bf16[1024,512]{1,0:T(8,128)(2,1)S(1)} %pad_maximum_fusion.22), channel_id=1, source_target_pairs={{0,2},{1,3},{2,0},{3,1},{4,6},{5,7},{6,4},{7,5},{8,10},{9,11},{10,... | collective-permute-start | bytes 3145736 | tf_op jit(solution)/shard_map/ppermute | solution.py:40
  10.8 24.7 %collective-permute-start.1 = (bf16[1024,512]{1,0:T(8,128)(2,1)S(1)}, bf16[1024,512]{1,0:T(8,128)(2,1)}, u32[]{:S(2)}, u32[]{:S(2)}) collective-permute-start(bf16[1024,512]{1,0:T(8,128)(2,1)S(1)} %pad_maximum_fusion.22), channel_id=1, source_target_pairs={{0,4},{1,5},{2,6},{3,7},{4,0},{5,1},{6,2},{7,3},{8,12},{9,13},{10,... | collective-permute-start | bytes 3145736 | tf_op jit(solution)/shard_map/ppermute | solution.py:40
  12.3 14.8 %collective-permute-start.2 = (bf16[512,512]{1,0:T(8,128)(2,1)}, bf16[512,512]{1,0:T(8,128)(2,1)S(1)}, u32[]{:S(2)}, u32[]{:S(2)}) collective-permute-start(bf16[512,512]{1,0:T(8,128)(2,1)} %bitcast.52), channel_id=1, source_target_pairs={{0,24},{8,0},{16,8},{24,16},{1,25},{9,1},{17,9},{25,17},{2,26},{10... | collective-permute-start | bytes 1572872 | tf_op jit(solution)/shard_map/ppermute | solution.py:44
  27.1 13.6 %collective-permute-start.3 = (bf16[512,512]{1,0:T(8,128)(2,1)S(1)}, bf16[512,512]{1,0:T(8,128)(2,1)S(1)}, u32[]{:S(2)}, u32[]{:S(2)}) collective-permute-start(bf16[512,512]{1,0:T(8,128)(2,1)S(1)} %collective-permute-done.2), channel_id=1, source_target_pairs={{0,24},{8,0},{16,8},{24,16},{1,25},{9,1},{17,9},{25,17},{2,26},{10... | collective-permute-start | bytes 1572872 | tf_op jit(solution)/shard_map/ppermute | solution.py:44
  34.8 51.7 %collective-permute-start.6 = (bf16[4096,512]{1,0:T(8,128)(2,1)}, bf16[4096,512]{1,0:T(8,128)(2,1)}, u32[]{:S(2)}, u32[]{:S(2)}) collective-permute-start(bf16[4096,512]{1,0:T(8,128)(2,1)} %bitcast_dynamic-update-slice_fusion), channel_id=1, source_target_pairs={{0,1},{1,0},{2,3},{3,2},{4,5},{5,4},{6,7},{7,6},{8,9},{9,8},{10,11... | collective-permute-start | bytes 12582920 | tf_op jit(solution)/shard_map/ppermute | solution.py:40
  42.6 34.0 %collective-permute-start.4 = (bf16[1536,512]{1,0:T(8,128)(2,1)}, bf16[1536,512]{1,0:T(8,128)(2,1)}, u32[]{:S(2)}, u32[]{:S(2)}) collective-permute-start(bf16[1536,512]{1,0:T(8,128)(2,1)} %get-tuple-element.40), channel_id=1, source_target_pairs={{0,2},{1,3},{2,0},{3,1},{4,6},{5,7},{6,4},{7,5},{8,10},{9,11},{10,... | collective-permute-start | bytes 4718600 | tf_op jit(solution)/shard_map/ppermute | solution.py:40
  43.2 33.8 %collective-permute-start.5 = (bf16[1536,512]{1,0:T(8,128)(2,1)}, bf16[1536,512]{1,0:T(8,128)(2,1)}, u32[]{:S(2)}, u32[]{:S(2)}) collective-permute-start(bf16[1536,512]{1,0:T(8,128)(2,1)} %get-tuple-element.41), channel_id=1, source_target_pairs={{0,4},{1,5},{2,6},{3,7},{4,0},{5,1},{6,2},{7,3},{8,12},{9,13},{10,... | collective-permute-start | bytes 4718600 | tf_op jit(solution)/shard_map/ppermute | solution.py:40
  43.7 16.7 %collective-permute-start.9 = (bf16[512,512]{1,0:T(8,128)(2,1)S(1)}, bf16[512,512]{1,0:T(8,128)(2,1)}, u32[]{:S(2)}, u32[]{:S(2)}) collective-permute-start(bf16[512,512]{1,0:T(8,128)(2,1)S(1)} %bitcast.56), channel_id=1, source_target_pairs={{0,24},{8,0},{16,8},{24,16},{1,25},{9,1},{17,9},{25,17},{2,26},{10... | collective-permute-start | bytes 1572872 | tf_op jit(solution)/shard_map/ppermute | solution.py:44
  52.2 27.6 %collective-permute-start.8 = (bf16[512,512]{1,0:T(8,128)(2,1)S(1)}, bf16[512,512]{1,0:T(8,128)(2,1)S(1)}, u32[]{:S(2)}, u32[]{:S(2)}) collective-permute-start(bf16[512,512]{1,0:T(8,128)(2,1)S(1)} %bitcast.53), channel_id=1, source_target_pairs={{0,8},{8,16},{16,24},{24,0},{1,9},{9,17},{17,25},{25,1},{2,10},{10... | collective-permute-start | bytes 1572872 | tf_op jit(solution)/shard_map/ppermute | solution.py:44
  60.4 19.5 %collective-permute-start.10 = (bf16[512,512]{1,0:T(8,128)(2,1)}, bf16[512,512]{1,0:T(8,128)(2,1)S(1)}, u32[]{:S(2)}, u32[]{:S(2)}) collective-permute-start(bf16[512,512]{1,0:T(8,128)(2,1)} %collective-permute-done.9), channel_id=1, source_target_pairs={{0,24},{8,0},{16,8},{24,16},{1,25},{9,1},{17,9},{25,17},{2,26},{10... | collective-permute-start | bytes 1572872 | tf_op jit(solution)/shard_map/ppermute | solution.py:44
  80.1 32.6 %collective-permute-start.12 = (bf16[1536,512]{1,0:T(8,128)(2,1)S(1)}, bf16[1536,512]{1,0:T(8,128)(2,1)S(1)}, u32[]{:S(2)}, u32[]{:S(2)}) collective-permute-start(bf16[1536,512]{1,0:T(8,128)(2,1)S(1)} %get-tuple-element.49), channel_id=1, source_target_pairs={{0,2},{1,3},{2,0},{3,1},{4,6},{5,7},{6,4},{7,5},{8,10},{9,11},{10,... | collective-permute-start | bytes 4718600 | tf_op jit(solution)/shard_map/ppermute | solution.py:40
  81.7 32.2 %collective-permute-start.13 = (bf16[1536,512]{1,0:T(8,128)(2,1)S(1)}, bf16[1536,512]{1,0:T(8,128)(2,1)S(1)}, u32[]{:S(2)}, u32[]{:S(2)}) collective-permute-start(bf16[1536,512]{1,0:T(8,128)(2,1)S(1)} %get-tuple-element.50), channel_id=1, source_target_pairs={{0,4},{1,5},{2,6},{3,7},{4,0},{5,1},{6,2},{7,3},{8,12},{9,13},{10,... | collective-permute-start | bytes 4718600 | tf_op jit(solution)/shard_map/ppermute | solution.py:40
  82.8 31.3 %collective-permute-start.11 = (bf16[512,512]{1,0:T(8,128)(2,1)S(1)}, bf16[512,512]{1,0:T(8,128)(2,1)S(1)}, u32[]{:S(2)}, u32[]{:S(2)}) collective-permute-start(bf16[512,512]{1,0:T(8,128)(2,1)S(1)} %bitcast.58), channel_id=1, source_target_pairs={{0,8},{8,16},{16,24},{24,0},{1,9},{9,17},{17,25},{25,1},{2,10},{10... | collective-permute-start | bytes 1572872 | tf_op jit(solution)/shard_map/ppermute | solution.py:44
  89.3 26.1 %collective-permute-start.7 = (f32[512,512]{1,0:T(8,128)S(1)}, f32[512,512]{1,0:T(8,128)S(1)}, u32[]{:S(2)}, u32[]{:S(2)}) collective-permute-start(f32[512,512]{1,0:T(8,128)S(1)} %fusion.15), channel_id=1, source_target_pairs={{0,1},{1,0},{2,3},{3,2},{4,5},{5,4},{6,7},{7,6},{8,9},{9,8},{10,11... | collective-permute-start | bytes 3145736 | tf_op jit(solution)/shard_map/ppermute | solution.py:40
  113.9 2.7 collective-permute-start.14
  116.8 36.7 %collective-permute-start.15 = (bf16[1536,512]{1,0:T(8,128)(2,1)S(1)}, bf16[1536,512]{1,0:T(8,128)(2,1)S(1)}, u32[]{:S(2)}, u32[]{:S(2)}) collective-permute-start(bf16[1536,512]{1,0:T(8,128)(2,1)S(1)} %get-tuple-element.54), channel_id=1, source_target_pairs={{0,2},{1,3},{2,0},{3,1},{4,6},{5,7},{6,4},{7,5},{8,10},{9,11},{10,... | collective-permute-start | bytes 4718600 | tf_op jit(solution)/shard_map/ppermute | solution.py:40
  117.4 36.3 %collective-permute-start.16 = (bf16[1536,512]{1,0:T(8,128)(2,1)S(1)}, bf16[1536,512]{1,0:T(8,128)(2,1)S(1)}, u32[]{:S(2)}, u32[]{:S(2)}) collective-permute-start(bf16[1536,512]{1,0:T(8,128)(2,1)S(1)} %get-tuple-element.55), channel_id=1, source_target_pairs={{0,4},{1,5},{2,6},{3,7},{4,0},{5,1},{6,2},{7,3},{8,12},{9,13},{10,... | collective-permute-start | bytes 4718600 | tf_op jit(solution)/shard_map/ppermute | solution.py:40
  122.2 39.0 %collective-permute-start.18 = (f32[512,512]{1,0:T(8,128)S(1)}, f32[512,512]{1,0:T(8,128)S(1)}, u32[]{:S(2)}, u32[]{:S(2)}) collective-permute-start(f32[512,512]{1,0:T(8,128)S(1)} %fusion.3), channel_id=1, source_target_pairs={{0,1},{1,0},{2,3},{3,2},{4,5},{5,4},{6,7},{7,6},{8,9},{9,8},{10,11... | collective-permute-start | bytes 3145736 | tf_op jit(solution)/shard_map/ppermute | solution.py:40
  126.0 40.0 %collective-permute-start.17 = (f32[512,512]{1,0:T(8,128)}, f32[512,512]{1,0:T(8,128)}, u32[]{:S(2)}, u32[]{:S(2)}) collective-permute-start(f32[512,512]{1,0:T(8,128)} %fusion.5), channel_id=1, source_target_pairs={{0,1},{1,0},{2,3},{3,2},{4,5},{5,4},{6,7},{7,6},{8,9},{9,8},{10,11... | collective-permute-start | bytes 3145736 | tf_op jit(solution)/shard_map/ppermute | solution.py:40
  161.2 19.4 %collective-permute-start.29 = (f32[512,512]{1,0:T(8,128)}, f32[512,512]{1,0:T(8,128)}, u32[]{:S(2)}, u32[]{:S(2)}) collective-permute-start(f32[512,512]{1,0:T(8,128)} %fusion.1), channel_id=1, source_target_pairs={{0,1},{1,0},{2,3},{3,2},{4,5},{5,4},{6,7},{7,6},{8,9},{9,8},{10,11... | collective-permute-start | bytes 3145736 | tf_op jit(solution)/shard_map/ppermute | solution.py:40
  163.3 17.2 %collective-permute-start.19 = (bf16[512,512]{1,0:T(8,128)(2,1)}, bf16[512,512]{1,0:T(8,128)(2,1)}, u32[]{:S(2)}, u32[]{:S(2)}) collective-permute-start(bf16[512,512]{1,0:T(8,128)(2,1)} %add_convert_fusion.2), channel_id=1, source_target_pairs={{0,8},{8,16},{16,24},{24,0},{1,9},{9,17},{17,25},{25,1},{2,10},{10... | collective-permute-start | bytes 1572872 | tf_op jit(solution)/shard_map/ppermute | solution.py:44
  180.5 16.8 %collective-permute-start.20 = (bf16[512,512]{1,0:T(8,128)(2,1)S(1)}, bf16[512,512]{1,0:T(8,128)(2,1)S(1)}, u32[]{:S(2)}, u32[]{:S(2)}) collective-permute-start(bf16[512,512]{1,0:T(8,128)(2,1)S(1)} %broadcast_select_fusion), channel_id=1, source_target_pairs={{0,8},{8,16},{16,24},{24,0},{1,9},{9,17},{17,25},{25,1},{2,10},{10... | collective-permute-start | bytes 1572872 | tf_op jit(solution)/shard_map/ppermute | solution.py:44
  183.9 24.6 %collective-permute-start.30 = (bf16[512,512]{1,0:T(8,128)(2,1)}, bf16[512,512]{1,0:T(8,128)(2,1)}, u32[]{:S(2)}, u32[]{:S(2)}) collective-permute-start(bf16[512,512]{1,0:T(8,128)(2,1)} %add_convert_fusion), channel_id=1, source_target_pairs={{0,24},{8,0},{16,8},{24,16},{1,25},{9,1},{17,9},{25,17},{2,26},{10... | collective-permute-start | bytes 1572872 | tf_op jit(solution)/shard_map/ppermute | solution.py:44
  198.2 14.1 %collective-permute-start.21 = (bf16[512,512]{1,0:T(8,128)(2,1)}, bf16[512,512]{1,0:T(8,128)(2,1)}, u32[]{:S(2)}, u32[]{:S(2)}) collective-permute-start(bf16[512,512]{1,0:T(8,128)(2,1)} %get-tuple-element.60), channel_id=1, source_target_pairs={{0,2},{1,3},{2,0},{3,1},{4,6},{5,7},{6,4},{7,5},{8,10},{9,11},{10,... | collective-permute-start | bytes 1572872 | tf_op jit(solution)/shard_map/ppermute | solution.py:40
  200.6 11.8 %collective-permute-start.22 = (bf16[512,512]{1,0:T(8,128)(2,1)}, bf16[512,512]{1,0:T(8,128)(2,1)}, u32[]{:S(2)}, u32[]{:S(2)}) collective-permute-start(bf16[512,512]{1,0:T(8,128)(2,1)} %get-tuple-element.61), channel_id=1, source_target_pairs={{0,4},{1,5},{2,6},{3,7},{4,0},{5,1},{6,2},{7,3},{8,12},{9,13},{10,... | collective-permute-start | bytes 1572872 | tf_op jit(solution)/shard_map/ppermute | solution.py:40
  215.3 5.0 %collective-permute-start.26 = (f32[512,512]{1,0:T(8,128)S(1)}, f32[512,512]{1,0:T(8,128)S(1)}, u32[]{:S(2)}, u32[]{:S(2)}) collective-permute-start(f32[512,512]{1,0:T(8,128)S(1)} %fusion.9), channel_id=1, source_target_pairs={{0,1},{1,0},{2,3},{3,2},{4,5},{5,4},{6,7},{7,6},{8,9},{9,8},{10,11... | collective-permute-start | bytes 3145736 | tf_op jit(solution)/shard_map/ppermute | solution.py:40
  219.9 7.8 %collective-permute-start.25 = (f32[512,512]{1,0:T(8,128)}, f32[512,512]{1,0:T(8,128)}, u32[]{:S(2)}, u32[]{:S(2)}) collective-permute-start(f32[512,512]{1,0:T(8,128)} %fusion.11), channel_id=1, source_target_pairs={{0,1},{1,0},{2,3},{3,2},{4,5},{5,4},{6,7},{7,6},{8,9},{9,8},{10,11... | collective-permute-start | bytes 3145736 | tf_op jit(solution)/shard_map/ppermute | solution.py:40
  222.5 18.5 %collective-permute-start.27 = (bf16[512,512]{1,0:T(8,128)(2,1)}, bf16[512,512]{1,0:T(8,128)(2,1)}, u32[]{:S(2)}, u32[]{:S(2)}) collective-permute-start(bf16[512,512]{1,0:T(8,128)(2,1)} %add_convert_fusion.1), channel_id=1, source_target_pairs={{0,8},{8,16},{16,24},{24,0},{1,9},{9,17},{17,25},{25,1},{2,10},{10... | collective-permute-start | bytes 1572872 | tf_op jit(solution)/shard_map/ppermute | solution.py:44
  226.9 18.1 %collective-permute-start.23 = (f32[512,512]{1,0:T(8,128)}, f32[512,512]{1,0:T(8,128)}, u32[]{:S(2)}, u32[]{:S(2)}) collective-permute-start(f32[512,512]{1,0:T(8,128)} %fusion.13), channel_id=1, source_target_pairs={{0,1},{1,0},{2,3},{3,2},{4,5},{5,4},{6,7},{7,6},{8,9},{9,8},{10,11... | collective-permute-start | bytes 3145736 | tf_op jit(solution)/shard_map/ppermute | solution.py:40
  245.1 17.0 %collective-permute-start.28 = (bf16[512,512]{1,0:T(8,128)(2,1)}, bf16[512,512]{1,0:T(8,128)(2,1)}, u32[]{:S(2)}, u32[]{:S(2)}) collective-permute-start(bf16[512,512]{1,0:T(8,128)(2,1)} %fusion.19), channel_id=1, source_target_pairs={{0,8},{8,16},{16,24},{24,0},{1,9},{9,17},{17,25},{25,1},{2,10},{10... | collective-permute-start | bytes 1572872 | tf_op jit(solution)/shard_map/ppermute | solution.py:44
  248.7 22.9 %collective-permute-start.24 = (bf16[512,512]{1,0:T(8,128)(2,1)}, bf16[512,512]{1,0:T(8,128)(2,1)S(1)}, u32[]{:S(2)}, u32[]{:S(2)}) collective-permute-start(bf16[512,512]{1,0:T(8,128)(2,1)} %fusion.17), channel_id=1, source_target_pairs={{0,24},{8,0},{16,8},{24,16},{1,25},{9,1},{17,9},{25,17},{2,26},{10... | collective-permute-start | bytes 1572872 | tf_op jit(solution)/shard_map/ppermute | solution.py:44
  (33 other events, 809.8 us)
Sparse Core Ops, SparseCore 0:
  212.5 40.6 all-gather.1

commit v14 on v13

--- a/solution.py
+++ b/solution.py
@@ -133,17 +133,18 @@
     due += [fetch(1, 3, gate)] + rotate(groups[0], begun(0, gate))
 
     gate, due = due, slot(3, due)
-    due += rotate(groups[1], begun(1, gate))
-    in_from_behind = send_ahead(0, pass_on(0), [])
-    due.append(in_from_behind)
+    rotate(groups[1], begun(1, gate))
+    passed_in = pass_on(0)
+    due.append(passed_in)
 
     gate, due = due, slot(4, due)
-    rotate(groups[2], begun(2, gate))
-    rot_in = after(keep(0, in_from_behind, send_behind(0)), due)
+    in_from_behind = send_ahead(0, passed_in, gate)
+    ready = rotate(groups[2], begun(2, gate))
+    in_from_ahead = send_behind(0)
+    passed_out = pass_on(1)
+    ready += rotate(groups[3], after(evens[3], due))
+    rot_in = after(keep(0, in_from_behind, in_from_ahead), ready)
     all_rot_in = lax.all_gather(rot_in, "tensor", axis=1, tiled=True)
-
-    passed_out = pass_on(1)
-    rotate(groups[3], evens[3])
     rot_out = keep(1, send_ahead(1, passed_out, []), send_behind(1))
     return product_and_divide(rot_out, all_rot_in, eig_lambda, tokens)
 

time: 291 us -> 286 us (0.983)
  the two profiles are of different devices: /device:TPU:0 before, /device:TPU:16 now
where the time goes in v14:
time: 286 us; the launch traced here: 284 us
  waiting for transfers between devices  152 us (53%)
  matrix products  45.3 us (16%)
  starting transfers between devices  36.8 us (13%)
  local copies, waits for them, and re-layouts  22.2 us (8%)
  between operations  15.2 us (5%)
  other arithmetic  12 us (4%)
    ppermute x12, waiting for transfers between devices, shift(): return lax.ppermute(block, 'dp', [(z, (z + by) % n) for z in range(n)])  94.6 us
    ppermute x19, waiting for transfers between devices, swap(): lax.ppermute(block, 'tensor', [(j, j ^ bit) for j in range(X + Y + CORE +...  57.4 us
    dot_general x16, matrix products, dot(): return jnp.dot(a, b, preferred_element_type=jnp.float32)  36.7 us
    ppermute x12, starting transfers between devices, shift(): return lax.ppermute(block, 'dp', [(z, (z + by) % n) for z in range(n)])  22.5 us
    ppermute x19, starting transfers between devices, swap(): lax.ppermute(block, 'tensor', [(j, j ^ bit) for j in range(X + Y + CORE +...  14.3 us
    unnamed x79, local copies, waits for them, and re-layouts  10.2 us
    dot_general x1, matrix products, product_and_divide(): lax.dot_general(rot_out, all_rot_in, contract, preferred_element_type=jnp...  8.69 us
  transfers between devices with their start and end apart: 32, of which 19 were waited for; matrix products, arithmetic and copies ran while one was open for 22% of the time, Pallas kernels for 0%

profile of v14, /device:TPU:16, one launch (start us, length us, event | category | flops | bytes accessed | tf_op | source)
XLA Modules:
  0.0 283.5 jit_solution(5991003820220438471)
XLA Ops:
  11.3 12.9 %collective-permute-done.2 = bf16[512,512]{1,0:T(8,128)(2,1)S(1)} collective-permute-done((bf16[512,512]{1,0:T(8,128)(2,1)}, bf16[512,512]{1,0:T(8,128)(2,1)S(1)}, u32[]{:S(2)}, u32[]{:S(2)}) %collective-permute-start.2) | collective-permute-done | bytes 524320 | tf_op jit(solution)/shard_map/ppermute | solution.py:44
  24.7 8.1 %collective-permute-done = bf16[1024,512]{1,0:T(8,128)(2,1)S(1)} collective-permute-done((bf16[1024,512]{1,0:T(8,128)(2,1)S(1)}, bf16[1024,512]{1,0:T(8,128)(2,1)S(1)}, u32[]{:S(2)}, u32[]{:S(2)}) %collective-permute-start) | collective-permute-done | bytes 1048608 | tf_op jit(solution)/shard_map/ppermute | solution.py:40
  34.9 3.1 %collective-permute-done.3 = bf16[512,512]{1,0:T(8,128)(2,1)S(1)} collective-permute-done((bf16[512,512]{1,0:T(8,128)(2,1)S(1)}, bf16[512,512]{1,0:T(8,128)(2,1)S(1)}, u32[]{:S(2)}, u32[]{:S(2)}) %collective-permute-start.3) | collective-permute-done | bytes 524320 | tf_op jit(solution)/shard_map/ppermute | solution.py:44
  41.0 2.0 bitcast_dynamic-update-slice_fusion.7
  53.6 3.6 %collective-permute-start.9 = (bf16[512,512]{1,0:T(8,128)(2,1)S(1)}, bf16[512,512]{1,0:T(8,128)(2,1)S(1)}, u32[]{:S(2)}, u32[]{:S(2)}) collective-permute-start(bf16[512,512]{1,0:T(8,128)(2,1)S(1)} %bitcast.57), channel_id=1, source_target_pairs={{0,8},{8,16},{16,24},{24,0},{1,9},{9,17},{17,25},{25,1},{2,10},{10... | collective-permute-start | bytes 1572872 | tf_op jit(solution)/shard_map/ppermute | solution.py:44
  57.2 11.2 %collective-permute-done.8 = bf16[512,512]{1,0:T(8,128)(2,1)S(1)} collective-permute-done((bf16[512,512]{1,0:T(8,128)(2,1)}, bf16[512,512]{1,0:T(8,128)(2,1)S(1)}, u32[]{:S(2)}, u32[]{:S(2)}) %collective-permute-start.8) | collective-permute-done | bytes 524320 | tf_op jit(solution)/shard_map/ppermute | solution.py:44
  68.4 5.8 %collective-permute-done.4 = bf16[1536,512]{1,0:T(8,128)(2,1)} collective-permute-done((bf16[1536,512]{1,0:T(8,128)(2,1)}, bf16[1536,512]{1,0:T(8,128)(2,1)}, u32[]{:S(2)}, u32[]{:S(2)}) %collective-permute-start.4) | collective-permute-done | bytes 1572896 | tf_op jit(solution)/shard_map/ppermute | solution.py:40
  77.4 3.0 %collective-permute-done.9 = bf16[512,512]{1,0:T(8,128)(2,1)S(1)} collective-permute-done((bf16[512,512]{1,0:T(8,128)(2,1)S(1)}, bf16[512,512]{1,0:T(8,128)(2,1)S(1)}, u32[]{:S(2)}, u32[]{:S(2)}) %collective-permute-start.9) | collective-permute-done | bytes 524320 | tf_op jit(solution)/shard_map/ppermute | solution.py:44
  80.4 10.3 %collective-permute-done.10 = bf16[512,512]{1,0:T(8,128)(2,1)S(1)} collective-permute-done((bf16[512,512]{1,0:T(8,128)(2,1)S(1)}, bf16[512,512]{1,0:T(8,128)(2,1)S(1)}, u32[]{:S(2)}, u32[]{:S(2)}) %collective-permute-start.10) | collective-permute-done | bytes 524320 | tf_op jit(solution)/shard_map/ppermute | solution.py:44
  96.3 3.6 %collective-permute-start.13 = (bf16[512,512]{1,0:T(8,128)(2,1)}, bf16[512,512]{1,0:T(8,128)(2,1)S(1)}, u32[]{:S(2)}, u32[]{:S(2)}) collective-permute-start(bf16[512,512]{1,0:T(8,128)(2,1)} %bitcast.2), channel_id=1, source_target_pairs={{0,8},{8,16},{16,24},{24,0},{1,9},{9,17},{17,25},{25,1},{2,10},{10... | collective-permute-start | bytes 1572872 | tf_op jit(solution)/shard_map/ppermute | solution.py:44
  102.5 24.8 %collective-permute-done.11 = bf16[1536,512]{1,0:T(8,128)(2,1)S(1)} collective-permute-done((bf16[1536,512]{1,0:T(8,128)(2,1)S(1)}, bf16[1536,512]{1,0:T(8,128)(2,1)S(1)}, u32[]{:S(2)}, u32[]{:S(2)}) %collective-permute-start.11) | collective-permute-done | bytes 1572896 | tf_op jit(solution)/shard_map/ppermute | solution.py:40
  131.0 2.8 %fusion.15 = f32[512,512]{1,0:T(8,128)S(1)} fusion(bf16[512,2048]{1,0:T(8,128)(2,1)S(1)} %pad_maximum_fusion.1, bf16[4096,512]{1,0:T(8,128)(2,1)} %collective-permute-done.6), kind=kOutput, calls=%fused_computation.38 | convolution fusion | flops 1073741824 | bytes 5242880 | tf_op jit(solution)/shard_map/dot_general | solution.py:22
  133.9 2.8 %fusion.7 = f32[512,512]{1,0:T(8,128)S(1)} fusion(bf16[512,2048]{1,0:T(8,128)(2,1)S(1)} %pad_maximum_fusion, bf16[4096,512]{1,0:T(8,128)(2,1)} %collective-permute-done.6), kind=kOutput, calls=%fused_computation.30 | convolution fusion | flops 1073741824 | bytes 5242880 | tf_op jit(solution)/shard_map/dot_general | solution.py:22
  137.3 2.8 fusion.5
  140.2 3.8 %fusion.1 = f32[512,512]{1,0:T(8,128)} fusion(bf16[512,2048]{1,0:T(8,128)(2,1)S(1)} %pad_maximum_fusion.4, bf16[4096,512]{1,0:T(8,128)(2,1)} %collective-permute-done.6), kind=kOutput, calls=%fused_computation.24 | convolution fusion | flops 1073741824 | bytes 5242880 | tf_op jit(solution)/shard_map/dot_general | solution.py:22
  150.5 2.1 add_convert_fusion.3
  152.6 3.3 %collective-permute-start.18 = (bf16[512,512]{1,0:T(8,128)(2,1)}, bf16[512,512]{1,0:T(8,128)(2,1)}, u32[]{:S(2)}, u32[]{:S(2)}) collective-permute-start(bf16[512,512]{1,0:T(8,128)(2,1)} %add_convert_fusion.3), channel_id=1, source_target_pairs={{0,8},{8,16},{16,24},{24,0},{1,9},{9,17},{17,25},{25,1},{2,10},{10... | collective-permute-start | bytes 1572872 | tf_op jit(solution)/shard_map/ppermute | solution.py:44
  157.1 10.0 %collective-permute-done.18 = bf16[512,512]{1,0:T(8,128)(2,1)} collective-permute-done((bf16[512,512]{1,0:T(8,128)(2,1)}, bf16[512,512]{1,0:T(8,128)(2,1)}, u32[]{:S(2)}, u32[]{:S(2)}) %collective-permute-start.18) | collective-permute-done | bytes 524320 | tf_op jit(solution)/shard_map/ppermute | solution.py:44
  167.1 3.3 %fusion.19 = bf16[512,512]{1,0:T(8,128)(2,1)S(1)} fusion(bf16[512,512]{1,0:T(8,128)(2,1)} %collective-permute-done.18, f32[512,512]{1,0:T(8,128)} %collective-permute-done.29, pred[]{:T(512)S(6)} %eq.19, bf16[512,2048]{1,0:T(8,128)(2,1)S(1)} %pad_maximum_fusion.4, bf16[512,512]{1,0:T(8,128)(2,1)} %copy-done.23, bf16[512,512]{1,0:T(8,128)(2,1)} %copy-done.25, ...), kind=kOutput, calls=%fused_computation.51 | convolution fusion | flops 1082916864 | bytes 6291457 | tf_op jit(solution)/shard_map/dot_general | solution.py:22
  170.4 14.7 %collective-permute-done.15 = bf16[1536,512]{1,0:T(8,128)(2,1)} collective-permute-done((bf16[1536,512]{1,0:T(8,128)(2,1)}, bf16[1536,512]{1,0:T(8,128)(2,1)}, u32[]{:S(2)}, u32[]{:S(2)}) %collective-permute-start.15) | collective-permute-done | bytes 1572896 | tf_op jit(solution)/shard_map/ppermute | solution.py:40
  192.1 2.8 %fusion.9 = f32[512,512]{1,0:T(8,128)S(1)} fusion(bf16[512,2048]{1,0:T(8,128)(2,1)S(1)} %pad_maximum_fusion.9, bf16[4096,512]{1,0:T(8,128)(2,1)} %collective-permute-done.6), kind=kOutput, calls=%fused_computation.32 | convolution fusion | flops 1073741824 | bytes 5242880 | tf_op jit(solution)/shard_map/dot_general | solution.py:22
  195.0 3.4 %collective-permute-start.30 = (bf16[512,512]{1,0:T(8,128)(2,1)S(1)}, bf16[512,512]{1,0:T(8,128)(2,1)S(1)}, u32[]{:S(2)}, u32[]{:S(2)}) collective-permute-start(bf16[512,512]{1,0:T(8,128)(2,1)S(1)} %fusion.19), channel_id=1, source_target_pairs={{0,8},{8,16},{16,24},{24,0},{1,9},{9,17},{17,25},{25,1},{2,10},{10... | collective-permute-start | bytes 1572872 | tf_op jit(solution)/shard_map/ppermute | solution.py:44
  198.4 2.8 fusion.3
  203.0 2.8 %fusion.11 = f32[512,512]{1,0:T(8,128)S(1)} fusion(bf16[512,2048]{1,0:T(8,128)(2,1)S(1)} %pad_maximum_fusion.6, bf16[4096,512]{1,0:T(8,128)(2,1)} %collective-permute-done.6), kind=kOutput, calls=%fused_computation.34 | convolution fusion | flops 1073741824 | bytes 5242880 | tf_op jit(solution)/shard_map/dot_general | solution.py:22
  206.0 3.0 %fusion.13 = f32[512,512]{1,0:T(8,128)S(1)} fusion(bf16[512,2048]{1,0:T(8,128)(2,1)S(1)} %pad_maximum_fusion.7, bf16[4096,512]{1,0:T(8,128)(2,1)} %collective-permute-done.6), kind=kOutput, calls=%fused_computation.36 | convolution fusion | flops 1073741824 | bytes 5242880 | tf_op jit(solution)/shard_map/dot_general | solution.py:22
  216.1 10.2 %collective-permute-done.28 = bf16[512,512]{1,0:T(8,128)(2,1)S(1)} collective-permute-done((bf16[512,512]{1,0:T(8,128)(2,1)S(1)}, bf16[512,512]{1,0:T(8,128)(2,1)S(1)}, u32[]{:S(2)}, u32[]{:S(2)}) %collective-permute-start.28) | collective-permute-done | bytes 524320 | tf_op jit(solution)/shard_map/ppermute | solution.py:44
  227.3 3.6 %collective-permute-start.25 = (bf16[512,512]{1,0:T(8,128)(2,1)S(1)}, bf16[512,512]{1,0:T(8,128)(2,1)S(1)}, u32[]{:S(2)}, u32[]{:S(2)}) collective-permute-start(bf16[512,512]{1,0:T(8,128)(2,1)S(1)} %add_convert_fusion.2), channel_id=1, source_target_pairs={{0,8},{8,16},{16,24},{24,0},{1,9},{9,17},{17,25},{25,1},{2,10},{10... | collective-permute-start | bytes 1572872 | tf_op jit(solution)/shard_map/ppermute | solution.py:44
  231.5 10.1 %collective-permute-done.25 = bf16[512,512]{1,0:T(8,128)(2,1)S(1)} collective-permute-done((bf16[512,512]{1,0:T(8,128)(2,1)S(1)}, bf16[512,512]{1,0:T(8,128)(2,1)S(1)}, u32[]{:S(2)}, u32[]{:S(2)}) %collective-permute-start.25) | collective-permute-done | bytes 524320 | tf_op jit(solution)/shard_map/ppermute | solution.py:44
  241.6 2.5 collective-permute-start.26
  244.1 11.2 %collective-permute-done.26 = bf16[512,512]{1,0:T(8,128)(2,1)S(1)} collective-permute-done((bf16[512,512]{1,0:T(8,128)(2,1)S(1)}, bf16[512,512]{1,0:T(8,128)(2,1)S(1)}, u32[]{:S(2)}, u32[]{:S(2)}) %collective-permute-start.26) | collective-permute-done | bytes 524320 | tf_op jit(solution)/shard_map/ppermute | solution.py:44
  255.3 12.6 %collective-permute-done.22 = bf16[512,512]{1,0:T(8,128)(2,1)S(1)} collective-permute-done((bf16[512,512]{1,0:T(8,128)(2,1)S(1)}, bf16[512,512]{1,0:T(8,128)(2,1)S(1)}, u32[]{:S(2)}, u32[]{:S(2)}) %collective-permute-start.22) | collective-permute-done | bytes 524320 | tf_op jit(solution)/shard_map/ppermute | solution.py:44
  268.0 8.7 %fusion = bf16[1,512,4096]{2,1,0:T(8,128)(2,1)} fusion(bf16[512,4096]{1,0:T(8,128)(2,1)} %param.11, bf16[512,4096]{1,0:T(8,128)(2,1)} %all-gather.2.cloned.1.call-done, bf16[512,512]{1,0:T(8,128)(2,1)S(1)} %copy-done.18, bf16[512,512]{1,0:T(8,128)(2,1)S(1)} %collective-permute-done.22, bf16[512,512]{1,0:T(8,128)(2,1)S(1)} %collective-permute-done.26, ...), kind=kOutput, calls=%fused_computation.1 | convolution fusion | flops 2158493696 | bytes 14155778 | tf_op jit(solution)/shard_map/dot_general | solution.py:13
  (156 shorter events, 60.3 us)
Async XLA Ops:
  6.5 261.4 %all-gather.2.cloned.1.call-start = ((), (), s32[]{:S(2)}) async-start(), calls=%async_computation | async-start | bytes 4718592 | tf_op jit(solution)/shard_map/all_gather | solution.py:147
  7.8 25.0 %collective-permute-start = (bf16[1024,512]{1,0:T(8,128)(2,1)S(1)}, bf16[1024,512]{1,0:T(8,128)(2,1)S(1)}, u32[]{:S(2)}, u32[]{:S(2)}) collective-permute-start(bf16[1024,512]{1,0:T(8,128)(2,1)S(1)} %pad_maximum_fusion.22), channel_id=1, source_target_pairs={{0,2},{1,3},{2,0},{3,1},{4,6},{5,7},{6,4},{7,5},{8,10},{9,11},{10,... | collective-permute-start | bytes 3145736 | tf_op jit(solution)/shard_map/ppermute | solution.py:40
  9.4 24.6 %collective-permute-start.1 = (bf16[1024,512]{1,0:T(8,128)(2,1)S(1)}, bf16[1024,512]{1,0:T(8,128)(2,1)S(1)}, u32[]{:S(2)}, u32[]{:S(2)}) collective-permute-start(bf16[1024,512]{1,0:T(8,128)(2,1)S(1)} %pad_maximum_fusion.22), channel_id=1, source_target_pairs={{0,4},{1,5},{2,6},{3,7},{4,0},{5,1},{6,2},{7,3},{8,12},{9,13},{10,... | collective-permute-start | bytes 3145736 | tf_op jit(solution)/shard_map/ppermute | solution.py:40
  10.9 13.3 %collective-permute-start.2 = (bf16[512,512]{1,0:T(8,128)(2,1)}, bf16[512,512]{1,0:T(8,128)(2,1)S(1)}, u32[]{:S(2)}, u32[]{:S(2)}) collective-permute-start(bf16[512,512]{1,0:T(8,128)(2,1)} %bitcast.56), channel_id=1, source_target_pairs={{0,24},{8,0},{16,8},{24,16},{1,25},{9,1},{17,9},{25,17},{2,26},{10... | collective-permute-start | bytes 1572872 | tf_op jit(solution)/shard_map/ppermute | solution.py:44
  24.2 13.8 %collective-permute-start.3 = (bf16[512,512]{1,0:T(8,128)(2,1)S(1)}, bf16[512,512]{1,0:T(8,128)(2,1)S(1)}, u32[]{:S(2)}, u32[]{:S(2)}) collective-permute-start(bf16[512,512]{1,0:T(8,128)(2,1)S(1)} %collective-permute-done.2), channel_id=1, source_target_pairs={{0,24},{8,0},{16,8},{24,16},{1,25},{9,1},{17,9},{25,17},{2,26},{10... | collective-permute-start | bytes 1572872 | tf_op jit(solution)/shard_map/ppermute | solution.py:44
  39.9 34.3 %collective-permute-start.4 = (bf16[1536,512]{1,0:T(8,128)(2,1)}, bf16[1536,512]{1,0:T(8,128)(2,1)}, u32[]{:S(2)}, u32[]{:S(2)}) collective-permute-start(bf16[1536,512]{1,0:T(8,128)(2,1)} %get-tuple-element.43), channel_id=1, source_target_pairs={{0,2},{1,3},{2,0},{3,1},{4,6},{5,7},{6,4},{7,5},{8,10},{9,11},{10,... | collective-permute-start | bytes 4718600 | tf_op jit(solution)/shard_map/ppermute | solution.py:40
  40.5 34.0 %collective-permute-start.5 = (bf16[1536,512]{1,0:T(8,128)(2,1)}, bf16[1536,512]{1,0:T(8,128)(2,1)}, u32[]{:S(2)}, u32[]{:S(2)}) collective-permute-start(bf16[1536,512]{1,0:T(8,128)(2,1)} %get-tuple-element.44), channel_id=1, source_target_pairs={{0,4},{1,5},{2,6},{3,7},{4,0},{5,1},{6,2},{7,3},{8,12},{9,13},{10,... | collective-permute-start | bytes 4718600 | tf_op jit(solution)/shard_map/ppermute | solution.py:40
  51.9 79.1 %collective-permute-start.6 = (bf16[4096,512]{1,0:T(8,128)(2,1)}, bf16[4096,512]{1,0:T(8,128)(2,1)}, u32[]{:S(2)}, u32[]{:S(2)}) collective-permute-start(bf16[4096,512]{1,0:T(8,128)(2,1)} %bitcast_dynamic-update-slice_fusion), channel_id=1, source_target_pairs={{0,1},{1,0},{2,3},{3,2},{4,5},{5,4},{6,7},{7,6},{8,9},{9,8},{10,11... | collective-permute-start | bytes 12582920 | tf_op jit(solution)/shard_map/ppermute | solution.py:40
  51.9 16.5 %collective-permute-start.8 = (bf16[512,512]{1,0:T(8,128)(2,1)}, bf16[512,512]{1,0:T(8,128)(2,1)S(1)}, u32[]{:S(2)}, u32[]{:S(2)}) collective-permute-start(bf16[512,512]{1,0:T(8,128)(2,1)} %bitcast.2), channel_id=1, source_target_pairs={{0,24},{8,0},{16,8},{24,16},{1,25},{9,1},{17,9},{25,17},{2,26},{10... | collective-permute-start | bytes 1572872 | tf_op jit(solution)/shard_map/ppermute | solution.py:44
  53.6 26.8 %collective-permute-start.9 = (bf16[512,512]{1,0:T(8,128)(2,1)S(1)}, bf16[512,512]{1,0:T(8,128)(2,1)S(1)}, u32[]{:S(2)}, u32[]{:S(2)}) collective-permute-start(bf16[512,512]{1,0:T(8,128)(2,1)S(1)} %bitcast.57), channel_id=1, source_target_pairs={{0,8},{8,16},{16,24},{24,0},{1,9},{9,17},{17,25},{25,1},{2,10},{10... | collective-permute-start | bytes 1572872 | tf_op jit(solution)/shard_map/ppermute | solution.py:44
  68.4 22.3 %collective-permute-start.10 = (bf16[512,512]{1,0:T(8,128)(2,1)S(1)}, bf16[512,512]{1,0:T(8,128)(2,1)S(1)}, u32[]{:S(2)}, u32[]{:S(2)}) collective-permute-start(bf16[512,512]{1,0:T(8,128)(2,1)S(1)} %collective-permute-done.8), channel_id=1, source_target_pairs={{0,24},{8,0},{16,8},{24,16},{1,25},{9,1},{17,9},{25,17},{2,26},{10... | collective-permute-start | bytes 1572872 | tf_op jit(solution)/shard_map/ppermute | solution.py:44
  91.0 36.3 %collective-permute-start.11 = (bf16[1536,512]{1,0:T(8,128)(2,1)S(1)}, bf16[1536,512]{1,0:T(8,128)(2,1)S(1)}, u32[]{:S(2)}, u32[]{:S(2)}) collective-permute-start(bf16[1536,512]{1,0:T(8,128)(2,1)S(1)} %get-tuple-element.51), channel_id=1, source_target_pairs={{0,2},{1,3},{2,0},{3,1},{4,6},{5,7},{6,4},{7,5},{8,10},{9,11},{10,... | collective-permute-start | bytes 4718600 | tf_op jit(solution)/shard_map/ppermute | solution.py:40
  92.6 35.9 %collective-permute-start.12 = (bf16[1536,512]{1,0:T(8,128)(2,1)S(1)}, bf16[1536,512]{1,0:T(8,128)(2,1)S(1)}, u32[]{:S(2)}, u32[]{:S(2)}) collective-permute-start(bf16[1536,512]{1,0:T(8,128)(2,1)S(1)} %get-tuple-element.52), channel_id=1, source_target_pairs={{0,4},{1,5},{2,6},{3,7},{4,0},{5,1},{6,2},{7,3},{8,12},{9,13},{10,... | collective-permute-start | bytes 4718600 | tf_op jit(solution)/shard_map/ppermute | solution.py:40
  96.3 48.2 %collective-permute-start.13 = (bf16[512,512]{1,0:T(8,128)(2,1)}, bf16[512,512]{1,0:T(8,128)(2,1)S(1)}, u32[]{:S(2)}, u32[]{:S(2)}) collective-permute-start(bf16[512,512]{1,0:T(8,128)(2,1)} %bitcast.2), channel_id=1, source_target_pairs={{0,8},{8,16},{16,24},{24,0},{1,9},{9,17},{17,25},{25,1},{2,10},{10... | collective-permute-start | bytes 1572872 | tf_op jit(solution)/shard_map/ppermute | solution.py:44
  133.8 12.6 %collective-permute-start.7 = (f32[512,512]{1,0:T(8,128)S(1)}, f32[512,512]{1,0:T(8,128)S(1)}, u32[]{:S(2)}, u32[]{:S(2)}) collective-permute-start(f32[512,512]{1,0:T(8,128)S(1)} %fusion.15), channel_id=1, source_target_pairs={{0,1},{1,0},{2,3},{3,2},{4,5},{5,4},{6,7},{7,6},{8,9},{9,8},{10,11... | collective-permute-start | bytes 3145736 | tf_op jit(solution)/shard_map/ppermute | solution.py:40
  136.7 10.7 %collective-permute-start.14 = (f32[512,512]{1,0:T(8,128)S(1)}, f32[512,512]{1,0:T(8,128)S(1)}, u32[]{:S(2)}, u32[]{:S(2)}) collective-permute-start(f32[512,512]{1,0:T(8,128)S(1)} %fusion.7), channel_id=1, source_target_pairs={{0,1},{1,0},{2,3},{3,2},{4,5},{5,4},{6,7},{7,6},{8,9},{9,8},{10,11... | collective-permute-start | bytes 3145736 | tf_op jit(solution)/shard_map/ppermute | solution.py:40
  140.2 10.3 %collective-permute-start.17 = (f32[512,512]{1,0:T(8,128)S(1)}, f32[512,512]{1,0:T(8,128)S(1)}, u32[]{:S(2)}, u32[]{:S(2)}) collective-permute-start(f32[512,512]{1,0:T(8,128)S(1)} %fusion.5), channel_id=1, source_target_pairs={{0,1},{1,0},{2,3},{3,2},{4,5},{5,4},{6,7},{7,6},{8,9},{9,8},{10,11... | collective-permute-start | bytes 3145736 | tf_op jit(solution)/shard_map/ppermute | solution.py:40
  144.1 13.0 %collective-permute-start.29 = (f32[512,512]{1,0:T(8,128)}, f32[512,512]{1,0:T(8,128)}, u32[]{:S(2)}, u32[]{:S(2)}) collective-permute-start(f32[512,512]{1,0:T(8,128)} %fusion.1), channel_id=1, source_target_pairs={{0,1},{1,0},{2,3},{3,2},{4,5},{5,4},{6,7},{7,6},{8,9},{9,8},{10,11... | collective-permute-start | bytes 3145736 | tf_op jit(solution)/shard_map/ppermute | solution.py:40
  148.4 36.7 %collective-permute-start.15 = (bf16[1536,512]{1,0:T(8,128)(2,1)}, bf16[1536,512]{1,0:T(8,128)(2,1)}, u32[]{:S(2)}, u32[]{:S(2)}) collective-permute-start(bf16[1536,512]{1,0:T(8,128)(2,1)} %get-tuple-element.57), channel_id=1, source_target_pairs={{0,2},{1,3},{2,0},{3,1},{4,6},{5,7},{6,4},{7,5},{8,10},{9,11},{10,... | collective-permute-start | bytes 4718600 | tf_op jit(solution)/shard_map/ppermute | solution.py:40
  148.9 36.4 %collective-permute-start.16 = (bf16[1536,512]{1,0:T(8,128)(2,1)}, bf16[1536,512]{1,0:T(8,128)(2,1)}, u32[]{:S(2)}, u32[]{:S(2)}) collective-permute-start(bf16[1536,512]{1,0:T(8,128)(2,1)} %get-tuple-element.58), channel_id=1, source_target_pairs={{0,4},{1,5},{2,6},{3,7},{4,0},{5,1},{6,2},{7,3},{8,12},{9,13},{10,... | collective-permute-start | bytes 4718600 | tf_op jit(solution)/shard_map/ppermute | solution.py:40
  152.6 14.5 %collective-permute-start.18 = (bf16[512,512]{1,0:T(8,128)(2,1)}, bf16[512,512]{1,0:T(8,128)(2,1)}, u32[]{:S(2)}, u32[]{:S(2)}) collective-permute-start(bf16[512,512]{1,0:T(8,128)(2,1)} %add_convert_fusion.3), channel_id=1, source_target_pairs={{0,8},{8,16},{16,24},{24,0},{1,9},{9,17},{17,25},{25,1},{2,10},{10... | collective-permute-start | bytes 1572872 | tf_op jit(solution)/shard_map/ppermute | solution.py:44
  188.4 13.1 %collective-permute-start.19 = (bf16[512,512]{1,0:T(8,128)(2,1)S(1)}, bf16[512,512]{1,0:T(8,128)(2,1)S(1)}, u32[]{:S(2)}, u32[]{:S(2)}) collective-permute-start(bf16[512,512]{1,0:T(8,128)(2,1)S(1)} %get-tuple-element.62), channel_id=1, source_target_pairs={{0,2},{1,3},{2,0},{3,1},{4,6},{5,7},{6,4},{7,5},{8,10},{9,11},{10,... | collective-permute-start | bytes 1572872 | tf_op jit(solution)/shard_map/ppermute | solution.py:40
  189.9 12.4 %collective-permute-start.20 = (bf16[512,512]{1,0:T(8,128)(2,1)S(1)}, bf16[512,512]{1,0:T(8,128)(2,1)S(1)}, u32[]{:S(2)}, u32[]{:S(2)}) collective-permute-start(bf16[512,512]{1,0:T(8,128)(2,1)S(1)} %get-tuple-element.63), channel_id=1, source_target_pairs={{0,4},{1,5},{2,6},{3,7},{4,0},{5,1},{6,2},{7,3},{8,12},{9,13},{10,... | collective-permute-start | bytes 1572872 | tf_op jit(solution)/shard_map/ppermute | solution.py:40
  194.9 17.3 %collective-permute-start.24 = (f32[512,512]{1,0:T(8,128)S(1)}, f32[512,512]{1,0:T(8,128)S(1)}, u32[]{:S(2)}, u32[]{:S(2)}) collective-permute-start(f32[512,512]{1,0:T(8,128)S(1)} %fusion.9), channel_id=1, source_target_pairs={{0,1},{1,0},{2,3},{3,2},{4,5},{5,4},{6,7},{7,6},{8,9},{9,8},{10,11... | collective-permute-start | bytes 3145736 | tf_op jit(solution)/shard_map/ppermute | solution.py:40
  195.0 21.1 %collective-permute-start.30 = (bf16[512,512]{1,0:T(8,128)(2,1)S(1)}, bf16[512,512]{1,0:T(8,128)(2,1)S(1)}, u32[]{:S(2)}, u32[]{:S(2)}) collective-permute-start(bf16[512,512]{1,0:T(8,128)(2,1)S(1)} %fusion.19), channel_id=1, source_target_pairs={{0,8},{8,16},{16,24},{24,0},{1,9},{9,17},{17,25},{25,1},{2,10},{10... | collective-permute-start | bytes 1572872 | tf_op jit(solution)/shard_map/ppermute | solution.py:44
  201.3 8.1 %collective-permute-start.27 = (f32[512,512]{1,0:T(8,128)S(1)}, f32[512,512]{1,0:T(8,128)S(1)}, u32[]{:S(2)}, u32[]{:S(2)}) collective-permute-start(f32[512,512]{1,0:T(8,128)S(1)} %fusion.3), channel_id=1, source_target_pairs={{0,1},{1,0},{2,3},{3,2},{4,5},{5,4},{6,7},{7,6},{8,9},{9,8},{10,11... | collective-permute-start | bytes 3145736 | tf_op jit(solution)/shard_map/ppermute | solution.py:40
  205.9 7.7 %collective-permute-start.23 = (f32[512,512]{1,0:T(8,128)S(1)}, f32[512,512]{1,0:T(8,128)S(1)}, u32[]{:S(2)}, u32[]{:S(2)}) collective-permute-start(f32[512,512]{1,0:T(8,128)S(1)} %fusion.11), channel_id=1, source_target_pairs={{0,1},{1,0},{2,3},{3,2},{4,5},{5,4},{6,7},{7,6},{8,9},{9,8},{10,11... | collective-permute-start | bytes 3145736 | tf_op jit(solution)/shard_map/ppermute | solution.py:40
  209.0 5.9 %collective-permute-start.21 = (f32[512,512]{1,0:T(8,128)S(1)}, f32[512,512]{1,0:T(8,128)S(1)}, u32[]{:S(2)}, u32[]{:S(2)}) collective-permute-start(f32[512,512]{1,0:T(8,128)S(1)} %fusion.13), channel_id=1, source_target_pairs={{0,1},{1,0},{2,3},{3,2},{4,5},{5,4},{6,7},{7,6},{8,9},{9,8},{10,11... | collective-permute-start | bytes 3145736 | tf_op jit(solution)/shard_map/ppermute | solution.py:40
  210.7 15.6 %collective-permute-start.28 = (bf16[512,512]{1,0:T(8,128)(2,1)S(1)}, bf16[512,512]{1,0:T(8,128)(2,1)S(1)}, u32[]{:S(2)}, u32[]{:S(2)}) collective-permute-start(bf16[512,512]{1,0:T(8,128)(2,1)S(1)} %add_convert_fusion.1), channel_id=1, source_target_pairs={{0,24},{8,0},{16,8},{24,16},{1,25},{9,1},{17,9},{25,17},{2,26},{10... | collective-permute-start | bytes 1572872 | tf_op jit(solution)/shard_map/ppermute | solution.py:44
  227.3 14.2 %collective-permute-start.25 = (bf16[512,512]{1,0:T(8,128)(2,1)S(1)}, bf16[512,512]{1,0:T(8,128)(2,1)S(1)}, u32[]{:S(2)}, u32[]{:S(2)}) collective-permute-start(bf16[512,512]{1,0:T(8,128)(2,1)S(1)} %add_convert_fusion.2), channel_id=1, source_target_pairs={{0,8},{8,16},{16,24},{24,0},{1,9},{9,17},{17,25},{25,1},{2,10},{10... | collective-permute-start | bytes 1572872 | tf_op jit(solution)/shard_map/ppermute | solution.py:44
  241.6 13.8 %collective-permute-start.26 = (bf16[512,512]{1,0:T(8,128)(2,1)S(1)}, bf16[512,512]{1,0:T(8,128)(2,1)S(1)}, u32[]{:S(2)}, u32[]{:S(2)}) collective-permute-start(bf16[512,512]{1,0:T(8,128)(2,1)S(1)} %broadcast_select_fusion), channel_id=1, source_target_pairs={{0,8},{8,16},{16,24},{24,0},{1,9},{9,17},{17,25},{25,1},{2,10},{10... | collective-permute-start | bytes 1572872 | tf_op jit(solution)/shard_map/ppermute | solution.py:44
  244.1 23.9 %collective-permute-start.22 = (bf16[512,512]{1,0:T(8,128)(2,1)S(1)}, bf16[512,512]{1,0:T(8,128)(2,1)S(1)}, u32[]{:S(2)}, u32[]{:S(2)}) collective-permute-start(bf16[512,512]{1,0:T(8,128)(2,1)S(1)} %fusion.17), channel_id=1, source_target_pairs={{0,24},{8,0},{16,8},{24,16},{1,25},{9,1},{17,9},{25,17},{2,26},{10... | collective-permute-start | bytes 1572872 | tf_op jit(solution)/shard_map/ppermute | solution.py:44
  (36 other events, 651.2 us)
Sparse Core Ops, SparseCore 0:
  227.4 39.5 all-gather.1

commit v15 on v14

--- a/solution.py
+++ b/solution.py
@@ -63,7 +63,7 @@
     found = [0, X, Y, X + Y]
     held = (basis_in_held[0], basis_out_held[0])
     ours = [in_order(block, column, found) for block in held]
-    theirs = jnp.split(swap(jnp.concatenate([in_order(block, column, [CORE + i for i in found]) for block in held]), CORE), 2)
+    theirs = [swap(in_order(block, column, [CORE + i for i in found]), CORE) for block in held]
 
     pieces = {(0, 0): own[0], (1, 0): own[1]}
     rotated = {}
@@ -120,7 +120,7 @@
 
     stacks, evens = {}, {}
     due = slot(0, [])
-    due += [fetch(0, 1, []), fetch(0, 2, [])]
+    due += [fetch(0, 1, []), fetch(0, 2, [])] + theirs
 
     gate, due = due, slot(1, due)
     due += [fetch(0, 3, gate), fetch(1, 1, gate), fetch(1, 2, gate)]

time: 286 us -> 263 us (0.920)
  matrix products: 45.3 us -> 32.5 us
  local copies, waits for them, and re-layouts: 22.2 us -> 13 us
  waiting for transfers between devices: 152 us -> 159 us
  other arithmetic: 12 us -> 7.97 us
  starting transfers between devices: 36.8 us -> 33.2 us
    dot_general x16, matrix products: 36.7 us -> 23.8 us  [dot(): return jnp.dot(a, b, preferred_element_type=jnp.float32)]
    ppermute x12, waiting for transfers between devices: 94.6 us -> 104 us  [shift(): return lax.ppermute(block, 'dp', [(z, (z + by) % n) for z in range(n)])]
    unnamed x79 -> x70, local copies, waits for them, and re-layouts: 10.2 us -> 3.16 us
    ppermute x12, starting transfers between devices: 22.5 us -> 17.8 us  [shift(): return lax.ppermute(block, 'dp', [(z, (z + by) % n) for z in range(n)])]
    ppermute x19 -> x20, waiting for transfers between devices: 57.4 us -> 54.6 us  [swap(): lax.ppermute(block, 'tensor', [(j, j ^ bit) for j in range(X + Y + CORE +...]
    ppermute x19 -> x20, starting transfers between devices: 14.3 us -> 15.4 us  [swap(): lax.ppermute(block, 'tensor', [(j, j ^ bit) for j in range(X + Y + CORE +...]
  transfers between devices with their start and end apart: 32 -> 33, of which waited for: 19 -> 18; matrix products, arithmetic and copies ran while one was open for 22% -> 14% of each run, Pallas kernels for 0% -> 0%
where the time goes in v15:
time: 263 us; the launch traced here: 261 us
  waiting for transfers between devices  159 us (60%)
  starting transfers between devices  33.2 us (13%)
  matrix products  32.5 us (12%)
  between operations  15.3 us (6%)
  local copies, waits for them, and re-layouts  13 us (5%)
  other arithmetic  7.97 us (3%)
    ppermute x12, waiting for transfers between devices, shift(): return lax.ppermute(block, 'dp', [(z, (z + by) % n) for z in range(n)])  104 us
    ppermute x20, waiting for transfers between devices, swap(): lax.ppermute(block, 'tensor', [(j, j ^ bit) for j in range(X + Y + CORE +...  54.6 us
    dot_general x16, matrix products, dot(): return jnp.dot(a, b, preferred_element_type=jnp.float32)  23.8 us
    ppermute x12, starting transfers between devices, shift(): return lax.ppermute(block, 'dp', [(z, (z + by) % n) for z in range(n)])  17.8 us
    ppermute x20, starting transfers between devices, swap(): lax.ppermute(block, 'tensor', [(j, j ^ bit) for j in range(X + Y + CORE +...  15.4 us
    dot_general x1, matrix products, product_and_divide(): lax.dot_general(rot_out, all_rot_in, contract, preferred_element_type=jnp...  8.7 us
  transfers between devices with their start and end apart: 33, of which 18 were waited for; matrix products, arithmetic and copies ran while one was open for 14% of the time, Pallas kernels for 0%

profile of v15, /device:TPU:16, one launch (start us, length us, event | category | flops | bytes accessed | tf_op | source)
XLA Modules:
  0.0 260.7 jit_solution(17365680496431471955)
XLA Ops:
  6.5 3.9 %dynamic-slice_bitcast_fusion.3 = (bf16[512,512]{1,0:T(8,128)(2,1)S(1)}, bf16[512,512]{1,0:T(8,128)(2,1)S(1)}, bf16[512,512]{1,0:T(8,128)(2,1)S(1)}, bf16[512,51...) fusion(bf16[1,4096,512]{2,1,0:T(8,128)(2,1)} %param.8, ...), kind=kLoop, calls=%fused_computation.44 | loop fusion | bytes 16777248 | tf_op jit(solution)/shard_map/dynamic_slice | solution.py:49
  12.8 1.6 collective-permute-start
  14.4 1.5 collective-permute-start.1
  16.4 13.0 %collective-permute-done.2 = bf16[512,512]{1,0:T(8,128)(2,1)S(1)} collective-permute-done((bf16[512,512]{1,0:T(8,128)(2,1)S(1)}, bf16[512,512]{1,0:T(8,128)(2,1)S(1)}, u32[]{:S(2)}, u32[]{:S(2)}) %collective-permute-start.2) | collective-permute-done | bytes 524320 | tf_op jit(solution)/shard_map/ppermute | solution.py:44
  29.8 8.3 %collective-permute-done = bf16[1024,512]{1,0:T(8,128)(2,1)S(1)} collective-permute-done((bf16[1024,512]{1,0:T(8,128)(2,1)S(1)}, bf16[1024,512]{1,0:T(8,128)(2,1)S(1)}, u32[]{:S(2)}, u32[]{:S(2)}) %collective-permute-start) | collective-permute-done | bytes 1048608 | tf_op jit(solution)/shard_map/ppermute | solution.py:40
  39.5 4.0 %collective-permute-done.3 = bf16[512,512]{1,0:T(8,128)(2,1)S(1)} collective-permute-done((bf16[512,512]{1,0:T(8,128)(2,1)S(1)}, bf16[512,512]{1,0:T(8,128)(2,1)S(1)}, u32[]{:S(2)}, u32[]{:S(2)}) %collective-permute-start.3) | collective-permute-done | bytes 524320 | tf_op jit(solution)/shard_map/ppermute | solution.py:44
  44.9 3.5 %collective-permute-start.10 = (bf16[512,512]{1,0:T(8,128)(2,1)S(1)}, bf16[512,512]{1,0:T(8,128)(2,1)S(1)}, u32[]{:S(2)}, u32[]{:S(2)}) collective-permute-start(bf16[512,512]{1,0:T(8,128)(2,1)S(1)} %bitcast.65), channel_id=1, source_target_pairs={{0,8},{8,16},{16,24},{24,0},{1,9},{9,17},{17,25},{25,1},{2,10},{10... | collective-permute-start | bytes 1572872 | tf_op jit(solution)/shard_map/ppermute | solution.py:44
  48.4 12.8 %collective-permute-done.9 = bf16[512,512]{1,0:T(8,128)(2,1)S(1)} collective-permute-done((bf16[512,512]{1,0:T(8,128)(2,1)S(1)}, bf16[512,512]{1,0:T(8,128)(2,1)S(1)}, u32[]{:S(2)}, u32[]{:S(2)}) %collective-permute-start.9) | collective-permute-done | bytes 524320 | tf_op jit(solution)/shard_map/ppermute | solution.py:44
  61.3 8.7 %collective-permute-done.10 = bf16[512,512]{1,0:T(8,128)(2,1)S(1)} collective-permute-done((bf16[512,512]{1,0:T(8,128)(2,1)S(1)}, bf16[512,512]{1,0:T(8,128)(2,1)S(1)}, u32[]{:S(2)}, u32[]{:S(2)}) %collective-permute-start.10) | collective-permute-done | bytes 524320 | tf_op jit(solution)/shard_map/ppermute | solution.py:44
  70.0 10.2 %collective-permute-done.11 = bf16[512,512]{1,0:T(8,128)(2,1)S(1)} collective-permute-done((bf16[512,512]{1,0:T(8,128)(2,1)S(1)}, bf16[512,512]{1,0:T(8,128)(2,1)S(1)}, u32[]{:S(2)}, u32[]{:S(2)}) %collective-permute-start.11) | collective-permute-done | bytes 524320 | tf_op jit(solution)/shard_map/ppermute | solution.py:44
  80.3 6.7 %collective-permute-start.14 = (bf16[512,512]{1,0:T(8,128)(2,1)S(1)}, bf16[512,512]{1,0:T(8,128)(2,1)S(1)}, u32[]{:S(2)}, u32[]{:S(2)}) collective-permute-start(bf16[512,512]{1,0:T(8,128)(2,1)S(1)} %bitcast.69), channel_id=1, source_target_pairs={{0,8},{8,16},{16,24},{24,0},{1,9},{9,17},{17,25},{25,1},{2,10},{10... | collective-permute-start | bytes 1572872 | tf_op jit(solution)/shard_map/ppermute | solution.py:44
  88.1 1.6 collective-permute-start.12
  89.6 1.6 collective-permute-start.13
  96.9 20.5 %collective-permute-done.12 = bf16[1536,512]{1,0:T(8,128)(2,1)S(1)} collective-permute-done((bf16[1536,512]{1,0:T(8,128)(2,1)S(1)}, bf16[1536,512]{1,0:T(8,128)(2,1)S(1)}, u32[]{:S(2)}, u32[]{:S(2)}) %collective-permute-start.12) | collective-permute-done | bytes 1572896 | tf_op jit(solution)/shard_map/ppermute | solution.py:40
  124.4 2.2 fusion.29
  127.1 1.9 pad_maximum_fusion.20
  129.6 1.5 collective-permute-start.17
  131.1 2.1 add_convert_fusion.3
  134.8 12.0 %collective-permute-done.19 = bf16[512,512]{1,0:T(8,128)(2,1)} collective-permute-done((bf16[512,512]{1,0:T(8,128)(2,1)}, bf16[512,512]{1,0:T(8,128)(2,1)}, u32[]{:S(2)}, u32[]{:S(2)}) %collective-permute-start.19) | collective-permute-done | bytes 524320 | tf_op jit(solution)/shard_map/ppermute | solution.py:44
  146.8 3.3 %fusion.3 = bf16[512,512]{1,0:T(8,128)(2,1)S(1)} fusion(bf16[512,512]{1,0:T(8,128)(2,1)} %collective-permute-done.19, f32[512,512]{1,0:T(8,128)} %collective-permute-done.30, pred[]{:T(512)S(6)} %eq.19, bf16[512,2048]{1,0:T(8,128)(2,1)S(1)} %pad_maximum_fusion.6, bf16[512,512]{1,0:T(8,128)(2,1)} %copy-done.25, bf16[512,512]{1,0:T(8,128)(2,1)} %copy-done.27, ...), kind=kOutput, calls=%fused_computation.37 | convolution fusion | flops 1082916864 | bytes 6291457 | tf_op jit(solution)/shard_map/dot_general | solution.py:22
  150.1 15.6 %collective-permute-done.16 = bf16[1536,512]{1,0:T(8,128)(2,1)} collective-permute-done((bf16[1536,512]{1,0:T(8,128)(2,1)}, bf16[1536,512]{1,0:T(8,128)(2,1)}, u32[]{:S(2)}, u32[]{:S(2)}) %collective-permute-start.16) | collective-permute-done | bytes 1572896 | tf_op jit(solution)/shard_map/ppermute | solution.py:40
  167.7 1.5 fusion.15
  170.9 1.5 collective-permute-start.20
  177.0 6.4 %collective-permute-done.20 = bf16[512,512]{1,0:T(8,128)(2,1)S(1)} collective-permute-done((bf16[512,512]{1,0:T(8,128)(2,1)S(1)}, bf16[512,512]{1,0:T(8,128)(2,1)S(1)}, u32[]{:S(2)}, u32[]{:S(2)}) %collective-permute-start.20) | collective-permute-done | bytes 524320 | tf_op jit(solution)/shard_map/ppermute | solution.py:40
  190.4 1.8 collective-permute-start.29
  196.0 8.3 %collective-permute-done.29 = bf16[512,512]{1,0:T(8,128)(2,1)S(1)} collective-permute-done((bf16[512,512]{1,0:T(8,128)(2,1)S(1)}, bf16[512,512]{1,0:T(8,128)(2,1)S(1)}, u32[]{:S(2)}, u32[]{:S(2)}) %collective-permute-start.29) | collective-permute-done | bytes 524320 | tf_op jit(solution)/shard_map/ppermute | solution.py:44
  205.3 2.1 collective-permute-start.26
  208.1 10.3 %collective-permute-done.26 = bf16[512,512]{1,0:T(8,128)(2,1)S(1)} collective-permute-done((bf16[512,512]{1,0:T(8,128)(2,1)S(1)}, bf16[512,512]{1,0:T(8,128)(2,1)S(1)}, u32[]{:S(2)}, u32[]{:S(2)}) %collective-permute-start.26) | collective-permute-done | bytes 524320 | tf_op jit(solution)/shard_map/ppermute | solution.py:44
  218.4 2.1 collective-permute-start.27
  220.6 10.3 %collective-permute-done.27 = bf16[512,512]{1,0:T(8,128)(2,1)S(1)} collective-permute-done((bf16[512,512]{1,0:T(8,128)(2,1)S(1)}, bf16[512,512]{1,0:T(8,128)(2,1)S(1)}, u32[]{:S(2)}, u32[]{:S(2)}) %collective-permute-start.27) | collective-permute-done | bytes 524320 | tf_op jit(solution)/shard_map/ppermute | solution.py:44
  230.8 14.3 %collective-permute-done.23 = bf16[512,512]{1,0:T(8,128)(2,1)S(1)} collective-permute-done((bf16[512,512]{1,0:T(8,128)(2,1)S(1)}, bf16[512,512]{1,0:T(8,128)(2,1)S(1)}, u32[]{:S(2)}, u32[]{:S(2)}) %collective-permute-start.23) | collective-permute-done | bytes 524320 | tf_op jit(solution)/shard_map/ppermute | solution.py:44
  245.2 8.7 %fusion = bf16[1,512,4096]{2,1,0:T(8,128)(2,1)} fusion(bf16[512,4096]{1,0:T(8,128)(2,1)} %param.11, bf16[512,4096]{1,0:T(8,128)(2,1)} %all-gather.2.cloned.1.call-done, bf16[512,512]{1,0:T(8,128)(2,1)S(1)} %copy-done.29, bf16[512,512]{1,0:T(8,128)(2,1)S(1)} %collective-permute-done.23, bf16[512,512]{1,0:T(8,128)(2,1)S(1)} %collective-permute-done.27, ...), kind=kOutput, calls=%fused_computation.1 | convolution fusion | flops 2158493696 | bytes 14155778 | tf_op jit(solution)/shard_map/dot_general | solution.py:13
  (149 shorter events, 41.3 us)
Async XLA Ops:
  6.5 238.7 %all-gather.2.cloned.1.call-start = ((), (), s32[]{:S(2)}) async-start(), calls=%async_computation | async-start | bytes 4718592 | tf_op jit(solution)/shard_map/all_gather | solution.py:147
  10.7 33.1 %collective-permute-start.5 = (bf16[2048,512]{1,0:T(8,128)(2,1)S(1)}, bf16[2048,512]{1,0:T(8,128)(2,1)S(1)}, u32[]{:S(2)}, u32[]{:S(2)}) collective-permute-start(bf16[2048,512]{1,0:T(8,128)(2,1)S(1)} %pad_maximum_fusion.1), channel_id=1, source_target_pairs={{0,1},{1,0},{2,3},{3,2},{4,5},{5,4},{6,7},{7,6},{8,9},{9,8},{10,11... | collective-permute-start | bytes 6291464 | tf_op jit(solution)/shard_map/ppermute | solution.py:40
  10.9 32.8 %collective-permute-start.4 = (bf16[2048,512]{1,0:T(8,128)(2,1)S(1)}, bf16[2048,512]{1,0:T(8,128)(2,1)S(1)}, u32[]{:S(2)}, u32[]{:S(2)}) collective-permute-start(bf16[2048,512]{1,0:T(8,128)(2,1)S(1)} %pad_maximum_fusion), channel_id=1, source_target_pairs={{0,1},{1,0},{2,3},{3,2},{4,5},{5,4},{6,7},{7,6},{8,9},{9,8},{10,11... | collective-permute-start | bytes 6291464 | tf_op jit(solution)/shard_map/ppermute | solution.py:40
  12.8 25.3 %collective-permute-start = (bf16[1024,512]{1,0:T(8,128)(2,1)S(1)}, bf16[1024,512]{1,0:T(8,128)(2,1)S(1)}, u32[]{:S(2)}, u32[]{:S(2)}) collective-permute-start(bf16[1024,512]{1,0:T(8,128)(2,1)S(1)} %pad_maximum_fusion.24), channel_id=1, source_target_pairs={{0,2},{1,3},{2,0},{3,1},{4,6},{5,7},{6,4},{7,5},{8,10},{9,11},{10,... | collective-permute-start | bytes 3145736 | tf_op jit(solution)/shard_map/ppermute | solution.py:40
  14.4 25.0 %collective-permute-start.1 = (bf16[1024,512]{1,0:T(8,128)(2,1)S(1)}, bf16[1024,512]{1,0:T(8,128)(2,1)S(1)}, u32[]{:S(2)}, u32[]{:S(2)}) collective-permute-start(bf16[1024,512]{1,0:T(8,128)(2,1)S(1)} %pad_maximum_fusion.24), channel_id=1, source_target_pairs={{0,4},{1,5},{2,6},{3,7},{4,0},{5,1},{6,2},{7,3},{8,12},{9,13},{10,... | collective-permute-start | bytes 3145736 | tf_op jit(solution)/shard_map/ppermute | solution.py:40
  15.9 13.4 %collective-permute-start.2 = (bf16[512,512]{1,0:T(8,128)(2,1)S(1)}, bf16[512,512]{1,0:T(8,128)(2,1)S(1)}, u32[]{:S(2)}, u32[]{:S(2)}) collective-permute-start(bf16[512,512]{1,0:T(8,128)(2,1)S(1)} %bitcast.64), channel_id=1, source_target_pairs={{0,24},{8,0},{16,8},{24,16},{1,25},{9,1},{17,9},{25,17},{2,26},{10... | collective-permute-start | bytes 1572872 | tf_op jit(solution)/shard_map/ppermute | solution.py:44
  29.4 14.2 %collective-permute-start.3 = (bf16[512,512]{1,0:T(8,128)(2,1)S(1)}, bf16[512,512]{1,0:T(8,128)(2,1)S(1)}, u32[]{:S(2)}, u32[]{:S(2)}) collective-permute-start(bf16[512,512]{1,0:T(8,128)(2,1)S(1)} %collective-permute-done.2), channel_id=1, source_target_pairs={{0,24},{8,0},{16,8},{24,16},{1,25},{9,1},{17,9},{25,17},{2,26},{10... | collective-permute-start | bytes 1572872 | tf_op jit(solution)/shard_map/ppermute | solution.py:44
  43.8 36.5 %collective-permute-start.6 = (bf16[1536,512]{1,0:T(8,128)(2,1)S(1)}, bf16[1536,512]{1,0:T(8,128)(2,1)S(1)}, u32[]{:S(2)}, u32[]{:S(2)}) collective-permute-start(bf16[1536,512]{1,0:T(8,128)(2,1)S(1)} %get-tuple-element.43), channel_id=1, source_target_pairs={{0,2},{1,3},{2,0},{3,1},{4,6},{5,7},{6,4},{7,5},{8,10},{9,11},{10,... | collective-permute-start | bytes 4718600 | tf_op jit(solution)/shard_map/ppermute | solution.py:40
  44.4 35.9 %collective-permute-start.7 = (bf16[1536,512]{1,0:T(8,128)(2,1)S(1)}, bf16[1536,512]{1,0:T(8,128)(2,1)S(1)}, u32[]{:S(2)}, u32[]{:S(2)}) collective-permute-start(bf16[1536,512]{1,0:T(8,128)(2,1)S(1)} %get-tuple-element.44), channel_id=1, source_target_pairs={{0,4},{1,5},{2,6},{3,7},{4,0},{5,1},{6,2},{7,3},{8,12},{9,13},{10,... | collective-permute-start | bytes 4718600 | tf_op jit(solution)/shard_map/ppermute | solution.py:40
  44.9 16.4 %collective-permute-start.9 = (bf16[512,512]{1,0:T(8,128)(2,1)S(1)}, bf16[512,512]{1,0:T(8,128)(2,1)S(1)}, u32[]{:S(2)}, u32[]{:S(2)}) collective-permute-start(bf16[512,512]{1,0:T(8,128)(2,1)S(1)} %bitcast.68), channel_id=1, source_target_pairs={{0,24},{8,0},{16,8},{24,16},{1,25},{9,1},{17,9},{25,17},{2,26},{10... | collective-permute-start | bytes 1572872 | tf_op jit(solution)/shard_map/ppermute | solution.py:44
  44.9 25.1 %collective-permute-start.10 = (bf16[512,512]{1,0:T(8,128)(2,1)S(1)}, bf16[512,512]{1,0:T(8,128)(2,1)S(1)}, u32[]{:S(2)}, u32[]{:S(2)}) collective-permute-start(bf16[512,512]{1,0:T(8,128)(2,1)S(1)} %bitcast.65), channel_id=1, source_target_pairs={{0,8},{8,16},{16,24},{24,0},{1,9},{9,17},{17,25},{25,1},{2,10},{10... | collective-permute-start | bytes 1572872 | tf_op jit(solution)/shard_map/ppermute | solution.py:44
  61.3 19.0 %collective-permute-start.11 = (bf16[512,512]{1,0:T(8,128)(2,1)S(1)}, bf16[512,512]{1,0:T(8,128)(2,1)S(1)}, u32[]{:S(2)}, u32[]{:S(2)}) collective-permute-start(bf16[512,512]{1,0:T(8,128)(2,1)S(1)} %collective-permute-done.9), channel_id=1, source_target_pairs={{0,24},{8,0},{16,8},{24,16},{1,25},{9,1},{17,9},{25,17},{2,26},{10... | collective-permute-start | bytes 1572872 | tf_op jit(solution)/shard_map/ppermute | solution.py:44
  80.3 46.9 %collective-permute-start.14 = (bf16[512,512]{1,0:T(8,128)(2,1)S(1)}, bf16[512,512]{1,0:T(8,128)(2,1)S(1)}, u32[]{:S(2)}, u32[]{:S(2)}) collective-permute-start(bf16[512,512]{1,0:T(8,128)(2,1)S(1)} %bitcast.69), channel_id=1, source_target_pairs={{0,8},{8,16},{16,24},{24,0},{1,9},{9,17},{17,25},{25,1},{2,10},{10... | collective-permute-start | bytes 1572872 | tf_op jit(solution)/shard_map/ppermute | solution.py:44
  88.1 29.3 %collective-permute-start.12 = (bf16[1536,512]{1,0:T(8,128)(2,1)S(1)}, bf16[1536,512]{1,0:T(8,128)(2,1)S(1)}, u32[]{:S(2)}, u32[]{:S(2)}) collective-permute-start(bf16[1536,512]{1,0:T(8,128)(2,1)S(1)} %get-tuple-element.51), channel_id=1, source_target_pairs={{0,2},{1,3},{2,0},{3,1},{4,6},{5,7},{6,4},{7,5},{8,10},{9,11},{10,... | collective-permute-start | bytes 4718600 | tf_op jit(solution)/shard_map/ppermute | solution.py:40
  89.6 29.0 %collective-permute-start.13 = (bf16[1536,512]{1,0:T(8,128)(2,1)S(1)}, bf16[1536,512]{1,0:T(8,128)(2,1)S(1)}, u32[]{:S(2)}, u32[]{:S(2)}) collective-permute-start(bf16[1536,512]{1,0:T(8,128)(2,1)S(1)} %get-tuple-element.52), channel_id=1, source_target_pairs={{0,4},{1,5},{2,6},{3,7},{4,0},{5,1},{6,2},{7,3},{8,12},{9,13},{10,... | collective-permute-start | bytes 4718600 | tf_op jit(solution)/shard_map/ppermute | solution.py:40
  92.5 30.0 %collective-permute-start.15 = (f32[512,512]{1,0:T(8,128)S(1)}, f32[512,512]{1,0:T(8,128)S(1)}, u32[]{:S(2)}, u32[]{:S(2)}) collective-permute-start(f32[512,512]{1,0:T(8,128)S(1)} %fusion.23), channel_id=1, source_target_pairs={{0,1},{1,0},{2,3},{3,2},{4,5},{5,4},{6,7},{7,6},{8,9},{9,8},{10,11... | collective-permute-start | bytes 3145736 | tf_op jit(solution)/shard_map/ppermute | solution.py:40
  93.8 29.6 %collective-permute-start.8 = (f32[512,512]{1,0:T(8,128)S(1)}, f32[512,512]{1,0:T(8,128)S(1)}, u32[]{:S(2)}, u32[]{:S(2)}) collective-permute-start(f32[512,512]{1,0:T(8,128)S(1)} %fusion.22), channel_id=1, source_target_pairs={{0,1},{1,0},{2,3},{3,2},{4,5},{5,4},{6,7},{7,6},{8,9},{9,8},{10,11... | collective-permute-start | bytes 3145736 | tf_op jit(solution)/shard_map/ppermute | solution.py:40
  122.3 8.8 %collective-permute-start.18 = (f32[512,512]{1,0:T(8,128)S(1)}, f32[512,512]{1,0:T(8,128)S(1)}, u32[]{:S(2)}, u32[]{:S(2)}) collective-permute-start(f32[512,512]{1,0:T(8,128)S(1)} %fusion.24), channel_id=1, source_target_pairs={{0,1},{1,0},{2,3},{3,2},{4,5},{5,4},{6,7},{7,6},{8,9},{9,8},{10,11... | collective-permute-start | bytes 3145736 | tf_op jit(solution)/shard_map/ppermute | solution.py:40
  126.6 8.1 %collective-permute-start.30 = (f32[512,512]{1,0:T(8,128)}, f32[512,512]{1,0:T(8,128)}, u32[]{:S(2)}, u32[]{:S(2)}) collective-permute-start(f32[512,512]{1,0:T(8,128)} %fusion.29), channel_id=1, source_target_pairs={{0,1},{1,0},{2,3},{3,2},{4,5},{5,4},{6,7},{7,6},{8,9},{9,8},{10,11... | collective-permute-start | bytes 3145736 | tf_op jit(solution)/shard_map/ppermute | solution.py:40
  129.0 36.6 %collective-permute-start.16 = (bf16[1536,512]{1,0:T(8,128)(2,1)}, bf16[1536,512]{1,0:T(8,128)(2,1)}, u32[]{:S(2)}, u32[]{:S(2)}) collective-permute-start(bf16[1536,512]{1,0:T(8,128)(2,1)} %get-tuple-element.57), channel_id=1, source_target_pairs={{0,2},{1,3},{2,0},{3,1},{4,6},{5,7},{6,4},{7,5},{8,10},{9,11},{10,... | collective-permute-start | bytes 4718600 | tf_op jit(solution)/shard_map/ppermute | solution.py:40
  129.6 36.4 %collective-permute-start.17 = (bf16[1536,512]{1,0:T(8,128)(2,1)}, bf16[1536,512]{1,0:T(8,128)(2,1)}, u32[]{:S(2)}, u32[]{:S(2)}) collective-permute-start(bf16[1536,512]{1,0:T(8,128)(2,1)} %get-tuple-element.58), channel_id=1, source_target_pairs={{0,4},{1,5},{2,6},{3,7},{4,0},{5,1},{6,2},{7,3},{8,12},{9,13},{10,... | collective-permute-start | bytes 4718600 | tf_op jit(solution)/shard_map/ppermute | solution.py:40
  133.2 13.6 %collective-permute-start.19 = (bf16[512,512]{1,0:T(8,128)(2,1)}, bf16[512,512]{1,0:T(8,128)(2,1)}, u32[]{:S(2)}, u32[]{:S(2)}) collective-permute-start(bf16[512,512]{1,0:T(8,128)(2,1)} %add_convert_fusion.3), channel_id=1, source_target_pairs={{0,8},{8,16},{16,24},{24,0},{1,9},{9,17},{17,25},{25,1},{2,10},{10... | collective-permute-start | bytes 1572872 | tf_op jit(solution)/shard_map/ppermute | solution.py:44
  165.9 30.1 %collective-permute-start.31 = (bf16[512,512]{1,0:T(8,128)(2,1)S(1)}, bf16[512,512]{1,0:T(8,128)(2,1)S(1)}, u32[]{:S(2)}, u32[]{:S(2)}) collective-permute-start(bf16[512,512]{1,0:T(8,128)(2,1)S(1)} %fusion.3), channel_id=1, source_target_pairs={{0,8},{8,16},{16,24},{24,0},{1,9},{9,17},{17,25},{25,1},{2,10},{10... | collective-permute-start | bytes 1572872 | tf_op jit(solution)/shard_map/ppermute | solution.py:44
  170.9 12.5 %collective-permute-start.20 = (bf16[512,512]{1,0:T(8,128)(2,1)S(1)}, bf16[512,512]{1,0:T(8,128)(2,1)S(1)}, u32[]{:S(2)}, u32[]{:S(2)}) collective-permute-start(bf16[512,512]{1,0:T(8,128)(2,1)S(1)} %get-tuple-element.62), channel_id=1, source_target_pairs={{0,2},{1,3},{2,0},{3,1},{4,6},{5,7},{6,4},{7,5},{8,10},{9,11},{10,... | collective-permute-start | bytes 1572872 | tf_op jit(solution)/shard_map/ppermute | solution.py:40
  172.4 12.1 %collective-permute-start.21 = (bf16[512,512]{1,0:T(8,128)(2,1)S(1)}, bf16[512,512]{1,0:T(8,128)(2,1)S(1)}, u32[]{:S(2)}, u32[]{:S(2)}) collective-permute-start(bf16[512,512]{1,0:T(8,128)(2,1)S(1)} %get-tuple-element.63), channel_id=1, source_target_pairs={{0,4},{1,5},{2,6},{3,7},{4,0},{5,1},{6,2},{7,3},{8,12},{9,13},{10,... | collective-permute-start | bytes 1572872 | tf_op jit(solution)/shard_map/ppermute | solution.py:40
  175.1 17.1 %collective-permute-start.25 = (f32[512,512]{1,0:T(8,128)S(1)}, f32[512,512]{1,0:T(8,128)S(1)}, u32[]{:S(2)}, u32[]{:S(2)}) collective-permute-start(f32[512,512]{1,0:T(8,128)S(1)} %fusion.27), channel_id=1, source_target_pairs={{0,1},{1,0},{2,3},{3,2},{4,5},{5,4},{6,7},{7,6},{8,9},{9,8},{10,11... | collective-permute-start | bytes 3145736 | tf_op jit(solution)/shard_map/ppermute | solution.py:40
  176.5 12.6 %collective-permute-start.28 = (f32[512,512]{1,0:T(8,128)S(1)}, f32[512,512]{1,0:T(8,128)S(1)}, u32[]{:S(2)}, u32[]{:S(2)}) collective-permute-start(f32[512,512]{1,0:T(8,128)S(1)} %fusion.28), channel_id=1, source_target_pairs={{0,1},{1,0},{2,3},{3,2},{4,5},{5,4},{6,7},{7,6},{8,9},{9,8},{10,11... | collective-permute-start | bytes 3145736 | tf_op jit(solution)/shard_map/ppermute | solution.py:40
  187.2 6.3 %collective-permute-start.24 = (f32[512,512]{1,0:T(8,128)S(1)}, f32[512,512]{1,0:T(8,128)S(1)}, u32[]{:S(2)}, u32[]{:S(2)}) collective-permute-start(f32[512,512]{1,0:T(8,128)S(1)} %fusion.26), channel_id=1, source_target_pairs={{0,1},{1,0},{2,3},{3,2},{4,5},{5,4},{6,7},{7,6},{8,9},{9,8},{10,11... | collective-permute-start | bytes 3145736 | tf_op jit(solution)/shard_map/ppermute | solution.py:40
  190.4 13.9 %collective-permute-start.29 = (bf16[512,512]{1,0:T(8,128)(2,1)S(1)}, bf16[512,512]{1,0:T(8,128)(2,1)S(1)}, u32[]{:S(2)}, u32[]{:S(2)}) collective-permute-start(bf16[512,512]{1,0:T(8,128)(2,1)S(1)} %add_convert_fusion.1), channel_id=1, source_target_pairs={{0,24},{8,0},{16,8},{24,16},{1,25},{9,1},{17,9},{25,17},{2,26},{10... | collective-permute-start | bytes 1572872 | tf_op jit(solution)/shard_map/ppermute | solution.py:44
  205.3 13.1 %collective-permute-start.26 = (bf16[512,512]{1,0:T(8,128)(2,1)S(1)}, bf16[512,512]{1,0:T(8,128)(2,1)S(1)}, u32[]{:S(2)}, u32[]{:S(2)}) collective-permute-start(bf16[512,512]{1,0:T(8,128)(2,1)S(1)} %add_convert_fusion.2), channel_id=1, source_target_pairs={{0,8},{8,16},{16,24},{24,0},{1,9},{9,17},{17,25},{25,1},{2,10},{10... | collective-permute-start | bytes 1572872 | tf_op jit(solution)/shard_map/ppermute | solution.py:44
  218.4 12.4 %collective-permute-start.27 = (bf16[512,512]{1,0:T(8,128)(2,1)S(1)}, bf16[512,512]{1,0:T(8,128)(2,1)S(1)}, u32[]{:S(2)}, u32[]{:S(2)}) collective-permute-start(bf16[512,512]{1,0:T(8,128)(2,1)S(1)} %broadcast_select_fusion), channel_id=1, source_target_pairs={{0,8},{8,16},{16,24},{24,0},{1,9},{9,17},{17,25},{25,1},{2,10},{10... | collective-permute-start | bytes 1572872 | tf_op jit(solution)/shard_map/ppermute | solution.py:44
  220.6 24.6 %collective-permute-start.23 = (bf16[512,512]{1,0:T(8,128)(2,1)S(1)}, bf16[512,512]{1,0:T(8,128)(2,1)S(1)}, u32[]{:S(2)}, u32[]{:S(2)}) collective-permute-start(bf16[512,512]{1,0:T(8,128)(2,1)S(1)} %fusion.1), channel_id=1, source_target_pairs={{0,24},{8,0},{16,8},{24,16},{1,25},{9,1},{17,9},{25,17},{2,26},{10... | collective-permute-start | bytes 1572872 | tf_op jit(solution)/shard_map/ppermute | solution.py:44
  (36 other events, 1159.4 us)
Sparse Core Ops, SparseCore 0:
  205.4 38.0 all-gather.1

commit v16 on v14

--- a/solution.py
+++ b/solution.py
@@ -60,11 +60,6 @@
     own = (acts[0], grads[0])
     tokens = acts.shape[1]
     behind = [(me - owners[side, column]) % n_dp for side in (0, 1)]
-    found = [0, X, Y, X + Y]
-    held = (basis_in_held[0], basis_out_held[0])
-    ours = [in_order(block, column, found) for block in held]
-    theirs = jnp.split(swap(jnp.concatenate([in_order(block, column, [CORE + i for i in found]) for block in held]), CORE), 2)
-
     pieces = {(0, 0): own[0], (1, 0): own[1]}
     rotated = {}
 
@@ -73,9 +68,13 @@
         pieces[side, i] = shift(after(block, gate), by, n_dp)
         return pieces[side, i]
 
-    def rotate(group, evens):
-        crossing = [swap(dot(even, theirs[side]), CORE) for (side, _), even in zip(group, evens)]
-        for (side, i), even, other in zip(group, evens, crossing):
+    def cross(group, evens, gate):
+        halves = [dot(even, theirs[side]) for (side, _), even in zip(group, evens)]
+        return [swap(block, CORE) for block in after(halves, gate)]
+
+    def rotate(group, evens, crossed=None):
+        crossed = cross(group, evens, []) if crossed is None else crossed
+        for (side, i), even, other in zip(group, evens, crossed):
             rotated[side, i] = (dot(even, ours[side]) + other).astype(jnp.bfloat16)
         return [rotated[key] for key in group]
 
@@ -121,29 +120,33 @@
     stacks, evens = {}, {}
     due = slot(0, [])
     due += [fetch(0, 1, []), fetch(0, 2, [])]
+    found = [0, X, Y, X + Y]
+    held = after([basis_in_held[0], basis_out_held[0]], pieces[0, 1])
+    theirs = [swap(in_order(block, column, [CORE + i for i in found]), CORE) for block in held]
+    ours = [in_order(block, column, found) for block in held]
+    due += theirs
 
     gate, due = due, slot(1, due)
     due += [fetch(0, 3, gate), fetch(1, 1, gate), fetch(1, 2, gate)]
 
-    def begun(at, gate):
-        corner = after(stacks[at][1][:16, :128], gate)
-        return after(evens[at], swap(corner, CORE))
+    gate, due = due, slot(2, due)
+    due += [fetch(1, 3, gate)]
+    evens[0] = after(evens[0], pieces[1, 3])
 
-    gate, due = due, slot(2, due)
-    due += [fetch(1, 3, gate)] + rotate(groups[0], begun(0, gate))
-
+    crossed = cross(groups[0], evens[0], due)
     gate, due = due, slot(3, due)
-    rotate(groups[1], begun(1, gate))
+    rotate(groups[1], after(evens[1], crossed))
+    rotate(groups[0], evens[0], crossed)
     passed_in = pass_on(0)
     due.append(passed_in)
 
     gate, due = due, slot(4, due)
     in_from_behind = send_ahead(0, passed_in, gate)
-    ready = rotate(groups[2], begun(2, gate))
+    rotate(groups[2], evens[2])
     in_from_ahead = send_behind(0)
     passed_out = pass_on(1)
-    ready += rotate(groups[3], after(evens[3], due))
-    rot_in = after(keep(0, in_from_behind, in_from_ahead), ready)
+    rotate(groups[3], after(evens[3], [rotated[key] for key in groups[2]]))
+    rot_in = after(keep(0, in_from_behind, in_from_ahead), due)
     all_rot_in = lax.all_gather(rot_in, "tensor", axis=1, tiled=True)
     rot_out = keep(1, send_ahead(1, passed_out, []), send_behind(1))
     return product_and_divide(rot_out, all_rot_in, eig_lambda, tokens)

time: 286 us -> 299 us (1.045)
  waiting for transfers between devices: 152 us -> 179 us
  local copies, waits for them, and re-layouts: 22.2 us -> 10.5 us
  matrix products: 45.3 us -> 51.5 us
  other arithmetic: 12 us -> 6.59 us
  starting transfers between devices: 36.8 us -> 31.4 us
    ppermute x19 -> x20, waiting for transfers between devices: 57.4 us -> 92.6 us  [swap(): lax.ppermute(block, 'tensor', [(j, j ^ bit) for j in range(X + Y + CORE +...]
    ppermute x12, waiting for transfers between devices: 94.6 us -> 86.1 us  [shift(): return lax.ppermute(block, 'dp', [(z, (z + by) % n) for z in range(n)])]
    unnamed x79 -> x88, local copies, waits for them, and re-layouts: 10.2 us -> 1.81 us
    dot_general x16 -> x15, matrix products: 36.7 us -> 40.7 us  [dot(): return jnp.dot(a, b, preferred_element_type=jnp.float32)]
    ppermute x12, starting transfers between devices: 22.5 us -> 18.9 us  [shift(): return lax.ppermute(block, 'dp', [(z, (z + by) % n) for z in range(n)])]
    dynamic_slice x2 -> x1, local copies, waits for them, and re-layouts: 1.79 us -> 5.26 us  [in_order(): lax.dynamic_slice(held, ((column ^ i) * width, 0), (width, held.shape[1]))]
    concatenate x3, other arithmetic: 4.05 us -> 0.65 us  [slot(): jnp.concatenate(to_y, axis=0)]
    ppermute x19 -> x20, starting transfers between devices: 14.3 us -> 12.5 us  [swap(): lax.ppermute(block, 'tensor', [(j, j ^ bit) for j in range(X + Y + CORE +...]
  transfers between devices with their start and end apart: 32 -> 33, of which waited for: 19 -> 20; matrix products, arithmetic and copies ran while one was open for 22% -> 17% of each run, Pallas kernels for 0% -> 0%
where the time goes in v16:
time: 299 us; the launch traced here: 294 us
  waiting for transfers between devices  179 us (60%)
  matrix products  51.5 us (17%)
  starting transfers between devices  31.4 us (11%)
  between operations  15.3 us (5%)
  local copies, waits for them, and re-layouts  10.5 us (4%)
  other arithmetic  6.59 us (2%)
    ppermute x20, waiting for transfers between devices, swap(): lax.ppermute(block, 'tensor', [(j, j ^ bit) for j in range(X + Y + CORE +...  92.6 us
    ppermute x12, waiting for transfers between devices, shift(): return lax.ppermute(block, 'dp', [(z, (z + by) % n) for z in range(n)])  86.1 us
    dot_general x15, matrix products, dot(): return jnp.dot(a, b, preferred_element_type=jnp.float32)  40.7 us
    ppermute x12, starting transfers between devices, shift(): return lax.ppermute(block, 'dp', [(z, (z + by) % n) for z in range(n)])  18.9 us
    ppermute x20, starting transfers between devices, swap(): lax.ppermute(block, 'tensor', [(j, j ^ bit) for j in range(X + Y + CORE +...  12.5 us
    dot_general x1, matrix products, product_and_divide(): lax.dot_general(rot_out, all_rot_in, contract, preferred_element_type=jnp...  10.8 us
  transfers between devices with their start and end apart: 33, of which 20 were waited for; matrix products, arithmetic and copies ran while one was open for 17% of the time, Pallas kernels for 0%

profile of v16, /device:TPU:16, one launch (start us, length us, event | category | flops | bytes accessed | tf_op | source)
XLA Modules:
  0.0 293.9 jit_solution(8090527709602552474)
XLA Ops:
  7.0 13.4 %collective-permute-done.2 = bf16[512,512]{1,0:T(8,128)(2,1)S(1)} collective-permute-done((bf16[512,512]{1,0:T(8,128)(2,1)}, bf16[512,512]{1,0:T(8,128)(2,1)S(1)}, u32[]{:S(2)}, u32[]{:S(2)}) %collective-permute-start.2) | collective-permute-done | bytes 524320 | tf_op jit(solution)/shard_map/ppermute | solution.py:44
  20.4 5.3 %constant_dynamic-slice_fusion.4 = (bf16[512,512]{1,0:T(8,128)(2,1)S(1)}, bf16[512,512]{1,0:T(8,128)(2,1)S(1)}, bf16[512,512]{1,0:T(8,128)(2,1)S(1)}, bf16[512,5...) fusion(bf16[4096,512]{1,0:T(8,128)(2,1)} %bitcast.29, ...), kind=kLoop, calls=%fused_computation.54 | loop fusion | bytes 16777248 | tf_op jit(solution)/shard_map/dynamic_slice | solution.py:49
  31.2 21.6 %collective-permute-done = bf16[1024,512]{1,0:T(8,128)(2,1)S(1)} collective-permute-done((bf16[1024,512]{1,0:T(8,128)(2,1)S(1)}, bf16[1024,512]{1,0:T(8,128)(2,1)S(1)}, u32[]{:S(2)}, u32[]{:S(2)}) %collective-permute-start) | collective-permute-done | bytes 1048608 | tf_op jit(solution)/shard_map/ppermute | solution.py:40
  57.0 2.9 collective-permute-start.8
  59.9 12.8 %collective-permute-done.9 = bf16[512,512]{1,0:T(8,128)(2,1)S(1)} collective-permute-done((bf16[512,512]{1,0:T(8,128)(2,1)S(1)}, bf16[512,512]{1,0:T(8,128)(2,1)S(1)}, u32[]{:S(2)}, u32[]{:S(2)}) %collective-permute-start.9) | collective-permute-done | bytes 524320 | tf_op jit(solution)/shard_map/ppermute | solution.py:44
  72.8 16.9 %collective-permute-done.6 = bf16[1536,512]{1,0:T(8,128)(2,1)S(1)} collective-permute-done((bf16[1536,512]{1,0:T(8,128)(2,1)S(1)}, bf16[1536,512]{1,0:T(8,128)(2,1)S(1)}, u32[]{:S(2)}, u32[]{:S(2)}) %collective-permute-start.6) | collective-permute-done | bytes 1572896 | tf_op jit(solution)/shard_map/ppermute | solution.py:40
  90.2 2.7 collective-permute-done.10
  95.1 4.1 %collective-permute-start.11 = (bf16[512,512]{1,0:T(8,128)(2,1)S(1)}, bf16[512,512]{1,0:T(8,128)(2,1)S(1)}, u32[]{:S(2)}, u32[]{:S(2)}) collective-permute-start(bf16[512,512]{1,0:T(8,128)(2,1)S(1)} %bitcast.37), channel_id=1, source_target_pairs={{0,8},{8,16},{16,24},{24,0},{1,9},{9,17},{17,25},{25,1},{2,10},{10... | collective-permute-start | bytes 1572872 | tf_op jit(solution)/shard_map/ppermute | solution.py:44
  99.8 7.0 %collective-permute-done.11 = bf16[512,512]{1,0:T(8,128)(2,1)S(1)} collective-permute-done((bf16[512,512]{1,0:T(8,128)(2,1)S(1)}, bf16[512,512]{1,0:T(8,128)(2,1)S(1)}, u32[]{:S(2)}, u32[]{:S(2)}) %collective-permute-start.11) | collective-permute-done | bytes 524320 | tf_op jit(solution)/shard_map/ppermute | solution.py:44
  109.3 17.8 %collective-permute-done.12 = bf16[1536,512]{1,0:T(8,128)(2,1)S(1)} collective-permute-done((bf16[1536,512]{1,0:T(8,128)(2,1)S(1)}, bf16[1536,512]{1,0:T(8,128)(2,1)S(1)}, u32[]{:S(2)}, u32[]{:S(2)}) %collective-permute-start.12) | collective-permute-done | bytes 1572896 | tf_op jit(solution)/shard_map/ppermute | solution.py:40
  133.7 2.2 fusion.32
  136.4 29.2 %collective-permute-done.15 = bf16[1536,512]{1,0:T(8,128)(2,1)S(1)} collective-permute-done((bf16[1536,512]{1,0:T(8,128)(2,1)S(1)}, bf16[1536,512]{1,0:T(8,128)(2,1)S(1)}, u32[]{:S(2)}, u32[]{:S(2)}) %collective-permute-start.15) | collective-permute-done | bytes 1572896 | tf_op jit(solution)/shard_map/ppermute | solution.py:40
  168.3 2.3 fusion.14
  172.7 3.3 %collective-permute-start.19 = (bf16[512,512]{1,0:T(8,128)(2,1)}, bf16[512,512]{1,0:T(8,128)(2,1)}, u32[]{:S(2)}, u32[]{:S(2)}) collective-permute-start(bf16[512,512]{1,0:T(8,128)(2,1)} %fusion.2), channel_id=1, source_target_pairs={{0,8},{8,16},{16,24},{24,0},{1,9},{9,17},{17,25},{25,1},{2,10},{10... | collective-permute-start | bytes 1572872 | tf_op jit(solution)/shard_map/ppermute | solution.py:44
  176.1 2.2 fusion.15
  179.6 6.9 %collective-permute-done.19 = bf16[512,512]{1,0:T(8,128)(2,1)} collective-permute-done((bf16[512,512]{1,0:T(8,128)(2,1)}, bf16[512,512]{1,0:T(8,128)(2,1)}, u32[]{:S(2)}, u32[]{:S(2)}) %collective-permute-start.19) | collective-permute-done | bytes 524320 | tf_op jit(solution)/shard_map/ppermute | solution.py:44
  186.6 4.7 %fusion.7 = bf16[512,512]{1,0:T(8,128)(2,1)} fusion(bf16[512,512]{1,0:T(8,128)(2,1)} %collective-permute-done.19, f32[512,512]{1,0:T(8,128)} %collective-permute-done.30, bf16[512,2048]{1,0:T(8,128)(2,1)} %copy-done.1, pred[]{:T(512)S(6)} %eq.19, bf16[512,512]{1,0:T(8,128)(2,1)} %copy-done.24, bf16[512,512]{1,0:T(8,128)(2,1)} %copy-done.26, ...), kind=kOutput, calls=%fused_computation.38 | convolution fusion | flops 1082916864 | bytes 6291457 | tf_op jit(solution)/shard_map/dot_general | solution.py:22
  191.3 2.5 collective-permute-start.31
  193.8 3.3 %fusion.3 = bf16[512,512]{1,0:T(8,128)(2,1)} fusion(f32[512,512]{1,0:T(8,128)} %collective-permute-done.22, bf16[512,512]{1,0:T(8,128)(2,1)S(1)} %copy-done.38, bf16[512,512]{1,0:T(8,128)(2,1)S(1)} %copy-done.36, bf16[512,512]{1,0:T(8,128)(2,1)S(1)} %get-tuple-element.116, bf16[512,512]{1,0:T(8,128)(2,1)S(1)} %copy-done.32, ...), kind=kOutput, calls=%fused_computation.34 | convolution fusion | flops 1091043328 | bytes 5767168 | tf_op jit(solution)/shard_map/dot_general | solution.py:22
  199.0 5.7 %collective-permute-done.31 = bf16[512,512]{1,0:T(8,128)(2,1)} collective-permute-done((bf16[512,512]{1,0:T(8,128)(2,1)}, bf16[512,512]{1,0:T(8,128)(2,1)}, u32[]{:S(2)}, u32[]{:S(2)}) %collective-permute-start.31) | collective-permute-done | bytes 524320 | tf_op jit(solution)/shard_map/ppermute | solution.py:44
  204.7 12.8 %collective-permute-done.29 = bf16[512,512]{1,0:T(8,128)(2,1)} collective-permute-done((bf16[512,512]{1,0:T(8,128)(2,1)}, bf16[512,512]{1,0:T(8,128)(2,1)}, u32[]{:S(2)}, u32[]{:S(2)}) %collective-permute-start.29) | collective-permute-done | bytes 524320 | tf_op jit(solution)/shard_map/ppermute | solution.py:44
  217.4 4.7 %fusion.8 = bf16[512,512]{1,0:T(8,128)(2,1)} fusion(f32[512,512]{1,0:T(8,128)} %copy-done.43, bf16[512,2048]{1,0:T(8,128)(2,1)} %copy-done, bf16[512,512]{1,0:T(8,128)(2,1)} %collective-permute-done.29, bf16[512,512]{1,0:T(8,128)(2,1)} %collective-permute-done.31, pred[]{:T(512)S(6)} %eq.20, pred[]{:T(512)S(6)} %eq.19, bf16[512,512]{1,0:T(8,128)(2,1)} %copy-done.24, ...), kind=kOutput, calls=%fused_computation.39 | convolution fusion | flops 1083179008 | bytes 6815746 | tf_op jit(solution)/shard_map/dot_general | solution.py:22
  222.2 2.9 collective-permute-done.23
  225.1 4.0 %fusion.4 = bf16[512,512]{1,0:T(8,128)(2,1)} fusion(f32[512,512]{1,0:T(8,128)S(1)} %collective-permute-done.23, bf16[512,512]{1,0:T(8,128)(2,1)} %copy-done.34, bf16[512,512]{1,0:T(8,128)(2,1)S(1)} %get-tuple-element.122, bf16[512,512]{1,0:T(8,128)(2,1)} %copy-done.33, bf16[512,512]{1,0:T(8,128)(2,1)} %copy-done.30, ...), kind=kOutput, calls=%fused_computation.35 | convolution fusion | flops 1091043328 | bytes 5767168 | tf_op jit(solution)/shard_map/dot_general | solution.py:22
  235.3 2.2 fusion.34
  239.1 3.6 %fusion.20 = f32[512,512]{1,0:T(8,128)S(1)} fusion(bf16[512,2048]{1,0:T(8,128)(2,1)} %copy-done.2, bf16[512,512]{1,0:T(8,128)(2,1)} %get-tuple-element.143, bf16[512,512]{1,0:T(8,128)(2,1)} %get-tuple-element.142, bf16[512,512]{1,0:T(8,128)(2,1)} %get-tuple-element.141, bf16[512,512]{1,0:T(8,128)(2,1)} %get-tuple-element.144), kind=kOutput, calls=%fused_computation.72 | convolution fusion | flops 1082130432 | bytes 5242880 | tf_op jit(solution)/shard_map/dot_general | solution.py:22
  242.8 3.4 %add_convert_fusion.1 = bf16[512,512]{1,0:T(8,128)(2,1)} fusion(f32[512,512]{1,0:T(8,128)} %collective-permute-done.24, bf16[512,2048]{1,0:T(8,128)(2,1)S(1)} %copy-done.4, bf16[512,512]{1,0:T(8,128)(2,1)S(1)} %copy-done.20, bf16[512,512]{1,0:T(8,128)(2,1)S(1)} %copy-done.19, bf16[512,512]{1,0:T(8,128)(2,1)S(1)} %copy-done.18, ...), kind=kOutput, calls=%fused_computation.43 | convolution fusion | flops 1082654720 | bytes 5767168 | tf_op jit(solution)/shard_map/dot_general | solution.py:22
  248.0 5.0 %collective-permute-done.27 = bf16[512,512]{1,0:T(8,128)(2,1)S(1)} collective-permute-done((bf16[512,512]{1,0:T(8,128)(2,1)}, bf16[512,512]{1,0:T(8,128)(2,1)S(1)}, u32[]{:S(2)}, u32[]{:S(2)}) %collective-permute-start.27) | collective-permute-done | bytes 524320 | tf_op jit(solution)/shard_map/ppermute | solution.py:44
  254.1 2.5 collective-permute-start.28
  256.6 10.6 %collective-permute-done.25 = bf16[512,512]{1,0:T(8,128)(2,1)} collective-permute-done((bf16[512,512]{1,0:T(8,128)(2,1)}, bf16[512,512]{1,0:T(8,128)(2,1)}, u32[]{:S(2)}, u32[]{:S(2)}) %collective-permute-start.25) | collective-permute-done | bytes 524320 | tf_op jit(solution)/shard_map/ppermute | solution.py:44
  267.2 9.2 %collective-permute-done.28 = bf16[512,512]{1,0:T(8,128)(2,1)S(1)} collective-permute-done((bf16[512,512]{1,0:T(8,128)(2,1)}, bf16[512,512]{1,0:T(8,128)(2,1)S(1)}, u32[]{:S(2)}, u32[]{:S(2)}) %collective-permute-start.28) | collective-permute-done | bytes 524320 | tf_op jit(solution)/shard_map/ppermute | solution.py:44
  276.3 10.8 %fusion = bf16[1,512,4096]{2,1,0:T(8,128)(2,1)} fusion(bf16[512,4096]{1,0:T(8,128)(2,1)} %param.11, bf16[512,4096]{1,0:T(8,128)(2,1)} %all-gather.2.cloned.1.call-done, f32[512,512]{1,0:T(8,128)} %copy-done.42, bf16[512,2048]{1,0:T(8,128)(2,1)S(1)} %pad_maximum_fusion.3, bf16[512,512]{1,0:T(8,128)(2,1)} %collective-permute-done.25, ...), kind=kOutput, calls=%fused_computation.1 | convolution fusion | flops 3241148416 | bytes 18874370 | tf_op jit(solution)/shard_map/dot_general | solution.py:13
  (161 shorter events, 40.2 us)
Async XLA Ops:
  6.5 269.8 %all-gather.2.cloned.1.call-start = ((), (), s32[]{:S(2)}) async-start(), calls=%async_computation | async-start | bytes 4718592 | tf_op jit(solution)/shard_map/all_gather | solution.py:150
  6.5 13.9 %collective-permute-start.2 = (bf16[512,512]{1,0:T(8,128)(2,1)}, bf16[512,512]{1,0:T(8,128)(2,1)S(1)}, u32[]{:S(2)}, u32[]{:S(2)}) collective-permute-start(bf16[512,512]{1,0:T(8,128)(2,1)} %bitcast.31), channel_id=1, source_target_pairs={{0,24},{8,0},{16,8},{24,16},{1,25},{9,1},{17,9},{25,17},{2,26},{10... | collective-permute-start | bytes 1572872 | tf_op jit(solution)/shard_map/ppermute | solution.py:44
  25.8 28.6 %collective-permute-start.5 = (bf16[2048,512]{1,0:T(8,128)(2,1)S(1)}, bf16[2048,512]{1,0:T(8,128)(2,1)S(1)}, u32[]{:S(2)}, u32[]{:S(2)}) collective-permute-start(bf16[2048,512]{1,0:T(8,128)(2,1)S(1)} %pad_maximum_fusion.1), channel_id=1, source_target_pairs={{0,1},{1,0},{2,3},{3,2},{4,5},{5,4},{6,7},{7,6},{8,9},{9,8},{10,11... | collective-permute-start | bytes 6291464 | tf_op jit(solution)/shard_map/ppermute | solution.py:40
  26.1 28.3 %collective-permute-start.4 = (bf16[2048,512]{1,0:T(8,128)(2,1)S(1)}, bf16[2048,512]{1,0:T(8,128)(2,1)S(1)}, u32[]{:S(2)}, u32[]{:S(2)}) collective-permute-start(bf16[2048,512]{1,0:T(8,128)(2,1)S(1)} %pad_maximum_fusion), channel_id=1, source_target_pairs={{0,1},{1,0},{2,3},{3,2},{4,5},{5,4},{6,7},{7,6},{8,9},{9,8},{10,11... | collective-permute-start | bytes 6291464 | tf_op jit(solution)/shard_map/ppermute | solution.py:40
  27.7 25.1 %collective-permute-start = (bf16[1024,512]{1,0:T(8,128)(2,1)S(1)}, bf16[1024,512]{1,0:T(8,128)(2,1)S(1)}, u32[]{:S(2)}, u32[]{:S(2)}) collective-permute-start(bf16[1024,512]{1,0:T(8,128)(2,1)S(1)} %pad_maximum_fusion.24), channel_id=1, source_target_pairs={{0,2},{1,3},{2,0},{3,1},{4,6},{5,7},{6,4},{7,5},{8,10},{9,11},{10,... | collective-permute-start | bytes 3145736 | tf_op jit(solution)/shard_map/ppermute | solution.py:40
  29.3 24.8 %collective-permute-start.1 = (bf16[1024,512]{1,0:T(8,128)(2,1)S(1)}, bf16[1024,512]{1,0:T(8,128)(2,1)S(1)}, u32[]{:S(2)}, u32[]{:S(2)}) collective-permute-start(bf16[1024,512]{1,0:T(8,128)(2,1)S(1)} %pad_maximum_fusion.24), channel_id=1, source_target_pairs={{0,4},{1,5},{2,6},{3,7},{4,0},{5,1},{6,2},{7,3},{8,12},{9,13},{10,... | collective-permute-start | bytes 3145736 | tf_op jit(solution)/shard_map/ppermute | solution.py:40
  30.8 23.4 %collective-permute-start.3 = (bf16[512,512]{1,0:T(8,128)(2,1)S(1)}, bf16[512,512]{1,0:T(8,128)(2,1)S(1)}, u32[]{:S(2)}, u32[]{:S(2)}) collective-permute-start(bf16[512,512]{1,0:T(8,128)(2,1)S(1)} %collective-permute-done.2), channel_id=1, source_target_pairs={{0,24},{8,0},{16,8},{24,16},{1,25},{9,1},{17,9},{25,17},{2,26},{10... | collective-permute-start | bytes 1572872 | tf_op jit(solution)/shard_map/ppermute | solution.py:44
  54.4 35.2 %collective-permute-start.6 = (bf16[1536,512]{1,0:T(8,128)(2,1)S(1)}, bf16[1536,512]{1,0:T(8,128)(2,1)S(1)}, u32[]{:S(2)}, u32[]{:S(2)}) collective-permute-start(bf16[1536,512]{1,0:T(8,128)(2,1)S(1)} %get-tuple-element.53), channel_id=1, source_target_pairs={{0,2},{1,3},{2,0},{3,1},{4,6},{5,7},{6,4},{7,5},{8,10},{9,11},{10,... | collective-permute-start | bytes 4718600 | tf_op jit(solution)/shard_map/ppermute | solution.py:40
  55.0 34.9 %collective-permute-start.7 = (bf16[1536,512]{1,0:T(8,128)(2,1)S(1)}, bf16[1536,512]{1,0:T(8,128)(2,1)S(1)}, u32[]{:S(2)}, u32[]{:S(2)}) collective-permute-start(bf16[1536,512]{1,0:T(8,128)(2,1)S(1)} %get-tuple-element.54), channel_id=1, source_target_pairs={{0,4},{1,5},{2,6},{3,7},{4,0},{5,1},{6,2},{7,3},{8,12},{9,13},{10,... | collective-permute-start | bytes 4718600 | tf_op jit(solution)/shard_map/ppermute | solution.py:40
  56.6 16.2 %collective-permute-start.9 = (bf16[512,512]{1,0:T(8,128)(2,1)S(1)}, bf16[512,512]{1,0:T(8,128)(2,1)S(1)}, u32[]{:S(2)}, u32[]{:S(2)}) collective-permute-start(bf16[512,512]{1,0:T(8,128)(2,1)S(1)} %bitcast.36), channel_id=1, source_target_pairs={{0,24},{8,0},{16,8},{24,16},{1,25},{9,1},{17,9},{25,17},{2,26},{10... | collective-permute-start | bytes 1572872 | tf_op jit(solution)/shard_map/ppermute | solution.py:44
  57.0 33.2 %collective-permute-start.8 = (bf16[512,512]{1,0:T(8,128)(2,1)S(1)}, bf16[512,512]{1,0:T(8,128)(2,1)S(1)}, u32[]{:S(2)}, u32[]{:S(2)}) collective-permute-start(bf16[512,512]{1,0:T(8,128)(2,1)S(1)} %bitcast.33), channel_id=1, source_target_pairs={{0,8},{8,16},{16,24},{24,0},{1,9},{9,17},{17,25},{25,1},{2,10},{10... | collective-permute-start | bytes 1572872 | tf_op jit(solution)/shard_map/ppermute | solution.py:44
  72.8 20.1 %collective-permute-start.10 = (bf16[512,512]{1,0:T(8,128)(2,1)S(1)}, bf16[512,512]{1,0:T(8,128)(2,1)S(1)}, u32[]{:S(2)}, u32[]{:S(2)}) collective-permute-start(bf16[512,512]{1,0:T(8,128)(2,1)S(1)} %collective-permute-done.9), channel_id=1, source_target_pairs={{0,24},{8,0},{16,8},{24,16},{1,25},{9,1},{17,9},{25,17},{2,26},{10... | collective-permute-start | bytes 1572872 | tf_op jit(solution)/shard_map/ppermute | solution.py:44
  93.1 34.1 %collective-permute-start.12 = (bf16[1536,512]{1,0:T(8,128)(2,1)S(1)}, bf16[1536,512]{1,0:T(8,128)(2,1)S(1)}, u32[]{:S(2)}, u32[]{:S(2)}) collective-permute-start(bf16[1536,512]{1,0:T(8,128)(2,1)S(1)} %get-tuple-element.63), channel_id=1, source_target_pairs={{0,2},{1,3},{2,0},{3,1},{4,6},{5,7},{6,4},{7,5},{8,10},{9,11},{10,... | collective-permute-start | bytes 4718600 | tf_op jit(solution)/shard_map/ppermute | solution.py:40
  94.6 33.6 %collective-permute-start.13 = (bf16[1536,512]{1,0:T(8,128)(2,1)S(1)}, bf16[1536,512]{1,0:T(8,128)(2,1)S(1)}, u32[]{:S(2)}, u32[]{:S(2)}) collective-permute-start(bf16[1536,512]{1,0:T(8,128)(2,1)S(1)} %get-tuple-element.64), channel_id=1, source_target_pairs={{0,4},{1,5},{2,6},{3,7},{4,0},{5,1},{6,2},{7,3},{8,12},{9,13},{10,... | collective-permute-start | bytes 4718600 | tf_op jit(solution)/shard_map/ppermute | solution.py:40
  95.1 11.7 %collective-permute-start.11 = (bf16[512,512]{1,0:T(8,128)(2,1)S(1)}, bf16[512,512]{1,0:T(8,128)(2,1)S(1)}, u32[]{:S(2)}, u32[]{:S(2)}) collective-permute-start(bf16[512,512]{1,0:T(8,128)(2,1)S(1)} %bitcast.37), channel_id=1, source_target_pairs={{0,8},{8,16},{16,24},{24,0},{1,9},{9,17},{17,25},{25,1},{2,10},{10... | collective-permute-start | bytes 1572872 | tf_op jit(solution)/shard_map/ppermute | solution.py:44
  128.2 4.2 %collective-permute-start.17 = (f32[512,512]{1,0:T(8,128)S(1)}, f32[512,512]{1,0:T(8,128)S(1)}, u32[]{:S(2)}, u32[]{:S(2)}) collective-permute-start(f32[512,512]{1,0:T(8,128)S(1)} %fusion.30), channel_id=1, source_target_pairs={{0,1},{1,0},{2,3},{3,2},{4,5},{5,4},{6,7},{7,6},{8,9},{9,8},{10,11... | collective-permute-start | bytes 3145736 | tf_op jit(solution)/shard_map/ppermute | solution.py:40
  129.2 36.4 %collective-permute-start.15 = (bf16[1536,512]{1,0:T(8,128)(2,1)S(1)}, bf16[1536,512]{1,0:T(8,128)(2,1)S(1)}, u32[]{:S(2)}, u32[]{:S(2)}) collective-permute-start(bf16[1536,512]{1,0:T(8,128)(2,1)S(1)} %get-tuple-element.68), channel_id=1, source_target_pairs={{0,2},{1,3},{2,0},{3,1},{4,6},{5,7},{6,4},{7,5},{8,10},{9,11},{10,... | collective-permute-start | bytes 4718600 | tf_op jit(solution)/shard_map/ppermute | solution.py:40
  130.0 36.0 %collective-permute-start.16 = (bf16[1536,512]{1,0:T(8,128)(2,1)S(1)}, bf16[1536,512]{1,0:T(8,128)(2,1)S(1)}, u32[]{:S(2)}, u32[]{:S(2)}) collective-permute-start(bf16[1536,512]{1,0:T(8,128)(2,1)S(1)} %get-tuple-element.69), channel_id=1, source_target_pairs={{0,4},{1,5},{2,6},{3,7},{4,0},{5,1},{6,2},{7,3},{8,12},{9,13},{10,... | collective-permute-start | bytes 4718600 | tf_op jit(solution)/shard_map/ppermute | solution.py:40
  135.9 34.7 %collective-permute-start.18 = (f32[512,512]{1,0:T(8,128)S(1)}, f32[512,512]{1,0:T(8,128)S(1)}, u32[]{:S(2)}, u32[]{:S(2)}) collective-permute-start(f32[512,512]{1,0:T(8,128)S(1)} %fusion.33), channel_id=1, source_target_pairs={{0,1},{1,0},{2,3},{3,2},{4,5},{5,4},{6,7},{7,6},{8,9},{9,8},{10,11... | collective-permute-start | bytes 3145736 | tf_op jit(solution)/shard_map/ppermute | solution.py:40
  136.0 43.6 %collective-permute-start.30 = (f32[512,512]{1,0:T(8,128)}, f32[512,512]{1,0:T(8,128)}, u32[]{:S(2)}, u32[]{:S(2)}) collective-permute-start(f32[512,512]{1,0:T(8,128)} %fusion.32), channel_id=1, source_target_pairs={{0,1},{1,0},{2,3},{3,2},{4,5},{5,4},{6,7},{7,6},{8,9},{9,8},{10,11... | collective-permute-start | bytes 3145736 | tf_op jit(solution)/shard_map/ppermute | solution.py:40
  172.7 13.8 %collective-permute-start.19 = (bf16[512,512]{1,0:T(8,128)(2,1)}, bf16[512,512]{1,0:T(8,128)(2,1)}, u32[]{:S(2)}, u32[]{:S(2)}) collective-permute-start(bf16[512,512]{1,0:T(8,128)(2,1)} %fusion.2), channel_id=1, source_target_pairs={{0,8},{8,16},{16,24},{24,0},{1,9},{9,17},{17,25},{25,1},{2,10},{10... | collective-permute-start | bytes 1572872 | tf_op jit(solution)/shard_map/ppermute | solution.py:44
  178.3 15.4 %collective-permute-start.22 = (f32[512,512]{1,0:T(8,128)}, f32[512,512]{1,0:T(8,128)}, u32[]{:S(2)}, u32[]{:S(2)}) collective-permute-start(f32[512,512]{1,0:T(8,128)} %fusion.15), channel_id=1, source_target_pairs={{0,1},{1,0},{2,3},{3,2},{4,5},{5,4},{6,7},{7,6},{8,9},{9,8},{10,11... | collective-permute-start | bytes 3145736 | tf_op jit(solution)/shard_map/ppermute | solution.py:40
  191.3 13.4 %collective-permute-start.31 = (bf16[512,512]{1,0:T(8,128)(2,1)}, bf16[512,512]{1,0:T(8,128)(2,1)}, u32[]{:S(2)}, u32[]{:S(2)}) collective-permute-start(bf16[512,512]{1,0:T(8,128)(2,1)} %fusion.7), channel_id=1, source_target_pairs={{0,8},{8,16},{16,24},{24,0},{1,9},{9,17},{17,25},{25,1},{2,10},{10... | collective-permute-start | bytes 1572872 | tf_op jit(solution)/shard_map/ppermute | solution.py:44
  197.1 20.3 %collective-permute-start.29 = (bf16[512,512]{1,0:T(8,128)(2,1)}, bf16[512,512]{1,0:T(8,128)(2,1)}, u32[]{:S(2)}, u32[]{:S(2)}) collective-permute-start(bf16[512,512]{1,0:T(8,128)(2,1)} %fusion.3), channel_id=1, source_target_pairs={{0,24},{8,0},{16,8},{24,16},{1,25},{9,1},{17,9},{25,17},{2,26},{10... | collective-permute-start | bytes 1572872 | tf_op jit(solution)/shard_map/ppermute | solution.py:44
  197.1 25.0 %collective-permute-start.20 = (bf16[512,512]{1,0:T(8,128)(2,1)}, bf16[512,512]{1,0:T(8,128)(2,1)}, u32[]{:S(2)}, u32[]{:S(2)}) collective-permute-start(bf16[512,512]{1,0:T(8,128)(2,1)} %get-tuple-element.76), channel_id=1, source_target_pairs={{0,2},{1,3},{2,0},{3,1},{4,6},{5,7},{6,4},{7,5},{8,10},{9,11},{10,... | collective-permute-start | bytes 1572872 | tf_op jit(solution)/shard_map/ppermute | solution.py:40
  198.4 23.6 %collective-permute-start.21 = (bf16[512,512]{1,0:T(8,128)(2,1)}, bf16[512,512]{1,0:T(8,128)(2,1)}, u32[]{:S(2)}, u32[]{:S(2)}) collective-permute-start(bf16[512,512]{1,0:T(8,128)(2,1)} %get-tuple-element.77), channel_id=1, source_target_pairs={{0,4},{1,5},{2,6},{3,7},{4,0},{5,1},{6,2},{7,3},{8,12},{9,13},{10,... | collective-permute-start | bytes 1572872 | tf_op jit(solution)/shard_map/ppermute | solution.py:40
  222.1 2.9 collective-permute-start.23
  237.5 5.2 %collective-permute-start.24 = (f32[512,512]{1,0:T(8,128)}, f32[512,512]{1,0:T(8,128)}, u32[]{:S(2)}, u32[]{:S(2)}) collective-permute-start(f32[512,512]{1,0:T(8,128)} %fusion.35), channel_id=1, source_target_pairs={{0,1},{1,0},{2,3},{3,2},{4,5},{5,4},{6,7},{7,6},{8,9},{9,8},{10,11... | collective-permute-start | bytes 3145736 | tf_op jit(solution)/shard_map/ppermute | solution.py:40
  237.7 15.3 %collective-permute-start.26 = (f32[512,512]{1,0:T(8,128)}, f32[512,512]{1,0:T(8,128)S(1)}, u32[]{:S(2)}, u32[]{:S(2)}) collective-permute-start(f32[512,512]{1,0:T(8,128)} %fusion.34), channel_id=1, source_target_pairs={{0,1},{1,0},{2,3},{3,2},{4,5},{5,4},{6,7},{7,6},{8,9},{9,8},{10,11... | collective-permute-start | bytes 3145736 | tf_op jit(solution)/shard_map/ppermute | solution.py:40
  238.8 14.2 %collective-permute-start.27 = (bf16[512,512]{1,0:T(8,128)(2,1)}, bf16[512,512]{1,0:T(8,128)(2,1)S(1)}, u32[]{:S(2)}, u32[]{:S(2)}) collective-permute-start(bf16[512,512]{1,0:T(8,128)(2,1)} %fusion.4), channel_id=1, source_target_pairs={{0,8},{8,16},{16,24},{24,0},{1,9},{9,17},{17,25},{25,1},{2,10},{10... | collective-permute-start | bytes 1572872 | tf_op jit(solution)/shard_map/ppermute | solution.py:44
  246.2 21.0 %collective-permute-start.25 = (bf16[512,512]{1,0:T(8,128)(2,1)}, bf16[512,512]{1,0:T(8,128)(2,1)}, u32[]{:S(2)}, u32[]{:S(2)}) collective-permute-start(bf16[512,512]{1,0:T(8,128)(2,1)} %add_convert_fusion.1), channel_id=1, source_target_pairs={{0,24},{8,0},{16,8},{24,16},{1,25},{9,1},{17,9},{25,17},{2,26},{10... | collective-permute-start | bytes 1572872 | tf_op jit(solution)/shard_map/ppermute | solution.py:44
  254.1 22.2 %collective-permute-start.28 = (bf16[512,512]{1,0:T(8,128)(2,1)}, bf16[512,512]{1,0:T(8,128)(2,1)S(1)}, u32[]{:S(2)}, u32[]{:S(2)}) collective-permute-start(bf16[512,512]{1,0:T(8,128)(2,1)} %fusion.10), channel_id=1, source_target_pairs={{0,8},{8,16},{16,24},{24,0},{1,9},{9,17},{17,25},{25,1},{2,10},{10... | collective-permute-start | bytes 1572872 | tf_op jit(solution)/shard_map/ppermute | solution.py:44
  (45 other events, 1263.6 us)
Sparse Core Ops, SparseCore 0:
  222.2 36.4 all-gather.1

commit v17 on v16

--- a/solution.py
+++ b/solution.py
@@ -68,15 +68,14 @@
         pieces[side, i] = shift(after(block, gate), by, n_dp)
         return pieces[side, i]
 
-    def cross(group, evens, gate):
-        halves = [dot(even, theirs[side]) for (side, _), even in zip(group, evens)]
-        return [swap(block, CORE) for block in after(halves, gate)]
+    def half_product(key, even):
+        return dot(even, theirs[key[0]])
 
-    def rotate(group, evens, crossed=None):
-        crossed = cross(group, evens, []) if crossed is None else crossed
-        for (side, i), even, other in zip(group, evens, crossed):
-            rotated[side, i] = (dot(even, ours[side]) + other).astype(jnp.bfloat16)
-        return [rotated[key] for key in group]
+    def rotate(key, even, crossed):
+        rotated[key] = (dot(even, ours[key[0]]) + crossed).astype(jnp.bfloat16)
+
+    def cross(block, gate):
+        return swap(after(block, gate), CORE)
 
     def pass_on(side):
         return shift(rotated[side, 2], 1, n_dp)
@@ -95,58 +94,71 @@
     groups = [[(0, 0), (1, 0)], [(0, 1), (0, 2)], [(0, 3), (1, 2)], [(1, 1), (1, 3)]]
     first, second = slice(0, tokens), slice(tokens, 2 * tokens)
 
-    def slot(at, gate):
+    def begin(at, gate):
         to_x, to_y = [], []
         if at:
-            stack, x, y = stacks[at - 1]
+            _, x, y = stacks[at - 1]
             to_x.append(y[second])
             to_y.append(x[first])
         if at < len(groups):
-            new = jnp.concatenate([pieces[key] for key in groups[at]], axis=0)
-            to_x.append(new)
-            to_y.append(new)
+            stacks[at] = jnp.concatenate([pieces[key] for key in groups[at]], axis=0)
+            to_x.append(stacks[at])
+            to_y.append(stacks[at])
         to_x, to_y = after((jnp.concatenate(to_x, axis=0), jnp.concatenate(to_y, axis=0)), gate)
-        got = [swap(to_x, X), swap(to_y, Y)]
-        from_x, from_y = after(got, [])
+        return [swap(to_x, X), swap(to_y, Y)]
+
+    def end(at, got, others):
+        (from_x, from_y), others = lax.optimization_barrier((got, others))
         if at:
-            evens[at - 1] = [
-                jnp.concatenate([stack[first], x[first], y[first], from_y[:tokens]], axis=1),
-                jnp.concatenate([stack[second], x[second], y[second], from_x[:tokens]], axis=1),
-            ]
+            stack, x, y = stacks[at - 1]
+            evens[groups[at - 1][0]] = jnp.concatenate([stack[first], x[first], y[first], from_y[:tokens]], axis=1)
+            evens[groups[at - 1][1]] = jnp.concatenate([stack[second], x[second], y[second], from_x[:tokens]], axis=1)
         if at < len(groups):
-            stacks[at] = (new, from_x[-2 * tokens :], from_y[-2 * tokens :])
-        return got
+            stacks[at] = (stacks[at], from_x[-2 * tokens :], from_y[-2 * tokens :])
+        return [from_x, from_y] + others
+
+    found = [0, X, Y, X + Y]
+    held = [basis_in_held[0], basis_out_held[0]]
+
+    def rows_for_other(side, gate):
+        return swap(in_order(after(held[side], gate), column, [CORE + i for i in found]), CORE)
 
     stacks, evens = {}, {}
-    due = slot(0, [])
-    due += [fetch(0, 1, []), fetch(0, 2, [])]
-    found = [0, X, Y, X + Y]
-    held = after([basis_in_held[0], basis_out_held[0]], pieces[0, 1])
-    theirs = [swap(in_order(block, column, [CORE + i for i in found]), CORE) for block in held]
     ours = [in_order(block, column, found) for block in held]
-    due += theirs
+    theirs = [rows_for_other(0, []), None]
+    gate = end(0, begin(0, []), [fetch(0, 1, []), fetch(0, 2, []), theirs[0]])
 
-    gate, due = due, slot(1, due)
-    due += [fetch(0, 3, gate), fetch(1, 1, gate), fetch(1, 2, gate)]
+    got = begin(1, gate)
+    gate = end(1, got, [fetch(0, 3, gate), fetch(1, 1, gate), fetch(1, 2, gate)])
 
-    gate, due = due, slot(2, due)
-    due += [fetch(1, 3, gate)]
-    evens[0] = after(evens[0], pieces[1, 3])
+    got = begin(2, gate)
+    theirs[1] = rows_for_other(1, gate)
+    half = half_product((0, 0), after(evens[0, 0], fetch(1, 3, gate)))
+    gate = end(2, got, [pieces[1, 3], half, theirs[1]])
 
-    crossed = cross(groups[0], evens[0], due)
-    gate, due = due, slot(3, due)
-    rotate(groups[1], after(evens[1], crossed))
-    rotate(groups[0], evens[0], crossed)
+    got = begin(3, gate)
+    crossed = cross(half, gate)
+    even, even_1 = after([evens[0, 2], evens[0, 1]], crossed)
+    rotate((0, 2), even, cross(half_product((0, 2), even), []))
     passed_in = pass_on(0)
-    due.append(passed_in)
+    rotate((0, 0), evens[0, 0], crossed)
+    half = half_product((0, 1), even_1)
+    gate = end(3, got, [passed_in, half])
 
-    gate, due = due, slot(4, due)
+    got = begin(4, gate)
+    crossed = cross(half, gate)
+    rotate((0, 1), even_1, crossed)
     in_from_behind = send_ahead(0, passed_in, gate)
-    rotate(groups[2], evens[2])
+    even, even_2 = after([evens[0, 3], evens[1, 2]], crossed)
+    rotate((0, 3), even, cross(half_product((0, 3), even), []))
     in_from_ahead = send_behind(0)
+    rotate((1, 2), even_2, cross(half_product((1, 2), even_2), []))
     passed_out = pass_on(1)
-    rotate(groups[3], after(evens[3], [rotated[key] for key in groups[2]]))
-    rot_in = after(keep(0, in_from_behind, in_from_ahead), due)
+    gate = end(4, got, [rotated[0, 3], rotated[1, 2]])
+
+    rot_in = after(keep(0, in_from_behind, in_from_ahead), gate)
+    for key in [(1, 1), (1, 3), (1, 0)]:
+        rotate(key, evens[key], cross(half_product(key, evens[key]), []))
     all_rot_in = lax.all_gather(rot_in, "tensor", axis=1, tiled=True)
     rot_out = keep(1, send_ahead(1, passed_out, []), send_behind(1))
     return product_and_divide(rot_out, all_rot_in, eig_lambda, tokens)

time: 299 us -> 283 us (0.946)
  waiting for transfers between devices: 179 us -> 153 us
  local copies, waits for them, and re-layouts: 10.5 us -> 17.4 us
  matrix products: 51.5 us -> 57 us
    ppermute x20, waiting for transfers between devices: 92.6 us -> 46.3 us  [swap(): lax.ppermute(block, 'tensor', [(j, j ^ bit) for j in range(X + Y + CORE +...]
    ppermute x12, waiting for transfers between devices: 86.1 us -> 106 us  [shift(): return lax.ppermute(block, 'dp', [(z, (z + by) % n) for z in range(n)])]
    dot_general x15 -> x16, matrix products: 40.7 us -> 47.7 us  [dot(): return jnp.dot(a, b, preferred_element_type=jnp.float32)]
    slice x7, local copies, waits for them, and re-layouts: 2.82 us -> 8.21 us  [the longest x3 4.62 us: end(): x[second]]
  transfers between devices with their start and end apart: 33 -> 33, of which waited for: 20 -> 15; matrix products, arithmetic and copies ran while one was open for 17% -> 20% of each run, Pallas kernels for 0% -> 0%
where the time goes in v17:
time: 283 us; the launch traced here: 278 us
  waiting for transfers between devices  153 us (54%)
  matrix products  57 us (20%)
  starting transfers between devices  29.8 us (11%)
  local copies, waits for them, and re-layouts  17.4 us (6%)
  between operations  15.5 us (5%)
  other arithmetic  5.72 us (2%)
    ppermute x12, waiting for transfers between devices, shift(): return lax.ppermute(block, 'dp', [(z, (z + by) % n) for z in range(n)])  106 us
    dot_general x16, matrix products, dot(): return jnp.dot(a, b, preferred_element_type=jnp.float32)  47.7 us
    ppermute x20, waiting for transfers between devices, swap(): lax.ppermute(block, 'tensor', [(j, j ^ bit) for j in range(X + Y + CORE +...  46.3 us
    ppermute x12, starting transfers between devices, shift(): return lax.ppermute(block, 'dp', [(z, (z + by) % n) for z in range(n)])  18.1 us
    ppermute x20, starting transfers between devices, swap(): lax.ppermute(block, 'tensor', [(j, j ^ bit) for j in range(X + Y + CORE +...  11.7 us
    dot_general x1, matrix products, product_and_divide(): lax.dot_general(rot_out, all_rot_in, contract, preferred_element_type=jnp...  9.34 us
  transfers between devices with their start and end apart: 33, of which 15 were waited for; matrix products, arithmetic and copies ran while one was open for 20% of the time, Pallas kernels for 0%

profile of v17, /device:TPU:16, one launch (start us, length us, event | category | flops | bytes accessed | tf_op | source)
XLA Modules:
  0.0 278.1 jit_solution(14504731626420371737)
XLA Ops:
  12.8 10.1 %collective-permute-done.2 = bf16[512,512]{1,0:T(8,128)(2,1)S(1)} collective-permute-done((bf16[512,512]{1,0:T(8,128)(2,1)S(1)}, bf16[512,512]{1,0:T(8,128)(2,1)S(1)}, u32[]{:S(2)}, u32[]{:S(2)}) %collective-permute-start.2) | collective-permute-done | bytes 524320 | tf_op jit(solution)/shard_map/ppermute | solution.py:44
  23.4 14.0 %collective-permute-done.3 = bf16[512,512]{1,0:T(8,128)(2,1)S(1)} collective-permute-done((bf16[512,512]{1,0:T(8,128)(2,1)S(1)}, bf16[512,512]{1,0:T(8,128)(2,1)S(1)}, u32[]{:S(2)}, u32[]{:S(2)}) %collective-permute-start.3) | collective-permute-done | bytes 524320 | tf_op jit(solution)/shard_map/ppermute | solution.py:44
  42.4 3.5 %collective-permute-start.7 = (bf16[512,512]{1,0:T(8,128)(2,1)S(1)}, bf16[512,512]{1,0:T(8,128)(2,1)S(1)}, u32[]{:S(2)}, u32[]{:S(2)}) collective-permute-start(bf16[512,512]{1,0:T(8,128)(2,1)S(1)} %bitcast.46), channel_id=1, source_target_pairs={{0,8},{8,16},{16,24},{24,0},{1,9},{9,17},{17,25},{25,1},{2,10},{10... | collective-permute-start | bytes 1572872 | tf_op jit(solution)/shard_map/ppermute | solution.py:44
  45.9 12.8 %collective-permute-done.8 = bf16[512,512]{1,0:T(8,128)(2,1)S(1)} collective-permute-done((bf16[512,512]{1,0:T(8,128)(2,1)S(1)}, bf16[512,512]{1,0:T(8,128)(2,1)S(1)}, u32[]{:S(2)}, u32[]{:S(2)}) %collective-permute-start.8) | collective-permute-done | bytes 524320 | tf_op jit(solution)/shard_map/ppermute | solution.py:44
  58.7 8.7 %collective-permute-done.7 = bf16[512,512]{1,0:T(8,128)(2,1)S(1)} collective-permute-done((bf16[512,512]{1,0:T(8,128)(2,1)S(1)}, bf16[512,512]{1,0:T(8,128)(2,1)S(1)}, u32[]{:S(2)}, u32[]{:S(2)}) %collective-permute-start.7) | collective-permute-done | bytes 524320 | tf_op jit(solution)/shard_map/ppermute | solution.py:44
  67.5 10.5 %collective-permute-done.9 = bf16[512,512]{1,0:T(8,128)(2,1)S(1)} collective-permute-done((bf16[512,512]{1,0:T(8,128)(2,1)S(1)}, bf16[512,512]{1,0:T(8,128)(2,1)S(1)}, u32[]{:S(2)}, u32[]{:S(2)}) %collective-permute-start.9) | collective-permute-done | bytes 524320 | tf_op jit(solution)/shard_map/ppermute | solution.py:44
  80.7 3.5 %collective-permute-start.12 = (bf16[512,512]{1,0:T(8,128)(2,1)S(1)}, bf16[512,512]{1,0:T(8,128)(2,1)S(1)}, u32[]{:S(2)}, u32[]{:S(2)}) collective-permute-start(bf16[512,512]{1,0:T(8,128)(2,1)S(1)} %bitcast.51), channel_id=1, source_target_pairs={{0,8},{8,16},{16,24},{24,0},{1,9},{9,17},{17,25},{25,1},{2,10},{10... | collective-permute-start | bytes 1572872 | tf_op jit(solution)/shard_map/ppermute | solution.py:44
  84.6 11.0 %collective-permute-done.12 = bf16[512,512]{1,0:T(8,128)(2,1)S(1)} collective-permute-done((bf16[512,512]{1,0:T(8,128)(2,1)S(1)}, bf16[512,512]{1,0:T(8,128)(2,1)S(1)}, u32[]{:S(2)}, u32[]{:S(2)}) %collective-permute-start.12) | collective-permute-done | bytes 524320 | tf_op jit(solution)/shard_map/ppermute | solution.py:44
  96.8 19.7 %collective-permute-done.13 = bf16[1536,512]{1,0:T(8,128)(2,1)S(1)} collective-permute-done((bf16[1536,512]{1,0:T(8,128)(2,1)S(1)}, bf16[1536,512]{1,0:T(8,128)(2,1)S(1)}, u32[]{:S(2)}, u32[]{:S(2)}) %collective-permute-start.13) | collective-permute-done | bytes 1572896 | tf_op jit(solution)/shard_map/ppermute | solution.py:40
  129.0 2.8 %fusion.1 = bf16[512,512]{1,0:T(8,128)(2,1)S(1)} fusion(f32[512,512]{1,0:T(8,128)} %collective-permute-done.18, bf16[512,2048]{1,0:T(8,128)(2,1)S(1)} %copy-done.7, bf16[512,512]{1,0:T(8,128)(2,1)S(1)} %get-tuple-element.101, bf16[512,512]{1,0:T(8,128)(2,1)S(1)} %get-tuple-element.102, bf16[512,512]{1,0:T(8,128)(2,1)S(1)} %get-tuple-element.100, ...), kind=kOutput, calls=%fused_computation.33 | convolution fusion | flops 1082654720 | bytes 5767168 | tf_op jit(solution)/shard_map/dot_general | solution.py:22
  131.9 3.6 %collective-permute-start.19 = (bf16[512,512]{1,0:T(8,128)(2,1)S(1)}, bf16[512,512]{1,0:T(8,128)(2,1)}, u32[]{:S(2)}, u32[]{:S(2)}) collective-permute-start(bf16[512,512]{1,0:T(8,128)(2,1)S(1)} %fusion.1), channel_id=1, source_target_pairs={{0,8},{8,16},{16,24},{24,0},{1,9},{9,17},{17,25},{25,1},{2,10},{10... | collective-permute-start | bytes 1572872 | tf_op jit(solution)/shard_map/ppermute | solution.py:44
  136.8 25.1 %collective-permute-done.15 = bf16[1536,512]{1,0:T(8,128)(2,1)} collective-permute-done((bf16[1536,512]{1,0:T(8,128)(2,1)}, bf16[1536,512]{1,0:T(8,128)(2,1)}, u32[]{:S(2)}, u32[]{:S(2)}) %collective-permute-start.15) | collective-permute-done | bytes 1572896 | tf_op jit(solution)/shard_map/ppermute | solution.py:40
  163.1 2.5 fusion.26
  165.6 2.4 fusion.27
  169.7 2.3 fusion.37
  174.9 4.2 %fusion.38 = f32[512,512]{1,0:T(8,128)} fusion(bf16[512,2048]{1,0:T(8,128)(2,1)S(1)} %pad_maximum_fusion.9, bf16[2048,512]{1,0:T(8,128)(2,1)} %copy-done.52), kind=kOutput, calls=%fused_computation.89 | convolution fusion | flops 1073741824 | bytes 5242880 | tf_op jit(solution)/shard_map/dot_general | solution.py:22
  179.2 3.3 %fusion.8 = bf16[512,512]{1,0:T(8,128)(2,1)} fusion(bf16[512,512]{1,0:T(8,128)(2,1)} %collective-permute-done.19, f32[512,512]{1,0:T(8,128)S(1)} %copy-done.59, bf16[512,2048]{1,0:T(8,128)(2,1)S(1)} %copy-done.3, pred[]{:T(512)S(6)} %eq.19, bf16[512,512]{1,0:T(8,128)(2,1)S(1)} %copy-done.42, bf16[512,512]{1,0:T(8,128)(2,1)S(1)} %copy-done.45, ...), kind=kOutput, calls=%fused_computation.40 | convolution fusion | flops 1082916864 | bytes 6291457 | tf_op jit(solution)/shard_map/dot_general | solution.py:22
  182.5 2.4 collective-permute-start.31
  184.8 3.3 %fusion.2 = bf16[512,512]{1,0:T(8,128)(2,1)} fusion(f32[512,512]{1,0:T(8,128)} %collective-permute-done.23, bf16[512,2048]{1,0:T(8,128)(2,1)S(1)} %copy-done.5, bf16[512,512]{1,0:T(8,128)(2,1)S(1)} %copy-done.42, bf16[512,512]{1,0:T(8,128)(2,1)S(1)} %copy-done.45, bf16[512,512]{1,0:T(8,128)(2,1)S(1)} %copy-done.39, bf16[512,512]{1,0:T(8,128)(2,1)S(1)} %copy-done.36), kind=kOutput, calls=%fused_computation.34 | convolution fusion | flops 1082654720 | bytes 5767168 | tf_op jit(solution)/shard_map/dot_general | solution.py:22
  189.6 4.1 %fusion.3 = bf16[512,512]{1,0:T(8,128)(2,1)} fusion(f32[512,512]{1,0:T(8,128)} %collective-permute-done.24, bf16[512,2048]{1,0:T(8,128)(2,1)S(1)} %pad_maximum_fusion.9, bf16[512,512]{1,0:T(8,128)(2,1)} %get-tuple-element.98, bf16[512,512]{1,0:T(8,128)(2,1)} %get-tuple-element.96, bf16[512,512]{1,0:T(8,128)(2,1)} %get-tuple-element.97, ...), kind=kOutput, calls=%fused_computation.35 | convolution fusion | flops 1082654720 | bytes 5767168 | tf_op jit(solution)/shard_map/dot_general | solution.py:22
  193.7 14.5 %collective-permute-done.31 = bf16[512,512]{1,0:T(8,128)(2,1)} collective-permute-done((bf16[512,512]{1,0:T(8,128)(2,1)}, bf16[512,512]{1,0:T(8,128)(2,1)}, u32[]{:S(2)}, u32[]{:S(2)}) %collective-permute-start.31) | collective-permute-done | bytes 524320 | tf_op jit(solution)/shard_map/ppermute | solution.py:44
  209.9 3.1 %fusion.9 = bf16[512,512]{1,0:T(8,128)(2,1)} fusion(f32[512,512]{1,0:T(8,128)S(1)} %copy-done.57, bf16[512,512]{1,0:T(8,128)(2,1)} %collective-permute-done.30, bf16[512,512]{1,0:T(8,128)(2,1)} %collective-permute-done.31, pred[]{:T(512)S(6)} %eq.20, pred[]{:T(512)S(6)} %eq.19, bf16[512,512]{1,0:T(8,128)(2,1)S(1)} %copy-done.15, ...), kind=kOutput, calls=%fused_computation.41 | convolution fusion | flops 1091567616 | bytes 6815746 | tf_op jit(solution)/shard_map/dot_general | solution.py:22
  213.1 4.1 %fusion.17 = f32[512,512]{1,0:T(8,128)} fusion(bf16[2048,512]{1,0:T(8,128)(2,1)} %copy-done.52, bf16[512,512]{1,0:T(8,128)(2,1)} %collective-permute-done.20, bf16[512,512]{1,0:T(8,128)(2,1)S(1)} %copy-done.29, bf16[512,512]{1,0:T(8,128)(2,1)S(1)} %copy-done.31, bf16[512,512]{1,0:T(8,128)(2,1)S(1)} %copy-done.22), kind=kOutput, calls=%fused_computation.58 | convolution fusion | flops 1082130432 | bytes 5242880 | tf_op jit(solution)/shard_map/dot_general | solution.py:22
  218.0 3.3 %fusion.16 = f32[512,512]{1,0:T(8,128)S(1)} fusion(bf16[2048,512]{1,0:T(8,128)(2,1)} %copy-done.52, bf16[512,512]{1,0:T(8,128)(2,1)} %collective-permute-done.21, bf16[512,512]{1,0:T(8,128)(2,1)S(1)} %copy-done.26, bf16[512,512]{1,0:T(8,128)(2,1)} %get-tuple-element.87, bf16[512,512]{1,0:T(8,128)(2,1)S(1)} %copy-done.20), kind=kOutput, calls=%fused_computation.57 | convolution fusion | flops 1082130432 | bytes 5242880 | tf_op jit(solution)/shard_map/dot_general | solution.py:22
  221.9 2.2 fusion.18
  225.3 3.5 %fusion.4 = bf16[512,512]{1,0:T(8,128)(2,1)} fusion(f32[512,512]{1,0:T(8,128)} %collective-permute-done.25, bf16[512,512]{1,0:T(8,128)(2,1)} %collective-permute-done.20, bf16[512,512]{1,0:T(8,128)(2,1)S(1)} %copy-done.30, bf16[512,512]{1,0:T(8,128)(2,1)S(1)} %copy-done.32, bf16[512,512]{1,0:T(8,128)(2,1)S(1)} %copy-done.22, ...), kind=kOutput, calls=%fused_computation.36 | convolution fusion | flops 1091043328 | bytes 5767168 | tf_op jit(solution)/shard_map/dot_general | solution.py:22
  229.8 8.6 %collective-permute-done.28 = bf16[512,512]{1,0:T(8,128)(2,1)S(1)} collective-permute-done((bf16[512,512]{1,0:T(8,128)(2,1)S(1)}, bf16[512,512]{1,0:T(8,128)(2,1)S(1)}, u32[]{:S(2)}, u32[]{:S(2)}) %collective-permute-start.28) | collective-permute-done | bytes 524320 | tf_op jit(solution)/shard_map/ppermute | solution.py:44
  238.4 3.1 %fusion.10 = bf16[512,512]{1,0:T(8,128)(2,1)} fusion(bf16[512,512]{1,0:T(8,128)(2,1)S(1)} %collective-permute-done.28, f32[512,512]{1,0:T(8,128)S(1)} %collective-permute-done.27, pred[]{:T(512)S(6)} %eq.17, bf16[512,512]{1,0:T(8,128)(2,1)} %collective-permute-done.21, bf16[512,512]{1,0:T(8,128)(2,1)S(1)} %copy-done.26, ...), kind=kOutput, calls=%fused_computation.42 | convolution fusion | flops 1091305472 | bytes 6291457 | tf_op jit(solution)/shard_map/dot_general | solution.py:22
  243.6 3.8 %fusion.19 = f32[512,512]{1,0:T(8,128)} fusion(bf16[512,512]{1,0:T(8,128)(2,1)S(1)} %copy-done.25, bf16[512,512]{1,0:T(8,128)(2,1)S(1)} %copy-done.9, bf16[512,512]{1,0:T(8,128)(2,1)S(1)} %copy-done.34, bf16[512,512]{1,0:T(8,128)(2,1)S(1)} %bitcast.53, bf16[512,512]{1,0:T(8,128)(2,1)} %get-tuple-element.98, bf16[512,512]{1,0:T(8,128)(2,1)} %get-tuple-element.96, ...), kind=kOutput, calls=%fused_computation.60 | convolution fusion | flops 1090519040 | bytes 5242880 | tf_op jit(solution)/shard_map/dot_general | solution.py:22
  247.4 4.9 %collective-permute-done.26 = bf16[512,512]{1,0:T(8,128)(2,1)} collective-permute-done((bf16[512,512]{1,0:T(8,128)(2,1)}, bf16[512,512]{1,0:T(8,128)(2,1)}, u32[]{:S(2)}, u32[]{:S(2)}) %collective-permute-start.26) | collective-permute-done | bytes 524320 | tf_op jit(solution)/shard_map/ppermute | solution.py:44
  252.3 9.6 %collective-permute-done.29 = bf16[512,512]{1,0:T(8,128)(2,1)S(1)} collective-permute-done((bf16[512,512]{1,0:T(8,128)(2,1)}, bf16[512,512]{1,0:T(8,128)(2,1)S(1)}, u32[]{:S(2)}, u32[]{:S(2)}) %collective-permute-start.29) | collective-permute-done | bytes 524320 | tf_op jit(solution)/shard_map/ppermute | solution.py:44
  261.9 9.3 %fusion = bf16[1,512,4096]{2,1,0:T(8,128)(2,1)} fusion(bf16[512,4096]{1,0:T(8,128)(2,1)} %param.11, bf16[512,4096]{1,0:T(8,128)(2,1)} %all-gather.2.cloned.1.call-done, f32[512,512]{1,0:T(8,128)} %fusion.19, f32[512,512]{1,0:T(8,128)} %collective-permute-done.11, bf16[512,512]{1,0:T(8,128)(2,1)} %collective-permute-done.26, ...), kind=kOutput, calls=%fused_computation.1 | convolution fusion | flops 2159017984 | bytes 15728642 | tf_op jit(solution)/shard_map/dot_general | solution.py:13
  (197 shorter events, 42.8 us)
Async XLA Ops:
  6.5 255.4 %all-gather.2.cloned.1.call-start = ((), (), s32[]{:S(2)}) async-start(), calls=%async_computation | async-start | bytes 4718592 | tf_op jit(solution)/shard_map/all_gather | solution.py:162
  8.4 29.0 %collective-permute-start.4 = (bf16[2048,512]{1,0:T(8,128)(2,1)S(1)}, bf16[2048,512]{1,0:T(8,128)(2,1)S(1)}, u32[]{:S(2)}, u32[]{:S(2)}) collective-permute-start(bf16[2048,512]{1,0:T(8,128)(2,1)S(1)} %pad_maximum_fusion), channel_id=1, source_target_pairs={{0,1},{1,0},{2,3},{3,2},{4,5},{5,4},{6,7},{7,6},{8,9},{9,8},{10,11... | collective-permute-start | bytes 6291464 | tf_op jit(solution)/shard_map/ppermute | solution.py:40
  9.2 13.7 %collective-permute-start.2 = (bf16[512,512]{1,0:T(8,128)(2,1)S(1)}, bf16[512,512]{1,0:T(8,128)(2,1)S(1)}, u32[]{:S(2)}, u32[]{:S(2)}) collective-permute-start(bf16[512,512]{1,0:T(8,128)(2,1)S(1)} %bitcast.44), channel_id=1, source_target_pairs={{0,24},{8,0},{16,8},{24,16},{1,25},{9,1},{17,9},{25,17},{2,26},{10... | collective-permute-start | bytes 1572872 | tf_op jit(solution)/shard_map/ppermute | solution.py:44
  9.8 27.6 %collective-permute-start = (bf16[1024,512]{1,0:T(8,128)(2,1)S(1)}, bf16[1024,512]{1,0:T(8,128)(2,1)S(1)}, u32[]{:S(2)}, u32[]{:S(2)}) collective-permute-start(bf16[1024,512]{1,0:T(8,128)(2,1)S(1)} %pad_maximum_fusion.24), channel_id=1, source_target_pairs={{0,2},{1,3},{2,0},{3,1},{4,6},{5,7},{6,4},{7,5},{8,10},{9,11},{10,... | collective-permute-start | bytes 3145736 | tf_op jit(solution)/shard_map/ppermute | solution.py:40
  11.3 26.0 %collective-permute-start.1 = (bf16[1024,512]{1,0:T(8,128)(2,1)S(1)}, bf16[1024,512]{1,0:T(8,128)(2,1)S(1)}, u32[]{:S(2)}, u32[]{:S(2)}) collective-permute-start(bf16[1024,512]{1,0:T(8,128)(2,1)S(1)} %pad_maximum_fusion.24), channel_id=1, source_target_pairs={{0,4},{1,5},{2,6},{3,7},{4,0},{5,1},{6,2},{7,3},{8,12},{9,13},{10,... | collective-permute-start | bytes 3145736 | tf_op jit(solution)/shard_map/ppermute | solution.py:40
  22.9 14.4 %collective-permute-start.3 = (bf16[512,512]{1,0:T(8,128)(2,1)S(1)}, bf16[512,512]{1,0:T(8,128)(2,1)S(1)}, u32[]{:S(2)}, u32[]{:S(2)}) collective-permute-start(bf16[512,512]{1,0:T(8,128)(2,1)S(1)} %collective-permute-done.2), channel_id=1, source_target_pairs={{0,24},{8,0},{16,8},{24,16},{1,25},{9,1},{17,9},{25,17},{2,26},{10... | collective-permute-start | bytes 1572872 | tf_op jit(solution)/shard_map/ppermute | solution.py:44
  39.3 38.6 %collective-permute-start.5 = (bf16[1536,512]{1,0:T(8,128)(2,1)S(1)}, bf16[1536,512]{1,0:T(8,128)(2,1)S(1)}, u32[]{:S(2)}, u32[]{:S(2)}) collective-permute-start(bf16[1536,512]{1,0:T(8,128)(2,1)S(1)} %get-tuple-element.57), channel_id=1, source_target_pairs={{0,2},{1,3},{2,0},{3,1},{4,6},{5,7},{6,4},{7,5},{8,10},{9,11},{10,... | collective-permute-start | bytes 4718600 | tf_op jit(solution)/shard_map/ppermute | solution.py:40
  40.8 37.1 %collective-permute-start.6 = (bf16[1536,512]{1,0:T(8,128)(2,1)S(1)}, bf16[1536,512]{1,0:T(8,128)(2,1)S(1)}, u32[]{:S(2)}, u32[]{:S(2)}) collective-permute-start(bf16[1536,512]{1,0:T(8,128)(2,1)S(1)} %get-tuple-element.58), channel_id=1, source_target_pairs={{0,4},{1,5},{2,6},{3,7},{4,0},{5,1},{6,2},{7,3},{8,12},{9,13},{10,... | collective-permute-start | bytes 4718600 | tf_op jit(solution)/shard_map/ppermute | solution.py:40
  42.4 16.4 %collective-permute-start.8 = (bf16[512,512]{1,0:T(8,128)(2,1)S(1)}, bf16[512,512]{1,0:T(8,128)(2,1)S(1)}, u32[]{:S(2)}, u32[]{:S(2)}) collective-permute-start(bf16[512,512]{1,0:T(8,128)(2,1)S(1)} %bitcast.50), channel_id=1, source_target_pairs={{0,24},{8,0},{16,8},{24,16},{1,25},{9,1},{17,9},{25,17},{2,26},{10... | collective-permute-start | bytes 1572872 | tf_op jit(solution)/shard_map/ppermute | solution.py:44
  42.4 25.1 %collective-permute-start.7 = (bf16[512,512]{1,0:T(8,128)(2,1)S(1)}, bf16[512,512]{1,0:T(8,128)(2,1)S(1)}, u32[]{:S(2)}, u32[]{:S(2)}) collective-permute-start(bf16[512,512]{1,0:T(8,128)(2,1)S(1)} %bitcast.46), channel_id=1, source_target_pairs={{0,8},{8,16},{16,24},{24,0},{1,9},{9,17},{17,25},{25,1},{2,10},{10... | collective-permute-start | bytes 1572872 | tf_op jit(solution)/shard_map/ppermute | solution.py:44
  58.7 19.2 %collective-permute-start.9 = (bf16[512,512]{1,0:T(8,128)(2,1)S(1)}, bf16[512,512]{1,0:T(8,128)(2,1)S(1)}, u32[]{:S(2)}, u32[]{:S(2)}) collective-permute-start(bf16[512,512]{1,0:T(8,128)(2,1)S(1)} %collective-permute-done.8), channel_id=1, source_target_pairs={{0,24},{8,0},{16,8},{24,16},{1,25},{9,1},{17,9},{25,17},{2,26},{10... | collective-permute-start | bytes 1572872 | tf_op jit(solution)/shard_map/ppermute | solution.py:44
  78.4 38.3 %collective-permute-start.10 = (bf16[2048,512]{1,0:T(8,128)(2,1)S(1)}, bf16[2048,512]{1,0:T(8,128)(2,1)S(1)}, u32[]{:S(2)}, u32[]{:S(2)}) collective-permute-start(bf16[2048,512]{1,0:T(8,128)(2,1)S(1)} %pad_maximum_fusion.3), channel_id=1, source_target_pairs={{0,1},{1,0},{2,3},{3,2},{4,5},{5,4},{6,7},{7,6},{8,9},{9,8},{10,11... | collective-permute-start | bytes 6291464 | tf_op jit(solution)/shard_map/ppermute | solution.py:40
  79.6 36.9 %collective-permute-start.13 = (bf16[1536,512]{1,0:T(8,128)(2,1)S(1)}, bf16[1536,512]{1,0:T(8,128)(2,1)S(1)}, u32[]{:S(2)}, u32[]{:S(2)}) collective-permute-start(bf16[1536,512]{1,0:T(8,128)(2,1)S(1)} %get-tuple-element.69), channel_id=1, source_target_pairs={{0,2},{1,3},{2,0},{3,1},{4,6},{5,7},{6,4},{7,5},{8,10},{9,11},{10,... | collective-permute-start | bytes 4718600 | tf_op jit(solution)/shard_map/ppermute | solution.py:40
  80.2 36.5 %collective-permute-start.14 = (bf16[1536,512]{1,0:T(8,128)(2,1)S(1)}, bf16[1536,512]{1,0:T(8,128)(2,1)S(1)}, u32[]{:S(2)}, u32[]{:S(2)}) collective-permute-start(bf16[1536,512]{1,0:T(8,128)(2,1)S(1)} %get-tuple-element.70), channel_id=1, source_target_pairs={{0,4},{1,5},{2,6},{3,7},{4,0},{5,1},{6,2},{7,3},{8,12},{9,13},{10,... | collective-permute-start | bytes 4718600 | tf_op jit(solution)/shard_map/ppermute | solution.py:40
  80.7 14.8 %collective-permute-start.12 = (bf16[512,512]{1,0:T(8,128)(2,1)S(1)}, bf16[512,512]{1,0:T(8,128)(2,1)S(1)}, u32[]{:S(2)}, u32[]{:S(2)}) collective-permute-start(bf16[512,512]{1,0:T(8,128)(2,1)S(1)} %bitcast.51), channel_id=1, source_target_pairs={{0,8},{8,16},{16,24},{24,0},{1,9},{9,17},{17,25},{25,1},{2,10},{10... | collective-permute-start | bytes 1572872 | tf_op jit(solution)/shard_map/ppermute | solution.py:44
  122.8 5.8 %collective-permute-start.18 = (f32[512,512]{1,0:T(8,128)}, f32[512,512]{1,0:T(8,128)}, u32[]{:S(2)}, u32[]{:S(2)}) collective-permute-start(f32[512,512]{1,0:T(8,128)} %fusion.35), channel_id=1, source_target_pairs={{0,1},{1,0},{2,3},{3,2},{4,5},{5,4},{6,7},{7,6},{8,9},{9,8},{10,11... | collective-permute-start | bytes 3145736 | tf_op jit(solution)/shard_map/ppermute | solution.py:40
  124.8 37.1 %collective-permute-start.15 = (bf16[1536,512]{1,0:T(8,128)(2,1)}, bf16[1536,512]{1,0:T(8,128)(2,1)}, u32[]{:S(2)}, u32[]{:S(2)}) collective-permute-start(bf16[1536,512]{1,0:T(8,128)(2,1)} %get-tuple-element.77), channel_id=1, source_target_pairs={{0,2},{1,3},{2,0},{3,1},{4,6},{5,7},{6,4},{7,5},{8,10},{9,11},{10,... | collective-permute-start | bytes 4718600 | tf_op jit(solution)/shard_map/ppermute | solution.py:40
  126.3 36.8 %collective-permute-start.16 = (bf16[1536,512]{1,0:T(8,128)(2,1)}, bf16[1536,512]{1,0:T(8,128)(2,1)}, u32[]{:S(2)}, u32[]{:S(2)}) collective-permute-start(bf16[1536,512]{1,0:T(8,128)(2,1)} %get-tuple-element.78), channel_id=1, source_target_pairs={{0,4},{1,5},{2,6},{3,7},{4,0},{5,1},{6,2},{7,3},{8,12},{9,13},{10,... | collective-permute-start | bytes 4718600 | tf_op jit(solution)/shard_map/ppermute | solution.py:40
  131.9 31.2 %collective-permute-start.19 = (bf16[512,512]{1,0:T(8,128)(2,1)S(1)}, bf16[512,512]{1,0:T(8,128)(2,1)}, u32[]{:S(2)}, u32[]{:S(2)}) collective-permute-start(bf16[512,512]{1,0:T(8,128)(2,1)S(1)} %fusion.1), channel_id=1, source_target_pairs={{0,8},{8,16},{16,24},{24,0},{1,9},{9,17},{17,25},{25,1},{2,10},{10... | collective-permute-start | bytes 1572872 | tf_op jit(solution)/shard_map/ppermute | solution.py:44
  163.1 6.4 %collective-permute-start.22 = (f32[512,512]{1,0:T(8,128)S(1)}, f32[512,512]{1,0:T(8,128)S(1)}, u32[]{:S(2)}, u32[]{:S(2)}) collective-permute-start(f32[512,512]{1,0:T(8,128)S(1)} %fusion.36), channel_id=1, source_target_pairs={{0,1},{1,0},{2,3},{3,2},{4,5},{5,4},{6,7},{7,6},{8,9},{9,8},{10,11... | collective-permute-start | bytes 3145736 | tf_op jit(solution)/shard_map/ppermute | solution.py:40
  171.9 12.9 %collective-permute-start.23 = (f32[512,512]{1,0:T(8,128)}, f32[512,512]{1,0:T(8,128)}, u32[]{:S(2)}, u32[]{:S(2)}) collective-permute-start(f32[512,512]{1,0:T(8,128)} %fusion.37), channel_id=1, source_target_pairs={{0,1},{1,0},{2,3},{3,2},{4,5},{5,4},{6,7},{7,6},{8,9},{9,8},{10,11... | collective-permute-start | bytes 3145736 | tf_op jit(solution)/shard_map/ppermute | solution.py:40
  173.8 19.8 %collective-permute-start.20 = (bf16[512,512]{1,0:T(8,128)(2,1)}, bf16[512,512]{1,0:T(8,128)(2,1)}, u32[]{:S(2)}, u32[]{:S(2)}) collective-permute-start(bf16[512,512]{1,0:T(8,128)(2,1)} %get-tuple-element.86), channel_id=1, source_target_pairs={{0,2},{1,3},{2,0},{3,1},{4,6},{5,7},{6,4},{7,5},{8,10},{9,11},{10,... | collective-permute-start | bytes 1572872 | tf_op jit(solution)/shard_map/ppermute | solution.py:40
  174.4 19.3 %collective-permute-start.21 = (bf16[512,512]{1,0:T(8,128)(2,1)S(1)}, bf16[512,512]{1,0:T(8,128)(2,1)}, u32[]{:S(2)}, u32[]{:S(2)}) collective-permute-start(bf16[512,512]{1,0:T(8,128)(2,1)S(1)} %copy-done.27), channel_id=1, source_target_pairs={{0,4},{1,5},{2,6},{3,7},{4,0},{5,1},{6,2},{7,3},{8,12},{9,13},{10,... | collective-permute-start | bytes 1572872 | tf_op jit(solution)/shard_map/ppermute | solution.py:40
  179.1 10.4 %collective-permute-start.24 = (f32[512,512]{1,0:T(8,128)}, f32[512,512]{1,0:T(8,128)}, u32[]{:S(2)}, u32[]{:S(2)}) collective-permute-start(f32[512,512]{1,0:T(8,128)} %fusion.38), channel_id=1, source_target_pairs={{0,1},{1,0},{2,3},{3,2},{4,5},{5,4},{6,7},{7,6},{8,9},{9,8},{10,11... | collective-permute-start | bytes 3145736 | tf_op jit(solution)/shard_map/ppermute | solution.py:40
  182.5 25.7 %collective-permute-start.31 = (bf16[512,512]{1,0:T(8,128)(2,1)}, bf16[512,512]{1,0:T(8,128)(2,1)}, u32[]{:S(2)}, u32[]{:S(2)}) collective-permute-start(bf16[512,512]{1,0:T(8,128)(2,1)} %fusion.8), channel_id=1, source_target_pairs={{0,8},{8,16},{16,24},{24,0},{1,9},{9,17},{17,25},{25,1},{2,10},{10... | collective-permute-start | bytes 1572872 | tf_op jit(solution)/shard_map/ppermute | solution.py:44
  188.1 21.7 %collective-permute-start.30 = (bf16[512,512]{1,0:T(8,128)(2,1)}, bf16[512,512]{1,0:T(8,128)(2,1)}, u32[]{:S(2)}, u32[]{:S(2)}) collective-permute-start(bf16[512,512]{1,0:T(8,128)(2,1)} %fusion.2), channel_id=1, source_target_pairs={{0,24},{8,0},{16,8},{24,16},{1,25},{9,1},{17,9},{25,17},{2,26},{10... | collective-permute-start | bytes 1572872 | tf_op jit(solution)/shard_map/ppermute | solution.py:44
  217.1 8.2 %collective-permute-start.25 = (f32[512,512]{1,0:T(8,128)}, f32[512,512]{1,0:T(8,128)}, u32[]{:S(2)}, u32[]{:S(2)}) collective-permute-start(f32[512,512]{1,0:T(8,128)} %fusion.17), channel_id=1, source_target_pairs={{0,1},{1,0},{2,3},{3,2},{4,5},{5,4},{6,7},{7,6},{8,9},{9,8},{10,11... | collective-permute-start | bytes 3145736 | tf_op jit(solution)/shard_map/ppermute | solution.py:40
  221.3 17.1 %collective-permute-start.27 = (f32[512,512]{1,0:T(8,128)S(1)}, f32[512,512]{1,0:T(8,128)S(1)}, u32[]{:S(2)}, u32[]{:S(2)}) collective-permute-start(f32[512,512]{1,0:T(8,128)S(1)} %fusion.16), channel_id=1, source_target_pairs={{0,1},{1,0},{2,3},{3,2},{4,5},{5,4},{6,7},{7,6},{8,9},{9,8},{10,11... | collective-permute-start | bytes 3145736 | tf_op jit(solution)/shard_map/ppermute | solution.py:40
  224.1 23.3 %collective-permute-start.11 = (f32[512,512]{1,0:T(8,128)}, f32[512,512]{1,0:T(8,128)}, u32[]{:S(2)}, u32[]{:S(2)}) collective-permute-start(f32[512,512]{1,0:T(8,128)} %fusion.18), channel_id=1, source_target_pairs={{0,1},{1,0},{2,3},{3,2},{4,5},{5,4},{6,7},{7,6},{8,9},{9,8},{10,11... | collective-permute-start | bytes 3145736 | tf_op jit(solution)/shard_map/ppermute | solution.py:40
  224.2 14.2 %collective-permute-start.28 = (bf16[512,512]{1,0:T(8,128)(2,1)S(1)}, bf16[512,512]{1,0:T(8,128)(2,1)S(1)}, u32[]{:S(2)}, u32[]{:S(2)}) collective-permute-start(bf16[512,512]{1,0:T(8,128)(2,1)S(1)} %copy-done.60), channel_id=1, source_target_pairs={{0,8},{8,16},{16,24},{24,0},{1,9},{9,17},{17,25},{25,1},{2,10},{10... | collective-permute-start | bytes 1572872 | tf_op jit(solution)/shard_map/ppermute | solution.py:44
  228.8 23.5 %collective-permute-start.26 = (bf16[512,512]{1,0:T(8,128)(2,1)}, bf16[512,512]{1,0:T(8,128)(2,1)}, u32[]{:S(2)}, u32[]{:S(2)}) collective-permute-start(bf16[512,512]{1,0:T(8,128)(2,1)} %fusion.4), channel_id=1, source_target_pairs={{0,24},{8,0},{16,8},{24,16},{1,25},{9,1},{17,9},{25,17},{2,26},{10... | collective-permute-start | bytes 1572872 | tf_op jit(solution)/shard_map/ppermute | solution.py:44
  241.5 20.4 %collective-permute-start.29 = (bf16[512,512]{1,0:T(8,128)(2,1)}, bf16[512,512]{1,0:T(8,128)(2,1)S(1)}, u32[]{:S(2)}, u32[]{:S(2)}) collective-permute-start(bf16[512,512]{1,0:T(8,128)(2,1)} %fusion.10), channel_id=1, source_target_pairs={{0,8},{8,16},{16,24},{24,0},{1,9},{9,17},{17,25},{25,1},{2,10},{10... | collective-permute-start | bytes 1572872 | tf_op jit(solution)/shard_map/ppermute | solution.py:44
  (62 other events, 667.8 us)
Sparse Core Ops, SparseCore 0:
  213.1 38.4 all-gather.1

commit v18 on v15

--- a/solution.py
+++ b/solution.py
@@ -63,7 +63,11 @@
     found = [0, X, Y, X + Y]
     held = (basis_in_held[0], basis_out_held[0])
     ours = [in_order(block, column, found) for block in held]
-    theirs = [swap(in_order(block, column, [CORE + i for i in found]), CORE) for block in held]
+
+    def rows_for_other(side, gate):
+        return swap(in_order(after(held[side], gate), column, [CORE + i for i in found]), CORE)
+
+    theirs = [rows_for_other(0, []), None]
 
     pieces = {(0, 0): own[0], (1, 0): own[1]}
     rotated = {}
@@ -120,33 +124,35 @@
 
     stacks, evens = {}, {}
     due = slot(0, [])
-    due += [fetch(0, 1, []), fetch(0, 2, [])] + theirs
+    due += [fetch(0, 1, []), fetch(0, 2, []), theirs[0]]
 
     gate, due = due, slot(1, due)
     due += [fetch(0, 3, gate), fetch(1, 1, gate), fetch(1, 2, gate)]
-
-    def begun(at, gate):
-        corner = after(stacks[at][1][:16, :128], gate)
-        return after(evens[at], swap(corner, CORE))
+    inverse = after(1 / (tokens * (eig_lambda.astype(jnp.float32) + damping)), [])
+    due.append(inverse)
 
     gate, due = due, slot(2, due)
-    due += [fetch(1, 3, gate)] + rotate(groups[0], begun(0, gate))
+    theirs[1] = rows_for_other(1, gate)
+    due += [fetch(1, 3, gate), theirs[1]]
 
     gate, due = due, slot(3, due)
-    rotate(groups[1], begun(1, gate))
+    rotate(groups[1], after(evens[1], gate))
     passed_in = pass_on(0)
     due.append(passed_in)
+    rotate(groups[0], after(evens[0], gate))
 
     gate, due = due, slot(4, due)
     in_from_behind = send_ahead(0, passed_in, gate)
-    ready = rotate(groups[2], begun(2, gate))
+    ready = rotate(groups[2], after(evens[2], gate))
     in_from_ahead = send_behind(0)
     passed_out = pass_on(1)
-    ready += rotate(groups[3], after(evens[3], due))
+    ready += rotate(groups[3], after(evens[3], rotated[0, 3]))
     rot_in = after(keep(0, in_from_behind, in_from_ahead), ready)
     all_rot_in = lax.all_gather(rot_in, "tensor", axis=1, tiled=True)
     rot_out = keep(1, send_ahead(1, passed_out, []), send_behind(1))
-    return product_and_divide(rot_out, all_rot_in, eig_lambda, tokens)
+    contract = (((0,), (0,)), ((), ()))
+    product = lax.dot_general(rot_out, all_rot_in, contract, preferred_element_type=jnp.float32)
+    return (product * inverse).astype(jnp.bfloat16)[None]
 
 
 def solution(mesh):

time: 263 us -> 257 us (0.977)
  waiting for transfers between devices: 159 us -> 131 us
  matrix products: 32.5 us -> 45.5 us
  local copies, waits for them, and re-layouts: 13 us -> 18.5 us
  other arithmetic: 7.97 us -> 11.7 us
    ppermute x12, waiting for transfers between devices: 104 us -> 54.6 us  [shift(): return lax.ppermute(block, 'dp', [(z, (z + by) % n) for z in range(n)])]
    ppermute x20, waiting for transfers between devices: 54.6 us -> 75.7 us  [swap(): lax.ppermute(block, 'tensor', [(j, j ^ bit) for j in range(X + Y + CORE +...]
    dot_general x16 -> x15, matrix products: 23.8 us -> 34.2 us  [dot(): return jnp.dot(a, b, preferred_element_type=jnp.float32)]
    div x0 -> x1, other arithmetic: none -> 4.51 us  [move_inputs(): 1 / (tokens * (eig_lambda.astype(jnp.float32) + damping))]
    unnamed x70, local copies, waits for them, and re-layouts: 3.16 us -> 7.45 us
    ppermute x20, starting transfers between devices: 15.4 us -> 11.4 us  [swap(): lax.ppermute(block, 'tensor', [(j, j ^ bit) for j in range(X + Y + CORE +...]
  transfers between devices with their start and end apart: 33 -> 33, of which waited for: 18 -> 18; matrix products, arithmetic and copies ran while one was open for 14% -> 20% of each run, Pallas kernels for 0% -> 0%
where the time goes in v18:
time: 257 us; the launch traced here: 253 us
  waiting for transfers between devices  131 us (51%)
  matrix products  45.5 us (18%)
  starting transfers between devices  31.4 us (12%)
  local copies, waits for them, and re-layouts  18.5 us (7%)
  between operations  15.1 us (6%)
  other arithmetic  11.7 us (5%)
    ppermute x20, waiting for transfers between devices, swap(): lax.ppermute(block, 'tensor', [(j, j ^ bit) for j in range(X + Y + CORE +...  75.7 us
    ppermute x12, waiting for transfers between devices, shift(): return lax.ppermute(block, 'dp', [(z, (z + by) % n) for z in range(n)])  54.6 us
    dot_general x15, matrix products, dot(): return jnp.dot(a, b, preferred_element_type=jnp.float32)  34.2 us
    ppermute x12, starting transfers between devices, shift(): return lax.ppermute(block, 'dp', [(z, (z + by) % n) for z in range(n)])  20 us
    ppermute x20, starting transfers between devices, swap(): lax.ppermute(block, 'tensor', [(j, j ^ bit) for j in range(X + Y + CORE +...  11.4 us
    dot_general x1, matrix products, move_inputs(): lax.dot_general(rot_out, all_rot_in, contract, preferred_element_type=jnp...  11.3 us
    unnamed x70, local copies, waits for them, and re-layouts  7.45 us
  transfers between devices with their start and end apart: 33, of which 18 were waited for; matrix products, arithmetic and copies ran while one was open for 20% of the time, Pallas kernels for 0%

profile of v18, /device:TPU:16, one launch (start us, length us, event | category | flops | bytes accessed | tf_op | source)
XLA Modules:
  0.0 252.6 jit_solution(791191414646428058)
XLA Ops:
  6.5 1.7 constant_dynamic-slice_fusion.8
  9.5 1.6 collective-permute-start
  13.0 12.7 %collective-permute-done.2 = bf16[512,512]{1,0:T(8,128)(2,1)S(1)} collective-permute-done((bf16[512,512]{1,0:T(8,128)(2,1)S(1)}, bf16[512,512]{1,0:T(8,128)(2,1)S(1)}, u32[]{:S(2)}, u32[]{:S(2)}) %collective-permute-start.2) | collective-permute-done | bytes 524320 | tf_op jit(solution)/shard_map/ppermute | solution.py:44
  26.1 8.3 %collective-permute-done = bf16[1024,512]{1,0:T(8,128)(2,1)S(1)} collective-permute-done((bf16[1024,512]{1,0:T(8,128)(2,1)S(1)}, bf16[1024,512]{1,0:T(8,128)(2,1)S(1)}, u32[]{:S(2)}, u32[]{:S(2)}) %collective-permute-start) | collective-permute-done | bytes 1048608 | tf_op jit(solution)/shard_map/ppermute | solution.py:40
  36.9 2.6 %collective-permute-done.3 = bf16[512,512]{1,0:T(8,128)(2,1)S(1)} collective-permute-done((bf16[512,512]{1,0:T(8,128)(2,1)S(1)}, bf16[512,512]{1,0:T(8,128)(2,1)S(1)}, u32[]{:S(2)}, u32[]{:S(2)}) %collective-permute-start.3) | collective-permute-done | bytes 524320 | tf_op jit(solution)/shard_map/ppermute | solution.py:44
  42.6 4.5 %multiply_divide_fusion = f32[512,4096]{1,0:T(8,128)} fusion(bf16[512,4096]{1,0:T(8,128)(2,1)S(1)} %copy-done), kind=kLoop, calls=%fused_computation.1 | loop fusion | flops 8388608 | bytes 12582912 | tf_op jit(solution)/shard_map/div | solution.py:131
  47.1 3.5 %collective-permute-start.7 = (bf16[512,512]{1,0:T(8,128)(2,1)S(1)}, bf16[512,512]{1,0:T(8,128)(2,1)S(1)}, u32[]{:S(2)}, u32[]{:S(2)}) collective-permute-start(bf16[512,512]{1,0:T(8,128)(2,1)S(1)} %bitcast.53), channel_id=1, source_target_pairs={{0,8},{8,16},{16,24},{24,0},{1,9},{9,17},{17,25},{25,1},{2,10},{10... | collective-permute-start | bytes 1572872 | tf_op jit(solution)/shard_map/ppermute | solution.py:44
  50.7 7.3 %collective-permute-done.8 = bf16[512,512]{1,0:T(8,128)(2,1)S(1)} collective-permute-done((bf16[512,512]{1,0:T(8,128)(2,1)S(1)}, bf16[512,512]{1,0:T(8,128)(2,1)S(1)}, u32[]{:S(2)}, u32[]{:S(2)}) %collective-permute-start.8) | collective-permute-done | bytes 524320 | tf_op jit(solution)/shard_map/ppermute | solution.py:44
  58.0 16.3 %collective-permute-done.5 = bf16[1536,512]{1,0:T(8,128)(2,1)S(1)} collective-permute-done((bf16[1536,512]{1,0:T(8,128)(2,1)S(1)}, bf16[1536,512]{1,0:T(8,128)(2,1)S(1)}, u32[]{:S(2)}, u32[]{:S(2)}) %collective-permute-start.5) | collective-permute-done | bytes 1572896 | tf_op jit(solution)/shard_map/ppermute | solution.py:40
  77.2 1.9 pad_maximum_fusion.16
  84.0 1.8 dynamic-slice_bitcast_fusion.3
  87.9 3.6 %collective-permute-start.12 = (bf16[512,512]{1,0:T(8,128)(2,1)S(1)}, bf16[512,512]{1,0:T(8,128)(2,1)S(1)}, u32[]{:S(2)}, u32[]{:S(2)}) collective-permute-start(bf16[512,512]{1,0:T(8,128)(2,1)S(1)} %bitcast.57), channel_id=1, source_target_pairs={{0,8},{8,16},{16,24},{24,0},{1,9},{9,17},{17,25},{25,1},{2,10},{10... | collective-permute-start | bytes 1572872 | tf_op jit(solution)/shard_map/ppermute | solution.py:44
  91.9 20.6 %collective-permute-done.10 = bf16[1536,512]{1,0:T(8,128)(2,1)} collective-permute-done((bf16[1536,512]{1,0:T(8,128)(2,1)}, bf16[1536,512]{1,0:T(8,128)(2,1)}, u32[]{:S(2)}, u32[]{:S(2)}) %collective-permute-start.10) | collective-permute-done | bytes 1572896 | tf_op jit(solution)/shard_map/ppermute | solution.py:40
  114.7 1.5 fusion.20
  125.8 3.0 %collective-permute-start.18 = (bf16[512,512]{1,0:T(8,128)(2,1)S(1)}, bf16[512,512]{1,0:T(8,128)(2,1)S(1)}, u32[]{:S(2)}, u32[]{:S(2)}) collective-permute-start(bf16[512,512]{1,0:T(8,128)(2,1)S(1)} %fusion.2), channel_id=1, source_target_pairs={{0,8},{8,16},{16,24},{24,0},{1,9},{9,17},{17,25},{25,1},{2,10},{10... | collective-permute-start | bytes 1572872 | tf_op jit(solution)/shard_map/ppermute | solution.py:44
  128.9 21.0 %collective-permute-done.15 = bf16[1536,512]{1,0:T(8,128)(2,1)S(1)} collective-permute-done((bf16[1536,512]{1,0:T(8,128)(2,1)S(1)}, bf16[1536,512]{1,0:T(8,128)(2,1)S(1)}, u32[]{:S(2)}, u32[]{:S(2)}) %collective-permute-start.15) | collective-permute-done | bytes 1572896 | tf_op jit(solution)/shard_map/ppermute | solution.py:40
  158.0 2.3 collective-permute-start.31
  160.3 2.8 %fusion.28 = f32[512,512]{1,0:T(8,128)S(1)} fusion(bf16[512,2048]{1,0:T(8,128)(2,1)S(1)} %pad_maximum_fusion.11, bf16[2048,512]{1,0:T(8,128)(2,1)} %collective-permute-done.13), kind=kOutput, calls=%fused_computation.82 | convolution fusion | flops 1073741824 | bytes 5242880 | tf_op jit(solution)/shard_map/dot_general | solution.py:22
  163.1 5.8 %collective-permute-done.19 = bf16[512,512]{1,0:T(8,128)(2,1)S(1)} collective-permute-done((bf16[512,512]{1,0:T(8,128)(2,1)S(1)}, bf16[512,512]{1,0:T(8,128)(2,1)S(1)}, u32[]{:S(2)}, u32[]{:S(2)}) %collective-permute-start.19) | collective-permute-done | bytes 524320 | tf_op jit(solution)/shard_map/ppermute | solution.py:40
  171.9 3.8 %fusion.27 = f32[512,512]{1,0:T(8,128)} fusion(bf16[512,2048]{1,0:T(8,128)(2,1)S(1)} %pad_maximum_fusion.8, bf16[2048,512]{1,0:T(8,128)(2,1)} %collective-permute-done.13), kind=kOutput, calls=%fused_computation.81 | convolution fusion | flops 1073741824 | bytes 5242880 | tf_op jit(solution)/shard_map/dot_general | solution.py:22
  175.7 3.9 %fusion.26 = f32[512,512]{1,0:T(8,128)} fusion(bf16[512,2048]{1,0:T(8,128)(2,1)S(1)} %pad_maximum_fusion.9, bf16[2048,512]{1,0:T(8,128)(2,1)} %collective-permute-done.13), kind=kOutput, calls=%fused_computation.80 | convolution fusion | flops 1073741824 | bytes 5242880 | tf_op jit(solution)/shard_map/dot_general | solution.py:22
  180.1 2.1 fusion.4
  182.2 4.4 %collective-permute-done.29 = bf16[512,512]{1,0:T(8,128)(2,1)S(1)} collective-permute-done((bf16[512,512]{1,0:T(8,128)(2,1)S(1)}, bf16[512,512]{1,0:T(8,128)(2,1)S(1)}, u32[]{:S(2)}, u32[]{:S(2)}) %collective-permute-start.29) | collective-permute-done | bytes 524320 | tf_op jit(solution)/shard_map/ppermute | solution.py:44
  186.5 2.1 fusion.8
  188.6 3.7 %add_convert_fusion = bf16[512,512]{1,0:T(8,128)(2,1)S(1)} fusion(f32[512,512]{1,0:T(8,128)} %collective-permute-done.24, bf16[512,2048]{1,0:T(8,128)(2,1)} %copy-done.5, bf16[512,512]{1,0:T(8,128)(2,1)} %copy-done.28, bf16[512,512]{1,0:T(8,128)(2,1)} %copy-done.30, bf16[512,512]{1,0:T(8,128)(2,1)} %copy-done.26, bf16[512,512]{1,0:T(8,128)(2,1)S(1)} %copy-done.25), kind=kOutput, calls=%fused_computation.43 | convolution fusion | flops 1082654720 | bytes 5767168 | tf_op jit(solution)/shard_map/dot_general | solution.py:22
  192.4 3.3 %add_convert_fusion.1 = bf16[512,512]{1,0:T(8,128)(2,1)} fusion(f32[512,512]{1,0:T(8,128)} %collective-permute-done.22, bf16[512,2048]{1,0:T(8,128)(2,1)S(1)} %copy-done.4, bf16[512,512]{1,0:T(8,128)(2,1)S(1)} %copy-done.29, bf16[512,512]{1,0:T(8,128)(2,1)S(1)} %copy-done.31, bf16[512,512]{1,0:T(8,128)(2,1)S(1)} %copy-done.27, ...), kind=kOutput, calls=%fused_computation.44 | convolution fusion | flops 1082654720 | bytes 5767168 | tf_op jit(solution)/shard_map/dot_general | solution.py:22
  195.7 3.6 %collective-permute-start.26 = (bf16[512,512]{1,0:T(8,128)(2,1)}, bf16[512,512]{1,0:T(8,128)(2,1)S(1)}, u32[]{:S(2)}, u32[]{:S(2)}) collective-permute-start(bf16[512,512]{1,0:T(8,128)(2,1)} %fusion.4), channel_id=1, source_target_pairs={{0,8},{8,16},{16,24},{24,0},{1,9},{9,17},{17,25},{25,1},{2,10},{10... | collective-permute-start | bytes 1572872 | tf_op jit(solution)/shard_map/ppermute | solution.py:44
  199.3 3.8 %fusion.23 = f32[512,512]{1,0:T(8,128)} fusion(bf16[512,2048]{1,0:T(8,128)(2,1)S(1)} %pad_maximum_fusion.2, bf16[2048,512]{1,0:T(8,128)(2,1)} %collective-permute-done.13), kind=kOutput, calls=%fused_computation.77 | convolution fusion | flops 1073741824 | bytes 5242880 | tf_op jit(solution)/shard_map/dot_general | solution.py:22
  203.7 17.8 %collective-permute-done.26 = bf16[512,512]{1,0:T(8,128)(2,1)S(1)} collective-permute-done((bf16[512,512]{1,0:T(8,128)(2,1)}, bf16[512,512]{1,0:T(8,128)(2,1)S(1)}, u32[]{:S(2)}, u32[]{:S(2)}) %collective-permute-start.26) | collective-permute-done | bytes 524320 | tf_op jit(solution)/shard_map/ppermute | solution.py:44
  222.4 2.4 collective-permute-start.27
  224.8 9.4 %collective-permute-done.27 = bf16[512,512]{1,0:T(8,128)(2,1)S(1)} collective-permute-done((bf16[512,512]{1,0:T(8,128)(2,1)}, bf16[512,512]{1,0:T(8,128)(2,1)S(1)}, u32[]{:S(2)}, u32[]{:S(2)}) %collective-permute-start.27) | collective-permute-done | bytes 524320 | tf_op jit(solution)/shard_map/ppermute | solution.py:44
  234.5 11.3 %fusion = bf16[1,512,4096]{2,1,0:T(8,128)(2,1)} fusion(f32[512,4096]{1,0:T(8,128)} %multiply_divide_fusion, bf16[512,4096]{1,0:T(8,128)(2,1)} %all-gather.2.cloned.1.call-done, f32[512,512]{1,0:T(8,128)} %collective-permute-done.14, bf16[512,2048]{1,0:T(8,128)(2,1)S(1)} %pad_maximum_fusion.2, bf16[512,512]{1,0:T(8,128)(2,1)} %collective-permute-done.23, ...), kind=kOutput, calls=%fused_computation.2 | convolution fusion | flops 3234856960 | bytes 23068674 | tf_op jit(solution)/shard_map/dot_general | solution.py:154
  (149 shorter events, 43.1 us)
Async XLA Ops:
  6.5 227.9 %all-gather.2.cloned.1.call-start = ((), (), s32[]{:S(2)}) async-start(), calls=%async_computation | async-start | bytes 4718592 | tf_op jit(solution)/shard_map/all_gather | solution.py:151
  8.4 31.9 %collective-permute-start.4 = (bf16[2048,512]{1,0:T(8,128)(2,1)S(1)}, bf16[2048,512]{1,0:T(8,128)(2,1)S(1)}, u32[]{:S(2)}, u32[]{:S(2)}) collective-permute-start(bf16[2048,512]{1,0:T(8,128)(2,1)S(1)} %pad_maximum_fusion), channel_id=1, source_target_pairs={{0,1},{1,0},{2,3},{3,2},{4,5},{5,4},{6,7},{7,6},{8,9},{9,8},{10,11... | collective-permute-start | bytes 6291464 | tf_op jit(solution)/shard_map/ppermute | solution.py:40
  9.5 25.0 %collective-permute-start = (bf16[1024,512]{1,0:T(8,128)(2,1)S(1)}, bf16[1024,512]{1,0:T(8,128)(2,1)S(1)}, u32[]{:S(2)}, u32[]{:S(2)}) collective-permute-start(bf16[1024,512]{1,0:T(8,128)(2,1)S(1)} %pad_maximum_fusion.24), channel_id=1, source_target_pairs={{0,2},{1,3},{2,0},{3,1},{4,6},{5,7},{6,4},{7,5},{8,10},{9,11},{10,... | collective-permute-start | bytes 3145736 | tf_op jit(solution)/shard_map/ppermute | solution.py:40
  11.0 24.6 %collective-permute-start.1 = (bf16[1024,512]{1,0:T(8,128)(2,1)S(1)}, bf16[1024,512]{1,0:T(8,128)(2,1)S(1)}, u32[]{:S(2)}, u32[]{:S(2)}) collective-permute-start(bf16[1024,512]{1,0:T(8,128)(2,1)S(1)} %pad_maximum_fusion.24), channel_id=1, source_target_pairs={{0,4},{1,5},{2,6},{3,7},{4,0},{5,1},{6,2},{7,3},{8,12},{9,13},{10,... | collective-permute-start | bytes 3145736 | tf_op jit(solution)/shard_map/ppermute | solution.py:40
  12.5 13.1 %collective-permute-start.2 = (bf16[512,512]{1,0:T(8,128)(2,1)S(1)}, bf16[512,512]{1,0:T(8,128)(2,1)S(1)}, u32[]{:S(2)}, u32[]{:S(2)}) collective-permute-start(bf16[512,512]{1,0:T(8,128)(2,1)S(1)} %bitcast.52), channel_id=1, source_target_pairs={{0,24},{8,0},{16,8},{24,16},{1,25},{9,1},{17,9},{25,17},{2,26},{10... | collective-permute-start | bytes 1572872 | tf_op jit(solution)/shard_map/ppermute | solution.py:44
  25.7 13.8 %collective-permute-start.3 = (bf16[512,512]{1,0:T(8,128)(2,1)S(1)}, bf16[512,512]{1,0:T(8,128)(2,1)S(1)}, u32[]{:S(2)}, u32[]{:S(2)}) collective-permute-start(bf16[512,512]{1,0:T(8,128)(2,1)S(1)} %collective-permute-done.2), channel_id=1, source_target_pairs={{0,24},{8,0},{16,8},{24,16},{1,25},{9,1},{17,9},{25,17},{2,26},{10... | collective-permute-start | bytes 1572872 | tf_op jit(solution)/shard_map/ppermute | solution.py:44
  40.3 34.0 %collective-permute-start.5 = (bf16[1536,512]{1,0:T(8,128)(2,1)S(1)}, bf16[1536,512]{1,0:T(8,128)(2,1)S(1)}, u32[]{:S(2)}, u32[]{:S(2)}) collective-permute-start(bf16[1536,512]{1,0:T(8,128)(2,1)S(1)} %get-tuple-element.44), channel_id=1, source_target_pairs={{0,2},{1,3},{2,0},{3,1},{4,6},{5,7},{6,4},{7,5},{8,10},{9,11},{10,... | collective-permute-start | bytes 4718600 | tf_op jit(solution)/shard_map/ppermute | solution.py:40
  40.8 33.7 %collective-permute-start.6 = (bf16[1536,512]{1,0:T(8,128)(2,1)S(1)}, bf16[1536,512]{1,0:T(8,128)(2,1)S(1)}, u32[]{:S(2)}, u32[]{:S(2)}) collective-permute-start(bf16[1536,512]{1,0:T(8,128)(2,1)S(1)} %get-tuple-element.45), channel_id=1, source_target_pairs={{0,4},{1,5},{2,6},{3,7},{4,0},{5,1},{6,2},{7,3},{8,12},{9,13},{10,... | collective-permute-start | bytes 4718600 | tf_op jit(solution)/shard_map/ppermute | solution.py:40
  41.6 16.4 %collective-permute-start.8 = (bf16[512,512]{1,0:T(8,128)(2,1)S(1)}, bf16[512,512]{1,0:T(8,128)(2,1)S(1)}, u32[]{:S(2)}, u32[]{:S(2)}) collective-permute-start(bf16[512,512]{1,0:T(8,128)(2,1)S(1)} %bitcast.56), channel_id=1, source_target_pairs={{0,24},{8,0},{16,8},{24,16},{1,25},{9,1},{17,9},{25,17},{2,26},{10... | collective-permute-start | bytes 1572872 | tf_op jit(solution)/shard_map/ppermute | solution.py:44
  47.1 29.7 %collective-permute-start.7 = (bf16[512,512]{1,0:T(8,128)(2,1)S(1)}, bf16[512,512]{1,0:T(8,128)(2,1)S(1)}, u32[]{:S(2)}, u32[]{:S(2)}) collective-permute-start(bf16[512,512]{1,0:T(8,128)(2,1)S(1)} %bitcast.53), channel_id=1, source_target_pairs={{0,8},{8,16},{16,24},{24,0},{1,9},{9,17},{17,25},{25,1},{2,10},{10... | collective-permute-start | bytes 1572872 | tf_op jit(solution)/shard_map/ppermute | solution.py:44
  58.0 19.2 %collective-permute-start.9 = (bf16[512,512]{1,0:T(8,128)(2,1)S(1)}, bf16[512,512]{1,0:T(8,128)(2,1)S(1)}, u32[]{:S(2)}, u32[]{:S(2)}) collective-permute-start(bf16[512,512]{1,0:T(8,128)(2,1)S(1)} %collective-permute-done.8), channel_id=1, source_target_pairs={{0,24},{8,0},{16,8},{24,16},{1,25},{9,1},{17,9},{25,17},{2,26},{10... | collective-permute-start | bytes 1572872 | tf_op jit(solution)/shard_map/ppermute | solution.py:44
  79.0 33.4 %collective-permute-start.10 = (bf16[1536,512]{1,0:T(8,128)(2,1)}, bf16[1536,512]{1,0:T(8,128)(2,1)}, u32[]{:S(2)}, u32[]{:S(2)}) collective-permute-start(bf16[1536,512]{1,0:T(8,128)(2,1)} %get-tuple-element.51), channel_id=1, source_target_pairs={{0,2},{1,3},{2,0},{3,1},{4,6},{5,7},{6,4},{7,5},{8,10},{9,11},{10,... | collective-permute-start | bytes 4718600 | tf_op jit(solution)/shard_map/ppermute | solution.py:40
  80.4 32.8 %collective-permute-start.11 = (bf16[1536,512]{1,0:T(8,128)(2,1)}, bf16[1536,512]{1,0:T(8,128)(2,1)}, u32[]{:S(2)}, u32[]{:S(2)}) collective-permute-start(bf16[1536,512]{1,0:T(8,128)(2,1)} %get-tuple-element.52), channel_id=1, source_target_pairs={{0,4},{1,5},{2,6},{3,7},{4,0},{5,1},{6,2},{7,3},{8,12},{9,13},{10,... | collective-permute-start | bytes 4718600 | tf_op jit(solution)/shard_map/ppermute | solution.py:40
  82.8 35.3 %collective-permute-start.13 = (bf16[2048,512]{1,0:T(8,128)(2,1)}, bf16[2048,512]{1,0:T(8,128)(2,1)}, u32[]{:S(2)}, u32[]{:S(2)}) collective-permute-start(bf16[2048,512]{1,0:T(8,128)(2,1)} %pad_maximum_fusion.3), channel_id=1, source_target_pairs={{0,1},{1,0},{2,3},{3,2},{4,5},{5,4},{6,7},{7,6},{8,9},{9,8},{10,11... | collective-permute-start | bytes 6291464 | tf_op jit(solution)/shard_map/ppermute | solution.py:40
  87.9 30.0 %collective-permute-start.12 = (bf16[512,512]{1,0:T(8,128)(2,1)S(1)}, bf16[512,512]{1,0:T(8,128)(2,1)S(1)}, u32[]{:S(2)}, u32[]{:S(2)}) collective-permute-start(bf16[512,512]{1,0:T(8,128)(2,1)S(1)} %bitcast.57), channel_id=1, source_target_pairs={{0,8},{8,16},{16,24},{24,0},{1,9},{9,17},{17,25},{25,1},{2,10},{10... | collective-permute-start | bytes 1572872 | tf_op jit(solution)/shard_map/ppermute | solution.py:44
  118.2 31.7 %collective-permute-start.15 = (bf16[1536,512]{1,0:T(8,128)(2,1)S(1)}, bf16[1536,512]{1,0:T(8,128)(2,1)S(1)}, u32[]{:S(2)}, u32[]{:S(2)}) collective-permute-start(bf16[1536,512]{1,0:T(8,128)(2,1)S(1)} %get-tuple-element.58), channel_id=1, source_target_pairs={{0,2},{1,3},{2,0},{3,1},{4,6},{5,7},{6,4},{7,5},{8,10},{9,11},{10,... | collective-permute-start | bytes 4718600 | tf_op jit(solution)/shard_map/ppermute | solution.py:40
  119.2 31.6 %collective-permute-start.16 = (bf16[1536,512]{1,0:T(8,128)(2,1)S(1)}, bf16[1536,512]{1,0:T(8,128)(2,1)S(1)}, u32[]{:S(2)}, u32[]{:S(2)}) collective-permute-start(bf16[1536,512]{1,0:T(8,128)(2,1)S(1)} %get-tuple-element.59), channel_id=1, source_target_pairs={{0,4},{1,5},{2,6},{3,7},{4,0},{5,1},{6,2},{7,3},{8,12},{9,13},{10,... | collective-permute-start | bytes 4718600 | tf_op jit(solution)/shard_map/ppermute | solution.py:40
  122.7 59.5 %collective-permute-start.28 = (f32[512,512]{1,0:T(8,128)S(1)}, f32[512,512]{1,0:T(8,128)S(1)}, u32[]{:S(2)}, u32[]{:S(2)}) collective-permute-start(f32[512,512]{1,0:T(8,128)S(1)} %fusion.29), channel_id=1, source_target_pairs={{0,1},{1,0},{2,3},{3,2},{4,5},{5,4},{6,7},{7,6},{8,9},{9,8},{10,11... | collective-permute-start | bytes 3145736 | tf_op jit(solution)/shard_map/ppermute | solution.py:40
  124.5 32.2 %collective-permute-start.30 = (f32[512,512]{1,0:T(8,128)S(1)}, f32[512,512]{1,0:T(8,128)S(1)}, u32[]{:S(2)}, u32[]{:S(2)}) collective-permute-start(f32[512,512]{1,0:T(8,128)S(1)} %fusion.30), channel_id=1, source_target_pairs={{0,1},{1,0},{2,3},{3,2},{4,5},{5,4},{6,7},{7,6},{8,9},{9,8},{10,11... | collective-permute-start | bytes 3145736 | tf_op jit(solution)/shard_map/ppermute | solution.py:40
  125.8 27.4 %collective-permute-start.18 = (bf16[512,512]{1,0:T(8,128)(2,1)S(1)}, bf16[512,512]{1,0:T(8,128)(2,1)S(1)}, u32[]{:S(2)}, u32[]{:S(2)}) collective-permute-start(bf16[512,512]{1,0:T(8,128)(2,1)S(1)} %fusion.2), channel_id=1, source_target_pairs={{0,8},{8,16},{16,24},{24,0},{1,9},{9,17},{17,25},{25,1},{2,10},{10... | collective-permute-start | bytes 1572872 | tf_op jit(solution)/shard_map/ppermute | solution.py:44
  154.5 15.6 %collective-permute-start.21 = (f32[512,512]{1,0:T(8,128)S(1)}, f32[512,512]{1,0:T(8,128)S(1)}, u32[]{:S(2)}, u32[]{:S(2)}) collective-permute-start(f32[512,512]{1,0:T(8,128)S(1)} %fusion.25), channel_id=1, source_target_pairs={{0,1},{1,0},{2,3},{3,2},{4,5},{5,4},{6,7},{7,6},{8,9},{9,8},{10,11... | collective-permute-start | bytes 3145736 | tf_op jit(solution)/shard_map/ppermute | solution.py:40
  154.6 14.3 %collective-permute-start.19 = (bf16[512,512]{1,0:T(8,128)(2,1)S(1)}, bf16[512,512]{1,0:T(8,128)(2,1)S(1)}, u32[]{:S(2)}, u32[]{:S(2)}) collective-permute-start(bf16[512,512]{1,0:T(8,128)(2,1)S(1)} %get-tuple-element.63), channel_id=1, source_target_pairs={{0,2},{1,3},{2,0},{3,1},{4,6},{5,7},{6,4},{7,5},{8,10},{9,11},{10,... | collective-permute-start | bytes 1572872 | tf_op jit(solution)/shard_map/ppermute | solution.py:40
  155.5 14.0 %collective-permute-start.20 = (bf16[512,512]{1,0:T(8,128)(2,1)S(1)}, bf16[512,512]{1,0:T(8,128)(2,1)S(1)}, u32[]{:S(2)}, u32[]{:S(2)}) collective-permute-start(bf16[512,512]{1,0:T(8,128)(2,1)S(1)} %get-tuple-element.64), channel_id=1, source_target_pairs={{0,4},{1,5},{2,6},{3,7},{4,0},{5,1},{6,2},{7,3},{8,12},{9,13},{10,... | collective-permute-start | bytes 1572872 | tf_op jit(solution)/shard_map/ppermute | solution.py:40
  158.0 24.2 %collective-permute-start.31 = (bf16[512,512]{1,0:T(8,128)(2,1)S(1)}, bf16[512,512]{1,0:T(8,128)(2,1)S(1)}, u32[]{:S(2)}, u32[]{:S(2)}) collective-permute-start(bf16[512,512]{1,0:T(8,128)(2,1)S(1)} %fusion.7), channel_id=1, source_target_pairs={{0,8},{8,16},{16,24},{24,0},{1,9},{9,17},{17,25},{25,1},{2,10},{10... | collective-permute-start | bytes 1572872 | tf_op jit(solution)/shard_map/ppermute | solution.py:44
  168.9 10.6 %collective-permute-start.25 = (f32[512,512]{1,0:T(8,128)S(1)}, f32[512,512]{1,0:T(8,128)S(1)}, u32[]{:S(2)}, u32[]{:S(2)}) collective-permute-start(f32[512,512]{1,0:T(8,128)S(1)} %fusion.28), channel_id=1, source_target_pairs={{0,1},{1,0},{2,3},{3,2},{4,5},{5,4},{6,7},{7,6},{8,9},{9,8},{10,11... | collective-permute-start | bytes 3145736 | tf_op jit(solution)/shard_map/ppermute | solution.py:40
  171.4 15.2 %collective-permute-start.29 = (bf16[512,512]{1,0:T(8,128)(2,1)S(1)}, bf16[512,512]{1,0:T(8,128)(2,1)S(1)}, u32[]{:S(2)}, u32[]{:S(2)}) collective-permute-start(bf16[512,512]{1,0:T(8,128)(2,1)S(1)} %fusion.3), channel_id=1, source_target_pairs={{0,24},{8,0},{16,8},{24,16},{1,25},{9,1},{17,9},{25,17},{2,26},{10... | collective-permute-start | bytes 1572872 | tf_op jit(solution)/shard_map/ppermute | solution.py:44
  175.7 12.9 %collective-permute-start.24 = (f32[512,512]{1,0:T(8,128)}, f32[512,512]{1,0:T(8,128)}, u32[]{:S(2)}, u32[]{:S(2)}) collective-permute-start(f32[512,512]{1,0:T(8,128)} %fusion.27), channel_id=1, source_target_pairs={{0,1},{1,0},{2,3},{3,2},{4,5},{5,4},{6,7},{7,6},{8,9},{9,8},{10,11... | collective-permute-start | bytes 3145736 | tf_op jit(solution)/shard_map/ppermute | solution.py:40
  179.6 12.8 %collective-permute-start.22 = (f32[512,512]{1,0:T(8,128)}, f32[512,512]{1,0:T(8,128)}, u32[]{:S(2)}, u32[]{:S(2)}) collective-permute-start(f32[512,512]{1,0:T(8,128)} %fusion.26), channel_id=1, source_target_pairs={{0,1},{1,0},{2,3},{3,2},{4,5},{5,4},{6,7},{7,6},{8,9},{9,8},{10,11... | collective-permute-start | bytes 3145736 | tf_op jit(solution)/shard_map/ppermute | solution.py:40
  195.7 25.9 %collective-permute-start.26 = (bf16[512,512]{1,0:T(8,128)(2,1)}, bf16[512,512]{1,0:T(8,128)(2,1)S(1)}, u32[]{:S(2)}, u32[]{:S(2)}) collective-permute-start(bf16[512,512]{1,0:T(8,128)(2,1)} %fusion.4), channel_id=1, source_target_pairs={{0,8},{8,16},{16,24},{24,0},{1,9},{9,17},{17,25},{25,1},{2,10},{10... | collective-permute-start | bytes 1572872 | tf_op jit(solution)/shard_map/ppermute | solution.py:44
  203.1 21.7 %collective-permute-start.14 = (f32[512,512]{1,0:T(8,128)}, f32[512,512]{1,0:T(8,128)}, u32[]{:S(2)}, u32[]{:S(2)}) collective-permute-start(f32[512,512]{1,0:T(8,128)} %fusion.23), channel_id=1, source_target_pairs={{0,1},{1,0},{2,3},{3,2},{4,5},{5,4},{6,7},{7,6},{8,9},{9,8},{10,11... | collective-permute-start | bytes 3145736 | tf_op jit(solution)/shard_map/ppermute | solution.py:40
  203.7 21.1 %collective-permute-start.23 = (bf16[512,512]{1,0:T(8,128)(2,1)}, bf16[512,512]{1,0:T(8,128)(2,1)}, u32[]{:S(2)}, u32[]{:S(2)}) collective-permute-start(bf16[512,512]{1,0:T(8,128)(2,1)} %add_convert_fusion.1), channel_id=1, source_target_pairs={{0,24},{8,0},{16,8},{24,16},{1,25},{9,1},{17,9},{25,17},{2,26},{10... | collective-permute-start | bytes 1572872 | tf_op jit(solution)/shard_map/ppermute | solution.py:44
  222.4 11.8 %collective-permute-start.27 = (bf16[512,512]{1,0:T(8,128)(2,1)}, bf16[512,512]{1,0:T(8,128)(2,1)S(1)}, u32[]{:S(2)}, u32[]{:S(2)}) collective-permute-start(bf16[512,512]{1,0:T(8,128)(2,1)} %broadcast_select_fusion), channel_id=1, source_target_pairs={{0,8},{8,16},{16,24},{24,0},{1,9},{9,17},{17,25},{25,1},{2,10},{10... | collective-permute-start | bytes 1572872 | tf_op jit(solution)/shard_map/ppermute | solution.py:44
  (36 other events, 465.9 us)
Sparse Core Ops, SparseCore 0:
  195.8 38.5 all-gather.1

commit v19 on v18

--- a/solution.py
+++ b/solution.py
@@ -70,7 +70,7 @@
     theirs = [rows_for_other(0, []), None]
 
     pieces = {(0, 0): own[0], (1, 0): own[1]}
-    rotated = {}
+    rotated, halves = {}, {}
 
     def fetch(side, i, gate):
         block, by = {1: (own[side], -1), 2: (pieces.get((side, 1)), -1), 3: (own[side], 1)}[i]
@@ -78,9 +78,10 @@
         return pieces[side, i]
 
     def rotate(group, evens):
-        crossing = [swap(dot(even, theirs[side]), CORE) for (side, _), even in zip(group, evens)]
-        for (side, i), even, other in zip(group, evens, crossing):
-            rotated[side, i] = (dot(even, ours[side]) + other).astype(jnp.bfloat16)
+        for (side, i), even in zip(group, evens):
+            halves[side, i] = dot(even, theirs[side])
+        for (side, i), even in zip(group, evens):
+            rotated[side, i] = (dot(even, ours[side]) + swap(halves[side, i], CORE)).astype(jnp.bfloat16)
         return [rotated[key] for key in group]
 
     def pass_on(side):
@@ -128,8 +129,6 @@
 
     gate, due = due, slot(1, due)
     due += [fetch(0, 3, gate), fetch(1, 1, gate), fetch(1, 2, gate)]
-    inverse = after(1 / (tokens * (eig_lambda.astype(jnp.float32) + damping)), [])
-    due.append(inverse)
 
     gate, due = due, slot(2, due)
     theirs[1] = rows_for_other(1, gate)
@@ -143,16 +142,15 @@
 
     gate, due = due, slot(4, due)
     in_from_behind = send_ahead(0, passed_in, gate)
-    ready = rotate(groups[2], after(evens[2], gate))
+    rotate(groups[2], after(evens[2], gate))
     in_from_ahead = send_behind(0)
     passed_out = pass_on(1)
-    ready += rotate(groups[3], after(evens[3], rotated[0, 3]))
-    rot_in = after(keep(0, in_from_behind, in_from_ahead), ready)
+    rotate(groups[3], after(evens[3], rotated[0, 3]))
+    begun = [rotated[1, 2], halves[1, 1], halves[1, 3]]
+    rot_in = after(keep(0, in_from_behind, in_from_ahead), begun)
     all_rot_in = lax.all_gather(rot_in, "tensor", axis=1, tiled=True)
     rot_out = keep(1, send_ahead(1, passed_out, []), send_behind(1))
-    contract = (((0,), (0,)), ((), ()))
-    product = lax.dot_general(rot_out, all_rot_in, contract, preferred_element_type=jnp.float32)
-    return (product * inverse).astype(jnp.bfloat16)[None]
+    return product_and_divide(rot_out, all_rot_in, eig_lambda, tokens)
 
 
 def solution(mesh):

time: 257 us -> 256 us (level)
  waiting for transfers between devices: 131 us -> 138 us
  other arithmetic: 11.7 us -> 6.71 us
  matrix products: 45.5 us -> 41.9 us
    ppermute x12, waiting for transfers between devices: 54.6 us -> 62.6 us  [shift(): return lax.ppermute(block, 'dp', [(z, (z + by) % n) for z in range(n)])]
    div x1 -> x0, other arithmetic: 4.51 us -> none  [move_inputs(): 1 / (tokens * (eig_lambda.astype(jnp.float32) + damping))]
    dot_general x15, matrix products: 34.2 us -> 31.2 us  [dot(): return jnp.dot(a, b, preferred_element_type=jnp.float32)]
  transfers between devices with their start and end apart: 33 -> 33, of which waited for: 18 -> 16; matrix products, arithmetic and copies ran while one was open for 20% -> 17% of each run, Pallas kernels for 0% -> 0%
where the time goes in v19:
time: 256 us; the launch traced here: 251 us
  waiting for transfers between devices  138 us (54%)
  matrix products  41.9 us (16%)
  starting transfers between devices  32.3 us (13%)
  local copies, waits for them, and re-layouts  17.1 us (7%)
  between operations  15.3 us (6%)
  other arithmetic  6.71 us (3%)
    ppermute x20, waiting for transfers between devices, swap(): lax.ppermute(block, 'tensor', [(j, j ^ bit) for j in range(X + Y + CORE +...  75.1 us
    ppermute x12, waiting for transfers between devices, shift(): return lax.ppermute(block, 'dp', [(z, (z + by) % n) for z in range(n)])  62.6 us
    dot_general x15, matrix products, dot(): return jnp.dot(a, b, preferred_element_type=jnp.float32)  31.2 us
    ppermute x12, starting transfers between devices, shift(): return lax.ppermute(block, 'dp', [(z, (z + by) % n) for z in range(n)])  21.1 us
    ppermute x20, starting transfers between devices, swap(): lax.ppermute(block, 'tensor', [(j, j ^ bit) for j in range(X + Y + CORE +...  11.2 us
    dot_general x1, matrix products, product_and_divide(): lax.dot_general(rot_out, all_rot_in, contract, preferred_element_type=jnp...  10.7 us
    unnamed x70, local copies, waits for them, and re-layouts  6.22 us
  transfers between devices with their start and end apart: 33, of which 16 were waited for; matrix products, arithmetic and copies ran while one was open for 17% of the time, Pallas kernels for 0%

profile of v19, /device:TPU:16, one launch (start us, length us, event | category | flops | bytes accessed | tf_op | source)
XLA Modules:
  0.0 251.1 jit_solution(10844352945065636236)
XLA Ops:
  6.5 1.7 constant_dynamic-slice_fusion.8
  9.5 1.6 collective-permute-start
  11.0 1.5 collective-permute-start.1
  13.0 12.7 %collective-permute-done.2 = bf16[512,512]{1,0:T(8,128)(2,1)S(1)} collective-permute-done((bf16[512,512]{1,0:T(8,128)(2,1)S(1)}, bf16[512,512]{1,0:T(8,128)(2,1)S(1)}, u32[]{:S(2)}, u32[]{:S(2)}) %collective-permute-start.2) | collective-permute-done | bytes 524320 | tf_op jit(solution)/shard_map/ppermute | solution.py:44
  26.1 8.3 %collective-permute-done = bf16[1024,512]{1,0:T(8,128)(2,1)S(1)} collective-permute-done((bf16[1024,512]{1,0:T(8,128)(2,1)S(1)}, bf16[1024,512]{1,0:T(8,128)(2,1)S(1)}, u32[]{:S(2)}, u32[]{:S(2)}) %collective-permute-start) | collective-permute-done | bytes 1048608 | tf_op jit(solution)/shard_map/ppermute | solution.py:40
  36.8 2.7 %collective-permute-done.3 = bf16[512,512]{1,0:T(8,128)(2,1)S(1)} collective-permute-done((bf16[512,512]{1,0:T(8,128)(2,1)S(1)}, bf16[512,512]{1,0:T(8,128)(2,1)S(1)}, u32[]{:S(2)}, u32[]{:S(2)}) %collective-permute-start.3) | collective-permute-done | bytes 524320 | tf_op jit(solution)/shard_map/ppermute | solution.py:44
  41.3 3.5 %collective-permute-start.7 = (bf16[512,512]{1,0:T(8,128)(2,1)S(1)}, bf16[512,512]{1,0:T(8,128)(2,1)S(1)}, u32[]{:S(2)}, u32[]{:S(2)}) collective-permute-start(bf16[512,512]{1,0:T(8,128)(2,1)S(1)} %bitcast.53), channel_id=1, source_target_pairs={{0,8},{8,16},{16,24},{24,0},{1,9},{9,17},{17,25},{25,1},{2,10},{10... | collective-permute-start | bytes 1572872 | tf_op jit(solution)/shard_map/ppermute | solution.py:44
  44.9 12.8 %collective-permute-done.8 = bf16[512,512]{1,0:T(8,128)(2,1)S(1)} collective-permute-done((bf16[512,512]{1,0:T(8,128)(2,1)S(1)}, bf16[512,512]{1,0:T(8,128)(2,1)S(1)}, u32[]{:S(2)}, u32[]{:S(2)}) %collective-permute-start.8) | collective-permute-done | bytes 524320 | tf_op jit(solution)/shard_map/ppermute | solution.py:44
  57.7 16.6 %collective-permute-done.5 = bf16[1536,512]{1,0:T(8,128)(2,1)S(1)} collective-permute-done((bf16[1536,512]{1,0:T(8,128)(2,1)S(1)}, bf16[1536,512]{1,0:T(8,128)(2,1)S(1)}, u32[]{:S(2)}, u32[]{:S(2)}) %collective-permute-start.5) | collective-permute-done | bytes 1572896 | tf_op jit(solution)/shard_map/ppermute | solution.py:40
  76.8 2.0 pad_maximum_fusion.16
  78.9 1.5 collective-permute-start.10
  84.3 1.8 dynamic-slice_bitcast_fusion.3
  88.2 3.6 %collective-permute-start.12 = (bf16[512,512]{1,0:T(8,128)(2,1)S(1)}, bf16[512,512]{1,0:T(8,128)(2,1)S(1)}, u32[]{:S(2)}, u32[]{:S(2)}) collective-permute-start(bf16[512,512]{1,0:T(8,128)(2,1)S(1)} %bitcast.57), channel_id=1, source_target_pairs={{0,8},{8,16},{16,24},{24,0},{1,9},{9,17},{17,25},{25,1},{2,10},{10... | collective-permute-start | bytes 1572872 | tf_op jit(solution)/shard_map/ppermute | solution.py:44
  92.1 20.0 %collective-permute-done.10 = bf16[1536,512]{1,0:T(8,128)(2,1)} collective-permute-done((bf16[1536,512]{1,0:T(8,128)(2,1)}, bf16[1536,512]{1,0:T(8,128)(2,1)}, u32[]{:S(2)}, u32[]{:S(2)}) %collective-permute-start.10) | collective-permute-done | bytes 1572896 | tf_op jit(solution)/shard_map/ppermute | solution.py:40
  114.7 1.5 fusion.21
  125.4 3.3 %collective-permute-start.18 = (bf16[512,512]{1,0:T(8,128)(2,1)S(1)}, bf16[512,512]{1,0:T(8,128)(2,1)S(1)}, u32[]{:S(2)}, u32[]{:S(2)}) collective-permute-start(bf16[512,512]{1,0:T(8,128)(2,1)S(1)} %fusion.2), channel_id=1, source_target_pairs={{0,8},{8,16},{16,24},{24,0},{1,9},{9,17},{17,25},{25,1},{2,10},{10... | collective-permute-start | bytes 1572872 | tf_op jit(solution)/shard_map/ppermute | solution.py:44
  128.7 21.0 %collective-permute-done.15 = bf16[1536,512]{1,0:T(8,128)(2,1)S(1)} collective-permute-done((bf16[1536,512]{1,0:T(8,128)(2,1)S(1)}, bf16[1536,512]{1,0:T(8,128)(2,1)S(1)}, u32[]{:S(2)}, u32[]{:S(2)}) %collective-permute-start.15) | collective-permute-done | bytes 1572896 | tf_op jit(solution)/shard_map/ppermute | solution.py:40
  153.8 1.5 collective-permute-start.19
  156.9 3.3 %collective-permute-start.31 = (bf16[512,512]{1,0:T(8,128)(2,1)S(1)}, bf16[512,512]{1,0:T(8,128)(2,1)S(1)}, u32[]{:S(2)}, u32[]{:S(2)}) collective-permute-start(bf16[512,512]{1,0:T(8,128)(2,1)S(1)} %fusion.7), channel_id=1, source_target_pairs={{0,8},{8,16},{16,24},{24,0},{1,9},{9,17},{17,25},{25,1},{2,10},{10... | collective-permute-start | bytes 1572872 | tf_op jit(solution)/shard_map/ppermute | solution.py:44
  160.2 2.8 %fusion.29 = f32[512,512]{1,0:T(8,128)S(1)} fusion(bf16[512,2048]{1,0:T(8,128)(2,1)S(1)} %pad_maximum_fusion.11, bf16[2048,512]{1,0:T(8,128)(2,1)} %collective-permute-done.13), kind=kOutput, calls=%fused_computation.81 | convolution fusion | flops 1073741824 | bytes 5242880 | tf_op jit(solution)/shard_map/dot_general | solution.py:22
  163.1 5.1 %collective-permute-done.19 = bf16[512,512]{1,0:T(8,128)(2,1)S(1)} collective-permute-done((bf16[512,512]{1,0:T(8,128)(2,1)S(1)}, bf16[512,512]{1,0:T(8,128)(2,1)S(1)}, u32[]{:S(2)}, u32[]{:S(2)}) %collective-permute-start.19) | collective-permute-done | bytes 524320 | tf_op jit(solution)/shard_map/ppermute | solution.py:40
  171.6 3.8 %fusion.28 = f32[512,512]{1,0:T(8,128)} fusion(bf16[512,2048]{1,0:T(8,128)(2,1)S(1)} %pad_maximum_fusion.8, bf16[2048,512]{1,0:T(8,128)(2,1)} %collective-permute-done.13), kind=kOutput, calls=%fused_computation.80 | convolution fusion | flops 1073741824 | bytes 5242880 | tf_op jit(solution)/shard_map/dot_general | solution.py:22
  175.4 3.8 %fusion.27 = f32[512,512]{1,0:T(8,128)} fusion(bf16[512,2048]{1,0:T(8,128)(2,1)S(1)} %pad_maximum_fusion.9, bf16[2048,512]{1,0:T(8,128)(2,1)} %collective-permute-done.13), kind=kOutput, calls=%fused_computation.79 | convolution fusion | flops 1073741824 | bytes 5242880 | tf_op jit(solution)/shard_map/dot_general | solution.py:22
  180.6 4.8 %collective-permute-done.29 = bf16[512,512]{1,0:T(8,128)(2,1)S(1)} collective-permute-done((bf16[512,512]{1,0:T(8,128)(2,1)S(1)}, bf16[512,512]{1,0:T(8,128)(2,1)S(1)}, u32[]{:S(2)}, u32[]{:S(2)}) %collective-permute-start.29) | collective-permute-done | bytes 524320 | tf_op jit(solution)/shard_map/ppermute | solution.py:44
  185.4 2.0 fusion.8
  188.8 4.1 %fusion.24 = f32[512,512]{1,0:T(8,128)} fusion(bf16[512,2048]{1,0:T(8,128)(2,1)S(1)} %pad_maximum_fusion.2, bf16[2048,512]{1,0:T(8,128)(2,1)} %collective-permute-done.13), kind=kOutput, calls=%fused_computation.76 | convolution fusion | flops 1073741824 | bytes 5242880 | tf_op jit(solution)/shard_map/dot_general | solution.py:22
  193.0 3.5 %collective-permute-start.26 = (bf16[512,512]{1,0:T(8,128)(2,1)S(1)}, bf16[512,512]{1,0:T(8,128)(2,1)S(1)}, u32[]{:S(2)}, u32[]{:S(2)}) collective-permute-start(bf16[512,512]{1,0:T(8,128)(2,1)S(1)} %fusion.4), channel_id=1, source_target_pairs={{0,8},{8,16},{16,24},{24,0},{1,9},{9,17},{17,25},{25,1},{2,10},{10... | collective-permute-start | bytes 1572872 | tf_op jit(solution)/shard_map/ppermute | solution.py:44
  197.8 3.3 %add_convert_fusion.1 = bf16[512,512]{1,0:T(8,128)(2,1)} fusion(f32[512,512]{1,0:T(8,128)} %collective-permute-done.22, bf16[512,2048]{1,0:T(8,128)(2,1)S(1)} %copy-done.5, bf16[512,512]{1,0:T(8,128)(2,1)S(1)} %copy-done.29, bf16[512,512]{1,0:T(8,128)(2,1)S(1)} %copy-done.31, bf16[512,512]{1,0:T(8,128)(2,1)S(1)} %copy-done.27, ...), kind=kOutput, calls=%fused_computation.43 | convolution fusion | flops 1082654720 | bytes 5767168 | tf_op jit(solution)/shard_map/dot_general | solution.py:22
  201.1 18.5 %collective-permute-done.26 = bf16[512,512]{1,0:T(8,128)(2,1)S(1)} collective-permute-done((bf16[512,512]{1,0:T(8,128)(2,1)S(1)}, bf16[512,512]{1,0:T(8,128)(2,1)S(1)}, u32[]{:S(2)}, u32[]{:S(2)}) %collective-permute-start.26) | collective-permute-done | bytes 524320 | tf_op jit(solution)/shard_map/ppermute | solution.py:44
  219.9 2.5 %collective-permute-start.27 = (bf16[512,512]{1,0:T(8,128)(2,1)S(1)}, bf16[512,512]{1,0:T(8,128)(2,1)}, u32[]{:S(2)}, u32[]{:S(2)}) collective-permute-start(bf16[512,512]{1,0:T(8,128)(2,1)S(1)} %fusion.10), channel_id=1, source_target_pairs={{0,8},{8,16},{16,24},{24,0},{1,9},{9,17},{17,25},{25,1},{2,10},{10... | collective-permute-start | bytes 1572872 | tf_op jit(solution)/shard_map/ppermute | solution.py:44
  222.4 11.2 %collective-permute-done.27 = bf16[512,512]{1,0:T(8,128)(2,1)} collective-permute-done((bf16[512,512]{1,0:T(8,128)(2,1)S(1)}, bf16[512,512]{1,0:T(8,128)(2,1)}, u32[]{:S(2)}, u32[]{:S(2)}) %collective-permute-start.27) | collective-permute-done | bytes 524320 | tf_op jit(solution)/shard_map/ppermute | solution.py:44
  233.6 10.7 %fusion = bf16[1,512,4096]{2,1,0:T(8,128)(2,1)} fusion(bf16[512,4096]{1,0:T(8,128)(2,1)} %param.11, bf16[512,4096]{1,0:T(8,128)(2,1)} %all-gather.2.cloned.1.call-done, f32[512,512]{1,0:T(8,128)} %collective-permute-done.14, bf16[512,2048]{1,0:T(8,128)(2,1)S(1)} %pad_maximum_fusion.2, bf16[512,512]{1,0:T(8,128)(2,1)} %collective-permute-done.23, ...), kind=kOutput, calls=%fused_computation.1 | convolution fusion | flops 3241148416 | bytes 18874370 | tf_op jit(solution)/shard_map/dot_general | solution.py:13
  (148 shorter events, 38.7 us)
Async XLA Ops:
  6.5 227.1 %all-gather.2.cloned.1.call-start = ((), (), s32[]{:S(2)}) async-start(), calls=%async_computation | async-start | bytes 4718592 | tf_op jit(solution)/shard_map/all_gather | solution.py:151
  8.4 31.9 %collective-permute-start.4 = (bf16[2048,512]{1,0:T(8,128)(2,1)S(1)}, bf16[2048,512]{1,0:T(8,128)(2,1)S(1)}, u32[]{:S(2)}, u32[]{:S(2)}) collective-permute-start(bf16[2048,512]{1,0:T(8,128)(2,1)S(1)} %pad_maximum_fusion), channel_id=1, source_target_pairs={{0,1},{1,0},{2,3},{3,2},{4,5},{5,4},{6,7},{7,6},{8,9},{9,8},{10,11... | collective-permute-start | bytes 6291464 | tf_op jit(solution)/shard_map/ppermute | solution.py:40
  9.5 25.0 %collective-permute-start = (bf16[1024,512]{1,0:T(8,128)(2,1)S(1)}, bf16[1024,512]{1,0:T(8,128)(2,1)S(1)}, u32[]{:S(2)}, u32[]{:S(2)}) collective-permute-start(bf16[1024,512]{1,0:T(8,128)(2,1)S(1)} %pad_maximum_fusion.24), channel_id=1, source_target_pairs={{0,2},{1,3},{2,0},{3,1},{4,6},{5,7},{6,4},{7,5},{8,10},{9,11},{10,... | collective-permute-start | bytes 3145736 | tf_op jit(solution)/shard_map/ppermute | solution.py:40
  11.0 24.6 %collective-permute-start.1 = (bf16[1024,512]{1,0:T(8,128)(2,1)S(1)}, bf16[1024,512]{1,0:T(8,128)(2,1)S(1)}, u32[]{:S(2)}, u32[]{:S(2)}) collective-permute-start(bf16[1024,512]{1,0:T(8,128)(2,1)S(1)} %pad_maximum_fusion.24), channel_id=1, source_target_pairs={{0,4},{1,5},{2,6},{3,7},{4,0},{5,1},{6,2},{7,3},{8,12},{9,13},{10,... | collective-permute-start | bytes 3145736 | tf_op jit(solution)/shard_map/ppermute | solution.py:40
  12.5 13.1 %collective-permute-start.2 = (bf16[512,512]{1,0:T(8,128)(2,1)S(1)}, bf16[512,512]{1,0:T(8,128)(2,1)S(1)}, u32[]{:S(2)}, u32[]{:S(2)}) collective-permute-start(bf16[512,512]{1,0:T(8,128)(2,1)S(1)} %bitcast.52), channel_id=1, source_target_pairs={{0,24},{8,0},{16,8},{24,16},{1,25},{9,1},{17,9},{25,17},{2,26},{10... | collective-permute-start | bytes 1572872 | tf_op jit(solution)/shard_map/ppermute | solution.py:44
  25.6 13.8 %collective-permute-start.3 = (bf16[512,512]{1,0:T(8,128)(2,1)S(1)}, bf16[512,512]{1,0:T(8,128)(2,1)S(1)}, u32[]{:S(2)}, u32[]{:S(2)}) collective-permute-start(bf16[512,512]{1,0:T(8,128)(2,1)S(1)} %collective-permute-done.2), channel_id=1, source_target_pairs={{0,24},{8,0},{16,8},{24,16},{1,25},{9,1},{17,9},{25,17},{2,26},{10... | collective-permute-start | bytes 1572872 | tf_op jit(solution)/shard_map/ppermute | solution.py:44
  40.3 34.0 %collective-permute-start.5 = (bf16[1536,512]{1,0:T(8,128)(2,1)S(1)}, bf16[1536,512]{1,0:T(8,128)(2,1)S(1)}, u32[]{:S(2)}, u32[]{:S(2)}) collective-permute-start(bf16[1536,512]{1,0:T(8,128)(2,1)S(1)} %get-tuple-element.44), channel_id=1, source_target_pairs={{0,2},{1,3},{2,0},{3,1},{4,6},{5,7},{6,4},{7,5},{8,10},{9,11},{10,... | collective-permute-start | bytes 4718600 | tf_op jit(solution)/shard_map/ppermute | solution.py:40
  40.8 33.7 %collective-permute-start.6 = (bf16[1536,512]{1,0:T(8,128)(2,1)S(1)}, bf16[1536,512]{1,0:T(8,128)(2,1)S(1)}, u32[]{:S(2)}, u32[]{:S(2)}) collective-permute-start(bf16[1536,512]{1,0:T(8,128)(2,1)S(1)} %get-tuple-element.45), channel_id=1, source_target_pairs={{0,4},{1,5},{2,6},{3,7},{4,0},{5,1},{6,2},{7,3},{8,12},{9,13},{10,... | collective-permute-start | bytes 4718600 | tf_op jit(solution)/shard_map/ppermute | solution.py:40
  41.3 16.4 %collective-permute-start.8 = (bf16[512,512]{1,0:T(8,128)(2,1)S(1)}, bf16[512,512]{1,0:T(8,128)(2,1)S(1)}, u32[]{:S(2)}, u32[]{:S(2)}) collective-permute-start(bf16[512,512]{1,0:T(8,128)(2,1)S(1)} %bitcast.56), channel_id=1, source_target_pairs={{0,24},{8,0},{16,8},{24,16},{1,25},{9,1},{17,9},{25,17},{2,26},{10... | collective-permute-start | bytes 1572872 | tf_op jit(solution)/shard_map/ppermute | solution.py:44
  41.3 35.4 %collective-permute-start.7 = (bf16[512,512]{1,0:T(8,128)(2,1)S(1)}, bf16[512,512]{1,0:T(8,128)(2,1)S(1)}, u32[]{:S(2)}, u32[]{:S(2)}) collective-permute-start(bf16[512,512]{1,0:T(8,128)(2,1)S(1)} %bitcast.53), channel_id=1, source_target_pairs={{0,8},{8,16},{16,24},{24,0},{1,9},{9,17},{17,25},{25,1},{2,10},{10... | collective-permute-start | bytes 1572872 | tf_op jit(solution)/shard_map/ppermute | solution.py:44
  57.7 19.0 %collective-permute-start.9 = (bf16[512,512]{1,0:T(8,128)(2,1)S(1)}, bf16[512,512]{1,0:T(8,128)(2,1)S(1)}, u32[]{:S(2)}, u32[]{:S(2)}) collective-permute-start(bf16[512,512]{1,0:T(8,128)(2,1)S(1)} %collective-permute-done.8), channel_id=1, source_target_pairs={{0,24},{8,0},{16,8},{24,16},{1,25},{9,1},{17,9},{25,17},{2,26},{10... | collective-permute-start | bytes 1572872 | tf_op jit(solution)/shard_map/ppermute | solution.py:44
  78.9 33.1 %collective-permute-start.10 = (bf16[1536,512]{1,0:T(8,128)(2,1)}, bf16[1536,512]{1,0:T(8,128)(2,1)}, u32[]{:S(2)}, u32[]{:S(2)}) collective-permute-start(bf16[1536,512]{1,0:T(8,128)(2,1)} %get-tuple-element.51), channel_id=1, source_target_pairs={{0,2},{1,3},{2,0},{3,1},{4,6},{5,7},{6,4},{7,5},{8,10},{9,11},{10,... | collective-permute-start | bytes 4718600 | tf_op jit(solution)/shard_map/ppermute | solution.py:40
  80.4 32.8 %collective-permute-start.11 = (bf16[1536,512]{1,0:T(8,128)(2,1)}, bf16[1536,512]{1,0:T(8,128)(2,1)}, u32[]{:S(2)}, u32[]{:S(2)}) collective-permute-start(bf16[1536,512]{1,0:T(8,128)(2,1)} %get-tuple-element.52), channel_id=1, source_target_pairs={{0,4},{1,5},{2,6},{3,7},{4,0},{5,1},{6,2},{7,3},{8,12},{9,13},{10,... | collective-permute-start | bytes 4718600 | tf_op jit(solution)/shard_map/ppermute | solution.py:40
  83.0 35.0 %collective-permute-start.13 = (bf16[2048,512]{1,0:T(8,128)(2,1)}, bf16[2048,512]{1,0:T(8,128)(2,1)}, u32[]{:S(2)}, u32[]{:S(2)}) collective-permute-start(bf16[2048,512]{1,0:T(8,128)(2,1)} %pad_maximum_fusion.3), channel_id=1, source_target_pairs={{0,1},{1,0},{2,3},{3,2},{4,5},{5,4},{6,7},{7,6},{8,9},{9,8},{10,11... | collective-permute-start | bytes 6291464 | tf_op jit(solution)/shard_map/ppermute | solution.py:40
  88.2 29.6 %collective-permute-start.12 = (bf16[512,512]{1,0:T(8,128)(2,1)S(1)}, bf16[512,512]{1,0:T(8,128)(2,1)S(1)}, u32[]{:S(2)}, u32[]{:S(2)}) collective-permute-start(bf16[512,512]{1,0:T(8,128)(2,1)S(1)} %bitcast.57), channel_id=1, source_target_pairs={{0,8},{8,16},{16,24},{24,0},{1,9},{9,17},{17,25},{25,1},{2,10},{10... | collective-permute-start | bytes 1572872 | tf_op jit(solution)/shard_map/ppermute | solution.py:44
  118.0 31.7 %collective-permute-start.15 = (bf16[1536,512]{1,0:T(8,128)(2,1)S(1)}, bf16[1536,512]{1,0:T(8,128)(2,1)S(1)}, u32[]{:S(2)}, u32[]{:S(2)}) collective-permute-start(bf16[1536,512]{1,0:T(8,128)(2,1)S(1)} %get-tuple-element.58), channel_id=1, source_target_pairs={{0,2},{1,3},{2,0},{3,1},{4,6},{5,7},{6,4},{7,5},{8,10},{9,11},{10,... | collective-permute-start | bytes 4718600 | tf_op jit(solution)/shard_map/ppermute | solution.py:40
  118.6 31.4 %collective-permute-start.16 = (bf16[1536,512]{1,0:T(8,128)(2,1)S(1)}, bf16[1536,512]{1,0:T(8,128)(2,1)S(1)}, u32[]{:S(2)}, u32[]{:S(2)}) collective-permute-start(bf16[1536,512]{1,0:T(8,128)(2,1)S(1)} %get-tuple-element.59), channel_id=1, source_target_pairs={{0,4},{1,5},{2,6},{3,7},{4,0},{5,1},{6,2},{7,3},{8,12},{9,13},{10,... | collective-permute-start | bytes 4718600 | tf_op jit(solution)/shard_map/ppermute | solution.py:40
  122.2 58.3 %collective-permute-start.28 = (f32[512,512]{1,0:T(8,128)S(1)}, f32[512,512]{1,0:T(8,128)S(1)}, u32[]{:S(2)}, u32[]{:S(2)}) collective-permute-start(f32[512,512]{1,0:T(8,128)S(1)} %fusion.30), channel_id=1, source_target_pairs={{0,1},{1,0},{2,3},{3,2},{4,5},{5,4},{6,7},{7,6},{8,9},{9,8},{10,11... | collective-permute-start | bytes 3145736 | tf_op jit(solution)/shard_map/ppermute | solution.py:40
  124.1 31.6 %collective-permute-start.30 = (f32[512,512]{1,0:T(8,128)S(1)}, f32[512,512]{1,0:T(8,128)S(1)}, u32[]{:S(2)}, u32[]{:S(2)}) collective-permute-start(f32[512,512]{1,0:T(8,128)S(1)} %fusion.31), channel_id=1, source_target_pairs={{0,1},{1,0},{2,3},{3,2},{4,5},{5,4},{6,7},{7,6},{8,9},{9,8},{10,11... | collective-permute-start | bytes 3145736 | tf_op jit(solution)/shard_map/ppermute | solution.py:40
  125.4 27.1 %collective-permute-start.18 = (bf16[512,512]{1,0:T(8,128)(2,1)S(1)}, bf16[512,512]{1,0:T(8,128)(2,1)S(1)}, u32[]{:S(2)}, u32[]{:S(2)}) collective-permute-start(bf16[512,512]{1,0:T(8,128)(2,1)S(1)} %fusion.2), channel_id=1, source_target_pairs={{0,8},{8,16},{16,24},{24,0},{1,9},{9,17},{17,25},{25,1},{2,10},{10... | collective-permute-start | bytes 1572872 | tf_op jit(solution)/shard_map/ppermute | solution.py:44
  153.7 16.2 %collective-permute-start.21 = (f32[512,512]{1,0:T(8,128)S(1)}, f32[512,512]{1,0:T(8,128)S(1)}, u32[]{:S(2)}, u32[]{:S(2)}) collective-permute-start(f32[512,512]{1,0:T(8,128)S(1)} %fusion.26), channel_id=1, source_target_pairs={{0,1},{1,0},{2,3},{3,2},{4,5},{5,4},{6,7},{7,6},{8,9},{9,8},{10,11... | collective-permute-start | bytes 3145736 | tf_op jit(solution)/shard_map/ppermute | solution.py:40
  153.8 14.3 %collective-permute-start.19 = (bf16[512,512]{1,0:T(8,128)(2,1)S(1)}, bf16[512,512]{1,0:T(8,128)(2,1)S(1)}, u32[]{:S(2)}, u32[]{:S(2)}) collective-permute-start(bf16[512,512]{1,0:T(8,128)(2,1)S(1)} %get-tuple-element.63), channel_id=1, source_target_pairs={{0,2},{1,3},{2,0},{3,1},{4,6},{5,7},{6,4},{7,5},{8,10},{9,11},{10,... | collective-permute-start | bytes 1572872 | tf_op jit(solution)/shard_map/ppermute | solution.py:40
  155.3 14.0 %collective-permute-start.20 = (bf16[512,512]{1,0:T(8,128)(2,1)S(1)}, bf16[512,512]{1,0:T(8,128)(2,1)S(1)}, u32[]{:S(2)}, u32[]{:S(2)}) collective-permute-start(bf16[512,512]{1,0:T(8,128)(2,1)S(1)} %get-tuple-element.64), channel_id=1, source_target_pairs={{0,4},{1,5},{2,6},{3,7},{4,0},{5,1},{6,2},{7,3},{8,12},{9,13},{10,... | collective-permute-start | bytes 1572872 | tf_op jit(solution)/shard_map/ppermute | solution.py:40
  156.9 23.6 %collective-permute-start.31 = (bf16[512,512]{1,0:T(8,128)(2,1)S(1)}, bf16[512,512]{1,0:T(8,128)(2,1)S(1)}, u32[]{:S(2)}, u32[]{:S(2)}) collective-permute-start(bf16[512,512]{1,0:T(8,128)(2,1)S(1)} %fusion.7), channel_id=1, source_target_pairs={{0,8},{8,16},{16,24},{24,0},{1,9},{9,17},{17,25},{25,1},{2,10},{10... | collective-permute-start | bytes 1572872 | tf_op jit(solution)/shard_map/ppermute | solution.py:44
  168.2 11.1 %collective-permute-start.25 = (f32[512,512]{1,0:T(8,128)S(1)}, f32[512,512]{1,0:T(8,128)S(1)}, u32[]{:S(2)}, u32[]{:S(2)}) collective-permute-start(f32[512,512]{1,0:T(8,128)S(1)} %fusion.29), channel_id=1, source_target_pairs={{0,1},{1,0},{2,3},{3,2},{4,5},{5,4},{6,7},{7,6},{8,9},{9,8},{10,11... | collective-permute-start | bytes 3145736 | tf_op jit(solution)/shard_map/ppermute | solution.py:40
  171.2 14.1 %collective-permute-start.29 = (bf16[512,512]{1,0:T(8,128)(2,1)S(1)}, bf16[512,512]{1,0:T(8,128)(2,1)S(1)}, u32[]{:S(2)}, u32[]{:S(2)}) collective-permute-start(bf16[512,512]{1,0:T(8,128)(2,1)S(1)} %fusion.3), channel_id=1, source_target_pairs={{0,24},{8,0},{16,8},{24,16},{1,25},{9,1},{17,9},{25,17},{2,26},{10... | collective-permute-start | bytes 1572872 | tf_op jit(solution)/shard_map/ppermute | solution.py:44
  187.4 10.3 %collective-permute-start.22 = (f32[512,512]{1,0:T(8,128)}, f32[512,512]{1,0:T(8,128)}, u32[]{:S(2)}, u32[]{:S(2)}) collective-permute-start(f32[512,512]{1,0:T(8,128)} %fusion.27), channel_id=1, source_target_pairs={{0,1},{1,0},{2,3},{3,2},{4,5},{5,4},{6,7},{7,6},{8,9},{9,8},{10,11... | collective-permute-start | bytes 3145736 | tf_op jit(solution)/shard_map/ppermute | solution.py:40
  188.3 31.3 %collective-permute-start.24 = (f32[512,512]{1,0:T(8,128)}, f32[512,512]{1,0:T(8,128)S(1)}, u32[]{:S(2)}, u32[]{:S(2)}) collective-permute-start(f32[512,512]{1,0:T(8,128)} %fusion.28), channel_id=1, source_target_pairs={{0,1},{1,0},{2,3},{3,2},{4,5},{5,4},{6,7},{7,6},{8,9},{9,8},{10,11... | collective-permute-start | bytes 3145736 | tf_op jit(solution)/shard_map/ppermute | solution.py:40
  192.9 29.5 %collective-permute-start.14 = (f32[512,512]{1,0:T(8,128)}, f32[512,512]{1,0:T(8,128)}, u32[]{:S(2)}, u32[]{:S(2)}) collective-permute-start(f32[512,512]{1,0:T(8,128)} %fusion.24), channel_id=1, source_target_pairs={{0,1},{1,0},{2,3},{3,2},{4,5},{5,4},{6,7},{7,6},{8,9},{9,8},{10,11... | collective-permute-start | bytes 3145736 | tf_op jit(solution)/shard_map/ppermute | solution.py:40
  193.0 26.6 %collective-permute-start.26 = (bf16[512,512]{1,0:T(8,128)(2,1)S(1)}, bf16[512,512]{1,0:T(8,128)(2,1)S(1)}, u32[]{:S(2)}, u32[]{:S(2)}) collective-permute-start(bf16[512,512]{1,0:T(8,128)(2,1)S(1)} %fusion.4), channel_id=1, source_target_pairs={{0,8},{8,16},{16,24},{24,0},{1,9},{9,17},{17,25},{25,1},{2,10},{10... | collective-permute-start | bytes 1572872 | tf_op jit(solution)/shard_map/ppermute | solution.py:44
  201.1 21.3 %collective-permute-start.23 = (bf16[512,512]{1,0:T(8,128)(2,1)}, bf16[512,512]{1,0:T(8,128)(2,1)}, u32[]{:S(2)}, u32[]{:S(2)}) collective-permute-start(bf16[512,512]{1,0:T(8,128)(2,1)} %add_convert_fusion.1), channel_id=1, source_target_pairs={{0,24},{8,0},{16,8},{24,16},{1,25},{9,1},{17,9},{25,17},{2,26},{10... | collective-permute-start | bytes 1572872 | tf_op jit(solution)/shard_map/ppermute | solution.py:44
  219.9 13.7 %collective-permute-start.27 = (bf16[512,512]{1,0:T(8,128)(2,1)S(1)}, bf16[512,512]{1,0:T(8,128)(2,1)}, u32[]{:S(2)}, u32[]{:S(2)}) collective-permute-start(bf16[512,512]{1,0:T(8,128)(2,1)S(1)} %fusion.10), channel_id=1, source_target_pairs={{0,8},{8,16},{16,24},{24,0},{1,9},{9,17},{17,25},{25,1},{2,10},{10... | collective-permute-start | bytes 1572872 | tf_op jit(solution)/shard_map/ppermute | solution.py:44
  (36 other events, 574.2 us)
Sparse Core Ops, SparseCore 0:
  187.5 39.6 all-gather.1

commit v20 on v19

--- a/solution.py
+++ b/solution.py
@@ -104,48 +104,56 @@
     def slot(at, gate):
         to_x, to_y = [], []
         if at:
-            stack, x, y = stacks[at - 1]
+            _, x, y = stacks[at - 1]
             to_x.append(y[second])
             to_y.append(x[first])
         if at < len(groups):
-            new = jnp.concatenate([pieces[key] for key in groups[at]], axis=0)
-            to_x.append(new)
-            to_y.append(new)
+            stacks[at] = jnp.concatenate([pieces[key] for key in groups[at]], axis=0)
+            to_x.append(stacks[at])
+            to_y.append(stacks[at])
         to_x, to_y = after((jnp.concatenate(to_x, axis=0), jnp.concatenate(to_y, axis=0)), gate)
-        got = [swap(to_x, X), swap(to_y, Y)]
-        from_x, from_y = after(got, [])
+        return [swap(to_x, X), swap(to_y, Y)]
+
+    def use(at, got, others):
+        from_x, from_y = after(got, others)
         if at:
+            stack, x, y = stacks[at - 1]
             evens[at - 1] = [
                 jnp.concatenate([stack[first], x[first], y[first], from_y[:tokens]], axis=1),
                 jnp.concatenate([stack[second], x[second], y[second], from_x[:tokens]], axis=1),
             ]
         if at < len(groups):
-            stacks[at] = (new, from_x[-2 * tokens :], from_y[-2 * tokens :])
-        return got
+            stacks[at] = (stacks[at], from_x[-2 * tokens :], from_y[-2 * tokens :])
 
     stacks, evens = {}, {}
     due = slot(0, [])
+    use(0, due, [])
     due += [fetch(0, 1, []), fetch(0, 2, []), theirs[0]]
 
     gate, due = due, slot(1, due)
+    use(1, due, [])
     due += [fetch(0, 3, gate), fetch(1, 1, gate), fetch(1, 2, gate)]
 
     gate, due = due, slot(2, due)
+    use(2, due, [])
     theirs[1] = rows_for_other(1, gate)
     due += [fetch(1, 3, gate), theirs[1]]
 
     gate, due = due, slot(3, due)
+    use(3, due, [])
     rotate(groups[1], after(evens[1], gate))
     passed_in = pass_on(0)
     due.append(passed_in)
-    rotate(groups[0], after(evens[0], gate))
+    rotate(groups[0][:1], after(evens[0][:1], gate))
 
     gate, due = due, slot(4, due)
     in_from_behind = send_ahead(0, passed_in, gate)
     rotate(groups[2], after(evens[2], gate))
     in_from_ahead = send_behind(0)
     passed_out = pass_on(1)
-    rotate(groups[3], after(evens[3], rotated[0, 3]))
+    rotate(groups[0][1:], after(evens[0][1:], passed_out))
+    use(4, due, rotated[0, 3])
+    rotate(groups[3], evens[3])
     begun = [rotated[1, 2], halves[1, 1], halves[1, 3]]
     rot_in = after(keep(0, in_from_behind, in_from_ahead), begun)
     all_rot_in = lax.all_gather(rot_in, "tensor", axis=1, tiled=True)

time: 256 us -> 259 us (1.012)
  waiting for transfers between devices: 138 us -> 141 us
    ppermute x12, waiting for transfers between devices: 62.6 us -> 66.3 us  [shift(): return lax.ppermute(block, 'dp', [(z, (z + by) % n) for z in range(n)])]
    unnamed x70 -> x92, local copies, waits for them, and re-layouts: 6.22 us -> 7.07 us
  transfers between devices with their start and end apart: 33 -> 33, of which waited for: 16 -> 17; matrix products, arithmetic and copies ran while one was open for 17% -> 17% of each run, Pallas kernels for 0% -> 0%
where the time goes in v20:
time: 259 us; the launch traced here: 255 us
  waiting for transfers between devices  141 us (54%)
  matrix products  39.4 us (15%)
  starting transfers between devices  32.4 us (13%)
  local copies, waits for them, and re-layouts  19.5 us (8%)
  between operations  15.2 us (6%)
  other arithmetic  7.26 us (3%)
    ppermute x20, waiting for transfers between devices, swap(): lax.ppermute(block, 'tensor', [(j, j ^ bit) for j in range(X + Y + CORE +...  75 us
    ppermute x12, waiting for transfers between devices, shift(): return lax.ppermute(block, 'dp', [(z, (z + by) % n) for z in range(n)])  66.3 us
    dot_general x15, matrix products, dot(): return jnp.dot(a, b, preferred_element_type=jnp.float32)  28.8 us
    ppermute x12, starting transfers between devices, shift(): return lax.ppermute(block, 'dp', [(z, (z + by) % n) for z in range(n)])  18.9 us
    ppermute x20, starting transfers between devices, swap(): lax.ppermute(block, 'tensor', [(j, j ^ bit) for j in range(X + Y + CORE +...  13.5 us
    dot_general x1, matrix products, product_and_divide(): lax.dot_general(rot_out, all_rot_in, contract, preferred_element_type=jnp...  10.6 us
    unnamed x92, local copies, waits for them, and re-layouts  7.07 us
  transfers between devices with their start and end apart: 33, of which 17 were waited for; matrix products, arithmetic and copies ran while one was open for 17% of the time, Pallas kernels for 0%

profile of v20, /device:TPU:16, one launch (start us, length us, event | category | flops | bytes accessed | tf_op | source)
XLA Modules:
  0.0 255.2 jit_solution(8420850458036845085)
XLA Ops:
  13.0 12.7 %collective-permute-done.2 = bf16[512,512]{1,0:T(8,128)(2,1)S(1)} collective-permute-done((bf16[512,512]{1,0:T(8,128)(2,1)S(1)}, bf16[512,512]{1,0:T(8,128)(2,1)S(1)}, u32[]{:S(2)}, u32[]{:S(2)}) %collective-permute-start.2) | collective-permute-done | bytes 524320 | tf_op jit(solution)/shard_map/ppermute | solution.py:44
  26.1 8.3 %collective-permute-done = bf16[1024,512]{1,0:T(8,128)(2,1)S(1)} collective-permute-done((bf16[1024,512]{1,0:T(8,128)(2,1)S(1)}, bf16[1024,512]{1,0:T(8,128)(2,1)S(1)}, u32[]{:S(2)}, u32[]{:S(2)}) %collective-permute-start) | collective-permute-done | bytes 1048608 | tf_op jit(solution)/shard_map/ppermute | solution.py:40
  36.8 2.7 %collective-permute-done.3 = bf16[512,512]{1,0:T(8,128)(2,1)S(1)} collective-permute-done((bf16[512,512]{1,0:T(8,128)(2,1)S(1)}, bf16[512,512]{1,0:T(8,128)(2,1)S(1)}, u32[]{:S(2)}, u32[]{:S(2)}) %collective-permute-start.3) | collective-permute-done | bytes 524320 | tf_op jit(solution)/shard_map/ppermute | solution.py:44
  40.8 3.5 %collective-permute-start.7 = (bf16[512,512]{1,0:T(8,128)(2,1)S(1)}, bf16[512,512]{1,0:T(8,128)(2,1)S(1)}, u32[]{:S(2)}, u32[]{:S(2)}) collective-permute-start(bf16[512,512]{1,0:T(8,128)(2,1)S(1)} %bitcast.49), channel_id=1, source_target_pairs={{0,8},{8,16},{16,24},{24,0},{1,9},{9,17},{17,25},{25,1},{2,10},{10... | collective-permute-start | bytes 1572872 | tf_op jit(solution)/shard_map/ppermute | solution.py:44
  44.4 12.8 %collective-permute-done.8 = bf16[512,512]{1,0:T(8,128)(2,1)S(1)} collective-permute-done((bf16[512,512]{1,0:T(8,128)(2,1)S(1)}, bf16[512,512]{1,0:T(8,128)(2,1)S(1)}, u32[]{:S(2)}, u32[]{:S(2)}) %collective-permute-start.8) | collective-permute-done | bytes 524320 | tf_op jit(solution)/shard_map/ppermute | solution.py:44
  57.2 16.6 %collective-permute-done.5 = bf16[1536,512]{1,0:T(8,128)(2,1)S(1)} collective-permute-done((bf16[1536,512]{1,0:T(8,128)(2,1)S(1)}, bf16[1536,512]{1,0:T(8,128)(2,1)S(1)}, u32[]{:S(2)}, u32[]{:S(2)}) %collective-permute-start.5) | collective-permute-done | bytes 1572896 | tf_op jit(solution)/shard_map/ppermute | solution.py:40
  79.5 3.6 %collective-permute-start.12 = (bf16[512,512]{1,0:T(8,128)(2,1)S(1)}, bf16[512,512]{1,0:T(8,128)(2,1)S(1)}, u32[]{:S(2)}, u32[]{:S(2)}) collective-permute-start(bf16[512,512]{1,0:T(8,128)(2,1)S(1)} %bitcast.53), channel_id=1, source_target_pairs={{0,8},{8,16},{16,24},{24,0},{1,9},{9,17},{17,25},{25,1},{2,10},{10... | collective-permute-start | bytes 1572872 | tf_op jit(solution)/shard_map/ppermute | solution.py:44
  83.1 25.9 %collective-permute-done.10 = bf16[1536,512]{1,0:T(8,128)(2,1)S(1)} collective-permute-done((bf16[1536,512]{1,0:T(8,128)(2,1)S(1)}, bf16[1536,512]{1,0:T(8,128)(2,1)S(1)}, u32[]{:S(2)}, u32[]{:S(2)}) %collective-permute-start.10) | collective-permute-done | bytes 1572896 | tf_op jit(solution)/shard_map/ppermute | solution.py:40
  112.3 1.9 pad_maximum_fusion.5
  114.2 1.8 pad_maximum_fusion.20
  117.9 2.3 fusion.30
  121.4 1.8 dynamic-slice_bitcast_fusion.7
  130.4 2.5 fusion.1
  132.9 3.4 %collective-permute-start.17 = (bf16[512,512]{1,0:T(8,128)(2,1)S(1)}, bf16[512,512]{1,0:T(8,128)(2,1)S(1)}, u32[]{:S(2)}, u32[]{:S(2)}) collective-permute-start(bf16[512,512]{1,0:T(8,128)(2,1)S(1)} %fusion.1), channel_id=1, source_target_pairs={{0,8},{8,16},{16,24},{24,0},{1,9},{9,17},{17,25},{25,1},{2,10},{10... | collective-permute-start | bytes 1572872 | tf_op jit(solution)/shard_map/ppermute | solution.py:44
  136.2 11.8 %collective-permute-done.14 = bf16[1536,512]{1,0:T(8,128)(2,1)} collective-permute-done((bf16[1536,512]{1,0:T(8,128)(2,1)}, bf16[1536,512]{1,0:T(8,128)(2,1)}, u32[]{:S(2)}, u32[]{:S(2)}) %collective-permute-start.14) | collective-permute-done | bytes 1572896 | tf_op jit(solution)/shard_map/ppermute | solution.py:40
  149.9 1.8 fusion.23
  157.9 2.5 collective-permute-start.31
  165.8 8.2 %collective-permute-done.21 = bf16[512,512]{1,0:T(8,128)(2,1)S(1)} collective-permute-done((bf16[512,512]{1,0:T(8,128)(2,1)S(1)}, bf16[512,512]{1,0:T(8,128)(2,1)S(1)}, u32[]{:S(2)}, u32[]{:S(2)}) %collective-permute-start.21) | collective-permute-done | bytes 524320 | tf_op jit(solution)/shard_map/ppermute | solution.py:40
  175.2 2.3 fusion.17
  177.5 2.3 fusion.16
  179.8 2.0 fusion.2
  181.9 4.8 %collective-permute-done.29 = bf16[512,512]{1,0:T(8,128)(2,1)S(1)} collective-permute-done((bf16[512,512]{1,0:T(8,128)(2,1)S(1)}, bf16[512,512]{1,0:T(8,128)(2,1)S(1)}, u32[]{:S(2)}, u32[]{:S(2)}) %collective-permute-start.29) | collective-permute-done | bytes 524320 | tf_op jit(solution)/shard_map/ppermute | solution.py:44
  186.7 2.1 fusion.10
  188.8 2.5 collective-permute-start.19
  193.8 9.6 %collective-permute-done.19 = bf16[512,512]{1,0:T(8,128)(2,1)} collective-permute-done((bf16[512,512]{1,0:T(8,128)(2,1)}, bf16[512,512]{1,0:T(8,128)(2,1)}, u32[]{:S(2)}, u32[]{:S(2)}) %collective-permute-start.19) | collective-permute-done | bytes 524320 | tf_op jit(solution)/shard_map/ppermute | solution.py:44
  203.5 2.2 fusion.32
  205.9 3.5 %fusion.11 = bf16[512,512]{1,0:T(8,128)(2,1)} fusion(bf16[512,512]{1,0:T(8,128)(2,1)} %collective-permute-done.19, f32[512,512]{1,0:T(8,128)} %collective-permute-done.26, pred[]{:T(512)S(6)} %eq.17, bf16[512,512]{1,0:T(8,128)(2,1)S(1)} %copy-done.45, bf16[512,512]{1,0:T(8,128)(2,1)S(1)} %copy-done.24, bf16[512,512]{1,0:T(8,128)(2,1)S(1)} %copy-done.26, ...), kind=kOutput, calls=%fused_computation.44 | convolution fusion | flops 1091305472 | bytes 6291457 | tf_op jit(solution)/shard_map/dot_general | solution.py:22
  209.4 2.5 collective-permute-start.27
  211.9 2.1 fusion.5
  214.0 9.9 %collective-permute-done.27 = bf16[512,512]{1,0:T(8,128)(2,1)} collective-permute-done((bf16[512,512]{1,0:T(8,128)(2,1)}, bf16[512,512]{1,0:T(8,128)(2,1)}, u32[]{:S(2)}, u32[]{:S(2)}) %collective-permute-start.27) | collective-permute-done | bytes 524320 | tf_op jit(solution)/shard_map/ppermute | solution.py:44
  223.9 13.8 %collective-permute-done.25 = bf16[512,512]{1,0:T(8,128)(2,1)} collective-permute-done((bf16[512,512]{1,0:T(8,128)(2,1)}, bf16[512,512]{1,0:T(8,128)(2,1)}, u32[]{:S(2)}, u32[]{:S(2)}) %collective-permute-start.25) | collective-permute-done | bytes 524320 | tf_op jit(solution)/shard_map/ppermute | solution.py:44
  237.7 10.6 %fusion = bf16[1,512,4096]{2,1,0:T(8,128)(2,1)} fusion(bf16[512,4096]{1,0:T(8,128)(2,1)} %param.11, bf16[512,4096]{1,0:T(8,128)(2,1)} %all-gather.2.cloned.1.call-done, f32[512,512]{1,0:T(8,128)} %collective-permute-done.20, bf16[512,2048]{1,0:T(8,128)(2,1)S(1)} %pad_maximum_fusion.1, bf16[512,512]{1,0:T(8,128)(2,1)} %collective-permute-done.25, ...), kind=kOutput, calls=%fused_computation.1 | convolution fusion | flops 3241148416 | bytes 18874370 | tf_op jit(solution)/shard_map/dot_general | solution.py:13
  (167 shorter events, 45.5 us)
Async XLA Ops:
  6.5 231.2 %all-gather.2.cloned.1.call-start = ((), (), s32[]{:S(2)}) async-start(), calls=%async_computation | async-start | bytes 4718592 | tf_op jit(solution)/shard_map/all_gather | solution.py:159
  8.4 31.3 %collective-permute-start.4 = (bf16[2048,512]{1,0:T(8,128)(2,1)S(1)}, bf16[2048,512]{1,0:T(8,128)(2,1)S(1)}, u32[]{:S(2)}, u32[]{:S(2)}) collective-permute-start(bf16[2048,512]{1,0:T(8,128)(2,1)S(1)} %pad_maximum_fusion), channel_id=1, source_target_pairs={{0,1},{1,0},{2,3},{3,2},{4,5},{5,4},{6,7},{7,6},{8,9},{9,8},{10,11... | collective-permute-start | bytes 6291464 | tf_op jit(solution)/shard_map/ppermute | solution.py:40
  9.5 25.0 %collective-permute-start = (bf16[1024,512]{1,0:T(8,128)(2,1)S(1)}, bf16[1024,512]{1,0:T(8,128)(2,1)S(1)}, u32[]{:S(2)}, u32[]{:S(2)}) collective-permute-start(bf16[1024,512]{1,0:T(8,128)(2,1)S(1)} %pad_maximum_fusion.24), channel_id=1, source_target_pairs={{0,2},{1,3},{2,0},{3,1},{4,6},{5,7},{6,4},{7,5},{8,10},{9,11},{10,... | collective-permute-start | bytes 3145736 | tf_op jit(solution)/shard_map/ppermute | solution.py:40
  11.0 24.6 %collective-permute-start.1 = (bf16[1024,512]{1,0:T(8,128)(2,1)S(1)}, bf16[1024,512]{1,0:T(8,128)(2,1)S(1)}, u32[]{:S(2)}, u32[]{:S(2)}) collective-permute-start(bf16[1024,512]{1,0:T(8,128)(2,1)S(1)} %pad_maximum_fusion.24), channel_id=1, source_target_pairs={{0,4},{1,5},{2,6},{3,7},{4,0},{5,1},{6,2},{7,3},{8,12},{9,13},{10,... | collective-permute-start | bytes 3145736 | tf_op jit(solution)/shard_map/ppermute | solution.py:40
  12.5 13.1 %collective-permute-start.2 = (bf16[512,512]{1,0:T(8,128)(2,1)S(1)}, bf16[512,512]{1,0:T(8,128)(2,1)S(1)}, u32[]{:S(2)}, u32[]{:S(2)}) collective-permute-start(bf16[512,512]{1,0:T(8,128)(2,1)S(1)} %bitcast.48), channel_id=1, source_target_pairs={{0,24},{8,0},{16,8},{24,16},{1,25},{9,1},{17,9},{25,17},{2,26},{10... | collective-permute-start | bytes 1572872 | tf_op jit(solution)/shard_map/ppermute | solution.py:44
  25.6 13.8 %collective-permute-start.3 = (bf16[512,512]{1,0:T(8,128)(2,1)S(1)}, bf16[512,512]{1,0:T(8,128)(2,1)S(1)}, u32[]{:S(2)}, u32[]{:S(2)}) collective-permute-start(bf16[512,512]{1,0:T(8,128)(2,1)S(1)} %collective-permute-done.2), channel_id=1, source_target_pairs={{0,24},{8,0},{16,8},{24,16},{1,25},{9,1},{17,9},{25,17},{2,26},{10... | collective-permute-start | bytes 1572872 | tf_op jit(solution)/shard_map/ppermute | solution.py:44
  39.7 34.1 %collective-permute-start.5 = (bf16[1536,512]{1,0:T(8,128)(2,1)S(1)}, bf16[1536,512]{1,0:T(8,128)(2,1)S(1)}, u32[]{:S(2)}, u32[]{:S(2)}) collective-permute-start(bf16[1536,512]{1,0:T(8,128)(2,1)S(1)} %get-tuple-element.42), channel_id=1, source_target_pairs={{0,2},{1,3},{2,0},{3,1},{4,6},{5,7},{6,4},{7,5},{8,10},{9,11},{10,... | collective-permute-start | bytes 4718600 | tf_op jit(solution)/shard_map/ppermute | solution.py:40
  40.3 33.7 %collective-permute-start.6 = (bf16[1536,512]{1,0:T(8,128)(2,1)S(1)}, bf16[1536,512]{1,0:T(8,128)(2,1)S(1)}, u32[]{:S(2)}, u32[]{:S(2)}) collective-permute-start(bf16[1536,512]{1,0:T(8,128)(2,1)S(1)} %get-tuple-element.43), channel_id=1, source_target_pairs={{0,4},{1,5},{2,6},{3,7},{4,0},{5,1},{6,2},{7,3},{8,12},{9,13},{10,... | collective-permute-start | bytes 4718600 | tf_op jit(solution)/shard_map/ppermute | solution.py:40
  40.8 16.4 %collective-permute-start.8 = (bf16[512,512]{1,0:T(8,128)(2,1)S(1)}, bf16[512,512]{1,0:T(8,128)(2,1)S(1)}, u32[]{:S(2)}, u32[]{:S(2)}) collective-permute-start(bf16[512,512]{1,0:T(8,128)(2,1)S(1)} %bitcast.52), channel_id=1, source_target_pairs={{0,24},{8,0},{16,8},{24,16},{1,25},{9,1},{17,9},{25,17},{2,26},{10... | collective-permute-start | bytes 1572872 | tf_op jit(solution)/shard_map/ppermute | solution.py:44
  40.8 35.0 %collective-permute-start.7 = (bf16[512,512]{1,0:T(8,128)(2,1)S(1)}, bf16[512,512]{1,0:T(8,128)(2,1)S(1)}, u32[]{:S(2)}, u32[]{:S(2)}) collective-permute-start(bf16[512,512]{1,0:T(8,128)(2,1)S(1)} %bitcast.49), channel_id=1, source_target_pairs={{0,8},{8,16},{16,24},{24,0},{1,9},{9,17},{17,25},{25,1},{2,10},{10... | collective-permute-start | bytes 1572872 | tf_op jit(solution)/shard_map/ppermute | solution.py:44
  57.2 18.7 %collective-permute-start.9 = (bf16[512,512]{1,0:T(8,128)(2,1)S(1)}, bf16[512,512]{1,0:T(8,128)(2,1)S(1)}, u32[]{:S(2)}, u32[]{:S(2)}) collective-permute-start(bf16[512,512]{1,0:T(8,128)(2,1)S(1)} %collective-permute-done.8), channel_id=1, source_target_pairs={{0,24},{8,0},{16,8},{24,16},{1,25},{9,1},{17,9},{25,17},{2,26},{10... | collective-permute-start | bytes 1572872 | tf_op jit(solution)/shard_map/ppermute | solution.py:44
  76.1 32.9 %collective-permute-start.10 = (bf16[1536,512]{1,0:T(8,128)(2,1)S(1)}, bf16[1536,512]{1,0:T(8,128)(2,1)S(1)}, u32[]{:S(2)}, u32[]{:S(2)}) collective-permute-start(bf16[1536,512]{1,0:T(8,128)(2,1)S(1)} %get-tuple-element.49), channel_id=1, source_target_pairs={{0,2},{1,3},{2,0},{3,1},{4,6},{5,7},{6,4},{7,5},{8,10},{9,11},{10,... | collective-permute-start | bytes 4718600 | tf_op jit(solution)/shard_map/ppermute | solution.py:40
  77.7 32.5 %collective-permute-start.11 = (bf16[1536,512]{1,0:T(8,128)(2,1)S(1)}, bf16[1536,512]{1,0:T(8,128)(2,1)S(1)}, u32[]{:S(2)}, u32[]{:S(2)}) collective-permute-start(bf16[1536,512]{1,0:T(8,128)(2,1)S(1)} %get-tuple-element.50), channel_id=1, source_target_pairs={{0,4},{1,5},{2,6},{3,7},{4,0},{5,1},{6,2},{7,3},{8,12},{9,13},{10,... | collective-permute-start | bytes 4718600 | tf_op jit(solution)/shard_map/ppermute | solution.py:40
  79.4 36.6 %collective-permute-start.13 = (bf16[2048,512]{1,0:T(8,128)(2,1)S(1)}, bf16[2048,512]{1,0:T(8,128)(2,1)S(1)}, u32[]{:S(2)}, u32[]{:S(2)}) collective-permute-start(bf16[2048,512]{1,0:T(8,128)(2,1)S(1)} %pad_maximum_fusion.2), channel_id=1, source_target_pairs={{0,1},{1,0},{2,3},{3,2},{4,5},{5,4},{6,7},{7,6},{8,9},{9,8},{10,11... | collective-permute-start | bytes 6291464 | tf_op jit(solution)/shard_map/ppermute | solution.py:40
  79.5 34.7 %collective-permute-start.12 = (bf16[512,512]{1,0:T(8,128)(2,1)S(1)}, bf16[512,512]{1,0:T(8,128)(2,1)S(1)}, u32[]{:S(2)}, u32[]{:S(2)}) collective-permute-start(bf16[512,512]{1,0:T(8,128)(2,1)S(1)} %bitcast.53), channel_id=1, source_target_pairs={{0,8},{8,16},{16,24},{24,0},{1,9},{9,17},{17,25},{25,1},{2,10},{10... | collective-permute-start | bytes 1572872 | tf_op jit(solution)/shard_map/ppermute | solution.py:44
  116.1 32.0 %collective-permute-start.14 = (bf16[1536,512]{1,0:T(8,128)(2,1)}, bf16[1536,512]{1,0:T(8,128)(2,1)}, u32[]{:S(2)}, u32[]{:S(2)}) collective-permute-start(bf16[1536,512]{1,0:T(8,128)(2,1)} %get-tuple-element.55), channel_id=1, source_target_pairs={{0,2},{1,3},{2,0},{3,1},{4,6},{5,7},{6,4},{7,5},{8,10},{9,11},{10,... | collective-permute-start | bytes 4718600 | tf_op jit(solution)/shard_map/ppermute | solution.py:40
  116.7 31.7 %collective-permute-start.15 = (bf16[1536,512]{1,0:T(8,128)(2,1)}, bf16[1536,512]{1,0:T(8,128)(2,1)}, u32[]{:S(2)}, u32[]{:S(2)}) collective-permute-start(bf16[1536,512]{1,0:T(8,128)(2,1)} %get-tuple-element.56), channel_id=1, source_target_pairs={{0,4},{1,5},{2,6},{3,7},{4,0},{5,1},{6,2},{7,3},{8,12},{9,13},{10,... | collective-permute-start | bytes 4718600 | tf_op jit(solution)/shard_map/ppermute | solution.py:40
  120.2 10.2 %collective-permute-start.16 = (f32[512,512]{1,0:T(8,128)}, f32[512,512]{1,0:T(8,128)}, u32[]{:S(2)}, u32[]{:S(2)}) collective-permute-start(f32[512,512]{1,0:T(8,128)} %fusion.30), channel_id=1, source_target_pairs={{0,1},{1,0},{2,3},{3,2},{4,5},{5,4},{6,7},{7,6},{8,9},{9,8},{10,11... | collective-permute-start | bytes 3145736 | tf_op jit(solution)/shard_map/ppermute | solution.py:40
  129.8 26.8 %collective-permute-start.30 = (f32[512,512]{1,0:T(8,128)S(1)}, f32[512,512]{1,0:T(8,128)S(1)}, u32[]{:S(2)}, u32[]{:S(2)}) collective-permute-start(f32[512,512]{1,0:T(8,128)S(1)} %fusion.35), channel_id=1, source_target_pairs={{0,1},{1,0},{2,3},{3,2},{4,5},{5,4},{6,7},{7,6},{8,9},{9,8},{10,11... | collective-permute-start | bytes 3145736 | tf_op jit(solution)/shard_map/ppermute | solution.py:40
  132.9 20.6 %collective-permute-start.17 = (bf16[512,512]{1,0:T(8,128)(2,1)S(1)}, bf16[512,512]{1,0:T(8,128)(2,1)S(1)}, u32[]{:S(2)}, u32[]{:S(2)}) collective-permute-start(bf16[512,512]{1,0:T(8,128)(2,1)S(1)} %fusion.1), channel_id=1, source_target_pairs={{0,8},{8,16},{16,24},{24,0},{1,9},{9,17},{17,25},{25,1},{2,10},{10... | collective-permute-start | bytes 1572872 | tf_op jit(solution)/shard_map/ppermute | solution.py:44
  154.7 9.7 %collective-permute-start.23 = (f32[512,512]{1,0:T(8,128)S(1)}, f32[512,512]{1,0:T(8,128)S(1)}, u32[]{:S(2)}, u32[]{:S(2)}) collective-permute-start(f32[512,512]{1,0:T(8,128)S(1)} %fusion.33), channel_id=1, source_target_pairs={{0,1},{1,0},{2,3},{3,2},{4,5},{5,4},{6,7},{7,6},{8,9},{9,8},{10,11... | collective-permute-start | bytes 3145736 | tf_op jit(solution)/shard_map/ppermute | solution.py:40
  156.1 25.8 %collective-permute-start.28 = (f32[512,512]{1,0:T(8,128)S(1)}, f32[512,512]{1,0:T(8,128)S(1)}, u32[]{:S(2)}, u32[]{:S(2)}) collective-permute-start(f32[512,512]{1,0:T(8,128)S(1)} %fusion.34), channel_id=1, source_target_pairs={{0,1},{1,0},{2,3},{3,2},{4,5},{5,4},{6,7},{7,6},{8,9},{9,8},{10,11... | collective-permute-start | bytes 3145736 | tf_op jit(solution)/shard_map/ppermute | solution.py:40
  157.9 24.0 %collective-permute-start.31 = (bf16[512,512]{1,0:T(8,128)(2,1)S(1)}, bf16[512,512]{1,0:T(8,128)(2,1)S(1)}, u32[]{:S(2)}, u32[]{:S(2)}) collective-permute-start(bf16[512,512]{1,0:T(8,128)(2,1)S(1)} %fusion.9), channel_id=1, source_target_pairs={{0,8},{8,16},{16,24},{24,0},{1,9},{9,17},{17,25},{25,1},{2,10},{10... | collective-permute-start | bytes 1572872 | tf_op jit(solution)/shard_map/ppermute | solution.py:44
  160.4 13.6 %collective-permute-start.21 = (bf16[512,512]{1,0:T(8,128)(2,1)S(1)}, bf16[512,512]{1,0:T(8,128)(2,1)S(1)}, u32[]{:S(2)}, u32[]{:S(2)}) collective-permute-start(bf16[512,512]{1,0:T(8,128)(2,1)S(1)} %get-tuple-element.62), channel_id=1, source_target_pairs={{0,2},{1,3},{2,0},{3,1},{4,6},{5,7},{6,4},{7,5},{8,10},{9,11},{10,... | collective-permute-start | bytes 1572872 | tf_op jit(solution)/shard_map/ppermute | solution.py:40
  161.8 13.3 %collective-permute-start.22 = (bf16[512,512]{1,0:T(8,128)(2,1)S(1)}, bf16[512,512]{1,0:T(8,128)(2,1)S(1)}, u32[]{:S(2)}, u32[]{:S(2)}) collective-permute-start(bf16[512,512]{1,0:T(8,128)(2,1)S(1)} %get-tuple-element.63), channel_id=1, source_target_pairs={{0,4},{1,5},{2,6},{3,7},{4,0},{5,1},{6,2},{7,3},{8,12},{9,13},{10,... | collective-permute-start | bytes 1572872 | tf_op jit(solution)/shard_map/ppermute | solution.py:40
  164.4 15.4 %collective-permute-start.18 = (f32[512,512]{1,0:T(8,128)S(1)}, f32[512,512]{1,0:T(8,128)S(1)}, u32[]{:S(2)}, u32[]{:S(2)}) collective-permute-start(f32[512,512]{1,0:T(8,128)S(1)} %fusion.31), channel_id=1, source_target_pairs={{0,1},{1,0},{2,3},{3,2},{4,5},{5,4},{6,7},{7,6},{8,9},{9,8},{10,11... | collective-permute-start | bytes 3145736 | tf_op jit(solution)/shard_map/ppermute | solution.py:40
  174.0 12.7 %collective-permute-start.29 = (bf16[512,512]{1,0:T(8,128)(2,1)S(1)}, bf16[512,512]{1,0:T(8,128)(2,1)S(1)}, u32[]{:S(2)}, u32[]{:S(2)}) collective-permute-start(bf16[512,512]{1,0:T(8,128)(2,1)S(1)} %fusion.4), channel_id=1, source_target_pairs={{0,24},{8,0},{16,8},{24,16},{1,25},{9,1},{17,9},{25,17},{2,26},{10... | collective-permute-start | bytes 1572872 | tf_op jit(solution)/shard_map/ppermute | solution.py:44
  188.7 17.0 %collective-permute-start.26 = (f32[512,512]{1,0:T(8,128)}, f32[512,512]{1,0:T(8,128)}, u32[]{:S(2)}, u32[]{:S(2)}) collective-permute-start(f32[512,512]{1,0:T(8,128)} %fusion.16), channel_id=1, source_target_pairs={{0,1},{1,0},{2,3},{3,2},{4,5},{5,4},{6,7},{7,6},{8,9},{9,8},{10,11... | collective-permute-start | bytes 3145736 | tf_op jit(solution)/shard_map/ppermute | solution.py:40
  188.8 14.6 %collective-permute-start.19 = (bf16[512,512]{1,0:T(8,128)(2,1)}, bf16[512,512]{1,0:T(8,128)(2,1)}, u32[]{:S(2)}, u32[]{:S(2)}) collective-permute-start(bf16[512,512]{1,0:T(8,128)(2,1)} %fusion.2), channel_id=1, source_target_pairs={{0,8},{8,16},{16,24},{24,0},{1,9},{9,17},{17,25},{25,1},{2,10},{10... | collective-permute-start | bytes 1572872 | tf_op jit(solution)/shard_map/ppermute | solution.py:44
  191.9 20.0 %collective-permute-start.24 = (f32[512,512]{1,0:T(8,128)}, f32[512,512]{1,0:T(8,128)S(1)}, u32[]{:S(2)}, u32[]{:S(2)}) collective-permute-start(f32[512,512]{1,0:T(8,128)} %fusion.17), channel_id=1, source_target_pairs={{0,1},{1,0},{2,3},{3,2},{4,5},{5,4},{6,7},{7,6},{8,9},{9,8},{10,11... | collective-permute-start | bytes 3145736 | tf_op jit(solution)/shard_map/ppermute | solution.py:40
  209.4 14.5 %collective-permute-start.27 = (bf16[512,512]{1,0:T(8,128)(2,1)}, bf16[512,512]{1,0:T(8,128)(2,1)}, u32[]{:S(2)}, u32[]{:S(2)}) collective-permute-start(bf16[512,512]{1,0:T(8,128)(2,1)} %fusion.11), channel_id=1, source_target_pairs={{0,8},{8,16},{16,24},{24,0},{1,9},{9,17},{17,25},{25,1},{2,10},{10... | collective-permute-start | bytes 1572872 | tf_op jit(solution)/shard_map/ppermute | solution.py:44
  214.0 23.7 %collective-permute-start.25 = (bf16[512,512]{1,0:T(8,128)(2,1)}, bf16[512,512]{1,0:T(8,128)(2,1)}, u32[]{:S(2)}, u32[]{:S(2)}) collective-permute-start(bf16[512,512]{1,0:T(8,128)(2,1)} %fusion.5), channel_id=1, source_target_pairs={{0,24},{8,0},{16,8},{24,16},{1,25},{9,1},{17,9},{25,17},{2,26},{10... | collective-permute-start | bytes 1572872 | tf_op jit(solution)/shard_map/ppermute | solution.py:44
  (47 other events, 702.0 us)
Sparse Core Ops, SparseCore 0:
  188.9 39.1 all-gather.1

commit v21 on v20

--- a/solution.py
+++ b/solution.py
@@ -137,21 +137,19 @@
     gate, due = due, slot(2, due)
     use(2, due, [])
     theirs[1] = rows_for_other(1, gate)
-    due += [fetch(1, 3, gate), theirs[1]]
+    due += [fetch(1, 3, gate), theirs[1]] + rotate(groups[0][:1], evens[0][:1])
 
     gate, due = due, slot(3, due)
     use(3, due, [])
     rotate(groups[1], after(evens[1], gate))
     passed_in = pass_on(0)
-    due.append(passed_in)
-    rotate(groups[0][:1], after(evens[0][:1], gate))
+    due += [passed_in] + rotate(groups[0][1:], after(evens[0][1:], gate))
 
     gate, due = due, slot(4, due)
     in_from_behind = send_ahead(0, passed_in, gate)
     rotate(groups[2], after(evens[2], gate))
     in_from_ahead = send_behind(0)
     passed_out = pass_on(1)
-    rotate(groups[0][1:], after(evens[0][1:], passed_out))
     use(4, due, rotated[0, 3])
     rotate(groups[3], evens[3])
     begun = [rotated[1, 2], halves[1, 1], halves[1, 3]]

time: 259 us -> 271 us (1.046)
  waiting for transfers between devices: 141 us -> 152 us
  matrix products: 39.4 us -> 44.9 us
  starting transfers between devices: 32.4 us -> 28.6 us
    ppermute x20, waiting for transfers between devices: 75 us -> 86.2 us  [swap(): lax.ppermute(block, 'tensor', [(j, j ^ bit) for j in range(X + Y + CORE +...]
    dot_general x15 -> x16, matrix products: 28.8 us -> 36.2 us  [dot(): return jnp.dot(a, b, preferred_element_type=jnp.float32)]
    ppermute x20, starting transfers between devices: 13.5 us -> 10.4 us  [swap(): lax.ppermute(block, 'tensor', [(j, j ^ bit) for j in range(X + Y + CORE +...]
    unnamed x92 -> x126, local copies, waits for them, and re-layouts: 7.07 us -> 7.2 us
  transfers between devices with their start and end apart: 33 -> 33, of which waited for: 17 -> 18; matrix products, arithmetic and copies ran while one was open for 17% -> 19% of each run, Pallas kernels for 0% -> 0%
where the time goes in v21:
time: 271 us; the launch traced here: 267 us
  waiting for transfers between devices  152 us (56%)
  matrix products  44.9 us (17%)
  starting transfers between devices  28.6 us (11%)
  local copies, waits for them, and re-layouts  19.6 us (7%)
  between operations  15.5 us (6%)
  other arithmetic  6.35 us (2%)
    ppermute x20, waiting for transfers between devices, swap(): lax.ppermute(block, 'tensor', [(j, j ^ bit) for j in range(X + Y + CORE +...  86.2 us
    ppermute x12, waiting for transfers between devices, shift(): return lax.ppermute(block, 'dp', [(z, (z + by) % n) for z in range(n)])  66.2 us
    dot_general x16, matrix products, dot(): return jnp.dot(a, b, preferred_element_type=jnp.float32)  36.2 us
    ppermute x12, starting transfers between devices, shift(): return lax.ppermute(block, 'dp', [(z, (z + by) % n) for z in range(n)])  18.2 us
    ppermute x20, starting transfers between devices, swap(): lax.ppermute(block, 'tensor', [(j, j ^ bit) for j in range(X + Y + CORE +...  10.4 us
    dot_general x1, matrix products, product_and_divide(): lax.dot_general(rot_out, all_rot_in, contract, preferred_element_type=jnp...  8.69 us
    unnamed x126, local copies, waits for them, and re-layouts  7.2 us
  transfers between devices with their start and end apart: 33, of which 18 were waited for; matrix products, arithmetic and copies ran while one was open for 19% of the time, Pallas kernels for 0%

profile of v21, /device:TPU:16, one launch (start us, length us, event | category | flops | bytes accessed | tf_op | source)
XLA Modules:
  0.0 267.4 jit_solution(7085236295467942260)
XLA Ops:
  13.0 12.7 %collective-permute-done.2 = bf16[512,512]{1,0:T(8,128)(2,1)S(1)} collective-permute-done((bf16[512,512]{1,0:T(8,128)(2,1)S(1)}, bf16[512,512]{1,0:T(8,128)(2,1)S(1)}, u32[]{:S(2)}, u32[]{:S(2)}) %collective-permute-start.2) | collective-permute-done | bytes 524320 | tf_op jit(solution)/shard_map/ppermute | solution.py:44
  26.1 8.3 %collective-permute-done = bf16[1024,512]{1,0:T(8,128)(2,1)S(1)} collective-permute-done((bf16[1024,512]{1,0:T(8,128)(2,1)S(1)}, bf16[1024,512]{1,0:T(8,128)(2,1)S(1)}, u32[]{:S(2)}, u32[]{:S(2)}) %collective-permute-start) | collective-permute-done | bytes 1048608 | tf_op jit(solution)/shard_map/ppermute | solution.py:40
  36.6 2.8 %collective-permute-done.3 = bf16[512,512]{1,0:T(8,128)(2,1)S(1)} collective-permute-done((bf16[512,512]{1,0:T(8,128)(2,1)S(1)}, bf16[512,512]{1,0:T(8,128)(2,1)S(1)}, u32[]{:S(2)}, u32[]{:S(2)}) %collective-permute-start.3) | collective-permute-done | bytes 524320 | tf_op jit(solution)/shard_map/ppermute | solution.py:44
  41.3 3.5 %collective-permute-start.7 = (bf16[512,512]{1,0:T(8,128)(2,1)S(1)}, bf16[512,512]{1,0:T(8,128)(2,1)S(1)}, u32[]{:S(2)}, u32[]{:S(2)}) collective-permute-start(bf16[512,512]{1,0:T(8,128)(2,1)S(1)} %bitcast.51), channel_id=1, source_target_pairs={{0,8},{8,16},{16,24},{24,0},{1,9},{9,17},{17,25},{25,1},{2,10},{10... | collective-permute-start | bytes 1572872 | tf_op jit(solution)/shard_map/ppermute | solution.py:44
  44.9 12.8 %collective-permute-done.8 = bf16[512,512]{1,0:T(8,128)(2,1)S(1)} collective-permute-done((bf16[512,512]{1,0:T(8,128)(2,1)S(1)}, bf16[512,512]{1,0:T(8,128)(2,1)S(1)}, u32[]{:S(2)}, u32[]{:S(2)}) %collective-permute-start.8) | collective-permute-done | bytes 524320 | tf_op jit(solution)/shard_map/ppermute | solution.py:44
  57.7 16.6 %collective-permute-done.5 = bf16[1536,512]{1,0:T(8,128)(2,1)S(1)} collective-permute-done((bf16[1536,512]{1,0:T(8,128)(2,1)S(1)}, bf16[1536,512]{1,0:T(8,128)(2,1)S(1)}, u32[]{:S(2)}, u32[]{:S(2)}) %collective-permute-start.5) | collective-permute-done | bytes 1572896 | tf_op jit(solution)/shard_map/ppermute | solution.py:40
  75.5 2.2 fusion.16
  78.9 1.9 pad_maximum_fusion.16
  84.7 1.9 copy-done
  86.8 3.3 %collective-permute-start.12 = (bf16[512,512]{1,0:T(8,128)(2,1)S(1)}, bf16[512,512]{1,0:T(8,128)(2,1)S(1)}, u32[]{:S(2)}, u32[]{:S(2)}) collective-permute-start(bf16[512,512]{1,0:T(8,128)(2,1)S(1)} %bitcast.47), channel_id=1, source_target_pairs={{0,8},{8,16},{16,24},{24,0},{1,9},{9,17},{17,25},{25,1},{2,10},{10... | collective-permute-start | bytes 1572872 | tf_op jit(solution)/shard_map/ppermute | solution.py:44
  91.7 3.3 %add_convert_fusion = bf16[512,512]{1,0:T(8,128)(2,1)} fusion(f32[512,512]{1,0:T(8,128)} %collective-permute-done.14, bf16[512,512]{1,0:T(8,128)(2,1)S(1)} %copy-done.30, bf16[512,512]{1,0:T(8,128)(2,1)S(1)} %copy-done.52, bf16[512,512]{1,0:T(8,128)(2,1)S(1)} %copy-done.10, bf16[512,512]{1,0:T(8,128)(2,1)S(1)} %bitcast.53, ...), kind=kOutput, calls=%fused_computation.43 | convolution fusion | flops 1091043328 | bytes 5767168 | tf_op jit(solution)/shard_map/dot_general | solution.py:22
  94.9 23.0 %collective-permute-done.10 = bf16[1536,512]{1,0:T(8,128)(2,1)} collective-permute-done((bf16[1536,512]{1,0:T(8,128)(2,1)}, bf16[1536,512]{1,0:T(8,128)(2,1)}, u32[]{:S(2)}, u32[]{:S(2)}) %collective-permute-start.10) | collective-permute-done | bytes 1572896 | tf_op jit(solution)/shard_map/ppermute | solution.py:40
  129.8 2.2 fusion.36
  133.3 3.5 %collective-permute-start.19 = (bf16[512,512]{1,0:T(8,128)(2,1)S(1)}, bf16[512,512]{1,0:T(8,128)(2,1)S(1)}, u32[]{:S(2)}, u32[]{:S(2)}) collective-permute-start(bf16[512,512]{1,0:T(8,128)(2,1)S(1)} %fusion.2), channel_id=1, source_target_pairs={{0,8},{8,16},{16,24},{24,0},{1,9},{9,17},{17,25},{25,1},{2,10},{10... | collective-permute-start | bytes 1572872 | tf_op jit(solution)/shard_map/ppermute | solution.py:44
  136.8 2.1 fusion.1
  138.9 26.0 %collective-permute-done.16 = bf16[1536,512]{1,0:T(8,128)(2,1)S(1)} collective-permute-done((bf16[1536,512]{1,0:T(8,128)(2,1)S(1)}, bf16[1536,512]{1,0:T(8,128)(2,1)S(1)}, u32[]{:S(2)}, u32[]{:S(2)}) %collective-permute-start.16) | collective-permute-done | bytes 1572896 | tf_op jit(solution)/shard_map/ppermute | solution.py:40
  169.3 2.2 fusion.34
  172.9 3.4 %fusion.8 = bf16[512,512]{1,0:T(8,128)(2,1)S(1)} fusion(bf16[512,512]{1,0:T(8,128)(2,1)} %copy-done.61, f32[512,512]{1,0:T(8,128)} %collective-permute-done.30, bf16[512,2048]{1,0:T(8,128)(2,1)S(1)} %copy-done.3, pred[]{:T(512)S(6)} %eq.19, bf16[512,512]{1,0:T(8,128)(2,1)} %copy-done.47, bf16[512,512]{1,0:T(8,128)(2,1)} %copy-done.49, ...), kind=kOutput, calls=%fused_computation.40 | convolution fusion | flops 1082916864 | bytes 6291457 | tf_op jit(solution)/shard_map/dot_general | solution.py:22
  176.3 3.1 %collective-permute-start.31 = (bf16[512,512]{1,0:T(8,128)(2,1)S(1)}, bf16[512,512]{1,0:T(8,128)(2,1)S(1)}, u32[]{:S(2)}, u32[]{:S(2)}) collective-permute-start(bf16[512,512]{1,0:T(8,128)(2,1)S(1)} %fusion.8), channel_id=1, source_target_pairs={{0,8},{8,16},{16,24},{24,0},{1,9},{9,17},{17,25},{25,1},{2,10},{10... | collective-permute-start | bytes 1572872 | tf_op jit(solution)/shard_map/ppermute | solution.py:44
  179.5 1.7 collective-permute-start.20
  183.0 2.6 fusion.3
  185.6 8.1 %collective-permute-done.20 = bf16[512,512]{1,0:T(8,128)(2,1)S(1)} collective-permute-done((bf16[512,512]{1,0:T(8,128)(2,1)S(1)}, bf16[512,512]{1,0:T(8,128)(2,1)S(1)}, u32[]{:S(2)}, u32[]{:S(2)}) %collective-permute-start.20) | collective-permute-done | bytes 524320 | tf_op jit(solution)/shard_map/ppermute | solution.py:40
  195.0 2.2 fusion.15
  197.2 2.2 fusion.14
  199.5 2.1 fusion.6
  204.5 1.7 collective-permute-start.27
  207.1 12.1 %collective-permute-done.27 = bf16[512,512]{1,0:T(8,128)(2,1)} collective-permute-done((bf16[512,512]{1,0:T(8,128)(2,1)}, bf16[512,512]{1,0:T(8,128)(2,1)}, u32[]{:S(2)}, u32[]{:S(2)}) %collective-permute-start.27) | collective-permute-done | bytes 524320 | tf_op jit(solution)/shard_map/ppermute | solution.py:44
  219.1 4.2 %fusion.9 = bf16[512,512]{1,0:T(8,128)(2,1)} fusion(bf16[512,512]{1,0:T(8,128)(2,1)} %collective-permute-done.27, f32[512,512]{1,0:T(8,128)} %collective-permute-done.25, pred[]{:T(512)S(6)} %eq.17, bf16[512,512]{1,0:T(8,128)(2,1)} %copy-done.60, bf16[512,512]{1,0:T(8,128)(2,1)S(1)} %copy-done.28, bf16[512,512]{1,0:T(8,128)(2,1)S(1)} %copy-done.27, ...), kind=kOutput, calls=%fused_computation.41 | convolution fusion | flops 1091305472 | bytes 6291457 | tf_op jit(solution)/shard_map/dot_general | solution.py:22
  225.0 2.5 fusion.4
  227.9 9.1 %collective-permute-done.28 = bf16[512,512]{1,0:T(8,128)(2,1)S(1)} collective-permute-done((bf16[512,512]{1,0:T(8,128)(2,1)}, bf16[512,512]{1,0:T(8,128)(2,1)S(1)}, u32[]{:S(2)}, u32[]{:S(2)}) %collective-permute-start.28) | collective-permute-done | bytes 524320 | tf_op jit(solution)/shard_map/ppermute | solution.py:44
  237.0 14.8 %collective-permute-done.24 = bf16[512,512]{1,0:T(8,128)(2,1)S(1)} collective-permute-done((bf16[512,512]{1,0:T(8,128)(2,1)S(1)}, bf16[512,512]{1,0:T(8,128)(2,1)S(1)}, u32[]{:S(2)}, u32[]{:S(2)}) %collective-permute-start.24) | collective-permute-done | bytes 524320 | tf_op jit(solution)/shard_map/ppermute | solution.py:44
  251.9 8.7 %fusion = bf16[1,512,4096]{2,1,0:T(8,128)(2,1)} fusion(bf16[512,4096]{1,0:T(8,128)(2,1)} %param.11, bf16[512,4096]{1,0:T(8,128)(2,1)} %all-gather.2.cloned.1.call-done, bf16[512,512]{1,0:T(8,128)(2,1)S(1)} %copy-done.62, bf16[512,512]{1,0:T(8,128)(2,1)S(1)} %collective-permute-done.24, bf16[512,512]{1,0:T(8,128)(2,1)S(1)} %collective-permute-done.28, ...), kind=kOutput, calls=%fused_computation.1 | convolution fusion | flops 2158493696 | bytes 14155778 | tf_op jit(solution)/shard_map/dot_general | solution.py:13
  (202 shorter events, 45.0 us)
Async XLA Ops:
  6.5 245.3 %all-gather.2.cloned.1.call-start = ((), (), s32[]{:S(2)}) async-start(), calls=%async_computation | async-start | bytes 4718592 | tf_op jit(solution)/shard_map/all_gather | solution.py:157
  8.4 31.9 %collective-permute-start.4 = (bf16[2048,512]{1,0:T(8,128)(2,1)S(1)}, bf16[2048,512]{1,0:T(8,128)(2,1)S(1)}, u32[]{:S(2)}, u32[]{:S(2)}) collective-permute-start(bf16[2048,512]{1,0:T(8,128)(2,1)S(1)} %pad_maximum_fusion), channel_id=1, source_target_pairs={{0,1},{1,0},{2,3},{3,2},{4,5},{5,4},{6,7},{7,6},{8,9},{9,8},{10,11... | collective-permute-start | bytes 6291464 | tf_op jit(solution)/shard_map/ppermute | solution.py:40
  9.5 25.0 %collective-permute-start = (bf16[1024,512]{1,0:T(8,128)(2,1)S(1)}, bf16[1024,512]{1,0:T(8,128)(2,1)S(1)}, u32[]{:S(2)}, u32[]{:S(2)}) collective-permute-start(bf16[1024,512]{1,0:T(8,128)(2,1)S(1)} %pad_maximum_fusion.24), channel_id=1, source_target_pairs={{0,2},{1,3},{2,0},{3,1},{4,6},{5,7},{6,4},{7,5},{8,10},{9,11},{10,... | collective-permute-start | bytes 3145736 | tf_op jit(solution)/shard_map/ppermute | solution.py:40
  11.0 24.6 %collective-permute-start.1 = (bf16[1024,512]{1,0:T(8,128)(2,1)S(1)}, bf16[1024,512]{1,0:T(8,128)(2,1)S(1)}, u32[]{:S(2)}, u32[]{:S(2)}) collective-permute-start(bf16[1024,512]{1,0:T(8,128)(2,1)S(1)} %pad_maximum_fusion.24), channel_id=1, source_target_pairs={{0,4},{1,5},{2,6},{3,7},{4,0},{5,1},{6,2},{7,3},{8,12},{9,13},{10,... | collective-permute-start | bytes 3145736 | tf_op jit(solution)/shard_map/ppermute | solution.py:40
  12.5 13.1 %collective-permute-start.2 = (bf16[512,512]{1,0:T(8,128)(2,1)S(1)}, bf16[512,512]{1,0:T(8,128)(2,1)S(1)}, u32[]{:S(2)}, u32[]{:S(2)}) collective-permute-start(bf16[512,512]{1,0:T(8,128)(2,1)S(1)} %bitcast.50), channel_id=1, source_target_pairs={{0,24},{8,0},{16,8},{24,16},{1,25},{9,1},{17,9},{25,17},{2,26},{10... | collective-permute-start | bytes 1572872 | tf_op jit(solution)/shard_map/ppermute | solution.py:44
  25.6 13.8 %collective-permute-start.3 = (bf16[512,512]{1,0:T(8,128)(2,1)S(1)}, bf16[512,512]{1,0:T(8,128)(2,1)S(1)}, u32[]{:S(2)}, u32[]{:S(2)}) collective-permute-start(bf16[512,512]{1,0:T(8,128)(2,1)S(1)} %collective-permute-done.2), channel_id=1, source_target_pairs={{0,24},{8,0},{16,8},{24,16},{1,25},{9,1},{17,9},{25,17},{2,26},{10... | collective-permute-start | bytes 1572872 | tf_op jit(solution)/shard_map/ppermute | solution.py:44
  40.3 34.0 %collective-permute-start.5 = (bf16[1536,512]{1,0:T(8,128)(2,1)S(1)}, bf16[1536,512]{1,0:T(8,128)(2,1)S(1)}, u32[]{:S(2)}, u32[]{:S(2)}) collective-permute-start(bf16[1536,512]{1,0:T(8,128)(2,1)S(1)} %get-tuple-element.41), channel_id=1, source_target_pairs={{0,2},{1,3},{2,0},{3,1},{4,6},{5,7},{6,4},{7,5},{8,10},{9,11},{10,... | collective-permute-start | bytes 4718600 | tf_op jit(solution)/shard_map/ppermute | solution.py:40
  40.8 33.7 %collective-permute-start.6 = (bf16[1536,512]{1,0:T(8,128)(2,1)S(1)}, bf16[1536,512]{1,0:T(8,128)(2,1)S(1)}, u32[]{:S(2)}, u32[]{:S(2)}) collective-permute-start(bf16[1536,512]{1,0:T(8,128)(2,1)S(1)} %get-tuple-element.42), channel_id=1, source_target_pairs={{0,4},{1,5},{2,6},{3,7},{4,0},{5,1},{6,2},{7,3},{8,12},{9,13},{10,... | collective-permute-start | bytes 4718600 | tf_op jit(solution)/shard_map/ppermute | solution.py:40
  41.3 16.4 %collective-permute-start.8 = (bf16[512,512]{1,0:T(8,128)(2,1)S(1)}, bf16[512,512]{1,0:T(8,128)(2,1)S(1)}, u32[]{:S(2)}, u32[]{:S(2)}) collective-permute-start(bf16[512,512]{1,0:T(8,128)(2,1)S(1)} %bitcast.46), channel_id=1, source_target_pairs={{0,24},{8,0},{16,8},{24,16},{1,25},{9,1},{17,9},{25,17},{2,26},{10... | collective-permute-start | bytes 1572872 | tf_op jit(solution)/shard_map/ppermute | solution.py:44
  41.3 37.5 %collective-permute-start.7 = (bf16[512,512]{1,0:T(8,128)(2,1)S(1)}, bf16[512,512]{1,0:T(8,128)(2,1)S(1)}, u32[]{:S(2)}, u32[]{:S(2)}) collective-permute-start(bf16[512,512]{1,0:T(8,128)(2,1)S(1)} %bitcast.51), channel_id=1, source_target_pairs={{0,8},{8,16},{16,24},{24,0},{1,9},{9,17},{17,25},{25,1},{2,10},{10... | collective-permute-start | bytes 1572872 | tf_op jit(solution)/shard_map/ppermute | solution.py:44
  57.7 21.2 %collective-permute-start.9 = (bf16[512,512]{1,0:T(8,128)(2,1)S(1)}, bf16[512,512]{1,0:T(8,128)(2,1)S(1)}, u32[]{:S(2)}, u32[]{:S(2)}) collective-permute-start(bf16[512,512]{1,0:T(8,128)(2,1)S(1)} %collective-permute-done.8), channel_id=1, source_target_pairs={{0,24},{8,0},{16,8},{24,16},{1,25},{9,1},{17,9},{25,17},{2,26},{10... | collective-permute-start | bytes 1572872 | tf_op jit(solution)/shard_map/ppermute | solution.py:44
  77.7 12.8 %collective-permute-start.14 = (f32[512,512]{1,0:T(8,128)}, f32[512,512]{1,0:T(8,128)}, u32[]{:S(2)}, u32[]{:S(2)}) collective-permute-start(f32[512,512]{1,0:T(8,128)} %fusion.16), channel_id=1, source_target_pairs={{0,1},{1,0},{2,3},{3,2},{4,5},{5,4},{6,7},{7,6},{8,9},{9,8},{10,11... | collective-permute-start | bytes 3145736 | tf_op jit(solution)/shard_map/ppermute | solution.py:40
  80.8 37.1 %collective-permute-start.10 = (bf16[1536,512]{1,0:T(8,128)(2,1)}, bf16[1536,512]{1,0:T(8,128)(2,1)}, u32[]{:S(2)}, u32[]{:S(2)}) collective-permute-start(bf16[1536,512]{1,0:T(8,128)(2,1)} %get-tuple-element.48), channel_id=1, source_target_pairs={{0,2},{1,3},{2,0},{3,1},{4,6},{5,7},{6,4},{7,5},{8,10},{9,11},{10,... | collective-permute-start | bytes 4718600 | tf_op jit(solution)/shard_map/ppermute | solution.py:40
  82.3 36.8 %collective-permute-start.11 = (bf16[1536,512]{1,0:T(8,128)(2,1)}, bf16[1536,512]{1,0:T(8,128)(2,1)}, u32[]{:S(2)}, u32[]{:S(2)}) collective-permute-start(bf16[1536,512]{1,0:T(8,128)(2,1)} %get-tuple-element.49), channel_id=1, source_target_pairs={{0,4},{1,5},{2,6},{3,7},{4,0},{5,1},{6,2},{7,3},{8,12},{9,13},{10,... | collective-permute-start | bytes 4718600 | tf_op jit(solution)/shard_map/ppermute | solution.py:40
  84.6 39.0 %collective-permute-start.13 = (bf16[2048,512]{1,0:T(8,128)(2,1)S(1)}, bf16[2048,512]{1,0:T(8,128)(2,1)S(1)}, u32[]{:S(2)}, u32[]{:S(2)}) collective-permute-start(bf16[2048,512]{1,0:T(8,128)(2,1)S(1)} %pad_maximum_fusion.2), channel_id=1, source_target_pairs={{0,1},{1,0},{2,3},{3,2},{4,5},{5,4},{6,7},{7,6},{8,9},{9,8},{10,11... | collective-permute-start | bytes 6291464 | tf_op jit(solution)/shard_map/ppermute | solution.py:40
  86.8 36.8 %collective-permute-start.12 = (bf16[512,512]{1,0:T(8,128)(2,1)S(1)}, bf16[512,512]{1,0:T(8,128)(2,1)S(1)}, u32[]{:S(2)}, u32[]{:S(2)}) collective-permute-start(bf16[512,512]{1,0:T(8,128)(2,1)S(1)} %bitcast.47), channel_id=1, source_target_pairs={{0,8},{8,16},{16,24},{24,0},{1,9},{9,17},{17,25},{25,1},{2,10},{10... | collective-permute-start | bytes 1572872 | tf_op jit(solution)/shard_map/ppermute | solution.py:44
  128.0 8.8 %collective-permute-start.15 = (f32[512,512]{1,0:T(8,128)S(1)}, f32[512,512]{1,0:T(8,128)S(1)}, u32[]{:S(2)}, u32[]{:S(2)}) collective-permute-start(f32[512,512]{1,0:T(8,128)S(1)} %fusion.32), channel_id=1, source_target_pairs={{0,1},{1,0},{2,3},{3,2},{4,5},{5,4},{6,7},{7,6},{8,9},{9,8},{10,11... | collective-permute-start | bytes 3145736 | tf_op jit(solution)/shard_map/ppermute | solution.py:40
  128.5 36.4 %collective-permute-start.16 = (bf16[1536,512]{1,0:T(8,128)(2,1)S(1)}, bf16[1536,512]{1,0:T(8,128)(2,1)S(1)}, u32[]{:S(2)}, u32[]{:S(2)}) collective-permute-start(bf16[1536,512]{1,0:T(8,128)(2,1)S(1)} %get-tuple-element.55), channel_id=1, source_target_pairs={{0,2},{1,3},{2,0},{3,1},{4,6},{5,7},{6,4},{7,5},{8,10},{9,11},{10,... | collective-permute-start | bytes 4718600 | tf_op jit(solution)/shard_map/ppermute | solution.py:40
  129.1 36.1 %collective-permute-start.17 = (bf16[1536,512]{1,0:T(8,128)(2,1)S(1)}, bf16[1536,512]{1,0:T(8,128)(2,1)S(1)}, u32[]{:S(2)}, u32[]{:S(2)}) collective-permute-start(bf16[1536,512]{1,0:T(8,128)(2,1)S(1)} %get-tuple-element.56), channel_id=1, source_target_pairs={{0,4},{1,5},{2,6},{3,7},{4,0},{5,1},{6,2},{7,3},{8,12},{9,13},{10,... | collective-permute-start | bytes 4718600 | tf_op jit(solution)/shard_map/ppermute | solution.py:40
  132.0 40.8 %collective-permute-start.30 = (f32[512,512]{1,0:T(8,128)}, f32[512,512]{1,0:T(8,128)}, u32[]{:S(2)}, u32[]{:S(2)}) collective-permute-start(f32[512,512]{1,0:T(8,128)} %fusion.36), channel_id=1, source_target_pairs={{0,1},{1,0},{2,3},{3,2},{4,5},{5,4},{6,7},{7,6},{8,9},{9,8},{10,11... | collective-permute-start | bytes 3145736 | tf_op jit(solution)/shard_map/ppermute | solution.py:40
  133.3 36.0 %collective-permute-start.19 = (bf16[512,512]{1,0:T(8,128)(2,1)S(1)}, bf16[512,512]{1,0:T(8,128)(2,1)S(1)}, u32[]{:S(2)}, u32[]{:S(2)}) collective-permute-start(bf16[512,512]{1,0:T(8,128)(2,1)S(1)} %fusion.2), channel_id=1, source_target_pairs={{0,8},{8,16},{16,24},{24,0},{1,9},{9,17},{17,25},{25,1},{2,10},{10... | collective-permute-start | bytes 1572872 | tf_op jit(solution)/shard_map/ppermute | solution.py:44
  171.5 11.4 %collective-permute-start.22 = (f32[512,512]{1,0:T(8,128)}, f32[512,512]{1,0:T(8,128)}, u32[]{:S(2)}, u32[]{:S(2)}) collective-permute-start(f32[512,512]{1,0:T(8,128)} %fusion.34), channel_id=1, source_target_pairs={{0,1},{1,0},{2,3},{3,2},{4,5},{5,4},{6,7},{7,6},{8,9},{9,8},{10,11... | collective-permute-start | bytes 3145736 | tf_op jit(solution)/shard_map/ppermute | solution.py:40
  176.3 26.4 %collective-permute-start.31 = (bf16[512,512]{1,0:T(8,128)(2,1)S(1)}, bf16[512,512]{1,0:T(8,128)(2,1)S(1)}, u32[]{:S(2)}, u32[]{:S(2)}) collective-permute-start(bf16[512,512]{1,0:T(8,128)(2,1)S(1)} %fusion.8), channel_id=1, source_target_pairs={{0,8},{8,16},{16,24},{24,0},{1,9},{9,17},{17,25},{25,1},{2,10},{10... | collective-permute-start | bytes 1572872 | tf_op jit(solution)/shard_map/ppermute | solution.py:44
  179.5 14.3 %collective-permute-start.20 = (bf16[512,512]{1,0:T(8,128)(2,1)S(1)}, bf16[512,512]{1,0:T(8,128)(2,1)S(1)}, u32[]{:S(2)}, u32[]{:S(2)}) collective-permute-start(bf16[512,512]{1,0:T(8,128)(2,1)S(1)} %copy-done.25), channel_id=1, source_target_pairs={{0,2},{1,3},{2,0},{3,1},{4,6},{5,7},{6,4},{7,5},{8,10},{9,11},{10,... | collective-permute-start | bytes 1572872 | tf_op jit(solution)/shard_map/ppermute | solution.py:40
  181.2 13.8 %collective-permute-start.21 = (bf16[512,512]{1,0:T(8,128)(2,1)S(1)}, bf16[512,512]{1,0:T(8,128)(2,1)S(1)}, u32[]{:S(2)}, u32[]{:S(2)}) collective-permute-start(bf16[512,512]{1,0:T(8,128)(2,1)S(1)} %copy-done.26), channel_id=1, source_target_pairs={{0,4},{1,5},{2,6},{3,7},{4,0},{5,1},{6,2},{7,3},{8,12},{9,13},{10,... | collective-permute-start | bytes 1572872 | tf_op jit(solution)/shard_map/ppermute | solution.py:40
  182.8 16.6 %collective-permute-start.26 = (f32[512,512]{1,0:T(8,128)S(1)}, f32[512,512]{1,0:T(8,128)S(1)}, u32[]{:S(2)}, u32[]{:S(2)}) collective-permute-start(f32[512,512]{1,0:T(8,128)S(1)} %fusion.35), channel_id=1, source_target_pairs={{0,1},{1,0},{2,3},{3,2},{4,5},{5,4},{6,7},{7,6},{8,9},{9,8},{10,11... | collective-permute-start | bytes 3145736 | tf_op jit(solution)/shard_map/ppermute | solution.py:40
  185.5 18.0 %collective-permute-start.29 = (bf16[512,512]{1,0:T(8,128)(2,1)S(1)}, bf16[512,512]{1,0:T(8,128)(2,1)S(1)}, u32[]{:S(2)}, u32[]{:S(2)}) collective-permute-start(bf16[512,512]{1,0:T(8,128)(2,1)S(1)} %fusion.3), channel_id=1, source_target_pairs={{0,24},{8,0},{16,8},{24,16},{1,25},{9,1},{17,9},{25,17},{2,26},{10... | collective-permute-start | bytes 1572872 | tf_op jit(solution)/shard_map/ppermute | solution.py:44
  204.4 14.7 %collective-permute-start.25 = (f32[512,512]{1,0:T(8,128)}, f32[512,512]{1,0:T(8,128)}, u32[]{:S(2)}, u32[]{:S(2)}) collective-permute-start(f32[512,512]{1,0:T(8,128)} %fusion.14), channel_id=1, source_target_pairs={{0,1},{1,0},{2,3},{3,2},{4,5},{5,4},{6,7},{7,6},{8,9},{9,8},{10,11... | collective-permute-start | bytes 3145736 | tf_op jit(solution)/shard_map/ppermute | solution.py:40
  204.5 14.6 %collective-permute-start.27 = (bf16[512,512]{1,0:T(8,128)(2,1)}, bf16[512,512]{1,0:T(8,128)(2,1)}, u32[]{:S(2)}, u32[]{:S(2)}) collective-permute-start(bf16[512,512]{1,0:T(8,128)(2,1)} %fusion.6), channel_id=1, source_target_pairs={{0,8},{8,16},{16,24},{24,0},{1,9},{9,17},{17,25},{25,1},{2,10},{10... | collective-permute-start | bytes 1572872 | tf_op jit(solution)/shard_map/ppermute | solution.py:44
  206.2 18.8 %collective-permute-start.23 = (f32[512,512]{1,0:T(8,128)}, f32[512,512]{1,0:T(8,128)}, u32[]{:S(2)}, u32[]{:S(2)}) collective-permute-start(f32[512,512]{1,0:T(8,128)} %fusion.15), channel_id=1, source_target_pairs={{0,1},{1,0},{2,3},{3,2},{4,5},{5,4},{6,7},{7,6},{8,9},{9,8},{10,11... | collective-permute-start | bytes 3145736 | tf_op jit(solution)/shard_map/ppermute | solution.py:40
  223.3 13.7 %collective-permute-start.28 = (bf16[512,512]{1,0:T(8,128)(2,1)}, bf16[512,512]{1,0:T(8,128)(2,1)S(1)}, u32[]{:S(2)}, u32[]{:S(2)}) collective-permute-start(bf16[512,512]{1,0:T(8,128)(2,1)} %fusion.9), channel_id=1, source_target_pairs={{0,8},{8,16},{16,24},{24,0},{1,9},{9,17},{17,25},{25,1},{2,10},{10... | collective-permute-start | bytes 1572872 | tf_op jit(solution)/shard_map/ppermute | solution.py:44
  227.5 24.4 %collective-permute-start.24 = (bf16[512,512]{1,0:T(8,128)(2,1)S(1)}, bf16[512,512]{1,0:T(8,128)(2,1)S(1)}, u32[]{:S(2)}, u32[]{:S(2)}) collective-permute-start(bf16[512,512]{1,0:T(8,128)(2,1)S(1)} %fusion.4), channel_id=1, source_target_pairs={{0,24},{8,0},{16,8},{24,16},{1,25},{9,1},{17,9},{25,17},{2,26},{10... | collective-permute-start | bytes 1572872 | tf_op jit(solution)/shard_map/ppermute | solution.py:44
  (64 other events, 640.2 us)
Sparse Core Ops, SparseCore 0:
  204.5 37.6 all-gather.1

commit v22 on v19

--- a/solution.py
+++ b/solution.py
@@ -137,8 +137,7 @@
     gate, due = due, slot(3, due)
     rotate(groups[1], after(evens[1], gate))
     passed_in = pass_on(0)
-    due.append(passed_in)
-    rotate(groups[0], after(evens[0], gate))
+    due += [passed_in] + rotate(groups[0][:1], after(evens[0][:1], gate))
 
     gate, due = due, slot(4, due)
     in_from_behind = send_ahead(0, passed_in, gate)
@@ -149,6 +148,8 @@
     begun = [rotated[1, 2], halves[1, 1], halves[1, 3]]
     rot_in = after(keep(0, in_from_behind, in_from_ahead), begun)
     all_rot_in = lax.all_gather(rot_in, "tensor", axis=1, tiled=True)
+    rotate(groups[0][1:], after(evens[0][1:], [rotated[1, 1], rotated[1, 3]]))
+    rotated[1, 0] = after(rotated[1, 0], [])
     rot_out = keep(1, send_ahead(1, passed_out, []), send_behind(1))
     return product_and_divide(rot_out, all_rot_in, eig_lambda, tokens)
 

time: 256 us -> 254 us (level)
    ppermute x12, waiting for transfers between devices: 62.6 us -> 56.3 us  [shift(): return lax.ppermute(block, 'dp', [(z, (z + by) % n) for z in range(n)])]
    ppermute x20, waiting for transfers between devices: 75.1 us -> 80 us  [swap(): lax.ppermute(block, 'tensor', [(j, j ^ bit) for j in range(X + Y + CORE +...]
    dot_general x15 -> x16, matrix products: 31.2 us -> 33.9 us  [dot(): return jnp.dot(a, b, preferred_element_type=jnp.float32)]
    unnamed x70 -> x68, local copies, waits for them, and re-layouts: 6.22 us -> 4.83 us
  transfers between devices with their start and end apart: 33 -> 33, of which waited for: 16 -> 18; matrix products, arithmetic and copies ran while one was open for 17% -> 19% of each run, Pallas kernels for 0% -> 0%
where the time goes in v22:
time: 254 us; the launch traced here: 250 us
  waiting for transfers between devices  136 us (54%)
  matrix products  42.5 us (17%)
  starting transfers between devices  31.6 us (12%)
  local copies, waits for them, and re-layouts  15.8 us (6%)
  between operations  15.3 us (6%)
  other arithmetic  8.8 us (3%)
    ppermute x20, waiting for transfers between devices, swap(): lax.ppermute(block, 'tensor', [(j, j ^ bit) for j in range(X + Y + CORE +...  80 us
    ppermute x12, waiting for transfers between devices, shift(): return lax.ppermute(block, 'dp', [(z, (z + by) % n) for z in range(n)])  56.3 us
    dot_general x16, matrix products, dot(): return jnp.dot(a, b, preferred_element_type=jnp.float32)  33.9 us
    ppermute x12, starting transfers between devices, shift(): return lax.ppermute(block, 'dp', [(z, (z + by) % n) for z in range(n)])  19.7 us
    ppermute x20, starting transfers between devices, swap(): lax.ppermute(block, 'tensor', [(j, j ^ bit) for j in range(X + Y + CORE +...  11.9 us
    dot_general x1, matrix products, product_and_divide(): lax.dot_general(rot_out, all_rot_in, contract, preferred_element_type=jnp...  8.66 us
  transfers between devices with their start and end apart: 33, of which 18 were waited for; matrix products, arithmetic and copies ran while one was open for 19% of the time, Pallas kernels for 0%

profile of v22, /device:TPU:16, one launch (start us, length us, event | category | flops | bytes accessed | tf_op | source)
XLA Modules:
  0.0 250.3 jit_solution(7320234592386609376)
XLA Ops:
  6.5 1.7 constant_dynamic-slice_fusion.8
  9.5 1.6 collective-permute-start
  13.0 12.7 %collective-permute-done.2 = bf16[512,512]{1,0:T(8,128)(2,1)S(1)} collective-permute-done((bf16[512,512]{1,0:T(8,128)(2,1)S(1)}, bf16[512,512]{1,0:T(8,128)(2,1)S(1)}, u32[]{:S(2)}, u32[]{:S(2)}) %collective-permute-start.2) | collective-permute-done | bytes 524320 | tf_op jit(solution)/shard_map/ppermute | solution.py:44
  26.1 8.3 %collective-permute-done = bf16[1024,512]{1,0:T(8,128)(2,1)S(1)} collective-permute-done((bf16[1024,512]{1,0:T(8,128)(2,1)S(1)}, bf16[1024,512]{1,0:T(8,128)(2,1)S(1)}, u32[]{:S(2)}, u32[]{:S(2)}) %collective-permute-start) | collective-permute-done | bytes 1048608 | tf_op jit(solution)/shard_map/ppermute | solution.py:40
  36.7 2.7 %collective-permute-done.3 = bf16[512,512]{1,0:T(8,128)(2,1)S(1)} collective-permute-done((bf16[512,512]{1,0:T(8,128)(2,1)S(1)}, bf16[512,512]{1,0:T(8,128)(2,1)S(1)}, u32[]{:S(2)}, u32[]{:S(2)}) %collective-permute-start.3) | collective-permute-done | bytes 524320 | tf_op jit(solution)/shard_map/ppermute | solution.py:44
  41.3 3.5 %collective-permute-start.8 = (bf16[512,512]{1,0:T(8,128)(2,1)S(1)}, bf16[512,512]{1,0:T(8,128)(2,1)S(1)}, u32[]{:S(2)}, u32[]{:S(2)}) collective-permute-start(bf16[512,512]{1,0:T(8,128)(2,1)S(1)} %bitcast.53), channel_id=1, source_target_pairs={{0,8},{8,16},{16,24},{24,0},{1,9},{9,17},{17,25},{25,1},{2,10},{10... | collective-permute-start | bytes 1572872 | tf_op jit(solution)/shard_map/ppermute | solution.py:44
  44.9 12.8 %collective-permute-done.7 = bf16[512,512]{1,0:T(8,128)(2,1)S(1)} collective-permute-done((bf16[512,512]{1,0:T(8,128)(2,1)S(1)}, bf16[512,512]{1,0:T(8,128)(2,1)S(1)}, u32[]{:S(2)}, u32[]{:S(2)}) %collective-permute-start.7) | collective-permute-done | bytes 524320 | tf_op jit(solution)/shard_map/ppermute | solution.py:44
  57.7 16.6 %collective-permute-done.5 = bf16[1536,512]{1,0:T(8,128)(2,1)S(1)} collective-permute-done((bf16[1536,512]{1,0:T(8,128)(2,1)S(1)}, bf16[1536,512]{1,0:T(8,128)(2,1)S(1)}, u32[]{:S(2)}, u32[]{:S(2)}) %collective-permute-start.5) | collective-permute-done | bytes 1572896 | tf_op jit(solution)/shard_map/ppermute | solution.py:40
  76.8 1.9 pad_maximum_fusion.16
  84.2 1.8 dynamic-slice_bitcast_fusion.7
  86.0 3.6 %collective-permute-start.12 = (bf16[512,512]{1,0:T(8,128)(2,1)S(1)}, bf16[512,512]{1,0:T(8,128)(2,1)S(1)}, u32[]{:S(2)}, u32[]{:S(2)}) collective-permute-start(bf16[512,512]{1,0:T(8,128)(2,1)S(1)} %bitcast.57), channel_id=1, source_target_pairs={{0,8},{8,16},{16,24},{24,0},{1,9},{9,17},{17,25},{25,1},{2,10},{10... | collective-permute-start | bytes 1572872 | tf_op jit(solution)/shard_map/ppermute | solution.py:44
  89.9 21.9 %collective-permute-done.10 = bf16[1536,512]{1,0:T(8,128)(2,1)} collective-permute-done((bf16[1536,512]{1,0:T(8,128)(2,1)}, bf16[1536,512]{1,0:T(8,128)(2,1)}, u32[]{:S(2)}, u32[]{:S(2)}) %collective-permute-start.10) | collective-permute-done | bytes 1572896 | tf_op jit(solution)/shard_map/ppermute | solution.py:40
  114.5 1.5 fusion.17
  126.4 3.4 %collective-permute-start.17 = (bf16[512,512]{1,0:T(8,128)(2,1)S(1)}, bf16[512,512]{1,0:T(8,128)(2,1)S(1)}, u32[]{:S(2)}, u32[]{:S(2)}) collective-permute-start(bf16[512,512]{1,0:T(8,128)(2,1)S(1)} %fusion.1), channel_id=1, source_target_pairs={{0,8},{8,16},{16,24},{24,0},{1,9},{9,17},{17,25},{25,1},{2,10},{10... | collective-permute-start | bytes 1572872 | tf_op jit(solution)/shard_map/ppermute | solution.py:44
  131.0 27.7 %collective-permute-done.14 = bf16[1536,512]{1,0:T(8,128)(2,1)S(1)} collective-permute-done((bf16[1536,512]{1,0:T(8,128)(2,1)S(1)}, bf16[1536,512]{1,0:T(8,128)(2,1)S(1)}, u32[]{:S(2)}, u32[]{:S(2)}) %collective-permute-start.14) | collective-permute-done | bytes 1572896 | tf_op jit(solution)/shard_map/ppermute | solution.py:40
  165.6 3.5 %collective-permute-start.31 = (bf16[512,512]{1,0:T(8,128)(2,1)S(1)}, bf16[512,512]{1,0:T(8,128)(2,1)S(1)}, u32[]{:S(2)}, u32[]{:S(2)}) collective-permute-start(bf16[512,512]{1,0:T(8,128)(2,1)S(1)} %fusion.6), channel_id=1, source_target_pairs={{0,8},{8,16},{16,24},{24,0},{1,9},{9,17},{17,25},{25,1},{2,10},{10... | collective-permute-start | bytes 1572872 | tf_op jit(solution)/shard_map/ppermute | solution.py:44
  169.1 2.8 %fusion.28 = f32[512,512]{1,0:T(8,128)S(1)} fusion(bf16[512,2048]{1,0:T(8,128)(2,1)S(1)} %pad_maximum_fusion.10, bf16[2048,512]{1,0:T(8,128)(2,1)} %collective-permute-done.13), kind=kOutput, calls=%fused_computation.82 | convolution fusion | flops 1073741824 | bytes 5242880 | tf_op jit(solution)/shard_map/dot_general | solution.py:22
  176.7 3.8 %fusion.25 = f32[512,512]{1,0:T(8,128)} fusion(bf16[512,2048]{1,0:T(8,128)(2,1)S(1)} %pad_maximum_fusion.7, bf16[2048,512]{1,0:T(8,128)(2,1)} %collective-permute-done.13), kind=kOutput, calls=%fused_computation.79 | convolution fusion | flops 1073741824 | bytes 5242880 | tf_op jit(solution)/shard_map/dot_general | solution.py:22
  180.5 3.8 %fusion.26 = f32[512,512]{1,0:T(8,128)} fusion(bf16[512,2048]{1,0:T(8,128)(2,1)S(1)} %pad_maximum_fusion.8, bf16[2048,512]{1,0:T(8,128)(2,1)} %collective-permute-done.13), kind=kOutput, calls=%fused_computation.80 | convolution fusion | flops 1073741824 | bytes 5242880 | tf_op jit(solution)/shard_map/dot_general | solution.py:22
  184.4 2.1 fusion.4
  186.4 5.8 %collective-permute-done.31 = bf16[512,512]{1,0:T(8,128)(2,1)S(1)} collective-permute-done((bf16[512,512]{1,0:T(8,128)(2,1)S(1)}, bf16[512,512]{1,0:T(8,128)(2,1)S(1)}, u32[]{:S(2)}, u32[]{:S(2)}) %collective-permute-start.31) | collective-permute-done | bytes 524320 | tf_op jit(solution)/shard_map/ppermute | solution.py:44
  194.5 1.6 pad_maximum_fusion.1
  196.1 1.8 collective-permute-start.27
  197.9 2.1 add_convert_fusion.1
  200.0 2.1 add_convert_fusion.2
  202.1 4.1 %fusion.27 = f32[512,512]{1,0:T(8,128)} fusion(bf16[512,2048]{1,0:T(8,128)(2,1)S(1)} %pad_maximum_fusion.1, bf16[2048,512]{1,0:T(8,128)(2,1)} %collective-permute-done.13), kind=kOutput, calls=%fused_computation.81 | convolution fusion | flops 1073741824 | bytes 5242880 | tf_op jit(solution)/shard_map/dot_general | solution.py:22
  207.5 2.8 %collective-permute-done.27 = bf16[512,512]{1,0:T(8,128)(2,1)S(1)} collective-permute-done((bf16[512,512]{1,0:T(8,128)(2,1)}, bf16[512,512]{1,0:T(8,128)(2,1)S(1)}, u32[]{:S(2)}, u32[]{:S(2)}) %collective-permute-start.27) | collective-permute-done | bytes 524320 | tf_op jit(solution)/shard_map/ppermute | solution.py:44
  210.4 2.4 collective-permute-start.28
  212.7 3.1 %fusion.11 = f32[512,512]{1,0:T(8,128)S(1)} fusion(bf16[512,2048]{1,0:T(8,128)(2,1)} %copy-done.2, bf16[512,512]{1,0:T(8,128)(2,1)} %copy-done.27, bf16[512,512]{1,0:T(8,128)(2,1)} %copy-done.29, bf16[512,512]{1,0:T(8,128)(2,1)S(1)} %copy-done.26, bf16[512,512]{1,0:T(8,128)(2,1)S(1)} %copy-done.23), kind=kOutput, calls=%fused_computation.65 | convolution fusion | flops 1082130432 | bytes 5242880 | tf_op jit(solution)/shard_map/dot_general | solution.py:22
  216.1 8.2 %collective-permute-done.25 = bf16[512,512]{1,0:T(8,128)(2,1)} collective-permute-done((bf16[512,512]{1,0:T(8,128)(2,1)}, bf16[512,512]{1,0:T(8,128)(2,1)}, u32[]{:S(2)}, u32[]{:S(2)}) %collective-permute-start.25) | collective-permute-done | bytes 524320 | tf_op jit(solution)/shard_map/ppermute | solution.py:44
  224.3 10.5 %collective-permute-done.28 = bf16[512,512]{1,0:T(8,128)(2,1)S(1)} collective-permute-done((bf16[512,512]{1,0:T(8,128)(2,1)S(1)}, bf16[512,512]{1,0:T(8,128)(2,1)S(1)}, u32[]{:S(2)}, u32[]{:S(2)}) %collective-permute-start.28) | collective-permute-done | bytes 524320 | tf_op jit(solution)/shard_map/ppermute | solution.py:44
  234.8 8.7 %fusion = bf16[1,512,4096]{2,1,0:T(8,128)(2,1)} fusion(bf16[512,4096]{1,0:T(8,128)(2,1)} %param.11, bf16[512,4096]{1,0:T(8,128)(2,1)} %all-gather.2.cloned.1.call-done, bf16[512,512]{1,0:T(8,128)(2,1)S(1)} %add_convert_fusion, bf16[512,512]{1,0:T(8,128)(2,1)} %collective-permute-done.25, bf16[512,512]{1,0:T(8,128)(2,1)S(1)} %collective-permute-done.28, ...), kind=kOutput, calls=%fused_computation.1 | convolution fusion | flops 2158493696 | bytes 14155778 | tf_op jit(solution)/shard_map/dot_general | solution.py:13
  (149 shorter events, 44.2 us)
Async XLA Ops:
  6.5 228.3 %all-gather.2.cloned.1.call-start = ((), (), s32[]{:S(2)}) async-start(), calls=%async_computation | async-start | bytes 4718592 | tf_op jit(solution)/shard_map/all_gather | solution.py:150
  8.4 31.9 %collective-permute-start.4 = (bf16[2048,512]{1,0:T(8,128)(2,1)S(1)}, bf16[2048,512]{1,0:T(8,128)(2,1)S(1)}, u32[]{:S(2)}, u32[]{:S(2)}) collective-permute-start(bf16[2048,512]{1,0:T(8,128)(2,1)S(1)} %pad_maximum_fusion), channel_id=1, source_target_pairs={{0,1},{1,0},{2,3},{3,2},{4,5},{5,4},{6,7},{7,6},{8,9},{9,8},{10,11... | collective-permute-start | bytes 6291464 | tf_op jit(solution)/shard_map/ppermute | solution.py:40
  9.5 25.0 %collective-permute-start = (bf16[1024,512]{1,0:T(8,128)(2,1)S(1)}, bf16[1024,512]{1,0:T(8,128)(2,1)S(1)}, u32[]{:S(2)}, u32[]{:S(2)}) collective-permute-start(bf16[1024,512]{1,0:T(8,128)(2,1)S(1)} %pad_maximum_fusion.24), channel_id=1, source_target_pairs={{0,2},{1,3},{2,0},{3,1},{4,6},{5,7},{6,4},{7,5},{8,10},{9,11},{10,... | collective-permute-start | bytes 3145736 | tf_op jit(solution)/shard_map/ppermute | solution.py:40
  11.0 24.6 %collective-permute-start.1 = (bf16[1024,512]{1,0:T(8,128)(2,1)S(1)}, bf16[1024,512]{1,0:T(8,128)(2,1)S(1)}, u32[]{:S(2)}, u32[]{:S(2)}) collective-permute-start(bf16[1024,512]{1,0:T(8,128)(2,1)S(1)} %pad_maximum_fusion.24), channel_id=1, source_target_pairs={{0,4},{1,5},{2,6},{3,7},{4,0},{5,1},{6,2},{7,3},{8,12},{9,13},{10,... | collective-permute-start | bytes 3145736 | tf_op jit(solution)/shard_map/ppermute | solution.py:40
  12.5 13.1 %collective-permute-start.2 = (bf16[512,512]{1,0:T(8,128)(2,1)S(1)}, bf16[512,512]{1,0:T(8,128)(2,1)S(1)}, u32[]{:S(2)}, u32[]{:S(2)}) collective-permute-start(bf16[512,512]{1,0:T(8,128)(2,1)S(1)} %bitcast.52), channel_id=1, source_target_pairs={{0,24},{8,0},{16,8},{24,16},{1,25},{9,1},{17,9},{25,17},{2,26},{10... | collective-permute-start | bytes 1572872 | tf_op jit(solution)/shard_map/ppermute | solution.py:44
  25.7 13.8 %collective-permute-start.3 = (bf16[512,512]{1,0:T(8,128)(2,1)S(1)}, bf16[512,512]{1,0:T(8,128)(2,1)S(1)}, u32[]{:S(2)}, u32[]{:S(2)}) collective-permute-start(bf16[512,512]{1,0:T(8,128)(2,1)S(1)} %collective-permute-done.2), channel_id=1, source_target_pairs={{0,24},{8,0},{16,8},{24,16},{1,25},{9,1},{17,9},{25,17},{2,26},{10... | collective-permute-start | bytes 1572872 | tf_op jit(solution)/shard_map/ppermute | solution.py:44
  40.3 34.0 %collective-permute-start.5 = (bf16[1536,512]{1,0:T(8,128)(2,1)S(1)}, bf16[1536,512]{1,0:T(8,128)(2,1)S(1)}, u32[]{:S(2)}, u32[]{:S(2)}) collective-permute-start(bf16[1536,512]{1,0:T(8,128)(2,1)S(1)} %get-tuple-element.44), channel_id=1, source_target_pairs={{0,2},{1,3},{2,0},{3,1},{4,6},{5,7},{6,4},{7,5},{8,10},{9,11},{10,... | collective-permute-start | bytes 4718600 | tf_op jit(solution)/shard_map/ppermute | solution.py:40
  40.8 33.7 %collective-permute-start.6 = (bf16[1536,512]{1,0:T(8,128)(2,1)S(1)}, bf16[1536,512]{1,0:T(8,128)(2,1)S(1)}, u32[]{:S(2)}, u32[]{:S(2)}) collective-permute-start(bf16[1536,512]{1,0:T(8,128)(2,1)S(1)} %get-tuple-element.45), channel_id=1, source_target_pairs={{0,4},{1,5},{2,6},{3,7},{4,0},{5,1},{6,2},{7,3},{8,12},{9,13},{10,... | collective-permute-start | bytes 4718600 | tf_op jit(solution)/shard_map/ppermute | solution.py:40
  41.3 16.4 %collective-permute-start.7 = (bf16[512,512]{1,0:T(8,128)(2,1)S(1)}, bf16[512,512]{1,0:T(8,128)(2,1)S(1)}, u32[]{:S(2)}, u32[]{:S(2)}) collective-permute-start(bf16[512,512]{1,0:T(8,128)(2,1)S(1)} %bitcast.56), channel_id=1, source_target_pairs={{0,24},{8,0},{16,8},{24,16},{1,25},{9,1},{17,9},{25,17},{2,26},{10... | collective-permute-start | bytes 1572872 | tf_op jit(solution)/shard_map/ppermute | solution.py:44
  41.3 35.4 %collective-permute-start.8 = (bf16[512,512]{1,0:T(8,128)(2,1)S(1)}, bf16[512,512]{1,0:T(8,128)(2,1)S(1)}, u32[]{:S(2)}, u32[]{:S(2)}) collective-permute-start(bf16[512,512]{1,0:T(8,128)(2,1)S(1)} %bitcast.53), channel_id=1, source_target_pairs={{0,8},{8,16},{16,24},{24,0},{1,9},{9,17},{17,25},{25,1},{2,10},{10... | collective-permute-start | bytes 1572872 | tf_op jit(solution)/shard_map/ppermute | solution.py:44
  57.7 19.1 %collective-permute-start.9 = (bf16[512,512]{1,0:T(8,128)(2,1)S(1)}, bf16[512,512]{1,0:T(8,128)(2,1)S(1)}, u32[]{:S(2)}, u32[]{:S(2)}) collective-permute-start(bf16[512,512]{1,0:T(8,128)(2,1)S(1)} %collective-permute-done.7), channel_id=1, source_target_pairs={{0,24},{8,0},{16,8},{24,16},{1,25},{9,1},{17,9},{25,17},{2,26},{10... | collective-permute-start | bytes 1572872 | tf_op jit(solution)/shard_map/ppermute | solution.py:44
  78.7 33.1 %collective-permute-start.10 = (bf16[1536,512]{1,0:T(8,128)(2,1)}, bf16[1536,512]{1,0:T(8,128)(2,1)}, u32[]{:S(2)}, u32[]{:S(2)}) collective-permute-start(bf16[1536,512]{1,0:T(8,128)(2,1)} %get-tuple-element.51), channel_id=1, source_target_pairs={{0,2},{1,3},{2,0},{3,1},{4,6},{5,7},{6,4},{7,5},{8,10},{9,11},{10,... | collective-permute-start | bytes 4718600 | tf_op jit(solution)/shard_map/ppermute | solution.py:40
  80.2 32.8 %collective-permute-start.11 = (bf16[1536,512]{1,0:T(8,128)(2,1)}, bf16[1536,512]{1,0:T(8,128)(2,1)}, u32[]{:S(2)}, u32[]{:S(2)}) collective-permute-start(bf16[1536,512]{1,0:T(8,128)(2,1)} %get-tuple-element.52), channel_id=1, source_target_pairs={{0,4},{1,5},{2,6},{3,7},{4,0},{5,1},{6,2},{7,3},{8,12},{9,13},{10,... | collective-permute-start | bytes 4718600 | tf_op jit(solution)/shard_map/ppermute | solution.py:40
  82.8 34.9 %collective-permute-start.13 = (bf16[2048,512]{1,0:T(8,128)(2,1)}, bf16[2048,512]{1,0:T(8,128)(2,1)}, u32[]{:S(2)}, u32[]{:S(2)}) collective-permute-start(bf16[2048,512]{1,0:T(8,128)(2,1)} %pad_maximum_fusion.2), channel_id=1, source_target_pairs={{0,1},{1,0},{2,3},{3,2},{4,5},{5,4},{6,7},{7,6},{8,9},{9,8},{10,11... | collective-permute-start | bytes 6291464 | tf_op jit(solution)/shard_map/ppermute | solution.py:40
  86.0 31.7 %collective-permute-start.12 = (bf16[512,512]{1,0:T(8,128)(2,1)S(1)}, bf16[512,512]{1,0:T(8,128)(2,1)S(1)}, u32[]{:S(2)}, u32[]{:S(2)}) collective-permute-start(bf16[512,512]{1,0:T(8,128)(2,1)S(1)} %bitcast.57), channel_id=1, source_target_pairs={{0,8},{8,16},{16,24},{24,0},{1,9},{9,17},{17,25},{25,1},{2,10},{10... | collective-permute-start | bytes 1572872 | tf_op jit(solution)/shard_map/ppermute | solution.py:44
  120.2 5.0 %collective-permute-start.16 = (f32[512,512]{1,0:T(8,128)S(1)}, f32[512,512]{1,0:T(8,128)S(1)}, u32[]{:S(2)}, u32[]{:S(2)}) collective-permute-start(f32[512,512]{1,0:T(8,128)S(1)} %fusion.22), channel_id=1, source_target_pairs={{0,1},{1,0},{2,3},{3,2},{4,5},{5,4},{6,7},{7,6},{8,9},{9,8},{10,11... | collective-permute-start | bytes 3145736 | tf_op jit(solution)/shard_map/ppermute | solution.py:40
  121.8 8.0 %collective-permute-start.18 = (f32[512,512]{1,0:T(8,128)S(1)}, f32[512,512]{1,0:T(8,128)S(1)}, u32[]{:S(2)}, u32[]{:S(2)}) collective-permute-start(f32[512,512]{1,0:T(8,128)S(1)} %fusion.23), channel_id=1, source_target_pairs={{0,1},{1,0},{2,3},{3,2},{4,5},{5,4},{6,7},{7,6},{8,9},{9,8},{10,11... | collective-permute-start | bytes 3145736 | tf_op jit(solution)/shard_map/ppermute | solution.py:40
  122.3 36.4 %collective-permute-start.14 = (bf16[1536,512]{1,0:T(8,128)(2,1)S(1)}, bf16[1536,512]{1,0:T(8,128)(2,1)S(1)}, u32[]{:S(2)}, u32[]{:S(2)}) collective-permute-start(bf16[1536,512]{1,0:T(8,128)(2,1)S(1)} %get-tuple-element.57), channel_id=1, source_target_pairs={{0,2},{1,3},{2,0},{3,1},{4,6},{5,7},{6,4},{7,5},{8,10},{9,11},{10,... | collective-permute-start | bytes 4718600 | tf_op jit(solution)/shard_map/ppermute | solution.py:40
  122.9 36.1 %collective-permute-start.15 = (bf16[1536,512]{1,0:T(8,128)(2,1)S(1)}, bf16[1536,512]{1,0:T(8,128)(2,1)S(1)}, u32[]{:S(2)}, u32[]{:S(2)}) collective-permute-start(bf16[1536,512]{1,0:T(8,128)(2,1)S(1)} %get-tuple-element.58), channel_id=1, source_target_pairs={{0,4},{1,5},{2,6},{3,7},{4,0},{5,1},{6,2},{7,3},{8,12},{9,13},{10,... | collective-permute-start | bytes 4718600 | tf_op jit(solution)/shard_map/ppermute | solution.py:40
  125.1 39.3 %collective-permute-start.30 = (f32[512,512]{1,0:T(8,128)S(1)}, f32[512,512]{1,0:T(8,128)S(1)}, u32[]{:S(2)}, u32[]{:S(2)}) collective-permute-start(f32[512,512]{1,0:T(8,128)S(1)} %fusion.29), channel_id=1, source_target_pairs={{0,1},{1,0},{2,3},{3,2},{4,5},{5,4},{6,7},{7,6},{8,9},{9,8},{10,11... | collective-permute-start | bytes 3145736 | tf_op jit(solution)/shard_map/ppermute | solution.py:40
  126.4 32.8 %collective-permute-start.17 = (bf16[512,512]{1,0:T(8,128)(2,1)S(1)}, bf16[512,512]{1,0:T(8,128)(2,1)S(1)}, u32[]{:S(2)}, u32[]{:S(2)}) collective-permute-start(bf16[512,512]{1,0:T(8,128)(2,1)S(1)} %fusion.1), channel_id=1, source_target_pairs={{0,8},{8,16},{16,24},{24,0},{1,9},{9,17},{17,25},{25,1},{2,10},{10... | collective-permute-start | bytes 1572872 | tf_op jit(solution)/shard_map/ppermute | solution.py:44
  160.8 12.9 %collective-permute-start.19 = (bf16[512,512]{1,0:T(8,128)(2,1)S(1)}, bf16[512,512]{1,0:T(8,128)(2,1)S(1)}, u32[]{:S(2)}, u32[]{:S(2)}) collective-permute-start(bf16[512,512]{1,0:T(8,128)(2,1)S(1)} %get-tuple-element.63), channel_id=1, source_target_pairs={{0,2},{1,3},{2,0},{3,1},{4,6},{5,7},{6,4},{7,5},{8,10},{9,11},{10,... | collective-permute-start | bytes 1572872 | tf_op jit(solution)/shard_map/ppermute | solution.py:40
  162.3 12.5 %collective-permute-start.20 = (bf16[512,512]{1,0:T(8,128)(2,1)S(1)}, bf16[512,512]{1,0:T(8,128)(2,1)S(1)}, u32[]{:S(2)}, u32[]{:S(2)}) collective-permute-start(bf16[512,512]{1,0:T(8,128)(2,1)S(1)} %get-tuple-element.64), channel_id=1, source_target_pairs={{0,4},{1,5},{2,6},{3,7},{4,0},{5,1},{6,2},{7,3},{8,12},{9,13},{10,... | collective-permute-start | bytes 1572872 | tf_op jit(solution)/shard_map/ppermute | solution.py:40
  164.3 11.1 %collective-permute-start.21 = (f32[512,512]{1,0:T(8,128)S(1)}, f32[512,512]{1,0:T(8,128)S(1)}, u32[]{:S(2)}, u32[]{:S(2)}) collective-permute-start(f32[512,512]{1,0:T(8,128)S(1)} %fusion.24), channel_id=1, source_target_pairs={{0,1},{1,0},{2,3},{3,2},{4,5},{5,4},{6,7},{7,6},{8,9},{9,8},{10,11... | collective-permute-start | bytes 3145736 | tf_op jit(solution)/shard_map/ppermute | solution.py:40
  165.6 26.6 %collective-permute-start.31 = (bf16[512,512]{1,0:T(8,128)(2,1)S(1)}, bf16[512,512]{1,0:T(8,128)(2,1)S(1)}, u32[]{:S(2)}, u32[]{:S(2)}) collective-permute-start(bf16[512,512]{1,0:T(8,128)(2,1)S(1)} %fusion.6), channel_id=1, source_target_pairs={{0,8},{8,16},{16,24},{24,0},{1,9},{9,17},{17,25},{25,1},{2,10},{10... | collective-permute-start | bytes 1572872 | tf_op jit(solution)/shard_map/ppermute | solution.py:44
  172.0 12.3 %collective-permute-start.26 = (f32[512,512]{1,0:T(8,128)S(1)}, f32[512,512]{1,0:T(8,128)S(1)}, u32[]{:S(2)}, u32[]{:S(2)}) collective-permute-start(f32[512,512]{1,0:T(8,128)S(1)} %fusion.28), channel_id=1, source_target_pairs={{0,1},{1,0},{2,3},{3,2},{4,5},{5,4},{6,7},{7,6},{8,9},{9,8},{10,11... | collective-permute-start | bytes 3145736 | tf_op jit(solution)/shard_map/ppermute | solution.py:40
  176.6 16.4 %collective-permute-start.29 = (bf16[512,512]{1,0:T(8,128)(2,1)S(1)}, bf16[512,512]{1,0:T(8,128)(2,1)S(1)}, u32[]{:S(2)}, u32[]{:S(2)}) collective-permute-start(bf16[512,512]{1,0:T(8,128)(2,1)S(1)} %fusion.3), channel_id=1, source_target_pairs={{0,24},{8,0},{16,8},{24,16},{1,25},{9,1},{17,9},{25,17},{2,26},{10... | collective-permute-start | bytes 1572872 | tf_op jit(solution)/shard_map/ppermute | solution.py:44
  194.0 6.1 %collective-permute-start.22 = (f32[512,512]{1,0:T(8,128)}, f32[512,512]{1,0:T(8,128)S(1)}, u32[]{:S(2)}, u32[]{:S(2)}) collective-permute-start(f32[512,512]{1,0:T(8,128)} %fusion.25), channel_id=1, source_target_pairs={{0,1},{1,0},{2,3},{3,2},{4,5},{5,4},{6,7},{7,6},{8,9},{9,8},{10,11... | collective-permute-start | bytes 3145736 | tf_op jit(solution)/shard_map/ppermute | solution.py:40
  196.1 14.2 %collective-permute-start.27 = (bf16[512,512]{1,0:T(8,128)(2,1)}, bf16[512,512]{1,0:T(8,128)(2,1)S(1)}, u32[]{:S(2)}, u32[]{:S(2)}) collective-permute-start(bf16[512,512]{1,0:T(8,128)(2,1)} %fusion.4), channel_id=1, source_target_pairs={{0,8},{8,16},{16,24},{24,0},{1,9},{9,17},{17,25},{25,1},{2,10},{10... | collective-permute-start | bytes 1572872 | tf_op jit(solution)/shard_map/ppermute | solution.py:44
  206.2 9.6 %collective-permute-start.24 = (f32[512,512]{1,0:T(8,128)}, f32[512,512]{1,0:T(8,128)S(1)}, u32[]{:S(2)}, u32[]{:S(2)}) collective-permute-start(f32[512,512]{1,0:T(8,128)} %fusion.27), channel_id=1, source_target_pairs={{0,1},{1,0},{2,3},{3,2},{4,5},{5,4},{6,7},{7,6},{8,9},{9,8},{10,11... | collective-permute-start | bytes 3145736 | tf_op jit(solution)/shard_map/ppermute | solution.py:40
  206.9 17.4 %collective-permute-start.25 = (bf16[512,512]{1,0:T(8,128)(2,1)}, bf16[512,512]{1,0:T(8,128)(2,1)}, u32[]{:S(2)}, u32[]{:S(2)}) collective-permute-start(bf16[512,512]{1,0:T(8,128)(2,1)} %add_convert_fusion.1), channel_id=1, source_target_pairs={{0,24},{8,0},{16,8},{24,16},{1,25},{9,1},{17,9},{25,17},{2,26},{10... | collective-permute-start | bytes 1572872 | tf_op jit(solution)/shard_map/ppermute | solution.py:44
  210.4 24.5 %collective-permute-start.28 = (bf16[512,512]{1,0:T(8,128)(2,1)S(1)}, bf16[512,512]{1,0:T(8,128)(2,1)S(1)}, u32[]{:S(2)}, u32[]{:S(2)}) collective-permute-start(bf16[512,512]{1,0:T(8,128)(2,1)S(1)} %broadcast_select_fusion), channel_id=1, source_target_pairs={{0,8},{8,16},{16,24},{24,0},{1,9},{9,17},{17,25},{25,1},{2,10},{10... | collective-permute-start | bytes 1572872 | tf_op jit(solution)/shard_map/ppermute | solution.py:44
  (35 other events, 402.4 us)
Sparse Core Ops, SparseCore 0:
  194.0 37.1 all-gather.1

commit v23 on v21

--- a/solution.py
+++ b/solution.py
@@ -137,24 +137,27 @@
     gate, due = due, slot(2, due)
     use(2, due, [])
     theirs[1] = rows_for_other(1, gate)
-    due += [fetch(1, 3, gate), theirs[1]] + rotate(groups[0][:1], evens[0][:1])
+    due += [fetch(1, 3, gate), theirs[1]]
 
     gate, due = due, slot(3, due)
     use(3, due, [])
     rotate(groups[1], after(evens[1], gate))
     passed_in = pass_on(0)
-    due += [passed_in] + rotate(groups[0][1:], after(evens[0][1:], gate))
+    due += [passed_in] + rotate(groups[0][:1], after(evens[0][:1], gate))
 
     gate, due = due, slot(4, due)
     in_from_behind = send_ahead(0, passed_in, gate)
-    rotate(groups[2], after(evens[2], gate))
+    rotate(groups[2][:1], after(evens[2][:1], gate))
     in_from_ahead = send_behind(0)
+    rotate(groups[2][1:], after(evens[2][1:], rotated[0, 3]))
     passed_out = pass_on(1)
     use(4, due, rotated[0, 3])
     rotate(groups[3], evens[3])
     begun = [rotated[1, 2], halves[1, 1], halves[1, 3]]
     rot_in = after(keep(0, in_from_behind, in_from_ahead), begun)
     all_rot_in = lax.all_gather(rot_in, "tensor", axis=1, tiled=True)
+    rotate(groups[0][1:], after(evens[0][1:], [rotated[1, 1], rotated[1, 3]]))
+    rotated[1, 0] = after(rotated[1, 0], [])
     rot_out = keep(1, send_ahead(1, passed_out, []), send_behind(1))
     return product_and_divide(rot_out, all_rot_in, eig_lambda, tokens)
 

time: 271 us -> 255 us (0.941); the launches traced: 267 us -> 255 us
  waiting for transfers between devices: 152 us -> 140 us
  local copies, waits for them, and re-layouts: 19.6 us -> 16.4 us
  other arithmetic: 6.35 us -> 9.44 us
    ppermute x12, waiting for transfers between devices: 66.2 us -> 52.4 us  [shift(): return lax.ppermute(block, 'dp', [(z, (z + by) % n) for z in range(n)])]
    unnamed x126 -> x80, local copies, waits for them, and re-layouts: 7.2 us -> 4.12 us
  transfers between devices with their start and end apart: 33 -> 33, of which waited for: 18 -> 16; matrix products, arithmetic and copies ran while one was open for 19% -> 19% of each run, Pallas kernels for 0% -> 0%
where the time goes in v23:
time: 255 us
  waiting for transfers between devices  140 us (55%)
  matrix products  45.1 us (18%)
  starting transfers between devices  28.7 us (11%)
  local copies, waits for them, and re-layouts  16.4 us (6%)
  between operations  15.3 us (6%)
  other arithmetic  9.44 us (4%)
    ppermute x20, waiting for transfers between devices, swap(): lax.ppermute(block, 'tensor', [(j, j ^ bit) for j in range(X + Y + CORE +...  87.3 us
    ppermute x12, waiting for transfers between devices, shift(): return lax.ppermute(block, 'dp', [(z, (z + by) % n) for z in range(n)])  52.4 us
    dot_general x16, matrix products, dot(): return jnp.dot(a, b, preferred_element_type=jnp.float32)  36.5 us
    ppermute x12, starting transfers between devices, shift(): return lax.ppermute(block, 'dp', [(z, (z + by) % n) for z in range(n)])  16.1 us
    ppermute x20, starting transfers between devices, swap(): lax.ppermute(block, 'tensor', [(j, j ^ bit) for j in range(X + Y + CORE +...  12.6 us
    dot_general x1, matrix products, product_and_divide(): lax.dot_general(rot_out, all_rot_in, contract, preferred_element_type=jnp...  8.64 us
  transfers between devices with their start and end apart: 33, of which 16 were waited for; matrix products, arithmetic and copies ran while one was open for 19% of the time, Pallas kernels for 0%

profile of v23, /device:TPU:16, one launch (start us, length us, event | category | flops | bytes accessed | tf_op | source)
XLA Modules:
  0.0 254.6 jit_solution(9651083458272875301)
XLA Ops:
  6.5 1.7 constant_dynamic-slice_fusion.8
  9.5 1.6 collective-permute-start
  11.0 1.5 collective-permute-start.1
  13.0 12.7 %collective-permute-done.2 = bf16[512,512]{1,0:T(8,128)(2,1)S(1)} collective-permute-done((bf16[512,512]{1,0:T(8,128)(2,1)S(1)}, bf16[512,512]{1,0:T(8,128)(2,1)S(1)}, u32[]{:S(2)}, u32[]{:S(2)}) %collective-permute-start.2) | collective-permute-done | bytes 524320 | tf_op jit(solution)/shard_map/ppermute | solution.py:44
  26.1 8.3 %collective-permute-done = bf16[1024,512]{1,0:T(8,128)(2,1)S(1)} collective-permute-done((bf16[1024,512]{1,0:T(8,128)(2,1)S(1)}, bf16[1024,512]{1,0:T(8,128)(2,1)S(1)}, u32[]{:S(2)}, u32[]{:S(2)}) %collective-permute-start) | collective-permute-done | bytes 1048608 | tf_op jit(solution)/shard_map/ppermute | solution.py:40
  36.8 2.7 %collective-permute-done.3 = bf16[512,512]{1,0:T(8,128)(2,1)S(1)} collective-permute-done((bf16[512,512]{1,0:T(8,128)(2,1)S(1)}, bf16[512,512]{1,0:T(8,128)(2,1)S(1)}, u32[]{:S(2)}, u32[]{:S(2)}) %collective-permute-start.3) | collective-permute-done | bytes 524320 | tf_op jit(solution)/shard_map/ppermute | solution.py:44
  41.3 3.5 %collective-permute-start.8 = (bf16[512,512]{1,0:T(8,128)(2,1)S(1)}, bf16[512,512]{1,0:T(8,128)(2,1)S(1)}, u32[]{:S(2)}, u32[]{:S(2)}) collective-permute-start(bf16[512,512]{1,0:T(8,128)(2,1)S(1)} %bitcast.49), channel_id=1, source_target_pairs={{0,8},{8,16},{16,24},{24,0},{1,9},{9,17},{17,25},{25,1},{2,10},{10... | collective-permute-start | bytes 1572872 | tf_op jit(solution)/shard_map/ppermute | solution.py:44
  44.9 12.8 %collective-permute-done.7 = bf16[512,512]{1,0:T(8,128)(2,1)S(1)} collective-permute-done((bf16[512,512]{1,0:T(8,128)(2,1)S(1)}, bf16[512,512]{1,0:T(8,128)(2,1)S(1)}, u32[]{:S(2)}, u32[]{:S(2)}) %collective-permute-start.7) | collective-permute-done | bytes 524320 | tf_op jit(solution)/shard_map/ppermute | solution.py:44
  57.7 16.6 %collective-permute-done.5 = bf16[1536,512]{1,0:T(8,128)(2,1)S(1)} collective-permute-done((bf16[1536,512]{1,0:T(8,128)(2,1)S(1)}, bf16[1536,512]{1,0:T(8,128)(2,1)S(1)}, u32[]{:S(2)}, u32[]{:S(2)}) %collective-permute-start.5) | collective-permute-done | bytes 1572896 | tf_op jit(solution)/shard_map/ppermute | solution.py:40
  76.8 2.0 pad_maximum_fusion.16
  78.7 1.5 collective-permute-start.10
  84.4 1.8 dynamic-slice_bitcast_fusion.7
  86.2 3.6 %collective-permute-start.12 = (bf16[512,512]{1,0:T(8,128)(2,1)S(1)}, bf16[512,512]{1,0:T(8,128)(2,1)S(1)}, u32[]{:S(2)}, u32[]{:S(2)}) collective-permute-start(bf16[512,512]{1,0:T(8,128)(2,1)S(1)} %bitcast.53), channel_id=1, source_target_pairs={{0,8},{8,16},{16,24},{24,0},{1,9},{9,17},{17,25},{25,1},{2,10},{10... | collective-permute-start | bytes 1572872 | tf_op jit(solution)/shard_map/ppermute | solution.py:44
  90.1 21.8 %collective-permute-done.10 = bf16[1536,512]{1,0:T(8,128)(2,1)} collective-permute-done((bf16[1536,512]{1,0:T(8,128)(2,1)}, bf16[1536,512]{1,0:T(8,128)(2,1)}, u32[]{:S(2)}, u32[]{:S(2)}) %collective-permute-start.10) | collective-permute-done | bytes 1572896 | tf_op jit(solution)/shard_map/ppermute | solution.py:40
  114.6 1.5 fusion.23
  127.9 3.4 %collective-permute-start.17 = (bf16[512,512]{1,0:T(8,128)(2,1)S(1)}, bf16[512,512]{1,0:T(8,128)(2,1)S(1)}, u32[]{:S(2)}, u32[]{:S(2)}) collective-permute-start(bf16[512,512]{1,0:T(8,128)(2,1)S(1)} %fusion.1), channel_id=1, source_target_pairs={{0,8},{8,16},{16,24},{24,0},{1,9},{9,17},{17,25},{25,1},{2,10},{10... | collective-permute-start | bytes 1572872 | tf_op jit(solution)/shard_map/ppermute | solution.py:44
  132.5 26.4 %collective-permute-done.14 = bf16[1536,512]{1,0:T(8,128)(2,1)S(1)} collective-permute-done((bf16[1536,512]{1,0:T(8,128)(2,1)S(1)}, bf16[1536,512]{1,0:T(8,128)(2,1)S(1)}, u32[]{:S(2)}, u32[]{:S(2)}) %collective-permute-start.14) | collective-permute-done | bytes 1572896 | tf_op jit(solution)/shard_map/ppermute | solution.py:40
  162.3 3.0 %collective-permute-start.31 = (bf16[512,512]{1,0:T(8,128)(2,1)S(1)}, bf16[512,512]{1,0:T(8,128)(2,1)S(1)}, u32[]{:S(2)}, u32[]{:S(2)}) collective-permute-start(bf16[512,512]{1,0:T(8,128)(2,1)S(1)} %fusion.7), channel_id=1, source_target_pairs={{0,8},{8,16},{16,24},{24,0},{1,9},{9,17},{17,25},{25,1},{2,10},{10... | collective-permute-start | bytes 1572872 | tf_op jit(solution)/shard_map/ppermute | solution.py:44
  165.4 1.5 collective-permute-start.19
  169.8 9.7 %collective-permute-done.19 = bf16[512,512]{1,0:T(8,128)(2,1)S(1)} collective-permute-done((bf16[512,512]{1,0:T(8,128)(2,1)S(1)}, bf16[512,512]{1,0:T(8,128)(2,1)S(1)}, u32[]{:S(2)}, u32[]{:S(2)}) %collective-permute-start.19) | collective-permute-done | bytes 524320 | tf_op jit(solution)/shard_map/ppermute | solution.py:40
  180.7 4.0 %fusion.32 = f32[512,512]{1,0:T(8,128)} fusion(bf16[512,2048]{1,0:T(8,128)(2,1)S(1)} %pad_maximum_fusion.11, bf16[2048,512]{1,0:T(8,128)(2,1)} %collective-permute-done.13), kind=kOutput, calls=%fused_computation.86 | convolution fusion | flops 1073741824 | bytes 5242880 | tf_op jit(solution)/shard_map/dot_general | solution.py:22
  184.7 3.9 %fusion.13 = f32[512,512]{1,0:T(8,128)} fusion(bf16[2048,512]{1,0:T(8,128)(2,1)} %collective-permute-done.13, bf16[512,512]{1,0:T(8,128)(2,1)S(1)} %collective-permute-done.20, bf16[512,512]{1,0:T(8,128)(2,1)S(1)} %get-tuple-element.93, bf16[512,512]{1,0:T(8,128)(2,1)S(1)} %get-tuple-element.62, bf16[512,512]{1,0:T(8,128)(2,1)S(1)} %copy-done.16), kind=kOutput, calls=%fused_computation.57 | convolution fusion | flops 1082130432 | bytes 5242880 | tf_op jit(solution)/shard_map/dot_general | solution.py:22
  188.6 3.8 %fusion.12 = f32[512,512]{1,0:T(8,128)} fusion(bf16[2048,512]{1,0:T(8,128)(2,1)} %collective-permute-done.13, bf16[512,512]{1,0:T(8,128)(2,1)S(1)} %collective-permute-done.19, bf16[512,512]{1,0:T(8,128)(2,1)S(1)} %get-tuple-element.61, bf16[512,512]{1,0:T(8,128)(2,1)S(1)} %get-tuple-element.90, bf16[512,512]{1,0:T(8,128)(2,1)S(1)} %collective-permute-done.12), kind=kOutput, calls=%fused_computation.56 | convolution fusion | flops 1082130432 | bytes 5242880 | tf_op jit(solution)/shard_map/dot_general | solution.py:22
  193.3 4.0 %add_convert_fusion = bf16[512,512]{1,0:T(8,128)(2,1)} fusion(f32[512,512]{1,0:T(8,128)} %collective-permute-done.26, bf16[512,2048]{1,0:T(8,128)(2,1)S(1)} %pad_maximum_fusion.11, bf16[512,512]{1,0:T(8,128)(2,1)} %get-tuple-element.73, bf16[512,512]{1,0:T(8,128)(2,1)} %get-tuple-element.74, bf16[512,512]{1,0:T(8,128)(2,1)} %get-tuple-element.72, ...), kind=kOutput, calls=%fused_computation.40 | convolution fusion | flops 1082654720 | bytes 5767168 | tf_op jit(solution)/shard_map/dot_general | solution.py:22
  198.0 1.6 pad_maximum_fusion.1
  200.4 2.0 fusion.5
  202.5 2.0 fusion.4
  204.5 4.0 %fusion.31 = f32[512,512]{1,0:T(8,128)} fusion(bf16[512,2048]{1,0:T(8,128)(2,1)S(1)} %pad_maximum_fusion.1, bf16[2048,512]{1,0:T(8,128)(2,1)} %collective-permute-done.13), kind=kOutput, calls=%fused_computation.85 | convolution fusion | flops 1073741824 | bytes 5242880 | tf_op jit(solution)/shard_map/dot_general | solution.py:22
  210.6 14.8 %collective-permute-done.27 = bf16[512,512]{1,0:T(8,128)(2,1)S(1)} collective-permute-done((bf16[512,512]{1,0:T(8,128)(2,1)}, bf16[512,512]{1,0:T(8,128)(2,1)S(1)}, u32[]{:S(2)}, u32[]{:S(2)}) %collective-permute-start.27) | collective-permute-done | bytes 524320 | tf_op jit(solution)/shard_map/ppermute | solution.py:44
  225.5 2.8 %fusion.19 = f32[512,512]{1,0:T(8,128)S(1)} fusion(bf16[512,2048]{1,0:T(8,128)(2,1)S(1)} %pad_maximum_fusion.1, bf16[512,512]{1,0:T(8,128)(2,1)} %get-tuple-element.73, bf16[512,512]{1,0:T(8,128)(2,1)} %get-tuple-element.74, bf16[512,512]{1,0:T(8,128)(2,1)} %get-tuple-element.72, bf16[512,512]{1,0:T(8,128)(2,1)} %get-tuple-element.71), kind=kOutput, calls=%fused_computation.73 | convolution fusion | flops 1082130432 | bytes 5242880 | tf_op jit(solution)/shard_map/dot_general | solution.py:22
  229.7 9.4 %collective-permute-done.28 = bf16[512,512]{1,0:T(8,128)(2,1)S(1)} collective-permute-done((bf16[512,512]{1,0:T(8,128)(2,1)S(1)}, bf16[512,512]{1,0:T(8,128)(2,1)S(1)}, u32[]{:S(2)}, u32[]{:S(2)}) %collective-permute-start.28) | collective-permute-done | bytes 524320 | tf_op jit(solution)/shard_map/ppermute | solution.py:44
  239.1 8.6 %fusion = bf16[1,512,4096]{2,1,0:T(8,128)(2,1)} fusion(bf16[512,4096]{1,0:T(8,128)(2,1)} %param.11, bf16[512,4096]{1,0:T(8,128)(2,1)} %all-gather.2.cloned.1.call-done, bf16[512,512]{1,0:T(8,128)(2,1)S(1)} %add_convert_fusion.1, bf16[512,512]{1,0:T(8,128)(2,1)} %collective-permute-done.25, bf16[512,512]{1,0:T(8,128)(2,1)S(1)} %collective-permute-done.28, ...), kind=kOutput, calls=%fused_computation.1 | convolution fusion | flops 2158493696 | bytes 14155778 | tf_op jit(solution)/shard_map/dot_general | solution.py:13
  (159 shorter events, 40.9 us)
Async XLA Ops:
  6.5 232.6 %all-gather.2.cloned.1.call-start = ((), (), s32[]{:S(2)}) async-start(), calls=%async_computation | async-start | bytes 4718592 | tf_op jit(solution)/shard_map/all_gather | solution.py:158
  8.4 31.9 %collective-permute-start.4 = (bf16[2048,512]{1,0:T(8,128)(2,1)S(1)}, bf16[2048,512]{1,0:T(8,128)(2,1)S(1)}, u32[]{:S(2)}, u32[]{:S(2)}) collective-permute-start(bf16[2048,512]{1,0:T(8,128)(2,1)S(1)} %pad_maximum_fusion), channel_id=1, source_target_pairs={{0,1},{1,0},{2,3},{3,2},{4,5},{5,4},{6,7},{7,6},{8,9},{9,8},{10,11... | collective-permute-start | bytes 6291464 | tf_op jit(solution)/shard_map/ppermute | solution.py:40
  9.5 25.0 %collective-permute-start = (bf16[1024,512]{1,0:T(8,128)(2,1)S(1)}, bf16[1024,512]{1,0:T(8,128)(2,1)S(1)}, u32[]{:S(2)}, u32[]{:S(2)}) collective-permute-start(bf16[1024,512]{1,0:T(8,128)(2,1)S(1)} %pad_maximum_fusion.24), channel_id=1, source_target_pairs={{0,2},{1,3},{2,0},{3,1},{4,6},{5,7},{6,4},{7,5},{8,10},{9,11},{10,... | collective-permute-start | bytes 3145736 | tf_op jit(solution)/shard_map/ppermute | solution.py:40
  11.0 24.6 %collective-permute-start.1 = (bf16[1024,512]{1,0:T(8,128)(2,1)S(1)}, bf16[1024,512]{1,0:T(8,128)(2,1)S(1)}, u32[]{:S(2)}, u32[]{:S(2)}) collective-permute-start(bf16[1024,512]{1,0:T(8,128)(2,1)S(1)} %pad_maximum_fusion.24), channel_id=1, source_target_pairs={{0,4},{1,5},{2,6},{3,7},{4,0},{5,1},{6,2},{7,3},{8,12},{9,13},{10,... | collective-permute-start | bytes 3145736 | tf_op jit(solution)/shard_map/ppermute | solution.py:40
  12.5 13.1 %collective-permute-start.2 = (bf16[512,512]{1,0:T(8,128)(2,1)S(1)}, bf16[512,512]{1,0:T(8,128)(2,1)S(1)}, u32[]{:S(2)}, u32[]{:S(2)}) collective-permute-start(bf16[512,512]{1,0:T(8,128)(2,1)S(1)} %bitcast.48), channel_id=1, source_target_pairs={{0,24},{8,0},{16,8},{24,16},{1,25},{9,1},{17,9},{25,17},{2,26},{10... | collective-permute-start | bytes 1572872 | tf_op jit(solution)/shard_map/ppermute | solution.py:44
  25.7 13.8 %collective-permute-start.3 = (bf16[512,512]{1,0:T(8,128)(2,1)S(1)}, bf16[512,512]{1,0:T(8,128)(2,1)S(1)}, u32[]{:S(2)}, u32[]{:S(2)}) collective-permute-start(bf16[512,512]{1,0:T(8,128)(2,1)S(1)} %collective-permute-done.2), channel_id=1, source_target_pairs={{0,24},{8,0},{16,8},{24,16},{1,25},{9,1},{17,9},{25,17},{2,26},{10... | collective-permute-start | bytes 1572872 | tf_op jit(solution)/shard_map/ppermute | solution.py:44
  40.3 34.0 %collective-permute-start.5 = (bf16[1536,512]{1,0:T(8,128)(2,1)S(1)}, bf16[1536,512]{1,0:T(8,128)(2,1)S(1)}, u32[]{:S(2)}, u32[]{:S(2)}) collective-permute-start(bf16[1536,512]{1,0:T(8,128)(2,1)S(1)} %get-tuple-element.42), channel_id=1, source_target_pairs={{0,2},{1,3},{2,0},{3,1},{4,6},{5,7},{6,4},{7,5},{8,10},{9,11},{10,... | collective-permute-start | bytes 4718600 | tf_op jit(solution)/shard_map/ppermute | solution.py:40
  40.8 33.7 %collective-permute-start.6 = (bf16[1536,512]{1,0:T(8,128)(2,1)S(1)}, bf16[1536,512]{1,0:T(8,128)(2,1)S(1)}, u32[]{:S(2)}, u32[]{:S(2)}) collective-permute-start(bf16[1536,512]{1,0:T(8,128)(2,1)S(1)} %get-tuple-element.43), channel_id=1, source_target_pairs={{0,4},{1,5},{2,6},{3,7},{4,0},{5,1},{6,2},{7,3},{8,12},{9,13},{10,... | collective-permute-start | bytes 4718600 | tf_op jit(solution)/shard_map/ppermute | solution.py:40
  41.3 16.4 %collective-permute-start.7 = (bf16[512,512]{1,0:T(8,128)(2,1)S(1)}, bf16[512,512]{1,0:T(8,128)(2,1)S(1)}, u32[]{:S(2)}, u32[]{:S(2)}) collective-permute-start(bf16[512,512]{1,0:T(8,128)(2,1)S(1)} %bitcast.52), channel_id=1, source_target_pairs={{0,24},{8,0},{16,8},{24,16},{1,25},{9,1},{17,9},{25,17},{2,26},{10... | collective-permute-start | bytes 1572872 | tf_op jit(solution)/shard_map/ppermute | solution.py:44
  41.3 35.4 %collective-permute-start.8 = (bf16[512,512]{1,0:T(8,128)(2,1)S(1)}, bf16[512,512]{1,0:T(8,128)(2,1)S(1)}, u32[]{:S(2)}, u32[]{:S(2)}) collective-permute-start(bf16[512,512]{1,0:T(8,128)(2,1)S(1)} %bitcast.49), channel_id=1, source_target_pairs={{0,8},{8,16},{16,24},{24,0},{1,9},{9,17},{17,25},{25,1},{2,10},{10... | collective-permute-start | bytes 1572872 | tf_op jit(solution)/shard_map/ppermute | solution.py:44
  57.7 19.0 %collective-permute-start.9 = (bf16[512,512]{1,0:T(8,128)(2,1)S(1)}, bf16[512,512]{1,0:T(8,128)(2,1)S(1)}, u32[]{:S(2)}, u32[]{:S(2)}) collective-permute-start(bf16[512,512]{1,0:T(8,128)(2,1)S(1)} %collective-permute-done.7), channel_id=1, source_target_pairs={{0,24},{8,0},{16,8},{24,16},{1,25},{9,1},{17,9},{25,17},{2,26},{10... | collective-permute-start | bytes 1572872 | tf_op jit(solution)/shard_map/ppermute | solution.py:44
  78.7 33.1 %collective-permute-start.10 = (bf16[1536,512]{1,0:T(8,128)(2,1)}, bf16[1536,512]{1,0:T(8,128)(2,1)}, u32[]{:S(2)}, u32[]{:S(2)}) collective-permute-start(bf16[1536,512]{1,0:T(8,128)(2,1)} %get-tuple-element.49), channel_id=1, source_target_pairs={{0,2},{1,3},{2,0},{3,1},{4,6},{5,7},{6,4},{7,5},{8,10},{9,11},{10,... | collective-permute-start | bytes 4718600 | tf_op jit(solution)/shard_map/ppermute | solution.py:40
  80.2 32.8 %collective-permute-start.11 = (bf16[1536,512]{1,0:T(8,128)(2,1)}, bf16[1536,512]{1,0:T(8,128)(2,1)}, u32[]{:S(2)}, u32[]{:S(2)}) collective-permute-start(bf16[1536,512]{1,0:T(8,128)(2,1)} %get-tuple-element.50), channel_id=1, source_target_pairs={{0,4},{1,5},{2,6},{3,7},{4,0},{5,1},{6,2},{7,3},{8,12},{9,13},{10,... | collective-permute-start | bytes 4718600 | tf_op jit(solution)/shard_map/ppermute | solution.py:40
  82.9 34.8 %collective-permute-start.13 = (bf16[2048,512]{1,0:T(8,128)(2,1)}, bf16[2048,512]{1,0:T(8,128)(2,1)}, u32[]{:S(2)}, u32[]{:S(2)}) collective-permute-start(bf16[2048,512]{1,0:T(8,128)(2,1)} %pad_maximum_fusion.2), channel_id=1, source_target_pairs={{0,1},{1,0},{2,3},{3,2},{4,5},{5,4},{6,7},{7,6},{8,9},{9,8},{10,11... | collective-permute-start | bytes 6291464 | tf_op jit(solution)/shard_map/ppermute | solution.py:40
  86.2 31.5 %collective-permute-start.12 = (bf16[512,512]{1,0:T(8,128)(2,1)S(1)}, bf16[512,512]{1,0:T(8,128)(2,1)S(1)}, u32[]{:S(2)}, u32[]{:S(2)}) collective-permute-start(bf16[512,512]{1,0:T(8,128)(2,1)S(1)} %bitcast.53), channel_id=1, source_target_pairs={{0,8},{8,16},{16,24},{24,0},{1,9},{9,17},{17,25},{25,1},{2,10},{10... | collective-permute-start | bytes 1572872 | tf_op jit(solution)/shard_map/ppermute | solution.py:44
  120.4 6.2 %collective-permute-start.16 = (f32[512,512]{1,0:T(8,128)S(1)}, f32[512,512]{1,0:T(8,128)S(1)}, u32[]{:S(2)}, u32[]{:S(2)}) collective-permute-start(f32[512,512]{1,0:T(8,128)S(1)} %fusion.28), channel_id=1, source_target_pairs={{0,1},{1,0},{2,3},{3,2},{4,5},{5,4},{6,7},{7,6},{8,9},{9,8},{10,11... | collective-permute-start | bytes 3145736 | tf_op jit(solution)/shard_map/ppermute | solution.py:40
  122.0 9.3 %collective-permute-start.18 = (f32[512,512]{1,0:T(8,128)S(1)}, f32[512,512]{1,0:T(8,128)S(1)}, u32[]{:S(2)}, u32[]{:S(2)}) collective-permute-start(f32[512,512]{1,0:T(8,128)S(1)} %fusion.29), channel_id=1, source_target_pairs={{0,1},{1,0},{2,3},{3,2},{4,5},{5,4},{6,7},{7,6},{8,9},{9,8},{10,11... | collective-permute-start | bytes 3145736 | tf_op jit(solution)/shard_map/ppermute | solution.py:40
  122.6 36.4 %collective-permute-start.14 = (bf16[1536,512]{1,0:T(8,128)(2,1)S(1)}, bf16[1536,512]{1,0:T(8,128)(2,1)S(1)}, u32[]{:S(2)}, u32[]{:S(2)}) collective-permute-start(bf16[1536,512]{1,0:T(8,128)(2,1)S(1)} %get-tuple-element.55), channel_id=1, source_target_pairs={{0,2},{1,3},{2,0},{3,1},{4,6},{5,7},{6,4},{7,5},{8,10},{9,11},{10,... | collective-permute-start | bytes 4718600 | tf_op jit(solution)/shard_map/ppermute | solution.py:40
  123.1 36.1 %collective-permute-start.15 = (bf16[1536,512]{1,0:T(8,128)(2,1)S(1)}, bf16[1536,512]{1,0:T(8,128)(2,1)S(1)}, u32[]{:S(2)}, u32[]{:S(2)}) collective-permute-start(bf16[1536,512]{1,0:T(8,128)(2,1)S(1)} %get-tuple-element.56), channel_id=1, source_target_pairs={{0,4},{1,5},{2,6},{3,7},{4,0},{5,1},{6,2},{7,3},{8,12},{9,13},{10,... | collective-permute-start | bytes 4718600 | tf_op jit(solution)/shard_map/ppermute | solution.py:40
  126.6 34.4 %collective-permute-start.30 = (f32[512,512]{1,0:T(8,128)S(1)}, f32[512,512]{1,0:T(8,128)S(1)}, u32[]{:S(2)}, u32[]{:S(2)}) collective-permute-start(f32[512,512]{1,0:T(8,128)S(1)} %fusion.33), channel_id=1, source_target_pairs={{0,1},{1,0},{2,3},{3,2},{4,5},{5,4},{6,7},{7,6},{8,9},{9,8},{10,11... | collective-permute-start | bytes 3145736 | tf_op jit(solution)/shard_map/ppermute | solution.py:40
  127.9 31.7 %collective-permute-start.17 = (bf16[512,512]{1,0:T(8,128)(2,1)S(1)}, bf16[512,512]{1,0:T(8,128)(2,1)S(1)}, u32[]{:S(2)}, u32[]{:S(2)}) collective-permute-start(bf16[512,512]{1,0:T(8,128)(2,1)S(1)} %fusion.1), channel_id=1, source_target_pairs={{0,8},{8,16},{16,24},{24,0},{1,9},{9,17},{17,25},{25,1},{2,10},{10... | collective-permute-start | bytes 1572872 | tf_op jit(solution)/shard_map/ppermute | solution.py:44
  160.9 7.4 %collective-permute-start.21 = (f32[512,512]{1,0:T(8,128)S(1)}, f32[512,512]{1,0:T(8,128)S(1)}, u32[]{:S(2)}, u32[]{:S(2)}) collective-permute-start(f32[512,512]{1,0:T(8,128)S(1)} %fusion.30), channel_id=1, source_target_pairs={{0,1},{1,0},{2,3},{3,2},{4,5},{5,4},{6,7},{7,6},{8,9},{9,8},{10,11... | collective-permute-start | bytes 3145736 | tf_op jit(solution)/shard_map/ppermute | solution.py:40
  162.3 30.2 %collective-permute-start.31 = (bf16[512,512]{1,0:T(8,128)(2,1)S(1)}, bf16[512,512]{1,0:T(8,128)(2,1)S(1)}, u32[]{:S(2)}, u32[]{:S(2)}) collective-permute-start(bf16[512,512]{1,0:T(8,128)(2,1)S(1)} %fusion.7), channel_id=1, source_target_pairs={{0,8},{8,16},{16,24},{24,0},{1,9},{9,17},{17,25},{25,1},{2,10},{10... | collective-permute-start | bytes 1572872 | tf_op jit(solution)/shard_map/ppermute | solution.py:44
  165.4 14.1 %collective-permute-start.19 = (bf16[512,512]{1,0:T(8,128)(2,1)S(1)}, bf16[512,512]{1,0:T(8,128)(2,1)S(1)}, u32[]{:S(2)}, u32[]{:S(2)}) collective-permute-start(bf16[512,512]{1,0:T(8,128)(2,1)S(1)} %get-tuple-element.61), channel_id=1, source_target_pairs={{0,2},{1,3},{2,0},{3,1},{4,6},{5,7},{6,4},{7,5},{8,10},{9,11},{10,... | collective-permute-start | bytes 1572872 | tf_op jit(solution)/shard_map/ppermute | solution.py:40
  166.9 13.8 %collective-permute-start.20 = (bf16[512,512]{1,0:T(8,128)(2,1)S(1)}, bf16[512,512]{1,0:T(8,128)(2,1)S(1)}, u32[]{:S(2)}, u32[]{:S(2)}) collective-permute-start(bf16[512,512]{1,0:T(8,128)(2,1)S(1)} %get-tuple-element.62), channel_id=1, source_target_pairs={{0,4},{1,5},{2,6},{3,7},{4,0},{5,1},{6,2},{7,3},{8,12},{9,13},{10,... | collective-permute-start | bytes 1572872 | tf_op jit(solution)/shard_map/ppermute | solution.py:40
  169.6 22.8 %collective-permute-start.29 = (bf16[512,512]{1,0:T(8,128)(2,1)S(1)}, bf16[512,512]{1,0:T(8,128)(2,1)S(1)}, u32[]{:S(2)}, u32[]{:S(2)}) collective-permute-start(bf16[512,512]{1,0:T(8,128)(2,1)S(1)} %fusion.3), channel_id=1, source_target_pairs={{0,24},{8,0},{16,8},{24,16},{1,25},{9,1},{17,9},{25,17},{2,26},{10... | collective-permute-start | bytes 1572872 | tf_op jit(solution)/shard_map/ppermute | solution.py:44
  184.7 8.6 %collective-permute-start.26 = (f32[512,512]{1,0:T(8,128)}, f32[512,512]{1,0:T(8,128)}, u32[]{:S(2)}, u32[]{:S(2)}) collective-permute-start(f32[512,512]{1,0:T(8,128)} %fusion.32), channel_id=1, source_target_pairs={{0,1},{1,0},{2,3},{3,2},{4,5},{5,4},{6,7},{7,6},{8,9},{9,8},{10,11... | collective-permute-start | bytes 3145736 | tf_op jit(solution)/shard_map/ppermute | solution.py:40
  197.9 4.6 %collective-permute-start.22 = (f32[512,512]{1,0:T(8,128)}, f32[512,512]{1,0:T(8,128)S(1)}, u32[]{:S(2)}, u32[]{:S(2)}) collective-permute-start(f32[512,512]{1,0:T(8,128)} %fusion.13), channel_id=1, source_target_pairs={{0,1},{1,0},{2,3},{3,2},{4,5},{5,4},{6,7},{7,6},{8,9},{9,8},{10,11... | collective-permute-start | bytes 3145736 | tf_op jit(solution)/shard_map/ppermute | solution.py:40
  199.6 25.8 %collective-permute-start.27 = (bf16[512,512]{1,0:T(8,128)(2,1)}, bf16[512,512]{1,0:T(8,128)(2,1)S(1)}, u32[]{:S(2)}, u32[]{:S(2)}) collective-permute-start(bf16[512,512]{1,0:T(8,128)(2,1)} %add_convert_fusion), channel_id=1, source_target_pairs={{0,8},{8,16},{16,24},{24,0},{1,9},{9,17},{17,25},{25,1},{2,10},{10... | collective-permute-start | bytes 1572872 | tf_op jit(solution)/shard_map/ppermute | solution.py:44
  208.5 19.8 %collective-permute-start.24 = (f32[512,512]{1,0:T(8,128)}, f32[512,512]{1,0:T(8,128)}, u32[]{:S(2)}, u32[]{:S(2)}) collective-permute-start(f32[512,512]{1,0:T(8,128)} %fusion.31), channel_id=1, source_target_pairs={{0,1},{1,0},{2,3},{3,2},{4,5},{5,4},{6,7},{7,6},{8,9},{9,8},{10,11... | collective-permute-start | bytes 3145736 | tf_op jit(solution)/shard_map/ppermute | solution.py:40
  209.5 20.2 %collective-permute-start.25 = (bf16[512,512]{1,0:T(8,128)(2,1)}, bf16[512,512]{1,0:T(8,128)(2,1)}, u32[]{:S(2)}, u32[]{:S(2)}) collective-permute-start(bf16[512,512]{1,0:T(8,128)(2,1)} %fusion.5), channel_id=1, source_target_pairs={{0,24},{8,0},{16,8},{24,16},{1,25},{9,1},{17,9},{25,17},{2,26},{10... | collective-permute-start | bytes 1572872 | tf_op jit(solution)/shard_map/ppermute | solution.py:44
  225.5 13.6 %collective-permute-start.28 = (bf16[512,512]{1,0:T(8,128)(2,1)S(1)}, bf16[512,512]{1,0:T(8,128)(2,1)S(1)}, u32[]{:S(2)}, u32[]{:S(2)}) collective-permute-start(bf16[512,512]{1,0:T(8,128)(2,1)S(1)} %broadcast_select_fusion), channel_id=1, source_target_pairs={{0,8},{8,16},{16,24},{24,0},{1,9},{9,17},{17,25},{25,1},{2,10},{10... | collective-permute-start | bytes 1572872 | tf_op jit(solution)/shard_map/ppermute | solution.py:44
  (41 other events, 350.3 us)
Sparse Core Ops, SparseCore 0:
  197.4 36.3 all-gather.1

commit v24 on v19

--- a/solution.py
+++ b/solution.py
@@ -137,8 +137,7 @@
     gate, due = due, slot(3, due)
     rotate(groups[1], after(evens[1], gate))
     passed_in = pass_on(0)
-    due.append(passed_in)
-    rotate(groups[0], after(evens[0], gate))
+    due += [passed_in] + rotate(groups[0], after(evens[0], gate))
 
     gate, due = due, slot(4, due)
     in_from_behind = send_ahead(0, passed_in, gate)

time: 256 us -> 260 us (1.016)
  waiting for transfers between devices: 138 us -> 148 us
  matrix products: 41.9 us -> 35.6 us
    ppermute x12, waiting for transfers between devices: 62.6 us -> 69 us  [shift(): return lax.ppermute(block, 'dp', [(z, (z + by) % n) for z in range(n)])]
    dot_general x15 -> x16, matrix products: 31.2 us -> 27 us  [dot(): return jnp.dot(a, b, preferred_element_type=jnp.float32)]
    ppermute x20, waiting for transfers between devices: 75.1 us -> 78.6 us  [swap(): lax.ppermute(block, 'tensor', [(j, j ^ bit) for j in range(X + Y + CORE +...]
    unnamed x70 -> x58, local copies, waits for them, and re-layouts: 6.22 us -> 7.55 us
  transfers between devices with their start and end apart: 33 -> 33, of which waited for: 16 -> 18; matrix products, arithmetic and copies ran while one was open for 17% -> 16% of each run, Pallas kernels for 0% -> 0%
where the time goes in v24:
time: 260 us; the launch traced here: 256 us
  waiting for transfers between devices  148 us (57%)
  matrix products  35.6 us (14%)
  starting transfers between devices  31.2 us (12%)
  local copies, waits for them, and re-layouts  18.5 us (7%)
  between operations  15.2 us (6%)
  other arithmetic  8.04 us (3%)
    ppermute x20, waiting for transfers between devices, swap(): lax.ppermute(block, 'tensor', [(j, j ^ bit) for j in range(X + Y + CORE +...  78.6 us
    ppermute x12, waiting for transfers between devices, shift(): return lax.ppermute(block, 'dp', [(z, (z + by) % n) for z in range(n)])  69 us
    dot_general x16, matrix products, dot(): return jnp.dot(a, b, preferred_element_type=jnp.float32)  27 us
    ppermute x12, starting transfers between devices, shift(): return lax.ppermute(block, 'dp', [(z, (z + by) % n) for z in range(n)])  19 us
    ppermute x20, starting transfers between devices, swap(): lax.ppermute(block, 'tensor', [(j, j ^ bit) for j in range(X + Y + CORE +...  12.2 us
    dot_general x1, matrix products, product_and_divide(): lax.dot_general(rot_out, all_rot_in, contract, preferred_element_type=jnp...  8.67 us
    unnamed x58, local copies, waits for them, and re-layouts  7.55 us
  transfers between devices with their start and end apart: 33, of which 18 were waited for; matrix products, arithmetic and copies ran while one was open for 16% of the time, Pallas kernels for 0%

profile of v24, /device:TPU:16, one launch (start us, length us, event | category | flops | bytes accessed | tf_op | source)
XLA Modules:
  0.0 256.2 jit_solution(10517955114530255119)
XLA Ops:
  6.5 1.7 constant_dynamic-slice_fusion.8
  9.5 1.6 collective-permute-start
  13.0 12.7 %collective-permute-done.2 = bf16[512,512]{1,0:T(8,128)(2,1)S(1)} collective-permute-done((bf16[512,512]{1,0:T(8,128)(2,1)S(1)}, bf16[512,512]{1,0:T(8,128)(2,1)S(1)}, u32[]{:S(2)}, u32[]{:S(2)}) %collective-permute-start.2) | collective-permute-done | bytes 524320 | tf_op jit(solution)/shard_map/ppermute | solution.py:44
  26.1 8.3 %collective-permute-done = bf16[1024,512]{1,0:T(8,128)(2,1)S(1)} collective-permute-done((bf16[1024,512]{1,0:T(8,128)(2,1)S(1)}, bf16[1024,512]{1,0:T(8,128)(2,1)S(1)}, u32[]{:S(2)}, u32[]{:S(2)}) %collective-permute-start) | collective-permute-done | bytes 1048608 | tf_op jit(solution)/shard_map/ppermute | solution.py:40
  36.8 2.7 %collective-permute-done.3 = bf16[512,512]{1,0:T(8,128)(2,1)S(1)} collective-permute-done((bf16[512,512]{1,0:T(8,128)(2,1)S(1)}, bf16[512,512]{1,0:T(8,128)(2,1)S(1)}, u32[]{:S(2)}, u32[]{:S(2)}) %collective-permute-start.3) | collective-permute-done | bytes 524320 | tf_op jit(solution)/shard_map/ppermute | solution.py:44
  41.3 3.5 %collective-permute-start.7 = (bf16[512,512]{1,0:T(8,128)(2,1)S(1)}, bf16[512,512]{1,0:T(8,128)(2,1)S(1)}, u32[]{:S(2)}, u32[]{:S(2)}) collective-permute-start(bf16[512,512]{1,0:T(8,128)(2,1)S(1)} %bitcast.53), channel_id=1, source_target_pairs={{0,8},{8,16},{16,24},{24,0},{1,9},{9,17},{17,25},{25,1},{2,10},{10... | collective-permute-start | bytes 1572872 | tf_op jit(solution)/shard_map/ppermute | solution.py:44
  44.9 12.8 %collective-permute-done.8 = bf16[512,512]{1,0:T(8,128)(2,1)S(1)} collective-permute-done((bf16[512,512]{1,0:T(8,128)(2,1)S(1)}, bf16[512,512]{1,0:T(8,128)(2,1)S(1)}, u32[]{:S(2)}, u32[]{:S(2)}) %collective-permute-start.8) | collective-permute-done | bytes 524320 | tf_op jit(solution)/shard_map/ppermute | solution.py:44
  57.7 16.6 %collective-permute-done.5 = bf16[1536,512]{1,0:T(8,128)(2,1)S(1)} collective-permute-done((bf16[1536,512]{1,0:T(8,128)(2,1)S(1)}, bf16[1536,512]{1,0:T(8,128)(2,1)S(1)}, u32[]{:S(2)}, u32[]{:S(2)}) %collective-permute-start.5) | collective-permute-done | bytes 1572896 | tf_op jit(solution)/shard_map/ppermute | solution.py:40
  76.8 1.9 pad_maximum_fusion.16
  82.5 1.8 dynamic-slice_bitcast_fusion.3
  86.6 3.6 %collective-permute-start.12 = (bf16[512,512]{1,0:T(8,128)(2,1)S(1)}, bf16[512,512]{1,0:T(8,128)(2,1)S(1)}, u32[]{:S(2)}, u32[]{:S(2)}) collective-permute-start(bf16[512,512]{1,0:T(8,128)(2,1)S(1)} %bitcast.57), channel_id=1, source_target_pairs={{0,8},{8,16},{16,24},{24,0},{1,9},{9,17},{17,25},{25,1},{2,10},{10... | collective-permute-start | bytes 1572872 | tf_op jit(solution)/shard_map/ppermute | solution.py:44
  91.7 20.1 %collective-permute-done.10 = bf16[1536,512]{1,0:T(8,128)(2,1)} collective-permute-done((bf16[1536,512]{1,0:T(8,128)(2,1)}, bf16[1536,512]{1,0:T(8,128)(2,1)}, u32[]{:S(2)}, u32[]{:S(2)}) %collective-permute-start.10) | collective-permute-done | bytes 1572896 | tf_op jit(solution)/shard_map/ppermute | solution.py:40
  114.6 1.5 fusion.18
  127.8 3.5 %collective-permute-start.18 = (bf16[512,512]{1,0:T(8,128)(2,1)S(1)}, bf16[512,512]{1,0:T(8,128)(2,1)S(1)}, u32[]{:S(2)}, u32[]{:S(2)}) collective-permute-start(bf16[512,512]{1,0:T(8,128)(2,1)S(1)} %fusion.2), channel_id=1, source_target_pairs={{0,8},{8,16},{16,24},{24,0},{1,9},{9,17},{17,25},{25,1},{2,10},{10... | collective-permute-start | bytes 1572872 | tf_op jit(solution)/shard_map/ppermute | solution.py:44
  132.6 2.0 fusion.1
  134.6 26.0 %collective-permute-done.15 = bf16[1536,512]{1,0:T(8,128)(2,1)S(1)} collective-permute-done((bf16[1536,512]{1,0:T(8,128)(2,1)S(1)}, bf16[1536,512]{1,0:T(8,128)(2,1)S(1)}, u32[]{:S(2)}, u32[]{:S(2)}) %collective-permute-start.15) | collective-permute-done | bytes 1572896 | tf_op jit(solution)/shard_map/ppermute | solution.py:40
  162.6 1.5 collective-permute-start.20
  167.5 3.4 %collective-permute-start.31 = (bf16[512,512]{1,0:T(8,128)(2,1)S(1)}, bf16[512,512]{1,0:T(8,128)(2,1)S(1)}, u32[]{:S(2)}, u32[]{:S(2)}) collective-permute-start(bf16[512,512]{1,0:T(8,128)(2,1)S(1)} %fusion.7), channel_id=1, source_target_pairs={{0,8},{8,16},{16,24},{24,0},{1,9},{9,17},{17,25},{25,1},{2,10},{10... | collective-permute-start | bytes 1572872 | tf_op jit(solution)/shard_map/ppermute | solution.py:44
  172.4 3.5 %collective-permute-done.20 = bf16[512,512]{1,0:T(8,128)(2,1)S(1)} collective-permute-done((bf16[512,512]{1,0:T(8,128)(2,1)S(1)}, bf16[512,512]{1,0:T(8,128)(2,1)S(1)}, u32[]{:S(2)}, u32[]{:S(2)}) %collective-permute-start.20) | collective-permute-done | bytes 524320 | tf_op jit(solution)/shard_map/ppermute | solution.py:40
  179.0 2.3 fusion.27
  181.3 2.3 fusion.28
  183.6 2.1 fusion.5
  185.6 8.3 %collective-permute-done.31 = bf16[512,512]{1,0:T(8,128)(2,1)S(1)} collective-permute-done((bf16[512,512]{1,0:T(8,128)(2,1)S(1)}, bf16[512,512]{1,0:T(8,128)(2,1)S(1)}, u32[]{:S(2)}, u32[]{:S(2)}) %collective-permute-start.31) | collective-permute-done | bytes 524320 | tf_op jit(solution)/shard_map/ppermute | solution.py:44
  196.2 1.7 collective-permute-start.27
  198.5 3.4 %fusion.13 = f32[512,512]{1,0:T(8,128)S(1)} fusion(bf16[512,2048]{1,0:T(8,128)(2,1)} %copy-done.1, bf16[512,512]{1,0:T(8,128)(2,1)} %copy-done.22, bf16[512,512]{1,0:T(8,128)(2,1)} %copy-done.24, bf16[512,512]{1,0:T(8,128)(2,1)} %copy-done.20, bf16[512,512]{1,0:T(8,128)(2,1)} %copy-done.18), kind=kOutput, calls=%fused_computation.66 | convolution fusion | flops 1082130432 | bytes 5242880 | tf_op jit(solution)/shard_map/dot_general | solution.py:22
  202.0 8.4 %collective-permute-done.27 = bf16[512,512]{1,0:T(8,128)(2,1)} collective-permute-done((bf16[512,512]{1,0:T(8,128)(2,1)}, bf16[512,512]{1,0:T(8,128)(2,1)}, u32[]{:S(2)}, u32[]{:S(2)}) %collective-permute-start.27) | collective-permute-done | bytes 524320 | tf_op jit(solution)/shard_map/ppermute | solution.py:44
  210.4 2.1 fusion.8
  213.2 2.5 add_convert_fusion.1
  215.7 1.6 collective-permute-start.24
  217.4 8.5 %collective-permute-done.28 = bf16[512,512]{1,0:T(8,128)(2,1)S(1)} collective-permute-done((bf16[512,512]{1,0:T(8,128)(2,1)}, bf16[512,512]{1,0:T(8,128)(2,1)S(1)}, u32[]{:S(2)}, u32[]{:S(2)}) %collective-permute-start.28) | collective-permute-done | bytes 524320 | tf_op jit(solution)/shard_map/ppermute | solution.py:44
  225.8 14.9 %collective-permute-done.24 = bf16[512,512]{1,0:T(8,128)(2,1)S(1)} collective-permute-done((bf16[512,512]{1,0:T(8,128)(2,1)S(1)}, bf16[512,512]{1,0:T(8,128)(2,1)S(1)}, u32[]{:S(2)}, u32[]{:S(2)}) %collective-permute-start.24) | collective-permute-done | bytes 524320 | tf_op jit(solution)/shard_map/ppermute | solution.py:44
  240.7 8.7 %fusion = bf16[1,512,4096]{2,1,0:T(8,128)(2,1)} fusion(bf16[512,4096]{1,0:T(8,128)(2,1)} %param.11, bf16[512,4096]{1,0:T(8,128)(2,1)} %all-gather.2.cloned.1.call-done, bf16[512,512]{1,0:T(8,128)(2,1)} %fusion.1, bf16[512,512]{1,0:T(8,128)(2,1)S(1)} %collective-permute-done.24, bf16[512,512]{1,0:T(8,128)(2,1)S(1)} %collective-permute-done.28, pred[]{:T(512)S(6)} %eq.18, ...), kind=kOutput, calls=%fused_computation.1 | convolution fusion | flops 2158493696 | bytes 14155778 | tf_op jit(solution)/shard_map/dot_general | solution.py:13
  (138 shorter events, 45.6 us)
Async XLA Ops:
  6.5 234.2 %all-gather.2.cloned.1.call-start = ((), (), s32[]{:S(2)}) async-start(), calls=%async_computation | async-start | bytes 4718592 | tf_op jit(solution)/shard_map/all_gather | solution.py:150
  8.4 31.9 %collective-permute-start.4 = (bf16[2048,512]{1,0:T(8,128)(2,1)S(1)}, bf16[2048,512]{1,0:T(8,128)(2,1)S(1)}, u32[]{:S(2)}, u32[]{:S(2)}) collective-permute-start(bf16[2048,512]{1,0:T(8,128)(2,1)S(1)} %pad_maximum_fusion), channel_id=1, source_target_pairs={{0,1},{1,0},{2,3},{3,2},{4,5},{5,4},{6,7},{7,6},{8,9},{9,8},{10,11... | collective-permute-start | bytes 6291464 | tf_op jit(solution)/shard_map/ppermute | solution.py:40
  9.5 25.0 %collective-permute-start = (bf16[1024,512]{1,0:T(8,128)(2,1)S(1)}, bf16[1024,512]{1,0:T(8,128)(2,1)S(1)}, u32[]{:S(2)}, u32[]{:S(2)}) collective-permute-start(bf16[1024,512]{1,0:T(8,128)(2,1)S(1)} %pad_maximum_fusion.24), channel_id=1, source_target_pairs={{0,2},{1,3},{2,0},{3,1},{4,6},{5,7},{6,4},{7,5},{8,10},{9,11},{10,... | collective-permute-start | bytes 3145736 | tf_op jit(solution)/shard_map/ppermute | solution.py:40
  11.0 24.6 %collective-permute-start.1 = (bf16[1024,512]{1,0:T(8,128)(2,1)S(1)}, bf16[1024,512]{1,0:T(8,128)(2,1)S(1)}, u32[]{:S(2)}, u32[]{:S(2)}) collective-permute-start(bf16[1024,512]{1,0:T(8,128)(2,1)S(1)} %pad_maximum_fusion.24), channel_id=1, source_target_pairs={{0,4},{1,5},{2,6},{3,7},{4,0},{5,1},{6,2},{7,3},{8,12},{9,13},{10,... | collective-permute-start | bytes 3145736 | tf_op jit(solution)/shard_map/ppermute | solution.py:40
  12.5 13.1 %collective-permute-start.2 = (bf16[512,512]{1,0:T(8,128)(2,1)S(1)}, bf16[512,512]{1,0:T(8,128)(2,1)S(1)}, u32[]{:S(2)}, u32[]{:S(2)}) collective-permute-start(bf16[512,512]{1,0:T(8,128)(2,1)S(1)} %bitcast.52), channel_id=1, source_target_pairs={{0,24},{8,0},{16,8},{24,16},{1,25},{9,1},{17,9},{25,17},{2,26},{10... | collective-permute-start | bytes 1572872 | tf_op jit(solution)/shard_map/ppermute | solution.py:44
  25.7 13.8 %collective-permute-start.3 = (bf16[512,512]{1,0:T(8,128)(2,1)S(1)}, bf16[512,512]{1,0:T(8,128)(2,1)S(1)}, u32[]{:S(2)}, u32[]{:S(2)}) collective-permute-start(bf16[512,512]{1,0:T(8,128)(2,1)S(1)} %collective-permute-done.2), channel_id=1, source_target_pairs={{0,24},{8,0},{16,8},{24,16},{1,25},{9,1},{17,9},{25,17},{2,26},{10... | collective-permute-start | bytes 1572872 | tf_op jit(solution)/shard_map/ppermute | solution.py:44
  40.3 34.0 %collective-permute-start.5 = (bf16[1536,512]{1,0:T(8,128)(2,1)S(1)}, bf16[1536,512]{1,0:T(8,128)(2,1)S(1)}, u32[]{:S(2)}, u32[]{:S(2)}) collective-permute-start(bf16[1536,512]{1,0:T(8,128)(2,1)S(1)} %get-tuple-element.44), channel_id=1, source_target_pairs={{0,2},{1,3},{2,0},{3,1},{4,6},{5,7},{6,4},{7,5},{8,10},{9,11},{10,... | collective-permute-start | bytes 4718600 | tf_op jit(solution)/shard_map/ppermute | solution.py:40
  40.8 33.7 %collective-permute-start.6 = (bf16[1536,512]{1,0:T(8,128)(2,1)S(1)}, bf16[1536,512]{1,0:T(8,128)(2,1)S(1)}, u32[]{:S(2)}, u32[]{:S(2)}) collective-permute-start(bf16[1536,512]{1,0:T(8,128)(2,1)S(1)} %get-tuple-element.45), channel_id=1, source_target_pairs={{0,4},{1,5},{2,6},{3,7},{4,0},{5,1},{6,2},{7,3},{8,12},{9,13},{10,... | collective-permute-start | bytes 4718600 | tf_op jit(solution)/shard_map/ppermute | solution.py:40
  41.3 16.4 %collective-permute-start.8 = (bf16[512,512]{1,0:T(8,128)(2,1)S(1)}, bf16[512,512]{1,0:T(8,128)(2,1)S(1)}, u32[]{:S(2)}, u32[]{:S(2)}) collective-permute-start(bf16[512,512]{1,0:T(8,128)(2,1)S(1)} %bitcast.56), channel_id=1, source_target_pairs={{0,24},{8,0},{16,8},{24,16},{1,25},{9,1},{17,9},{25,17},{2,26},{10... | collective-permute-start | bytes 1572872 | tf_op jit(solution)/shard_map/ppermute | solution.py:44
  41.3 35.4 %collective-permute-start.7 = (bf16[512,512]{1,0:T(8,128)(2,1)S(1)}, bf16[512,512]{1,0:T(8,128)(2,1)S(1)}, u32[]{:S(2)}, u32[]{:S(2)}) collective-permute-start(bf16[512,512]{1,0:T(8,128)(2,1)S(1)} %bitcast.53), channel_id=1, source_target_pairs={{0,8},{8,16},{16,24},{24,0},{1,9},{9,17},{17,25},{25,1},{2,10},{10... | collective-permute-start | bytes 1572872 | tf_op jit(solution)/shard_map/ppermute | solution.py:44
  57.7 19.0 %collective-permute-start.9 = (bf16[512,512]{1,0:T(8,128)(2,1)S(1)}, bf16[512,512]{1,0:T(8,128)(2,1)S(1)}, u32[]{:S(2)}, u32[]{:S(2)}) collective-permute-start(bf16[512,512]{1,0:T(8,128)(2,1)S(1)} %collective-permute-done.8), channel_id=1, source_target_pairs={{0,24},{8,0},{16,8},{24,16},{1,25},{9,1},{17,9},{25,17},{2,26},{10... | collective-permute-start | bytes 1572872 | tf_op jit(solution)/shard_map/ppermute | solution.py:44
  78.7 33.1 %collective-permute-start.10 = (bf16[1536,512]{1,0:T(8,128)(2,1)}, bf16[1536,512]{1,0:T(8,128)(2,1)}, u32[]{:S(2)}, u32[]{:S(2)}) collective-permute-start(bf16[1536,512]{1,0:T(8,128)(2,1)} %get-tuple-element.51), channel_id=1, source_target_pairs={{0,2},{1,3},{2,0},{3,1},{4,6},{5,7},{6,4},{7,5},{8,10},{9,11},{10,... | collective-permute-start | bytes 4718600 | tf_op jit(solution)/shard_map/ppermute | solution.py:40
  80.2 32.8 %collective-permute-start.11 = (bf16[1536,512]{1,0:T(8,128)(2,1)}, bf16[1536,512]{1,0:T(8,128)(2,1)}, u32[]{:S(2)}, u32[]{:S(2)}) collective-permute-start(bf16[1536,512]{1,0:T(8,128)(2,1)} %get-tuple-element.52), channel_id=1, source_target_pairs={{0,4},{1,5},{2,6},{3,7},{4,0},{5,1},{6,2},{7,3},{8,12},{9,13},{10,... | collective-permute-start | bytes 4718600 | tf_op jit(solution)/shard_map/ppermute | solution.py:40
  85.6 32.3 %collective-permute-start.13 = (bf16[2048,512]{1,0:T(8,128)(2,1)S(1)}, bf16[2048,512]{1,0:T(8,128)(2,1)S(1)}, u32[]{:S(2)}, u32[]{:S(2)}) collective-permute-start(bf16[2048,512]{1,0:T(8,128)(2,1)S(1)} %pad_maximum_fusion.3), channel_id=1, source_target_pairs={{0,1},{1,0},{2,3},{3,2},{4,5},{5,4},{6,7},{7,6},{8,9},{9,8},{10,11... | collective-permute-start | bytes 6291464 | tf_op jit(solution)/shard_map/ppermute | solution.py:40
  86.6 31.1 %collective-permute-start.12 = (bf16[512,512]{1,0:T(8,128)(2,1)S(1)}, bf16[512,512]{1,0:T(8,128)(2,1)S(1)}, u32[]{:S(2)}, u32[]{:S(2)}) collective-permute-start(bf16[512,512]{1,0:T(8,128)(2,1)S(1)} %bitcast.57), channel_id=1, source_target_pairs={{0,8},{8,16},{16,24},{24,0},{1,9},{9,17},{17,25},{25,1},{2,10},{10... | collective-permute-start | bytes 1572872 | tf_op jit(solution)/shard_map/ppermute | solution.py:44
  121.9 5.9 %collective-permute-start.19 = (f32[512,512]{1,0:T(8,128)S(1)}, f32[512,512]{1,0:T(8,128)S(1)}, u32[]{:S(2)}, u32[]{:S(2)}) collective-permute-start(f32[512,512]{1,0:T(8,128)S(1)} %fusion.25), channel_id=1, source_target_pairs={{0,1},{1,0},{2,3},{3,2},{4,5},{5,4},{6,7},{7,6},{8,9},{9,8},{10,11... | collective-permute-start | bytes 3145736 | tf_op jit(solution)/shard_map/ppermute | solution.py:40
  123.7 8.9 %collective-permute-start.14 = (f32[512,512]{1,0:T(8,128)S(1)}, f32[512,512]{1,0:T(8,128)S(1)}, u32[]{:S(2)}, u32[]{:S(2)}) collective-permute-start(f32[512,512]{1,0:T(8,128)S(1)} %fusion.23), channel_id=1, source_target_pairs={{0,1},{1,0},{2,3},{3,2},{4,5},{5,4},{6,7},{7,6},{8,9},{9,8},{10,11... | collective-permute-start | bytes 3145736 | tf_op jit(solution)/shard_map/ppermute | solution.py:40
  123.8 36.8 %collective-permute-start.15 = (bf16[1536,512]{1,0:T(8,128)(2,1)S(1)}, bf16[1536,512]{1,0:T(8,128)(2,1)S(1)}, u32[]{:S(2)}, u32[]{:S(2)}) collective-permute-start(bf16[1536,512]{1,0:T(8,128)(2,1)S(1)} %get-tuple-element.58), channel_id=1, source_target_pairs={{0,2},{1,3},{2,0},{3,1},{4,6},{5,7},{6,4},{7,5},{8,10},{9,11},{10,... | collective-permute-start | bytes 4718600 | tf_op jit(solution)/shard_map/ppermute | solution.py:40
  124.4 36.5 %collective-permute-start.16 = (bf16[1536,512]{1,0:T(8,128)(2,1)S(1)}, bf16[1536,512]{1,0:T(8,128)(2,1)S(1)}, u32[]{:S(2)}, u32[]{:S(2)}) collective-permute-start(bf16[1536,512]{1,0:T(8,128)(2,1)S(1)} %get-tuple-element.59), channel_id=1, source_target_pairs={{0,4},{1,5},{2,6},{3,7},{4,0},{5,1},{6,2},{7,3},{8,12},{9,13},{10,... | collective-permute-start | bytes 4718600 | tf_op jit(solution)/shard_map/ppermute | solution.py:40
  126.4 39.8 %collective-permute-start.30 = (f32[512,512]{1,0:T(8,128)S(1)}, f32[512,512]{1,0:T(8,128)S(1)}, u32[]{:S(2)}, u32[]{:S(2)}) collective-permute-start(f32[512,512]{1,0:T(8,128)S(1)} %fusion.30), channel_id=1, source_target_pairs={{0,1},{1,0},{2,3},{3,2},{4,5},{5,4},{6,7},{7,6},{8,9},{9,8},{10,11... | collective-permute-start | bytes 3145736 | tf_op jit(solution)/shard_map/ppermute | solution.py:40
  127.8 33.3 %collective-permute-start.18 = (bf16[512,512]{1,0:T(8,128)(2,1)S(1)}, bf16[512,512]{1,0:T(8,128)(2,1)S(1)}, u32[]{:S(2)}, u32[]{:S(2)}) collective-permute-start(bf16[512,512]{1,0:T(8,128)(2,1)S(1)} %fusion.2), channel_id=1, source_target_pairs={{0,8},{8,16},{16,24},{24,0},{1,9},{9,17},{17,25},{25,1},{2,10},{10... | collective-permute-start | bytes 1572872 | tf_op jit(solution)/shard_map/ppermute | solution.py:44
  162.6 13.3 %collective-permute-start.20 = (bf16[512,512]{1,0:T(8,128)(2,1)S(1)}, bf16[512,512]{1,0:T(8,128)(2,1)S(1)}, u32[]{:S(2)}, u32[]{:S(2)}) collective-permute-start(bf16[512,512]{1,0:T(8,128)(2,1)S(1)} %get-tuple-element.64), channel_id=1, source_target_pairs={{0,2},{1,3},{2,0},{3,1},{4,6},{5,7},{6,4},{7,5},{8,10},{9,11},{10,... | collective-permute-start | bytes 1572872 | tf_op jit(solution)/shard_map/ppermute | solution.py:40
  164.2 12.9 %collective-permute-start.21 = (bf16[512,512]{1,0:T(8,128)(2,1)S(1)}, bf16[512,512]{1,0:T(8,128)(2,1)S(1)}, u32[]{:S(2)}, u32[]{:S(2)}) collective-permute-start(bf16[512,512]{1,0:T(8,128)(2,1)S(1)} %get-tuple-element.65), channel_id=1, source_target_pairs={{0,4},{1,5},{2,6},{3,7},{4,0},{5,1},{6,2},{7,3},{8,12},{9,13},{10,... | collective-permute-start | bytes 1572872 | tf_op jit(solution)/shard_map/ppermute | solution.py:40
  166.2 11.5 %collective-permute-start.22 = (f32[512,512]{1,0:T(8,128)S(1)}, f32[512,512]{1,0:T(8,128)S(1)}, u32[]{:S(2)}, u32[]{:S(2)}) collective-permute-start(f32[512,512]{1,0:T(8,128)S(1)} %fusion.26), channel_id=1, source_target_pairs={{0,1},{1,0},{2,3},{3,2},{4,5},{5,4},{6,7},{7,6},{8,9},{9,8},{10,11... | collective-permute-start | bytes 3145736 | tf_op jit(solution)/shard_map/ppermute | solution.py:40
  167.5 26.4 %collective-permute-start.31 = (bf16[512,512]{1,0:T(8,128)(2,1)S(1)}, bf16[512,512]{1,0:T(8,128)(2,1)S(1)}, u32[]{:S(2)}, u32[]{:S(2)}) collective-permute-start(bf16[512,512]{1,0:T(8,128)(2,1)S(1)} %fusion.7), channel_id=1, source_target_pairs={{0,8},{8,16},{16,24},{24,0},{1,9},{9,17},{17,25},{25,1},{2,10},{10... | collective-permute-start | bytes 1572872 | tf_op jit(solution)/shard_map/ppermute | solution.py:44
  172.1 11.4 %collective-permute-start.26 = (f32[512,512]{1,0:T(8,128)S(1)}, f32[512,512]{1,0:T(8,128)S(1)}, u32[]{:S(2)}, u32[]{:S(2)}) collective-permute-start(f32[512,512]{1,0:T(8,128)S(1)} %fusion.29), channel_id=1, source_target_pairs={{0,1},{1,0},{2,3},{3,2},{4,5},{5,4},{6,7},{7,6},{8,9},{9,8},{10,11... | collective-permute-start | bytes 3145736 | tf_op jit(solution)/shard_map/ppermute | solution.py:40
  178.9 15.8 %collective-permute-start.29 = (bf16[512,512]{1,0:T(8,128)(2,1)S(1)}, bf16[512,512]{1,0:T(8,128)(2,1)S(1)}, u32[]{:S(2)}, u32[]{:S(2)}) collective-permute-start(bf16[512,512]{1,0:T(8,128)(2,1)S(1)} %fusion.4), channel_id=1, source_target_pairs={{0,24},{8,0},{16,8},{24,16},{1,25},{9,1},{17,9},{25,17},{2,26},{10... | collective-permute-start | bytes 1572872 | tf_op jit(solution)/shard_map/ppermute | solution.py:44
  195.6 14.8 %collective-permute-start.25 = (f32[512,512]{1,0:T(8,128)}, f32[512,512]{1,0:T(8,128)S(1)}, u32[]{:S(2)}, u32[]{:S(2)}) collective-permute-start(f32[512,512]{1,0:T(8,128)} %fusion.28), channel_id=1, source_target_pairs={{0,1},{1,0},{2,3},{3,2},{4,5},{5,4},{6,7},{7,6},{8,9},{9,8},{10,11... | collective-permute-start | bytes 3145736 | tf_op jit(solution)/shard_map/ppermute | solution.py:40
  195.7 17.5 %collective-permute-start.23 = (f32[512,512]{1,0:T(8,128)}, f32[512,512]{1,0:T(8,128)}, u32[]{:S(2)}, u32[]{:S(2)}) collective-permute-start(f32[512,512]{1,0:T(8,128)} %fusion.27), channel_id=1, source_target_pairs={{0,1},{1,0},{2,3},{3,2},{4,5},{5,4},{6,7},{7,6},{8,9},{9,8},{10,11... | collective-permute-start | bytes 3145736 | tf_op jit(solution)/shard_map/ppermute | solution.py:40
  196.2 14.2 %collective-permute-start.27 = (bf16[512,512]{1,0:T(8,128)(2,1)}, bf16[512,512]{1,0:T(8,128)(2,1)}, u32[]{:S(2)}, u32[]{:S(2)}) collective-permute-start(bf16[512,512]{1,0:T(8,128)(2,1)} %fusion.5), channel_id=1, source_target_pairs={{0,8},{8,16},{16,24},{24,0},{1,9},{9,17},{17,25},{25,1},{2,10},{10... | collective-permute-start | bytes 1572872 | tf_op jit(solution)/shard_map/ppermute | solution.py:44
  212.5 13.3 %collective-permute-start.28 = (bf16[512,512]{1,0:T(8,128)(2,1)}, bf16[512,512]{1,0:T(8,128)(2,1)S(1)}, u32[]{:S(2)}, u32[]{:S(2)}) collective-permute-start(bf16[512,512]{1,0:T(8,128)(2,1)} %fusion.8), channel_id=1, source_target_pairs={{0,8},{8,16},{16,24},{24,0},{1,9},{9,17},{17,25},{25,1},{2,10},{10... | collective-permute-start | bytes 1572872 | tf_op jit(solution)/shard_map/ppermute | solution.py:44
  215.7 25.0 %collective-permute-start.24 = (bf16[512,512]{1,0:T(8,128)(2,1)S(1)}, bf16[512,512]{1,0:T(8,128)(2,1)S(1)}, u32[]{:S(2)}, u32[]{:S(2)}) collective-permute-start(bf16[512,512]{1,0:T(8,128)(2,1)S(1)} %add_convert_fusion.1), channel_id=1, source_target_pairs={{0,24},{8,0},{16,8},{24,16},{1,25},{9,1},{17,9},{25,17},{2,26},{10... | collective-permute-start | bytes 1572872 | tf_op jit(solution)/shard_map/ppermute | solution.py:44
  (30 other events, 530.4 us)
Sparse Core Ops, SparseCore 0:
  195.7 37.1 all-gather.1
